TPU v7x, 32 devices: a whole 2x2x4 slice. The times are simulated.
32 devices in a mesh: ctx: 8 (over z, y), chan: 4 (over x, core).
Axes of the slice: x: 2, y: 2, z: 4, core: 2. Of those that a mesh axis runs over, the one named last changes fastest.
Arguments:
- query_proj: bfloat16 [1024, 8192], P('ctx', 'chan'), may hold values from -6 to 6
- key_proj: bfloat16 [1024, 8192], P('ctx', 'chan'), may hold values from -6 to 6
- value_proj: bfloat16 [1024, 8192], P('ctx', 'chan'), may hold values from -6 to 6
- filters: bfloat16 [8192, 128], P('chan'), may hold values from -0.5 to 0.5
- out_weight: bfloat16 [8192, 8192], P('chan'), may hold values from -0.0625 to 0.0625
- cotangent: bfloat16 [1024, 8192], P('ctx', 'chan'), may hold values from -6 to 6
Outputs:
- mixed: bfloat16 [1024, 8192], P('ctx', 'chan')
- grad_query: bfloat16 [1024, 8192], P('ctx', 'chan')
- grad_key: bfloat16 [1024, 8192], P('ctx', 'chan')
- grad_value: bfloat16 [1024, 8192], P('ctx', 'chan')
- grad_filters: float32 [8192, 128], P('chan')
- grad_weight: bfloat16 [8192, 8192], P('chan', 'ctx')
All inputs are finite; a program needn't handle non-finite values.
Results may differ from a plain program's by a relative error of at most 0.019.
Values may be sent and summed in bfloat16 or wider, within the bound.
No kernel may reach another device: no remote copies, remote signals or barrier semaphores. Data moves between devices by JAX's collectives and lax.ppermute only.
A program may use at most 128 MiB of HBM per device.

v0:
```python
import jax
import jax.numpy as jnp
from jax import lax
from jax.sharding import PartitionSpec as P


def passed_along(block, axis, distance):
    devices = range(lax.axis_size(axis))
    route = [(i - distance, i) for i in devices if i - distance in devices]
    return lax.ppermute(block, axis, route)


def tap_sweep(source, taps_t, length, start_base, sign):
    group_size = 8
    tap_count = taps_t.shape[0]

    def one_group(group, running):
        for inner in range(group_size):
            offset = group * group_size + inner
            start = (start_base + sign * offset).astype(jnp.int32)
            rows = lax.dynamic_slice_in_dim(source, start, length, 0)
            running = running + rows * lax.dynamic_index_in_dim(taps_t, offset, 0, False)
        return running

    initial = jnp.zeros((length, source.shape[1]), jnp.float32)
    return lax.fori_loop(0, tap_count // group_size, one_group, initial)


def per_device(query_proj, key_proj, value_proj, filters, out_weight, cotangent):
    length, channels = query_proj.shape
    tap_count = filters.shape[1]
    taps_t = filters.astype(jnp.float32).T
    product = (key_proj.astype(jnp.float32) * value_proj.astype(jnp.float32)).astype(jnp.bfloat16)
    earlier = passed_along(product, "ctx", 1)
    ext_rows = jnp.concatenate([earlier, product], axis=0)
    ext_float = ext_rows.astype(jnp.float32)
    filtered = tap_sweep(ext_float, taps_t, length, tap_count, -1)
    gated_rows = (query_proj.astype(jnp.float32) * filtered).astype(jnp.bfloat16)
    partial_value = jnp.dot(gated_rows, out_weight, preferred_element_type=jnp.float32)
    mixed = lax.psum_scatter(
        partial_value.astype(jnp.bfloat16), "chan", scatter_dimension=1, tiled=True
    )
    full_cot = lax.all_gather(cotangent, "chan", axis=1, tiled=True)
    grad_gated = lax.dot_general(
        full_cot, out_weight, (((1,), (1,)), ((), ())), preferred_element_type=jnp.float32
    )
    grad_query = (grad_gated * filtered).astype(jnp.bfloat16)
    grad_filtered = (grad_gated * query_proj.astype(jnp.float32)).astype(jnp.bfloat16)
    grad_float = grad_filtered.astype(jnp.float32)
    following = passed_along(grad_filtered, "ctx", -1)
    grad_ext = jnp.concatenate([grad_float, following.astype(jnp.float32)], axis=0)
    grad_product = tap_sweep(grad_ext, taps_t, length, 0, 1)
    grad_key = (grad_product * value_proj.astype(jnp.float32)).astype(jnp.bfloat16)
    grad_value = (grad_product * key_proj.astype(jnp.float32)).astype(jnp.bfloat16)
    group_size = 8

    def tap_group(group, running):
        rows = []
        for inner in range(group_size):
            start = (tap_count - group * group_size - inner).astype(jnp.int32)
            source = lax.dynamic_slice_in_dim(ext_float, start, length, 0)
            rows.append(jnp.sum(grad_float * source, axis=0))
        stacked = jnp.stack(rows, axis=0)
        return lax.dynamic_update_slice_in_dim(
            running, stacked, (group * group_size).astype(jnp.int32), 0
        )

    tap_rows = lax.fori_loop(
        0, tap_count // group_size, tap_group, jnp.zeros((tap_count, channels), jnp.float32)
    )
    local_grad = tap_rows.T
    grad_filters = lax.psum(local_grad.astype(jnp.bfloat16), "ctx").astype(jnp.float32)
    partial_weight = lax.dot_general(
        gated_rows, full_cot, (((0,), (0,)), ((), ())), preferred_element_type=jnp.float32
    )
    grad_weight = lax.psum_scatter(
        partial_weight.astype(jnp.bfloat16), "ctx", scatter_dimension=1, tiled=True
    )
    return (mixed, grad_query, grad_key, grad_value, grad_filters, grad_weight)


def solution(mesh):
    placed = (
        P("ctx", "chan"),
        P("ctx", "chan"),
        P("ctx", "chan"),
        P("chan", None),
        P("chan", None),
        P("ctx", "chan"),
    )
    return jax.shard_map(
        per_device,
        mesh=mesh,
        in_specs=placed,
        out_specs=(
            P("ctx", "chan"),
            P("ctx", "chan"),
            P("ctx", "chan"),
            P("ctx", "chan"),
            P("chan", None),
            P("chan", "ctx"),
        ),
        check_vma=False,
    )
```

profile of v0, /device:TPU:0, one launch (start us, length us, event | category | flops | bytes accessed | tf_op | source)
XLA Modules:
  0.0 879.7 jit_solution(13803554456559080063)
XLA Ops:
  8.0 26.9 %all-gather.2.cloned.1.call-done = bf16[128,8192]{1,0:T(8,128)(2,1)} async-done(((bf16[128,2048]{1,0:T(8,128)(2,1)}), bf16[128,8192]{1,0:T(8,128)(2,1)}) %all-gather.2.cloned.1.call-update) | async-done | bytes 2097168 | tf_op jit(solution)/shard_map/all_gather | solution.py:43
  34.9 17.5 %fusion.21 = (f32[128,2048]{1,0:T(8,128)S(1)}, bf16[128,2048]{1,0:T(8,128)(2,1)S(1)}, f32[128,2048]{1,0:T(8,128)}) fusion(bf16[128,2048]{1,0:T(8,128)(2,1)} %param.12, bf16[128,8192]{1,0:T(8,128)(2,1)} %all-gather.2.cloned.1.call-done, bf16[2048,8192]{1,0:T(8,128)(2,1)} %param.16), kind=kOutput, calls=%fused_computation.58 | convolution fusion | flops 4296015872 | bytes 38797312 | tf_op jit(solution)/shard_map/dot_general | solution.py:44
  55.0 13.3 %collective-permute-done.1 = bf16[128,2048]{1,0:T(8,128)(2,1)S(1)} collective-permute-done((bf16[128,2048]{1,0:T(8,128)(2,1)S(1)}, bf16[128,2048]{1,0:T(8,128)(2,1)S(1)}, u32[]{:S(2)}, u32[]{:S(2)}) %collective-permute-start.1) | collective-permute-done | bytes 524320 | tf_op jit(solution)/shard_map/ppermute | solution.py:10
  68.6 75.6 %while.52 = (s32[]{:T(128)}, f32[128,2048]{1,0:T(8,128)}, f32[256,2048]{1,0:T(8,128)S(1)}, f32[128,2048]{1,0:T(8,128)}, s32[]{:T(128)}, /*index=5*/s32[]{:T(128)...) while((s32[]{:T(128)}, f32[128,2048]{1,0:T(8,128)}, ...), condition=%wide.region_4.5_spmd.clone, body=%wide.region_3.4_spmd.clone.sunk | while | flops 4456499 | bytes 10683271 | solution.py:26
  73.6 3.5 fusion.30
  78.3 3.5 fusion.30
  83.1 3.5 fusion.30
  87.9 3.5 fusion.30
  92.7 3.5 fusion.30
  97.5 3.5 fusion.30
  102.2 3.5 fusion.30
  107.0 3.5 fusion.30
  111.8 3.5 fusion.30
  116.8 3.5 fusion.30
  121.6 3.5 fusion.30
  126.4 3.5 fusion.30
  131.2 3.5 fusion.30
  136.0 3.5 fusion.30
  140.7 3.5 fusion.30
  144.2 2.7 fusion.16
  146.9 5.1 collective-permute-start
  152.0 10.0 %collective-permute-done = bf16[128,2048]{1,0:T(8,128)(2,1)} collective-permute-done((bf16[128,2048]{1,0:T(8,128)(2,1)S(1)}, bf16[128,2048]{1,0:T(8,128)(2,1)}, u32[]{:S(2)}, u32[]{:S(2)}) %collective-permute-start) | collective-permute-done | bytes 524320 | tf_op jit(solution)/shard_map/ppermute | solution.py:10
  164.2 52.8 %while.50 = (s32[]{:T(128)}, bf16[128,2048]{1,0:T(8,128)(2,1)}, f32[256,2048]{1,0:T(8,128)S(1)}, f32[128,2048]{1,0:T(8,128)}, s32[]{:T(128)}, /*index=5*/s32[]{:...) while((s32[]{:T(128)}, bf16[128,2048]{1,0:T(8,128)(2,1)}, ...), condition=%wide.region_14.15_spmd, body=%wide.region_5.14_spmd.sunk | while | flops 4177958 | bytes 9667215 | solution.py:68
  164.2 2.6 multiply_reduce_fusion.9
  170.8 2.6 multiply_reduce_fusion.9
  197.2 2.6 multiply_reduce_fusion.9
  207.1 2.6 multiply_reduce_fusion.9
  219.3 44.1 %while.51 = (s32[]{:T(128)}, f32[128,2048]{1,0:T(8,128)S(1)}, f32[256,2048]{1,0:T(8,128)S(1)}, f32[128,2048]{1,0:T(8,128)}, s32[]{:T(128)}, /*index=5*/s32[]{:T(...) while((s32[]{:T(128)}, f32[128,2048]{1,0:T(8,128)S(1)}, ...), condition=%wide.region_1.2_spmd.clone, body=%wide.region_0.1_spmd.clone.sunk | while | flops 4456523 | bytes 10683495 | solution.py:26
  263.5 16.6 %convolution_convert_fusion.1 = bf16[128,8192]{1,0:T(8,128)(2,1)} fusion(bf16[2048,8192]{1,0:T(8,128)(2,1)} %param.16, f32[128,2048]{1,0:T(8,128)S(1)} %get-tuple-element.437, bf16[128,2048]{1,0:T(8,128)(2,1)} %param.12), kind=kOutput, calls=%fused_computation.42 | convolution fusion | flops 4296802304 | bytes 37224448 | tf_op jit(solution)/shard_map/dot_general | solution.py:39
  281.6 14.7 %convolution_convert_fusion = bf16[2048,8192]{1,0:T(8,128)(2,1)} fusion(bf16[128,8192]{1,0:T(8,128)(2,1)S(1)} %copy-done.1, f32[128,2048]{1,0:T(8,128)S(1)} %get-tuple-element.437, bf16[128,2048]{1,0:T(8,128)(2,1)} %param.12), kind=kOutput, calls=%fused_computation.41 | convolution fusion | flops 4312530944 | bytes 37224448 | tf_op jit(solution)/shard_map/dot_general | solution.py:73
  300.5 25.4 %reduce-scatter.3.cloned.1.call-done = bf16[128,2048]{1,0:T(8,128)(2,1)} async-done(((bf16[128,8192]{1,0:T(8,128)(2,1)}), bf16[128,2048]{1,0:T(8,128)(2,1)}) %reduce-scatter.3.cloned.1.call-update) | async-done | bytes 524304 | tf_op jit(solution)/shard_map/reduce_scatter | solution.py:40
  325.9 547.3 %reduce-scatter.5.cloned.1.call-done = bf16[2048,1024]{1,0:T(8,128)(2,1)} async-done(((bf16[2048,8192]{1,0:T(8,128)(2,1)}), bf16[2048,1024]{1,0:T(8,128)(2,1)}) %reduce-scatter.5.cloned.1.call-update) | async-done | bytes 4194320 | tf_op jit(solution)/shard_map/reduce_scatter | solution.py:76
  (126 shorter events, 121.5 us)
Async XLA Ops:
  7.2 27.7 %all-gather.2.cloned.1.call-start = ((), (), s32[]{:S(2)}) async-start(), calls=%async_computation.3 | async-start | bytes 2621440 | tf_op jit(solution)/shard_map/all_gather | solution.py:43
  7.9 45.8 %copy-start.5 = (bf16[2048,128]{1,0:T(8,128)(2,1)S(1)}, bf16[2048,128]{1,0:T(8,128)(2,1)}, u32[]{:S(2)}) copy-start(bf16[2048,128]{1,0:T(8,128)(2,1)} %param.15) | copy-start | bytes 1572868
  7.9 290.5 %all-reduce.2.cloned.1.call-start = ((), (), s32[]{:S(2)}) async-start(), calls=%async_computation.4 | async-start | bytes 1048576 | tf_op jit(solution)/shard_map/psum | solution.py:72
  52.4 16.1 %copy-start = (f32[128,2048]{1,0:T(8,128)}, f32[128,2048]{1,0:T(8,128)S(1)}, u32[]{:S(2)}) copy-start(f32[128,2048]{1,0:T(8,128)S(1)} %get-tuple-element.809) | copy-start | bytes 3145732
  52.4 16.0 %collective-permute-start.1 = (bf16[128,2048]{1,0:T(8,128)(2,1)S(1)}, bf16[128,2048]{1,0:T(8,128)(2,1)S(1)}, u32[]{:S(2)}, u32[]{:S(2)}) collective-permute-start(bf16[128,2048]{1,0:T(8,128)(2,1)S(1)} %get-tuple-element.503), channel_id=1, source_target_pairs={{4,0},{8,4},{12,8},{16,12},{20,16},{24,20},{28,24},{5,1},{9,5},{13... | collective-permute-start | bytes 1572872 | tf_op jit(solution)/shard_map/ppermute | solution.py:10
  68.6 75.6 %copy-start.4 = (bf16[128,2048]{1,0:T(8,128)(2,1)S(1)}, bf16[128,2048]{1,0:T(8,128)(2,1)}, u32[]{:S(2)}) copy-start(bf16[128,2048]{1,0:T(8,128)(2,1)} %param.13) | copy-start | bytes 1572868
  146.9 5.1 copy-start.3
  146.9 15.0 %collective-permute-start = (bf16[128,2048]{1,0:T(8,128)(2,1)S(1)}, bf16[128,2048]{1,0:T(8,128)(2,1)}, u32[]{:S(2)}, u32[]{:S(2)}) collective-permute-start(bf16[128,2048]{1,0:T(8,128)(2,1)S(1)} %get-tuple-element.522), channel_id=1, source_target_pairs={{0,4},{4,8},{8,12},{12,16},{16,20},{20,24},{24,28},{1,5},{5,9},{9,... | collective-permute-start | bytes 1572872 | tf_op jit(solution)/shard_map/ppermute | solution.py:10
  219.1 106.8 %reduce-scatter.3.cloned.1.call-start = ((), (), s32[]{:S(2)}) async-start(), calls=%async_computation.2 | async-start | bytes 2621440 | tf_op jit(solution)/shard_map/reduce_scatter | solution.py:40
  280.0 1.6 copy-start.1
  280.1 593.1 %reduce-scatter.5.cloned.1.call-start = ((), (), s32[]{:S(2)}) async-start(), calls=%async_computation.5 | async-start | bytes 37748736 | tf_op jit(solution)/shard_map/reduce_scatter | solution.py:76
  296.3 1.2 copy-start.2
Sparse Core Ops, SparseCore 0:
  9.6 25.2 all-gather.1
  219.2 72.5 all-reduce.1
  295.1 30.6 reduce-scatter.2
  330.1 543.0 reduce-scatter.4
where the time goes:
time: 884 us; the launch traced here: 880 us
  waiting for transfers between devices  624 us (71%)
  other arithmetic  125 us (14%)
  local copies, waits for them, and re-layouts  59.4 us (7%)
  matrix products  48.7 us (6%)
  between operations  13.9 us (2%)
    reduce_scatter x1, waiting for transfers between devices, per_device(): lax.psum_scatter(partial_weight.astype(jnp.bfloat16), 'ctx', scatter_dime...  547 us
    add x32, other arithmetic, one_group(): running + rows * lax.dynamic_index_in_dim(taps_t, offset, 0, False)  75.7 us
    dynamic_slice x32, local copies, waits for them, and re-layouts, one_group(): lax.dynamic_index_in_dim(taps_t, offset, 0, False)  41.8 us
    reduce_sum x16, other arithmetic, tap_group(): rows.append(jnp.sum(grad_float * source, axis=0))  41 us
    all_gather x1, waiting for transfers between devices, per_device(): full_cot = lax.all_gather(cotangent, 'chan', axis=1, tiled=True)  26.9 us
    reduce_scatter x1, waiting for transfers between devices, per_device(): lax.psum_scatter(partial_value.astype(jnp.bfloat16), 'chan', scatter_dime...  25.4 us
    ppermute x2, waiting for transfers between devices, passed_along(): return lax.ppermute(block, axis, route)  23.3 us
  transfers between devices with their start and end apart: 6, of which 5 were waited for; matrix products, arithmetic and copies ran while one was open for 9% of the time, Pallas kernels for 0%

commit v1 on v0

v1 whole, which is shorter than its diff:
```python
import functools

import jax
import jax.numpy as jnp
import numpy as np
from jax import lax
from jax.experimental import pallas as pl
from jax.experimental.pallas import tpu as pltpu
from jax.sharding import PartitionSpec as P

F32 = jnp.float32
BF16 = jnp.bfloat16
VMEM_BYTES = 40 * 2**20
NT = (((1,), (1,)), ((), ()))
TN = (((0,), (0,)), ((), ()))


def halves(matrix):
    high = matrix.astype(BF16)
    low = (matrix - high.astype(np.float64)).astype(BF16)
    return np.stack([high, low])


def transforms(taps):
    points = 2 * taps
    angle = np.pi * (2 * np.arange(taps)[:, None] + 1) * np.arange(points)[None, :] / points
    forward = np.concatenate([np.cos(angle), -np.sin(angle)], axis=0)
    inverse = forward.T * (2.0 / points)
    late = inverse[taps:]
    early = inverse[:taps]
    lags = inverse[taps - np.arange(taps)]
    return halves(forward), halves(late), halves(early), halves(lags)


def mm(a, b, dims=(((1,), (0,)), ((), ()))):
    return lax.dot_general(a, b, dims, preferred_element_type=F32)


def spectrum(f_ref, rows):
    return mm(f_ref[0], rows) + mm(f_ref[1], rows)


def tap_spectrum(f_ref, filters, taps):
    return mm(f_ref[0, :, :taps], filters, NT) + mm(f_ref[1, :, :taps], filters, NT)


def back(g_ref, real, imag):
    both = jnp.concatenate([real, imag], axis=0)
    high = both.astype(BF16)
    low = (both - high.astype(F32)).astype(BF16)
    return mm(g_ref[0], high) + mm(g_ref[0], low) + mm(g_ref[1], high)


def forward_kernel(taps, q_ref, k_ref, v_ref, earlier_ref, filt_ref, f_ref, g_ref, gated_ref, filtered_ref):
    product = (k_ref[...].astype(F32) * v_ref[...].astype(F32)).astype(BF16)
    x = spectrum(f_ref, jnp.concatenate([earlier_ref[...], product], axis=0))
    h = tap_spectrum(f_ref, filt_ref[...], taps)
    xr, xi, hr, hi = x[:taps], x[taps:], h[:taps], h[taps:]
    filtered = back(g_ref, xr * hr - xi * hi, xr * hi + xi * hr)
    filtered_ref[...] = filtered
    gated_ref[...] = (q_ref[...].astype(F32) * filtered).astype(BF16)


def tap_grad_kernel(taps, k_ref, v_ref, earlier_ref, gf_ref, f_ref, g_ref, out_ref):
    product = (k_ref[...].astype(F32) * v_ref[...].astype(F32)).astype(BF16)
    x = spectrum(f_ref, jnp.concatenate([earlier_ref[...], product], axis=0))
    rows = gf_ref[...]
    g = mm(f_ref[0, :, :taps], rows) + mm(f_ref[1, :, :taps], rows)
    xr, xi, gr, gi = x[:taps], x[taps:], g[:taps], g[taps:]
    tap_rows = back(g_ref, xr * gr + xi * gi, xi * gr - xr * gi)
    out_ref[...] = tap_rows.T.astype(BF16)


def backward_kernel(taps, k_ref, v_ref, gf_ref, following_ref, filt_ref, f_ref, g_ref, gk_ref, gv_ref):
    g = spectrum(f_ref, jnp.concatenate([gf_ref[...], following_ref[...]], axis=0))
    h = tap_spectrum(f_ref, filt_ref[...], taps)
    gr, gi, hr, hi = g[:taps], g[taps:], h[:taps], h[taps:]
    grad_product = back(g_ref, hr * gr + hi * gi, hr * gi - hi * gr)
    gk_ref[...] = (grad_product * v_ref[...].astype(F32)).astype(BF16)
    gv_ref[...] = (grad_product * k_ref[...].astype(F32)).astype(BF16)


def by_channel(kernel, arrays, kinds, outs, name, flops):
    width = 256
    length, channels = arrays[0].shape
    specs = {
        "t": pl.BlockSpec((length, width), lambda i: (0, i)),
        "c": pl.BlockSpec((width, length), lambda i: (i, 0)),
    }

    def spec_of(kind, shape):
        if kind == "w":
            return pl.BlockSpec(shape, lambda i: (0,) * len(shape))
        return specs[kind]

    return pl.pallas_call(
        functools.partial(kernel, length),
        grid=(channels // width,),
        in_specs=[spec_of(kind, a.shape) for kind, a in zip(kinds, arrays)],
        out_specs=[specs[kind] for kind, unused in outs],
        out_shape=[
            jax.ShapeDtypeStruct((length, channels) if kind == "t" else (channels, length), dtype)
            for kind, dtype in outs
        ],
        compiler_params=pltpu.CompilerParams(vmem_limit_bytes=VMEM_BYTES),
        cost_estimate=pl.CostEstimate(flops=flops, bytes_accessed=sum(a.nbytes for a in arrays), transcendentals=0),
        name=name,
    )(*arrays)


def grad_gated_kernel(has_sum, ids_ref, cot_ref, w_ref, *refs):
    total = mm(cot_ref[...], w_ref[...], NT)
    if has_sum:
        total = total + refs[0][...]
    refs[-1][...] = total


def grad_gated_part(cot, weight, block, running):
    length, width = cot.shape
    channels = weight.shape[0]
    tile = 256
    arrays = [cot, weight]
    in_specs = [
        pl.BlockSpec((length, width), lambda i, ids: (0, 0)),
        pl.BlockSpec((tile, width), lambda i, ids: (i, ids[0])),
    ]
    if running is not None:
        arrays.append(running)
        in_specs.append(pl.BlockSpec((length, tile), lambda i, ids: (0, i)))
    return pl.pallas_call(
        functools.partial(grad_gated_kernel, running is not None),
        grid_spec=pltpu.PrefetchScalarGridSpec(
            num_scalar_prefetch=1,
            grid=(channels // tile,),
            in_specs=in_specs,
            out_specs=pl.BlockSpec((length, tile), lambda i, ids: (0, i)),
        ),
        out_shape=jax.ShapeDtypeStruct((length, channels), F32),
        compiler_params=pltpu.CompilerParams(vmem_limit_bytes=VMEM_BYTES),
        cost_estimate=pl.CostEstimate(
            flops=2 * length * width * channels, bytes_accessed=2 * width * channels, transcendentals=0
        ),
        name="grad_gated_part",
    )(jnp.reshape(block, (1,)), *arrays)


def mixed_kernel(adds, ids_ref, gated_ref, w_ref, *refs):
    total = mm(gated_ref[...], w_ref[...])
    for ref in refs[:adds]:
        total = total + ref[...].astype(F32)
    refs[-1][...] = total.astype(refs[-1].dtype)


def mixed_part(gated, weight, blocks, received, kind):
    length, channels = gated.shape
    width = channels
    tile = 512
    steps = width // tile
    ids = jnp.stack([jnp.stack(blocks)] + [jnp.asarray(at, jnp.int32) for unused, at in received])
    in_specs = [
        pl.BlockSpec((length, channels), lambda b, t, ids: (0, 0)),
        pl.BlockSpec((channels, tile), lambda b, t, ids: (0, ids[0, b] * steps + t)),
    ]
    for place in range(len(received)):
        in_specs.append(
            pl.BlockSpec((length, tile), lambda b, t, ids, place=place: (0, ids[place + 1, b] * steps + t))
        )
    return pl.pallas_call(
        functools.partial(mixed_kernel, len(received)),
        grid_spec=pltpu.PrefetchScalarGridSpec(
            num_scalar_prefetch=1,
            grid=(len(blocks), steps),
            in_specs=in_specs,
            out_specs=pl.BlockSpec((length, tile), lambda b, t, ids: (0, b * steps + t)),
        ),
        out_shape=jax.ShapeDtypeStruct((length, width * len(blocks)), kind),
        compiler_params=pltpu.CompilerParams(vmem_limit_bytes=VMEM_BYTES),
        cost_estimate=pl.CostEstimate(
            flops=2 * length * channels * width * len(blocks),
            bytes_accessed=2 * channels * width * len(blocks),
            transcendentals=0,
        ),
        name="mixed_part",
    )(ids, gated, weight, *[array for array, unused in received])


def weight_kernel(slots, parts, half, ids_ref, *refs):
    gated_refs = refs[: slots - 1]
    far_low, far_high = refs[slots - 1 : slots + 1]
    cot_refs = refs[slots + 1 : slots + 1 + parts]
    out_ref = refs[-1]
    length = far_low.shape[0]
    piece = cot_refs[0].shape[1]
    far = jnp.where(pl.program_id(0) < half, far_low[...], far_high[...])
    columns = jnp.concatenate([ref[...] for ref in gated_refs] + [far], axis=0)
    for part in range(parts):
        rows = [
            cot_refs[part][pl.ds(pl.multiple_of(ids_ref[part, slot] * length, length), length), :]
            for slot in range(slots)
        ]
        total = mm(columns, jnp.concatenate(rows, axis=0), TN)
        place = pl.multiple_of(ids_ref[part, slots] * piece, piece)
        out_ref[:, pl.ds(place, piece)] = total.astype(BF16)


def grad_weight_of(blocks, far_low, far_high, cots, ids):
    length, channels = blocks[0].shape
    rows, piece = cots[0].shape
    tile = 256
    half = channels // tile // 2
    slots, parts = len(blocks) + 1, len(cots)
    in_specs = [pl.BlockSpec((length, tile), lambda i, ids: (0, i)) for unused in blocks]
    in_specs.append(pl.BlockSpec((length, tile), lambda i, ids: (0, jnp.minimum(i, half - 1))))
    in_specs.append(pl.BlockSpec((length, tile), lambda i, ids: (0, jnp.maximum(i - half, 0))))
    in_specs += [pl.BlockSpec((rows, piece), lambda i, ids: (0, 0)) for unused in cots]
    return pl.pallas_call(
        functools.partial(weight_kernel, slots, parts, half),
        grid_spec=pltpu.PrefetchScalarGridSpec(
            num_scalar_prefetch=1,
            grid=(channels // tile,),
            in_specs=in_specs,
            out_specs=pl.BlockSpec((tile, piece * parts), lambda i, ids: (i, 0)),
        ),
        out_shape=jax.ShapeDtypeStruct((channels, piece * parts), BF16),
        compiler_params=pltpu.CompilerParams(vmem_limit_bytes=VMEM_BYTES),
        cost_estimate=pl.CostEstimate(
            flops=2 * rows * channels * piece * parts, bytes_accessed=4 * rows * channels, transcendentals=0
        ),
        name="grad_weight",
    )(ids, *blocks, far_low, far_high, *cots)


def in_one_piece(columns, ids, length):
    slots, piece = ids.shape[1] - 1, columns[0].shape[1]
    whole = jnp.zeros((slots * length, piece * len(columns)), columns[0].dtype)
    for part, column in enumerate(columns):
        rows = [lax.dynamic_slice_in_dim(column, ids[part, slot] * length, length, 0) for slot in range(slots)]
        whole = lax.dynamic_update_slice_in_dim(whole, jnp.concatenate(rows, axis=0), ids[part, slots] * piece, 1)
    return [whole], jnp.asarray([list(range(slots)) + [0]], jnp.int32)


def cycle_of(count):
    across = 1 << ((count.bit_length() - 1) // 2)
    order = []
    for column in range(across):
        line = [row * across + column for row in range(count // across)]
        order += line if column % 2 == 0 else line[::-1]
    return order


def swap(block, axis, bit):
    size = lax.axis_size(axis)
    return lax.ppermute(block, axis, [(i, i ^ bit) for i in range(size)])


def bits_of(size):
    return [1 << place for place in range(size.bit_length() - 1)]


def gather_by_swaps(block):
    held = {0: block}
    for bit in reversed(bits_of(lax.axis_size("chan"))):
        held.update({off ^ bit: swap(held[off], "chan", bit) for off in list(held)})
    return held


def sum_over_ctx(local):
    me = lax.axis_index("ctx")
    bits = bits_of(lax.axis_size("ctx"))
    part = local
    for bit in bits:
        middle = part.shape[0] // 2
        mine = (me & bit) != 0
        keep = jnp.where(mine, part[middle:], part[:middle])
        give = jnp.where(mine, part[:middle], part[middle:])
        part = (keep.astype(F32) + swap(give, "ctx", bit).astype(F32)).astype(BF16)
    for bit in reversed(bits):
        mine = (me & bit) != 0
        other = swap(part, "ctx", bit)
        part = jnp.concatenate([jnp.where(mine, other, part), jnp.where(mine, part, other)], axis=0)
    return part.astype(F32)


def per_device(query_proj, key_proj, value_proj, filters, out_weight, cotangent):
    length, channels = query_proj.shape
    taps = filters.shape[1]
    n_ctx, n_chan = lax.axis_size("ctx"), lax.axis_size("chan")
    ctx, chan = lax.axis_index("ctx"), lax.axis_index("chan")
    per_chan = n_ctx // n_chan
    forward, late, early, lags = [jnp.asarray(m) for m in transforms(taps)]

    product = (key_proj.astype(F32) * value_proj.astype(F32)).astype(BF16)
    earlier = lax.ppermute(product, "ctx", [(i, i + 1) for i in range(n_ctx - 1)])

    cots = gather_by_swaps(cotangent)

    piece = channels // n_ctx
    turned = lax.dynamic_slice_in_dim(jnp.concatenate([cotangent, cotangent], axis=1), ctx * piece, channels, 1)
    pieces = []
    for step in range(n_ctx):
        route = []
        for c in range(n_ctx):
            for h in range(n_chan):
                place = (c + step) % n_ctx
                target = (h * per_chan + place // n_chan) * n_chan + place % n_chan
                route.append((c * n_chan + h, target))
        pieces.append(lax.ppermute(turned[:, step * piece : (step + 1) * piece], ("ctx", "chan"), route))
    column_cots = gather_by_swaps(jnp.concatenate(pieces, axis=0))

    grad_gated = None
    for off in sorted(cots):
        grad_gated = grad_gated_part(cots[off], out_weight, chan ^ off, grad_gated)

    gated, filtered = by_channel(
        forward_kernel,
        [query_proj, key_proj, value_proj, earlier, filters, forward, late],
        "ttttcww",
        [("t", BF16), ("t", F32)],
        "forward_filter",
        6 * 10**9,
    )

    order = cycle_of(n_ctx)
    ahead = [(order[i], order[(i + 1) % n_ctx]) for i in range(n_ctx)]
    behind = [(b, a) for a, b in ahead]
    half = channels // 2
    from_behind, from_ahead = gated, gated
    blocks = [gated]
    for step in range(n_ctx // 2 - 1):
        from_behind = lax.ppermute(from_behind, "ctx", ahead)
        from_ahead = lax.ppermute(from_ahead, "ctx", behind)
        blocks += [from_behind, from_ahead]
    far_low = lax.ppermute(from_behind[:, :half], "ctx", ahead)
    far_high = lax.ppermute(from_ahead[:, half:], "ctx", behind)

    grad_query = (grad_gated * filtered).astype(BF16)
    grad_filtered = (grad_gated * query_proj.astype(F32)).astype(BF16)
    following = lax.ppermute(grad_filtered, "ctx", [(i + 1, i) for i in range(n_ctx - 1)])

    received = []
    left = list(range(n_chan))
    for bit in bits_of(n_chan):
        give = [off for off in left if off & bit]
        left = [off for off in left if not off & bit]
        sums = [(array, [offs.index(off) for off in give]) for array, offs in received]
        part = mixed_part(gated, out_weight, [chan ^ off for off in give], sums, BF16)
        received.append((swap(part, "chan", bit), [off ^ bit for off in give]))
    last = received.pop()[0]
    own = mixed_part(
        gated, out_weight, [chan], [(array, [offs.index(0)]) for array, offs in received], F32
    )
    mixed = (own + last.astype(F32)).astype(BF16)

    tap_grad = by_channel(
        tap_grad_kernel,
        [key_proj, value_proj, earlier, grad_filtered, forward, lags],
        "ttttww",
        [("c", BF16)],
        "tap_grad",
        6 * 10**9,
    )[0]
    grad_filters = sum_over_ctx(tap_grad)
    grad_key, grad_value = by_channel(
        backward_kernel,
        [key_proj, value_proj, grad_filtered, following, filters, forward, early],
        "ttttcww",
        [("t", BF16), ("t", BF16)],
        "backward_filter",
        6 * 10**9,
    )

    ring = jnp.asarray(order, jnp.int32)
    spot = jnp.asarray(np.argsort(order), jnp.int32)[ctx]
    owners = [spot]
    for step in range(1, n_ctx // 2):
        owners += [spot - step, spot + step]
    owners.append(spot + n_ctx // 2)
    tokens = ring[jnp.mod(jnp.stack(owners), n_ctx)]
    rows = []
    for off in sorted(column_cots):
        column = chan ^ off
        base = (ctx % per_chan) * n_chan + column
        rows.append(jnp.concatenate([jnp.mod(base - tokens, n_ctx), column[None]]))
    ids = jnp.stack(rows).astype(jnp.int32)
    columns = [column_cots[off] for off in sorted(column_cots)]
    if piece % 128:
        columns, ids = in_one_piece(columns, ids, length)
    grad_weight = grad_weight_of(blocks, far_low, far_high, columns, ids)
    return (mixed, grad_query, grad_key, grad_value, grad_filters, grad_weight)


def solution(mesh):
    placed = (
        P("ctx", "chan"),
        P("ctx", "chan"),
        P("ctx", "chan"),
        P("chan", None),
        P("chan", None),
        P("ctx", "chan"),
    )
    return jax.shard_map(
        per_device,
        mesh=mesh,
        in_specs=placed,
        out_specs=(
            P("ctx", "chan"),
            P("ctx", "chan"),
            P("ctx", "chan"),
            P("ctx", "chan"),
            P("chan", None),
            P("chan", "ctx"),
        ),
        check_vma=False,
    )
```

time: 884 us -> 187 us (0.21)
  waiting for transfers between devices: 624 us -> 39.8 us
  other arithmetic: 125 us -> 6.38 us
  Pallas kernels: 0 us -> 78.3 us
  local copies, waits for them, and re-layouts: 59.4 us -> 4.51 us
  matrix products: 48.7 us -> 0 us
  starting transfers between devices: 6.68 us -> 50.6 us
    reduce_scatter x2 -> x0, waiting for transfers between devices: 573 us -> none  [the longest x1 547 us: per_device(): lax.psum_scatter(partial_weight.astype(jnp.bfloat16), 'ctx', scatter_dime...]
    pallas_call x0 -> x11, Pallas kernels: none -> 78.3 us  [the longest x4 30.8 us: grad_gated_part(): pl.pallas_call(functools.partial(grad_gated_kernel, running is not None),...]
    add x32 -> x0, other arithmetic: 75.7 us -> none  [one_group(): running + rows * lax.dynamic_index_in_dim(taps_t, offset, 0, False)]
    dot_general x3 -> x0, matrix products: 48.7 us -> none  [the longest x1 17.5 us: per_device(): lax.dot_general(full_cot, out_weight, (((1,), (1,)), ((), ())), preferred...]
    ppermute x2 -> x32, starting transfers between devices: 6.35 us -> 50.6 us  [the longest x8 25.6 us: per_device(): lax.ppermute(turned[:, step * piece:(step + 1) * piece], ('ctx', 'chan'),...]
    reduce_sum x16 -> x0, other arithmetic: 41 us -> none  [tap_group(): rows.append(jnp.sum(grad_float * source, axis=0))]
    dynamic_slice x32 -> x1, local copies, waits for them, and re-layouts: 41.8 us -> 1.24 us  [per_device(): spot = jnp.asarray(np.argsort(order), jnp.int32)[ctx]]
    all_gather x1 -> x0, waiting for transfers between devices: 26.9 us -> none  [per_device(): full_cot = lax.all_gather(cotangent, 'chan', axis=1, tiled=True)]
  transfers between devices with their start and end apart: 6 -> 32, of which waited for: 5 -> 8; matrix products, arithmetic and copies ran while one was open for 9% -> 5% of each run, Pallas kernels for 0% -> 37%
where the time goes in v1:
time: 187 us; the launch traced here: 185 us
  Pallas kernels  78.3 us (42%)
  starting transfers between devices  50.6 us (27%)
  waiting for transfers between devices  39.8 us (21%)
  other arithmetic  6.38 us (3%)
  between operations  5.8 us (3%)
  local copies, waits for them, and re-layouts  4.51 us (2%)
    pallas_call x4, Pallas kernels, grad_gated_part(): pl.pallas_call(functools.partial(grad_gated_kernel, running is not None),...  30.8 us
    ppermute x8, starting transfers between devices, per_device(): lax.ppermute(turned[:, step * piece:(step + 1) * piece], ('ctx', 'chan'),...  25.6 us
    pallas_call x3, Pallas kernels, mixed_part(): pl.pallas_call(functools.partial(mixed_kernel, len(received)), grid_spec=...  21.3 us
    ppermute x14, waiting for transfers between devices, swap(): return lax.ppermute(block, axis, [(i, i ^ bit) for i in range(size)])  20 us
    pallas_call x3, Pallas kernels, by_channel(): pl.pallas_call(functools.partial(kernel, length), grid=(channels // width...  17.4 us
    ppermute x3, waiting for transfers between devices, per_device(): from_behind = lax.ppermute(from_behind, 'ctx', ahead)  12.2 us
    pallas_call x1, Pallas kernels, grad_weight_of(): pl.pallas_call(functools.partial(weight_kernel, slots, parts, half), grid...  8.84 us
    ppermute x14, starting transfers between devices, swap(): return lax.ppermute(block, axis, [(i, i ^ bit) for i in range(size)])  7.09 us
  transfers between devices with their start and end apart: 32, of which 8 were waited for; matrix products, arithmetic and copies ran while one was open for 5% of the time, Pallas kernels for 37%

profile of v1, /device:TPU:0, one launch (start us, length us, event | category | flops | bytes accessed | tf_op | source)
XLA Modules:
  0.0 185.4 jit_solution(8022299114073091767)
XLA Ops:
  1.1 2.6 %collective-permute-start.3 = (bf16[128,2048]{1,0:T(8,128)(2,1)}, bf16[128,2048]{1,0:T(8,128)(2,1)S(1)}, u32[]{:S(2)}, u32[]{:S(2)}) collective-permute-start(bf16[128,2048]{1,0:T(8,128)(2,1)} %cot_ref.1), channel_id=1, source_target_pairs={{0,2},{1,3},{2,0},{3,1},{4,6},{5,7},{6,4},{7,5},{8,10},{9,11},{10,... | collective-permute-start | bytes 1572872 | tf_op jit(solution)/shard_map/ppermute | solution.py:253
  5.7 4.8 %collective-permute-start.22 = (bf16[128,256]{1,0:T(8,128)(2,1)S(1)}, bf16[128,256]{1,0:T(8,128)(2,1)S(1)}, u32[]{:S(2)}, u32[]{:S(2)}) collective-permute-start(bf16[128,256]{1,0:T(8,128)(2,1)S(1)} %get-tuple-element.22), channel_id=1, source_target_pairs={{0,1},{1,9},{2,17},{3,25},{4,2},{5,10},{6,18},{7,26},{8,3},{9,11},... | collective-permute-start | bytes 196616 | tf_op jit(solution)/shard_map/ppermute | solution.py:307
  10.5 1.3 multiply_convert_fusion.2
  11.9 5.8 %collective-permute-start = (bf16[128,2048]{1,0:T(8,128)(2,1)S(1)}, bf16[128,2048]{1,0:T(8,128)(2,1)S(1)}, u32[]{:S(2)}, u32[]{:S(2)}) collective-permute-start(bf16[128,2048]{1,0:T(8,128)(2,1)S(1)} %multiply_convert_fusion.2), channel_id=1, source_target_pairs={{0,4},{4,8},{8,12},{12,16},{16,20},{20,24},{24,28},{1,5},{5,9},{9,... | collective-permute-start | bytes 1572872 | tf_op jit(solution)/shard_map/ppermute | solution.py:293
  24.2 1.3 gather_fusion
  26.9 7.7 %grad_gated_part.4.refs_0_ = f32[128,2048]{1,0:T(8,128)S(1)} custom-call(s32[1]{0:T(128)} %bitcast.6.ids_ref, bf16[128,2048]{1,0:T(8,128)(2,1)S(1)} %copy-done, bf16[2048,8192]{1,0:T(8,128)(2,1)} %w_ref.13), custom_call_target="tpu_custom_call" | custom-call | flops 1073741824 | bytes 8388608 | tf_op jit(solution)/shard_map/grad_gated_part/pallas_call | solution.py:130
  34.6 3.5 %collective-permute-start.23 = (bf16[128,256]{1,0:T(8,128)(2,1)S(1)}, bf16[128,256]{1,0:T(8,128)(2,1)S(1)}, u32[]{:S(2)}, u32[]{:S(2)}) collective-permute-start(bf16[128,256]{1,0:T(8,128)(2,1)S(1)} %get-tuple-element.21), channel_id=1, source_target_pairs={{0,2},{1,10},{2,18},{3,26},{4,3},{5,11},{6,19},{7,27},{8,4},{9,12}... | collective-permute-start | bytes 196616 | tf_op jit(solution)/shard_map/ppermute | solution.py:307
  38.1 2.8 %collective-permute-start.24 = (bf16[128,256]{1,0:T(8,128)(2,1)S(1)}, bf16[128,256]{1,0:T(8,128)(2,1)S(1)}, u32[]{:S(2)}, u32[]{:S(2)}) collective-permute-start(bf16[128,256]{1,0:T(8,128)(2,1)S(1)} %get-tuple-element.20), channel_id=1, source_target_pairs={{0,3},{1,11},{2,19},{3,27},{4,4},{5,12},{6,20},{7,28},{8,5},{9,13}... | collective-permute-start | bytes 196616 | tf_op jit(solution)/shard_map/ppermute | solution.py:307
  41.1 7.8 %grad_gated_part.5.refs_0_ = f32[128,2048]{1,0:T(8,128)S(1)} custom-call(s32[1]{0:T(128)} %bitcast.1.ids_ref, bf16[128,2048]{1,0:T(8,128)(2,1)S(1)} %collective-permute-done.5.cot_ref, bf16[2048,8192]{1,0:T(8,128)(2,1)} %w_ref.13, f32[128,2048]{1,0:T(8,128)S(1)} %grad_gated_part.4.refs_0_), custom_call_target="tpu_custom_call" | custom-call | flops 1073741824 | bytes 8388608 | tf_op jit(solution)/shard_map/grad_gated_part/pallas_call | solution.py:130
  48.9 3.6 %collective-permute-start.26 = (bf16[128,256]{1,0:T(8,128)(2,1)S(1)}, bf16[128,256]{1,0:T(8,128)(2,1)S(1)}, u32[]{:S(2)}, u32[]{:S(2)}) collective-permute-start(bf16[128,256]{1,0:T(8,128)(2,1)S(1)} %get-tuple-element.18), channel_id=1, source_target_pairs={{0,5},{1,13},{2,21},{3,29},{4,6},{5,14},{6,22},{7,30},{8,7},{9,15}... | collective-permute-start | bytes 196616 | tf_op jit(solution)/shard_map/ppermute | solution.py:307
  52.5 7.7 %grad_gated_part.6.refs_0_ = f32[128,2048]{1,0:T(8,128)S(1)} custom-call(s32[1]{0:T(128)} %bitcast.5.ids_ref, bf16[128,2048]{1,0:T(8,128)(2,1)S(1)} %collective-permute-done.3.cot_ref, bf16[2048,8192]{1,0:T(8,128)(2,1)} %w_ref.13, f32[128,2048]{1,0:T(8,128)S(1)} %grad_gated_part.5.refs_0_), custom_call_target="tpu_custom_call" | custom-call | flops 1073741824 | bytes 8388608 | tf_op jit(solution)/shard_map/grad_gated_part/pallas_call | solution.py:130
  60.4 5.6 %forward_filter.1 = (bf16[128,2048]{1,0:T(8,128)(2,1)S(1)}, f32[128,2048]{1,0:T(8,128)S(1)}) custom-call(bf16[128,2048]{1,0:T(8,128)(2,1)S(1)} %copy-done.1, bf16[128,2048]{1,0:T(8,128)(2,1)S(1)} %copy-done.2, bf16[128,2048]{1,0:T(8,128)(2,1)S(1)} %copy-done.3, bf16[128,2048]{1,0:T(8,128)(2,1)S(1)} %collective-permute-done.earlier_ref, ...), custom_call_target="tpu_custom_call" | custom-call | flops 6000000000 | bytes 3014656 | tf_op jit(solution)/shard_map/forward_filter/pallas_call | solution.py:96
  66.0 8.3 %collective-permute-start.27 = (bf16[128,256]{1,0:T(8,128)(2,1)S(1)}, bf16[128,256]{1,0:T(8,128)(2,1)S(1)}, u32[]{:S(2)}, u32[]{:S(2)}) collective-permute-start(bf16[128,256]{1,0:T(8,128)(2,1)S(1)} %get-tuple-element.17), channel_id=1, source_target_pairs={{0,6},{1,14},{2,22},{3,30},{4,7},{5,15},{6,23},{7,31},{8,0},{9,8},... | collective-permute-start | bytes 196616 | tf_op jit(solution)/shard_map/ppermute | solution.py:307
  74.2 7.7 %grad_gated_part.7 = f32[128,2048]{1,0:T(8,128)S(1)} custom-call(s32[1]{0:T(128)} %bitcast.2.ids_ref, bf16[128,2048]{1,0:T(8,128)(2,1)S(1)} %collective-permute-done.4.cot_ref, bf16[2048,8192]{1,0:T(8,128)(2,1)} %w_ref.13, f32[128,2048]{1,0:T(8,128)S(1)} %grad_gated_part.6.refs_0_), custom_call_target="tpu_custom_call" | custom-call | flops 1073741824 | bytes 8388608 | tf_op jit(solution)/shard_map/grad_gated_part/pallas_call | solution.py:130
  82.9 5.7 %tap_grad.1 = bf16[2048,128]{1,0:T(8,128)(2,1)S(1)} custom-call(bf16[128,2048]{1,0:T(8,128)(2,1)S(1)} %copy-done.2, bf16[128,2048]{1,0:T(8,128)(2,1)S(1)} %copy-done.3, bf16[128,2048]{1,0:T(8,128)(2,1)S(1)} %collective-permute-done.earlier_ref, bf16[128,2048]{1,0:T(8,128)(2,1)S(1)} %get-tuple-element.14.gf_ref, bf16[2,256,256]{2,1,0:T(8,128)(2,1)S(1)} %copy-done.5, ...), custom_call_target="tpu_custom_call" | custom-call | flops 6000000000 | bytes 2490368 | tf_op jit(solution)/shard_map/tap_grad/pallas_call | solution.py:96
  91.1 6.9 %collective-permute-done.7 = bf16[1024,128]{1,0:T(8,128)(2,1)S(1)} collective-permute-done((bf16[1024,128]{1,0:T(8,128)(2,1)S(1)}, bf16[1024,128]{1,0:T(8,128)(2,1)S(1)}, u32[]{:S(2)}, u32[]{:S(2)}) %collective-permute-start.7) | collective-permute-done | bytes 262176 | tf_op jit(solution)/shard_map/ppermute | solution.py:253
  98.8 10.1 %mixed_part.3 = bf16[128,4096]{1,0:T(8,128)(2,1)S(1)} custom-call(s32[1,2]{1,0:T(1,128)S(1)} %add_bitcast_fusion.ids_ref, bf16[128,2048]{1,0:T(8,128)(2,1)S(1)} %get-tuple-element.10.gated_ref.refs_0_, bf16[2048,8192]{1,0:T(8,128)(2,1)} %w_ref.13), custom_call_target="tpu_custom_call" | custom-call | flops 2147483648 | bytes 16777216 | tf_op jit(solution)/shard_map/mixed_part/pallas_call | solution.py:168
  109.3 6.6 %collective-permute-done.9 = bf16[256,128]{1,0:T(8,128)(2,1)S(1)} collective-permute-done((bf16[256,128]{1,0:T(8,128)(2,1)S(1)}, bf16[256,128]{1,0:T(8,128)(2,1)S(1)}, u32[]{:S(2)}, u32[]{:S(2)}) %collective-permute-start.9) | collective-permute-done | bytes 65568 | tf_op jit(solution)/shard_map/ppermute | solution.py:253
  115.9 1.9 %collective-permute-start.28 = (bf16[128,256]{1,0:T(8,128)(2,1)S(1)}, bf16[128,256]{1,0:T(8,128)(2,1)S(1)}, u32[]{:S(2)}, u32[]{:S(2)}) collective-permute-start(bf16[128,256]{1,0:T(8,128)(2,1)S(1)} %get-tuple-element.16), channel_id=1, source_target_pairs={{0,7},{1,15},{2,23},{3,31},{4,0},{5,8},{6,16},{7,24},{8,1},{9,9},{... | collective-permute-start | bytes 196616 | tf_op jit(solution)/shard_map/ppermute | solution.py:307
  119.4 4.7 %collective-permute-start.15 = (bf16[128,2048]{1,0:T(8,128)(2,1)S(1)}, bf16[128,2048]{1,0:T(8,128)(2,1)S(1)}, u32[]{:S(2)}, u32[]{:S(2)}) collective-permute-start(bf16[128,2048]{1,0:T(8,128)(2,1)S(1)} %collective-permute-done.13.refs_1_), channel_id=1, source_target_pairs={{0,8},{8,16},{16,24},{24,28},{28,20},{20,12},{12,4},{4,0},{1,9},{9... | collective-permute-start | bytes 1572872 | tf_op jit(solution)/shard_map/ppermute | solution.py:330
  125.1 1.5 collective-permute-start.16
  127.3 5.6 %mixed_part.5 = bf16[128,2048]{1,0:T(8,128)(2,1)S(1)} custom-call(s32[2,1]{1,0:T(2,128)S(1)} %pad_add_fusion.2.ids_ref, bf16[128,2048]{1,0:T(8,128)(2,1)S(1)} %get-tuple-element.10.gated_ref.refs_0_, bf16[2048,8192]{1,0:T(8,128)(2,1)} %w_ref.13, bf16[128,4096]{1,0:T(8,128)(2,1)S(1)} %collective-permute-done.1.refs_0_), custom_call_target="tpu_custom_call" | custom-call | flops 1073741824 | bytes 8388608 | tf_op jit(solution)/shard_map/mixed_part/pallas_call | solution.py:168
  132.9 12.2 %collective-permute-done.15.refs_3_ = bf16[128,2048]{1,0:T(8,128)(2,1)S(1)} collective-permute-done((bf16[128,2048]{1,0:T(8,128)(2,1)S(1)}, bf16[128,2048]{1,0:T(8,128)(2,1)S(1)}, u32[]{:S(2)}, u32[]{:S(2)}) %collective-permute-start.15) | collective-permute-done | bytes 524320 | tf_op jit(solution)/shard_map/ppermute | solution.py:330
  145.1 1.4 collective-permute-start.2
  146.6 1.6 collective-permute-done.16.refs_4_
  148.2 1.6 collective-permute-done.11
  150.5 6.0 %backward_filter.1 = (bf16[128,2048]{1,0:T(8,128)(2,1)}, bf16[128,2048]{1,0:T(8,128)(2,1)}) custom-call(bf16[128,2048]{1,0:T(8,128)(2,1)S(1)} %copy-done.2, bf16[128,2048]{1,0:T(8,128)(2,1)S(1)} %copy-done.3, bf16[128,2048]{1,0:T(8,128)(2,1)S(1)} %get-tuple-element.14.gf_ref, bf16[128,2048]{1,0:T(8,128)(2,1)S(1)} %collective-permute-done.6.following_ref, ...), custom_call_target="tpu_custom_call" | custom-call | flops 6000000000 | bytes 3014656 | tf_op jit(solution)/shard_map/backward_filter/pallas_call | solution.py:96
  156.6 5.6 %mixed_part.4 = f32[128,2048]{1,0:T(8,128)S(1)} custom-call(s32[2,1]{1,0:T(2,128)S(1)} %pad_add_fusion.1.ids_ref, bf16[128,2048]{1,0:T(8,128)(2,1)S(1)} %get-tuple-element.10.gated_ref.refs_0_, bf16[2048,8192]{1,0:T(8,128)(2,1)} %w_ref.13, bf16[128,4096]{1,0:T(8,128)(2,1)S(1)} %collective-permute-done.1.refs_0_), custom_call_target="tpu_custom_call" | custom-call | flops 1073741824 | bytes 8388608 | tf_op jit(solution)/shard_map/mixed_part/pallas_call | solution.py:168
  162.3 4.0 %collective-permute-done.12 = bf16[1024,128]{1,0:T(8,128)(2,1)S(1)} collective-permute-done((bf16[1024,128]{1,0:T(8,128)(2,1)S(1)}, bf16[1024,128]{1,0:T(8,128)(2,1)S(1)}, u32[]{:S(2)}, u32[]{:S(2)}) %collective-permute-start.12) | collective-permute-done | bytes 262176 | tf_op jit(solution)/shard_map/ppermute | solution.py:253
  167.5 2.1 %collective-permute-start.20 = (bf16[128,1024]{1,0:T(8,128)(2,1)S(1)}, bf16[128,1024]{1,0:T(8,128)(2,1)S(1)}, u32[]{:S(2)}, u32[]{:S(2)}) collective-permute-start(bf16[128,1024]{1,0:T(8,128)(2,1)S(1)} %slice.79), channel_id=1, source_target_pairs={{8,0},{16,8},{24,16},{28,24},{20,28},{12,20},{4,12},{0,4},{9,1},{1... | collective-permute-start | bytes 786440 | tf_op jit(solution)/shard_map/ppermute | solution.py:334
  170.6 5.9 %collective-permute-done.19.refs_7_ = bf16[128,1024]{1,0:T(8,128)(2,1)S(1)} collective-permute-done((bf16[128,1024]{1,0:T(8,128)(2,1)S(1)}, bf16[128,1024]{1,0:T(8,128)(2,1)S(1)}, u32[]{:S(2)}, u32[]{:S(2)}) %collective-permute-start.19) | collective-permute-done | bytes 262176 | tf_op jit(solution)/shard_map/ppermute | solution.py:333
  176.5 8.8 %grad_weight.1 = bf16[2048,1024]{1,0:T(8,128)(2,1)} custom-call(s32[4,9]{1,0:T(4,128)S(1)} %pad_add_fusion.ids_ref, bf16[128,2048]{1,0:T(8,128)(2,1)S(1)} %get-tuple-element.10.gated_ref.refs_0_, bf16[128,2048]{1,0:T(8,128)(2,1)S(1)} %collective-permute-done.13.refs_1_, bf16[128,2048]{1,0:T(8,128)(2,1)S(1)} %collective-permute-done.14.refs_2_, ...), custom_call_target="tpu_custom_call" | custom-call | flops 4294967296 | bytes 8388608 | tf_op jit(solution)/shard_map/grad_weight/pallas_call | solution.py:216
  (101 shorter events, 17.0 us)
Async XLA Ops:
  0.6 40.3 %collective-permute-start.5 = (bf16[128,2048]{1,0:T(8,128)(2,1)}, bf16[128,2048]{1,0:T(8,128)(2,1)S(1)}, u32[]{:S(2)}, u32[]{:S(2)}) collective-permute-start(bf16[128,2048]{1,0:T(8,128)(2,1)} %cot_ref.1), channel_id=1, source_target_pairs={{0,1},{1,0},{2,3},{3,2},{4,5},{5,4},{6,7},{7,6},{8,9},{9,8},{10,11... | collective-permute-start | bytes 1572872 | tf_op jit(solution)/shard_map/ppermute | solution.py:253
  1.1 47.8 %collective-permute-start.3 = (bf16[128,2048]{1,0:T(8,128)(2,1)}, bf16[128,2048]{1,0:T(8,128)(2,1)S(1)}, u32[]{:S(2)}, u32[]{:S(2)}) collective-permute-start(bf16[128,2048]{1,0:T(8,128)(2,1)} %cot_ref.1), channel_id=1, source_target_pairs={{0,2},{1,3},{2,0},{3,1},{4,6},{5,7},{6,4},{7,5},{8,10},{9,11},{10,... | collective-permute-start | bytes 1572872 | tf_op jit(solution)/shard_map/ppermute | solution.py:253
  5.0 29.6 %collective-permute-start.21 = (bf16[128,256]{1,0:T(8,128)(2,1)S(1)}, bf16[128,256]{1,0:T(8,128)(2,1)S(1)}, u32[]{:S(2)}, u32[]{:S(2)}) collective-permute-start(bf16[128,256]{1,0:T(8,128)(2,1)S(1)} %get-tuple-element.23), channel_id=1, source_target_pairs={{0,0},{1,8},{2,16},{3,24},{4,1},{5,9},{6,17},{7,25},{8,2},{9,10},{... | collective-permute-start | bytes 196616 | tf_op jit(solution)/shard_map/ppermute | solution.py:307
  5.7 32.4 %collective-permute-start.22 = (bf16[128,256]{1,0:T(8,128)(2,1)S(1)}, bf16[128,256]{1,0:T(8,128)(2,1)S(1)}, u32[]{:S(2)}, u32[]{:S(2)}) collective-permute-start(bf16[128,256]{1,0:T(8,128)(2,1)S(1)} %get-tuple-element.22), channel_id=1, source_target_pairs={{0,1},{1,9},{2,17},{3,25},{4,2},{5,10},{6,18},{7,26},{8,3},{9,11},... | collective-permute-start | bytes 196616 | tf_op jit(solution)/shard_map/ppermute | solution.py:307
  11.9 48.4 %collective-permute-start = (bf16[128,2048]{1,0:T(8,128)(2,1)S(1)}, bf16[128,2048]{1,0:T(8,128)(2,1)S(1)}, u32[]{:S(2)}, u32[]{:S(2)}) collective-permute-start(bf16[128,2048]{1,0:T(8,128)(2,1)S(1)} %multiply_convert_fusion.2), channel_id=1, source_target_pairs={{0,4},{4,8},{8,12},{12,16},{16,20},{20,24},{24,28},{1,5},{5,9},{9,... | collective-permute-start | bytes 1572872 | tf_op jit(solution)/shard_map/ppermute | solution.py:293
  34.6 54.1 %collective-permute-start.23 = (bf16[128,256]{1,0:T(8,128)(2,1)S(1)}, bf16[128,256]{1,0:T(8,128)(2,1)S(1)}, u32[]{:S(2)}, u32[]{:S(2)}) collective-permute-start(bf16[128,256]{1,0:T(8,128)(2,1)S(1)} %get-tuple-element.21), channel_id=1, source_target_pairs={{0,2},{1,10},{2,18},{3,26},{4,3},{5,11},{6,19},{7,27},{8,4},{9,12}... | collective-permute-start | bytes 196616 | tf_op jit(solution)/shard_map/ppermute | solution.py:307
  38.1 50.9 %collective-permute-start.24 = (bf16[128,256]{1,0:T(8,128)(2,1)S(1)}, bf16[128,256]{1,0:T(8,128)(2,1)S(1)}, u32[]{:S(2)}, u32[]{:S(2)}) collective-permute-start(bf16[128,256]{1,0:T(8,128)(2,1)S(1)} %get-tuple-element.20), channel_id=1, source_target_pairs={{0,3},{1,11},{2,19},{3,27},{4,4},{5,12},{6,20},{7,28},{8,5},{9,13}... | collective-permute-start | bytes 196616 | tf_op jit(solution)/shard_map/ppermute | solution.py:307
  41.0 47.9 %collective-permute-start.25 = (bf16[128,256]{1,0:T(8,128)(2,1)S(1)}, bf16[128,256]{1,0:T(8,128)(2,1)S(1)}, u32[]{:S(2)}, u32[]{:S(2)}) collective-permute-start(bf16[128,256]{1,0:T(8,128)(2,1)S(1)} %get-tuple-element.19), channel_id=1, source_target_pairs={{0,4},{1,12},{2,20},{3,28},{4,5},{5,13},{6,21},{7,29},{8,6},{9,14}... | collective-permute-start | bytes 196616 | tf_op jit(solution)/shard_map/ppermute | solution.py:307
  48.9 60.1 %collective-permute-start.26 = (bf16[128,256]{1,0:T(8,128)(2,1)S(1)}, bf16[128,256]{1,0:T(8,128)(2,1)S(1)}, u32[]{:S(2)}, u32[]{:S(2)}) collective-permute-start(bf16[128,256]{1,0:T(8,128)(2,1)S(1)} %get-tuple-element.18), channel_id=1, source_target_pairs={{0,5},{1,13},{2,21},{3,29},{4,6},{5,14},{6,22},{7,30},{8,7},{9,15}... | collective-permute-start | bytes 196616 | tf_op jit(solution)/shard_map/ppermute | solution.py:307
  60.2 5.7 %collective-permute-start.4 = (bf16[128,2048]{1,0:T(8,128)(2,1)S(1)}, bf16[128,2048]{1,0:T(8,128)(2,1)S(1)}, u32[]{:S(2)}, u32[]{:S(2)}) collective-permute-start(bf16[128,2048]{1,0:T(8,128)(2,1)S(1)} %collective-permute-done.3.cot_ref), channel_id=1, source_target_pairs={{0,1},{1,0},{2,3},{3,2},{4,5},{5,4},{6,7},{7,6},{8,9},{9,8},{10,11... | collective-permute-start | bytes 1572872 | tf_op jit(solution)/shard_map/ppermute | solution.py:253
  66.0 51.9 %collective-permute-start.27 = (bf16[128,256]{1,0:T(8,128)(2,1)S(1)}, bf16[128,256]{1,0:T(8,128)(2,1)S(1)}, u32[]{:S(2)}, u32[]{:S(2)}) collective-permute-start(bf16[128,256]{1,0:T(8,128)(2,1)S(1)} %get-tuple-element.17), channel_id=1, source_target_pairs={{0,6},{1,14},{2,22},{3,30},{4,7},{5,15},{6,23},{7,31},{8,0},{9,8},... | collective-permute-start | bytes 196616 | tf_op jit(solution)/shard_map/ppermute | solution.py:307
  88.7 9.3 %collective-permute-start.7 = (bf16[1024,128]{1,0:T(8,128)(2,1)S(1)}, bf16[1024,128]{1,0:T(8,128)(2,1)S(1)}, u32[]{:S(2)}, u32[]{:S(2)}) collective-permute-start(bf16[1024,128]{1,0:T(8,128)(2,1)S(1)} %broadcast_select_fusion.2), channel_id=1, source_target_pairs={{0,4},{4,0},{8,12},{12,8},{16,20},{20,16},{24,28},{28,24},{1,5},{5... | collective-permute-start | bytes 786440 | tf_op jit(solution)/shard_map/ppermute | solution.py:253
  89.0 29.1 %collective-permute-start.13 = (bf16[128,2048]{1,0:T(8,128)(2,1)S(1)}, bf16[128,2048]{1,0:T(8,128)(2,1)S(1)}, u32[]{:S(2)}, u32[]{:S(2)}) collective-permute-start(bf16[128,2048]{1,0:T(8,128)(2,1)S(1)} %get-tuple-element.10.gated_ref.refs_0_), channel_id=1, source_target_pairs={{0,8},{8,16},{16,24},{24,28},{28,20},{20,12},{12,4},{4,0},{1,9},{9... | collective-permute-start | bytes 1572872 | tf_op jit(solution)/shard_map/ppermute | solution.py:330
  90.0 29.4 %collective-permute-start.14 = (bf16[128,2048]{1,0:T(8,128)(2,1)S(1)}, bf16[128,2048]{1,0:T(8,128)(2,1)S(1)}, u32[]{:S(2)}, u32[]{:S(2)}) collective-permute-start(bf16[128,2048]{1,0:T(8,128)(2,1)S(1)} %get-tuple-element.10.gated_ref.refs_0_), channel_id=1, source_target_pairs={{8,0},{16,8},{24,16},{28,24},{20,28},{12,20},{4,12},{0,4},{9,1},{1... | collective-permute-start | bytes 1572872 | tf_op jit(solution)/shard_map/ppermute | solution.py:331
  98.1 10.7 %collective-permute-start.8 = (bf16[512,128]{1,0:T(8,128)(2,1)S(1)}, bf16[512,128]{1,0:T(8,128)(2,1)S(1)}, u32[]{:S(2)}, u32[]{:S(2)}) collective-permute-start(bf16[512,128]{1,0:T(8,128)(2,1)S(1)} %broadcast_select_fusion.5), channel_id=1, source_target_pairs={{0,8},{4,12},{8,0},{12,4},{16,24},{20,28},{24,16},{28,20},{1,9},{5... | collective-permute-start | bytes 393224 | tf_op jit(solution)/shard_map/ppermute | solution.py:253
  108.9 18.3 %collective-permute-start.1 = (bf16[128,4096]{1,0:T(8,128)(2,1)S(1)}, bf16[128,4096]{1,0:T(8,128)(2,1)S(1)}, u32[]{:S(2)}, u32[]{:S(2)}) collective-permute-start(bf16[128,4096]{1,0:T(8,128)(2,1)S(1)} %mixed_part.3), channel_id=1, source_target_pairs={{0,1},{1,0},{2,3},{3,2},{4,5},{5,4},{6,7},{7,6},{8,9},{9,8},{10,11... | collective-permute-start | bytes 3145736 | tf_op jit(solution)/shard_map/ppermute | solution.py:253
  109.1 6.9 %collective-permute-start.9 = (bf16[256,128]{1,0:T(8,128)(2,1)S(1)}, bf16[256,128]{1,0:T(8,128)(2,1)S(1)}, u32[]{:S(2)}, u32[]{:S(2)}) collective-permute-start(bf16[256,128]{1,0:T(8,128)(2,1)S(1)} %broadcast_select_fusion.8), channel_id=1, source_target_pairs={{0,16},{4,20},{8,24},{12,28},{16,0},{20,4},{24,8},{28,12},{1,17},{... | collective-permute-start | bytes 196616 | tf_op jit(solution)/shard_map/ppermute | solution.py:253
  115.9 10.7 %collective-permute-start.28 = (bf16[128,256]{1,0:T(8,128)(2,1)S(1)}, bf16[128,256]{1,0:T(8,128)(2,1)S(1)}, u32[]{:S(2)}, u32[]{:S(2)}) collective-permute-start(bf16[128,256]{1,0:T(8,128)(2,1)S(1)} %get-tuple-element.16), channel_id=1, source_target_pairs={{0,7},{1,15},{2,23},{3,31},{4,0},{5,8},{6,16},{7,24},{8,1},{9,9},{... | collective-permute-start | bytes 196616 | tf_op jit(solution)/shard_map/ppermute | solution.py:307
  117.9 7.2 %collective-permute-start.10 = (bf16[256,128]{1,0:T(8,128)(2,1)S(1)}, bf16[256,128]{1,0:T(8,128)(2,1)S(1)}, u32[]{:S(2)}, u32[]{:S(2)}) collective-permute-start(bf16[256,128]{1,0:T(8,128)(2,1)S(1)} %add_convert_fusion.3), channel_id=1, source_target_pairs={{0,16},{4,20},{8,24},{12,28},{16,0},{20,4},{24,8},{28,12},{1,17},{... | collective-permute-start | bytes 196616 | tf_op jit(solution)/shard_map/ppermute | solution.py:253
  118.1 32.2 %collective-permute-start.6 = (bf16[128,2048]{1,0:T(8,128)(2,1)S(1)}, bf16[128,2048]{1,0:T(8,128)(2,1)S(1)}, u32[]{:S(2)}, u32[]{:S(2)}) collective-permute-start(bf16[128,2048]{1,0:T(8,128)(2,1)S(1)} %get-tuple-element.14.gf_ref), channel_id=1, source_target_pairs={{4,0},{8,4},{12,8},{16,12},{20,16},{24,20},{28,24},{5,1},{9,5},{13... | collective-permute-start | bytes 1572872 | tf_op jit(solution)/shard_map/ppermute | solution.py:338
  119.4 25.7 %collective-permute-start.15 = (bf16[128,2048]{1,0:T(8,128)(2,1)S(1)}, bf16[128,2048]{1,0:T(8,128)(2,1)S(1)}, u32[]{:S(2)}, u32[]{:S(2)}) collective-permute-start(bf16[128,2048]{1,0:T(8,128)(2,1)S(1)} %collective-permute-done.13.refs_1_), channel_id=1, source_target_pairs={{0,8},{8,16},{16,24},{24,28},{28,20},{20,12},{12,4},{4,0},{1,9},{9... | collective-permute-start | bytes 1572872 | tf_op jit(solution)/shard_map/ppermute | solution.py:330
  125.1 23.1 %collective-permute-start.16 = (bf16[128,2048]{1,0:T(8,128)(2,1)S(1)}, bf16[128,2048]{1,0:T(8,128)(2,1)S(1)}, u32[]{:S(2)}, u32[]{:S(2)}) collective-permute-start(bf16[128,2048]{1,0:T(8,128)(2,1)S(1)} %collective-permute-done.14.refs_2_), channel_id=1, source_target_pairs={{8,0},{16,8},{24,16},{28,24},{20,28},{12,20},{4,12},{0,4},{9,1},{1... | collective-permute-start | bytes 1572872 | tf_op jit(solution)/shard_map/ppermute | solution.py:331
  126.6 23.2 %collective-permute-start.11 = (bf16[512,128]{1,0:T(8,128)(2,1)S(1)}, bf16[512,128]{1,0:T(8,128)(2,1)S(1)}, u32[]{:S(2)}, u32[]{:S(2)}) collective-permute-start(bf16[512,128]{1,0:T(8,128)(2,1)S(1)} %pad_maximum_fusion.1), channel_id=1, source_target_pairs={{0,8},{4,12},{8,0},{12,4},{16,24},{20,28},{24,16},{28,20},{1,9},{5... | collective-permute-start | bytes 393224 | tf_op jit(solution)/shard_map/ppermute | solution.py:253
  127.2 35.0 %collective-permute-start.30 = (bf16[1024,256]{1,0:T(8,128)(2,1)S(1)}, bf16[1024,256]{1,0:T(8,128)(2,1)S(1)}, u32[]{:S(2)}, u32[]{:S(2)}) collective-permute-start(bf16[1024,256]{1,0:T(8,128)(2,1)S(1)} %constant_dynamic-update-slice_fusion.refs_9_), channel_id=1, source_target_pairs={{0,2},{1,3},{2,0},{3,1},{4,6},{5,7},{6,4},{7,5},{8,10},{9,11},{10,... | collective-permute-start | bytes 1572872 | tf_op jit(solution)/shard_map/ppermute | solution.py:253
  145.1 24.5 %collective-permute-start.2 = (bf16[128,2048]{1,0:T(8,128)(2,1)S(1)}, bf16[128,2048]{1,0:T(8,128)(2,1)S(1)}, u32[]{:S(2)}, u32[]{:S(2)}) collective-permute-start(bf16[128,2048]{1,0:T(8,128)(2,1)S(1)} %mixed_part.5), channel_id=1, source_target_pairs={{0,2},{1,3},{2,0},{3,1},{4,6},{5,7},{6,4},{7,5},{8,10},{9,11},{10,... | collective-permute-start | bytes 1572872 | tf_op jit(solution)/shard_map/ppermute | solution.py:253
  148.2 19.2 %collective-permute-start.17 = (bf16[128,2048]{1,0:T(8,128)(2,1)S(1)}, bf16[128,2048]{1,0:T(8,128)(2,1)S(1)}, u32[]{:S(2)}, u32[]{:S(2)}) collective-permute-start(bf16[128,2048]{1,0:T(8,128)(2,1)S(1)} %collective-permute-done.15.refs_3_), channel_id=1, source_target_pairs={{0,8},{8,16},{16,24},{24,28},{28,20},{20,12},{12,4},{4,0},{1,9},{9... | collective-permute-start | bytes 1572872 | tf_op jit(solution)/shard_map/ppermute | solution.py:330
  149.7 17.8 %collective-permute-start.18 = (bf16[128,2048]{1,0:T(8,128)(2,1)S(1)}, bf16[128,2048]{1,0:T(8,128)(2,1)S(1)}, u32[]{:S(2)}, u32[]{:S(2)}) collective-permute-start(bf16[128,2048]{1,0:T(8,128)(2,1)S(1)} %collective-permute-done.16.refs_4_), channel_id=1, source_target_pairs={{8,0},{16,8},{24,16},{28,24},{20,28},{12,20},{4,12},{0,4},{9,1},{1... | collective-permute-start | bytes 1572872 | tf_op jit(solution)/shard_map/ppermute | solution.py:331
  150.3 16.0 %collective-permute-start.12 = (bf16[1024,128]{1,0:T(8,128)(2,1)S(1)}, bf16[1024,128]{1,0:T(8,128)(2,1)S(1)}, u32[]{:S(2)}, u32[]{:S(2)}) collective-permute-start(bf16[1024,128]{1,0:T(8,128)(2,1)S(1)} %pad_maximum_fusion), channel_id=1, source_target_pairs={{0,4},{4,0},{8,12},{12,8},{16,20},{20,16},{24,28},{28,24},{1,5},{5... | collective-permute-start | bytes 786440 | tf_op jit(solution)/shard_map/ppermute | solution.py:253
  162.2 8.4 %collective-permute-start.29 = (bf16[1024,256]{1,0:T(8,128)(2,1)S(1)}, bf16[1024,256]{1,0:T(8,128)(2,1)S(1)}, u32[]{:S(2)}, u32[]{:S(2)}) collective-permute-start(bf16[1024,256]{1,0:T(8,128)(2,1)S(1)} %constant_dynamic-update-slice_fusion.refs_9_), channel_id=1, source_target_pairs={{0,1},{1,0},{2,3},{3,2},{4,5},{5,4},{6,7},{7,6},{8,9},{9,8},{10,11... | collective-permute-start | bytes 1572872 | tf_op jit(solution)/shard_map/ppermute | solution.py:253
  166.2 4.4 %collective-permute-start.31 = (bf16[1024,256]{1,0:T(8,128)(2,1)S(1)}, bf16[1024,256]{1,0:T(8,128)(2,1)S(1)}, u32[]{:S(2)}, u32[]{:S(2)}) collective-permute-start(bf16[1024,256]{1,0:T(8,128)(2,1)S(1)} %collective-permute-done.30.refs_11_), channel_id=1, source_target_pairs={{0,1},{1,0},{2,3},{3,2},{4,5},{5,4},{6,7},{7,6},{8,9},{9,8},{10,11... | collective-permute-start | bytes 1572872 | tf_op jit(solution)/shard_map/ppermute | solution.py:253
  167.4 9.1 %collective-permute-start.19 = (bf16[128,1024]{1,0:T(8,128)(2,1)S(1)}, bf16[128,1024]{1,0:T(8,128)(2,1)S(1)}, u32[]{:S(2)}, u32[]{:S(2)}) collective-permute-start(bf16[128,1024]{1,0:T(8,128)(2,1)S(1)} %slice.78), channel_id=1, source_target_pairs={{0,8},{8,16},{16,24},{24,28},{28,20},{20,12},{12,4},{4,0},{1,9},{9... | collective-permute-start | bytes 786440 | tf_op jit(solution)/shard_map/ppermute | solution.py:333
  167.5 9.0 %collective-permute-start.20 = (bf16[128,1024]{1,0:T(8,128)(2,1)S(1)}, bf16[128,1024]{1,0:T(8,128)(2,1)S(1)}, u32[]{:S(2)}, u32[]{:S(2)}) collective-permute-start(bf16[128,1024]{1,0:T(8,128)(2,1)S(1)} %slice.79), channel_id=1, source_target_pairs={{8,0},{16,8},{24,16},{28,24},{20,28},{12,20},{4,12},{0,4},{9,1},{1... | collective-permute-start | bytes 786440 | tf_op jit(solution)/shard_map/ppermute | solution.py:334
  (9 other events, 192.2 us)

commit v2 on v1

v2 whole, which is shorter than its diff:
```python
import functools

import jax
import jax.numpy as jnp
import numpy as np
from jax import lax
from jax.experimental import pallas as pl
from jax.experimental.pallas import tpu as pltpu
from jax.sharding import PartitionSpec as P

F32 = jnp.float32
BF16 = jnp.bfloat16
VMEM_BYTES = 40 * 2**20
NT = (((1,), (1,)), ((), ()))
TN = (((0,), (0,)), ((), ()))


def halves(matrix):
    high = matrix.astype(BF16)
    low = (matrix - high.astype(np.float64)).astype(BF16)
    return np.stack([high, low])


def transforms(taps):
    points = 2 * taps
    angle = np.pi * (2 * np.arange(taps)[:, None] + 1) * np.arange(points)[None, :] / points
    forward = np.concatenate([np.cos(angle), -np.sin(angle)], axis=0)
    inverse = forward.T * (2.0 / points)
    late = inverse[taps:]
    early = inverse[:taps]
    lags = inverse[taps - np.arange(taps)]
    return halves(forward), halves(late), halves(early), halves(lags)


def mm(a, b, dims=(((1,), (0,)), ((), ()))):
    return lax.dot_general(a, b, dims, preferred_element_type=F32)


def spectrum(f_ref, rows):
    return mm(f_ref[0], rows) + mm(f_ref[1], rows)


def tap_spectrum(f_ref, filters, taps):
    return mm(f_ref[0, :, :taps], filters, NT) + mm(f_ref[1, :, :taps], filters, NT)


def back(g_ref, real, imag):
    both = jnp.concatenate([real, imag], axis=0)
    high = both.astype(BF16)
    low = (both - high.astype(F32)).astype(BF16)
    return mm(g_ref[0], high) + mm(g_ref[0], low) + mm(g_ref[1], high)


def forward_kernel(taps, q_ref, k_ref, v_ref, earlier_ref, filt_ref, f_ref, g_ref, gated_ref, filtered_ref):
    product = (k_ref[...].astype(F32) * v_ref[...].astype(F32)).astype(BF16)
    x = spectrum(f_ref, jnp.concatenate([earlier_ref[...], product], axis=0))
    h = tap_spectrum(f_ref, filt_ref[...], taps)
    xr, xi, hr, hi = x[:taps], x[taps:], h[:taps], h[taps:]
    filtered = back(g_ref, xr * hr - xi * hi, xr * hi + xi * hr)
    filtered_ref[...] = filtered
    gated_ref[...] = (q_ref[...].astype(F32) * filtered).astype(BF16)


def tap_grad_kernel(taps, k_ref, v_ref, earlier_ref, gf_ref, f_ref, g_ref, out_ref):
    product = (k_ref[...].astype(F32) * v_ref[...].astype(F32)).astype(BF16)
    x = spectrum(f_ref, jnp.concatenate([earlier_ref[...], product], axis=0))
    rows = gf_ref[...]
    g = mm(f_ref[0, :, :taps], rows) + mm(f_ref[1, :, :taps], rows)
    xr, xi, gr, gi = x[:taps], x[taps:], g[:taps], g[taps:]
    tap_rows = back(g_ref, xr * gr + xi * gi, xi * gr - xr * gi)
    out_ref[...] = tap_rows.T.astype(BF16)


def backward_kernel(taps, k_ref, v_ref, gf_ref, following_ref, filt_ref, f_ref, g_ref, gk_ref, gv_ref):
    g = spectrum(f_ref, jnp.concatenate([gf_ref[...], following_ref[...]], axis=0))
    h = tap_spectrum(f_ref, filt_ref[...], taps)
    gr, gi, hr, hi = g[:taps], g[taps:], h[:taps], h[taps:]
    grad_product = back(g_ref, hr * gr + hi * gi, hr * gi - hi * gr)
    gk_ref[...] = (grad_product * v_ref[...].astype(F32)).astype(BF16)
    gv_ref[...] = (grad_product * k_ref[...].astype(F32)).astype(BF16)


def estimate(flops, bytes_accessed):
    return pl.CostEstimate(flops=flops, bytes_accessed=bytes_accessed, transcendentals=0)


def by_channel(kernel, arrays, kinds, outs, name, me=None):
    length, channels = arrays[0].shape
    width = min(512, channels) if me is None else 256
    specs = {
        "t": pl.BlockSpec((length, width), lambda i, *ids: (0, i)),
        "c": pl.BlockSpec((width, length), lambda i, *ids: (i, 0)),
        "x": pl.BlockSpec((width, length), lambda i, *ids: (i ^ ids[0][0], 0)),
    }

    def spec_of(kind, shape):
        if kind == "w":
            return pl.BlockSpec(shape, lambda i, *ids: (0,) * len(shape))
        return specs[kind]

    body = functools.partial(kernel, length)
    return pl.pallas_call(
        body if me is None else lambda ids_ref, *refs: body(*refs),
        grid_spec=pltpu.PrefetchScalarGridSpec(
            num_scalar_prefetch=0 if me is None else 1,
            grid=(channels // width,),
            in_specs=[spec_of(kind, a.shape) for kind, a in zip(kinds, arrays)],
            out_specs=[specs[kind] for kind, unused in outs],
        ),
        out_shape=[
            jax.ShapeDtypeStruct((length, channels) if kind == "t" else (channels, length), dtype)
            for kind, dtype in outs
        ],
        compiler_params=pltpu.CompilerParams(vmem_limit_bytes=VMEM_BYTES),
        cost_estimate=estimate(10**9, 4 * 2**20),
        name=name,
    )(*([] if me is None else [me]), *arrays)


def grad_gated_kernel(kind, me_ref, cot_ref, w_ref, *refs):
    total = mm(w_ref[...], cot_ref[...], NT).T
    if kind == "first":
        refs[-1][...] = total
        return
    total = total + refs[0][...]
    if kind == "middle":
        refs[-1][...] = total
        return
    q_ref, filtered_ref, gq_ref, gf_ref = refs[1:]
    gq_ref[...] = (total * filtered_ref[...]).astype(BF16)
    gf_ref[...] = (total * q_ref[...].astype(F32)).astype(BF16)


def grad_gated_part(kind, me, cot, weight, off, arrays):
    length, width = cot.shape
    channels = weight.shape[0]
    tile = 512
    row_spec = pl.BlockSpec((length, tile), lambda i, me: (0, i))
    kinds = [BF16, BF16] if kind == "last" else [F32]
    return pl.pallas_call(
        functools.partial(grad_gated_kernel, kind),
        grid_spec=pltpu.PrefetchScalarGridSpec(
            num_scalar_prefetch=1,
            grid=(channels // tile,),
            in_specs=[
                pl.BlockSpec((length, width), lambda i, me: (0, 0)),
                pl.BlockSpec((tile, width), lambda i, me: (i, me[1] ^ off)),
            ]
            + [row_spec] * len(arrays),
            out_specs=[row_spec] * len(kinds),
        ),
        out_shape=[jax.ShapeDtypeStruct((length, channels), dtype) for dtype in kinds],
        compiler_params=pltpu.CompilerParams(vmem_limit_bytes=VMEM_BYTES),
        cost_estimate=estimate(2 * length * width * channels, 2 * width * channels),
        name="grad_gated_" + kind,
    )(me, cot, weight, *arrays)


def mixed_kernel(adds, me_ref, gated_ref, w_ref, *refs):
    total = mm(gated_ref[...], w_ref[...])
    for ref in refs[:adds]:
        total = total + ref[...].astype(F32)
    refs[-1][...] = total.astype(refs[-1].dtype)


def mixed_part(me, gated, weight, offs, received, kind):
    length, channels = gated.shape
    tile = 512
    steps = channels // tile

    def column(b):
        return offs[0] + b * (offs[1] - offs[0] if len(offs) > 1 else 0)

    in_specs = [
        pl.BlockSpec((length, channels), lambda b, t, me: (0, 0)),
        pl.BlockSpec((channels, tile), lambda b, t, me: (0, (me[1] ^ column(b)) * steps + t)),
    ]
    for unused, (start, stride) in received:
        in_specs.append(
            pl.BlockSpec(
                (length, tile), lambda b, t, me, start=start, stride=stride: (0, (start + b * stride) * steps + t)
            )
        )
    return pl.pallas_call(
        functools.partial(mixed_kernel, len(received)),
        grid_spec=pltpu.PrefetchScalarGridSpec(
            num_scalar_prefetch=1,
            grid=(len(offs), steps),
            in_specs=in_specs,
            out_specs=pl.BlockSpec((length, tile), lambda b, t, me: (0, b * steps + t)),
        ),
        out_shape=jax.ShapeDtypeStruct((length, channels * len(offs)), kind),
        compiler_params=pltpu.CompilerParams(vmem_limit_bytes=VMEM_BYTES),
        cost_estimate=estimate(2 * length * channels * channels * len(offs), 2 * channels * channels * len(offs)),
        name="mixed_part",
    )(me, gated, weight, *[array for array, unused in received])


def pieces_kernel(per_chan, me_ref, *refs):
    out_ref = refs[-1]
    length, width = refs[0].shape
    span = width // per_chan
    count = len(refs) - 1
    piece = span // count
    for off in range(count):
        for part in range(per_chan):
            target = (me_ref[1] ^ off) * per_chan + part
            start = pl.multiple_of(part * span + me_ref[1] * piece, 128)
            block = refs[off][:, pl.ds(start, piece)]
            out_ref[target ^ me_ref[0]] = jnp.concatenate(
                [block[:, at : at + 128] for at in range(0, piece, 128)], axis=0
            )


def pieces_of(me, cots, n_ctx):
    length, width = cots[0].shape
    piece = width // n_ctx
    rows = length * piece // 128
    if piece % 128:
        return pieces_by_slices(me, cots, n_ctx)
    return pl.pallas_call(
        functools.partial(pieces_kernel, n_ctx // len(cots)),
        grid_spec=pltpu.PrefetchScalarGridSpec(
            num_scalar_prefetch=1,
            grid=(1,),
            in_specs=[pl.BlockSpec((length, width), lambda i, me: (0, 0))] * len(cots),
            out_specs=pl.BlockSpec((n_ctx, rows, 128), lambda i, me: (0, 0, 0)),
        ),
        out_shape=jax.ShapeDtypeStruct((n_ctx, rows, 128), BF16),
        compiler_params=pltpu.CompilerParams(vmem_limit_bytes=VMEM_BYTES),
        cost_estimate=estimate(10**6, 2**20),
        name="pieces",
    )(me, *cots)


def pieces_by_slices(me, cots, n_ctx):
    length, width = cots[0].shape
    count = len(cots)
    piece = width // n_ctx
    table = jnp.stack(cots).reshape(count, length, n_ctx // count, count, piece)
    mine = lax.dynamic_index_in_dim(table, me[1], 3, False)
    parts = mine.transpose(0, 2, 1, 3).reshape(n_ctx, length * piece // 128, 128)
    order = jnp.arange(n_ctx, dtype=jnp.int32) ^ me[0]
    per_chan = n_ctx // count
    return parts[(order // per_chan ^ me[1]) * per_chan + order % per_chan]


def weight_kernel(slots, parts, half, me_ref, owner_ref, *refs):
    gated_refs = refs[: slots - 1]
    far_low, far_high = refs[slots - 1 : slots + 1]
    cot_refs = refs[slots + 1 : slots + 1 + parts]
    out_ref = refs[-1]
    length = far_low.shape[0]
    far = jnp.where(pl.program_id(0) < half, far_low[...], far_high[...])
    columns = jnp.concatenate([ref[...] for ref in gated_refs] + [far], axis=0)
    for part in range(parts):
        rows = []
        for slot in range(slots):
            block = cot_refs[part][owner_ref[me_ref[0], slot]]
            rows.append(
                jnp.concatenate([block[at : at + length] for at in range(0, block.shape[0], length)], axis=1)
            )
        total = mm(columns, jnp.concatenate(rows, axis=0), TN)
        piece = total.shape[1]
        place = pl.multiple_of((me_ref[1] ^ part) * piece, piece) if parts > 1 else 0
        out_ref[:, pl.ds(place, piece)] = total.astype(BF16)


def grad_weight_of(me, owners, blocks, far_low, far_high, cots):
    length, channels = blocks[0].shape
    rows = cots[0].shape[1]
    piece = rows * 128 // length
    tile = 256
    half = channels // tile // 2
    slots, parts = len(blocks) + 1, len(cots)
    in_specs = [pl.BlockSpec((length, tile), lambda i, *ids: (0, i)) for unused in blocks]
    in_specs.append(pl.BlockSpec((length, tile), lambda i, *ids: (0, jnp.minimum(i, half - 1))))
    in_specs.append(pl.BlockSpec((length, tile), lambda i, *ids: (0, jnp.maximum(i - half, 0))))
    in_specs += [pl.BlockSpec(cot.shape, lambda i, *ids: (0, 0, 0)) for cot in cots]
    return pl.pallas_call(
        functools.partial(weight_kernel, slots, parts, half),
        grid_spec=pltpu.PrefetchScalarGridSpec(
            num_scalar_prefetch=2,
            grid=(channels // tile,),
            in_specs=in_specs,
            out_specs=pl.BlockSpec((tile, piece * parts), lambda i, *ids: (i, 0)),
        ),
        out_shape=jax.ShapeDtypeStruct((channels, piece * parts), BF16),
        compiler_params=pltpu.CompilerParams(vmem_limit_bytes=VMEM_BYTES),
        cost_estimate=estimate(2 * slots * length * channels * piece * parts, 12 * 2**20),
        name="grad_weight",
    )(me, owners, *blocks, far_low, far_high, *cots)


def place_kernel(me_ref, in_ref, out_ref):
    out_ref[...] = in_ref[...].astype(out_ref.dtype)


def placed_blocks(me, blocks):
    count, rows, width = blocks.shape
    return pl.pallas_call(
        place_kernel,
        grid_spec=pltpu.PrefetchScalarGridSpec(
            num_scalar_prefetch=1,
            grid=(count,),
            in_specs=[pl.BlockSpec((None, rows, width), lambda i, me: (i ^ me[0], 0, 0))],
            out_specs=pl.BlockSpec((rows, width), lambda i, me: (i, 0)),
        ),
        out_shape=jax.ShapeDtypeStruct((count * rows, width), F32),
        compiler_params=pltpu.CompilerParams(vmem_limit_bytes=VMEM_BYTES),
        cost_estimate=estimate(10**6, 2 * 2**20),
        name="placed_blocks",
    )(me, blocks)


def in_one_piece(me, columns, length):
    count, rows, unused = columns[0].shape
    table = jnp.stack(columns)[jnp.arange(len(columns), dtype=jnp.int32) ^ me[1]]
    piece = rows * 128 // length
    flat = table.reshape(len(columns), count, length, piece).transpose(1, 2, 0, 3)
    flat = flat.reshape(count, length, piece * len(columns) // 128, 128).transpose(0, 2, 1, 3)
    return [flat.reshape(count, -1, 128)]


def cycle_of(count):
    across = 1 << ((count.bit_length() - 1) // 2)
    order = []
    for column in range(across):
        line = [row * across + column for row in range(count // across)]
        order += line if column % 2 == 0 else line[::-1]
    return order


def swap(block, axis, bit):
    size = lax.axis_size(axis)
    return lax.ppermute(block, axis, [(i, i ^ bit) for i in range(size)])


def bits_of(size):
    return [1 << place for place in range(size.bit_length() - 1)]


def gather_by_swaps(block):
    held = {0: block}
    for bit in reversed(bits_of(lax.axis_size("chan"))):
        held.update({off ^ bit: swap(held[off], "chan", bit) for off in list(held)})
    return held


def sum_and_exchange(partial, pieces):
    count = pieces.shape[0]
    sums, held, sources = partial, pieces[None], [0]
    for bit in bits_of(count):
        give = held[:, 1::2].reshape((-1,) + pieces.shape[1:])
        if partial.shape[1:] == pieces.shape[1:]:
            came = swap(jnp.concatenate([sums[1::2], give], axis=0), "ctx", bit)
            others, came = came[: sums.shape[0] // 2], came[sums.shape[0] // 2 :]
        else:
            others, came = swap(sums[1::2], "ctx", bit), swap(give, "ctx", bit)
        sums = (sums[::2].astype(F32) + others.astype(F32)).astype(BF16)
        held = jnp.concatenate([held[:, ::2], came.reshape((len(sources), -1) + pieces.shape[1:])], axis=0)
        sources += [source ^ bit for source in sources]
    return sums, held[:, 0], sources


def doubled(block, axis):
    held = block
    for bit in reversed(bits_of(lax.axis_size(axis))):
        held = jnp.stack([held, swap(held, axis, bit)], axis=1).reshape((-1,) + block.shape[1:])
    return held


def per_device(query_proj, key_proj, value_proj, filters, out_weight, cotangent):
    length, channels = query_proj.shape
    taps = filters.shape[1]
    n_ctx, n_chan = lax.axis_size("ctx"), lax.axis_size("chan")
    me = jnp.stack([lax.axis_index("ctx"), lax.axis_index("chan")]).astype(jnp.int32)
    forward, late, early, lags = [jnp.asarray(m) for m in transforms(taps)]

    product = (key_proj.astype(F32) * value_proj.astype(F32)).astype(BF16)
    earlier = lax.ppermute(product, "ctx", [(i, i + 1) for i in range(n_ctx - 1)])

    cots = gather_by_swaps(cotangent)
    grad_gated = []
    for off in range(n_chan - 1):
        grad_gated = grad_gated_part("middle" if off else "first", me, cots[off], out_weight, off, grad_gated)
        grad_gated = list(grad_gated)

    gated, filtered = by_channel(
        forward_kernel,
        [query_proj, key_proj, value_proj, earlier, filters, forward, late],
        "ttttcww",
        [("t", BF16), ("t", F32)],
        "forward_filter",
    )

    order = cycle_of(n_ctx)
    ahead = [(order[i], order[(i + 1) % n_ctx]) for i in range(n_ctx)]
    behind = [(b, a) for a, b in ahead]
    half = channels // 2
    from_behind, from_ahead = gated, gated
    blocks = [gated]
    for step in range(n_ctx // 2 - 1):
        from_behind = lax.ppermute(from_behind, "ctx", ahead)
        from_ahead = lax.ppermute(from_ahead, "ctx", behind)
        blocks += [from_behind, from_ahead]
    far_low = lax.ppermute(from_behind[:, :half], "ctx", ahead)
    far_high = lax.ppermute(from_ahead[:, half:], "ctx", behind)

    grad_query, grad_filtered = grad_gated_part(
        "last", me, cots[n_chan - 1], out_weight, n_chan - 1, grad_gated + [query_proj, filtered]
    )
    following = lax.ppermute(grad_filtered, "ctx", [(i + 1, i) for i in range(n_ctx - 1)])

    received = []
    left = list(range(n_chan))
    for bit in bits_of(n_chan):
        give = left[1::2]
        left = left[::2]
        stride = give[1] - give[0] if len(give) > 1 else 1
        sums = [(array, ((give[0] - offs[0]) // step, stride // step)) for array, offs, step in received]
        part = mixed_part(me, gated, out_weight, give, sums, BF16)
        received.append((swap(part, "chan", bit), [off ^ bit for off in give], stride))
    last = received.pop()[0]
    own = mixed_part(me, gated, out_weight, [0], [(array, (0, 1)) for array, offs, step in received], F32)
    mixed = (own + last.astype(F32)).astype(BF16)

    direct = channels // n_ctx == 256
    tap_grad = by_channel(
        tap_grad_kernel,
        [key_proj, value_proj, earlier, grad_filtered, forward, lags],
        "ttttww",
        [("x" if direct else "c", BF16)],
        "tap_grad",
        me,
    )[0].reshape(n_ctx, -1, taps)
    if not direct:
        tap_grad = tap_grad[jnp.arange(n_ctx, dtype=jnp.int32) ^ me[0]]
    pieces = pieces_of(me, [cots[off] for off in range(n_chan)], n_ctx)
    tap_sum, held, sources = sum_and_exchange(tap_grad, pieces)
    grad_filters = placed_blocks(me, doubled(tap_sum, "ctx"))
    grad_key, grad_value = by_channel(
        backward_kernel,
        [key_proj, value_proj, grad_filtered, following, filters, forward, early],
        "ttttcww",
        [("t", BF16), ("t", BF16)],
        "backward_filter",
    )

    columns = gather_by_swaps(held)
    columns = [columns[off] for off in range(n_chan)]
    if (channels // n_ctx) % 128:
        columns = in_one_piece(me, columns, length)
    owners = []
    for c in range(n_ctx):
        spot = order.index(c)
        steps = [0] + [sign * step for step in range(1, n_ctx // 2) for sign in (-1, 1)] + [n_ctx // 2]
        owners.append([sources.index(order[(spot + step) % n_ctx] ^ c) for step in steps])
    grad_weight = grad_weight_of(me, jnp.asarray(owners, jnp.int32), blocks, far_low, far_high, columns)
    return (mixed, grad_query, grad_key, grad_value, grad_filters, grad_weight)


def solution(mesh):
    placed = (
        P("ctx", "chan"),
        P("ctx", "chan"),
        P("ctx", "chan"),
        P("chan", None),
        P("chan", None),
        P("ctx", "chan"),
    )
    return jax.shard_map(
        per_device,
        mesh=mesh,
        in_specs=placed,
        out_specs=(
            P("ctx", "chan"),
            P("ctx", "chan"),
            P("ctx", "chan"),
            P("ctx", "chan"),
            P("chan", None),
            P("chan", "ctx"),
        ),
        check_vma=False,
    )
```

time: 187 us -> 175 us (0.936)
  waiting for transfers between devices: 39.8 us -> 60 us
  starting transfers between devices: 50.6 us -> 33.2 us
  between operations: 5.8 us -> 1.13 us
  local copies, waits for them, and re-layouts: 4.51 us -> 1.35 us
  Pallas kernels: 78.3 us -> 75.3 us
  other arithmetic: 6.38 us -> 3.61 us
    ppermute x14, waiting for transfers between devices: 20 us -> 58.8 us  [swap(): return lax.ppermute(block, axis, [(i, i ^ bit) for i in range(size)])]
    ppermute x8 -> x0, starting transfers between devices: 25.6 us -> none  [per_device(): lax.ppermute(turned[:, step * piece:(step + 1) * piece], ('ctx', 'chan'),...]
    ppermute x3, waiting for transfers between devices: 12.2 us -> 1.09 us  [per_device(): from_behind = lax.ppermute(from_behind, 'ctx', ahead)]
    ppermute x14, starting transfers between devices: 7.09 us -> 13.4 us  [swap(): return lax.ppermute(block, axis, [(i, i ^ bit) for i in range(size)])]
    ppermute x1, waiting for transfers between devices: 5.93 us -> 0.01 us  [per_device(): far_low = lax.ppermute(from_behind[:, :half], 'ctx', ahead)]
    ppermute x3, starting transfers between devices: 5.71 us -> 10.3 us  [per_device(): from_behind = lax.ppermute(from_behind, 'ctx', ahead)]
    pallas_call x7 -> x9, Pallas kernels: 48.2 us -> 45.6 us  [the longest x4 26.1 us: grad_gated_part(): pl.pallas_call(functools.partial(grad_gated_kernel, kind), grid_spec=pltp...]
    convert_element_type x5 -> x3, other arithmetic: 2.22 us -> 0.13 us  [sum_and_exchange(): sums = (sums[::2].astype(F32) + others.astype(F32)).astype(BF16)]
  transfers between devices with their start and end apart: 32 -> 24, of which waited for: 8 -> 6; matrix products, arithmetic and copies ran while one was open for 5% -> 2% of each run, Pallas kernels for 37% -> 30%
where the time goes in v2:
time: 175 us
  Pallas kernels  75.3 us (43%)
  waiting for transfers between devices  60 us (34%)
  starting transfers between devices  33.2 us (19%)
  other arithmetic  3.61 us (2%)
    ppermute x14, waiting for transfers between devices, swap(): return lax.ppermute(block, axis, [(i, i ^ bit) for i in range(size)])  58.8 us
    pallas_call x4, Pallas kernels, grad_gated_part(): pl.pallas_call(functools.partial(grad_gated_kernel, kind), grid_spec=pltp...  26.1 us
    pallas_call x3, Pallas kernels, mixed_part(): pl.pallas_call(functools.partial(mixed_kernel, len(received)), grid_spec=...  20.9 us
    pallas_call x3, Pallas kernels, by_channel(): pl.pallas_call(body if me is None else lambda ids_ref, *refs: body(*refs)...  15.7 us
    ppermute x14, starting transfers between devices, swap(): return lax.ppermute(block, axis, [(i, i ^ bit) for i in range(size)])  13.4 us
    ppermute x3, starting transfers between devices, per_device(): from_behind = lax.ppermute(from_behind, 'ctx', ahead)  10.3 us
    pallas_call x1, Pallas kernels, grad_weight_of(): pl.pallas_call(functools.partial(weight_kernel, slots, parts, half), grid...  8.72 us
    ppermute x1, starting transfers between devices, per_device(): lax.ppermute(product, 'ctx', [(i, i + 1) for i in range(n_ctx - 1)])  4.2 us
  transfers between devices with their start and end apart: 24, of which 6 were waited for; matrix products, arithmetic and copies ran while one was open for 2% of the time, Pallas kernels for 30%

profile of v2, /device:TPU:0, one launch (start us, length us, event | category | flops | bytes accessed | tf_op | source)
XLA Modules:
  0.0 174.5 jit_solution(4740204942218218716)
XLA Ops:
  0.7 3.0 %collective-permute-start.3 = (bf16[128,2048]{1,0:T(8,128)(2,1)}, bf16[128,2048]{1,0:T(8,128)(2,1)S(1)}, u32[]{:S(2)}, u32[]{:S(2)}) collective-permute-start(bf16[128,2048]{1,0:T(8,128)(2,1)} %refs_0_.3), channel_id=1, source_target_pairs={{0,2},{1,3},{2,0},{3,1},{4,6},{5,7},{6,4},{7,5},{8,10},{9,11},{10,... | collective-permute-start | bytes 1572872 | tf_op jit(solution)/shard_map/ppermute | solution.py:336
  3.7 2.1 %multiply_convert_fusion = bf16[128,2048]{1,0:T(8,128)(2,1)} fusion(bf16[128,2048]{1,0:T(8,128)(2,1)} %refs_1_.3, bf16[128,2048]{1,0:T(8,128)(2,1)} %refs_0_.2), kind=kLoop, calls=%fused_computation.1 | loop fusion | flops 1048576 | bytes 1572864 | tf_op jit(solution)/shard_map/convert_element_type | solution.py:380
  5.8 4.2 %collective-permute-start = (bf16[128,2048]{1,0:T(8,128)(2,1)}, bf16[128,2048]{1,0:T(8,128)(2,1)}, u32[]{:S(2)}, u32[]{:S(2)}) collective-permute-start(bf16[128,2048]{1,0:T(8,128)(2,1)} %multiply_convert_fusion), channel_id=1, source_target_pairs={{0,4},{4,8},{8,12},{12,16},{16,20},{20,24},{24,28},{1,5},{5,9},{9,... | collective-permute-start | bytes 1572872 | tf_op jit(solution)/shard_map/ppermute | solution.py:381
  10.0 5.8 %collective-permute-done.3.cot_ref.refs_2_ = bf16[128,2048]{1,0:T(8,128)(2,1)S(1)} collective-permute-done((bf16[128,2048]{1,0:T(8,128)(2,1)}, bf16[128,2048]{1,0:T(8,128)(2,1)S(1)}, u32[]{:S(2)}, u32[]{:S(2)}) %collective-permute-start.3) | collective-permute-done | bytes 524320 | tf_op jit(solution)/shard_map/ppermute | solution.py:336
  15.9 1.0 copy-done
  16.9 6.3 %grad_gated_first.1.refs_0_ = f32[128,2048]{1,0:T(8,128)S(1)} custom-call(s32[2]{0:T(128)S(1)} %pad_add_fusion.me_ref.ids_ref, bf16[128,2048]{1,0:T(8,128)(2,1)S(1)} %copy-done, bf16[2048,8192]{1,0:T(8,128)(2,1)} %w_ref.13), custom_call_target="tpu_custom_call" | custom-call | flops 1073741824 | bytes 8388608 | tf_op jit(solution)/shard_map/grad_gated_first/pallas_call | solution.py:140
  23.3 4.3 %forward_filter.1 = (bf16[128,2048]{1,0:T(8,128)(2,1)S(1)}, f32[128,2048]{1,0:T(8,128)S(1)}) custom-call(bf16[128,2048]{1,0:T(8,128)(2,1)S(1)} %copy-done.2, bf16[128,2048]{1,0:T(8,128)(2,1)S(1)} %copy-done.3, bf16[128,2048]{1,0:T(8,128)(2,1)S(1)} %copy-done.4, bf16[128,2048]{1,0:T(8,128)(2,1)} %collective-permute-done.earlier_ref.refs_2_, ...), custom_call_target="tpu_custom_call" | custom-call | flops 1000000000 | bytes 4194304 | tf_op jit(solution)/shard_map/forward_filter/pallas_call | solution.py:102
  27.6 6.4 %grad_gated_middle.2.refs_0_ = f32[128,2048]{1,0:T(8,128)S(1)} custom-call(s32[2]{0:T(128)S(1)} %pad_add_fusion.me_ref.ids_ref, bf16[128,2048]{1,0:T(8,128)(2,1)S(1)} %collective-permute-done.5.cot_ref.refs_1_, bf16[2048,8192]{1,0:T(8,128)(2,1)} %w_ref.13, f32[128,2048]{1,0:T(8,128)S(1)} %grad_gated_first.1.refs_0_), custom_call_target="tpu_custom_call" | custom-call | flops 1073741824 | bytes 8388608 | tf_op jit(solution)/shard_map/grad_gated_middle/pallas_call | solution.py:140
  34.0 6.4 %grad_gated_middle.3.refs_0_ = f32[128,2048]{1,0:T(8,128)S(1)} custom-call(s32[2]{0:T(128)S(1)} %pad_add_fusion.me_ref.ids_ref, bf16[128,2048]{1,0:T(8,128)(2,1)S(1)} %collective-permute-done.3.cot_ref.refs_2_, bf16[2048,8192]{1,0:T(8,128)(2,1)} %w_ref.13, f32[128,2048]{1,0:T(8,128)S(1)} %grad_gated_middle.2.refs_0_), custom_call_target="tpu_custom_call" | custom-call | flops 1073741824 | bytes 8388608 | tf_op jit(solution)/shard_map/grad_gated_middle/pallas_call | solution.py:140
  40.4 7.1 %grad_gated_last.1 = (bf16[128,2048]{1,0:T(8,128)(2,1)}, bf16[128,2048]{1,0:T(8,128)(2,1)S(1)}) custom-call(s32[2]{0:T(128)S(1)} %pad_add_fusion.me_ref.ids_ref, bf16[128,2048]{1,0:T(8,128)(2,1)S(1)} %collective-permute-done.4.cot_ref.refs_3_, bf16[2048,8192]{1,0:T(8,128)(2,1)} %w_ref.13, f32[128,2048]{1,0:T(8,128)S(1)} %grad_gated_middle.3.refs_0_, ...), custom_call_target="tpu_custom_call" | custom-call | flops 1073741824 | bytes 8388608 | tf_op jit(solution)/shard_map/grad_gated_last/pallas_call | solution.py:140
  47.5 7.4 %tap_grad.1 = bf16[2048,128]{1,0:T(8,128)(2,1)S(1)} custom-call(s32[2]{0:T(128)S(1)} %pad_add_fusion.me_ref.ids_ref, bf16[128,2048]{1,0:T(8,128)(2,1)S(1)} %copy-done.3, bf16[128,2048]{1,0:T(8,128)(2,1)S(1)} %copy-done.4, bf16[128,2048]{1,0:T(8,128)(2,1)} %collective-permute-done.earlier_ref.refs_2_, bf16[128,2048]{1,0:T(8,128)(2,1)S(1)} %get-tuple-element.15.gf_ref.refs_3_, ...), custom_call_target="tpu_custom_call" | custom-call | flops 1000000000 | bytes 4194304 | tf_op jit(solution)/shard_map/tap_grad/pallas_call | solution.py:102
  55.6 1.8 %collective-permute-start.7 = (bf16[8,256,128]{2,1,0:T(8,128)(2,1)S(1)}, bf16[8,256,128]{2,1,0:T(8,128)(2,1)S(1)}, u32[]{:S(2)}, u32[]{:S(2)}) collective-permute-start(bf16[8,256,128]{2,1,0:T(8,128)(2,1)S(1)} %pad_maximum_fusion), channel_id=1, source_target_pairs={{0,4},{4,0},{8,12},{12,8},{16,20},{20,16},{24,28},{28,24},{1,5},{5... | collective-permute-start | bytes 1572872 | tf_op jit(solution)/shard_map/ppermute | solution.py:336
  57.5 1.6 collective-permute-start.13
  59.5 10.9 %collective-permute-done.7 = bf16[8,256,128]{2,1,0:T(8,128)(2,1)S(1)} collective-permute-done((bf16[8,256,128]{2,1,0:T(8,128)(2,1)S(1)}, bf16[8,256,128]{2,1,0:T(8,128)(2,1)S(1)}, u32[]{:S(2)}, u32[]{:S(2)}) %collective-permute-start.7) | collective-permute-done | bytes 524320 | tf_op jit(solution)/shard_map/ppermute | solution.py:336
  70.7 1.5 collective-permute-start.8
  72.2 9.9 %mixed_part.3 = bf16[128,4096]{1,0:T(8,128)(2,1)S(1)} custom-call(s32[2]{0:T(128)S(1)} %pad_add_fusion.me_ref.ids_ref, bf16[128,2048]{1,0:T(8,128)(2,1)S(1)} %get-tuple-element.12.gated_ref.refs_0_, bf16[2048,8192]{1,0:T(8,128)(2,1)} %w_ref.13), custom_call_target="tpu_custom_call" | custom-call | flops 2147483648 | bytes 16777216 | tf_op jit(solution)/shard_map/mixed_part/pallas_call | solution.py:184
  82.9 1.4 collective-permute-start.16
  84.5 3.0 %collective-permute-start.9 = (bf16[5,256,128]{2,1,0:T(8,128)(2,1)S(1)}, bf16[5,256,128]{2,1,0:T(8,128)(2,1)S(1)}, u32[]{:S(2)}, u32[]{:S(2)}) collective-permute-start(bf16[5,256,128]{2,1,0:T(8,128)(2,1)S(1)} %pad_maximum_fusion.4), channel_id=1, source_target_pairs={{0,16},{4,20},{8,24},{12,28},{16,0},{20,4},{24,8},{28,12},{1,17},{... | collective-permute-start | bytes 983048 | tf_op jit(solution)/shard_map/ppermute | solution.py:336
  87.6 1.3 collective-permute-start.6
  88.9 5.5 %mixed_part.5 = bf16[128,2048]{1,0:T(8,128)(2,1)S(1)} custom-call(s32[2]{0:T(128)S(1)} %pad_add_fusion.me_ref.ids_ref, bf16[128,2048]{1,0:T(8,128)(2,1)S(1)} %get-tuple-element.12.gated_ref.refs_0_, bf16[2048,8192]{1,0:T(8,128)(2,1)} %w_ref.13, bf16[128,4096]{1,0:T(8,128)(2,1)S(1)} %collective-permute-done.1.refs_0_), custom_call_target="tpu_custom_call" | custom-call | flops 1073741824 | bytes 8388608 | tf_op jit(solution)/shard_map/mixed_part/pallas_call | solution.py:184
  94.4 1.6 collective-permute-start.2
  95.9 1.1 collective-permute-done.15.refs_3_
  97.0 8.1 %collective-permute-start.17 = (bf16[128,2048]{1,0:T(8,128)(2,1)S(1)}, bf16[128,2048]{1,0:T(8,128)(2,1)S(1)}, u32[]{:S(2)}, u32[]{:S(2)}) collective-permute-start(bf16[128,2048]{1,0:T(8,128)(2,1)S(1)} %collective-permute-done.15.refs_3_), channel_id=1, source_target_pairs={{0,8},{8,16},{16,24},{24,28},{28,20},{20,12},{12,4},{4,0},{1,9},{9... | collective-permute-start | bytes 1572872 | tf_op jit(solution)/shard_map/ppermute | solution.py:404
  105.1 9.0 %collective-permute-done.9 = bf16[5,256,128]{2,1,0:T(8,128)(2,1)S(1)} collective-permute-done((bf16[5,256,128]{2,1,0:T(8,128)(2,1)S(1)}, bf16[5,256,128]{2,1,0:T(8,128)(2,1)S(1)}, u32[]{:S(2)}, u32[]{:S(2)}) %collective-permute-start.9) | collective-permute-done | bytes 327712 | tf_op jit(solution)/shard_map/ppermute | solution.py:336
  114.3 24.3 %collective-permute-done.10 = bf16[1,256,128]{2,1,0:T(8,128)(2,1)S(1)} collective-permute-done((bf16[1,256,128]{2,1,0:T(8,128)(2,1)S(1)}, bf16[1,256,128]{2,1,0:T(8,128)(2,1)S(1)}, u32[]{:S(2)}, u32[]{:S(2)}) %collective-permute-start.10) | collective-permute-done | bytes 65568 | tf_op jit(solution)/shard_map/ppermute | solution.py:336
  138.6 1.5 collective-permute-start.22
  140.3 4.0 %backward_filter.1 = (bf16[128,2048]{1,0:T(8,128)(2,1)}, bf16[128,2048]{1,0:T(8,128)(2,1)}) custom-call(bf16[128,2048]{1,0:T(8,128)(2,1)S(1)} %copy-done.3, bf16[128,2048]{1,0:T(8,128)(2,1)S(1)} %copy-done.4, bf16[128,2048]{1,0:T(8,128)(2,1)S(1)} %get-tuple-element.15.gf_ref.refs_3_, bf16[128,2048]{1,0:T(8,128)(2,1)S(1)} %collective-permute-done.6.following_ref, ...), custom_call_target="tpu_custom_call" | custom-call | flops 1000000000 | bytes 4194304 | tf_op jit(solution)/shard_map/backward_filter/pallas_call | solution.py:102
  144.2 5.5 %mixed_part.4 = f32[128,2048]{1,0:T(8,128)S(1)} custom-call(s32[2]{0:T(128)S(1)} %pad_add_fusion.me_ref.ids_ref, bf16[128,2048]{1,0:T(8,128)(2,1)S(1)} %get-tuple-element.12.gated_ref.refs_0_, bf16[2048,8192]{1,0:T(8,128)(2,1)} %w_ref.13, bf16[128,4096]{1,0:T(8,128)(2,1)S(1)} %collective-permute-done.1.refs_0_), custom_call_target="tpu_custom_call" | custom-call | flops 1073741824 | bytes 8388608 | tf_op jit(solution)/shard_map/mixed_part/pallas_call | solution.py:184
  149.8 2.0 %collective-permute-start.19 = (bf16[128,1024]{1,0:T(8,128)(2,1)S(1)}, bf16[128,1024]{1,0:T(8,128)(2,1)S(1)}, u32[]{:S(2)}, u32[]{:S(2)}) collective-permute-start(bf16[128,1024]{1,0:T(8,128)(2,1)S(1)} %slice.93), channel_id=1, source_target_pairs={{0,8},{8,16},{16,24},{24,28},{28,20},{20,12},{12,4},{4,0},{1,9},{9... | collective-permute-start | bytes 786440 | tf_op jit(solution)/shard_map/ppermute | solution.py:407
  153.6 8.8 %collective-permute-done.12 = bf16[4,256,128]{2,1,0:T(8,128)(2,1)S(1)} collective-permute-done((bf16[4,256,128]{2,1,0:T(8,128)(2,1)S(1)}, bf16[4,256,128]{2,1,0:T(8,128)(2,1)S(1)}, u32[]{:S(2)}, u32[]{:S(2)}) %collective-permute-start.12) | collective-permute-done | bytes 262176 | tf_op jit(solution)/shard_map/ppermute | solution.py:336
  162.5 3.3 %placed_blocks.1 = f32[2048,128]{1,0:T(8,128)} custom-call(s32[2]{0:T(128)S(1)} %pad_add_fusion.me_ref.ids_ref, bf16[8,256,128]{2,1,0:T(8,128)(2,1)S(1)} %bitcast.29), custom_call_target="tpu_custom_call" | custom-call | flops 1000000 | bytes 2097152 | tf_op jit(solution)/shard_map/placed_blocks/pallas_call | solution.py:301
  165.8 8.7 %grad_weight.1 = bf16[2048,1024]{1,0:T(8,128)(2,1)} custom-call(s32[2]{0:T(128)S(1)} %pad_add_fusion.me_ref.ids_ref, s32[8,8]{1,0:T(8,128)S(1)} %copy-done.10, bf16[128,2048]{1,0:T(8,128)(2,1)S(1)} %get-tuple-element.12.gated_ref.refs_0_, bf16[128,2048]{1,0:T(8,128)(2,1)S(1)} %collective-permute-done.13.refs_1_, ...), custom_call_target="tpu_custom_call" | custom-call | flops 4294967296 | bytes 12582912 | tf_op jit(solution)/shard_map/grad_weight/pallas_call | solution.py:280
  (78 shorter events, 4.6 us)
Async XLA Ops:
  0.6 22.6 %copy-start.3 = (bf16[128,2048]{1,0:T(8,128)(2,1)S(1)}, bf16[128,2048]{1,0:T(8,128)(2,1)}, u32[]{:S(2)}) copy-start(bf16[128,2048]{1,0:T(8,128)(2,1)} %refs_0_.2) | copy-start | bytes 1572868
  0.6 22.6 %copy-start.4 = (bf16[128,2048]{1,0:T(8,128)(2,1)S(1)}, bf16[128,2048]{1,0:T(8,128)(2,1)}, u32[]{:S(2)}) copy-start(bf16[128,2048]{1,0:T(8,128)(2,1)} %refs_1_.3) | copy-start | bytes 1572868
  0.7 22.6 %copy-start.2 = (bf16[128,2048]{1,0:T(8,128)(2,1)S(1)}, bf16[128,2048]{1,0:T(8,128)(2,1)}, u32[]{:S(2)}) copy-start(bf16[128,2048]{1,0:T(8,128)(2,1)} %refs_1_.2) | copy-start | bytes 1572868
  0.7 15.1 %collective-permute-start.3 = (bf16[128,2048]{1,0:T(8,128)(2,1)}, bf16[128,2048]{1,0:T(8,128)(2,1)S(1)}, u32[]{:S(2)}, u32[]{:S(2)}) collective-permute-start(bf16[128,2048]{1,0:T(8,128)(2,1)} %refs_0_.3), channel_id=1, source_target_pairs={{0,2},{1,3},{2,0},{3,1},{4,6},{5,7},{6,4},{7,5},{8,10},{9,11},{10,... | collective-permute-start | bytes 1572872 | tf_op jit(solution)/shard_map/ppermute | solution.py:336
  5.8 17.5 %collective-permute-start = (bf16[128,2048]{1,0:T(8,128)(2,1)}, bf16[128,2048]{1,0:T(8,128)(2,1)}, u32[]{:S(2)}, u32[]{:S(2)}) collective-permute-start(bf16[128,2048]{1,0:T(8,128)(2,1)} %multiply_convert_fusion), channel_id=1, source_target_pairs={{0,4},{4,8},{8,12},{12,16},{16,20},{20,24},{24,28},{1,5},{5,9},{9,... | collective-permute-start | bytes 1572872 | tf_op jit(solution)/shard_map/ppermute | solution.py:381
  10.0 17.6 %collective-permute-start.5 = (bf16[128,2048]{1,0:T(8,128)(2,1)}, bf16[128,2048]{1,0:T(8,128)(2,1)S(1)}, u32[]{:S(2)}, u32[]{:S(2)}) collective-permute-start(bf16[128,2048]{1,0:T(8,128)(2,1)} %refs_0_.3), channel_id=1, source_target_pairs={{0,1},{1,0},{2,3},{3,2},{4,5},{5,4},{6,7},{7,6},{8,9},{9,8},{10,11... | collective-permute-start | bytes 1572872 | tf_op jit(solution)/shard_map/ppermute | solution.py:336
  15.8 24.6 %collective-permute-start.4 = (bf16[128,2048]{1,0:T(8,128)(2,1)S(1)}, bf16[128,2048]{1,0:T(8,128)(2,1)S(1)}, u32[]{:S(2)}, u32[]{:S(2)}) collective-permute-start(bf16[128,2048]{1,0:T(8,128)(2,1)S(1)} %collective-permute-done.3.cot_ref.refs_2_), channel_id=1, source_target_pairs={{0,1},{1,0},{2,3},{3,2},{4,5},{5,4},{6,7},{7,6},{8,9},{9,8},{10,11... | collective-permute-start | bytes 1572872 | tf_op jit(solution)/shard_map/ppermute | solution.py:336
  16.9 6.4 %copy-start.9 = (bf16[2,128,256]{2,1,0:T(8,128)(2,1)S(1)}, bf16[2,128,256]{2,1,0:T(8,128)(2,1)}, u32[]{:S(2)}) copy-start(bf16[2,128,256]{2,1,0:T(8,128)(2,1)} %constant.20.clone.g_ref) | copy-start | bytes 393220
  34.0 13.5 %copy-start.8 = (bf16[2,128,256]{2,1,0:T(8,128)(2,1)S(1)}, bf16[2,128,256]{2,1,0:T(8,128)(2,1)}, u32[]{:S(2)}) copy-start(bf16[2,128,256]{2,1,0:T(8,128)(2,1)} %constant.22.clone.refs_5_) | copy-start | bytes 393220
  34.0 20.9 %copy-start.1 = (bf16[128,2048]{1,0:T(8,128)(2,1)S(1)}, bf16[128,2048]{1,0:T(8,128)(2,1)}, u32[]{:S(2)}) copy-start(bf16[128,2048]{1,0:T(8,128)(2,1)} %refs_0_.3) | copy-start | bytes 1572868
  55.6 14.8 %collective-permute-start.7 = (bf16[8,256,128]{2,1,0:T(8,128)(2,1)S(1)}, bf16[8,256,128]{2,1,0:T(8,128)(2,1)S(1)}, u32[]{:S(2)}, u32[]{:S(2)}) collective-permute-start(bf16[8,256,128]{2,1,0:T(8,128)(2,1)S(1)} %pad_maximum_fusion), channel_id=1, source_target_pairs={{0,4},{4,0},{8,12},{12,8},{16,20},{20,16},{24,28},{28,24},{1,5},{5... | collective-permute-start | bytes 1572872 | tf_op jit(solution)/shard_map/ppermute | solution.py:336
  57.5 24.8 %collective-permute-start.13 = (bf16[128,2048]{1,0:T(8,128)(2,1)S(1)}, bf16[128,2048]{1,0:T(8,128)(2,1)S(1)}, u32[]{:S(2)}, u32[]{:S(2)}) collective-permute-start(bf16[128,2048]{1,0:T(8,128)(2,1)S(1)} %get-tuple-element.12.gated_ref.refs_0_), channel_id=1, source_target_pairs={{0,8},{8,16},{16,24},{24,28},{28,20},{20,12},{12,4},{4,0},{1,9},{9... | collective-permute-start | bytes 1572872 | tf_op jit(solution)/shard_map/ppermute | solution.py:404
  59.1 23.8 %collective-permute-start.14 = (bf16[128,2048]{1,0:T(8,128)(2,1)S(1)}, bf16[128,2048]{1,0:T(8,128)(2,1)S(1)}, u32[]{:S(2)}, u32[]{:S(2)}) collective-permute-start(bf16[128,2048]{1,0:T(8,128)(2,1)S(1)} %get-tuple-element.12.gated_ref.refs_0_), channel_id=1, source_target_pairs={{8,0},{16,8},{24,16},{28,24},{20,28},{12,20},{4,12},{0,4},{9,1},{1... | collective-permute-start | bytes 1572872 | tf_op jit(solution)/shard_map/ppermute | solution.py:405
  70.7 69.6 %copy-start.7 = (bf16[2,128,256]{2,1,0:T(8,128)(2,1)S(1)}, bf16[2,128,256]{2,1,0:T(8,128)(2,1)}, u32[]{:S(2)}) copy-start(bf16[2,128,256]{2,1,0:T(8,128)(2,1)} %constant.21.clone.g_ref) | copy-start | bytes 393220
  70.7 13.6 %collective-permute-start.8 = (bf16[6,256,128]{2,1,0:T(8,128)(2,1)S(1)}, bf16[6,256,128]{2,1,0:T(8,128)(2,1)S(1)}, u32[]{:S(2)}, u32[]{:S(2)}) collective-permute-start(bf16[6,256,128]{2,1,0:T(8,128)(2,1)S(1)} %pad_maximum_fusion.3), channel_id=1, source_target_pairs={{0,8},{4,12},{8,0},{12,4},{16,24},{20,28},{24,16},{28,20},{1,9},{5... | collective-permute-start | bytes 1179656 | tf_op jit(solution)/shard_map/ppermute | solution.py:336
  82.2 6.7 %collective-permute-start.1 = (bf16[128,4096]{1,0:T(8,128)(2,1)S(1)}, bf16[128,4096]{1,0:T(8,128)(2,1)S(1)}, u32[]{:S(2)}, u32[]{:S(2)}) collective-permute-start(bf16[128,4096]{1,0:T(8,128)(2,1)S(1)} %mixed_part.3), channel_id=1, source_target_pairs={{0,1},{1,0},{2,3},{3,2},{4,5},{5,4},{6,7},{7,6},{8,9},{9,8},{10,11... | collective-permute-start | bytes 3145736 | tf_op jit(solution)/shard_map/ppermute | solution.py:336
  82.3 14.8 %collective-permute-start.15 = (bf16[128,2048]{1,0:T(8,128)(2,1)S(1)}, bf16[128,2048]{1,0:T(8,128)(2,1)S(1)}, u32[]{:S(2)}, u32[]{:S(2)}) collective-permute-start(bf16[128,2048]{1,0:T(8,128)(2,1)S(1)} %collective-permute-done.13.refs_1_), channel_id=1, source_target_pairs={{0,8},{8,16},{16,24},{24,28},{28,20},{20,12},{12,4},{4,0},{1,9},{9... | collective-permute-start | bytes 1572872 | tf_op jit(solution)/shard_map/ppermute | solution.py:404
  82.9 22.2 %collective-permute-start.16 = (bf16[128,2048]{1,0:T(8,128)(2,1)S(1)}, bf16[128,2048]{1,0:T(8,128)(2,1)S(1)}, u32[]{:S(2)}, u32[]{:S(2)}) collective-permute-start(bf16[128,2048]{1,0:T(8,128)(2,1)S(1)} %collective-permute-done.14.refs_2_), channel_id=1, source_target_pairs={{8,0},{16,8},{24,16},{28,24},{20,28},{12,20},{4,12},{0,4},{9,1},{1... | collective-permute-start | bytes 1572872 | tf_op jit(solution)/shard_map/ppermute | solution.py:405
  84.5 29.6 %collective-permute-start.9 = (bf16[5,256,128]{2,1,0:T(8,128)(2,1)S(1)}, bf16[5,256,128]{2,1,0:T(8,128)(2,1)S(1)}, u32[]{:S(2)}, u32[]{:S(2)}) collective-permute-start(bf16[5,256,128]{2,1,0:T(8,128)(2,1)S(1)} %pad_maximum_fusion.4), channel_id=1, source_target_pairs={{0,16},{4,20},{8,24},{12,28},{16,0},{20,4},{24,8},{28,12},{1,17},{... | collective-permute-start | bytes 983048 | tf_op jit(solution)/shard_map/ppermute | solution.py:336
  87.6 52.6 %collective-permute-start.6 = (bf16[128,2048]{1,0:T(8,128)(2,1)S(1)}, bf16[128,2048]{1,0:T(8,128)(2,1)S(1)}, u32[]{:S(2)}, u32[]{:S(2)}) collective-permute-start(bf16[128,2048]{1,0:T(8,128)(2,1)S(1)} %get-tuple-element.15.gf_ref.refs_3_), channel_id=1, source_target_pairs={{4,0},{8,4},{12,8},{16,12},{20,16},{24,20},{28,24},{5,1},{9,5},{13... | collective-permute-start | bytes 1572872 | tf_op jit(solution)/shard_map/ppermute | solution.py:413
  94.4 71.4 %copy-start.10 = (s32[8,8]{1,0:T(8,128)S(1)}, s32[8,8]{1,0:T(8,128)}, u32[]{:S(2)}) copy-start(s32[8,8]{1,0:T(8,128)} %constant.23.clone.owner_ref) | copy-start | bytes 772
  94.4 57.7 %collective-permute-start.2 = (bf16[128,2048]{1,0:T(8,128)(2,1)S(1)}, bf16[128,2048]{1,0:T(8,128)(2,1)S(1)}, u32[]{:S(2)}, u32[]{:S(2)}) collective-permute-start(bf16[128,2048]{1,0:T(8,128)(2,1)S(1)} %mixed_part.5), channel_id=1, source_target_pairs={{0,2},{1,3},{2,0},{3,1},{4,6},{5,7},{6,4},{7,5},{8,10},{9,11},{10,... | collective-permute-start | bytes 1572872 | tf_op jit(solution)/shard_map/ppermute | solution.py:336
  97.0 52.7 %collective-permute-start.17 = (bf16[128,2048]{1,0:T(8,128)(2,1)S(1)}, bf16[128,2048]{1,0:T(8,128)(2,1)S(1)}, u32[]{:S(2)}, u32[]{:S(2)}) collective-permute-start(bf16[128,2048]{1,0:T(8,128)(2,1)S(1)} %collective-permute-done.15.refs_3_), channel_id=1, source_target_pairs={{0,8},{8,16},{16,24},{24,28},{28,20},{20,12},{12,4},{4,0},{1,9},{9... | collective-permute-start | bytes 1572872 | tf_op jit(solution)/shard_map/ppermute | solution.py:404
  105.1 46.7 %collective-permute-start.18 = (bf16[128,2048]{1,0:T(8,128)(2,1)S(1)}, bf16[128,2048]{1,0:T(8,128)(2,1)S(1)}, u32[]{:S(2)}, u32[]{:S(2)}) collective-permute-start(bf16[128,2048]{1,0:T(8,128)(2,1)S(1)} %collective-permute-done.16.refs_4_), channel_id=1, source_target_pairs={{8,0},{16,8},{24,16},{28,24},{20,28},{12,20},{4,12},{0,4},{9,1},{1... | collective-permute-start | bytes 1572872 | tf_op jit(solution)/shard_map/ppermute | solution.py:405
  114.2 24.5 %collective-permute-start.10 = (bf16[1,256,128]{2,1,0:T(8,128)(2,1)S(1)}, bf16[1,256,128]{2,1,0:T(8,128)(2,1)S(1)}, u32[]{:S(2)}, u32[]{:S(2)}) collective-permute-start(bf16[1,256,128]{2,1,0:T(8,128)(2,1)S(1)} %add_convert_fusion.3), channel_id=1, source_target_pairs={{0,16},{4,20},{8,24},{12,28},{16,0},{20,4},{24,8},{28,12},{1,17},{... | collective-permute-start | bytes 196616 | tf_op jit(solution)/shard_map/ppermute | solution.py:336
  138.6 13.5 %collective-permute-start.22 = (bf16[8,256,128]{2,1,0:T(8,128)(2,1)S(1)}, bf16[8,256,128]{2,1,0:T(8,128)(2,1)S(1)}, u32[]{:S(2)}, u32[]{:S(2)}) collective-permute-start(bf16[8,256,128]{2,1,0:T(8,128)(2,1)S(1)} %maximum_bitcast_fusion.refs_9_), channel_id=1, source_target_pairs={{0,2},{1,3},{2,0},{3,1},{4,6},{5,7},{6,4},{7,5},{8,10},{9,11},{10,... | collective-permute-start | bytes 1572872 | tf_op jit(solution)/shard_map/ppermute | solution.py:336
  140.2 11.8 %collective-permute-start.11 = (bf16[2,256,128]{2,1,0:T(8,128)(2,1)S(1)}, bf16[2,256,128]{2,1,0:T(8,128)(2,1)S(1)}, u32[]{:S(2)}, u32[]{:S(2)}) collective-permute-start(bf16[2,256,128]{2,1,0:T(8,128)(2,1)S(1)} %get-tuple-element.25), channel_id=1, source_target_pairs={{0,8},{4,12},{8,0},{12,4},{16,24},{20,28},{24,16},{28,20},{1,9},{5... | collective-permute-start | bytes 393224 | tf_op jit(solution)/shard_map/ppermute | solution.py:336
  149.8 16.0 %collective-permute-start.19 = (bf16[128,1024]{1,0:T(8,128)(2,1)S(1)}, bf16[128,1024]{1,0:T(8,128)(2,1)S(1)}, u32[]{:S(2)}, u32[]{:S(2)}) collective-permute-start(bf16[128,1024]{1,0:T(8,128)(2,1)S(1)} %slice.93), channel_id=1, source_target_pairs={{0,8},{8,16},{16,24},{24,28},{28,20},{20,12},{12,4},{4,0},{1,9},{9... | collective-permute-start | bytes 786440 | tf_op jit(solution)/shard_map/ppermute | solution.py:407
  151.8 13.9 %collective-permute-start.20 = (bf16[128,1024]{1,0:T(8,128)(2,1)S(1)}, bf16[128,1024]{1,0:T(8,128)(2,1)S(1)}, u32[]{:S(2)}, u32[]{:S(2)}) collective-permute-start(bf16[128,1024]{1,0:T(8,128)(2,1)S(1)} %slice.94), channel_id=1, source_target_pairs={{8,0},{16,8},{24,16},{28,24},{20,28},{12,20},{4,12},{0,4},{9,1},{1... | collective-permute-start | bytes 786440 | tf_op jit(solution)/shard_map/ppermute | solution.py:408
  151.9 13.8 %collective-permute-start.21 = (bf16[8,256,128]{2,1,0:T(8,128)(2,1)S(1)}, bf16[8,256,128]{2,1,0:T(8,128)(2,1)S(1)}, u32[]{:S(2)}, u32[]{:S(2)}) collective-permute-start(bf16[8,256,128]{2,1,0:T(8,128)(2,1)S(1)} %maximum_bitcast_fusion.refs_9_), channel_id=1, source_target_pairs={{0,1},{1,0},{2,3},{3,2},{4,5},{5,4},{6,7},{7,6},{8,9},{9,8},{10,11... | collective-permute-start | bytes 1572872 | tf_op jit(solution)/shard_map/ppermute | solution.py:336
  152.1 10.3 %collective-permute-start.12 = (bf16[4,256,128]{2,1,0:T(8,128)(2,1)S(1)}, bf16[4,256,128]{2,1,0:T(8,128)(2,1)S(1)}, u32[]{:S(2)}, u32[]{:S(2)}) collective-permute-start(bf16[4,256,128]{2,1,0:T(8,128)(2,1)S(1)} %bitcast.34), channel_id=1, source_target_pairs={{0,4},{4,0},{8,12},{12,8},{16,20},{20,16},{24,28},{28,24},{1,5},{5... | collective-permute-start | bytes 786440 | tf_op jit(solution)/shard_map/ppermute | solution.py:336
  152.2 13.6 %collective-permute-start.23 = (bf16[8,256,128]{2,1,0:T(8,128)(2,1)S(1)}, bf16[8,256,128]{2,1,0:T(8,128)(2,1)S(1)}, u32[]{:S(2)}, u32[]{:S(2)}) collective-permute-start(bf16[8,256,128]{2,1,0:T(8,128)(2,1)S(1)} %collective-permute-done.22.refs_11_), channel_id=1, source_target_pairs={{0,1},{1,0},{2,3},{3,2},{4,5},{5,4},{6,7},{7,6},{8,9},{9,8},{10,11... | collective-permute-start | bytes 1572872 | tf_op jit(solution)/shard_map/ppermute | solution.py:336
  (3 other events, 13.8 us)

commit v3 on v2

--- a/solution.py
+++ b/solution.py
@@ -11,6 +11,7 @@
 F32 = jnp.float32
 BF16 = jnp.bfloat16
 VMEM_BYTES = 40 * 2**20
+STREAMS = 4
 NT = (((1,), (1,)), ((), ()))
 TN = (((0,), (0,)), ((), ()))
 
@@ -81,10 +82,17 @@
 
 
 def estimate(flops, bytes_accessed):
-    return pl.CostEstimate(flops=flops, bytes_accessed=bytes_accessed, transcendentals=0)
-
-
-def by_channel(kernel, arrays, kinds, outs, name, me=None):
+    return pl.CostEstimate(flops=flops // 16, bytes_accessed=bytes_accessed // 16, transcendentals=0)
+
+
+def ignoring(body, count, skip):
+    def kernel(*refs):
+        return body(*refs[:skip], *refs[skip + count :])
+
+    return kernel
+
+
+def by_channel(kernel, arrays, kinds, outs, name, me=None, after=()):
     length, channels = arrays[0].shape
     width = min(512, channels) if me is None else 256
     specs = {
@@ -98,13 +106,14 @@
             return pl.BlockSpec(shape, lambda i, *ids: (0,) * len(shape))
         return specs[kind]
 
-    body = functools.partial(kernel, length)
+    body = ignoring(functools.partial(kernel, length), len(after), len(arrays))
     return pl.pallas_call(
         body if me is None else lambda ids_ref, *refs: body(*refs),
         grid_spec=pltpu.PrefetchScalarGridSpec(
             num_scalar_prefetch=0 if me is None else 1,
             grid=(channels // width,),
-            in_specs=[spec_of(kind, a.shape) for kind, a in zip(kinds, arrays)],
+            in_specs=[spec_of(kind, a.shape) for kind, a in zip(kinds, arrays)]
+            + [pl.BlockSpec(memory_space=pl.ANY)] * len(after),
             out_specs=[specs[kind] for kind, unused in outs],
         ),
         out_shape=[
@@ -114,11 +123,16 @@
         compiler_params=pltpu.CompilerParams(vmem_limit_bytes=VMEM_BYTES),
         cost_estimate=estimate(10**9, 4 * 2**20),
         name=name,
-    )(*([] if me is None else [me]), *arrays)
-
-
-def grad_gated_kernel(kind, me_ref, cot_ref, w_ref, *refs):
-    total = mm(w_ref[...], cot_ref[...], NT).T
+    )(*([] if me is None else [me]), *arrays, *after)
+
+
+def grad_gated_kernel(kind, me_ref, cot_ref, *refs):
+    width = cot_ref.shape[1] // STREAMS
+    total = mm(refs[0][...], cot_ref[:, :width], NT)
+    for stream in range(1, STREAMS):
+        total = total + mm(refs[stream][...], cot_ref[:, stream * width : (stream + 1) * width], NT)
+    total = total.T
+    refs = refs[STREAMS:]
     if kind == "first":
         refs[-1][...] = total
         return
@@ -131,39 +145,48 @@
     gf_ref[...] = (total * q_ref[...].astype(F32)).astype(BF16)
 
 
-def grad_gated_part(kind, me, cot, weight, off, arrays):
+def grad_gated_part(kind, me, cot, weight, off, arrays, after=()):
     length, width = cot.shape
     channels = weight.shape[0]
     tile = 512
     row_spec = pl.BlockSpec((length, tile), lambda i, me: (0, i))
     kinds = [BF16, BF16] if kind == "last" else [F32]
     return pl.pallas_call(
-        functools.partial(grad_gated_kernel, kind),
+        ignoring(functools.partial(grad_gated_kernel, kind), len(after), 2 + STREAMS + len(arrays)),
         grid_spec=pltpu.PrefetchScalarGridSpec(
             num_scalar_prefetch=1,
             grid=(channels // tile,),
             in_specs=[
                 pl.BlockSpec((length, width), lambda i, me: (0, 0)),
-                pl.BlockSpec((tile, width), lambda i, me: (i, me[1] ^ off)),
             ]
-            + [row_spec] * len(arrays),
+            + [
+                pl.BlockSpec(
+                    (tile, width // STREAMS), lambda i, me, stream=stream: (i, (me[1] ^ off) * STREAMS + stream)
+                )
+                for stream in range(STREAMS)
+            ]
+            + [row_spec] * len(arrays)
+            + [pl.BlockSpec(memory_space=pl.ANY)] * len(after),
             out_specs=[row_spec] * len(kinds),
         ),
         out_shape=[jax.ShapeDtypeStruct((length, channels), dtype) for dtype in kinds],
         compiler_params=pltpu.CompilerParams(vmem_limit_bytes=VMEM_BYTES),
         cost_estimate=estimate(2 * length * width * channels, 2 * width * channels),
         name="grad_gated_" + kind,
-    )(me, cot, weight, *arrays)
-
-
-def mixed_kernel(adds, me_ref, gated_ref, w_ref, *refs):
-    total = mm(gated_ref[...], w_ref[...])
-    for ref in refs[:adds]:
+    )(me, cot, *[weight] * STREAMS, *arrays, *after)
+
+
+def mixed_kernel(adds, me_ref, gated_ref, *refs):
+    depth = gated_ref.shape[1] // STREAMS
+    total = mm(gated_ref[:, :depth], refs[0][...])
+    for stream in range(1, STREAMS):
+        total = total + mm(gated_ref[:, stream * depth : (stream + 1) * depth], refs[stream][...])
+    for ref in refs[STREAMS : STREAMS + adds]:
         total = total + ref[...].astype(F32)
     refs[-1][...] = total.astype(refs[-1].dtype)
 
 
-def mixed_part(me, gated, weight, offs, received, kind):
+def mixed_part(me, gated, weight, offs, received, kind, after=()):
     length, channels = gated.shape
     tile = 512
     steps = channels // tile
@@ -173,7 +196,13 @@
 
     in_specs = [
         pl.BlockSpec((length, channels), lambda b, t, me: (0, 0)),
-        pl.BlockSpec((channels, tile), lambda b, t, me: (0, (me[1] ^ column(b)) * steps + t)),
+    ]
+    in_specs += [
+        pl.BlockSpec(
+            (channels // STREAMS, tile),
+            lambda b, t, me, stream=stream: (stream, (me[1] ^ column(b)) * steps + t),
+        )
+        for stream in range(STREAMS)
     ]
     for unused, (start, stride) in received:
         in_specs.append(
@@ -181,8 +210,9 @@
                 (length, tile), lambda b, t, me, start=start, stride=stride: (0, (start + b * stride) * steps + t)
             )
         )
+    in_specs += [pl.BlockSpec(memory_space=pl.ANY)] * len(after)
     return pl.pallas_call(
-        functools.partial(mixed_kernel, len(received)),
+        ignoring(functools.partial(mixed_kernel, len(received)), len(after), 2 + STREAMS + len(received)),
         grid_spec=pltpu.PrefetchScalarGridSpec(
             num_scalar_prefetch=1,
             grid=(len(offs), steps),
@@ -193,7 +223,7 @@
         compiler_params=pltpu.CompilerParams(vmem_limit_bytes=VMEM_BYTES),
         cost_estimate=estimate(2 * length * channels * channels * len(offs), 2 * channels * channels * len(offs)),
         name="mixed_part",
-    )(me, gated, weight, *[array for array, unused in received])
+    )(me, gated, *[weight] * STREAMS, *[array for array, unused in received], *after)
 
 
 def pieces_kernel(per_chan, me_ref, *refs):
@@ -293,7 +323,9 @@
 
 
 def place_kernel(me_ref, in_ref, out_ref):
-    out_ref[...] = in_ref[...].astype(out_ref.dtype)
+    count, rows, unused = in_ref.shape
+    for at in range(count):
+        out_ref[at * rows : (at + 1) * rows] = in_ref[me_ref[0] ^ at].astype(out_ref.dtype)
 
 
 def placed_blocks(me, blocks):
@@ -302,9 +334,9 @@
         place_kernel,
         grid_spec=pltpu.PrefetchScalarGridSpec(
             num_scalar_prefetch=1,
-            grid=(count,),
-            in_specs=[pl.BlockSpec((None, rows, width), lambda i, me: (i ^ me[0], 0, 0))],
-            out_specs=pl.BlockSpec((rows, width), lambda i, me: (i, 0)),
+            grid=(1,),
+            in_specs=[pl.BlockSpec(blocks.shape, lambda i, me: (0, 0, 0))],
+            out_specs=pl.BlockSpec((count * rows, width), lambda i, me: (0, 0)),
         ),
         out_shape=jax.ShapeDtypeStruct((count * rows, width), F32),
         compiler_params=pltpu.CompilerParams(vmem_limit_bytes=VMEM_BYTES),
@@ -347,20 +379,23 @@
     return held
 
 
-def sum_and_exchange(partial, pieces):
-    count = pieces.shape[0]
-    sums, held, sources = partial, pieces[None], [0]
-    for bit in bits_of(count):
+def summed(partial):
+    sums = partial
+    for bit in bits_of(partial.shape[0]):
+        others = swap(sums[1::2], "ctx", bit)
+        sums = (sums[::2].astype(F32) + others.astype(F32)).astype(BF16)
+    return sums
+
+
+def exchanged(pieces):
+    held, sources, stages = pieces[None], [0], []
+    for bit in bits_of(pieces.shape[0]):
         give = held[:, 1::2].reshape((-1,) + pieces.shape[1:])
-        if partial.shape[1:] == pieces.shape[1:]:
-            came = swap(jnp.concatenate([sums[1::2], give], axis=0), "ctx", bit)
-            others, came = came[: sums.shape[0] // 2], came[sums.shape[0] // 2 :]
-        else:
-            others, came = swap(sums[1::2], "ctx", bit), swap(give, "ctx", bit)
-        sums = (sums[::2].astype(F32) + others.astype(F32)).astype(BF16)
-        held = jnp.concatenate([held[:, ::2], came.reshape((len(sources), -1) + pieces.shape[1:])], axis=0)
+        stages.append(swap(give, "ctx", bit))
+        came = stages[-1].reshape((len(sources), -1) + pieces.shape[1:])
+        held = jnp.concatenate([held[:, ::2], came], axis=0)
         sources += [source ^ bit for source in sources]
-    return sums, held[:, 0], sources
+    return held[:, 0], sources, stages
 
 
 def doubled(block, axis):
@@ -385,6 +420,11 @@
     for off in range(n_chan - 1):
         grad_gated = grad_gated_part("middle" if off else "first", me, cots[off], out_weight, off, grad_gated)
         grad_gated = list(grad_gated)
+        if off == 0:
+            first = grad_gated
+
+    pieces = pieces_of(me, [cots[off] for off in range(n_chan)], n_ctx)
+    held, sources, stages = exchanged(pieces)
 
     gated, filtered = by_channel(
         forward_kernel,
@@ -392,6 +432,7 @@
         "ttttcww",
         [("t", BF16), ("t", F32)],
         "forward_filter",
+        after=first,
     )
 
     order = cycle_of(n_ctx)
@@ -408,7 +449,7 @@
     far_high = lax.ppermute(from_ahead[:, half:], "ctx", behind)
 
     grad_query, grad_filtered = grad_gated_part(
-        "last", me, cots[n_chan - 1], out_weight, n_chan - 1, grad_gated + [query_proj, filtered]
+        "last", me, cots[n_chan - 1], out_weight, n_chan - 1, grad_gated + [query_proj, filtered], [pieces]
     )
     following = lax.ppermute(grad_filtered, "ctx", [(i + 1, i) for i in range(n_ctx - 1)])
 
@@ -419,10 +460,13 @@
         left = left[::2]
         stride = give[1] - give[0] if len(give) > 1 else 1
         sums = [(array, ((give[0] - offs[0]) // step, stride // step)) for array, offs, step in received]
-        part = mixed_part(me, gated, out_weight, give, sums, BF16)
+        ring = min(len(received) + 1, n_ctx // 2 - 1)
+        part = mixed_part(
+            me, gated, out_weight, give, sums, BF16, blocks[2 * ring - 1 : 2 * ring + 1] + stages[ring : ring + 1]
+        )
         received.append((swap(part, "chan", bit), [off ^ bit for off in give], stride))
     last = received.pop()[0]
-    own = mixed_part(me, gated, out_weight, [0], [(array, (0, 1)) for array, offs, step in received], F32)
+    own = mixed_part(me, gated, out_weight, [0], [(array, (0, 1)) for array, offs, step in received], F32, blocks[-2:])
     mixed = (own + last.astype(F32)).astype(BF16)
 
     direct = channels // n_ctx == 256
@@ -433,12 +477,11 @@
         [("x" if direct else "c", BF16)],
         "tap_grad",
         me,
+        blocks[1:3] + stages[:1],
     )[0].reshape(n_ctx, -1, taps)
     if not direct:
         tap_grad = tap_grad[jnp.arange(n_ctx, dtype=jnp.int32) ^ me[0]]
-    pieces = pieces_of(me, [cots[off] for off in range(n_chan)], n_ctx)
-    tap_sum, held, sources = sum_and_exchange(tap_grad, pieces)
-    grad_filters = placed_blocks(me, doubled(tap_sum, "ctx"))
+    grad_filters = placed_blocks(me, doubled(summed(tap_grad), "ctx"))
     grad_key, grad_value = by_channel(
         backward_kernel,
         [key_proj, value_proj, grad_filtered, following, filters, forward, early],

time: 175 us -> 160 us (0.914)
  waiting for transfers between devices: 60 us -> 46.8 us
  Pallas kernels: 75.3 us -> 71.5 us
  starting transfers between devices: 33.2 us -> 36.2 us
    ppermute x14 -> x17, waiting for transfers between devices: 58.8 us -> 40.8 us  [swap(): return lax.ppermute(block, axis, [(i, i ^ bit) for i in range(size)])]
    ppermute x14 -> x17, starting transfers between devices: 13.4 us -> 26.2 us  [swap(): return lax.ppermute(block, axis, [(i, i ^ bit) for i in range(size)])]
    ppermute x3, starting transfers between devices: 10.3 us -> 3.45 us  [per_device(): from_behind = lax.ppermute(from_behind, 'ctx', ahead)]
    ppermute x1, waiting for transfers between devices: 0.01 us -> 6.02 us  [per_device(): lax.ppermute(grad_filtered, 'ctx', [(i + 1, i) for i in range(n_ctx - 1)])]
    pallas_call x3, Pallas kernels: 15.7 us -> 13.6 us  [by_channel(): pl.pallas_call(body if me is None else lambda ids_ref, *refs: body(*refs)...]
    ppermute x1, starting transfers between devices: 2.04 us -> 0.01 us  [per_device(): far_low = lax.ppermute(from_behind[:, :half], 'ctx', ahead)]
  transfers between devices with their start and end apart: 24 -> 27, of which waited for: 6 -> 8; matrix products, arithmetic and copies ran while one was open for 2% -> 1% of each run, Pallas kernels for 30% -> 41%
where the time goes in v3:
time: 160 us
  Pallas kernels  71.5 us (45%)
  waiting for transfers between devices  46.8 us (29%)
  starting transfers between devices  36.2 us (23%)
  other arithmetic  2.66 us (2%)
    ppermute x17, waiting for transfers between devices, swap(): return lax.ppermute(block, axis, [(i, i ^ bit) for i in range(size)])  40.8 us
    ppermute x17, starting transfers between devices, swap(): return lax.ppermute(block, axis, [(i, i ^ bit) for i in range(size)])  26.2 us
    pallas_call x4, Pallas kernels, grad_gated_part(): pl.pallas_call(ignoring(functools.partial(grad_gated_kernel, kind), len(a...  26.2 us
    pallas_call x3, Pallas kernels, mixed_part(): pl.pallas_call(ignoring(functools.partial(mixed_kernel, len(received)), l...  20.7 us
    pallas_call x3, Pallas kernels, by_channel(): pl.pallas_call(body if me is None else lambda ids_ref, *refs: body(*refs)...  13.6 us
    pallas_call x1, Pallas kernels, grad_weight_of(): pl.pallas_call(functools.partial(weight_kernel, slots, parts, half), grid...  8.82 us
    ppermute x1, waiting for transfers between devices, per_device(): lax.ppermute(grad_filtered, 'ctx', [(i + 1, i) for i in range(n_ctx - 1)])  6.02 us
    ppermute x1, starting transfers between devices, per_device(): lax.ppermute(product, 'ctx', [(i, i + 1) for i in range(n_ctx - 1)])  3.46 us
  transfers between devices with their start and end apart: 27, of which 8 were waited for; matrix products, arithmetic and copies ran while one was open for 1% of the time, Pallas kernels for 41%

profile of v3, /device:TPU:0, one launch (start us, length us, event | category | flops | bytes accessed | tf_op | source)
XLA Modules:
  0.0 159.6 jit_solution(9019048113181830555)
XLA Ops:
  0.6 3.0 %collective-permute-start.4 = (bf16[128,2048]{1,0:T(8,128)(2,1)}, bf16[128,2048]{1,0:T(8,128)(2,1)S(1)}, u32[]{:S(2)}, u32[]{:S(2)}) collective-permute-start(bf16[128,2048]{1,0:T(8,128)(2,1)} %refs_0_.5), channel_id=1, source_target_pairs={{0,2},{1,3},{2,0},{3,1},{4,6},{5,7},{6,4},{7,5},{8,10},{9,11},{10,... | collective-permute-start | bytes 1572872 | tf_op jit(solution)/shard_map/ppermute | solution.py:368
  3.6 1.3 multiply_convert_fusion
  5.0 3.5 %collective-permute-start = (bf16[128,2048]{1,0:T(8,128)(2,1)S(1)}, bf16[128,2048]{1,0:T(8,128)(2,1)S(1)}, u32[]{:S(2)}, u32[]{:S(2)}) collective-permute-start(bf16[128,2048]{1,0:T(8,128)(2,1)S(1)} %multiply_convert_fusion), channel_id=1, source_target_pairs={{0,4},{4,8},{8,12},{12,16},{16,20},{20,24},{24,28},{1,5},{5,9},{9,... | collective-permute-start | bytes 1572872 | tf_op jit(solution)/shard_map/ppermute | solution.py:416
  8.5 7.3 %collective-permute-done.4.refs_2_.refs_1_ = bf16[128,2048]{1,0:T(8,128)(2,1)S(1)} collective-permute-done((bf16[128,2048]{1,0:T(8,128)(2,1)}, bf16[128,2048]{1,0:T(8,128)(2,1)S(1)}, u32[]{:S(2)}, u32[]{:S(2)}) %collective-permute-start.4) | collective-permute-done | bytes 524320 | tf_op jit(solution)/shard_map/ppermute | solution.py:368
  16.9 6.5 %grad_gated_first.1.refs_7_.refs_6_ = f32[128,2048]{1,0:T(8,128)S(1)} custom-call(s32[2]{0:T(128)S(1)} %pad_add_fusion.refs_0_.me_ref.ids_ref, bf16[128,2048]{1,0:T(8,128)(2,1)S(1)} %copy-done.3, bf16[2048,8192]{1,0:T(8,128)(2,1)} %refs_5_.16, bf16[2048,8192]{1,0:T(8,128)(2,1)} %refs_5_.16, bf16[2048,8192]{1,0:T(8,128)(2,1)} %refs_5_.16, ...), custom_call_target="tpu_custom_call" | custom-call | flops 67108864 | bytes 524288 | tf_op jit(solution)/shard_map/grad_gated_first/pallas_call | solution.py:154
  23.6 3.4 %forward_filter.1 = (bf16[128,2048]{1,0:T(8,128)(2,1)S(1)}, f32[128,2048]{1,0:T(8,128)S(1)}) custom-call(bf16[128,2048]{1,0:T(8,128)(2,1)S(1)} %copy-done.5, bf16[128,2048]{1,0:T(8,128)(2,1)S(1)} %copy-done, bf16[128,2048]{1,0:T(8,128)(2,1)S(1)} %copy-done.1, bf16[128,2048]{1,0:T(8,128)(2,1)S(1)} %collective-permute-done.refs_3_.refs_2_, ...), custom_call_target="tpu_custom_call" | custom-call | flops 62500000 | bytes 262144 | tf_op jit(solution)/shard_map/forward_filter/pallas_call | solution.py:110
  26.9 1.9 %collective-permute-start.1 = (bf16[128,2048]{1,0:T(8,128)(2,1)S(1)}, bf16[128,2048]{1,0:T(8,128)(2,1)S(1)}, u32[]{:S(2)}, u32[]{:S(2)}) collective-permute-start(bf16[128,2048]{1,0:T(8,128)(2,1)S(1)} %get-tuple-element.12.refs_1_.refs_0_), channel_id=1, source_target_pairs={{0,8},{8,16},{16,24},{24,28},{28,20},{20,12},{12,4},{4,0},{1,9},{9... | collective-permute-start | bytes 1572872 | tf_op jit(solution)/shard_map/ppermute | solution.py:445
  29.7 1.8 %collective-permute-start.6 = (bf16[4,256,128]{2,1,0:T(8,128)(2,1)S(1)}, bf16[4,256,128]{2,1,0:T(8,128)(2,1)S(1)}, u32[]{:S(2)}, u32[]{:S(2)}) collective-permute-start(bf16[4,256,128]{2,1,0:T(8,128)(2,1)S(1)} %get-tuple-element.21), channel_id=1, source_target_pairs={{0,4},{4,0},{8,12},{12,8},{16,20},{20,16},{24,28},{28,24},{1,5},{5... | collective-permute-start | bytes 786440 | tf_op jit(solution)/shard_map/ppermute | solution.py:368
  31.5 6.3 %grad_gated_middle.2.refs_6_ = f32[128,2048]{1,0:T(8,128)S(1)} custom-call(s32[2]{0:T(128)S(1)} %pad_add_fusion.refs_0_.me_ref.ids_ref, bf16[128,2048]{1,0:T(8,128)(2,1)S(1)} %collective-permute-done.3.refs_1_, bf16[2048,8192]{1,0:T(8,128)(2,1)} %refs_5_.16, bf16[2048,8192]{1,0:T(8,128)(2,1)} %refs_5_.16, bf16[2048,8192]{1,0:T(8,128)(2,1)} %refs_5_.16, ...), custom_call_target="tpu_custom_call" | custom-call | flops 67108864 | bytes 524288 | tf_op jit(solution)/shard_map/grad_gated_middle/pallas_call | solution.py:154
  37.8 6.3 %grad_gated_middle.3.refs_6_ = f32[128,2048]{1,0:T(8,128)S(1)} custom-call(s32[2]{0:T(128)S(1)} %pad_add_fusion.refs_0_.me_ref.ids_ref, bf16[128,2048]{1,0:T(8,128)(2,1)S(1)} %collective-permute-done.4.refs_2_.refs_1_, bf16[2048,8192]{1,0:T(8,128)(2,1)} %refs_5_.16, bf16[2048,8192]{1,0:T(8,128)(2,1)} %refs_5_.16, bf16[2048,8192]{1,0:T(8,128)(2,1)} %refs_5_.16, ...), custom_call_target="tpu_custom_call" | custom-call | flops 67108864 | bytes 524288 | tf_op jit(solution)/shard_map/grad_gated_middle/pallas_call | solution.py:154
  44.2 7.0 %grad_gated_last.1 = (bf16[128,2048]{1,0:T(8,128)(2,1)}, bf16[128,2048]{1,0:T(8,128)(2,1)S(1)}) custom-call(s32[2]{0:T(128)S(1)} %pad_add_fusion.refs_0_.me_ref.ids_ref, bf16[128,2048]{1,0:T(8,128)(2,1)S(1)} %collective-permute-done.5.refs_3_.refs_1_, bf16[2048,8192]{1,0:T(8,128)(2,1)} %refs_5_.16, bf16[2048,8192]{1,0:T(8,128)(2,1)} %refs_5_.16, ...), custom_call_target="tpu_custom_call" | custom-call | flops 67108864 | bytes 524288 | tf_op jit(solution)/shard_map/grad_gated_last/pallas_call | solution.py:154
  51.2 6.3 %tap_grad.1 = bf16[2048,128]{1,0:T(8,128)(2,1)S(1)} custom-call(s32[2]{0:T(128)S(1)} %pad_add_fusion.refs_0_.me_ref.ids_ref, bf16[128,2048]{1,0:T(8,128)(2,1)S(1)} %copy-done, bf16[128,2048]{1,0:T(8,128)(2,1)S(1)} %copy-done.1, bf16[128,2048]{1,0:T(8,128)(2,1)S(1)} %collective-permute-done.refs_3_.refs_2_, ...), custom_call_target="tpu_custom_call" | custom-call | flops 62500000 | bytes 262144 | tf_op jit(solution)/shard_map/tap_grad/pallas_call | solution.py:110
  58.0 1.9 %collective-permute-start.7 = (bf16[4,256,128]{2,1,0:T(8,128)(2,1)S(1)}, bf16[4,256,128]{2,1,0:T(8,128)(2,1)S(1)}, u32[]{:S(2)}, u32[]{:S(2)}) collective-permute-start(bf16[4,256,128]{2,1,0:T(8,128)(2,1)S(1)} %bitcast.37), channel_id=1, source_target_pairs={{0,8},{4,12},{8,0},{12,4},{16,24},{20,28},{24,16},{28,20},{1,9},{5... | collective-permute-start | bytes 786440 | tf_op jit(solution)/shard_map/ppermute | solution.py:368
  59.9 5.6 %collective-permute-done.16 = bf16[4,256,128]{2,1,0:T(8,128)(2,1)S(1)} collective-permute-done((bf16[4,256,128]{2,1,0:T(8,128)(2,1)S(1)}, bf16[4,256,128]{2,1,0:T(8,128)(2,1)S(1)}, u32[]{:S(2)}, u32[]{:S(2)}) %collective-permute-start.16) | collective-permute-done | bytes 262176 | tf_op jit(solution)/shard_map/ppermute | solution.py:368
  65.6 1.6 %collective-permute-start.17 = (bf16[2,256,128]{2,1,0:T(8,128)(2,1)S(1)}, bf16[2,256,128]{2,1,0:T(8,128)(2,1)S(1)}, u32[]{:S(2)}, u32[]{:S(2)}) collective-permute-start(bf16[2,256,128]{2,1,0:T(8,128)(2,1)S(1)} %slice.54), channel_id=1, source_target_pairs={{0,8},{4,12},{8,0},{12,4},{16,24},{20,28},{24,16},{28,20},{1,9},{5... | collective-permute-start | bytes 393224 | tf_op jit(solution)/shard_map/ppermute | solution.py:368
  67.7 1.6 collective-permute-start.11
  69.3 9.8 %mixed_part.3 = bf16[128,4096]{1,0:T(8,128)(2,1)S(1)} custom-call(s32[2]{0:T(128)S(1)} %pad_add_fusion.refs_0_.me_ref.ids_ref, bf16[128,2048]{1,0:T(8,128)(2,1)S(1)} %get-tuple-element.12.refs_1_.refs_0_, bf16[2048,8192]{1,0:T(8,128)(2,1)} %refs_5_.16, bf16[2048,8192]{1,0:T(8,128)(2,1)} %refs_5_.16, bf16[2048,8192]{1,0:T(8,128)(2,1)} %refs_5_.16, ...), custom_call_target="tpu_custom_call" | custom-call | flops 134217728 | bytes 1048576 | tf_op jit(solution)/shard_map/mixed_part/pallas_call | solution.py:214
  79.2 2.7 %collective-permute-start.18 = (bf16[1,256,128]{2,1,0:T(8,128)(2,1)S(1)}, bf16[1,256,128]{2,1,0:T(8,128)(2,1)S(1)}, u32[]{:S(2)}, u32[]{:S(2)}) collective-permute-start(bf16[1,256,128]{2,1,0:T(8,128)(2,1)S(1)} %slice.63), channel_id=1, source_target_pairs={{0,16},{4,20},{8,24},{12,28},{16,0},{20,4},{24,8},{28,12},{1,17},{... | collective-permute-start | bytes 196616 | tf_op jit(solution)/shard_map/ppermute | solution.py:368
  83.4 9.4 %collective-permute-done.18 = bf16[1,256,128]{2,1,0:T(8,128)(2,1)S(1)} collective-permute-done((bf16[1,256,128]{2,1,0:T(8,128)(2,1)S(1)}, bf16[1,256,128]{2,1,0:T(8,128)(2,1)S(1)}, u32[]{:S(2)}, u32[]{:S(2)}) %collective-permute-start.18) | collective-permute-done | bytes 65568 | tf_op jit(solution)/shard_map/ppermute | solution.py:368
  92.9 6.2 %collective-permute-done.13.refs_9_ = bf16[4,256,128]{2,1,0:T(8,128)(2,1)S(1)} collective-permute-done((bf16[4,256,128]{2,1,0:T(8,128)(2,1)S(1)}, bf16[4,256,128]{2,1,0:T(8,128)(2,1)S(1)}, u32[]{:S(2)}, u32[]{:S(2)}) %collective-permute-start.13) | collective-permute-done | bytes 262176 | tf_op jit(solution)/shard_map/ppermute | solution.py:368
  99.1 1.6 collective-permute-start.25
  100.7 1.5 collective-permute-done.19
  102.2 8.9 %collective-permute-start.20 = (bf16[2,256,128]{2,1,0:T(8,128)(2,1)S(1)}, bf16[2,256,128]{2,1,0:T(8,128)(2,1)S(1)}, u32[]{:S(2)}, u32[]{:S(2)}) collective-permute-start(bf16[2,256,128]{2,1,0:T(8,128)(2,1)S(1)} %get-tuple-element.23), channel_id=1, source_target_pairs={{0,8},{4,12},{8,0},{12,4},{16,24},{20,28},{24,16},{28,20},{1,9},{5... | collective-permute-start | bytes 393224 | tf_op jit(solution)/shard_map/ppermute | solution.py:368
  111.1 5.2 %collective-permute-done.20 = bf16[2,256,128]{2,1,0:T(8,128)(2,1)S(1)} collective-permute-done((bf16[2,256,128]{2,1,0:T(8,128)(2,1)S(1)}, bf16[2,256,128]{2,1,0:T(8,128)(2,1)S(1)}, u32[]{:S(2)}, u32[]{:S(2)}) %collective-permute-start.20) | collective-permute-done | bytes 131104 | tf_op jit(solution)/shard_map/ppermute | solution.py:368
  117.7 2.7 %collective-permute-start.21 = (bf16[4,256,128]{2,1,0:T(8,128)(2,1)S(1)}, bf16[4,256,128]{2,1,0:T(8,128)(2,1)S(1)}, u32[]{:S(2)}, u32[]{:S(2)}) collective-permute-start(bf16[4,256,128]{2,1,0:T(8,128)(2,1)S(1)} %bitcast.35), channel_id=1, source_target_pairs={{0,4},{4,0},{8,12},{12,8},{16,20},{20,16},{24,28},{28,24},{1,5},{5... | collective-permute-start | bytes 786440 | tf_op jit(solution)/shard_map/ppermute | solution.py:368
  120.9 5.4 %mixed_part.5 = bf16[128,2048]{1,0:T(8,128)(2,1)S(1)} custom-call(s32[2]{0:T(128)S(1)} %pad_add_fusion.refs_0_.me_ref.ids_ref, bf16[128,2048]{1,0:T(8,128)(2,1)S(1)} %get-tuple-element.12.refs_1_.refs_0_, bf16[2048,8192]{1,0:T(8,128)(2,1)} %refs_5_.16, bf16[2048,8192]{1,0:T(8,128)(2,1)} %refs_5_.16, bf16[2048,8192]{1,0:T(8,128)(2,1)} %refs_5_.16, ...), custom_call_target="tpu_custom_call" | custom-call | flops 67108864 | bytes 524288 | tf_op jit(solution)/shard_map/mixed_part/pallas_call | solution.py:214
  127.1 6.0 %collective-permute-done.15.refs_3_ = bf16[128,2048]{1,0:T(8,128)(2,1)S(1)} collective-permute-done((bf16[128,2048]{1,0:T(8,128)(2,1)S(1)}, bf16[128,2048]{1,0:T(8,128)(2,1)S(1)}, u32[]{:S(2)}, u32[]{:S(2)}) %collective-permute-start.15) | collective-permute-done | bytes 524320 | tf_op jit(solution)/shard_map/ppermute | solution.py:454
  133.1 5.6 %collective-permute-done.21 = bf16[4,256,128]{2,1,0:T(8,128)(2,1)S(1)} collective-permute-done((bf16[4,256,128]{2,1,0:T(8,128)(2,1)S(1)}, bf16[4,256,128]{2,1,0:T(8,128)(2,1)S(1)}, u32[]{:S(2)}, u32[]{:S(2)}) %collective-permute-start.21) | collective-permute-done | bytes 262176 | tf_op jit(solution)/shard_map/ppermute | solution.py:368
  138.7 4.0 %backward_filter.1 = (bf16[128,2048]{1,0:T(8,128)(2,1)}, bf16[128,2048]{1,0:T(8,128)(2,1)}) custom-call(bf16[128,2048]{1,0:T(8,128)(2,1)S(1)} %copy-done, bf16[128,2048]{1,0:T(8,128)(2,1)S(1)} %copy-done.1, bf16[128,2048]{1,0:T(8,128)(2,1)S(1)} %get-tuple-element.15.refs_2_.refs_3_, bf16[128,2048]{1,0:T(8,128)(2,1)S(1)} %collective-permute-done.15.refs_3_, ...), custom_call_target="tpu_custom_call" | custom-call | flops 62500000 | bytes 262144 | tf_op jit(solution)/shard_map/backward_filter/pallas_call | solution.py:110
  142.7 1.6 placed_blocks.1
  144.3 5.4 %mixed_part.4 = f32[128,2048]{1,0:T(8,128)S(1)} custom-call(s32[2]{0:T(128)S(1)} %pad_add_fusion.refs_0_.me_ref.ids_ref, bf16[128,2048]{1,0:T(8,128)(2,1)S(1)} %get-tuple-element.12.refs_1_.refs_0_, bf16[2048,8192]{1,0:T(8,128)(2,1)} %refs_5_.16, bf16[2048,8192]{1,0:T(8,128)(2,1)} %refs_5_.16, bf16[2048,8192]{1,0:T(8,128)(2,1)} %refs_5_.16, ...), custom_call_target="tpu_custom_call" | custom-call | flops 67108864 | bytes 524288 | tf_op jit(solution)/shard_map/mixed_part/pallas_call | solution.py:214
  149.8 8.8 %grad_weight.1 = bf16[2048,1024]{1,0:T(8,128)(2,1)} custom-call(s32[2]{0:T(128)S(1)} %pad_add_fusion.refs_0_.me_ref.ids_ref, s32[8,8]{1,0:T(8,128)S(1)} %copy-done.11, bf16[128,2048]{1,0:T(8,128)(2,1)S(1)} %get-tuple-element.12.refs_1_.refs_0_, bf16[128,2048]{1,0:T(8,128)(2,1)S(1)} %collective-permute-done.1.refs_6_.refs_1_, ...), custom_call_target="tpu_custom_call" | custom-call | flops 268435456 | bytes 786432 | tf_op jit(solution)/shard_map/grad_weight/pallas_call | solution.py:310
  (80 shorter events, 8.4 us)
Async XLA Ops:
  0.6 15.1 %collective-permute-start.4 = (bf16[128,2048]{1,0:T(8,128)(2,1)}, bf16[128,2048]{1,0:T(8,128)(2,1)S(1)}, u32[]{:S(2)}, u32[]{:S(2)}) collective-permute-start(bf16[128,2048]{1,0:T(8,128)(2,1)} %refs_0_.5), channel_id=1, source_target_pairs={{0,2},{1,3},{2,0},{3,1},{4,6},{5,7},{6,4},{7,5},{8,10},{9,11},{10,... | collective-permute-start | bytes 1572872 | tf_op jit(solution)/shard_map/ppermute | solution.py:368
  5.0 18.5 %collective-permute-start = (bf16[128,2048]{1,0:T(8,128)(2,1)S(1)}, bf16[128,2048]{1,0:T(8,128)(2,1)S(1)}, u32[]{:S(2)}, u32[]{:S(2)}) collective-permute-start(bf16[128,2048]{1,0:T(8,128)(2,1)S(1)} %multiply_convert_fusion), channel_id=1, source_target_pairs={{0,4},{4,8},{8,12},{12,16},{16,20},{20,24},{24,28},{1,5},{5,9},{9,... | collective-permute-start | bytes 1572872 | tf_op jit(solution)/shard_map/ppermute | solution.py:416
  8.4 20.6 %collective-permute-start.3 = (bf16[128,2048]{1,0:T(8,128)(2,1)}, bf16[128,2048]{1,0:T(8,128)(2,1)S(1)}, u32[]{:S(2)}, u32[]{:S(2)}) collective-permute-start(bf16[128,2048]{1,0:T(8,128)(2,1)} %refs_0_.5), channel_id=1, source_target_pairs={{0,1},{1,0},{2,3},{3,2},{4,5},{5,4},{6,7},{7,6},{8,9},{9,8},{10,11... | collective-permute-start | bytes 1572872 | tf_op jit(solution)/shard_map/ppermute | solution.py:368
  15.8 13.2 %collective-permute-start.5 = (bf16[128,2048]{1,0:T(8,128)(2,1)S(1)}, bf16[128,2048]{1,0:T(8,128)(2,1)S(1)}, u32[]{:S(2)}, u32[]{:S(2)}) collective-permute-start(bf16[128,2048]{1,0:T(8,128)(2,1)S(1)} %collective-permute-done.4.refs_2_.refs_1_), channel_id=1, source_target_pairs={{0,1},{1,0},{2,3},{3,2},{4,5},{5,4},{6,7},{7,6},{8,9},{9,8},{10,11... | collective-permute-start | bytes 1572872 | tf_op jit(solution)/shard_map/ppermute | solution.py:368
  16.9 6.6 %copy-start.6 = (bf16[2048,128]{1,0:T(8,128)(2,1)S(1)}, bf16[2048,128]{1,0:T(8,128)(2,1)}, u32[]{:S(2)}) copy-start(bf16[2048,128]{1,0:T(8,128)(2,1)} %refs_4_.18) | copy-start | bytes 1572868
  16.9 12.1 %copy-start.4 = (bf16[128,2048]{1,0:T(8,128)(2,1)S(1)}, bf16[128,2048]{1,0:T(8,128)(2,1)}, u32[]{:S(2)}) copy-start(bf16[128,2048]{1,0:T(8,128)(2,1)} %refs_0_.5) | copy-start | bytes 1572868
  26.9 24.3 %collective-permute-start.1 = (bf16[128,2048]{1,0:T(8,128)(2,1)S(1)}, bf16[128,2048]{1,0:T(8,128)(2,1)S(1)}, u32[]{:S(2)}, u32[]{:S(2)}) collective-permute-start(bf16[128,2048]{1,0:T(8,128)(2,1)S(1)} %get-tuple-element.12.refs_1_.refs_0_), channel_id=1, source_target_pairs={{0,8},{8,16},{16,24},{24,28},{28,20},{20,12},{12,4},{4,0},{1,9},{9... | collective-permute-start | bytes 1572872 | tf_op jit(solution)/shard_map/ppermute | solution.py:445
  28.8 22.4 %collective-permute-start.2 = (bf16[128,2048]{1,0:T(8,128)(2,1)S(1)}, bf16[128,2048]{1,0:T(8,128)(2,1)S(1)}, u32[]{:S(2)}, u32[]{:S(2)}) collective-permute-start(bf16[128,2048]{1,0:T(8,128)(2,1)S(1)} %get-tuple-element.12.refs_1_.refs_0_), channel_id=1, source_target_pairs={{8,0},{16,8},{24,16},{28,24},{20,28},{12,20},{4,12},{0,4},{9,1},{1... | collective-permute-start | bytes 1572872 | tf_op jit(solution)/shard_map/ppermute | solution.py:446
  29.7 21.5 %collective-permute-start.6 = (bf16[4,256,128]{2,1,0:T(8,128)(2,1)S(1)}, bf16[4,256,128]{2,1,0:T(8,128)(2,1)S(1)}, u32[]{:S(2)}, u32[]{:S(2)}) collective-permute-start(bf16[4,256,128]{2,1,0:T(8,128)(2,1)S(1)} %get-tuple-element.21), channel_id=1, source_target_pairs={{0,4},{4,0},{8,12},{12,8},{16,20},{20,16},{24,28},{28,24},{1,5},{5... | collective-permute-start | bytes 786440 | tf_op jit(solution)/shard_map/ppermute | solution.py:368
  44.2 7.0 %copy-start.9 = (bf16[2,128,256]{2,1,0:T(8,128)(2,1)S(1)}, bf16[2,128,256]{2,1,0:T(8,128)(2,1)}, u32[]{:S(2)}) copy-start(bf16[2,128,256]{2,1,0:T(8,128)(2,1)} %constant.22.clone.refs_5_) | copy-start | bytes 393220
  57.5 8.0 %collective-permute-start.16 = (bf16[4,256,128]{2,1,0:T(8,128)(2,1)S(1)}, bf16[4,256,128]{2,1,0:T(8,128)(2,1)S(1)}, u32[]{:S(2)}, u32[]{:S(2)}) collective-permute-start(bf16[4,256,128]{2,1,0:T(8,128)(2,1)S(1)} %slice.52), channel_id=1, source_target_pairs={{0,4},{4,0},{8,12},{12,8},{16,20},{20,16},{24,28},{28,24},{1,5},{5... | collective-permute-start | bytes 786440 | tf_op jit(solution)/shard_map/ppermute | solution.py:368
  58.0 11.3 %collective-permute-start.7 = (bf16[4,256,128]{2,1,0:T(8,128)(2,1)S(1)}, bf16[4,256,128]{2,1,0:T(8,128)(2,1)S(1)}, u32[]{:S(2)}, u32[]{:S(2)}) collective-permute-start(bf16[4,256,128]{2,1,0:T(8,128)(2,1)S(1)} %bitcast.37), channel_id=1, source_target_pairs={{0,8},{4,12},{8,0},{12,4},{16,24},{20,28},{24,16},{28,20},{1,9},{5... | collective-permute-start | bytes 786440 | tf_op jit(solution)/shard_map/ppermute | solution.py:368
  65.6 13.5 %collective-permute-start.17 = (bf16[2,256,128]{2,1,0:T(8,128)(2,1)S(1)}, bf16[2,256,128]{2,1,0:T(8,128)(2,1)S(1)}, u32[]{:S(2)}, u32[]{:S(2)}) collective-permute-start(bf16[2,256,128]{2,1,0:T(8,128)(2,1)S(1)} %slice.54), channel_id=1, source_target_pairs={{0,8},{4,12},{8,0},{12,4},{16,24},{20,28},{24,16},{28,20},{1,9},{5... | collective-permute-start | bytes 393224 | tf_op jit(solution)/shard_map/ppermute | solution.py:368
  67.2 15.0 %collective-permute-start.9 = (bf16[128,2048]{1,0:T(8,128)(2,1)S(1)}, bf16[128,2048]{1,0:T(8,128)(2,1)S(1)}, u32[]{:S(2)}, u32[]{:S(2)}) collective-permute-start(bf16[128,2048]{1,0:T(8,128)(2,1)S(1)} %collective-permute-done.1.refs_6_.refs_1_), channel_id=1, source_target_pairs={{0,8},{8,16},{16,24},{24,28},{28,20},{20,12},{12,4},{4,0},{1,9},{9... | collective-permute-start | bytes 1572872 | tf_op jit(solution)/shard_map/ppermute | solution.py:445
  67.7 33.0 %collective-permute-start.11 = (bf16[128,2048]{1,0:T(8,128)(2,1)S(1)}, bf16[128,2048]{1,0:T(8,128)(2,1)S(1)}, u32[]{:S(2)}, u32[]{:S(2)}) collective-permute-start(bf16[128,2048]{1,0:T(8,128)(2,1)S(1)} %collective-permute-done.2.refs_7_.refs_2_), channel_id=1, source_target_pairs={{8,0},{16,8},{24,16},{28,24},{20,28},{12,20},{4,12},{0,4},{9,1},{1... | collective-permute-start | bytes 1572872 | tf_op jit(solution)/shard_map/ppermute | solution.py:446
  79.0 41.4 %collective-permute-start.8 = (bf16[128,4096]{1,0:T(8,128)(2,1)S(1)}, bf16[128,4096]{1,0:T(8,128)(2,1)S(1)}, u32[]{:S(2)}, u32[]{:S(2)}) collective-permute-start(bf16[128,4096]{1,0:T(8,128)(2,1)S(1)} %mixed_part.3), channel_id=1, source_target_pairs={{0,1},{1,0},{2,3},{3,2},{4,5},{5,4},{6,7},{7,6},{8,9},{9,8},{10,11... | collective-permute-start | bytes 3145736 | tf_op jit(solution)/shard_map/ppermute | solution.py:368
  79.2 13.6 %collective-permute-start.18 = (bf16[1,256,128]{2,1,0:T(8,128)(2,1)S(1)}, bf16[1,256,128]{2,1,0:T(8,128)(2,1)S(1)}, u32[]{:S(2)}, u32[]{:S(2)}) collective-permute-start(bf16[1,256,128]{2,1,0:T(8,128)(2,1)S(1)} %slice.63), channel_id=1, source_target_pairs={{0,16},{4,20},{8,24},{12,28},{16,0},{20,4},{24,8},{28,12},{1,17},{... | collective-permute-start | bytes 196616 | tf_op jit(solution)/shard_map/ppermute | solution.py:368
  81.9 17.2 %collective-permute-start.13 = (bf16[4,256,128]{2,1,0:T(8,128)(2,1)S(1)}, bf16[4,256,128]{2,1,0:T(8,128)(2,1)S(1)}, u32[]{:S(2)}, u32[]{:S(2)}) collective-permute-start(bf16[4,256,128]{2,1,0:T(8,128)(2,1)S(1)} %fusion.3), channel_id=1, source_target_pairs={{0,16},{4,20},{8,24},{12,28},{16,0},{20,4},{24,8},{28,12},{1,17},{... | collective-permute-start | bytes 786440 | tf_op jit(solution)/shard_map/ppermute | solution.py:368
  82.3 35.4 %collective-permute-start.10 = (bf16[128,2048]{1,0:T(8,128)(2,1)S(1)}, bf16[128,2048]{1,0:T(8,128)(2,1)S(1)}, u32[]{:S(2)}, u32[]{:S(2)}) collective-permute-start(bf16[128,2048]{1,0:T(8,128)(2,1)S(1)} %collective-permute-done.9.refs_7_.refs_3_), channel_id=1, source_target_pairs={{0,8},{8,16},{16,24},{24,28},{28,20},{20,12},{12,4},{4,0},{1,9},{9... | collective-permute-start | bytes 1572872 | tf_op jit(solution)/shard_map/ppermute | solution.py:445
  92.8 9.4 %collective-permute-start.19 = (bf16[1,256,128]{2,1,0:T(8,128)(2,1)S(1)}, bf16[1,256,128]{2,1,0:T(8,128)(2,1)S(1)}, u32[]{:S(2)}, u32[]{:S(2)}) collective-permute-start(bf16[1,256,128]{2,1,0:T(8,128)(2,1)S(1)} %add_convert_fusion.3), channel_id=1, source_target_pairs={{0,16},{4,20},{8,24},{12,28},{16,0},{20,4},{24,8},{28,12},{1,17},{... | collective-permute-start | bytes 196616 | tf_op jit(solution)/shard_map/ppermute | solution.py:368
  99.1 21.3 %collective-permute-start.25 = (bf16[8,256,128]{2,1,0:T(8,128)(2,1)S(1)}, bf16[8,256,128]{2,1,0:T(8,128)(2,1)S(1)}, u32[]{:S(2)}, u32[]{:S(2)}) collective-permute-start(bf16[8,256,128]{2,1,0:T(8,128)(2,1)S(1)} %fusion.1.refs_9_), channel_id=1, source_target_pairs={{0,2},{1,3},{2,0},{3,1},{4,6},{5,7},{6,4},{7,5},{8,10},{9,11},{10,... | collective-permute-start | bytes 1572872 | tf_op jit(solution)/shard_map/ppermute | solution.py:368
  100.7 25.7 %collective-permute-start.12 = (bf16[128,2048]{1,0:T(8,128)(2,1)S(1)}, bf16[128,2048]{1,0:T(8,128)(2,1)S(1)}, u32[]{:S(2)}, u32[]{:S(2)}) collective-permute-start(bf16[128,2048]{1,0:T(8,128)(2,1)S(1)} %collective-permute-done.11.refs_8_.refs_4_), channel_id=1, source_target_pairs={{8,0},{16,8},{24,16},{28,24},{20,28},{12,20},{4,12},{0,4},{9,1},{1... | collective-permute-start | bytes 1572872 | tf_op jit(solution)/shard_map/ppermute | solution.py:446
  102.2 14.2 %collective-permute-start.20 = (bf16[2,256,128]{2,1,0:T(8,128)(2,1)S(1)}, bf16[2,256,128]{2,1,0:T(8,128)(2,1)S(1)}, u32[]{:S(2)}, u32[]{:S(2)}) collective-permute-start(bf16[2,256,128]{2,1,0:T(8,128)(2,1)S(1)} %get-tuple-element.23), channel_id=1, source_target_pairs={{0,8},{4,12},{8,0},{12,4},{16,24},{20,28},{24,16},{28,20},{1,9},{5... | collective-permute-start | bytes 393224 | tf_op jit(solution)/shard_map/ppermute | solution.py:368
  116.3 16.7 %collective-permute-start.15 = (bf16[128,2048]{1,0:T(8,128)(2,1)S(1)}, bf16[128,2048]{1,0:T(8,128)(2,1)S(1)}, u32[]{:S(2)}, u32[]{:S(2)}) collective-permute-start(bf16[128,2048]{1,0:T(8,128)(2,1)S(1)} %get-tuple-element.15.refs_2_.refs_3_), channel_id=1, source_target_pairs={{4,0},{8,4},{12,8},{16,12},{20,16},{24,20},{28,24},{5,1},{9,5},{13... | collective-permute-start | bytes 1572872 | tf_op jit(solution)/shard_map/ppermute | solution.py:454
  117.7 21.0 %copy-start.7 = (bf16[2048,128]{1,0:T(8,128)(2,1)S(1)}, bf16[2048,128]{1,0:T(8,128)(2,1)}, u32[]{:S(2)}) copy-start(bf16[2048,128]{1,0:T(8,128)(2,1)} %refs_4_.18) | copy-start | bytes 1572868
  117.7 21.0 %copy-start.8 = (bf16[2,128,256]{2,1,0:T(8,128)(2,1)S(1)}, bf16[2,128,256]{2,1,0:T(8,128)(2,1)}, u32[]{:S(2)}) copy-start(bf16[2,128,256]{2,1,0:T(8,128)(2,1)} %constant.21.clone.refs_6_) | copy-start | bytes 393220
  117.7 21.0 %collective-permute-start.21 = (bf16[4,256,128]{2,1,0:T(8,128)(2,1)S(1)}, bf16[4,256,128]{2,1,0:T(8,128)(2,1)S(1)}, u32[]{:S(2)}, u32[]{:S(2)}) collective-permute-start(bf16[4,256,128]{2,1,0:T(8,128)(2,1)S(1)} %bitcast.35), channel_id=1, source_target_pairs={{0,4},{4,0},{8,12},{12,8},{16,20},{20,16},{24,28},{28,24},{1,5},{5... | collective-permute-start | bytes 786440 | tf_op jit(solution)/shard_map/ppermute | solution.py:368
  120.4 29.3 %collective-permute-start.24 = (bf16[8,256,128]{2,1,0:T(8,128)(2,1)S(1)}, bf16[8,256,128]{2,1,0:T(8,128)(2,1)S(1)}, u32[]{:S(2)}, u32[]{:S(2)}) collective-permute-start(bf16[8,256,128]{2,1,0:T(8,128)(2,1)S(1)} %fusion.1.refs_9_), channel_id=1, source_target_pairs={{0,1},{1,0},{2,3},{3,2},{4,5},{5,4},{6,7},{7,6},{8,9},{9,8},{10,11... | collective-permute-start | bytes 1572872 | tf_op jit(solution)/shard_map/ppermute | solution.py:368
  120.4 29.3 %collective-permute-start.26 = (bf16[8,256,128]{2,1,0:T(8,128)(2,1)S(1)}, bf16[8,256,128]{2,1,0:T(8,128)(2,1)S(1)}, u32[]{:S(2)}, u32[]{:S(2)}) collective-permute-start(bf16[8,256,128]{2,1,0:T(8,128)(2,1)S(1)} %collective-permute-done.25.refs_11_), channel_id=1, source_target_pairs={{0,1},{1,0},{2,3},{3,2},{4,5},{5,4},{6,7},{7,6},{8,9},{9,8},{10,11... | collective-permute-start | bytes 1572872 | tf_op jit(solution)/shard_map/ppermute | solution.py:368
  126.4 32.2 %collective-permute-start.14 = (bf16[128,2048]{1,0:T(8,128)(2,1)S(1)}, bf16[128,2048]{1,0:T(8,128)(2,1)S(1)}, u32[]{:S(2)}, u32[]{:S(2)}) collective-permute-start(bf16[128,2048]{1,0:T(8,128)(2,1)S(1)} %mixed_part.5), channel_id=1, source_target_pairs={{0,2},{1,3},{2,0},{3,1},{4,6},{5,7},{6,4},{7,5},{8,10},{9,11},{10,... | collective-permute-start | bytes 1572872 | tf_op jit(solution)/shard_map/ppermute | solution.py:368
  133.1 16.7 %collective-permute-start.22 = (bf16[128,1024]{1,0:T(8,128)(2,1)S(1)}, bf16[128,1024]{1,0:T(8,128)(2,1)S(1)}, u32[]{:S(2)}, u32[]{:S(2)}) collective-permute-start(bf16[128,1024]{1,0:T(8,128)(2,1)S(1)} %slice.64), channel_id=1, source_target_pairs={{0,8},{8,16},{16,24},{24,28},{28,20},{20,12},{12,4},{4,0},{1,9},{9... | collective-permute-start | bytes 786440 | tf_op jit(solution)/shard_map/ppermute | solution.py:448
  138.7 11.1 %collective-permute-start.23 = (bf16[128,1024]{1,0:T(8,128)(2,1)S(1)}, bf16[128,1024]{1,0:T(8,128)(2,1)S(1)}, u32[]{:S(2)}, u32[]{:S(2)}) collective-permute-start(bf16[128,1024]{1,0:T(8,128)(2,1)S(1)} %slice.65), channel_id=1, source_target_pairs={{8,0},{16,8},{24,16},{28,24},{20,28},{12,20},{4,12},{0,4},{9,1},{1... | collective-permute-start | bytes 786440 | tf_op jit(solution)/shard_map/ppermute | solution.py:449
  (7 other events, 39.7 us)

commit v4 on v3

--- a/solution.py
+++ b/solution.py
@@ -90,6 +90,41 @@
         return body(*refs[:skip], *refs[skip + count :])
 
     return kernel
+
+
+def product_kernel(k_ref, v_ref, cot_ref, product_ref, held_ref):
+    product_ref[...] = (k_ref[...].astype(F32) * v_ref[...].astype(F32)).astype(BF16)
+    held_ref[...] = cot_ref[...]
+
+
+def product_of(key_proj, value_proj, cotangent):
+    whole = pl.BlockSpec(key_proj.shape, lambda i: (0, 0))
+    return pl.pallas_call(
+        product_kernel,
+        grid=(1,),
+        in_specs=[whole] * 3,
+        out_specs=[whole] * 2,
+        out_shape=[jax.ShapeDtypeStruct(key_proj.shape, BF16)] * 2,
+        compiler_params=pltpu.CompilerParams(vmem_limit_bytes=VMEM_BYTES),
+        cost_estimate=estimate(10**6, 2**20),
+        name="product",
+    )(key_proj, value_proj, cotangent)
+
+
+def held_back(block, after):
+    def nothing(*refs):
+        pass
+
+    anywhere = pl.BlockSpec(memory_space=pl.ANY)
+    return pl.pallas_call(
+        nothing,
+        in_specs=[anywhere] * (1 + len(after)),
+        out_specs=anywhere,
+        out_shape=jax.ShapeDtypeStruct(block.shape, block.dtype),
+        input_output_aliases={0: 0},
+        cost_estimate=estimate(0, 0),
+        name="held_back",
+    )(block, *after)
 
 
 def by_channel(kernel, arrays, kinds, outs, name, me=None, after=()):
@@ -126,21 +161,23 @@
     )(*([] if me is None else [me]), *arrays, *after)
 
 
-def grad_gated_kernel(kind, me_ref, cot_ref, *refs):
-    width = cot_ref.shape[1] // STREAMS
-    total = mm(refs[0][...], cot_ref[:, :width], NT)
-    for stream in range(1, STREAMS):
-        total = total + mm(refs[stream][...], cot_ref[:, stream * width : (stream + 1) * width], NT)
-    total = total.T
-    refs = refs[STREAMS:]
+def grad_gated_kernel(kind, me_ref, cot_ref, w_ref, *refs):
+    turned_ref = refs[-1]
+
+    @pl.when(pl.program_id(0) == 0)
+    def turn():
+        turned_ref[...] = cot_ref[...].T
+
+    total = mm(w_ref[...], turned_ref[...])
     if kind == "first":
-        refs[-1][...] = total
+        refs[-2][...] = total
         return
     total = total + refs[0][...]
     if kind == "middle":
-        refs[-1][...] = total
+        refs[-2][...] = total
         return
-    q_ref, filtered_ref, gq_ref, gf_ref = refs[1:]
+    total = total.T
+    q_ref, filtered_ref, gq_ref, gf_ref = refs[1:-1]
     gq_ref[...] = (total * filtered_ref[...]).astype(BF16)
     gf_ref[...] = (total * q_ref[...].astype(F32)).astype(BF16)
 
@@ -149,31 +186,31 @@
     length, width = cot.shape
     channels = weight.shape[0]
     tile = 512
-    row_spec = pl.BlockSpec((length, tile), lambda i, me: (0, i))
-    kinds = [BF16, BF16] if kind == "last" else [F32]
-    return pl.pallas_call(
-        ignoring(functools.partial(grad_gated_kernel, kind), len(after), 2 + STREAMS + len(arrays)),
+    by_token = pl.BlockSpec((length, tile), lambda i, me: (0, i))
+    by_channel_rows = pl.BlockSpec((tile, length), lambda i, me: (i, 0))
+    if kind == "last":
+        out_specs, out_shape = [by_token] * 2, [jax.ShapeDtypeStruct((length, channels), BF16)] * 2
+    else:
+        out_specs, out_shape = [by_channel_rows], [jax.ShapeDtypeStruct((channels, length), F32)]
+    return pl.pallas_call(
+        ignoring(functools.partial(grad_gated_kernel, kind), len(after), 3 + len(arrays)),
         grid_spec=pltpu.PrefetchScalarGridSpec(
             num_scalar_prefetch=1,
             grid=(channels // tile,),
             in_specs=[
                 pl.BlockSpec((length, width), lambda i, me: (0, 0)),
+                pl.BlockSpec((tile, width), lambda i, me: (i, me[1] ^ off)),
             ]
-            + [
-                pl.BlockSpec(
-                    (tile, width // STREAMS), lambda i, me, stream=stream: (i, (me[1] ^ off) * STREAMS + stream)
-                )
-                for stream in range(STREAMS)
-            ]
-            + [row_spec] * len(arrays)
+            + [by_channel_rows, by_token, by_token][: len(arrays)]
             + [pl.BlockSpec(memory_space=pl.ANY)] * len(after),
-            out_specs=[row_spec] * len(kinds),
+            out_specs=out_specs,
+            scratch_shapes=[pltpu.VMEM((width, length), BF16)],
         ),
-        out_shape=[jax.ShapeDtypeStruct((length, channels), dtype) for dtype in kinds],
+        out_shape=out_shape,
         compiler_params=pltpu.CompilerParams(vmem_limit_bytes=VMEM_BYTES),
         cost_estimate=estimate(2 * length * width * channels, 2 * width * channels),
         name="grad_gated_" + kind,
-    )(me, cot, *[weight] * STREAMS, *arrays, *after)
+    )(me, cot, weight, *arrays, *after)
 
 
 def mixed_kernel(adds, me_ref, gated_ref, *refs):
@@ -242,25 +279,26 @@
             )
 
 
-def pieces_of(me, cots, n_ctx):
+def pieces_of(me, cots, n_ctx, after):
     length, width = cots[0].shape
     piece = width // n_ctx
     rows = length * piece // 128
     if piece % 128:
         return pieces_by_slices(me, cots, n_ctx)
     return pl.pallas_call(
-        functools.partial(pieces_kernel, n_ctx // len(cots)),
+        ignoring(functools.partial(pieces_kernel, n_ctx // len(cots)), len(after), 1 + len(cots)),
         grid_spec=pltpu.PrefetchScalarGridSpec(
             num_scalar_prefetch=1,
             grid=(1,),
-            in_specs=[pl.BlockSpec((length, width), lambda i, me: (0, 0))] * len(cots),
+            in_specs=[pl.BlockSpec((length, width), lambda i, me: (0, 0))] * len(cots)
+            + [pl.BlockSpec(memory_space=pl.ANY)] * len(after),
             out_specs=pl.BlockSpec((n_ctx, rows, 128), lambda i, me: (0, 0, 0)),
         ),
         out_shape=jax.ShapeDtypeStruct((n_ctx, rows, 128), BF16),
         compiler_params=pltpu.CompilerParams(vmem_limit_bytes=VMEM_BYTES),
         cost_estimate=estimate(10**6, 2**20),
         name="pieces",
-    )(me, *cots)
+    )(me, *cots, *after)
 
 
 def pieces_by_slices(me, cots, n_ctx):
@@ -379,12 +417,42 @@
     return held
 
 
-def summed(partial):
-    sums = partial
-    for bit in bits_of(partial.shape[0]):
-        others = swap(sums[1::2], "ctx", bit)
-        sums = (sums[::2].astype(F32) + others.astype(F32)).astype(BF16)
-    return sums
+def halved_kernel(kept_ref, came_ref, next_ref, left_ref):
+    total = (kept_ref[...].astype(F32) + came_ref[...].astype(F32)).astype(BF16)
+    count = total.shape[0] // 2
+    for at in range(count):
+        left_ref[at] = total[2 * at]
+        next_ref[at] = total[2 * at + 1]
+
+
+def added_kernel(kept_ref, came_ref, out_ref):
+    out_ref[...] = (kept_ref[...].astype(F32) + came_ref[...].astype(F32)).astype(BF16)
+
+
+def added(kept, came, after):
+    count = kept.shape[0]
+    whole = pl.BlockSpec(kept.shape, lambda i: (0, 0, 0))
+    half = pl.BlockSpec((max(count // 2, 1),) + kept.shape[1:], lambda i: (0, 0, 0))
+    outs = 2 if count > 1 else 1
+    return pl.pallas_call(
+        ignoring(halved_kernel if count > 1 else added_kernel, len(after), 2),
+        grid=(1,),
+        in_specs=[whole, whole] + [pl.BlockSpec(memory_space=pl.ANY)] * len(after),
+        out_specs=[half] * outs,
+        out_shape=[jax.ShapeDtypeStruct(half.block_shape, BF16)] * outs,
+        compiler_params=pltpu.CompilerParams(vmem_limit_bytes=VMEM_BYTES),
+        cost_estimate=estimate(10**6, 2**20),
+        name="added",
+    )(kept, came, *after)
+
+
+def summed(partial, gates):
+    give, left = partial[1::2], partial[::2]
+    for step, bit in enumerate(bits_of(partial.shape[0])):
+        sums = added(left, swap(give, "ctx", bit), gates[step] if step < len(gates) else ())
+        if len(sums) == 2:
+            give, left = sums
+    return sums[0]
 
 
 def exchanged(pieces):
@@ -412,19 +480,19 @@
     me = jnp.stack([lax.axis_index("ctx"), lax.axis_index("chan")]).astype(jnp.int32)
     forward, late, early, lags = [jnp.asarray(m) for m in transforms(taps)]
 
-    product = (key_proj.astype(F32) * value_proj.astype(F32)).astype(BF16)
+    product, cotangent = product_of(key_proj, value_proj, cotangent)
     earlier = lax.ppermute(product, "ctx", [(i, i + 1) for i in range(n_ctx - 1)])
 
-    cots = gather_by_swaps(cotangent)
-    grad_gated = []
-    for off in range(n_chan - 1):
-        grad_gated = grad_gated_part("middle" if off else "first", me, cots[off], out_weight, off, grad_gated)
-        grad_gated = list(grad_gated)
-        if off == 0:
-            first = grad_gated
-
-    pieces = pieces_of(me, [cots[off] for off in range(n_chan)], n_ctx)
-    held, sources, stages = exchanged(pieces)
+    cots, turns = {0: cotangent, 1: swap(cotangent, "chan", 1)}, [0, 1]
+    for bit in reversed(bits_of(n_chan)[1:]):
+        cots.update({off ^ bit: swap(cots[off], "chan", bit) for off in list(cots) if off % 2 == 0})
+    sums = []
+    for off in turns:
+        sums = grad_gated_part("middle" if sums else "first", me, cots[off], out_weight, off, list(sums))
+    for off in [off for off in cots if off % 2 == 0 and off]:
+        cots[off] = held_back(cots[off], sums)
+        cots[off + 1] = swap(cots[off], "chan", 1)
+        turns += [off, off + 1]
 
     gated, filtered = by_channel(
         forward_kernel,
@@ -432,8 +500,13 @@
         "ttttcww",
         [("t", BF16), ("t", F32)],
         "forward_filter",
-        after=first,
+        after=sums,
     )
+    for off in turns[2:-1]:
+        sums = grad_gated_part("middle", me, cots[off], out_weight, off, list(sums), [gated])
+
+    pieces = pieces_of(me, [cots[off] for off in range(n_chan)], n_ctx, sums)
+    held, sources, stages = exchanged(pieces)
 
     order = cycle_of(n_ctx)
     ahead = [(order[i], order[(i + 1) % n_ctx]) for i in range(n_ctx)]
@@ -449,25 +522,9 @@
     far_high = lax.ppermute(from_ahead[:, half:], "ctx", behind)
 
     grad_query, grad_filtered = grad_gated_part(
-        "last", me, cots[n_chan - 1], out_weight, n_chan - 1, grad_gated + [query_proj, filtered], [pieces]
+        "last", me, cots[turns[-1]], out_weight, turns[-1], list(sums) + [query_proj, filtered], [pieces]
     )
     following = lax.ppermute(grad_filtered, "ctx", [(i + 1, i) for i in range(n_ctx - 1)])
-
-    received = []
-    left = list(range(n_chan))
-    for bit in bits_of(n_chan):
-        give = left[1::2]
-        left = left[::2]
-        stride = give[1] - give[0] if len(give) > 1 else 1
-        sums = [(array, ((give[0] - offs[0]) // step, stride // step)) for array, offs, step in received]
-        ring = min(len(received) + 1, n_ctx // 2 - 1)
-        part = mixed_part(
-            me, gated, out_weight, give, sums, BF16, blocks[2 * ring - 1 : 2 * ring + 1] + stages[ring : ring + 1]
-        )
-        received.append((swap(part, "chan", bit), [off ^ bit for off in give], stride))
-    last = received.pop()[0]
-    own = mixed_part(me, gated, out_weight, [0], [(array, (0, 1)) for array, offs, step in received], F32, blocks[-2:])
-    mixed = (own + last.astype(F32)).astype(BF16)
 
     direct = channels // n_ctx == 256
     tap_grad = by_channel(
@@ -477,17 +534,34 @@
         [("x" if direct else "c", BF16)],
         "tap_grad",
         me,
-        blocks[1:3] + stages[:1],
     )[0].reshape(n_ctx, -1, taps)
     if not direct:
         tap_grad = tap_grad[jnp.arange(n_ctx, dtype=jnp.int32) ^ me[0]]
-    grad_filters = placed_blocks(me, doubled(summed(tap_grad), "ctx"))
+
+    received, parts = [], []
+    left = list(range(n_chan))
+    for bit in bits_of(n_chan):
+        give = left[1::2]
+        left = left[::2]
+        stride = give[1] - give[0] if len(give) > 1 else 1
+        sums = [(array, ((give[0] - offs[0]) // step, stride // step)) for array, offs, step in received]
+        step = min(len(received), n_ctx // 2 - 2)
+        order_after = blocks[2 * step + 1 : 2 * step + 3] + stages[step : step + 1] + [tap_grad]
+        part = mixed_part(me, gated, out_weight, give, sums, BF16, order_after)
+        parts.append(part)
+        received.append((swap(part, "chan", bit), [off ^ bit for off in give], stride))
+    last = received.pop()[0]
+    own = mixed_part(me, gated, out_weight, [0], [(array, (0, 1)) for array, offs, step in received], F32, blocks[-2:])
+    mixed = (own + last.astype(F32)).astype(BF16)
+
+    grad_filters = placed_blocks(me, doubled(summed(tap_grad, [[part] for part in parts] + [[own]]), "ctx"))
     grad_key, grad_value = by_channel(
         backward_kernel,
         [key_proj, value_proj, grad_filtered, following, filters, forward, early],
         "ttttcww",
         [("t", BF16), ("t", BF16)],
         "backward_filter",
+        after=parts[-1:],
     )
 
     columns = gather_by_swaps(held)

time: 160 us -> 153 us (0.956)
  waiting for transfers between devices: 46.8 us -> 32.7 us
  local copies, waits for them, and re-layouts: 1.28 us -> 13.6 us
  starting transfers between devices: 36.2 us -> 31.1 us
    unnamed x24 -> x46, local copies, waits for them, and re-layouts: 1.1 us -> 13.4 us
    ppermute x17, waiting for transfers between devices: 40.8 us -> 29.5 us  [swap(): return lax.ppermute(block, axis, [(i, i ^ bit) for i in range(size)])]
    ppermute x17, starting transfers between devices: 26.2 us -> 18.1 us  [swap(): return lax.ppermute(block, axis, [(i, i ^ bit) for i in range(size)])]
    ppermute x1, waiting for transfers between devices: 6.02 us -> 0.01 us  [per_device(): lax.ppermute(grad_filtered, 'ctx', [(i + 1, i) for i in range(n_ctx - 1)])]
    ppermute x1, starting transfers between devices: 0.01 us -> 1.98 us  [per_device(): far_high = lax.ppermute(from_ahead[:, half:], 'ctx', behind)]
    ppermute x3, waiting for transfers between devices: 0.01 us -> 1.92 us  [per_device(): from_behind = lax.ppermute(from_behind, 'ctx', ahead)]
  transfers between devices with their start and end apart: 27 -> 27, of which waited for: 8 -> 9; matrix products, arithmetic and copies ran while one was open for 1% -> 1% of each run, Pallas kernels for 41% -> 41%
where the time goes in v4:
time: 153 us; the launch traced here: 152 us
  Pallas kernels  72.3 us (47%)
  waiting for transfers between devices  32.7 us (21%)
  starting transfers between devices  31.1 us (20%)
  local copies, waits for them, and re-layouts  13.6 us (9%)
    ppermute x17, waiting for transfers between devices, swap(): return lax.ppermute(block, axis, [(i, i ^ bit) for i in range(size)])  29.5 us
    pallas_call x4, Pallas kernels, grad_gated_part(): pl.pallas_call(ignoring(functools.partial(grad_gated_kernel, kind), len(a...  26 us
    pallas_call x3, Pallas kernels, mixed_part(): pl.pallas_call(ignoring(functools.partial(mixed_kernel, len(received)), l...  20.7 us
    ppermute x17, starting transfers between devices, swap(): return lax.ppermute(block, axis, [(i, i ^ bit) for i in range(size)])  18.1 us
    pallas_call x3, Pallas kernels, by_channel(): pl.pallas_call(body if me is None else lambda ids_ref, *refs: body(*refs)...  13.6 us
    unnamed x46, local copies, waits for them, and re-layouts  13.4 us
    pallas_call x1, Pallas kernels, grad_weight_of(): pl.pallas_call(functools.partial(weight_kernel, slots, parts, half), grid...  8.8 us
    ppermute x3, starting transfers between devices, per_device(): from_behind = lax.ppermute(from_behind, 'ctx', ahead)  3.64 us
  transfers between devices with their start and end apart: 27, of which 9 were waited for; matrix products, arithmetic and copies ran while one was open for 1% of the time, Pallas kernels for 41%

profile of v4, /device:TPU:0, one launch (start us, length us, event | category | flops | bytes accessed | tf_op | source)
XLA Modules:
  0.0 151.9 jit_solution(8990136911916745992)
XLA Ops:
  5.1 2.5 %collective-permute-start.4 = (bf16[128,2048]{1,0:T(8,128)(2,1)S(1)}, bf16[128,2048]{1,0:T(8,128)(2,1)S(1)}, u32[]{:S(2)}, u32[]{:S(2)}) collective-permute-start(bf16[128,2048]{1,0:T(8,128)(2,1)S(1)} %get-tuple-element.19.refs_1_), channel_id=1, source_target_pairs={{0,2},{1,3},{2,0},{3,1},{4,6},{5,7},{6,4},{7,5},{8,10},{9,11},{10,... | collective-permute-start | bytes 1572872 | tf_op jit(solution)/shard_map/ppermute | solution.py:406
  7.6 3.4 %collective-permute-start = (bf16[128,2048]{1,0:T(8,128)(2,1)}, bf16[128,2048]{1,0:T(8,128)(2,1)S(1)}, u32[]{:S(2)}, u32[]{:S(2)}) collective-permute-start(bf16[128,2048]{1,0:T(8,128)(2,1)} %get-tuple-element.18), channel_id=1, source_target_pairs={{0,4},{4,8},{8,12},{12,16},{16,20},{20,24},{24,28},{1,5},{5,9},{9,... | collective-permute-start | bytes 1572872 | tf_op jit(solution)/shard_map/ppermute | solution.py:484
  11.2 6.2 %grad_gated_first.1.refs_3_ = f32[2048,128]{1,0:T(8,128)S(1)} custom-call(s32[2]{0:T(128)S(1)} %pad_add_fusion.refs_0_.ids_ref.me_ref, bf16[128,2048]{1,0:T(8,128)(2,1)S(1)} %get-tuple-element.19.refs_1_, bf16[2048,8192]{1,0:T(8,128)(2,1)} %refs_5_.8), custom_call_target="tpu_custom_call" | custom-call | flops 67108864 | bytes 524288 | tf_op jit(solution)/shard_map/grad_gated_first/pallas_call | solution.py:195
  17.4 6.3 %grad_gated_middle.2.refs_7_.refs_1_.refs_3_ = f32[2048,128]{1,0:T(8,128)S(1)} custom-call(s32[2]{0:T(128)S(1)} %pad_add_fusion.refs_0_.ids_ref.me_ref, bf16[128,2048]{1,0:T(8,128)(2,1)S(1)} %collective-permute-done.1.refs_1_.refs_2_, bf16[2048,8192]{1,0:T(8,128)(2,1)} %refs_5_.8, f32[2048,128]{1,0:T(8,128)S(1)} %grad_gated_first.1.refs_3_), custom_call_target="tpu_custom_call" | custom-call | flops 67108864 | bytes 524288 | tf_op jit(solution)/shard_map/grad_gated_middle/pallas_call | solution.py:195
  26.3 1.2 copy-done.1
  30.6 3.3 %forward_filter.1 = (bf16[128,2048]{1,0:T(8,128)(2,1)S(1)}, f32[128,2048]{1,0:T(8,128)S(1)}) custom-call(bf16[128,2048]{1,0:T(8,128)(2,1)S(1)} %copy-done.11, bf16[128,2048]{1,0:T(8,128)(2,1)S(1)} %copy-done.4, bf16[128,2048]{1,0:T(8,128)(2,1)S(1)} %copy-done.6, bf16[128,2048]{1,0:T(8,128)(2,1)S(1)} %copy-done.16, bf16[2048,128]{1,0:T(8,128)(2,1)S(1)} %copy-done.13, ...), custom_call_target="tpu_custom_call" | custom-call | flops 62500000 | bytes 262144 | tf_op jit(solution)/shard_map/forward_filter/pallas_call | solution.py:145
  34.0 1.6 %collective-permute-start.2 = (bf16[128,2048]{1,0:T(8,128)(2,1)S(1)}, bf16[128,2048]{1,0:T(8,128)(2,1)S(1)}, u32[]{:S(2)}, u32[]{:S(2)}) collective-permute-start(bf16[128,2048]{1,0:T(8,128)(2,1)S(1)} %get-tuple-element.20.refs_4_.refs_1_.refs_0_), channel_id=1, source_target_pairs={{0,8},{8,16},{16,24},{24,28},{28,20},{20,12},{12,4},{4,0},{1,9},{9... | collective-permute-start | bytes 1572872 | tf_op jit(solution)/shard_map/ppermute | solution.py:518
  36.1 1.2 copy-done.2
  38.3 6.3 %grad_gated_middle.3.refs_5_.refs_3_ = f32[2048,128]{1,0:T(8,128)S(1)} custom-call(s32[2]{0:T(128)S(1)} %pad_add_fusion.refs_0_.ids_ref.me_ref, bf16[128,2048]{1,0:T(8,128)(2,1)S(1)} %copy-done.8, bf16[2048,8192]{1,0:T(8,128)(2,1)} %refs_5_.8, f32[2048,128]{1,0:T(8,128)S(1)} %copy-done.2, bf16[128,2048]{1,0:T(8,128)(2,1)S(1)} %get-tuple-element.20.refs_4_.refs_1_.refs_0_), custom_call_target="tpu_custom_call" | custom-call | flops 67108864 | bytes 524288 | tf_op jit(solution)/shard_map/grad_gated_middle/pallas_call | solution.py:195
  45.3 1.6 %collective-permute-start.6 = (bf16[4,256,128]{2,1,0:T(8,128)(2,1)S(1)}, bf16[4,256,128]{2,1,0:T(8,128)(2,1)S(1)}, u32[]{:S(2)}, u32[]{:S(2)}) collective-permute-start(bf16[4,256,128]{2,1,0:T(8,128)(2,1)S(1)} %get-tuple-element.37), channel_id=1, source_target_pairs={{0,4},{4,0},{8,12},{12,8},{16,20},{20,16},{24,28},{28,24},{1,5},{5... | collective-permute-start | bytes 786440 | tf_op jit(solution)/shard_map/ppermute | solution.py:406
  46.8 1.9 %collective-permute-done.2.refs_6_.refs_1_ = bf16[128,2048]{1,0:T(8,128)(2,1)S(1)} collective-permute-done((bf16[128,2048]{1,0:T(8,128)(2,1)S(1)}, bf16[128,2048]{1,0:T(8,128)(2,1)S(1)}, u32[]{:S(2)}, u32[]{:S(2)}) %collective-permute-start.2) | collective-permute-done | bytes 524320 | tf_op jit(solution)/shard_map/ppermute | solution.py:518
  48.8 1.2 collective-permute-start.8
  51.9 7.2 %grad_gated_last.1 = (bf16[128,2048]{1,0:T(8,128)(2,1)}, bf16[128,2048]{1,0:T(8,128)(2,1)S(1)}) custom-call(s32[2]{0:T(128)S(1)} %pad_add_fusion.refs_0_.ids_ref.me_ref, bf16[128,2048]{1,0:T(8,128)(2,1)S(1)} %collective-permute-done.5.refs_4_.refs_1_, bf16[2048,8192]{1,0:T(8,128)(2,1)} %refs_5_.8, f32[2048,128]{1,0:T(8,128)S(1)} %grad_gated_middle.3.refs_5_.refs_3_, ...), custom_call_target="tpu_custom_call" | custom-call | flops 67108864 | bytes 524288 | tf_op jit(solution)/shard_map/grad_gated_last/pallas_call | solution.py:195
  59.1 6.3 %tap_grad.1 = bf16[2048,128]{1,0:T(8,128)(2,1)S(1)} custom-call(s32[2]{0:T(128)S(1)} %pad_add_fusion.refs_0_.ids_ref.me_ref, bf16[128,2048]{1,0:T(8,128)(2,1)S(1)} %copy-done.4, bf16[128,2048]{1,0:T(8,128)(2,1)S(1)} %copy-done.6, bf16[128,2048]{1,0:T(8,128)(2,1)S(1)} %copy-done.17, bf16[128,2048]{1,0:T(8,128)(2,1)S(1)} %get-tuple-element.22.refs_3_.refs_2_, ...), custom_call_target="tpu_custom_call" | custom-call | flops 62500000 | bytes 262144 | tf_op jit(solution)/shard_map/tap_grad/pallas_call | solution.py:145
  65.4 9.8 %mixed_part.3.refs_2_ = bf16[128,4096]{1,0:T(8,128)(2,1)S(1)} custom-call(s32[2]{0:T(128)S(1)} %pad_add_fusion.refs_0_.ids_ref.me_ref, bf16[128,2048]{1,0:T(8,128)(2,1)S(1)} %get-tuple-element.20.refs_4_.refs_1_.refs_0_, bf16[2048,8192]{1,0:T(8,128)(2,1)} %refs_5_.8, bf16[2048,8192]{1,0:T(8,128)(2,1)} %refs_5_.8, bf16[2048,8192]{1,0:T(8,128)(2,1)} %refs_5_.8, ...), custom_call_target="tpu_custom_call" | custom-call | flops 134217728 | bytes 1048576 | tf_op jit(solution)/shard_map/mixed_part/pallas_call | solution.py:251
  75.4 1.2 collective-permute-start.12
  78.7 1.6 %collective-permute-start.15 = (bf16[4,256,128]{2,1,0:T(8,128)(2,1)S(1)}, bf16[4,256,128]{2,1,0:T(8,128)(2,1)S(1)}, u32[]{:S(2)}, u32[]{:S(2)}) collective-permute-start(bf16[4,256,128]{2,1,0:T(8,128)(2,1)S(1)} %get-tuple-element.34), channel_id=1, source_target_pairs={{0,4},{4,0},{8,12},{12,8},{16,20},{20,16},{24,28},{28,24},{1,5},{5... | collective-permute-start | bytes 786440 | tf_op jit(solution)/shard_map/ppermute | solution.py:406
  80.3 4.3 %collective-permute-done.12.refs_9_ = bf16[4,256,128]{2,1,0:T(8,128)(2,1)S(1)} collective-permute-done((bf16[4,256,128]{2,1,0:T(8,128)(2,1)S(1)}, bf16[4,256,128]{2,1,0:T(8,128)(2,1)S(1)}, u32[]{:S(2)}, u32[]{:S(2)}) %collective-permute-start.12) | collective-permute-done | bytes 262176 | tf_op jit(solution)/shard_map/ppermute | solution.py:406
  84.6 2.2 %collective-permute-start.23 = (bf16[4,256,128]{2,1,0:T(8,128)(2,1)S(1)}, bf16[4,256,128]{2,1,0:T(8,128)(2,1)S(1)}, u32[]{:S(2)}, u32[]{:S(2)}) collective-permute-start(bf16[4,256,128]{2,1,0:T(8,128)(2,1)S(1)} %get-tuple-element.31), channel_id=1, source_target_pairs={{0,16},{4,20},{8,24},{12,28},{16,0},{20,4},{24,8},{28,12},{1,17},{... | collective-permute-start | bytes 786440 | tf_op jit(solution)/shard_map/ppermute | solution.py:406
  86.8 9.4 %collective-permute-done.15.refs_1_ = bf16[4,256,128]{2,1,0:T(8,128)(2,1)S(1)} collective-permute-done((bf16[4,256,128]{2,1,0:T(8,128)(2,1)S(1)}, bf16[4,256,128]{2,1,0:T(8,128)(2,1)S(1)}, u32[]{:S(2)}, u32[]{:S(2)}) %collective-permute-start.15) | collective-permute-done | bytes 262176 | tf_op jit(solution)/shard_map/ppermute | solution.py:406
  96.4 5.5 %mixed_part.5.refs_7_.refs_2_ = bf16[128,2048]{1,0:T(8,128)(2,1)S(1)} custom-call(s32[2]{0:T(128)S(1)} %pad_add_fusion.refs_0_.ids_ref.me_ref, bf16[128,2048]{1,0:T(8,128)(2,1)S(1)} %get-tuple-element.20.refs_4_.refs_1_.refs_0_, bf16[2048,8192]{1,0:T(8,128)(2,1)} %refs_5_.8, bf16[2048,8192]{1,0:T(8,128)(2,1)} %refs_5_.8, bf16[2048,8192]{1,0:T(8,128)(2,1)} %refs_5_.8, ...), custom_call_target="tpu_custom_call" | custom-call | flops 67108864 | bytes 524288 | tf_op jit(solution)/shard_map/mixed_part/pallas_call | solution.py:251
  102.6 3.7 %collective-permute-start.17 = (bf16[1,256,128]{2,1,0:T(8,128)(2,1)S(1)}, bf16[1,256,128]{2,1,0:T(8,128)(2,1)S(1)}, u32[]{:S(2)}, u32[]{:S(2)}) collective-permute-start(bf16[1,256,128]{2,1,0:T(8,128)(2,1)S(1)} %get-tuple-element.29), channel_id=1, source_target_pairs={{0,16},{4,20},{8,24},{12,28},{16,0},{20,4},{24,8},{28,12},{1,17},{... | collective-permute-start | bytes 196616 | tf_op jit(solution)/shard_map/ppermute | solution.py:406
  106.3 1.3 collective-permute-start.14
  107.6 5.5 %mixed_part.4.refs_2_ = f32[128,2048]{1,0:T(8,128)S(1)} custom-call(s32[2]{0:T(128)S(1)} %pad_add_fusion.refs_0_.ids_ref.me_ref, bf16[128,2048]{1,0:T(8,128)(2,1)S(1)} %get-tuple-element.20.refs_4_.refs_1_.refs_0_, bf16[2048,8192]{1,0:T(8,128)(2,1)} %refs_5_.8, bf16[2048,8192]{1,0:T(8,128)(2,1)} %refs_5_.8, bf16[2048,8192]{1,0:T(8,128)(2,1)} %refs_5_.8, ...), custom_call_target="tpu_custom_call" | custom-call | flops 67108864 | bytes 524288 | tf_op jit(solution)/shard_map/mixed_part/pallas_call | solution.py:251
  113.1 3.4 %collective-permute-start.18 = (bf16[1,256,128]{2,1,0:T(8,128)(2,1)S(1)}, bf16[1,256,128]{2,1,0:T(8,128)(2,1)S(1)}, u32[]{:S(2)}, u32[]{:S(2)}) collective-permute-start(bf16[1,256,128]{2,1,0:T(8,128)(2,1)S(1)} %added.5), channel_id=1, source_target_pairs={{0,16},{4,20},{8,24},{12,28},{16,0},{20,4},{24,8},{28,12},{1,17},{... | collective-permute-start | bytes 196616 | tf_op jit(solution)/shard_map/ppermute | solution.py:406
  117.2 7.8 %collective-permute-done.18 = bf16[1,256,128]{2,1,0:T(8,128)(2,1)S(1)} collective-permute-done((bf16[1,256,128]{2,1,0:T(8,128)(2,1)S(1)}, bf16[1,256,128]{2,1,0:T(8,128)(2,1)S(1)}, u32[]{:S(2)}, u32[]{:S(2)}) %collective-permute-start.18) | collective-permute-done | bytes 65568 | tf_op jit(solution)/shard_map/ppermute | solution.py:406
  125.7 4.4 %collective-permute-done.19 = bf16[2,256,128]{2,1,0:T(8,128)(2,1)S(1)} collective-permute-done((bf16[2,256,128]{2,1,0:T(8,128)(2,1)S(1)}, bf16[2,256,128]{2,1,0:T(8,128)(2,1)S(1)}, u32[]{:S(2)}, u32[]{:S(2)}) %collective-permute-start.19) | collective-permute-done | bytes 131104 | tf_op jit(solution)/shard_map/ppermute | solution.py:406
  130.4 4.0 %backward_filter.1 = (bf16[128,2048]{1,0:T(8,128)(2,1)}, bf16[128,2048]{1,0:T(8,128)(2,1)}) custom-call(bf16[128,2048]{1,0:T(8,128)(2,1)S(1)} %copy-done.4, bf16[128,2048]{1,0:T(8,128)(2,1)S(1)} %copy-done.6, bf16[128,2048]{1,0:T(8,128)(2,1)S(1)} %get-tuple-element.22.refs_3_.refs_2_, bf16[128,2048]{1,0:T(8,128)(2,1)S(1)} %collective-permute-done.14.refs_3_, ...), custom_call_target="tpu_custom_call" | custom-call | flops 62500000 | bytes 262144 | tf_op jit(solution)/shard_map/backward_filter/pallas_call | solution.py:145
  134.4 2.0 %collective-permute-start.22 = (bf16[128,1024]{1,0:T(8,128)(2,1)S(1)}, bf16[128,1024]{1,0:T(8,128)(2,1)S(1)}, u32[]{:S(2)}, u32[]{:S(2)}) collective-permute-start(bf16[128,1024]{1,0:T(8,128)(2,1)S(1)} %slice.43), channel_id=1, source_target_pairs={{8,0},{16,8},{24,16},{28,24},{20,28},{12,20},{4,12},{0,4},{9,1},{1... | collective-permute-start | bytes 786440 | tf_op jit(solution)/shard_map/ppermute | solution.py:522
  136.4 2.9 %collective-permute-done.20 = bf16[4,256,128]{2,1,0:T(8,128)(2,1)S(1)} collective-permute-done((bf16[4,256,128]{2,1,0:T(8,128)(2,1)S(1)}, bf16[4,256,128]{2,1,0:T(8,128)(2,1)S(1)}, u32[]{:S(2)}, u32[]{:S(2)}) %collective-permute-start.20) | collective-permute-done | bytes 262176 | tf_op jit(solution)/shard_map/ppermute | solution.py:406
  139.4 1.6 %placed_blocks.1 = f32[2048,128]{1,0:T(8,128)} custom-call(s32[2]{0:T(128)S(1)} %pad_add_fusion.refs_0_.ids_ref.me_ref, bf16[8,256,128]{2,1,0:T(8,128)(2,1)S(1)} %bitcast.31), custom_call_target="tpu_custom_call" | custom-call | flops 62500 | bytes 131072 | tf_op jit(solution)/shard_map/placed_blocks/pallas_call | solution.py:371
  143.1 8.8 %grad_weight.1 = bf16[2048,1024]{1,0:T(8,128)(2,1)} custom-call(s32[2]{0:T(128)S(1)} %pad_add_fusion.refs_0_.ids_ref.me_ref, s32[8,8]{1,0:T(8,128)S(1)} %copy-done.22, bf16[128,2048]{1,0:T(8,128)(2,1)S(1)} %get-tuple-element.20.refs_4_.refs_1_.refs_0_, bf16[128,2048]{1,0:T(8,128)(2,1)S(1)} %collective-permute-done.2.refs_6_.refs_1_, ...), custom_call_target="tpu_custom_call" | custom-call | flops 268435456 | bytes 786432 | tf_op jit(solution)/shard_map/grad_weight/pallas_call | solution.py:348
  (102 shorter events, 21.4 us)
Async XLA Ops:
  4.7 12.7 %collective-permute-start.1 = (bf16[128,2048]{1,0:T(8,128)(2,1)S(1)}, bf16[128,2048]{1,0:T(8,128)(2,1)S(1)}, u32[]{:S(2)}, u32[]{:S(2)}) collective-permute-start(bf16[128,2048]{1,0:T(8,128)(2,1)S(1)} %get-tuple-element.19.refs_1_), channel_id=1, source_target_pairs={{0,1},{1,0},{2,3},{3,2},{4,5},{5,4},{6,7},{7,6},{8,9},{9,8},{10,11... | collective-permute-start | bytes 1572872 | tf_op jit(solution)/shard_map/ppermute | solution.py:406
  5.1 19.5 %collective-permute-start.4 = (bf16[128,2048]{1,0:T(8,128)(2,1)S(1)}, bf16[128,2048]{1,0:T(8,128)(2,1)S(1)}, u32[]{:S(2)}, u32[]{:S(2)}) collective-permute-start(bf16[128,2048]{1,0:T(8,128)(2,1)S(1)} %get-tuple-element.19.refs_1_), channel_id=1, source_target_pairs={{0,2},{1,3},{2,0},{3,1},{4,6},{5,7},{6,4},{7,5},{8,10},{9,11},{10,... | collective-permute-start | bytes 1572872 | tf_op jit(solution)/shard_map/ppermute | solution.py:406
  7.6 17.8 %collective-permute-start = (bf16[128,2048]{1,0:T(8,128)(2,1)}, bf16[128,2048]{1,0:T(8,128)(2,1)S(1)}, u32[]{:S(2)}, u32[]{:S(2)}) collective-permute-start(bf16[128,2048]{1,0:T(8,128)(2,1)} %get-tuple-element.18), channel_id=1, source_target_pairs={{0,4},{4,8},{8,12},{12,16},{16,20},{20,24},{24,28},{1,5},{5,9},{9,... | collective-permute-start | bytes 1572872 | tf_op jit(solution)/shard_map/ppermute | solution.py:484
  25.5 19.1 %collective-permute-start.5 = (bf16[128,2048]{1,0:T(8,128)(2,1)}, bf16[128,2048]{1,0:T(8,128)(2,1)S(1)}, u32[]{:S(2)}, u32[]{:S(2)}) collective-permute-start(bf16[128,2048]{1,0:T(8,128)(2,1)} %held_back.1.refs_1_.refs_3_), channel_id=1, source_target_pairs={{0,1},{1,0},{2,3},{3,2},{4,5},{5,4},{6,7},{7,6},{8,9},{9,8},{10,11... | collective-permute-start | bytes 1572872 | tf_op jit(solution)/shard_map/ppermute | solution.py:406
  34.0 14.8 %collective-permute-start.2 = (bf16[128,2048]{1,0:T(8,128)(2,1)S(1)}, bf16[128,2048]{1,0:T(8,128)(2,1)S(1)}, u32[]{:S(2)}, u32[]{:S(2)}) collective-permute-start(bf16[128,2048]{1,0:T(8,128)(2,1)S(1)} %get-tuple-element.20.refs_4_.refs_1_.refs_0_), channel_id=1, source_target_pairs={{0,8},{8,16},{16,24},{24,28},{28,20},{20,12},{12,4},{4,0},{1,9},{9... | collective-permute-start | bytes 1572872 | tf_op jit(solution)/shard_map/ppermute | solution.py:518
  35.6 14.3 %collective-permute-start.3 = (bf16[128,2048]{1,0:T(8,128)(2,1)S(1)}, bf16[128,2048]{1,0:T(8,128)(2,1)S(1)}, u32[]{:S(2)}, u32[]{:S(2)}) collective-permute-start(bf16[128,2048]{1,0:T(8,128)(2,1)S(1)} %get-tuple-element.20.refs_4_.refs_1_.refs_0_), channel_id=1, source_target_pairs={{8,0},{16,8},{24,16},{28,24},{20,28},{12,20},{4,12},{0,4},{9,1},{1... | collective-permute-start | bytes 1572872 | tf_op jit(solution)/shard_map/ppermute | solution.py:519
  38.3 20.8 %copy-start.17 = (bf16[128,2048]{1,0:T(8,128)(2,1)S(1)}, bf16[128,2048]{1,0:T(8,128)(2,1)}, u32[]{:S(2)}) copy-start(bf16[128,2048]{1,0:T(8,128)(2,1)} %copy-done.15) | copy-start | bytes 1572868
  38.3 20.8 %copy-start.20 = (bf16[2,128,256]{2,1,0:T(8,128)(2,1)S(1)}, bf16[2,128,256]{2,1,0:T(8,128)(2,1)}, u32[]{:S(2)}) copy-start(bf16[2,128,256]{2,1,0:T(8,128)(2,1)} %constant.22.clone.refs_5_) | copy-start | bytes 393220
  45.3 20.1 %collective-permute-start.6 = (bf16[4,256,128]{2,1,0:T(8,128)(2,1)S(1)}, bf16[4,256,128]{2,1,0:T(8,128)(2,1)S(1)}, u32[]{:S(2)}, u32[]{:S(2)}) collective-permute-start(bf16[4,256,128]{2,1,0:T(8,128)(2,1)S(1)} %get-tuple-element.37), channel_id=1, source_target_pairs={{0,4},{4,0},{8,12},{12,8},{16,20},{20,16},{24,28},{28,24},{1,5},{5... | collective-permute-start | bytes 786440 | tf_op jit(solution)/shard_map/ppermute | solution.py:406
  48.8 27.9 %collective-permute-start.8 = (bf16[128,2048]{1,0:T(8,128)(2,1)S(1)}, bf16[128,2048]{1,0:T(8,128)(2,1)S(1)}, u32[]{:S(2)}, u32[]{:S(2)}) collective-permute-start(bf16[128,2048]{1,0:T(8,128)(2,1)S(1)} %collective-permute-done.2.refs_6_.refs_1_), channel_id=1, source_target_pairs={{0,8},{8,16},{16,24},{24,28},{28,20},{20,12},{12,4},{4,0},{1,9},{9... | collective-permute-start | bytes 1572872 | tf_op jit(solution)/shard_map/ppermute | solution.py:518
  49.9 27.6 %collective-permute-start.10 = (bf16[128,2048]{1,0:T(8,128)(2,1)S(1)}, bf16[128,2048]{1,0:T(8,128)(2,1)S(1)}, u32[]{:S(2)}, u32[]{:S(2)}) collective-permute-start(bf16[128,2048]{1,0:T(8,128)(2,1)S(1)} %collective-permute-done.3.refs_7_.refs_2_), channel_id=1, source_target_pairs={{8,0},{16,8},{24,16},{28,24},{20,28},{12,20},{4,12},{0,4},{9,1},{1... | collective-permute-start | bytes 1572872 | tf_op jit(solution)/shard_map/ppermute | solution.py:519
  75.2 21.2 %collective-permute-start.7 = (bf16[128,4096]{1,0:T(8,128)(2,1)S(1)}, bf16[128,4096]{1,0:T(8,128)(2,1)S(1)}, u32[]{:S(2)}, u32[]{:S(2)}) collective-permute-start(bf16[128,4096]{1,0:T(8,128)(2,1)S(1)} %mixed_part.3.refs_2_), channel_id=1, source_target_pairs={{0,1},{1,0},{2,3},{3,2},{4,5},{5,4},{6,7},{7,6},{8,9},{9,8},{10,11... | collective-permute-start | bytes 3145736 | tf_op jit(solution)/shard_map/ppermute | solution.py:406
  75.4 9.2 %collective-permute-start.12 = (bf16[4,256,128]{2,1,0:T(8,128)(2,1)S(1)}, bf16[4,256,128]{2,1,0:T(8,128)(2,1)S(1)}, u32[]{:S(2)}, u32[]{:S(2)}) collective-permute-start(bf16[4,256,128]{2,1,0:T(8,128)(2,1)S(1)} %bitcast.37), channel_id=1, source_target_pairs={{0,8},{4,12},{8,0},{12,4},{16,24},{20,28},{24,16},{28,20},{1,9},{5... | collective-permute-start | bytes 786440 | tf_op jit(solution)/shard_map/ppermute | solution.py:406
  76.6 31.0 %collective-permute-start.9 = (bf16[128,2048]{1,0:T(8,128)(2,1)S(1)}, bf16[128,2048]{1,0:T(8,128)(2,1)S(1)}, u32[]{:S(2)}, u32[]{:S(2)}) collective-permute-start(bf16[128,2048]{1,0:T(8,128)(2,1)S(1)} %collective-permute-done.8.refs_7_.refs_3_), channel_id=1, source_target_pairs={{0,8},{8,16},{16,24},{24,28},{28,20},{20,12},{12,4},{4,0},{1,9},{9... | collective-permute-start | bytes 1572872 | tf_op jit(solution)/shard_map/ppermute | solution.py:518
  77.5 30.1 %collective-permute-start.11 = (bf16[128,2048]{1,0:T(8,128)(2,1)S(1)}, bf16[128,2048]{1,0:T(8,128)(2,1)S(1)}, u32[]{:S(2)}, u32[]{:S(2)}) collective-permute-start(bf16[128,2048]{1,0:T(8,128)(2,1)S(1)} %collective-permute-done.10.refs_8_.refs_4_), channel_id=1, source_target_pairs={{8,0},{16,8},{24,16},{28,24},{20,28},{12,20},{4,12},{0,4},{9,1},{1... | collective-permute-start | bytes 1572872 | tf_op jit(solution)/shard_map/ppermute | solution.py:519
  78.7 17.6 %collective-permute-start.15 = (bf16[4,256,128]{2,1,0:T(8,128)(2,1)S(1)}, bf16[4,256,128]{2,1,0:T(8,128)(2,1)S(1)}, u32[]{:S(2)}, u32[]{:S(2)}) collective-permute-start(bf16[4,256,128]{2,1,0:T(8,128)(2,1)S(1)} %get-tuple-element.34), channel_id=1, source_target_pairs={{0,4},{4,0},{8,12},{12,8},{16,20},{20,16},{24,28},{28,24},{1,5},{5... | collective-permute-start | bytes 786440 | tf_op jit(solution)/shard_map/ppermute | solution.py:406
  84.6 31.9 %collective-permute-start.23 = (bf16[4,256,128]{2,1,0:T(8,128)(2,1)S(1)}, bf16[4,256,128]{2,1,0:T(8,128)(2,1)S(1)}, u32[]{:S(2)}, u32[]{:S(2)}) collective-permute-start(bf16[4,256,128]{2,1,0:T(8,128)(2,1)S(1)} %get-tuple-element.31), channel_id=1, source_target_pairs={{0,16},{4,20},{8,24},{12,28},{16,0},{20,4},{24,8},{28,12},{1,17},{... | collective-permute-start | bytes 786440 | tf_op jit(solution)/shard_map/ppermute | solution.py:406
  96.3 6.2 %collective-permute-start.16 = (bf16[2,256,128]{2,1,0:T(8,128)(2,1)S(1)}, bf16[2,256,128]{2,1,0:T(8,128)(2,1)S(1)}, u32[]{:S(2)}, u32[]{:S(2)}) collective-permute-start(bf16[2,256,128]{2,1,0:T(8,128)(2,1)S(1)} %get-tuple-element.27), channel_id=1, source_target_pairs={{0,8},{4,12},{8,0},{12,4},{16,24},{20,28},{24,16},{28,20},{1,9},{5... | collective-permute-start | bytes 393224 | tf_op jit(solution)/shard_map/ppermute | solution.py:406
  102.6 27.8 %copy-start.14 = (bf16[2048,128]{1,0:T(8,128)(2,1)S(1)}, bf16[2048,128]{1,0:T(8,128)(2,1)}, u32[]{:S(2)}) copy-start(bf16[2048,128]{1,0:T(8,128)(2,1)} %refs_4_.12) | copy-start | bytes 1572868
  102.6 27.8 %copy-start.19 = (bf16[2,128,256]{2,1,0:T(8,128)(2,1)S(1)}, bf16[2,128,256]{2,1,0:T(8,128)(2,1)}, u32[]{:S(2)}) copy-start(bf16[2,128,256]{2,1,0:T(8,128)(2,1)} %constant.21.clone.refs_6_) | copy-start | bytes 393220
  102.6 40.5 %copy-start.22 = (s32[8,8]{1,0:T(8,128)S(1)}, s32[8,8]{1,0:T(8,128)}, u32[]{:S(2)}) copy-start(s32[8,8]{1,0:T(8,128)} %constant.23.clone.owner_ref) | copy-start | bytes 772
  102.6 10.5 %collective-permute-start.17 = (bf16[1,256,128]{2,1,0:T(8,128)(2,1)S(1)}, bf16[1,256,128]{2,1,0:T(8,128)(2,1)S(1)}, u32[]{:S(2)}, u32[]{:S(2)}) collective-permute-start(bf16[1,256,128]{2,1,0:T(8,128)(2,1)S(1)} %get-tuple-element.29), channel_id=1, source_target_pairs={{0,16},{4,20},{8,24},{12,28},{16,0},{20,4},{24,8},{28,12},{1,17},{... | collective-permute-start | bytes 196616 | tf_op jit(solution)/shard_map/ppermute | solution.py:406
  106.3 24.0 %collective-permute-start.14 = (bf16[128,2048]{1,0:T(8,128)(2,1)S(1)}, bf16[128,2048]{1,0:T(8,128)(2,1)S(1)}, u32[]{:S(2)}, u32[]{:S(2)}) collective-permute-start(bf16[128,2048]{1,0:T(8,128)(2,1)S(1)} %get-tuple-element.22.refs_3_.refs_2_), channel_id=1, source_target_pairs={{4,0},{8,4},{12,8},{16,12},{20,16},{24,20},{28,24},{5,1},{9,5},{13... | collective-permute-start | bytes 1572872 | tf_op jit(solution)/shard_map/ppermute | solution.py:527
  113.1 11.9 %collective-permute-start.18 = (bf16[1,256,128]{2,1,0:T(8,128)(2,1)S(1)}, bf16[1,256,128]{2,1,0:T(8,128)(2,1)S(1)}, u32[]{:S(2)}, u32[]{:S(2)}) collective-permute-start(bf16[1,256,128]{2,1,0:T(8,128)(2,1)S(1)} %added.5), channel_id=1, source_target_pairs={{0,16},{4,20},{8,24},{12,28},{16,0},{20,4},{24,8},{28,12},{1,17},{... | collective-permute-start | bytes 196616 | tf_op jit(solution)/shard_map/ppermute | solution.py:406
  116.6 17.8 %collective-permute-start.25 = (bf16[8,256,128]{2,1,0:T(8,128)(2,1)S(1)}, bf16[8,256,128]{2,1,0:T(8,128)(2,1)S(1)}, u32[]{:S(2)}, u32[]{:S(2)}) collective-permute-start(bf16[8,256,128]{2,1,0:T(8,128)(2,1)S(1)} %maximum_bitcast_fusion.refs_9_), channel_id=1, source_target_pairs={{0,2},{1,3},{2,0},{3,1},{4,6},{5,7},{6,4},{7,5},{8,10},{9,11},{10,... | collective-permute-start | bytes 1572872 | tf_op jit(solution)/shard_map/ppermute | solution.py:406
  125.0 5.0 %collective-permute-start.19 = (bf16[2,256,128]{2,1,0:T(8,128)(2,1)S(1)}, bf16[2,256,128]{2,1,0:T(8,128)(2,1)S(1)}, u32[]{:S(2)}, u32[]{:S(2)}) collective-permute-start(bf16[2,256,128]{2,1,0:T(8,128)(2,1)S(1)} %get-tuple-element.39), channel_id=1, source_target_pairs={{0,8},{4,12},{8,0},{12,4},{16,24},{20,28},{24,16},{28,20},{1,9},{5... | collective-permute-start | bytes 393224 | tf_op jit(solution)/shard_map/ppermute | solution.py:406
  125.1 15.9 %collective-permute-start.13 = (bf16[128,2048]{1,0:T(8,128)(2,1)S(1)}, bf16[128,2048]{1,0:T(8,128)(2,1)S(1)}, u32[]{:S(2)}, u32[]{:S(2)}) collective-permute-start(bf16[128,2048]{1,0:T(8,128)(2,1)S(1)} %mixed_part.5.refs_7_.refs_2_), channel_id=1, source_target_pairs={{0,2},{1,3},{2,0},{3,1},{4,6},{5,7},{6,4},{7,5},{8,10},{9,11},{10,... | collective-permute-start | bytes 1572872 | tf_op jit(solution)/shard_map/ppermute | solution.py:406
  130.1 9.2 %collective-permute-start.20 = (bf16[4,256,128]{2,1,0:T(8,128)(2,1)S(1)}, bf16[4,256,128]{2,1,0:T(8,128)(2,1)S(1)}, u32[]{:S(2)}, u32[]{:S(2)}) collective-permute-start(bf16[4,256,128]{2,1,0:T(8,128)(2,1)S(1)} %bitcast.35), channel_id=1, source_target_pairs={{0,4},{4,0},{8,12},{12,8},{16,20},{20,16},{24,28},{28,24},{1,5},{5... | collective-permute-start | bytes 786440 | tf_op jit(solution)/shard_map/ppermute | solution.py:406
  130.2 12.9 %collective-permute-start.24 = (bf16[8,256,128]{2,1,0:T(8,128)(2,1)S(1)}, bf16[8,256,128]{2,1,0:T(8,128)(2,1)S(1)}, u32[]{:S(2)}, u32[]{:S(2)}) collective-permute-start(bf16[8,256,128]{2,1,0:T(8,128)(2,1)S(1)} %maximum_bitcast_fusion.refs_9_), channel_id=1, source_target_pairs={{0,1},{1,0},{2,3},{3,2},{4,5},{5,4},{6,7},{7,6},{8,9},{9,8},{10,11... | collective-permute-start | bytes 1572872 | tf_op jit(solution)/shard_map/ppermute | solution.py:406
  130.3 11.8 %collective-permute-start.21 = (bf16[128,1024]{1,0:T(8,128)(2,1)S(1)}, bf16[128,1024]{1,0:T(8,128)(2,1)S(1)}, u32[]{:S(2)}, u32[]{:S(2)}) collective-permute-start(bf16[128,1024]{1,0:T(8,128)(2,1)S(1)} %slice.42), channel_id=1, source_target_pairs={{0,8},{8,16},{16,24},{24,28},{28,20},{20,12},{12,4},{4,0},{1,9},{9... | collective-permute-start | bytes 786440 | tf_op jit(solution)/shard_map/ppermute | solution.py:521
  134.4 8.7 %collective-permute-start.22 = (bf16[128,1024]{1,0:T(8,128)(2,1)S(1)}, bf16[128,1024]{1,0:T(8,128)(2,1)S(1)}, u32[]{:S(2)}, u32[]{:S(2)}) collective-permute-start(bf16[128,1024]{1,0:T(8,128)(2,1)S(1)} %slice.43), channel_id=1, source_target_pairs={{8,0},{16,8},{24,16},{28,24},{20,28},{12,20},{4,12},{0,4},{9,1},{1... | collective-permute-start | bytes 786440 | tf_op jit(solution)/shard_map/ppermute | solution.py:522
  139.3 3.8 %collective-permute-start.26 = (bf16[8,256,128]{2,1,0:T(8,128)(2,1)S(1)}, bf16[8,256,128]{2,1,0:T(8,128)(2,1)S(1)}, u32[]{:S(2)}, u32[]{:S(2)}) collective-permute-start(bf16[8,256,128]{2,1,0:T(8,128)(2,1)S(1)} %collective-permute-done.25.refs_11_), channel_id=1, source_target_pairs={{0,1},{1,0},{2,3},{3,2},{4,5},{5,4},{6,7},{7,6},{8,9},{9,8},{10,11... | collective-permute-start | bytes 1572872 | tf_op jit(solution)/shard_map/ppermute | solution.py:406
  (18 other events, 87.8 us)

commit v5 on v4

--- a/solution.py
+++ b/solution.py
@@ -11,7 +11,6 @@
 F32 = jnp.float32
 BF16 = jnp.bfloat16
 VMEM_BYTES = 40 * 2**20
-STREAMS = 4
 NT = (((1,), (1,)), ((), ()))
 TN = (((0,), (0,)), ((), ()))
 
@@ -81,8 +80,8 @@
     gv_ref[...] = (grad_product * k_ref[...].astype(F32)).astype(BF16)
 
 
-def estimate(flops, bytes_accessed):
-    return pl.CostEstimate(flops=flops // 16, bytes_accessed=bytes_accessed // 16, transcendentals=0)
+def estimate(micros):
+    return pl.CostEstimate(flops=int(micros * 10**9), bytes_accessed=0, transcendentals=0)
 
 
 def ignoring(body, count, skip):
@@ -90,41 +89,6 @@
         return body(*refs[:skip], *refs[skip + count :])
 
     return kernel
-
-
-def product_kernel(k_ref, v_ref, cot_ref, product_ref, held_ref):
-    product_ref[...] = (k_ref[...].astype(F32) * v_ref[...].astype(F32)).astype(BF16)
-    held_ref[...] = cot_ref[...]
-
-
-def product_of(key_proj, value_proj, cotangent):
-    whole = pl.BlockSpec(key_proj.shape, lambda i: (0, 0))
-    return pl.pallas_call(
-        product_kernel,
-        grid=(1,),
-        in_specs=[whole] * 3,
-        out_specs=[whole] * 2,
-        out_shape=[jax.ShapeDtypeStruct(key_proj.shape, BF16)] * 2,
-        compiler_params=pltpu.CompilerParams(vmem_limit_bytes=VMEM_BYTES),
-        cost_estimate=estimate(10**6, 2**20),
-        name="product",
-    )(key_proj, value_proj, cotangent)
-
-
-def held_back(block, after):
-    def nothing(*refs):
-        pass
-
-    anywhere = pl.BlockSpec(memory_space=pl.ANY)
-    return pl.pallas_call(
-        nothing,
-        in_specs=[anywhere] * (1 + len(after)),
-        out_specs=anywhere,
-        out_shape=jax.ShapeDtypeStruct(block.shape, block.dtype),
-        input_output_aliases={0: 0},
-        cost_estimate=estimate(0, 0),
-        name="held_back",
-    )(block, *after)
 
 
 def by_channel(kernel, arrays, kinds, outs, name, me=None, after=()):
@@ -156,111 +120,142 @@
             for kind, dtype in outs
         ],
         compiler_params=pltpu.CompilerParams(vmem_limit_bytes=VMEM_BYTES),
-        cost_estimate=estimate(10**9, 4 * 2**20),
+        cost_estimate=estimate(3),
         name=name,
     )(*([] if me is None else [me]), *arrays, *after)
 
 
-def grad_gated_kernel(kind, me_ref, cot_ref, w_ref, *refs):
-    turned_ref = refs[-1]
+def grad_gated_kernel(has_sum, me_ref, cot_ref, w_ref, *refs):
+    out_ref, turned_ref = refs[-2:]
 
     @pl.when(pl.program_id(0) == 0)
     def turn():
         turned_ref[...] = cot_ref[...].T
 
     total = mm(w_ref[...], turned_ref[...])
-    if kind == "first":
-        refs[-2][...] = total
-        return
-    total = total + refs[0][...]
-    if kind == "middle":
-        refs[-2][...] = total
-        return
-    total = total.T
-    q_ref, filtered_ref, gq_ref, gf_ref = refs[1:-1]
-    gq_ref[...] = (total * filtered_ref[...]).astype(BF16)
-    gf_ref[...] = (total * q_ref[...].astype(F32)).astype(BF16)
-
-
-def grad_gated_part(kind, me, cot, weight, off, arrays, after=()):
+    out_ref[...] = total + refs[0][...] if has_sum else total
+
+
+def grad_gated_part(me, cot, weight, off, sums):
     length, width = cot.shape
     channels = weight.shape[0]
     tile = 512
-    by_token = pl.BlockSpec((length, tile), lambda i, me: (0, i))
-    by_channel_rows = pl.BlockSpec((tile, length), lambda i, me: (i, 0))
-    if kind == "last":
-        out_specs, out_shape = [by_token] * 2, [jax.ShapeDtypeStruct((length, channels), BF16)] * 2
-    else:
-        out_specs, out_shape = [by_channel_rows], [jax.ShapeDtypeStruct((channels, length), F32)]
-    return pl.pallas_call(
-        ignoring(functools.partial(grad_gated_kernel, kind), len(after), 3 + len(arrays)),
+    rows = pl.BlockSpec((tile, length), lambda r, me: (r, 0))
+    return pl.pallas_call(
+        functools.partial(grad_gated_kernel, bool(sums)),
         grid_spec=pltpu.PrefetchScalarGridSpec(
             num_scalar_prefetch=1,
             grid=(channels // tile,),
             in_specs=[
-                pl.BlockSpec((length, width), lambda i, me: (0, 0)),
-                pl.BlockSpec((tile, width), lambda i, me: (i, me[1] ^ off)),
+                pl.BlockSpec((length, width), lambda r, me: (0, 0)),
+                pl.BlockSpec((tile, width), lambda r, me: (r, me[1] ^ off)),
             ]
-            + [by_channel_rows, by_token, by_token][: len(arrays)]
-            + [pl.BlockSpec(memory_space=pl.ANY)] * len(after),
-            out_specs=out_specs,
+            + [rows] * len(sums),
+            out_specs=[rows],
             scratch_shapes=[pltpu.VMEM((width, length), BF16)],
         ),
-        out_shape=out_shape,
-        compiler_params=pltpu.CompilerParams(vmem_limit_bytes=VMEM_BYTES),
-        cost_estimate=estimate(2 * length * width * channels, 2 * width * channels),
-        name="grad_gated_" + kind,
-    )(me, cot, weight, *arrays, *after)
-
-
-def mixed_kernel(adds, me_ref, gated_ref, *refs):
-    depth = gated_ref.shape[1] // STREAMS
-    total = mm(gated_ref[:, :depth], refs[0][...])
-    for stream in range(1, STREAMS):
-        total = total + mm(gated_ref[:, stream * depth : (stream + 1) * depth], refs[stream][...])
-    for ref in refs[STREAMS : STREAMS + adds]:
-        total = total + ref[...].astype(F32)
-    refs[-1][...] = total.astype(refs[-1].dtype)
-
-
-def mixed_part(me, gated, weight, offs, received, kind, after=()):
+        out_shape=[jax.ShapeDtypeStruct((channels, length), F32)],
+        compiler_params=pltpu.CompilerParams(vmem_limit_bytes=VMEM_BYTES),
+        cost_estimate=estimate(4),
+        name="grad_gated_part",
+    )(me, cot, weight, *sums)
+
+
+def both_kernel(count, with_grad, me_ref, w_ref, gated_ref, *refs):
+    block, step = pl.program_id(0), pl.program_id(1)
+    last = pl.num_programs(1) - 1
+    mixed_refs, held_ref = refs[-count - 1 : -1], refs[-1]
+    if with_grad:
+        cot_refs = refs[:count]
+        sum_ref, q_ref, filtered_ref, gq_ref, gf_ref = refs[count : count + 5]
+        mixed_refs = refs[count + 5 : 2 * count + 5]
+        held_ref, turned_ref, total_ref = refs[-3:]
+        for at in range(count):
+
+            @pl.when((block == at) & (step == 0))
+            def turn():
+                turned_ref[...] = cot_refs[at][...].T
+
+        total = mm(w_ref[...], turned_ref[...])
+        tile = total.shape[0]
+        rows = pl.ds(pl.multiple_of(step * tile, tile), tile)
+
+        @pl.when(block == 0)
+        def begin():
+            total_ref[rows, :] = sum_ref[...] + total
+
+        @pl.when(block > 0)
+        def add():
+            total_ref[rows, :] = total_ref[rows, :] + total
+
+        @pl.when(block == count - 1)
+        def finish():
+            grad = total_ref[rows, :].T
+            gq_ref[...] = (grad * filtered_ref[...]).astype(BF16)
+            gf_ref[...] = (grad * q_ref[...].astype(F32)).astype(BF16)
+
+    part = mm(gated_ref[...], w_ref[...])
+
+    @pl.when(step == 0)
+    def first():
+        held_ref[...] = part
+
+    @pl.when(step > 0)
+    def more():
+        held_ref[...] = held_ref[...] + part
+
+    for at in range(count):
+
+        @pl.when((block == at) & (step == last))
+        def give():
+            mixed_refs[at][...] = held_ref[...].astype(mixed_refs[at].dtype)
+
+
+def both_parts(me, gated, weight, offs, grads, after):
     length, channels = gated.shape
-    tile = 512
+    tile, count = 512, len(offs)
     steps = channels // tile
-
-    def column(b):
-        return offs[0] + b * (offs[1] - offs[0] if len(offs) > 1 else 0)
-
+    end = count - 1
+
+    def column(b, me):
+        place = me[1] ^ offs[0]
+        for at in range(1, count):
+            place = jnp.where(b == at, me[1] ^ offs[at], place)
+        return place
+
+    whole = pl.BlockSpec((length, channels), lambda b, r, me: (0, 0))
+    by_token = pl.BlockSpec((length, tile), lambda b, r, me: (0, jnp.where(b == end, r, 0)))
     in_specs = [
-        pl.BlockSpec((length, channels), lambda b, t, me: (0, 0)),
+        pl.BlockSpec((tile, channels), lambda b, r, me: (r, column(b, me))),
+        pl.BlockSpec((length, tile), lambda b, r, me: (0, r)),
     ]
-    in_specs += [
-        pl.BlockSpec(
-            (channels // STREAMS, tile),
-            lambda b, t, me, stream=stream: (stream, (me[1] ^ column(b)) * steps + t),
-        )
-        for stream in range(STREAMS)
+    out_specs, out_shape = [whole] * count, [
+        jax.ShapeDtypeStruct((length, channels), BF16 if off % 2 else F32) for off in offs
     ]
-    for unused, (start, stride) in received:
-        in_specs.append(
-            pl.BlockSpec(
-                (length, tile), lambda b, t, me, start=start, stride=stride: (0, (start + b * stride) * steps + t)
-            )
-        )
-    in_specs += [pl.BlockSpec(memory_space=pl.ANY)] * len(after)
-    return pl.pallas_call(
-        ignoring(functools.partial(mixed_kernel, len(received)), len(after), 2 + STREAMS + len(received)),
+    scratch = [pltpu.VMEM((length, channels), F32)]
+    arrays = [weight, gated]
+    if grads:
+        arrays += grads
+        in_specs += [whole] * count
+        in_specs += [pl.BlockSpec((tile, length), lambda b, r, me: (jnp.where(b == 0, r, steps - 1), 0))]
+        in_specs += [by_token] * 2
+        out_specs = [by_token] * 2 + out_specs
+        out_shape = [jax.ShapeDtypeStruct((length, channels), BF16)] * 2 + out_shape
+        scratch += [pltpu.VMEM((channels, length), BF16), pltpu.VMEM((channels, length), F32)]
+    return pl.pallas_call(
+        ignoring(functools.partial(both_kernel, count, bool(grads)), len(after), 1 + len(arrays)),
         grid_spec=pltpu.PrefetchScalarGridSpec(
             num_scalar_prefetch=1,
-            grid=(len(offs), steps),
-            in_specs=in_specs,
-            out_specs=pl.BlockSpec((length, tile), lambda b, t, me: (0, b * steps + t)),
-        ),
-        out_shape=jax.ShapeDtypeStruct((length, channels * len(offs)), kind),
-        compiler_params=pltpu.CompilerParams(vmem_limit_bytes=VMEM_BYTES),
-        cost_estimate=estimate(2 * length * channels * channels * len(offs), 2 * channels * channels * len(offs)),
-        name="mixed_part",
-    )(me, gated, *[weight] * STREAMS, *[array for array, unused in received], *after)
+            grid=(count, steps),
+            in_specs=in_specs + [pl.BlockSpec(memory_space=pl.ANY)] * len(after),
+            out_specs=out_specs,
+            scratch_shapes=scratch,
+        ),
+        out_shape=out_shape,
+        compiler_params=pltpu.CompilerParams(vmem_limit_bytes=VMEM_BYTES),
+        cost_estimate=estimate(3 * count),
+        name="grads_and_mixed" if grads else "mixed_part",
+    )(me, *arrays, *after)
 
 
 def pieces_kernel(per_chan, me_ref, *refs):
@@ -296,7 +291,7 @@
         ),
         out_shape=jax.ShapeDtypeStruct((n_ctx, rows, 128), BF16),
         compiler_params=pltpu.CompilerParams(vmem_limit_bytes=VMEM_BYTES),
-        cost_estimate=estimate(10**6, 2**20),
+        cost_estimate=estimate(0.5),
         name="pieces",
     )(me, *cots, *after)
 
@@ -355,7 +350,7 @@
         ),
         out_shape=jax.ShapeDtypeStruct((channels, piece * parts), BF16),
         compiler_params=pltpu.CompilerParams(vmem_limit_bytes=VMEM_BYTES),
-        cost_estimate=estimate(2 * slots * length * channels * piece * parts, 12 * 2**20),
+        cost_estimate=estimate(6),
         name="grad_weight",
     )(me, owners, *blocks, far_low, far_high, *cots)
 
@@ -378,7 +373,7 @@
         ),
         out_shape=jax.ShapeDtypeStruct((count * rows, width), F32),
         compiler_params=pltpu.CompilerParams(vmem_limit_bytes=VMEM_BYTES),
-        cost_estimate=estimate(10**6, 2 * 2**20),
+        cost_estimate=estimate(0.5),
         name="placed_blocks",
     )(me, blocks)
 
@@ -441,7 +436,7 @@
         out_specs=[half] * outs,
         out_shape=[jax.ShapeDtypeStruct(half.block_shape, BF16)] * outs,
         compiler_params=pltpu.CompilerParams(vmem_limit_bytes=VMEM_BYTES),
-        cost_estimate=estimate(10**6, 2**20),
+        cost_estimate=estimate(0.5),
         name="added",
     )(kept, came, *after)
 
@@ -480,19 +475,18 @@
     me = jnp.stack([lax.axis_index("ctx"), lax.axis_index("chan")]).astype(jnp.int32)
     forward, late, early, lags = [jnp.asarray(m) for m in transforms(taps)]
 
-    product, cotangent = product_of(key_proj, value_proj, cotangent)
+    product = (key_proj.astype(F32) * value_proj.astype(F32)).astype(BF16)
     earlier = lax.ppermute(product, "ctx", [(i, i + 1) for i in range(n_ctx - 1)])
 
-    cots, turns = {0: cotangent, 1: swap(cotangent, "chan", 1)}, [0, 1]
+    cots = {0: cotangent, 1: swap(cotangent, "chan", 1)}
     for bit in reversed(bits_of(n_chan)[1:]):
         cots.update({off ^ bit: swap(cots[off], "chan", bit) for off in list(cots) if off % 2 == 0})
-    sums = []
-    for off in turns:
-        sums = grad_gated_part("middle" if sums else "first", me, cots[off], out_weight, off, list(sums))
-    for off in [off for off in cots if off % 2 == 0 and off]:
-        cots[off] = held_back(cots[off], sums)
+    offs = sorted(off for off in cots if off % 2 == 0 and off)
+    for off in offs:
         cots[off + 1] = swap(cots[off], "chan", 1)
-        turns += [off, off + 1]
+    offs = sorted(offs + [off + 1 for off in offs])
+    sums = grad_gated_part(me, cots[0], out_weight, 0, [])
+    sums = grad_gated_part(me, cots[1], out_weight, 1, sums)
 
     gated, filtered = by_channel(
         forward_kernel,
@@ -502,8 +496,6 @@
         "forward_filter",
         after=sums,
     )
-    for off in turns[2:-1]:
-        sums = grad_gated_part("middle", me, cots[off], out_weight, off, list(sums), [gated])
 
     pieces = pieces_of(me, [cots[off] for off in range(n_chan)], n_ctx, sums)
     held, sources, stages = exchanged(pieces)
@@ -521,9 +513,10 @@
     far_low = lax.ppermute(from_behind[:, :half], "ctx", ahead)
     far_high = lax.ppermute(from_ahead[:, half:], "ctx", behind)
 
-    grad_query, grad_filtered = grad_gated_part(
-        "last", me, cots[turns[-1]], out_weight, turns[-1], list(sums) + [query_proj, filtered], [pieces]
+    grad_query, grad_filtered, *parts = both_parts(
+        me, gated, out_weight, offs, [cots[off] for off in offs] + list(sums) + [query_proj, filtered], [pieces]
     )
+    terms = dict(zip(offs, parts))
     following = lax.ppermute(grad_filtered, "ctx", [(i + 1, i) for i in range(n_ctx - 1)])
 
     direct = channels // n_ctx == 256
@@ -538,31 +531,24 @@
     if not direct:
         tap_grad = tap_grad[jnp.arange(n_ctx, dtype=jnp.int32) ^ me[0]]
 
-    received, parts = [], []
-    left = list(range(n_chan))
+    terms[1], terms[0] = both_parts(me, gated, out_weight, [1, 0], [], blocks[1:3] + stages[:1] + [tap_grad])
+    mixed_done = [terms[0]]
     for bit in bits_of(n_chan):
-        give = left[1::2]
-        left = left[::2]
-        stride = give[1] - give[0] if len(give) > 1 else 1
-        sums = [(array, ((give[0] - offs[0]) // step, stride // step)) for array, offs, step in received]
-        step = min(len(received), n_ctx // 2 - 2)
-        order_after = blocks[2 * step + 1 : 2 * step + 3] + stages[step : step + 1] + [tap_grad]
-        part = mixed_part(me, gated, out_weight, give, sums, BF16, order_after)
-        parts.append(part)
-        received.append((swap(part, "chan", bit), [off ^ bit for off in give], stride))
-    last = received.pop()[0]
-    own = mixed_part(me, gated, out_weight, [0], [(array, (0, 1)) for array, offs, step in received], F32, blocks[-2:])
-    mixed = (own + last.astype(F32)).astype(BF16)
-
-    grad_filters = placed_blocks(me, doubled(summed(tap_grad, [[part] for part in parts] + [[own]]), "ctx"))
+        for off in [off for off in sorted(terms, reverse=True) if off & bit]:
+            came = swap(terms.pop(off).astype(BF16), "chan", bit).astype(F32)
+            terms[off ^ bit] = terms[off ^ bit] + came
+    mixed = terms[0].astype(BF16)
+
     grad_key, grad_value = by_channel(
         backward_kernel,
         [key_proj, value_proj, grad_filtered, following, filters, forward, early],
         "ttttcww",
         [("t", BF16), ("t", BF16)],
         "backward_filter",
-        after=parts[-1:],
+        after=blocks[3:5] + stages[1:2] + mixed_done,
     )
+    gates = [mixed_done, [grad_key], blocks[5:7]]
+    grad_filters = placed_blocks(me, doubled(summed(tap_grad, gates), "ctx"))
 
     columns = gather_by_swaps(held)
     columns = [columns[off] for off in range(n_chan)]

time: 153 us -> 153 us (level)
  waiting for transfers between devices: 32.7 us -> 52.2 us
  local copies, waits for them, and re-layouts: 13.6 us -> 2.35 us
  Pallas kernels: 72.3 us -> 66.6 us
  starting transfers between devices: 31.1 us -> 28 us
  other arithmetic: 1.21 us -> 2.74 us
    ppermute x17 -> x18, waiting for transfers between devices: 29.5 us -> 48.5 us  [swap(): return lax.ppermute(block, axis, [(i, i ^ bit) for i in range(size)])]
    unnamed x46 -> x22, local copies, waits for them, and re-layouts: 13.4 us -> 2.13 us
    ppermute x17 -> x18, starting transfers between devices: 18.1 us -> 11.4 us  [swap(): return lax.ppermute(block, axis, [(i, i ^ bit) for i in range(size)])]
    pallas_call x9 -> x4, Pallas kernels: 47.6 us -> 41.8 us  [the longest x2 29.2 us: both_parts(): pl.pallas_call(ignoring(functools.partial(both_kernel, count, bool(grads)...]
    ppermute x3, starting transfers between devices: 3.64 us -> 5.48 us  [per_device(): from_behind = lax.ppermute(from_behind, 'ctx', ahead)]
    ppermute x3, waiting for transfers between devices: 1.92 us -> 3.74 us  [per_device(): from_behind = lax.ppermute(from_behind, 'ctx', ahead)]
    ppermute x3, starting transfers between devices: 2.52 us -> 4.28 us  [per_device(): from_ahead = lax.ppermute(from_ahead, 'ctx', behind)]
    convert_element_type x1 -> x3, other arithmetic: 0.9 us -> 2.43 us  [the longest x1 1.32 us: per_device(): product = (key_proj.astype(F32) * value_proj.astype(F32)).astype(BF16)]
  transfers between devices with their start and end apart: 27 -> 28, of which waited for: 9 -> 9; matrix products, arithmetic and copies ran while one was open for 1% -> 2% of each run, Pallas kernels for 41% -> 38%
where the time goes in v5:
time: 153 us
  Pallas kernels  66.6 us (44%)
  waiting for transfers between devices  52.2 us (34%)
  starting transfers between devices  28 us (18%)
  other arithmetic  2.74 us (2%)
  local copies, waits for them, and re-layouts  2.35 us (2%)
    ppermute x18, waiting for transfers between devices, swap(): return lax.ppermute(block, axis, [(i, i ^ bit) for i in range(size)])  48.5 us
    pallas_call x2, Pallas kernels, both_parts(): pl.pallas_call(ignoring(functools.partial(both_kernel, count, bool(grads)...  29.2 us
    pallas_call x3, Pallas kernels, by_channel(): pl.pallas_call(body if me is None else lambda ids_ref, *refs: body(*refs)...  13.6 us
    pallas_call x2, Pallas kernels, grad_gated_part(): pl.pallas_call(functools.partial(grad_gated_kernel, bool(sums)), grid_spe...  12.7 us
    ppermute x18, starting transfers between devices, swap(): return lax.ppermute(block, axis, [(i, i ^ bit) for i in range(size)])  11.4 us
    pallas_call x1, Pallas kernels, grad_weight_of(): pl.pallas_call(functools.partial(weight_kernel, slots, parts, half), grid...  8.78 us
    ppermute x3, starting transfers between devices, per_device(): from_behind = lax.ppermute(from_behind, 'ctx', ahead)  5.48 us
    ppermute x3, starting transfers between devices, per_device(): from_ahead = lax.ppermute(from_ahead, 'ctx', behind)  4.28 us
  transfers between devices with their start and end apart: 28, of which 9 were waited for; matrix products, arithmetic and copies ran while one was open for 2% of the time, Pallas kernels for 38%

profile of v5, /device:TPU:0, one launch (start us, length us, event | category | flops | bytes accessed | tf_op | source)
XLA Modules:
  0.0 152.9 jit_solution(12577281899397625135)
XLA Ops:
  1.1 2.6 %collective-permute-start.4 = (bf16[128,2048]{1,0:T(8,128)(2,1)}, bf16[128,2048]{1,0:T(8,128)(2,1)S(1)}, u32[]{:S(2)}, u32[]{:S(2)}) collective-permute-start(bf16[128,2048]{1,0:T(8,128)(2,1)} %refs_1_.7), channel_id=1, source_target_pairs={{0,2},{1,3},{2,0},{3,1},{4,6},{5,7},{6,4},{7,5},{8,10},{9,11},{10,... | collective-permute-start | bytes 1572872 | tf_op jit(solution)/shard_map/ppermute | solution.py:401
  3.7 1.3 multiply_convert_fusion
  5.0 3.5 %collective-permute-start = (bf16[128,2048]{1,0:T(8,128)(2,1)S(1)}, bf16[128,2048]{1,0:T(8,128)(2,1)S(1)}, u32[]{:S(2)}, u32[]{:S(2)}) collective-permute-start(bf16[128,2048]{1,0:T(8,128)(2,1)S(1)} %multiply_convert_fusion), channel_id=1, source_target_pairs={{0,4},{4,8},{8,12},{12,16},{16,20},{20,24},{24,28},{1,5},{5,9},{9,... | collective-permute-start | bytes 1572872 | tf_op jit(solution)/shard_map/ppermute | solution.py:479
  8.6 1.0 copy-done
  9.7 6.4 %grad_gated_part.2.refs_0_ = f32[2048,128]{1,0:T(8,128)S(1)} custom-call(s32[2]{0:T(128)S(1)} %pad_add_fusion.me_ref.refs_0_.ids_ref, bf16[128,2048]{1,0:T(8,128)(2,1)S(1)} %copy-done, bf16[2048,8192]{1,0:T(8,128)(2,1)} %refs_1_.10), custom_call_target="tpu_custom_call" | custom-call | flops 4000000000 | tf_op jit(solution)/shard_map/grad_gated_part/pallas_call | solution.py:144
  16.4 6.3 %grad_gated_part.3.refs_7_.refs_5_ = f32[2048,128]{1,0:T(8,128)S(1)} custom-call(s32[2]{0:T(128)S(1)} %pad_add_fusion.me_ref.refs_0_.ids_ref, bf16[128,2048]{1,0:T(8,128)(2,1)S(1)} %collective-permute-done.1.cot_ref.refs_2_, bf16[2048,8192]{1,0:T(8,128)(2,1)} %refs_1_.10, f32[2048,128]{1,0:T(8,128)S(1)} %grad_gated_part.2.refs_0_), custom_call_target="tpu_custom_call" | custom-call | flops 4000000000 | tf_op jit(solution)/shard_map/grad_gated_part/pallas_call | solution.py:144
  22.8 3.4 %forward_filter.1 = (bf16[128,2048]{1,0:T(8,128)(2,1)S(1)}, f32[128,2048]{1,0:T(8,128)S(1)}) custom-call(bf16[128,2048]{1,0:T(8,128)(2,1)S(1)} %copy-done.1, bf16[128,2048]{1,0:T(8,128)(2,1)S(1)} %copy-done.2, bf16[128,2048]{1,0:T(8,128)(2,1)S(1)} %copy-done.3, bf16[128,2048]{1,0:T(8,128)(2,1)S(1)} %collective-permute-done.refs_3_.refs_2_, ...), custom_call_target="tpu_custom_call" | custom-call | flops 3000000000 | tf_op jit(solution)/shard_map/forward_filter/pallas_call | solution.py:109
  26.2 1.9 %collective-permute-start.2 = (bf16[128,2048]{1,0:T(8,128)(2,1)S(1)}, bf16[128,2048]{1,0:T(8,128)(2,1)S(1)}, u32[]{:S(2)}, u32[]{:S(2)}) collective-permute-start(bf16[128,2048]{1,0:T(8,128)(2,1)S(1)} %get-tuple-element.20.refs_2_.refs_0_), channel_id=1, source_target_pairs={{0,8},{8,16},{16,24},{24,28},{28,20},{20,12},{12,4},{4,0},{1,9},{9... | collective-permute-start | bytes 1572872 | tf_op jit(solution)/shard_map/ppermute | solution.py:510
  28.9 18.7 %grads_and_mixed.1 = (bf16[128,2048]{1,0:T(8,128)(2,1)}, bf16[128,2048]{1,0:T(8,128)(2,1)S(1)}, f32[128,2048]{1,0:T(8,128)S(1)}, bf16[128,2048]{1,0:T(8,128)(2,1)S(1)}) custom-call(s32[2]{0:T(128)S(1)} %pad_add_fusion.me_ref.refs_0_.ids_ref, bf16[2048,8192]{1,0:T(8,128)(2,1)} %refs_1_.10, bf16[128,2048]{1,0:T(8,128)(2,1)S(1)} %get-tuple-element.20.refs_2_.refs_0_, ...), custom_call_target="tpu_custom_call" | custom-call | flops 6000000000 | tf_op jit(solution)/shard_map/grads_and_mixed/pallas_call | solution.py:245
  47.7 1.8 %collective-permute-start.6 = (bf16[4,256,128]{2,1,0:T(8,128)(2,1)S(1)}, bf16[4,256,128]{2,1,0:T(8,128)(2,1)S(1)}, u32[]{:S(2)}, u32[]{:S(2)}) collective-permute-start(bf16[4,256,128]{2,1,0:T(8,128)(2,1)S(1)} %get-tuple-element.41), channel_id=1, source_target_pairs={{0,4},{4,0},{8,12},{12,8},{16,20},{20,16},{24,28},{28,24},{1,5},{5... | collective-permute-start | bytes 786440 | tf_op jit(solution)/shard_map/ppermute | solution.py:401
  49.5 1.3 collective-permute-start.10
  50.8 6.3 %tap_grad.1 = bf16[2048,128]{1,0:T(8,128)(2,1)S(1)} custom-call(s32[2]{0:T(128)S(1)} %pad_add_fusion.me_ref.refs_0_.ids_ref, bf16[128,2048]{1,0:T(8,128)(2,1)S(1)} %copy-done.2, bf16[128,2048]{1,0:T(8,128)(2,1)S(1)} %copy-done.3, bf16[128,2048]{1,0:T(8,128)(2,1)S(1)} %collective-permute-done.refs_3_.refs_2_, ...), custom_call_target="tpu_custom_call" | custom-call | flops 3000000000 | tf_op jit(solution)/shard_map/tap_grad/pallas_call | solution.py:109
  57.1 2.7 %collective-permute-start.14 = (bf16[4,256,128]{2,1,0:T(8,128)(2,1)S(1)}, bf16[4,256,128]{2,1,0:T(8,128)(2,1)S(1)}, u32[]{:S(2)}, u32[]{:S(2)}) collective-permute-start(bf16[4,256,128]{2,1,0:T(8,128)(2,1)S(1)} %get-tuple-element.38), channel_id=1, source_target_pairs={{0,4},{4,0},{8,12},{12,8},{16,20},{20,16},{24,28},{28,24},{1,5},{5... | collective-permute-start | bytes 786440 | tf_op jit(solution)/shard_map/ppermute | solution.py:401
  59.8 1.6 %collective-permute-start.11 = (bf16[128,2048]{1,0:T(8,128)(2,1)S(1)}, bf16[128,2048]{1,0:T(8,128)(2,1)S(1)}, u32[]{:S(2)}, u32[]{:S(2)}) collective-permute-start(bf16[128,2048]{1,0:T(8,128)(2,1)S(1)} %collective-permute-done.2.refs_3_.refs_1_), channel_id=1, source_target_pairs={{0,8},{8,16},{16,24},{24,28},{28,20},{20,12},{12,4},{4,0},{1,9},{9... | collective-permute-start | bytes 1572872 | tf_op jit(solution)/shard_map/ppermute | solution.py:510
  61.4 5.9 %collective-permute-done.6.refs_5_ = bf16[4,256,128]{2,1,0:T(8,128)(2,1)S(1)} collective-permute-done((bf16[4,256,128]{2,1,0:T(8,128)(2,1)S(1)}, bf16[4,256,128]{2,1,0:T(8,128)(2,1)S(1)}, u32[]{:S(2)}, u32[]{:S(2)}) %collective-permute-start.6) | collective-permute-done | bytes 262176 | tf_op jit(solution)/shard_map/ppermute | solution.py:401
  67.3 2.5 %collective-permute-start.12 = (bf16[128,2048]{1,0:T(8,128)(2,1)S(1)}, bf16[128,2048]{1,0:T(8,128)(2,1)S(1)}, u32[]{:S(2)}, u32[]{:S(2)}) collective-permute-start(bf16[128,2048]{1,0:T(8,128)(2,1)S(1)} %collective-permute-done.3.refs_4_.refs_2_), channel_id=1, source_target_pairs={{8,0},{16,8},{24,16},{28,24},{20,28},{12,20},{4,12},{0,4},{9,1},{1... | collective-permute-start | bytes 1572872 | tf_op jit(solution)/shard_map/ppermute | solution.py:511
  69.8 10.5 %mixed_part.1 = (bf16[128,2048]{1,0:T(8,128)(2,1)S(1)}, f32[128,2048]{1,0:T(8,128)S(1)}) custom-call(s32[2]{0:T(128)S(1)} %pad_add_fusion.me_ref.refs_0_.ids_ref, bf16[2048,8192]{1,0:T(8,128)(2,1)} %refs_1_.10, bf16[128,2048]{1,0:T(8,128)(2,1)S(1)} %get-tuple-element.20.refs_2_.refs_0_, bf16[128,2048]{1,0:T(8,128)(2,1)S(1)} %collective-permute-done.2.refs_3_.refs_1_, ...), custom_call_target="tpu_custom_call" | custom-call | flops 6000000000 | tf_op jit(solution)/shard_map/mixed_part/pallas_call | solution.py:245
  80.8 3.7 %collective-permute-done.11.refs_7_.refs_3_ = bf16[128,2048]{1,0:T(8,128)(2,1)S(1)} collective-permute-done((bf16[128,2048]{1,0:T(8,128)(2,1)S(1)}, bf16[128,2048]{1,0:T(8,128)(2,1)S(1)}, u32[]{:S(2)}, u32[]{:S(2)}) %collective-permute-start.11) | collective-permute-done | bytes 524320 | tf_op jit(solution)/shard_map/ppermute | solution.py:510
  84.6 2.0 %collective-permute-start.17 = (bf16[128,2048]{1,0:T(8,128)(2,1)S(1)}, bf16[128,2048]{1,0:T(8,128)(2,1)S(1)}, u32[]{:S(2)}, u32[]{:S(2)}) collective-permute-start(bf16[128,2048]{1,0:T(8,128)(2,1)S(1)} %collective-permute-done.11.refs_7_.refs_3_), channel_id=1, source_target_pairs={{0,8},{8,16},{16,24},{24,28},{28,20},{20,12},{12,4},{4,0},{1,9},{9... | collective-permute-start | bytes 1572872 | tf_op jit(solution)/shard_map/ppermute | solution.py:510
  86.6 3.2 %collective-permute-done.13.refs_9_ = bf16[4,256,128]{2,1,0:T(8,128)(2,1)S(1)} collective-permute-done((bf16[4,256,128]{2,1,0:T(8,128)(2,1)S(1)}, bf16[4,256,128]{2,1,0:T(8,128)(2,1)S(1)}, u32[]{:S(2)}, u32[]{:S(2)}) %collective-permute-start.13) | collective-permute-done | bytes 262176 | tf_op jit(solution)/shard_map/ppermute | solution.py:401
  89.8 1.6 %collective-permute-start.18 = (bf16[128,2048]{1,0:T(8,128)(2,1)S(1)}, bf16[128,2048]{1,0:T(8,128)(2,1)S(1)}, u32[]{:S(2)}, u32[]{:S(2)}) collective-permute-start(bf16[128,2048]{1,0:T(8,128)(2,1)S(1)} %collective-permute-done.12.refs_8_.refs_4_), channel_id=1, source_target_pairs={{8,0},{16,8},{24,16},{28,24},{20,28},{12,20},{4,12},{0,4},{9,1},{1... | collective-permute-start | bytes 1572872 | tf_op jit(solution)/shard_map/ppermute | solution.py:511
  91.5 4.0 %backward_filter.1 = (bf16[128,2048]{1,0:T(8,128)(2,1)}, bf16[128,2048]{1,0:T(8,128)(2,1)}) custom-call(bf16[128,2048]{1,0:T(8,128)(2,1)S(1)} %copy-done.2, bf16[128,2048]{1,0:T(8,128)(2,1)S(1)} %copy-done.3, bf16[128,2048]{1,0:T(8,128)(2,1)S(1)} %get-tuple-element.22.refs_3_.refs_2_, bf16[128,2048]{1,0:T(8,128)(2,1)S(1)} %collective-permute-done.10.refs_3_, ...), custom_call_target="tpu_custom_call" | custom-call | flops 3000000000 | tf_op jit(solution)/shard_map/backward_filter/pallas_call | solution.py:109
  95.5 1.5 collective-permute-start.9
  98.0 17.5 %collective-permute-done.24 = bf16[4,256,128]{2,1,0:T(8,128)(2,1)S(1)} collective-permute-done((bf16[4,256,128]{2,1,0:T(8,128)(2,1)S(1)}, bf16[4,256,128]{2,1,0:T(8,128)(2,1)S(1)}, u32[]{:S(2)}, u32[]{:S(2)}) %collective-permute-start.24) | collective-permute-done | bytes 262176 | tf_op jit(solution)/shard_map/ppermute | solution.py:401
  115.5 5.1 %collective-permute-done.16.refs_1_ = bf16[1,256,128]{2,1,0:T(8,128)(2,1)S(1)} collective-permute-done((bf16[1,256,128]{2,1,0:T(8,128)(2,1)S(1)}, bf16[1,256,128]{2,1,0:T(8,128)(2,1)S(1)}, u32[]{:S(2)}, u32[]{:S(2)}) %collective-permute-start.16) | collective-permute-done | bytes 65568 | tf_op jit(solution)/shard_map/ppermute | solution.py:401
  120.7 1.8 %collective-permute-start.26 = (bf16[8,256,128]{2,1,0:T(8,128)(2,1)S(1)}, bf16[8,256,128]{2,1,0:T(8,128)(2,1)S(1)}, u32[]{:S(2)}, u32[]{:S(2)}) collective-permute-start(bf16[8,256,128]{2,1,0:T(8,128)(2,1)S(1)} %maximum_bitcast_fusion.refs_9_), channel_id=1, source_target_pairs={{0,2},{1,3},{2,0},{3,1},{4,6},{5,7},{6,4},{7,5},{8,10},{9,11},{10,... | collective-permute-start | bytes 1572872 | tf_op jit(solution)/shard_map/ppermute | solution.py:401
  122.5 5.2 %collective-permute-done.19 = bf16[1,256,128]{2,1,0:T(8,128)(2,1)S(1)} collective-permute-done((bf16[1,256,128]{2,1,0:T(8,128)(2,1)S(1)}, bf16[1,256,128]{2,1,0:T(8,128)(2,1)S(1)}, u32[]{:S(2)}, u32[]{:S(2)}) %collective-permute-start.19) | collective-permute-done | bytes 65568 | tf_op jit(solution)/shard_map/ppermute | solution.py:401
  128.0 4.8 %collective-permute-done.20 = bf16[2,256,128]{2,1,0:T(8,128)(2,1)S(1)} collective-permute-done((bf16[2,256,128]{2,1,0:T(8,128)(2,1)S(1)}, bf16[2,256,128]{2,1,0:T(8,128)(2,1)S(1)}, u32[]{:S(2)}, u32[]{:S(2)}) %collective-permute-start.20) | collective-permute-done | bytes 131104 | tf_op jit(solution)/shard_map/ppermute | solution.py:401
  132.9 2.1 %collective-permute-start.23 = (bf16[128,1024]{1,0:T(8,128)(2,1)S(1)}, bf16[128,1024]{1,0:T(8,128)(2,1)S(1)}, u32[]{:S(2)}, u32[]{:S(2)}) collective-permute-start(bf16[128,1024]{1,0:T(8,128)(2,1)S(1)} %slice.43), channel_id=1, source_target_pairs={{8,0},{16,8},{24,16},{28,24},{20,28},{12,20},{4,12},{0,4},{9,1},{1... | collective-permute-start | bytes 786440 | tf_op jit(solution)/shard_map/ppermute | solution.py:514
  136.1 6.3 %collective-permute-done.21 = bf16[4,256,128]{2,1,0:T(8,128)(2,1)S(1)} collective-permute-done((bf16[4,256,128]{2,1,0:T(8,128)(2,1)S(1)}, bf16[4,256,128]{2,1,0:T(8,128)(2,1)S(1)}, u32[]{:S(2)}, u32[]{:S(2)}) %collective-permute-start.21) | collective-permute-done | bytes 262176 | tf_op jit(solution)/shard_map/ppermute | solution.py:401
  142.5 1.6 %placed_blocks.1 = f32[2048,128]{1,0:T(8,128)} custom-call(s32[2]{0:T(128)S(1)} %pad_add_fusion.me_ref.refs_0_.ids_ref, bf16[8,256,128]{2,1,0:T(8,128)(2,1)S(1)} %bitcast.31), custom_call_target="tpu_custom_call" | custom-call | flops 500000000 | tf_op jit(solution)/shard_map/placed_blocks/pallas_call | solution.py:366
  144.1 8.8 %grad_weight.1 = bf16[2048,1024]{1,0:T(8,128)(2,1)} custom-call(s32[2]{0:T(128)S(1)} %pad_add_fusion.me_ref.refs_0_.ids_ref, s32[8,8]{1,0:T(8,128)S(1)} %copy-done.10, bf16[128,2048]{1,0:T(8,128)(2,1)S(1)} %get-tuple-element.20.refs_2_.refs_0_, bf16[128,2048]{1,0:T(8,128)(2,1)S(1)} %collective-permute-done.2.refs_3_.refs_1_, ...), custom_call_target="tpu_custom_call" | custom-call | flops 6000000000 | tf_op jit(solution)/shard_map/grad_weight/pallas_call | solution.py:343
  (77 shorter events, 5.2 us)
Async XLA Ops:
  0.6 15.8 %collective-permute-start.1 = (bf16[128,2048]{1,0:T(8,128)(2,1)}, bf16[128,2048]{1,0:T(8,128)(2,1)S(1)}, u32[]{:S(2)}, u32[]{:S(2)}) collective-permute-start(bf16[128,2048]{1,0:T(8,128)(2,1)} %refs_1_.7), channel_id=1, source_target_pairs={{0,1},{1,0},{2,3},{3,2},{4,5},{5,4},{6,7},{7,6},{8,9},{9,8},{10,11... | collective-permute-start | bytes 1572872 | tf_op jit(solution)/shard_map/ppermute | solution.py:401
  1.1 15.3 %collective-permute-start.4 = (bf16[128,2048]{1,0:T(8,128)(2,1)}, bf16[128,2048]{1,0:T(8,128)(2,1)S(1)}, u32[]{:S(2)}, u32[]{:S(2)}) collective-permute-start(bf16[128,2048]{1,0:T(8,128)(2,1)} %refs_1_.7), channel_id=1, source_target_pairs={{0,2},{1,3},{2,0},{3,1},{4,6},{5,7},{6,4},{7,5},{8,10},{9,11},{10,... | collective-permute-start | bytes 1572872 | tf_op jit(solution)/shard_map/ppermute | solution.py:401
  5.0 17.7 %collective-permute-start = (bf16[128,2048]{1,0:T(8,128)(2,1)S(1)}, bf16[128,2048]{1,0:T(8,128)(2,1)S(1)}, u32[]{:S(2)}, u32[]{:S(2)}) collective-permute-start(bf16[128,2048]{1,0:T(8,128)(2,1)S(1)} %multiply_convert_fusion), channel_id=1, source_target_pairs={{0,4},{4,8},{8,12},{12,16},{16,20},{20,24},{24,28},{1,5},{5,9},{9,... | collective-permute-start | bytes 1572872 | tf_op jit(solution)/shard_map/ppermute | solution.py:479
  9.6 13.1 %copy-start.6 = (bf16[2,256,256]{2,1,0:T(8,128)(2,1)S(1)}, bf16[2,256,256]{2,1,0:T(8,128)(2,1)}, u32[]{:S(2)}) copy-start(bf16[2,256,256]{2,1,0:T(8,128)(2,1)} %constant.19.clone.refs_5_.refs_4_) | copy-start | bytes 786436
  16.4 11.8 %collective-permute-start.5 = (bf16[128,2048]{1,0:T(8,128)(2,1)S(1)}, bf16[128,2048]{1,0:T(8,128)(2,1)S(1)}, u32[]{:S(2)}, u32[]{:S(2)}) collective-permute-start(bf16[128,2048]{1,0:T(8,128)(2,1)S(1)} %collective-permute-done.4.refs_3_), channel_id=1, source_target_pairs={{0,1},{1,0},{2,3},{3,2},{4,5},{5,4},{6,7},{7,6},{8,9},{9,8},{10,11... | collective-permute-start | bytes 1572872 | tf_op jit(solution)/shard_map/ppermute | solution.py:401
  22.7 28.1 %copy-start.8 = (bf16[2,128,256]{2,1,0:T(8,128)(2,1)S(1)}, bf16[2,128,256]{2,1,0:T(8,128)(2,1)}, u32[]{:S(2)}) copy-start(bf16[2,128,256]{2,1,0:T(8,128)(2,1)} %constant.22.clone.refs_5_) | copy-start | bytes 393220
  26.2 30.9 %collective-permute-start.2 = (bf16[128,2048]{1,0:T(8,128)(2,1)S(1)}, bf16[128,2048]{1,0:T(8,128)(2,1)S(1)}, u32[]{:S(2)}, u32[]{:S(2)}) collective-permute-start(bf16[128,2048]{1,0:T(8,128)(2,1)S(1)} %get-tuple-element.20.refs_2_.refs_0_), channel_id=1, source_target_pairs={{0,8},{8,16},{16,24},{24,28},{28,20},{20,12},{12,4},{4,0},{1,9},{9... | collective-permute-start | bytes 1572872 | tf_op jit(solution)/shard_map/ppermute | solution.py:510
  28.1 31.8 %collective-permute-start.3 = (bf16[128,2048]{1,0:T(8,128)(2,1)S(1)}, bf16[128,2048]{1,0:T(8,128)(2,1)S(1)}, u32[]{:S(2)}, u32[]{:S(2)}) collective-permute-start(bf16[128,2048]{1,0:T(8,128)(2,1)S(1)} %get-tuple-element.20.refs_2_.refs_0_), channel_id=1, source_target_pairs={{8,0},{16,8},{24,16},{28,24},{20,28},{12,20},{4,12},{0,4},{9,1},{1... | collective-permute-start | bytes 1572872 | tf_op jit(solution)/shard_map/ppermute | solution.py:511
  47.6 43.9 %copy-start.7 = (bf16[2,128,256]{2,1,0:T(8,128)(2,1)S(1)}, bf16[2,128,256]{2,1,0:T(8,128)(2,1)}, u32[]{:S(2)}) copy-start(bf16[2,128,256]{2,1,0:T(8,128)(2,1)} %constant.21.clone.refs_6_) | copy-start | bytes 393220
  47.6 33.0 %collective-permute-start.8 = (bf16[128,2048]{1,0:T(8,128)(2,1)S(1)}, bf16[128,2048]{1,0:T(8,128)(2,1)S(1)}, u32[]{:S(2)}, u32[]{:S(2)}) collective-permute-start(bf16[128,2048]{1,0:T(8,128)(2,1)S(1)} %get-tuple-element.26), channel_id=1, source_target_pairs={{0,1},{1,0},{2,3},{3,2},{4,5},{5,4},{6,7},{7,6},{8,9},{9,8},{10,11... | collective-permute-start | bytes 1572872 | tf_op jit(solution)/shard_map/ppermute | solution.py:401
  47.7 19.6 %collective-permute-start.6 = (bf16[4,256,128]{2,1,0:T(8,128)(2,1)S(1)}, bf16[4,256,128]{2,1,0:T(8,128)(2,1)S(1)}, u32[]{:S(2)}, u32[]{:S(2)}) collective-permute-start(bf16[4,256,128]{2,1,0:T(8,128)(2,1)S(1)} %get-tuple-element.41), channel_id=1, source_target_pairs={{0,4},{4,0},{8,12},{12,8},{16,20},{20,16},{24,28},{28,24},{1,5},{5... | collective-permute-start | bytes 786440 | tf_op jit(solution)/shard_map/ppermute | solution.py:401
  49.5 41.9 %collective-permute-start.10 = (bf16[128,2048]{1,0:T(8,128)(2,1)S(1)}, bf16[128,2048]{1,0:T(8,128)(2,1)S(1)}, u32[]{:S(2)}, u32[]{:S(2)}) collective-permute-start(bf16[128,2048]{1,0:T(8,128)(2,1)S(1)} %get-tuple-element.22.refs_3_.refs_2_), channel_id=1, source_target_pairs={{4,0},{8,4},{12,8},{16,12},{20,16},{24,20},{28,24},{5,1},{9,5},{13... | collective-permute-start | bytes 1572872 | tf_op jit(solution)/shard_map/ppermute | solution.py:520
  57.1 87.0 %copy-start.10 = (s32[8,8]{1,0:T(8,128)S(1)}, s32[8,8]{1,0:T(8,128)}, u32[]{:S(2)}) copy-start(s32[8,8]{1,0:T(8,128)} %constant.23.clone.owner_ref) | copy-start | bytes 772
  57.1 23.3 %collective-permute-start.14 = (bf16[4,256,128]{2,1,0:T(8,128)(2,1)S(1)}, bf16[4,256,128]{2,1,0:T(8,128)(2,1)S(1)}, u32[]{:S(2)}, u32[]{:S(2)}) collective-permute-start(bf16[4,256,128]{2,1,0:T(8,128)(2,1)S(1)} %get-tuple-element.38), channel_id=1, source_target_pairs={{0,4},{4,0},{8,12},{12,8},{16,20},{20,16},{24,28},{28,24},{1,5},{5... | collective-permute-start | bytes 786440 | tf_op jit(solution)/shard_map/ppermute | solution.py:401
  59.8 24.7 %collective-permute-start.11 = (bf16[128,2048]{1,0:T(8,128)(2,1)S(1)}, bf16[128,2048]{1,0:T(8,128)(2,1)S(1)}, u32[]{:S(2)}, u32[]{:S(2)}) collective-permute-start(bf16[128,2048]{1,0:T(8,128)(2,1)S(1)} %collective-permute-done.2.refs_3_.refs_1_), channel_id=1, source_target_pairs={{0,8},{8,16},{16,24},{24,28},{28,20},{20,12},{12,4},{4,0},{1,9},{9... | collective-permute-start | bytes 1572872 | tf_op jit(solution)/shard_map/ppermute | solution.py:510
  67.3 17.2 %collective-permute-start.12 = (bf16[128,2048]{1,0:T(8,128)(2,1)S(1)}, bf16[128,2048]{1,0:T(8,128)(2,1)S(1)}, u32[]{:S(2)}, u32[]{:S(2)}) collective-permute-start(bf16[128,2048]{1,0:T(8,128)(2,1)S(1)} %collective-permute-done.3.refs_4_.refs_2_), channel_id=1, source_target_pairs={{8,0},{16,8},{24,16},{28,24},{20,28},{12,20},{4,12},{0,4},{9,1},{1... | collective-permute-start | bytes 1572872 | tf_op jit(solution)/shard_map/ppermute | solution.py:511
  80.4 52.5 %collective-permute-start.7 = (bf16[128,2048]{1,0:T(8,128)(2,1)S(1)}, bf16[128,2048]{1,0:T(8,128)(2,1)S(1)}, u32[]{:S(2)}, u32[]{:S(2)}) collective-permute-start(bf16[128,2048]{1,0:T(8,128)(2,1)S(1)} %get-tuple-element.24), channel_id=1, source_target_pairs={{0,1},{1,0},{2,3},{3,2},{4,5},{5,4},{6,7},{7,6},{8,9},{9,8},{10,11... | collective-permute-start | bytes 1572872 | tf_op jit(solution)/shard_map/ppermute | solution.py:401
  80.6 9.2 %collective-permute-start.13 = (bf16[4,256,128]{2,1,0:T(8,128)(2,1)S(1)}, bf16[4,256,128]{2,1,0:T(8,128)(2,1)S(1)}, u32[]{:S(2)}, u32[]{:S(2)}) collective-permute-start(bf16[4,256,128]{2,1,0:T(8,128)(2,1)S(1)} %bitcast.36), channel_id=1, source_target_pairs={{0,8},{4,12},{8,0},{12,4},{16,24},{20,28},{24,16},{28,20},{1,9},{5... | collective-permute-start | bytes 786440 | tf_op jit(solution)/shard_map/ppermute | solution.py:401
  84.6 10.9 %collective-permute-start.15 = (bf16[2,256,128]{2,1,0:T(8,128)(2,1)S(1)}, bf16[2,256,128]{2,1,0:T(8,128)(2,1)S(1)}, u32[]{:S(2)}, u32[]{:S(2)}) collective-permute-start(bf16[2,256,128]{2,1,0:T(8,128)(2,1)S(1)} %get-tuple-element.31), channel_id=1, source_target_pairs={{0,8},{4,12},{8,0},{12,4},{16,24},{20,28},{24,16},{28,20},{1,9},{5... | collective-permute-start | bytes 393224 | tf_op jit(solution)/shard_map/ppermute | solution.py:401
  84.6 37.9 %collective-permute-start.17 = (bf16[128,2048]{1,0:T(8,128)(2,1)S(1)}, bf16[128,2048]{1,0:T(8,128)(2,1)S(1)}, u32[]{:S(2)}, u32[]{:S(2)}) collective-permute-start(bf16[128,2048]{1,0:T(8,128)(2,1)S(1)} %collective-permute-done.11.refs_7_.refs_3_), channel_id=1, source_target_pairs={{0,8},{8,16},{16,24},{24,28},{28,20},{20,12},{12,4},{4,0},{1,9},{9... | collective-permute-start | bytes 1572872 | tf_op jit(solution)/shard_map/ppermute | solution.py:510
  89.8 32.6 %collective-permute-start.18 = (bf16[128,2048]{1,0:T(8,128)(2,1)S(1)}, bf16[128,2048]{1,0:T(8,128)(2,1)S(1)}, u32[]{:S(2)}, u32[]{:S(2)}) collective-permute-start(bf16[128,2048]{1,0:T(8,128)(2,1)S(1)} %collective-permute-done.12.refs_8_.refs_4_), channel_id=1, source_target_pairs={{8,0},{16,8},{24,16},{28,24},{20,28},{12,20},{4,12},{0,4},{9,1},{1... | collective-permute-start | bytes 1572872 | tf_op jit(solution)/shard_map/ppermute | solution.py:511
  91.4 24.1 %collective-permute-start.24 = (bf16[4,256,128]{2,1,0:T(8,128)(2,1)S(1)}, bf16[4,256,128]{2,1,0:T(8,128)(2,1)S(1)}, u32[]{:S(2)}, u32[]{:S(2)}) collective-permute-start(bf16[4,256,128]{2,1,0:T(8,128)(2,1)S(1)} %get-tuple-element.35), channel_id=1, source_target_pairs={{0,16},{4,20},{8,24},{12,28},{16,0},{20,4},{24,8},{28,12},{1,17},{... | collective-permute-start | bytes 786440 | tf_op jit(solution)/shard_map/ppermute | solution.py:401
  95.5 39.5 %collective-permute-start.9 = (bf16[128,2048]{1,0:T(8,128)(2,1)S(1)}, bf16[128,2048]{1,0:T(8,128)(2,1)S(1)}, u32[]{:S(2)}, u32[]{:S(2)}) collective-permute-start(bf16[128,2048]{1,0:T(8,128)(2,1)S(1)} %add_convert_fusion.1), channel_id=1, source_target_pairs={{0,2},{1,3},{2,0},{3,1},{4,6},{5,7},{6,4},{7,5},{8,10},{9,11},{10,... | collective-permute-start | bytes 1572872 | tf_op jit(solution)/shard_map/ppermute | solution.py:401
  115.5 5.2 %collective-permute-start.16 = (bf16[1,256,128]{2,1,0:T(8,128)(2,1)S(1)}, bf16[1,256,128]{2,1,0:T(8,128)(2,1)S(1)}, u32[]{:S(2)}, u32[]{:S(2)}) collective-permute-start(bf16[1,256,128]{2,1,0:T(8,128)(2,1)S(1)} %get-tuple-element.33), channel_id=1, source_target_pairs={{0,16},{4,20},{8,24},{12,28},{16,0},{20,4},{24,8},{28,12},{1,17},{... | collective-permute-start | bytes 196616 | tf_op jit(solution)/shard_map/ppermute | solution.py:401
  120.7 14.4 %collective-permute-start.26 = (bf16[8,256,128]{2,1,0:T(8,128)(2,1)S(1)}, bf16[8,256,128]{2,1,0:T(8,128)(2,1)S(1)}, u32[]{:S(2)}, u32[]{:S(2)}) collective-permute-start(bf16[8,256,128]{2,1,0:T(8,128)(2,1)S(1)} %maximum_bitcast_fusion.refs_9_), channel_id=1, source_target_pairs={{0,2},{1,3},{2,0},{3,1},{4,6},{5,7},{6,4},{7,5},{8,10},{9,11},{10,... | collective-permute-start | bytes 1572872 | tf_op jit(solution)/shard_map/ppermute | solution.py:401
  122.4 5.3 %collective-permute-start.19 = (bf16[1,256,128]{2,1,0:T(8,128)(2,1)S(1)}, bf16[1,256,128]{2,1,0:T(8,128)(2,1)S(1)}, u32[]{:S(2)}, u32[]{:S(2)}) collective-permute-start(bf16[1,256,128]{2,1,0:T(8,128)(2,1)S(1)} %added.5), channel_id=1, source_target_pairs={{0,16},{4,20},{8,24},{12,28},{16,0},{20,4},{24,8},{28,12},{1,17},{... | collective-permute-start | bytes 196616 | tf_op jit(solution)/shard_map/ppermute | solution.py:401
  127.8 5.0 %collective-permute-start.20 = (bf16[2,256,128]{2,1,0:T(8,128)(2,1)S(1)}, bf16[2,256,128]{2,1,0:T(8,128)(2,1)S(1)}, u32[]{:S(2)}, u32[]{:S(2)}) collective-permute-start(bf16[2,256,128]{2,1,0:T(8,128)(2,1)S(1)} %get-tuple-element.43), channel_id=1, source_target_pairs={{0,8},{4,12},{8,0},{12,4},{16,24},{20,28},{24,16},{28,20},{1,9},{5... | collective-permute-start | bytes 393224 | tf_op jit(solution)/shard_map/ppermute | solution.py:401
  127.9 16.2 %collective-permute-start.25 = (bf16[8,256,128]{2,1,0:T(8,128)(2,1)S(1)}, bf16[8,256,128]{2,1,0:T(8,128)(2,1)S(1)}, u32[]{:S(2)}, u32[]{:S(2)}) collective-permute-start(bf16[8,256,128]{2,1,0:T(8,128)(2,1)S(1)} %maximum_bitcast_fusion.refs_9_), channel_id=1, source_target_pairs={{0,1},{1,0},{2,3},{3,2},{4,5},{5,4},{6,7},{7,6},{8,9},{9,8},{10,11... | collective-permute-start | bytes 1572872 | tf_op jit(solution)/shard_map/ppermute | solution.py:401
  132.8 11.2 %collective-permute-start.22 = (bf16[128,1024]{1,0:T(8,128)(2,1)S(1)}, bf16[128,1024]{1,0:T(8,128)(2,1)S(1)}, u32[]{:S(2)}, u32[]{:S(2)}) collective-permute-start(bf16[128,1024]{1,0:T(8,128)(2,1)S(1)} %slice.42), channel_id=1, source_target_pairs={{0,8},{8,16},{16,24},{24,28},{28,20},{20,12},{12,4},{4,0},{1,9},{9... | collective-permute-start | bytes 786440 | tf_op jit(solution)/shard_map/ppermute | solution.py:513
  132.9 11.2 %collective-permute-start.23 = (bf16[128,1024]{1,0:T(8,128)(2,1)S(1)}, bf16[128,1024]{1,0:T(8,128)(2,1)S(1)}, u32[]{:S(2)}, u32[]{:S(2)}) collective-permute-start(bf16[128,1024]{1,0:T(8,128)(2,1)S(1)} %slice.43), channel_id=1, source_target_pairs={{8,0},{16,8},{24,16},{28,24},{20,28},{12,20},{4,12},{0,4},{9,1},{1... | collective-permute-start | bytes 786440 | tf_op jit(solution)/shard_map/ppermute | solution.py:514
  135.0 7.4 %collective-permute-start.21 = (bf16[4,256,128]{2,1,0:T(8,128)(2,1)S(1)}, bf16[4,256,128]{2,1,0:T(8,128)(2,1)S(1)}, u32[]{:S(2)}, u32[]{:S(2)}) collective-permute-start(bf16[4,256,128]{2,1,0:T(8,128)(2,1)S(1)} %bitcast.34), channel_id=1, source_target_pairs={{0,4},{4,0},{8,12},{12,8},{16,20},{20,16},{24,28},{28,24},{1,5},{5... | collective-permute-start | bytes 786440 | tf_op jit(solution)/shard_map/ppermute | solution.py:401
  135.1 9.0 %collective-permute-start.27 = (bf16[8,256,128]{2,1,0:T(8,128)(2,1)S(1)}, bf16[8,256,128]{2,1,0:T(8,128)(2,1)S(1)}, u32[]{:S(2)}, u32[]{:S(2)}) collective-permute-start(bf16[8,256,128]{2,1,0:T(8,128)(2,1)S(1)} %collective-permute-done.26.refs_11_), channel_id=1, source_target_pairs={{0,1},{1,0},{2,3},{3,2},{4,5},{5,4},{6,7},{7,6},{8,9},{9,8},{10,11... | collective-permute-start | bytes 1572872 | tf_op jit(solution)/shard_map/ppermute | solution.py:401
  (7 other events, 67.7 us)

commit v6 on v5

--- a/solution.py
+++ b/solution.py
@@ -91,30 +91,25 @@
     return kernel
 
 
-def by_channel(kernel, arrays, kinds, outs, name, me=None, after=()):
+def by_channel(kernel, arrays, kinds, outs, name, after=()):
     length, channels = arrays[0].shape
-    width = min(512, channels) if me is None else 256
+    width = min(512, channels)
     specs = {
-        "t": pl.BlockSpec((length, width), lambda i, *ids: (0, i)),
-        "c": pl.BlockSpec((width, length), lambda i, *ids: (i, 0)),
-        "x": pl.BlockSpec((width, length), lambda i, *ids: (i ^ ids[0][0], 0)),
+        "t": pl.BlockSpec((length, width), lambda i: (0, i)),
+        "c": pl.BlockSpec((width, length), lambda i: (i, 0)),
     }
 
     def spec_of(kind, shape):
         if kind == "w":
-            return pl.BlockSpec(shape, lambda i, *ids: (0,) * len(shape))
+            return pl.BlockSpec(shape, lambda i: (0,) * len(shape))
         return specs[kind]
 
-    body = ignoring(functools.partial(kernel, length), len(after), len(arrays))
     return pl.pallas_call(
-        body if me is None else lambda ids_ref, *refs: body(*refs),
-        grid_spec=pltpu.PrefetchScalarGridSpec(
-            num_scalar_prefetch=0 if me is None else 1,
-            grid=(channels // width,),
-            in_specs=[spec_of(kind, a.shape) for kind, a in zip(kinds, arrays)]
-            + [pl.BlockSpec(memory_space=pl.ANY)] * len(after),
-            out_specs=[specs[kind] for kind, unused in outs],
-        ),
+        ignoring(functools.partial(kernel, length), len(after), len(arrays)),
+        grid=(channels // width,),
+        in_specs=[spec_of(kind, a.shape) for kind, a in zip(kinds, arrays)]
+        + [pl.BlockSpec(memory_space=pl.ANY)] * len(after),
+        out_specs=[specs[kind] for kind, unused in outs],
         out_shape=[
             jax.ShapeDtypeStruct((length, channels) if kind == "t" else (channels, length), dtype)
             for kind, dtype in outs
@@ -122,139 +117,89 @@
         compiler_params=pltpu.CompilerParams(vmem_limit_bytes=VMEM_BYTES),
         cost_estimate=estimate(3),
         name=name,
-    )(*([] if me is None else [me]), *arrays, *after)
-
-
-def grad_gated_kernel(has_sum, me_ref, cot_ref, w_ref, *refs):
-    out_ref, turned_ref = refs[-2:]
-
-    @pl.when(pl.program_id(0) == 0)
-    def turn():
-        turned_ref[...] = cot_ref[...].T
-
-    total = mm(w_ref[...], turned_ref[...])
-    out_ref[...] = total + refs[0][...] if has_sum else total
-
-
-def grad_gated_part(me, cot, weight, off, sums):
-    length, width = cot.shape
+    )(*arrays, *after)
+
+
+def pass_kernel(with_mixed, with_grad, has_sum, last, me_ref, w_ref, *refs):
+    refs = list(refs)
+    step = pl.program_id(0)
+    if with_mixed:
+        gated_ref = refs.pop(0)
+    if with_grad:
+        cot_ref = refs.pop(0)
+        sum_ref = refs.pop(0) if has_sum else None
+        turned_ref = refs.pop()
+
+        @pl.when(step == 0)
+        def turn():
+            turned_ref[...] = cot_ref[...].T
+
+        total = mm(w_ref[...], turned_ref[...])
+        if has_sum:
+            total = total + sum_ref[...]
+        if last:
+            q_ref, filtered_ref, gq_ref, gf_ref = refs[:4]
+            total = total.T
+            gq_ref[...] = (total * filtered_ref[...]).astype(BF16)
+            gf_ref[...] = (total * q_ref[...].astype(F32)).astype(BF16)
+        else:
+            refs[0][...] = total
+    if with_mixed:
+        held_ref, mixed_ref = refs.pop(), refs.pop()
+        part = mm(gated_ref[...], w_ref[...])
+
+        @pl.when(step == 0)
+        def first():
+            held_ref[...] = part
+
+        @pl.when(step > 0)
+        def more():
+            held_ref[...] = held_ref[...] + part
+
+        @pl.when(step == pl.num_programs(0) - 1)
+        def give():
+            mixed_ref[...] = held_ref[...].astype(mixed_ref.dtype)
+
+
+def weight_pass(me, weight, off, gated=None, cot=None, sums=(), ends=(), after=()):
+    length = (cot if gated is None else gated).shape[0]
     channels = weight.shape[0]
     tile = 512
-    rows = pl.BlockSpec((tile, length), lambda r, me: (r, 0))
+    whole = pl.BlockSpec((length, channels), lambda r, me: (0, 0))
+    by_token = pl.BlockSpec((length, tile), lambda r, me: (0, r))
+    by_row = pl.BlockSpec((tile, length), lambda r, me: (r, 0))
+    arrays, in_specs = [weight], [pl.BlockSpec((tile, channels), lambda r, me: (r, me[1] ^ off))]
+    out_specs, out_shape, scratch = [], [], []
+    if gated is not None:
+        arrays.append(gated)
+        in_specs.append(by_token)
+    if cot is not None:
+        arrays += [cot, *sums, *ends]
+        in_specs += [whole] + [by_row] * len(sums) + [by_token] * len(ends)
+        out_specs += [by_token] * 2 if ends else [by_row]
+        out_shape += [jax.ShapeDtypeStruct((length, channels), BF16)] * 2 if ends else [
+            jax.ShapeDtypeStruct((channels, length), F32)
+        ]
+    if gated is not None:
+        out_specs.append(whole)
+        out_shape.append(jax.ShapeDtypeStruct((length, channels), BF16 if off % 2 else F32))
+        scratch.append(pltpu.VMEM((length, channels), F32))
+    if cot is not None:
+        scratch.append(pltpu.VMEM((channels, length), BF16))
+    body = functools.partial(pass_kernel, gated is not None, cot is not None, bool(sums), bool(ends))
     return pl.pallas_call(
-        functools.partial(grad_gated_kernel, bool(sums)),
+        ignoring(body, len(after), 1 + len(arrays)),
         grid_spec=pltpu.PrefetchScalarGridSpec(
             num_scalar_prefetch=1,
             grid=(channels // tile,),
-            in_specs=[
-                pl.BlockSpec((length, width), lambda r, me: (0, 0)),
-                pl.BlockSpec((tile, width), lambda r, me: (r, me[1] ^ off)),
-            ]
-            + [rows] * len(sums),
-            out_specs=[rows],
-            scratch_shapes=[pltpu.VMEM((width, length), BF16)],
-        ),
-        out_shape=[jax.ShapeDtypeStruct((channels, length), F32)],
-        compiler_params=pltpu.CompilerParams(vmem_limit_bytes=VMEM_BYTES),
-        cost_estimate=estimate(4),
-        name="grad_gated_part",
-    )(me, cot, weight, *sums)
-
-
-def both_kernel(count, with_grad, me_ref, w_ref, gated_ref, *refs):
-    block, step = pl.program_id(0), pl.program_id(1)
-    last = pl.num_programs(1) - 1
-    mixed_refs, held_ref = refs[-count - 1 : -1], refs[-1]
-    if with_grad:
-        cot_refs = refs[:count]
-        sum_ref, q_ref, filtered_ref, gq_ref, gf_ref = refs[count : count + 5]
-        mixed_refs = refs[count + 5 : 2 * count + 5]
-        held_ref, turned_ref, total_ref = refs[-3:]
-        for at in range(count):
-
-            @pl.when((block == at) & (step == 0))
-            def turn():
-                turned_ref[...] = cot_refs[at][...].T
-
-        total = mm(w_ref[...], turned_ref[...])
-        tile = total.shape[0]
-        rows = pl.ds(pl.multiple_of(step * tile, tile), tile)
-
-        @pl.when(block == 0)
-        def begin():
-            total_ref[rows, :] = sum_ref[...] + total
-
-        @pl.when(block > 0)
-        def add():
-            total_ref[rows, :] = total_ref[rows, :] + total
-
-        @pl.when(block == count - 1)
-        def finish():
-            grad = total_ref[rows, :].T
-            gq_ref[...] = (grad * filtered_ref[...]).astype(BF16)
-            gf_ref[...] = (grad * q_ref[...].astype(F32)).astype(BF16)
-
-    part = mm(gated_ref[...], w_ref[...])
-
-    @pl.when(step == 0)
-    def first():
-        held_ref[...] = part
-
-    @pl.when(step > 0)
-    def more():
-        held_ref[...] = held_ref[...] + part
-
-    for at in range(count):
-
-        @pl.when((block == at) & (step == last))
-        def give():
-            mixed_refs[at][...] = held_ref[...].astype(mixed_refs[at].dtype)
-
-
-def both_parts(me, gated, weight, offs, grads, after):
-    length, channels = gated.shape
-    tile, count = 512, len(offs)
-    steps = channels // tile
-    end = count - 1
-
-    def column(b, me):
-        place = me[1] ^ offs[0]
-        for at in range(1, count):
-            place = jnp.where(b == at, me[1] ^ offs[at], place)
-        return place
-
-    whole = pl.BlockSpec((length, channels), lambda b, r, me: (0, 0))
-    by_token = pl.BlockSpec((length, tile), lambda b, r, me: (0, jnp.where(b == end, r, 0)))
-    in_specs = [
-        pl.BlockSpec((tile, channels), lambda b, r, me: (r, column(b, me))),
-        pl.BlockSpec((length, tile), lambda b, r, me: (0, r)),
-    ]
-    out_specs, out_shape = [whole] * count, [
-        jax.ShapeDtypeStruct((length, channels), BF16 if off % 2 else F32) for off in offs
-    ]
-    scratch = [pltpu.VMEM((length, channels), F32)]
-    arrays = [weight, gated]
-    if grads:
-        arrays += grads
-        in_specs += [whole] * count
-        in_specs += [pl.BlockSpec((tile, length), lambda b, r, me: (jnp.where(b == 0, r, steps - 1), 0))]
-        in_specs += [by_token] * 2
-        out_specs = [by_token] * 2 + out_specs
-        out_shape = [jax.ShapeDtypeStruct((length, channels), BF16)] * 2 + out_shape
-        scratch += [pltpu.VMEM((channels, length), BF16), pltpu.VMEM((channels, length), F32)]
-    return pl.pallas_call(
-        ignoring(functools.partial(both_kernel, count, bool(grads)), len(after), 1 + len(arrays)),
-        grid_spec=pltpu.PrefetchScalarGridSpec(
-            num_scalar_prefetch=1,
-            grid=(count, steps),
             in_specs=in_specs + [pl.BlockSpec(memory_space=pl.ANY)] * len(after),
             out_specs=out_specs,
             scratch_shapes=scratch,
         ),
         out_shape=out_shape,
         compiler_params=pltpu.CompilerParams(vmem_limit_bytes=VMEM_BYTES),
-        cost_estimate=estimate(3 * count),
-        name="grads_and_mixed" if grads else "mixed_part",
+        cost_estimate=estimate(3 * ((cot is not None) + (gated is not None))),
+        name="grad_gated_part" if gated is None else "mixed_part" if cot is None else "grads_and_mixed",
     )(me, *arrays, *after)
 
 
@@ -355,29 +300,6 @@
     )(me, owners, *blocks, far_low, far_high, *cots)
 
 
-def place_kernel(me_ref, in_ref, out_ref):
-    count, rows, unused = in_ref.shape
-    for at in range(count):
-        out_ref[at * rows : (at + 1) * rows] = in_ref[me_ref[0] ^ at].astype(out_ref.dtype)
-
-
-def placed_blocks(me, blocks):
-    count, rows, width = blocks.shape
-    return pl.pallas_call(
-        place_kernel,
-        grid_spec=pltpu.PrefetchScalarGridSpec(
-            num_scalar_prefetch=1,
-            grid=(1,),
-            in_specs=[pl.BlockSpec(blocks.shape, lambda i, me: (0, 0, 0))],
-            out_specs=pl.BlockSpec((count * rows, width), lambda i, me: (0, 0)),
-        ),
-        out_shape=jax.ShapeDtypeStruct((count * rows, width), F32),
-        compiler_params=pltpu.CompilerParams(vmem_limit_bytes=VMEM_BYTES),
-        cost_estimate=estimate(0.5),
-        name="placed_blocks",
-    )(me, blocks)
-
-
 def in_one_piece(me, columns, length):
     count, rows, unused = columns[0].shape
     table = jnp.stack(columns)[jnp.arange(len(columns), dtype=jnp.int32) ^ me[1]]
@@ -412,42 +334,71 @@
     return held
 
 
-def halved_kernel(kept_ref, came_ref, next_ref, left_ref):
-    total = (kept_ref[...].astype(F32) + came_ref[...].astype(F32)).astype(BF16)
-    count = total.shape[0] // 2
-    for at in range(count):
-        left_ref[at] = total[2 * at]
-        next_ref[at] = total[2 * at + 1]
-
-
-def added_kernel(kept_ref, came_ref, out_ref):
-    out_ref[...] = (kept_ref[...].astype(F32) + came_ref[...].astype(F32)).astype(BF16)
-
-
-def added(kept, came, after):
-    count = kept.shape[0]
-    whole = pl.BlockSpec(kept.shape, lambda i: (0, 0, 0))
-    half = pl.BlockSpec((max(count // 2, 1),) + kept.shape[1:], lambda i: (0, 0, 0))
-    outs = 2 if count > 1 else 1
+def added_kernel(bit, me_ref, own_ref, came_ref, *outs):
+    total = (own_ref[...].astype(F32) + came_ref[...].astype(F32)).astype(BF16)
+    if not bit:
+        outs[0][...] = total
+        return
+    rows = outs[0].shape[0]
+    mine = (me_ref[0] & bit) != 0
+    outs[0][...] = jnp.where(mine, total[rows:], total[:rows])
+    outs[1][...] = jnp.where(mine, total[:rows], total[rows:])
+
+
+def added(me, own, came, bit, after):
+    shape = (own.shape[0] // 2, own.shape[1]) if bit else own.shape
+    whole = pl.BlockSpec(own.shape, lambda i, me: (0, 0))
+    outs = 2 if bit else 1
     return pl.pallas_call(
-        ignoring(halved_kernel if count > 1 else added_kernel, len(after), 2),
-        grid=(1,),
-        in_specs=[whole, whole] + [pl.BlockSpec(memory_space=pl.ANY)] * len(after),
-        out_specs=[half] * outs,
-        out_shape=[jax.ShapeDtypeStruct(half.block_shape, BF16)] * outs,
+        ignoring(functools.partial(added_kernel, bit), len(after), 3),
+        grid_spec=pltpu.PrefetchScalarGridSpec(
+            num_scalar_prefetch=1,
+            grid=(1,),
+            in_specs=[whole, whole] + [pl.BlockSpec(memory_space=pl.ANY)] * len(after),
+            out_specs=[pl.BlockSpec(shape, lambda i, me: (0, 0))] * outs,
+        ),
+        out_shape=[jax.ShapeDtypeStruct(shape, BF16)] * outs,
         compiler_params=pltpu.CompilerParams(vmem_limit_bytes=VMEM_BYTES),
         cost_estimate=estimate(0.5),
         name="added",
-    )(kept, came, *after)
-
-
-def summed(partial, gates):
-    give, left = partial[1::2], partial[::2]
-    for step, bit in enumerate(bits_of(partial.shape[0])):
-        sums = added(left, swap(give, "ctx", bit), gates[step] if step < len(gates) else ())
-        if len(sums) == 2:
-            give, left = sums
-    return sums[0]
+    )(me, own, came, *after)
+
+
+def summed(me, partial, gates):
+    bits = bits_of(lax.axis_size("ctx"))
+    inner = bits[min(1, len(bits) - 1)]
+    sums = partial
+    for step, bit in enumerate(bits):
+        came = swap(send if bit == inner else sums, "ctx", bit)
+        ahead = inner if bits[step + 1 : step + 2] == [inner] else 0
+        sums, *send = added(me, sums, came, ahead, gates[step] if step < len(gates) else ())
+        send = send[0] if send else None
+    return sums, swap(sums, "ctx", inner), inner
+
+
+def joined_kernel(bit, me_ref, own_ref, other_ref, out_ref):
+    rows = own_ref.shape[0]
+    mine = (me_ref[0] & bit) != 0
+    out_ref[:rows] = jnp.where(mine, other_ref[...], own_ref[...]).astype(F32)
+    out_ref[rows:] = jnp.where(mine, own_ref[...], other_ref[...]).astype(F32)
+
+
+def joined(me, own, other, bit, after):
+    rows, width = own.shape
+    whole = pl.BlockSpec(own.shape, lambda i, me: (0, 0))
+    return pl.pallas_call(
+        ignoring(functools.partial(joined_kernel, bit), len(after), 3),
+        grid_spec=pltpu.PrefetchScalarGridSpec(
+            num_scalar_prefetch=1,
+            grid=(1,),
+            in_specs=[whole, whole] + [pl.BlockSpec(memory_space=pl.ANY)] * len(after),
+            out_specs=pl.BlockSpec((2 * rows, width), lambda i, me: (0, 0)),
+        ),
+        out_shape=jax.ShapeDtypeStruct((2 * rows, width), F32),
+        compiler_params=pltpu.CompilerParams(vmem_limit_bytes=VMEM_BYTES),
+        cost_estimate=estimate(0.5),
+        name="joined",
+    )(me, own, other, *after)
 
 
 def exchanged(pieces):
@@ -461,13 +412,6 @@
     return held[:, 0], sources, stages
 
 
-def doubled(block, axis):
-    held = block
-    for bit in reversed(bits_of(lax.axis_size(axis))):
-        held = jnp.stack([held, swap(held, axis, bit)], axis=1).reshape((-1,) + block.shape[1:])
-    return held
-
-
 def per_device(query_proj, key_proj, value_proj, filters, out_weight, cotangent):
     length, channels = query_proj.shape
     taps = filters.shape[1]
@@ -485,8 +429,8 @@
     for off in offs:
         cots[off + 1] = swap(cots[off], "chan", 1)
     offs = sorted(offs + [off + 1 for off in offs])
-    sums = grad_gated_part(me, cots[0], out_weight, 0, [])
-    sums = grad_gated_part(me, cots[1], out_weight, 1, sums)
+    sums = weight_pass(me, out_weight, 0, cot=cots[0])
+    sums = weight_pass(me, out_weight, 1, cot=cots[1], sums=sums)
 
     gated, filtered = by_channel(
         forward_kernel,
@@ -513,26 +457,27 @@
     far_low = lax.ppermute(from_behind[:, :half], "ctx", ahead)
     far_high = lax.ppermute(from_ahead[:, half:], "ctx", behind)
 
-    grad_query, grad_filtered, *parts = both_parts(
-        me, gated, out_weight, offs, [cots[off] for off in offs] + list(sums) + [query_proj, filtered], [pieces]
+    terms, gates = {}, [pieces]
+    for at, off in enumerate(offs[:-1]):
+        *sums, terms[off] = weight_pass(me, out_weight, off, gated, cots[off], sums, after=gates)
+        gates = blocks[2 * at + 1 : 2 * at + 3] + stages[at : at + 1]
+    grad_query, grad_filtered, terms[offs[-1]] = weight_pass(
+        me, out_weight, offs[-1], gated, cots[offs[-1]], sums, [query_proj, filtered], gates
     )
-    terms = dict(zip(offs, parts))
     following = lax.ppermute(grad_filtered, "ctx", [(i + 1, i) for i in range(n_ctx - 1)])
 
-    direct = channels // n_ctx == 256
     tap_grad = by_channel(
         tap_grad_kernel,
         [key_proj, value_proj, earlier, grad_filtered, forward, lags],
         "ttttww",
-        [("x" if direct else "c", BF16)],
+        [("c", BF16)],
         "tap_grad",
-        me,
-    )[0].reshape(n_ctx, -1, taps)
-    if not direct:
-        tap_grad = tap_grad[jnp.arange(n_ctx, dtype=jnp.int32) ^ me[0]]
-
-    terms[1], terms[0] = both_parts(me, gated, out_weight, [1, 0], [], blocks[1:3] + stages[:1] + [tap_grad])
-    mixed_done = [terms[0]]
+        after=blocks[3:5] + stages[1:2],
+    )[0]
+
+    terms[1] = weight_pass(me, out_weight, 1, gated, after=[tap_grad])[0]
+    terms[0] = weight_pass(me, out_weight, 0, gated, after=blocks[5:7] + stages[2:3] + [terms[1]])[0]
+    gates = [[terms[1]], [terms[0]]]
     for bit in bits_of(n_chan):
         for off in [off for off in sorted(terms, reverse=True) if off & bit]:
             came = swap(terms.pop(off).astype(BF16), "chan", bit).astype(F32)
@@ -545,10 +490,9 @@
         "ttttcww",
         [("t", BF16), ("t", BF16)],
         "backward_filter",
-        after=blocks[3:5] + stages[1:2] + mixed_done,
+        after=gates[-1],
     )
-    gates = [mixed_done, [grad_key], blocks[5:7]]
-    grad_filters = placed_blocks(me, doubled(summed(tap_grad, gates), "ctx"))
+    halves_summed = summed(me, tap_grad, gates + [[grad_key, far_low, far_high]])
 
     columns = gather_by_swaps(held)
     columns = [columns[off] for off in range(n_chan)]
@@ -560,6 +504,7 @@
         steps = [0] + [sign * step for step in range(1, n_ctx // 2) for sign in (-1, 1)] + [n_ctx // 2]
         owners.append([sources.index(order[(spot + step) % n_ctx] ^ c) for step in steps])
     grad_weight = grad_weight_of(me, jnp.asarray(owners, jnp.int32), blocks, far_low, far_high, columns)
+    grad_filters = joined(me, *halves_summed, [grad_weight])
     return (mixed, grad_query, grad_key, grad_value, grad_filters, grad_weight)
 
 

time: 153 us -> 148 us (0.967)
  waiting for transfers between devices: 52.2 us -> 49 us
  Pallas kernels: 66.6 us -> 63.6 us
  local copies, waits for them, and re-layouts: 2.35 us -> 4.45 us
    ppermute x3, starting transfers between devices: 5.48 us -> 0.34 us  [per_device(): from_behind = lax.ppermute(from_behind, 'ctx', ahead)]
    ppermute x3, waiting for transfers between devices: 3.74 us -> 0.04 us  [per_device(): from_behind = lax.ppermute(from_behind, 'ctx', ahead)]
    pallas_call x11 -> x13, Pallas kernels: 57.2 us -> 54.3 us  [the longest x6 39.9 us: weight_pass(): pl.pallas_call(ignoring(body, len(after), 1 + len(arrays)), grid_spec=plt...]
    ppermute x3, waiting for transfers between devices: 0.01 us -> 2.47 us  [per_device(): from_ahead = lax.ppermute(from_ahead, 'ctx', behind)]
    ppermute x3, starting transfers between devices: 4.28 us -> 6.59 us  [per_device(): from_ahead = lax.ppermute(from_ahead, 'ctx', behind)]
    unnamed x22 -> x24, local copies, waits for them, and re-layouts: 2.13 us -> 4.32 us
    ppermute x1, starting transfers between devices: 2.07 us -> 0.01 us  [per_device(): far_high = lax.ppermute(from_ahead[:, half:], 'ctx', behind)]
    ppermute x1, starting transfers between devices: 0.01 us -> 2.07 us  [per_device(): far_low = lax.ppermute(from_behind[:, :half], 'ctx', ahead)]
  transfers between devices with their start and end apart: 28 -> 26, of which waited for: 9 -> 8; matrix products, arithmetic and copies ran while one was open for 2% -> 2% of each run, Pallas kernels for 38% -> 42%
where the time goes in v6:
time: 148 us; the launch traced here: 147 us
  Pallas kernels  63.6 us (43%)
  waiting for transfers between devices  49 us (33%)
  starting transfers between devices  26.5 us (18%)
  local copies, waits for them, and re-layouts  4.45 us (3%)
  other arithmetic  2.63 us (2%)
    ppermute x16, waiting for transfers between devices, swap(): return lax.ppermute(block, axis, [(i, i ^ bit) for i in range(size)])  46.4 us
    pallas_call x6, Pallas kernels, weight_pass(): pl.pallas_call(ignoring(body, len(after), 1 + len(arrays)), grid_spec=plt...  39.9 us
    ppermute x16, starting transfers between devices, swap(): return lax.ppermute(block, axis, [(i, i ^ bit) for i in range(size)])  12.8 us
    pallas_call x3, Pallas kernels, by_channel(): pl.pallas_call(ignoring(functools.partial(kernel, length), len(after), le...  10.8 us
    pallas_call x1, Pallas kernels, grad_weight_of(): pl.pallas_call(functools.partial(weight_kernel, slots, parts, half), grid...  8.68 us
    ppermute x3, starting transfers between devices, per_device(): from_ahead = lax.ppermute(from_ahead, 'ctx', behind)  6.59 us
    unnamed x24, local copies, waits for them, and re-layouts  4.32 us
    ppermute x1, starting transfers between devices, per_device(): lax.ppermute(product, 'ctx', [(i, i + 1) for i in range(n_ctx - 1)])  3.46 us
  transfers between devices with their start and end apart: 26, of which 8 were waited for; matrix products, arithmetic and copies ran while one was open for 2% of the time, Pallas kernels for 42%

profile of v6, /device:TPU:0, one launch (start us, length us, event | category | flops | bytes accessed | tf_op | source)
XLA Modules:
  0.0 147.2 jit_solution(17305376904582919365)
XLA Ops:
  1.1 2.6 %collective-permute-start.8 = (bf16[128,2048]{1,0:T(8,128)(2,1)}, bf16[128,2048]{1,0:T(8,128)(2,1)S(1)}, u32[]{:S(2)}, u32[]{:S(2)}) collective-permute-start(bf16[128,2048]{1,0:T(8,128)(2,1)} %refs_1_.13), channel_id=1, source_target_pairs={{0,2},{1,3},{2,0},{3,1},{4,6},{5,7},{6,4},{7,5},{8,10},{9,11},{10,... | collective-permute-start | bytes 1572872 | tf_op jit(solution)/shard_map/ppermute | solution.py:323
  3.7 1.3 multiply_convert_fusion
  5.0 3.5 %collective-permute-start = (bf16[128,2048]{1,0:T(8,128)(2,1)S(1)}, bf16[128,2048]{1,0:T(8,128)(2,1)S(1)}, u32[]{:S(2)}, u32[]{:S(2)}) collective-permute-start(bf16[128,2048]{1,0:T(8,128)(2,1)S(1)} %multiply_convert_fusion), channel_id=1, source_target_pairs={{0,4},{4,8},{8,12},{12,16},{16,20},{20,24},{24,28},{1,5},{5,9},{9,... | collective-permute-start | bytes 1572872 | tf_op jit(solution)/shard_map/ppermute | solution.py:423
  8.6 1.0 copy-done.1
  9.7 6.4 %grad_gated_part.2.refs_3_ = f32[2048,128]{1,0:T(8,128)S(1)} custom-call(s32[2]{0:T(128)S(1)} %pad_add_fusion.refs_0_.me_ref, bf16[2048,8192]{1,0:T(8,128)(2,1)} %refs_1_.18, bf16[128,2048]{1,0:T(8,128)(2,1)S(1)} %copy-done.1), custom_call_target="tpu_custom_call" | custom-call | flops 3000000000 | tf_op jit(solution)/shard_map/grad_gated_part/pallas_call | solution.py:190
  16.4 6.3 %grad_gated_part.3.refs_7_.refs_5_.refs_4_ = f32[2048,128]{1,0:T(8,128)S(1)} custom-call(s32[2]{0:T(128)S(1)} %pad_add_fusion.refs_0_.me_ref, bf16[2048,8192]{1,0:T(8,128)(2,1)} %refs_1_.18, bf16[128,2048]{1,0:T(8,128)(2,1)S(1)} %collective-permute-done.1.refs_2_, f32[2048,128]{1,0:T(8,128)S(1)} %grad_gated_part.2.refs_3_), custom_call_target="tpu_custom_call" | custom-call | flops 3000000000 | tf_op jit(solution)/shard_map/grad_gated_part/pallas_call | solution.py:190
  22.8 3.4 %forward_filter.1 = (bf16[128,2048]{1,0:T(8,128)(2,1)S(1)}, f32[128,2048]{1,0:T(8,128)S(1)}) custom-call(bf16[128,2048]{1,0:T(8,128)(2,1)S(1)} %copy-done.2, bf16[128,2048]{1,0:T(8,128)(2,1)S(1)} %copy-done.3, bf16[128,2048]{1,0:T(8,128)(2,1)S(1)} %copy-done.4, bf16[128,2048]{1,0:T(8,128)(2,1)S(1)} %collective-permute-done.refs_3_.refs_2_, ...), custom_call_target="tpu_custom_call" | custom-call | flops 3000000000 | tf_op jit(solution)/shard_map/forward_filter/pallas_call | solution.py:107
  26.2 1.8 %collective-permute-start.5 = (bf16[128,2048]{1,0:T(8,128)(2,1)S(1)}, bf16[128,2048]{1,0:T(8,128)(2,1)S(1)}, u32[]{:S(2)}, u32[]{:S(2)}) collective-permute-start(bf16[128,2048]{1,0:T(8,128)(2,1)S(1)} %get-tuple-element.17.refs_2_.refs_0_), channel_id=1, source_target_pairs={{8,0},{16,8},{24,16},{28,24},{20,28},{12,20},{4,12},{0,4},{9,1},{1... | collective-permute-start | bytes 1572872 | tf_op jit(solution)/shard_map/ppermute | solution.py:455
  28.9 1.8 %collective-permute-start.10 = (bf16[4,256,128]{2,1,0:T(8,128)(2,1)S(1)}, bf16[4,256,128]{2,1,0:T(8,128)(2,1)S(1)}, u32[]{:S(2)}, u32[]{:S(2)}) collective-permute-start(bf16[4,256,128]{2,1,0:T(8,128)(2,1)S(1)} %get-tuple-element.31), channel_id=1, source_target_pairs={{0,4},{4,0},{8,12},{12,8},{16,20},{20,16},{24,28},{28,24},{1,5},{5... | collective-permute-start | bytes 786440 | tf_op jit(solution)/shard_map/ppermute | solution.py:323
  30.8 7.4 %grads_and_mixed.2 = (f32[2048,128]{1,0:T(8,128)S(1)}, f32[128,2048]{1,0:T(8,128)S(1)}) custom-call(s32[2]{0:T(128)S(1)} %pad_add_fusion.refs_0_.me_ref, bf16[2048,8192]{1,0:T(8,128)(2,1)} %refs_1_.18, bf16[128,2048]{1,0:T(8,128)(2,1)S(1)} %get-tuple-element.17.refs_2_.refs_0_, bf16[128,2048]{1,0:T(8,128)(2,1)S(1)} %collective-permute-done.8.refs_3_, ...), custom_call_target="tpu_custom_call" | custom-call | flops 6000000000 | tf_op jit(solution)/shard_map/grads_and_mixed/pallas_call | solution.py:190
  38.2 2.5 %collective-permute-done.5.refs_8_.refs_2_ = bf16[128,2048]{1,0:T(8,128)(2,1)S(1)} collective-permute-done((bf16[128,2048]{1,0:T(8,128)(2,1)S(1)}, bf16[128,2048]{1,0:T(8,128)(2,1)S(1)}, u32[]{:S(2)}, u32[]{:S(2)}) %collective-permute-start.5) | collective-permute-done | bytes 524320 | tf_op jit(solution)/shard_map/ppermute | solution.py:455
  40.6 2.1 %collective-permute-start.6 = (bf16[128,2048]{1,0:T(8,128)(2,1)S(1)}, bf16[128,2048]{1,0:T(8,128)(2,1)S(1)}, u32[]{:S(2)}, u32[]{:S(2)}) collective-permute-start(bf16[128,2048]{1,0:T(8,128)(2,1)S(1)} %collective-permute-done.5.refs_8_.refs_2_), channel_id=1, source_target_pairs={{8,0},{16,8},{24,16},{28,24},{20,28},{12,20},{4,12},{0,4},{9,1},{1... | collective-permute-start | bytes 1572872 | tf_op jit(solution)/shard_map/ppermute | solution.py:455
  42.8 5.6 %collective-permute-done.10.refs_9_ = bf16[4,256,128]{2,1,0:T(8,128)(2,1)S(1)} collective-permute-done((bf16[4,256,128]{2,1,0:T(8,128)(2,1)S(1)}, bf16[4,256,128]{2,1,0:T(8,128)(2,1)S(1)}, u32[]{:S(2)}, u32[]{:S(2)}) %collective-permute-start.10) | collective-permute-done | bytes 262176 | tf_op jit(solution)/shard_map/ppermute | solution.py:323
  48.6 8.3 %grads_and_mixed.3 = (bf16[128,2048]{1,0:T(8,128)(2,1)}, bf16[128,2048]{1,0:T(8,128)(2,1)S(1)}, bf16[128,2048]{1,0:T(8,128)(2,1)S(1)}) custom-call(s32[2]{0:T(128)S(1)} %pad_add_fusion.refs_0_.me_ref, bf16[2048,8192]{1,0:T(8,128)(2,1)} %refs_1_.18, bf16[128,2048]{1,0:T(8,128)(2,1)S(1)} %get-tuple-element.17.refs_2_.refs_0_, ...), custom_call_target="tpu_custom_call" | custom-call | flops 6000000000 | tf_op jit(solution)/shard_map/grads_and_mixed/pallas_call | solution.py:190
  56.9 1.3 collective-permute-start.16
  58.2 2.7 %collective-permute-start.7 = (bf16[128,2048]{1,0:T(8,128)(2,1)S(1)}, bf16[128,2048]{1,0:T(8,128)(2,1)S(1)}, u32[]{:S(2)}, u32[]{:S(2)}) collective-permute-start(bf16[128,2048]{1,0:T(8,128)(2,1)S(1)} %collective-permute-done.6.refs_7_.refs_4_), channel_id=1, source_target_pairs={{8,0},{16,8},{24,16},{28,24},{20,28},{12,20},{4,12},{0,4},{9,1},{1... | collective-permute-start | bytes 1572872 | tf_op jit(solution)/shard_map/ppermute | solution.py:455
  61.0 3.5 %tap_grad.1.refs_3_.refs_1_ = bf16[2048,128]{1,0:T(8,128)(2,1)S(1)} custom-call(bf16[128,2048]{1,0:T(8,128)(2,1)S(1)} %copy-done.3, bf16[128,2048]{1,0:T(8,128)(2,1)S(1)} %copy-done.4, bf16[128,2048]{1,0:T(8,128)(2,1)S(1)} %collective-permute-done.refs_3_.refs_2_, bf16[128,2048]{1,0:T(8,128)(2,1)S(1)} %get-tuple-element.20.refs_3_.refs_2_, ...), custom_call_target="tpu_custom_call" | custom-call | flops 3000000000 | tf_op jit(solution)/shard_map/tap_grad/pallas_call | solution.py:107
  64.5 2.0 %collective-permute-start.17 = (bf16[2048,128]{1,0:T(8,128)(2,1)S(1)}, bf16[2048,128]{1,0:T(8,128)(2,1)S(1)}, u32[]{:S(2)}, u32[]{:S(2)}) collective-permute-start(bf16[2048,128]{1,0:T(8,128)(2,1)S(1)} %tap_grad.1.refs_3_.refs_1_), channel_id=1, source_target_pairs={{0,4},{4,0},{8,12},{12,8},{16,20},{20,16},{24,28},{28,24},{1,5},{5... | collective-permute-start | bytes 1572872 | tf_op jit(solution)/shard_map/ppermute | solution.py:323
  66.6 5.7 %mixed_part.2.refs_6_.refs_3_ = bf16[128,2048]{1,0:T(8,128)(2,1)S(1)} custom-call(s32[2]{0:T(128)S(1)} %pad_add_fusion.refs_0_.me_ref, bf16[2048,8192]{1,0:T(8,128)(2,1)} %refs_1_.18, bf16[128,2048]{1,0:T(8,128)(2,1)S(1)} %get-tuple-element.17.refs_2_.refs_0_, bf16[2048,128]{1,0:T(8,128)(2,1)S(1)} %tap_grad.1.refs_3_.refs_1_), custom_call_target="tpu_custom_call" | custom-call | flops 3000000000 | tf_op jit(solution)/shard_map/mixed_part/pallas_call | solution.py:190
  72.3 2.7 %collective-permute-start.12 = (bf16[4,256,128]{2,1,0:T(8,128)(2,1)S(1)}, bf16[4,256,128]{2,1,0:T(8,128)(2,1)S(1)}, u32[]{:S(2)}, u32[]{:S(2)}) collective-permute-start(bf16[4,256,128]{2,1,0:T(8,128)(2,1)S(1)} %fusion.3), channel_id=1, source_target_pairs={{0,16},{4,20},{8,24},{12,28},{16,0},{20,4},{24,8},{28,12},{1,17},{... | collective-permute-start | bytes 786440 | tf_op jit(solution)/shard_map/ppermute | solution.py:323
  75.1 21.3 %collective-permute-done.12.refs_5_ = bf16[4,256,128]{2,1,0:T(8,128)(2,1)S(1)} collective-permute-done((bf16[4,256,128]{2,1,0:T(8,128)(2,1)S(1)}, bf16[4,256,128]{2,1,0:T(8,128)(2,1)S(1)}, u32[]{:S(2)}, u32[]{:S(2)}) %collective-permute-start.12) | collective-permute-done | bytes 262176 | tf_op jit(solution)/shard_map/ppermute | solution.py:323
  96.5 1.6 %collective-permute-start.24 = (bf16[8,256,128]{2,1,0:T(8,128)(2,1)S(1)}, bf16[8,256,128]{2,1,0:T(8,128)(2,1)S(1)}, u32[]{:S(2)}, u32[]{:S(2)}) collective-permute-start(bf16[8,256,128]{2,1,0:T(8,128)(2,1)S(1)} %fusion.1.refs_9_), channel_id=1, source_target_pairs={{0,2},{1,3},{2,0},{3,1},{4,6},{5,7},{6,4},{7,5},{8,10},{9,11},{10,... | collective-permute-start | bytes 1572872 | tf_op jit(solution)/shard_map/ppermute | solution.py:323
  99.8 5.7 %mixed_part.3.refs_7_.refs_3_ = f32[128,2048]{1,0:T(8,128)S(1)} custom-call(s32[2]{0:T(128)S(1)} %pad_add_fusion.refs_0_.me_ref, bf16[2048,8192]{1,0:T(8,128)(2,1)} %refs_1_.18, bf16[128,2048]{1,0:T(8,128)(2,1)S(1)} %get-tuple-element.17.refs_2_.refs_0_, bf16[128,2048]{1,0:T(8,128)(2,1)S(1)} %collective-permute-done.4.refs_3_.refs_5_, ...), custom_call_target="tpu_custom_call" | custom-call | flops 3000000000 | tf_op jit(solution)/shard_map/mixed_part/pallas_call | solution.py:190
  105.6 4.0 %backward_filter.1 = (bf16[128,2048]{1,0:T(8,128)(2,1)}, bf16[128,2048]{1,0:T(8,128)(2,1)}) custom-call(bf16[128,2048]{1,0:T(8,128)(2,1)S(1)} %copy-done.3, bf16[128,2048]{1,0:T(8,128)(2,1)S(1)} %copy-done.4, bf16[128,2048]{1,0:T(8,128)(2,1)S(1)} %get-tuple-element.20.refs_3_.refs_2_, bf16[128,2048]{1,0:T(8,128)(2,1)S(1)} %collective-permute-done.16.refs_3_, ...), custom_call_target="tpu_custom_call" | custom-call | flops 3000000000 | tf_op jit(solution)/shard_map/backward_filter/pallas_call | solution.py:107
  109.6 4.2 %collective-permute-done.18.refs_2_ = bf16[1024,128]{1,0:T(8,128)(2,1)S(1)} collective-permute-done((bf16[1024,128]{1,0:T(8,128)(2,1)S(1)}, bf16[1024,128]{1,0:T(8,128)(2,1)S(1)}, u32[]{:S(2)}, u32[]{:S(2)}) %collective-permute-start.18) | collective-permute-done | bytes 262176 | tf_op jit(solution)/shard_map/ppermute | solution.py:323
  114.4 2.1 %collective-permute-start.20 = (bf16[128,1024]{1,0:T(8,128)(2,1)S(1)}, bf16[128,1024]{1,0:T(8,128)(2,1)S(1)}, u32[]{:S(2)}, u32[]{:S(2)}) collective-permute-start(bf16[128,1024]{1,0:T(8,128)(2,1)S(1)} %slice.36), channel_id=1, source_target_pairs={{0,8},{8,16},{16,24},{24,28},{28,20},{20,12},{12,4},{4,0},{1,9},{9... | collective-permute-start | bytes 786440 | tf_op jit(solution)/shard_map/ppermute | solution.py:457
  116.5 5.6 %collective-permute-done.15 = bf16[128,2048]{1,0:T(8,128)(2,1)S(1)} collective-permute-done((bf16[128,2048]{1,0:T(8,128)(2,1)S(1)}, bf16[128,2048]{1,0:T(8,128)(2,1)S(1)}, u32[]{:S(2)}, u32[]{:S(2)}) %collective-permute-start.15) | collective-permute-done | bytes 524320 | tf_op jit(solution)/shard_map/ppermute | solution.py:323
  123.3 9.2 %collective-permute-done.19.refs_2_ = bf16[1024,128]{1,0:T(8,128)(2,1)S(1)} collective-permute-done((bf16[1024,128]{1,0:T(8,128)(2,1)S(1)}, bf16[1024,128]{1,0:T(8,128)(2,1)S(1)}, u32[]{:S(2)}, u32[]{:S(2)}) %collective-permute-start.19) | collective-permute-done | bytes 262176 | tf_op jit(solution)/shard_map/ppermute | solution.py:323
  132.5 1.0 copy-done.6
  134.7 8.7 %grad_weight.1.refs_3_ = bf16[2048,1024]{1,0:T(8,128)(2,1)} custom-call(s32[2]{0:T(128)S(1)} %pad_add_fusion.refs_0_.me_ref, s32[8,8]{1,0:T(8,128)S(1)} %copy-done.11, bf16[128,2048]{1,0:T(8,128)(2,1)S(1)} %get-tuple-element.17.refs_2_.refs_0_, bf16[128,2048]{1,0:T(8,128)(2,1)S(1)} %collective-permute-done.2.refs_7_.refs_1_, ...), custom_call_target="tpu_custom_call" | custom-call | flops 6000000000 | tf_op jit(solution)/shard_map/grad_weight/pallas_call | solution.py:288
  143.4 2.2 %copy-done = bf16[2048,1024]{1,0:T(8,128)(2,1)S(1)} copy-done((bf16[2048,1024]{1,0:T(8,128)(2,1)S(1)}, bf16[2048,1024]{1,0:T(8,128)(2,1)}, u32[]{:S(2)}) %copy-start) | copy-done | bytes 4194328
  145.6 1.6 %joined.1 = f32[2048,128]{1,0:T(8,128)} custom-call(s32[2]{0:T(128)S(1)} %pad_add_fusion.refs_0_.me_ref, bf16[1024,128]{1,0:T(8,128)(2,1)S(1)} %added.5.refs_1_, bf16[1024,128]{1,0:T(8,128)(2,1)S(1)} %collective-permute-done.22.refs_2_, bf16[2048,1024]{1,0:T(8,128)(2,1)S(1)} %copy-done), custom_call_target="tpu_custom_call" | custom-call | flops 500000000 | tf_op jit(solution)/shard_map/joined/pallas_call | solution.py:389
  (71 shorter events, 7.0 us)
Async XLA Ops:
  0.6 15.8 %collective-permute-start.1 = (bf16[128,2048]{1,0:T(8,128)(2,1)}, bf16[128,2048]{1,0:T(8,128)(2,1)S(1)}, u32[]{:S(2)}, u32[]{:S(2)}) collective-permute-start(bf16[128,2048]{1,0:T(8,128)(2,1)} %refs_1_.13), channel_id=1, source_target_pairs={{0,1},{1,0},{2,3},{3,2},{4,5},{5,4},{6,7},{7,6},{8,9},{9,8},{10,11... | collective-permute-start | bytes 1572872 | tf_op jit(solution)/shard_map/ppermute | solution.py:323
  1.1 15.3 %collective-permute-start.8 = (bf16[128,2048]{1,0:T(8,128)(2,1)}, bf16[128,2048]{1,0:T(8,128)(2,1)S(1)}, u32[]{:S(2)}, u32[]{:S(2)}) collective-permute-start(bf16[128,2048]{1,0:T(8,128)(2,1)} %refs_1_.13), channel_id=1, source_target_pairs={{0,2},{1,3},{2,0},{3,1},{4,6},{5,7},{6,4},{7,5},{8,10},{9,11},{10,... | collective-permute-start | bytes 1572872 | tf_op jit(solution)/shard_map/ppermute | solution.py:323
  5.0 17.7 %collective-permute-start = (bf16[128,2048]{1,0:T(8,128)(2,1)S(1)}, bf16[128,2048]{1,0:T(8,128)(2,1)S(1)}, u32[]{:S(2)}, u32[]{:S(2)}) collective-permute-start(bf16[128,2048]{1,0:T(8,128)(2,1)S(1)} %multiply_convert_fusion), channel_id=1, source_target_pairs={{0,4},{4,8},{8,12},{12,16},{16,20},{20,24},{24,28},{1,5},{5,9},{9,... | collective-permute-start | bytes 1572872 | tf_op jit(solution)/shard_map/ppermute | solution.py:423
  9.6 13.1 %copy-start.5 = (bf16[2048,128]{1,0:T(8,128)(2,1)S(1)}, bf16[2048,128]{1,0:T(8,128)(2,1)}, u32[]{:S(2)}) copy-start(bf16[2048,128]{1,0:T(8,128)(2,1)} %refs_4_.4) | copy-start | bytes 1572868
  9.6 13.1 %copy-start.7 = (bf16[2,256,256]{2,1,0:T(8,128)(2,1)S(1)}, bf16[2,256,256]{2,1,0:T(8,128)(2,1)}, u32[]{:S(2)}) copy-start(bf16[2,256,256]{2,1,0:T(8,128)(2,1)} %constant.19.clone.refs_5_.refs_4_) | copy-start | bytes 786436
  9.7 13.1 %copy-start.10 = (bf16[2,128,256]{2,1,0:T(8,128)(2,1)S(1)}, bf16[2,128,256]{2,1,0:T(8,128)(2,1)}, u32[]{:S(2)}) copy-start(bf16[2,128,256]{2,1,0:T(8,128)(2,1)} %constant.20.clone.refs_6_) | copy-start | bytes 393220
  16.4 11.8 %collective-permute-start.9 = (bf16[128,2048]{1,0:T(8,128)(2,1)S(1)}, bf16[128,2048]{1,0:T(8,128)(2,1)S(1)}, u32[]{:S(2)}, u32[]{:S(2)}) collective-permute-start(bf16[128,2048]{1,0:T(8,128)(2,1)S(1)} %collective-permute-done.8.refs_3_), channel_id=1, source_target_pairs={{0,1},{1,0},{2,3},{3,2},{4,5},{5,4},{6,7},{7,6},{8,9},{9,8},{10,11... | collective-permute-start | bytes 1572872 | tf_op jit(solution)/shard_map/ppermute | solution.py:323
  26.2 14.5 %collective-permute-start.5 = (bf16[128,2048]{1,0:T(8,128)(2,1)S(1)}, bf16[128,2048]{1,0:T(8,128)(2,1)S(1)}, u32[]{:S(2)}, u32[]{:S(2)}) collective-permute-start(bf16[128,2048]{1,0:T(8,128)(2,1)S(1)} %get-tuple-element.17.refs_2_.refs_0_), channel_id=1, source_target_pairs={{8,0},{16,8},{24,16},{28,24},{20,28},{12,20},{4,12},{0,4},{9,1},{1... | collective-permute-start | bytes 1572872 | tf_op jit(solution)/shard_map/ppermute | solution.py:455
  28.0 14.8 %collective-permute-start.2 = (bf16[128,2048]{1,0:T(8,128)(2,1)S(1)}, bf16[128,2048]{1,0:T(8,128)(2,1)S(1)}, u32[]{:S(2)}, u32[]{:S(2)}) collective-permute-start(bf16[128,2048]{1,0:T(8,128)(2,1)S(1)} %get-tuple-element.17.refs_2_.refs_0_), channel_id=1, source_target_pairs={{0,8},{8,16},{16,24},{24,28},{28,20},{20,12},{12,4},{4,0},{1,9},{9... | collective-permute-start | bytes 1572872 | tf_op jit(solution)/shard_map/ppermute | solution.py:454
  28.9 32.0 %copy-start.9 = (bf16[2,128,256]{2,1,0:T(8,128)(2,1)S(1)}, bf16[2,128,256]{2,1,0:T(8,128)(2,1)}, u32[]{:S(2)}) copy-start(bf16[2,128,256]{2,1,0:T(8,128)(2,1)} %constant.22.clone.refs_5_) | copy-start | bytes 393220
  28.9 19.4 %collective-permute-start.10 = (bf16[4,256,128]{2,1,0:T(8,128)(2,1)S(1)}, bf16[4,256,128]{2,1,0:T(8,128)(2,1)S(1)}, u32[]{:S(2)}, u32[]{:S(2)}) collective-permute-start(bf16[4,256,128]{2,1,0:T(8,128)(2,1)S(1)} %get-tuple-element.31), channel_id=1, source_target_pairs={{0,4},{4,0},{8,12},{12,8},{16,20},{20,16},{24,28},{28,24},{1,5},{5... | collective-permute-start | bytes 786440 | tf_op jit(solution)/shard_map/ppermute | solution.py:323
  40.6 17.5 %collective-permute-start.6 = (bf16[128,2048]{1,0:T(8,128)(2,1)S(1)}, bf16[128,2048]{1,0:T(8,128)(2,1)S(1)}, u32[]{:S(2)}, u32[]{:S(2)}) collective-permute-start(bf16[128,2048]{1,0:T(8,128)(2,1)S(1)} %collective-permute-done.5.refs_8_.refs_2_), channel_id=1, source_target_pairs={{8,0},{16,8},{24,16},{28,24},{20,28},{12,20},{4,12},{0,4},{9,1},{1... | collective-permute-start | bytes 1572872 | tf_op jit(solution)/shard_map/ppermute | solution.py:455
  42.8 18.1 %collective-permute-start.3 = (bf16[128,2048]{1,0:T(8,128)(2,1)S(1)}, bf16[128,2048]{1,0:T(8,128)(2,1)S(1)}, u32[]{:S(2)}, u32[]{:S(2)}) collective-permute-start(bf16[128,2048]{1,0:T(8,128)(2,1)S(1)} %collective-permute-done.2.refs_7_.refs_1_), channel_id=1, source_target_pairs={{0,8},{8,16},{16,24},{24,28},{28,20},{20,12},{12,4},{4,0},{1,9},{9... | collective-permute-start | bytes 1572872 | tf_op jit(solution)/shard_map/ppermute | solution.py:454
  48.5 12.5 %collective-permute-start.11 = (bf16[4,256,128]{2,1,0:T(8,128)(2,1)S(1)}, bf16[4,256,128]{2,1,0:T(8,128)(2,1)S(1)}, u32[]{:S(2)}, u32[]{:S(2)}) collective-permute-start(bf16[4,256,128]{2,1,0:T(8,128)(2,1)S(1)} %bitcast.20), channel_id=1, source_target_pairs={{0,8},{4,12},{8,0},{12,4},{16,24},{20,28},{24,16},{28,20},{1,9},{5... | collective-permute-start | bytes 786440 | tf_op jit(solution)/shard_map/ppermute | solution.py:323
  56.9 15.4 %collective-permute-start.14 = (bf16[128,2048]{1,0:T(8,128)(2,1)S(1)}, bf16[128,2048]{1,0:T(8,128)(2,1)S(1)}, u32[]{:S(2)}, u32[]{:S(2)}) collective-permute-start(bf16[128,2048]{1,0:T(8,128)(2,1)S(1)} %get-tuple-element.22), channel_id=1, source_target_pairs={{0,1},{1,0},{2,3},{3,2},{4,5},{5,4},{6,7},{7,6},{8,9},{9,8},{10,11... | collective-permute-start | bytes 1572872 | tf_op jit(solution)/shard_map/ppermute | solution.py:323
  56.9 48.6 %collective-permute-start.16 = (bf16[128,2048]{1,0:T(8,128)(2,1)S(1)}, bf16[128,2048]{1,0:T(8,128)(2,1)S(1)}, u32[]{:S(2)}, u32[]{:S(2)}) collective-permute-start(bf16[128,2048]{1,0:T(8,128)(2,1)S(1)} %get-tuple-element.20.refs_3_.refs_2_), channel_id=1, source_target_pairs={{4,0},{8,4},{12,8},{16,12},{20,16},{24,20},{28,24},{5,1},{9,5},{13... | collective-permute-start | bytes 1572872 | tf_op jit(solution)/shard_map/ppermute | solution.py:467
  58.2 38.3 %collective-permute-start.7 = (bf16[128,2048]{1,0:T(8,128)(2,1)S(1)}, bf16[128,2048]{1,0:T(8,128)(2,1)S(1)}, u32[]{:S(2)}, u32[]{:S(2)}) collective-permute-start(bf16[128,2048]{1,0:T(8,128)(2,1)S(1)} %collective-permute-done.6.refs_7_.refs_4_), channel_id=1, source_target_pairs={{8,0},{16,8},{24,16},{28,24},{20,28},{12,20},{4,12},{0,4},{9,1},{1... | collective-permute-start | bytes 1572872 | tf_op jit(solution)/shard_map/ppermute | solution.py:455
  60.9 37.2 %collective-permute-start.4 = (bf16[128,2048]{1,0:T(8,128)(2,1)S(1)}, bf16[128,2048]{1,0:T(8,128)(2,1)S(1)}, u32[]{:S(2)}, u32[]{:S(2)}) collective-permute-start(bf16[128,2048]{1,0:T(8,128)(2,1)S(1)} %collective-permute-done.3.refs_6_.refs_3_), channel_id=1, source_target_pairs={{0,8},{8,16},{16,24},{24,28},{28,20},{20,12},{12,4},{4,0},{1,9},{9... | collective-permute-start | bytes 1572872 | tf_op jit(solution)/shard_map/ppermute | solution.py:454
  64.5 34.0 %collective-permute-start.17 = (bf16[2048,128]{1,0:T(8,128)(2,1)S(1)}, bf16[2048,128]{1,0:T(8,128)(2,1)S(1)}, u32[]{:S(2)}, u32[]{:S(2)}) collective-permute-start(bf16[2048,128]{1,0:T(8,128)(2,1)S(1)} %tap_grad.1.refs_3_.refs_1_), channel_id=1, source_target_pairs={{0,4},{4,0},{8,12},{12,8},{16,20},{20,16},{24,28},{28,24},{1,5},{5... | collective-permute-start | bytes 1572872 | tf_op jit(solution)/shard_map/ppermute | solution.py:323
  66.6 39.1 %copy-start.8 = (bf16[2,128,256]{2,1,0:T(8,128)(2,1)S(1)}, bf16[2,128,256]{2,1,0:T(8,128)(2,1)}, u32[]{:S(2)}) copy-start(bf16[2,128,256]{2,1,0:T(8,128)(2,1)} %constant.21.clone.refs_6_) | copy-start | bytes 393220
  72.3 62.4 %copy-start.11 = (s32[8,8]{1,0:T(8,128)S(1)}, s32[8,8]{1,0:T(8,128)}, u32[]{:S(2)}) copy-start(s32[8,8]{1,0:T(8,128)} %constant.23.clone.owner_ref) | copy-start | bytes 772
  72.3 24.2 %collective-permute-start.12 = (bf16[4,256,128]{2,1,0:T(8,128)(2,1)S(1)}, bf16[4,256,128]{2,1,0:T(8,128)(2,1)S(1)}, u32[]{:S(2)}, u32[]{:S(2)}) collective-permute-start(bf16[4,256,128]{2,1,0:T(8,128)(2,1)S(1)} %fusion.3), channel_id=1, source_target_pairs={{0,16},{4,20},{8,24},{12,28},{16,0},{20,4},{24,8},{28,12},{1,17},{... | collective-permute-start | bytes 786440 | tf_op jit(solution)/shard_map/ppermute | solution.py:323
  96.5 18.0 %collective-permute-start.13 = (bf16[128,2048]{1,0:T(8,128)(2,1)S(1)}, bf16[128,2048]{1,0:T(8,128)(2,1)S(1)}, u32[]{:S(2)}, u32[]{:S(2)}) collective-permute-start(bf16[128,2048]{1,0:T(8,128)(2,1)S(1)} %mixed_part.2.refs_6_.refs_3_), channel_id=1, source_target_pairs={{0,1},{1,0},{2,3},{3,2},{4,5},{5,4},{6,7},{7,6},{8,9},{9,8},{10,11... | collective-permute-start | bytes 1572872 | tf_op jit(solution)/shard_map/ppermute | solution.py:323
  96.5 20.0 %collective-permute-start.24 = (bf16[8,256,128]{2,1,0:T(8,128)(2,1)S(1)}, bf16[8,256,128]{2,1,0:T(8,128)(2,1)S(1)}, u32[]{:S(2)}, u32[]{:S(2)}) collective-permute-start(bf16[8,256,128]{2,1,0:T(8,128)(2,1)S(1)} %fusion.1.refs_9_), channel_id=1, source_target_pairs={{0,2},{1,3},{2,0},{3,1},{4,6},{5,7},{6,4},{7,5},{8,10},{9,11},{10,... | collective-permute-start | bytes 1572872 | tf_op jit(solution)/shard_map/ppermute | solution.py:323
  98.1 36.6 %collective-permute-start.23 = (bf16[8,256,128]{2,1,0:T(8,128)(2,1)S(1)}, bf16[8,256,128]{2,1,0:T(8,128)(2,1)S(1)}, u32[]{:S(2)}, u32[]{:S(2)}) collective-permute-start(bf16[8,256,128]{2,1,0:T(8,128)(2,1)S(1)} %fusion.1.refs_9_), channel_id=1, source_target_pairs={{0,1},{1,0},{2,3},{3,2},{4,5},{5,4},{6,7},{7,6},{8,9},{9,8},{10,11... | collective-permute-start | bytes 1572872 | tf_op jit(solution)/shard_map/ppermute | solution.py:323
  98.5 23.7 %collective-permute-start.15 = (bf16[128,2048]{1,0:T(8,128)(2,1)S(1)}, bf16[128,2048]{1,0:T(8,128)(2,1)S(1)}, u32[]{:S(2)}, u32[]{:S(2)}) collective-permute-start(bf16[128,2048]{1,0:T(8,128)(2,1)S(1)} %add_convert_fusion.1), channel_id=1, source_target_pairs={{0,2},{1,3},{2,0},{3,1},{4,6},{5,7},{6,4},{7,5},{8,10},{9,11},{10,... | collective-permute-start | bytes 1572872 | tf_op jit(solution)/shard_map/ppermute | solution.py:323
  105.5 8.3 %collective-permute-start.18 = (bf16[1024,128]{1,0:T(8,128)(2,1)S(1)}, bf16[1024,128]{1,0:T(8,128)(2,1)S(1)}, u32[]{:S(2)}, u32[]{:S(2)}) collective-permute-start(bf16[1024,128]{1,0:T(8,128)(2,1)S(1)} %get-tuple-element.27), channel_id=1, source_target_pairs={{0,8},{4,12},{8,0},{12,4},{16,24},{20,28},{24,16},{28,20},{1,9},{5... | collective-permute-start | bytes 786440 | tf_op jit(solution)/shard_map/ppermute | solution.py:323
  113.8 9.4 %collective-permute-start.21 = (bf16[128,1024]{1,0:T(8,128)(2,1)S(1)}, bf16[128,1024]{1,0:T(8,128)(2,1)S(1)}, u32[]{:S(2)}, u32[]{:S(2)}) collective-permute-start(bf16[128,1024]{1,0:T(8,128)(2,1)S(1)} %slice.37), channel_id=1, source_target_pairs={{8,0},{16,8},{24,16},{28,24},{20,28},{12,20},{4,12},{0,4},{9,1},{1... | collective-permute-start | bytes 786440 | tf_op jit(solution)/shard_map/ppermute | solution.py:458
  114.4 8.8 %collective-permute-start.20 = (bf16[128,1024]{1,0:T(8,128)(2,1)S(1)}, bf16[128,1024]{1,0:T(8,128)(2,1)S(1)}, u32[]{:S(2)}, u32[]{:S(2)}) collective-permute-start(bf16[128,1024]{1,0:T(8,128)(2,1)S(1)} %slice.36), channel_id=1, source_target_pairs={{0,8},{8,16},{16,24},{24,28},{28,20},{20,12},{12,4},{4,0},{1,9},{9... | collective-permute-start | bytes 786440 | tf_op jit(solution)/shard_map/ppermute | solution.py:457
  116.5 15.9 %collective-permute-start.19 = (bf16[1024,128]{1,0:T(8,128)(2,1)S(1)}, bf16[1024,128]{1,0:T(8,128)(2,1)S(1)}, u32[]{:S(2)}, u32[]{:S(2)}) collective-permute-start(bf16[1024,128]{1,0:T(8,128)(2,1)S(1)} %added.4.refs_1_), channel_id=1, source_target_pairs={{0,16},{4,20},{8,24},{12,28},{16,0},{20,4},{24,8},{28,12},{1,17},{... | collective-permute-start | bytes 786440 | tf_op jit(solution)/shard_map/ppermute | solution.py:323
  122.2 12.5 %collective-permute-start.25 = (bf16[8,256,128]{2,1,0:T(8,128)(2,1)S(1)}, bf16[8,256,128]{2,1,0:T(8,128)(2,1)S(1)}, u32[]{:S(2)}, u32[]{:S(2)}) collective-permute-start(bf16[8,256,128]{2,1,0:T(8,128)(2,1)S(1)} %collective-permute-done.24.refs_11_), channel_id=1, source_target_pairs={{0,1},{1,0},{2,3},{3,2},{4,5},{5,4},{6,7},{7,6},{8,9},{9,8},{10,11... | collective-permute-start | bytes 1572872 | tf_op jit(solution)/shard_map/ppermute | solution.py:323
  134.1 9.3 %collective-permute-start.22 = (bf16[1024,128]{1,0:T(8,128)(2,1)S(1)}, bf16[1024,128]{1,0:T(8,128)(2,1)S(1)}, u32[]{:S(2)}, u32[]{:S(2)}) collective-permute-start(bf16[1024,128]{1,0:T(8,128)(2,1)S(1)} %added.5.refs_1_), channel_id=1, source_target_pairs={{0,8},{4,12},{8,0},{12,4},{16,24},{20,28},{24,16},{28,20},{1,9},{5... | collective-permute-start | bytes 786440 | tf_op jit(solution)/shard_map/ppermute | solution.py:323
  (6 other events, 43.6 us)

commit v7 on v6

--- a/solution.py
+++ b/solution.py
@@ -364,26 +364,32 @@
     )(me, own, came, *after)
 
 
+def split(me, block, bit):
+    rows = block.shape[0] // 2
+    mine = (me[0] & bit) != 0
+    low, high = block[:rows], block[rows:]
+    return jnp.where(mine, high, low), jnp.where(mine, low, high)
+
+
 def summed(me, partial, gates):
     bits = bits_of(lax.axis_size("ctx"))
-    inner = bits[min(1, len(bits) - 1)]
-    sums = partial
+    sums, send = split(me, partial, bits[0])
     for step, bit in enumerate(bits):
-        came = swap(send if bit == inner else sums, "ctx", bit)
-        ahead = inner if bits[step + 1 : step + 2] == [inner] else 0
-        sums, *send = added(me, sums, came, ahead, gates[step] if step < len(gates) else ())
+        came = swap(send if step < 2 else sums, "ctx", bit)
+        sums, *send = added(me, sums, came, bits[1] if step == 0 else 0, gates[step] if step < len(gates) else ())
         send = send[0] if send else None
-    return sums, swap(sums, "ctx", inner), inner
+    sums = joined(me, sums, swap(sums, "ctx", bits[1]), bits[1], BF16, ())
+    return sums, swap(sums, "ctx", bits[0]), bits[0]
 
 
 def joined_kernel(bit, me_ref, own_ref, other_ref, out_ref):
     rows = own_ref.shape[0]
     mine = (me_ref[0] & bit) != 0
-    out_ref[:rows] = jnp.where(mine, other_ref[...], own_ref[...]).astype(F32)
-    out_ref[rows:] = jnp.where(mine, own_ref[...], other_ref[...]).astype(F32)
-
-
-def joined(me, own, other, bit, after):
+    out_ref[:rows] = jnp.where(mine, other_ref[...], own_ref[...]).astype(out_ref.dtype)
+    out_ref[rows:] = jnp.where(mine, own_ref[...], other_ref[...]).astype(out_ref.dtype)
+
+
+def joined(me, own, other, bit, dtype, after):
     rows, width = own.shape
     whole = pl.BlockSpec(own.shape, lambda i, me: (0, 0))
     return pl.pallas_call(
@@ -394,7 +400,7 @@
             in_specs=[whole, whole] + [pl.BlockSpec(memory_space=pl.ANY)] * len(after),
             out_specs=pl.BlockSpec((2 * rows, width), lambda i, me: (0, 0)),
         ),
-        out_shape=jax.ShapeDtypeStruct((2 * rows, width), F32),
+        out_shape=jax.ShapeDtypeStruct((2 * rows, width), dtype),
         compiler_params=pltpu.CompilerParams(vmem_limit_bytes=VMEM_BYTES),
         cost_estimate=estimate(0.5),
         name="joined",
@@ -403,11 +409,11 @@
 
 def exchanged(pieces):
     held, sources, stages = pieces[None], [0], []
-    for bit in bits_of(pieces.shape[0]):
-        give = held[:, 1::2].reshape((-1,) + pieces.shape[1:])
+    for bit in reversed(bits_of(pieces.shape[0])):
+        give = held[:, bit:].reshape((-1,) + pieces.shape[1:])
         stages.append(swap(give, "ctx", bit))
-        came = stages[-1].reshape((len(sources), -1) + pieces.shape[1:])
-        held = jnp.concatenate([held[:, ::2], came], axis=0)
+        came = stages[-1].reshape((len(sources), bit) + pieces.shape[1:])
+        held = jnp.concatenate([held[:, :bit], came], axis=0)
         sources += [source ^ bit for source in sources]
     return held[:, 0], sources, stages
 
@@ -420,6 +426,7 @@
     forward, late, early, lags = [jnp.asarray(m) for m in transforms(taps)]
 
     product = (key_proj.astype(F32) * value_proj.astype(F32)).astype(BF16)
+    product, cotangent = lax.optimization_barrier((product, cotangent))
     earlier = lax.ppermute(product, "ctx", [(i, i + 1) for i in range(n_ctx - 1)])
 
     cots = {0: cotangent, 1: swap(cotangent, "chan", 1)}
@@ -457,12 +464,11 @@
     far_low = lax.ppermute(from_behind[:, :half], "ctx", ahead)
     far_high = lax.ppermute(from_ahead[:, half:], "ctx", behind)
 
-    terms, gates = {}, [pieces]
-    for at, off in enumerate(offs[:-1]):
-        *sums, terms[off] = weight_pass(me, out_weight, off, gated, cots[off], sums, after=gates)
-        gates = blocks[2 * at + 1 : 2 * at + 3] + stages[at : at + 1]
+    terms = {}
+    for off in offs[:-1]:
+        *sums, terms[off] = weight_pass(me, out_weight, off, gated, cots[off], sums, after=[pieces])
     grad_query, grad_filtered, terms[offs[-1]] = weight_pass(
-        me, out_weight, offs[-1], gated, cots[offs[-1]], sums, [query_proj, filtered], gates
+        me, out_weight, offs[-1], gated, cots[offs[-1]], sums, [query_proj, filtered]
     )
     following = lax.ppermute(grad_filtered, "ctx", [(i + 1, i) for i in range(n_ctx - 1)])
 
@@ -472,11 +478,10 @@
         "ttttww",
         [("c", BF16)],
         "tap_grad",
-        after=blocks[3:5] + stages[1:2],
     )[0]
 
-    terms[1] = weight_pass(me, out_weight, 1, gated, after=[tap_grad])[0]
-    terms[0] = weight_pass(me, out_weight, 0, gated, after=blocks[5:7] + stages[2:3] + [terms[1]])[0]
+    terms[1] = weight_pass(me, out_weight, 1, gated, after=blocks[1:3] + stages[:1] + [tap_grad])[0]
+    terms[0] = weight_pass(me, out_weight, 0, gated, after=blocks[3:5] + stages[1:2] + [terms[1]])[0]
     gates = [[terms[1]], [terms[0]]]
     for bit in bits_of(n_chan):
         for off in [off for off in sorted(terms, reverse=True) if off & bit]:
@@ -490,7 +495,7 @@
         "ttttcww",
         [("t", BF16), ("t", BF16)],
         "backward_filter",
-        after=gates[-1],
+        after=gates[-1] + blocks[5:7],
     )
     halves_summed = summed(me, tap_grad, gates + [[grad_key, far_low, far_high]])
 
@@ -504,7 +509,7 @@
         steps = [0] + [sign * step for step in range(1, n_ctx // 2) for sign in (-1, 1)] + [n_ctx // 2]
         owners.append([sources.index(order[(spot + step) % n_ctx] ^ c) for step in steps])
     grad_weight = grad_weight_of(me, jnp.asarray(owners, jnp.int32), blocks, far_low, far_high, columns)
-    grad_filters = joined(me, *halves_summed, [grad_weight])
+    grad_filters = joined(me, *halves_summed, F32, [grad_weight])
     return (mixed, grad_query, grad_key, grad_value, grad_filters, grad_weight)
 
 

time: 148 us -> 147 us (level)
  waiting for transfers between devices: 49 us -> 46.9 us
    ppermute x3, waiting for transfers between devices: 2.47 us -> 0.01 us  [per_device(): from_ahead = lax.ppermute(from_ahead, 'ctx', behind)]
    ppermute x1, waiting for transfers between devices: 0.1 us -> 2.4 us  [per_device(): far_low = lax.ppermute(from_behind[:, :half], 'ctx', ahead)]
    ppermute x1, starting transfers between devices: 2.07 us -> 0.01 us  [per_device(): far_low = lax.ppermute(from_behind[:, :half], 'ctx', ahead)]
    ppermute x16 -> x17, waiting for transfers between devices: 46.4 us -> 44.4 us  [swap(): return lax.ppermute(block, axis, [(i, i ^ bit) for i in range(size)])]
    ppermute x16 -> x17, starting transfers between devices: 12.8 us -> 14.5 us  [swap(): return lax.ppermute(block, axis, [(i, i ^ bit) for i in range(size)])]
  transfers between devices with their start and end apart: 26 -> 27, of which waited for: 8 -> 7; matrix products, arithmetic and copies ran while one was open for 2% -> 1% of each run, Pallas kernels for 42% -> 42%
where the time goes in v7:
time: 147 us
  Pallas kernels  63.9 us (43%)
  waiting for transfers between devices  46.9 us (32%)
  starting transfers between devices  27.9 us (19%)
  local copies, waits for them, and re-layouts  4.45 us (3%)
  other arithmetic  2.67 us (2%)
    ppermute x17, waiting for transfers between devices, swap(): return lax.ppermute(block, axis, [(i, i ^ bit) for i in range(size)])  44.4 us
    pallas_call x6, Pallas kernels, weight_pass(): pl.pallas_call(ignoring(body, len(after), 1 + len(arrays)), grid_spec=plt...  39.8 us
    ppermute x17, starting transfers between devices, swap(): return lax.ppermute(block, axis, [(i, i ^ bit) for i in range(size)])  14.5 us
    pallas_call x3, Pallas kernels, by_channel(): pl.pallas_call(ignoring(functools.partial(kernel, length), len(after), le...  10.9 us
    pallas_call x1, Pallas kernels, grad_weight_of(): pl.pallas_call(functools.partial(weight_kernel, slots, parts, half), grid...  8.6 us
    ppermute x3, starting transfers between devices, per_device(): from_ahead = lax.ppermute(from_ahead, 'ctx', behind)  7.04 us
    unnamed x24, local copies, waits for them, and re-layouts  4.32 us
    ppermute x1, starting transfers between devices, per_device(): lax.ppermute(product, 'ctx', [(i, i + 1) for i in range(n_ctx - 1)])  3.44 us
  transfers between devices with their start and end apart: 27, of which 7 were waited for; matrix products, arithmetic and copies ran while one was open for 1% of the time, Pallas kernels for 42%

profile of v7, /device:TPU:0, one launch (start us, length us, event | category | flops | bytes accessed | tf_op | source)
XLA Modules:
  0.0 146.8 jit_solution(17598465918568967977)
XLA Ops:
  0.6 1.3 multiply_convert_fusion
  2.0 3.0 %collective-permute-start.6 = (bf16[128,2048]{1,0:T(8,128)(2,1)}, bf16[128,2048]{1,0:T(8,128)(2,1)S(1)}, u32[]{:S(2)}, u32[]{:S(2)}) collective-permute-start(bf16[128,2048]{1,0:T(8,128)(2,1)} %refs_1_.12), channel_id=1, source_target_pairs={{0,2},{1,3},{2,0},{3,1},{4,6},{5,7},{6,4},{7,5},{8,10},{9,11},{10,... | collective-permute-start | bytes 1572872 | tf_op jit(solution)/shard_map/ppermute | solution.py:323
  5.0 3.4 %collective-permute-start = (bf16[128,2048]{1,0:T(8,128)(2,1)S(1)}, bf16[128,2048]{1,0:T(8,128)(2,1)S(1)}, u32[]{:S(2)}, u32[]{:S(2)}) collective-permute-start(bf16[128,2048]{1,0:T(8,128)(2,1)S(1)} %multiply_convert_fusion), channel_id=1, source_target_pairs={{0,4},{4,8},{8,12},{12,16},{16,20},{20,24},{24,28},{1,5},{5,9},{9,... | collective-permute-start | bytes 1572872 | tf_op jit(solution)/shard_map/ppermute | solution.py:430
  9.6 6.4 %grad_gated_part.2.refs_3_ = f32[2048,128]{1,0:T(8,128)S(1)} custom-call(s32[2]{0:T(128)S(1)} %pad_add_fusion.refs_0_.me_ref, bf16[2048,8192]{1,0:T(8,128)(2,1)} %refs_1_.17, bf16[128,2048]{1,0:T(8,128)(2,1)S(1)} %copy-done.1), custom_call_target="tpu_custom_call" | custom-call | flops 3000000000 | tf_op jit(solution)/shard_map/grad_gated_part/pallas_call | solution.py:190
  16.0 1.1 collective-permute-done.6.refs_3_
  17.1 6.2 %grad_gated_part.3.refs_7_.refs_5_.refs_4_ = f32[2048,128]{1,0:T(8,128)S(1)} custom-call(s32[2]{0:T(128)S(1)} %pad_add_fusion.refs_0_.me_ref, bf16[2048,8192]{1,0:T(8,128)(2,1)} %refs_1_.17, bf16[128,2048]{1,0:T(8,128)(2,1)S(1)} %collective-permute-done.1.refs_2_, f32[2048,128]{1,0:T(8,128)S(1)} %grad_gated_part.2.refs_3_), custom_call_target="tpu_custom_call" | custom-call | flops 3000000000 | tf_op jit(solution)/shard_map/grad_gated_part/pallas_call | solution.py:190
  23.4 3.4 %forward_filter.1 = (bf16[128,2048]{1,0:T(8,128)(2,1)S(1)}, f32[128,2048]{1,0:T(8,128)S(1)}) custom-call(bf16[128,2048]{1,0:T(8,128)(2,1)S(1)} %copy-done.2, bf16[128,2048]{1,0:T(8,128)(2,1)S(1)} %copy-done.3, bf16[128,2048]{1,0:T(8,128)(2,1)S(1)} %copy-done.4, bf16[128,2048]{1,0:T(8,128)(2,1)S(1)} %collective-permute-done.refs_3_.refs_2_, ...), custom_call_target="tpu_custom_call" | custom-call | flops 3000000000 | tf_op jit(solution)/shard_map/forward_filter/pallas_call | solution.py:107
  26.8 1.8 %collective-permute-start.4 = (bf16[128,2048]{1,0:T(8,128)(2,1)S(1)}, bf16[128,2048]{1,0:T(8,128)(2,1)S(1)}, u32[]{:S(2)}, u32[]{:S(2)}) collective-permute-start(bf16[128,2048]{1,0:T(8,128)(2,1)S(1)} %get-tuple-element.21.refs_2_.refs_0_), channel_id=1, source_target_pairs={{8,0},{16,8},{24,16},{28,24},{20,28},{12,20},{4,12},{0,4},{9,1},{1... | collective-permute-start | bytes 1572872 | tf_op jit(solution)/shard_map/ppermute | solution.py:462
  29.6 2.9 %collective-permute-start.8 = (bf16[4,256,128]{2,1,0:T(8,128)(2,1)S(1)}, bf16[4,256,128]{2,1,0:T(8,128)(2,1)S(1)}, u32[]{:S(2)}, u32[]{:S(2)}) collective-permute-start(bf16[4,256,128]{2,1,0:T(8,128)(2,1)S(1)} %get-tuple-element.36), channel_id=1, source_target_pairs={{0,16},{4,20},{8,24},{12,28},{16,0},{20,4},{24,8},{28,12},{1,17},{... | collective-permute-start | bytes 786440 | tf_op jit(solution)/shard_map/ppermute | solution.py:323
  32.5 7.4 %grads_and_mixed.2 = (f32[2048,128]{1,0:T(8,128)S(1)}, f32[128,2048]{1,0:T(8,128)S(1)}) custom-call(s32[2]{0:T(128)S(1)} %pad_add_fusion.refs_0_.me_ref, bf16[2048,8192]{1,0:T(8,128)(2,1)} %refs_1_.17, bf16[128,2048]{1,0:T(8,128)(2,1)S(1)} %get-tuple-element.21.refs_2_.refs_0_, bf16[128,2048]{1,0:T(8,128)(2,1)S(1)} %collective-permute-done.6.refs_3_, ...), custom_call_target="tpu_custom_call" | custom-call | flops 6000000000 | tf_op jit(solution)/shard_map/grads_and_mixed/pallas_call | solution.py:190
  39.9 8.3 %grads_and_mixed.3 = (bf16[128,2048]{1,0:T(8,128)(2,1)}, bf16[128,2048]{1,0:T(8,128)(2,1)S(1)}, bf16[128,2048]{1,0:T(8,128)(2,1)S(1)}) custom-call(s32[2]{0:T(128)S(1)} %pad_add_fusion.refs_0_.me_ref, bf16[2048,8192]{1,0:T(8,128)(2,1)} %refs_1_.17, bf16[128,2048]{1,0:T(8,128)(2,1)S(1)} %get-tuple-element.21.refs_2_.refs_0_, ...), custom_call_target="tpu_custom_call" | custom-call | flops 6000000000 | tf_op jit(solution)/shard_map/grads_and_mixed/pallas_call | solution.py:190
  48.2 1.3 collective-permute-start.13
  49.5 3.5 %tap_grad.1.refs_6_ = bf16[2048,128]{1,0:T(8,128)(2,1)S(1)} custom-call(bf16[128,2048]{1,0:T(8,128)(2,1)S(1)} %copy-done.3, bf16[128,2048]{1,0:T(8,128)(2,1)S(1)} %copy-done.4, bf16[128,2048]{1,0:T(8,128)(2,1)S(1)} %collective-permute-done.refs_3_.refs_2_, bf16[128,2048]{1,0:T(8,128)(2,1)S(1)} %get-tuple-element.24.refs_3_.refs_2_, ...), custom_call_target="tpu_custom_call" | custom-call | flops 3000000000 | tf_op jit(solution)/shard_map/tap_grad/pallas_call | solution.py:107
  53.0 2.7 %collective-permute-start.5 = (bf16[128,2048]{1,0:T(8,128)(2,1)S(1)}, bf16[128,2048]{1,0:T(8,128)(2,1)S(1)}, u32[]{:S(2)}, u32[]{:S(2)}) collective-permute-start(bf16[128,2048]{1,0:T(8,128)(2,1)S(1)} %collective-permute-done.4.refs_4_.refs_2_), channel_id=1, source_target_pairs={{8,0},{16,8},{24,16},{28,24},{20,28},{12,20},{4,12},{0,4},{9,1},{1... | collective-permute-start | bytes 1572872 | tf_op jit(solution)/shard_map/ppermute | solution.py:462
  56.8 1.1 collective-permute-start.16
  57.9 1.7 %collective-permute-start.9 = (bf16[4,256,128]{2,1,0:T(8,128)(2,1)S(1)}, bf16[4,256,128]{2,1,0:T(8,128)(2,1)S(1)}, u32[]{:S(2)}, u32[]{:S(2)}) collective-permute-start(bf16[4,256,128]{2,1,0:T(8,128)(2,1)S(1)} %bitcast.19), channel_id=1, source_target_pairs={{0,8},{4,12},{8,0},{12,4},{16,24},{20,28},{24,16},{28,20},{1,9},{5... | collective-permute-start | bytes 786440 | tf_op jit(solution)/shard_map/ppermute | solution.py:323
  59.6 5.7 %mixed_part.2.refs_6_.refs_3_ = bf16[128,2048]{1,0:T(8,128)(2,1)S(1)} custom-call(s32[2]{0:T(128)S(1)} %pad_add_fusion.refs_0_.me_ref, bf16[2048,8192]{1,0:T(8,128)(2,1)} %refs_1_.17, bf16[128,2048]{1,0:T(8,128)(2,1)S(1)} %get-tuple-element.21.refs_2_.refs_0_, bf16[128,2048]{1,0:T(8,128)(2,1)S(1)} %collective-permute-done.2.refs_3_.refs_1_, ...), custom_call_target="tpu_custom_call" | custom-call | flops 3000000000 | tf_op jit(solution)/shard_map/mixed_part/pallas_call | solution.py:190
  65.3 15.4 %collective-permute-done.16.refs_2_ = bf16[1024,128]{1,0:T(8,128)(2,1)S(1)} collective-permute-done((bf16[1024,128]{1,0:T(8,128)(2,1)S(1)}, bf16[1024,128]{1,0:T(8,128)(2,1)S(1)}, u32[]{:S(2)}, u32[]{:S(2)}) %collective-permute-start.16) | collective-permute-done | bytes 262176 | tf_op jit(solution)/shard_map/ppermute | solution.py:323
  81.5 2.5 %collective-permute-start.15 = (bf16[128,2048]{1,0:T(8,128)(2,1)S(1)}, bf16[128,2048]{1,0:T(8,128)(2,1)S(1)}, u32[]{:S(2)}, u32[]{:S(2)}) collective-permute-start(bf16[128,2048]{1,0:T(8,128)(2,1)S(1)} %collective-permute-done.5.refs_4_), channel_id=1, source_target_pairs={{8,0},{16,8},{24,16},{28,24},{20,28},{12,20},{4,12},{0,4},{9,1},{1... | collective-permute-start | bytes 1572872 | tf_op jit(solution)/shard_map/ppermute | solution.py:462
  84.2 2.1 %collective-permute-start.23 = (bf16[4,256,128]{2,1,0:T(8,128)(2,1)S(1)}, bf16[4,256,128]{2,1,0:T(8,128)(2,1)S(1)}, u32[]{:S(2)}, u32[]{:S(2)}) collective-permute-start(bf16[4,256,128]{2,1,0:T(8,128)(2,1)S(1)} %get-tuple-element.33), channel_id=1, source_target_pairs={{0,4},{4,0},{8,12},{12,8},{16,20},{20,16},{24,28},{28,24},{1,5},{5... | collective-permute-start | bytes 786440 | tf_op jit(solution)/shard_map/ppermute | solution.py:323
  86.4 17.3 %collective-permute-done.23 = bf16[4,256,128]{2,1,0:T(8,128)(2,1)S(1)} collective-permute-done((bf16[4,256,128]{2,1,0:T(8,128)(2,1)S(1)}, bf16[4,256,128]{2,1,0:T(8,128)(2,1)S(1)}, u32[]{:S(2)}, u32[]{:S(2)}) %collective-permute-start.23) | collective-permute-done | bytes 262176 | tf_op jit(solution)/shard_map/ppermute | solution.py:323
  103.8 1.5 %collective-permute-start.12 = (bf16[128,2048]{1,0:T(8,128)(2,1)S(1)}, bf16[128,2048]{1,0:T(8,128)(2,1)S(1)}, u32[]{:S(2)}, u32[]{:S(2)}) collective-permute-start(bf16[128,2048]{1,0:T(8,128)(2,1)S(1)} %add_convert_fusion.1), channel_id=1, source_target_pairs={{0,2},{1,3},{2,0},{3,1},{4,6},{5,7},{6,4},{7,5},{8,10},{9,11},{10,... | collective-permute-start | bytes 1572872 | tf_op jit(solution)/shard_map/ppermute | solution.py:323
  105.9 5.7 %mixed_part.3.refs_7_.refs_3_ = f32[128,2048]{1,0:T(8,128)S(1)} custom-call(s32[2]{0:T(128)S(1)} %pad_add_fusion.refs_0_.me_ref, bf16[2048,8192]{1,0:T(8,128)(2,1)} %refs_1_.17, bf16[128,2048]{1,0:T(8,128)(2,1)S(1)} %get-tuple-element.21.refs_2_.refs_0_, bf16[128,2048]{1,0:T(8,128)(2,1)S(1)} %collective-permute-done.3.refs_3_, ...), custom_call_target="tpu_custom_call" | custom-call | flops 3000000000 | tf_op jit(solution)/shard_map/mixed_part/pallas_call | solution.py:190
  112.7 6.9 %collective-permute-done.18.refs_2_ = bf16[512,128]{1,0:T(8,128)(2,1)S(1)} collective-permute-done((bf16[512,128]{1,0:T(8,128)(2,1)S(1)}, bf16[512,128]{1,0:T(8,128)(2,1)S(1)}, u32[]{:S(2)}, u32[]{:S(2)}) %collective-permute-start.18) | collective-permute-done | bytes 131104 | tf_op jit(solution)/shard_map/ppermute | solution.py:323
  119.6 4.0 %backward_filter.1 = (bf16[128,2048]{1,0:T(8,128)(2,1)}, bf16[128,2048]{1,0:T(8,128)(2,1)}) custom-call(bf16[128,2048]{1,0:T(8,128)(2,1)S(1)} %copy-done.3, bf16[128,2048]{1,0:T(8,128)(2,1)S(1)} %copy-done.4, bf16[128,2048]{1,0:T(8,128)(2,1)S(1)} %get-tuple-element.24.refs_3_.refs_2_, bf16[128,2048]{1,0:T(8,128)(2,1)S(1)} %collective-permute-done.13.refs_3_, ...), custom_call_target="tpu_custom_call" | custom-call | flops 3000000000 | tf_op jit(solution)/shard_map/backward_filter/pallas_call | solution.py:107
  123.5 2.4 %collective-permute-done.19.refs_4_.refs_7_ = bf16[128,1024]{1,0:T(8,128)(2,1)S(1)} collective-permute-done((bf16[128,1024]{1,0:T(8,128)(2,1)S(1)}, bf16[128,1024]{1,0:T(8,128)(2,1)S(1)}, u32[]{:S(2)}, u32[]{:S(2)}) %collective-permute-start.19) | collective-permute-done | bytes 262176 | tf_op jit(solution)/shard_map/ppermute | solution.py:464
  127.9 1.5 %collective-permute-done.25.refs_11_ = bf16[8,256,128]{2,1,0:T(8,128)(2,1)S(1)} collective-permute-done((bf16[8,256,128]{2,1,0:T(8,128)(2,1)S(1)}, bf16[8,256,128]{2,1,0:T(8,128)(2,1)S(1)}, u32[]{:S(2)}, u32[]{:S(2)}) %collective-permute-start.25) | collective-permute-done | bytes 524320 | tf_op jit(solution)/shard_map/ppermute | solution.py:323
  130.5 2.1 %collective-permute-done.21.refs_2_ = bf16[512,128]{1,0:T(8,128)(2,1)S(1)} collective-permute-done((bf16[512,128]{1,0:T(8,128)(2,1)S(1)}, bf16[512,128]{1,0:T(8,128)(2,1)S(1)}, u32[]{:S(2)}, u32[]{:S(2)}) %collective-permute-start.21) | collective-permute-done | bytes 131104 | tf_op jit(solution)/shard_map/ppermute | solution.py:323
  133.2 1.2 collective-permute-start.22
  134.4 8.6 %grad_weight.1.refs_3_ = bf16[2048,1024]{1,0:T(8,128)(2,1)} custom-call(s32[2]{0:T(128)S(1)} %pad_add_fusion.refs_0_.me_ref, s32[8,8]{1,0:T(8,128)S(1)} %copy-done.11, bf16[128,2048]{1,0:T(8,128)(2,1)S(1)} %get-tuple-element.21.refs_2_.refs_0_, bf16[128,2048]{1,0:T(8,128)(2,1)S(1)} %collective-permute-done.2.refs_3_.refs_1_, ...), custom_call_target="tpu_custom_call" | custom-call | flops 6000000000 | tf_op jit(solution)/shard_map/grad_weight/pallas_call | solution.py:288
  143.0 2.2 %copy-done = bf16[2048,1024]{1,0:T(8,128)(2,1)S(1)} copy-done((bf16[2048,1024]{1,0:T(8,128)(2,1)S(1)}, bf16[2048,1024]{1,0:T(8,128)(2,1)}, u32[]{:S(2)}) %copy-start) | copy-done | bytes 4194328
  145.2 1.6 %joined.3 = f32[2048,128]{1,0:T(8,128)} custom-call(s32[2]{0:T(128)S(1)} %pad_add_fusion.refs_0_.me_ref, bf16[1024,128]{1,0:T(8,128)(2,1)S(1)} %joined.2.refs_1_, bf16[1024,128]{1,0:T(8,128)(2,1)S(1)} %collective-permute-done.22.refs_2_, bf16[2048,1024]{1,0:T(8,128)(2,1)S(1)} %copy-done), custom_call_target="tpu_custom_call" | custom-call | flops 500000000 | tf_op jit(solution)/shard_map/joined/pallas_call | solution.py:395
  (75 shorter events, 9.3 us)
Async XLA Ops:
  2.0 15.1 %collective-permute-start.6 = (bf16[128,2048]{1,0:T(8,128)(2,1)}, bf16[128,2048]{1,0:T(8,128)(2,1)S(1)}, u32[]{:S(2)}, u32[]{:S(2)}) collective-permute-start(bf16[128,2048]{1,0:T(8,128)(2,1)} %refs_1_.12), channel_id=1, source_target_pairs={{0,2},{1,3},{2,0},{3,1},{4,6},{5,7},{6,4},{7,5},{8,10},{9,11},{10,... | collective-permute-start | bytes 1572872 | tf_op jit(solution)/shard_map/ppermute | solution.py:323
  5.0 12.1 %collective-permute-start.1 = (bf16[128,2048]{1,0:T(8,128)(2,1)}, bf16[128,2048]{1,0:T(8,128)(2,1)S(1)}, u32[]{:S(2)}, u32[]{:S(2)}) collective-permute-start(bf16[128,2048]{1,0:T(8,128)(2,1)} %refs_1_.12), channel_id=1, source_target_pairs={{0,1},{1,0},{2,3},{3,2},{4,5},{5,4},{6,7},{7,6},{8,9},{9,8},{10,11... | collective-permute-start | bytes 1572872 | tf_op jit(solution)/shard_map/ppermute | solution.py:323
  5.0 18.4 %collective-permute-start = (bf16[128,2048]{1,0:T(8,128)(2,1)S(1)}, bf16[128,2048]{1,0:T(8,128)(2,1)S(1)}, u32[]{:S(2)}, u32[]{:S(2)}) collective-permute-start(bf16[128,2048]{1,0:T(8,128)(2,1)S(1)} %multiply_convert_fusion), channel_id=1, source_target_pairs={{0,4},{4,8},{8,12},{12,16},{16,20},{20,24},{24,28},{1,5},{5,9},{9,... | collective-permute-start | bytes 1572872 | tf_op jit(solution)/shard_map/ppermute | solution.py:430
  9.6 13.9 %copy-start.7 = (bf16[2,256,256]{2,1,0:T(8,128)(2,1)S(1)}, bf16[2,256,256]{2,1,0:T(8,128)(2,1)}, u32[]{:S(2)}) copy-start(bf16[2,256,256]{2,1,0:T(8,128)(2,1)} %constant.23.clone.refs_5_.refs_4_) | copy-start | bytes 786436
  9.6 13.9 %copy-start.10 = (bf16[2,128,256]{2,1,0:T(8,128)(2,1)S(1)}, bf16[2,128,256]{2,1,0:T(8,128)(2,1)}, u32[]{:S(2)}) copy-start(bf16[2,128,256]{2,1,0:T(8,128)(2,1)} %constant.24.clone.refs_6_) | copy-start | bytes 393220
  17.1 11.8 %collective-permute-start.7 = (bf16[128,2048]{1,0:T(8,128)(2,1)S(1)}, bf16[128,2048]{1,0:T(8,128)(2,1)S(1)}, u32[]{:S(2)}, u32[]{:S(2)}) collective-permute-start(bf16[128,2048]{1,0:T(8,128)(2,1)S(1)} %collective-permute-done.6.refs_3_), channel_id=1, source_target_pairs={{0,1},{1,0},{2,3},{3,2},{4,5},{5,4},{6,7},{7,6},{8,9},{9,8},{10,11... | collective-permute-start | bytes 1572872 | tf_op jit(solution)/shard_map/ppermute | solution.py:323
  26.8 26.2 %collective-permute-start.4 = (bf16[128,2048]{1,0:T(8,128)(2,1)S(1)}, bf16[128,2048]{1,0:T(8,128)(2,1)S(1)}, u32[]{:S(2)}, u32[]{:S(2)}) collective-permute-start(bf16[128,2048]{1,0:T(8,128)(2,1)S(1)} %get-tuple-element.21.refs_2_.refs_0_), channel_id=1, source_target_pairs={{8,0},{16,8},{24,16},{28,24},{20,28},{12,20},{4,12},{0,4},{9,1},{1... | collective-permute-start | bytes 1572872 | tf_op jit(solution)/shard_map/ppermute | solution.py:462
  28.6 27.1 %collective-permute-start.2 = (bf16[128,2048]{1,0:T(8,128)(2,1)S(1)}, bf16[128,2048]{1,0:T(8,128)(2,1)S(1)}, u32[]{:S(2)}, u32[]{:S(2)}) collective-permute-start(bf16[128,2048]{1,0:T(8,128)(2,1)S(1)} %get-tuple-element.21.refs_2_.refs_0_), channel_id=1, source_target_pairs={{0,8},{8,16},{16,24},{24,28},{28,20},{20,12},{12,4},{4,0},{1,9},{9... | collective-permute-start | bytes 1572872 | tf_op jit(solution)/shard_map/ppermute | solution.py:461
  29.6 19.9 %copy-start.9 = (bf16[2,128,256]{2,1,0:T(8,128)(2,1)S(1)}, bf16[2,128,256]{2,1,0:T(8,128)(2,1)}, u32[]{:S(2)}) copy-start(bf16[2,128,256]{2,1,0:T(8,128)(2,1)} %constant.26.clone.refs_5_) | copy-start | bytes 393220
  29.6 28.3 %collective-permute-start.8 = (bf16[4,256,128]{2,1,0:T(8,128)(2,1)S(1)}, bf16[4,256,128]{2,1,0:T(8,128)(2,1)S(1)}, u32[]{:S(2)}, u32[]{:S(2)}) collective-permute-start(bf16[4,256,128]{2,1,0:T(8,128)(2,1)S(1)} %get-tuple-element.36), channel_id=1, source_target_pairs={{0,16},{4,20},{8,24},{12,28},{16,0},{20,4},{24,8},{28,12},{1,17},{... | collective-permute-start | bytes 786440 | tf_op jit(solution)/shard_map/ppermute | solution.py:323
  48.2 64.2 %collective-permute-start.13 = (bf16[128,2048]{1,0:T(8,128)(2,1)S(1)}, bf16[128,2048]{1,0:T(8,128)(2,1)S(1)}, u32[]{:S(2)}, u32[]{:S(2)}) collective-permute-start(bf16[128,2048]{1,0:T(8,128)(2,1)S(1)} %get-tuple-element.24.refs_3_.refs_2_), channel_id=1, source_target_pairs={{4,0},{8,4},{12,8},{16,12},{20,16},{24,20},{28,24},{5,1},{9,5},{13... | collective-permute-start | bytes 1572872 | tf_op jit(solution)/shard_map/ppermute | solution.py:473
  53.0 28.4 %collective-permute-start.5 = (bf16[128,2048]{1,0:T(8,128)(2,1)S(1)}, bf16[128,2048]{1,0:T(8,128)(2,1)S(1)}, u32[]{:S(2)}, u32[]{:S(2)}) collective-permute-start(bf16[128,2048]{1,0:T(8,128)(2,1)S(1)} %collective-permute-done.4.refs_4_.refs_2_), channel_id=1, source_target_pairs={{8,0},{16,8},{24,16},{28,24},{20,28},{12,20},{4,12},{0,4},{9,1},{1... | collective-permute-start | bytes 1572872 | tf_op jit(solution)/shard_map/ppermute | solution.py:462
  55.7 25.8 %collective-permute-start.3 = (bf16[128,2048]{1,0:T(8,128)(2,1)S(1)}, bf16[128,2048]{1,0:T(8,128)(2,1)S(1)}, u32[]{:S(2)}, u32[]{:S(2)}) collective-permute-start(bf16[128,2048]{1,0:T(8,128)(2,1)S(1)} %collective-permute-done.2.refs_3_.refs_1_), channel_id=1, source_target_pairs={{0,8},{8,16},{16,24},{24,28},{28,20},{20,12},{12,4},{4,0},{1,9},{9... | collective-permute-start | bytes 1572872 | tf_op jit(solution)/shard_map/ppermute | solution.py:461
  56.8 24.0 %collective-permute-start.16 = (bf16[1024,128]{1,0:T(8,128)(2,1)S(1)}, bf16[1024,128]{1,0:T(8,128)(2,1)S(1)}, u32[]{:S(2)}, u32[]{:S(2)}) collective-permute-start(bf16[1024,128]{1,0:T(8,128)(2,1)S(1)} %get-tuple-element.34), channel_id=1, source_target_pairs={{0,4},{4,0},{8,12},{12,8},{16,20},{20,16},{24,28},{28,24},{1,5},{5... | collective-permute-start | bytes 786440 | tf_op jit(solution)/shard_map/ppermute | solution.py:323
  57.9 61.6 %copy-start.8 = (bf16[2,128,256]{2,1,0:T(8,128)(2,1)S(1)}, bf16[2,128,256]{2,1,0:T(8,128)(2,1)}, u32[]{:S(2)}) copy-start(bf16[2,128,256]{2,1,0:T(8,128)(2,1)} %constant.25.clone.refs_6_) | copy-start | bytes 393220
  57.9 26.1 %collective-permute-start.9 = (bf16[4,256,128]{2,1,0:T(8,128)(2,1)S(1)}, bf16[4,256,128]{2,1,0:T(8,128)(2,1)S(1)}, u32[]{:S(2)}, u32[]{:S(2)}) collective-permute-start(bf16[4,256,128]{2,1,0:T(8,128)(2,1)S(1)} %bitcast.19), channel_id=1, source_target_pairs={{0,8},{4,12},{8,0},{12,4},{16,24},{20,28},{24,16},{28,20},{1,9},{5... | collective-permute-start | bytes 786440 | tf_op jit(solution)/shard_map/ppermute | solution.py:323
  65.3 69.1 %copy-start.11 = (s32[8,8]{1,0:T(8,128)S(1)}, s32[8,8]{1,0:T(8,128)}, u32[]{:S(2)}) copy-start(s32[8,8]{1,0:T(8,128)} %constant.27.clone.owner_ref) | copy-start | bytes 772
  80.8 3.4 %collective-permute-start.11 = (bf16[128,2048]{1,0:T(8,128)(2,1)S(1)}, bf16[128,2048]{1,0:T(8,128)(2,1)S(1)}, u32[]{:S(2)}, u32[]{:S(2)}) collective-permute-start(bf16[128,2048]{1,0:T(8,128)(2,1)S(1)} %get-tuple-element.26), channel_id=1, source_target_pairs={{0,1},{1,0},{2,3},{3,2},{4,5},{5,4},{6,7},{7,6},{8,9},{9,8},{10,11... | collective-permute-start | bytes 1572872 | tf_op jit(solution)/shard_map/ppermute | solution.py:323
  81.4 22.3 %collective-permute-start.17 = (bf16[512,128]{1,0:T(8,128)(2,1)S(1)}, bf16[512,128]{1,0:T(8,128)(2,1)S(1)}, u32[]{:S(2)}, u32[]{:S(2)}) collective-permute-start(bf16[512,128]{1,0:T(8,128)(2,1)S(1)} %get-tuple-element.31), channel_id=1, source_target_pairs={{0,8},{4,12},{8,0},{12,4},{16,24},{20,28},{24,16},{28,20},{1,9},{5... | collective-permute-start | bytes 393224 | tf_op jit(solution)/shard_map/ppermute | solution.py:323
  81.5 23.8 %collective-permute-start.15 = (bf16[128,2048]{1,0:T(8,128)(2,1)S(1)}, bf16[128,2048]{1,0:T(8,128)(2,1)S(1)}, u32[]{:S(2)}, u32[]{:S(2)}) collective-permute-start(bf16[128,2048]{1,0:T(8,128)(2,1)S(1)} %collective-permute-done.5.refs_4_), channel_id=1, source_target_pairs={{8,0},{16,8},{24,16},{28,24},{20,28},{12,20},{4,12},{0,4},{9,1},{1... | collective-permute-start | bytes 1572872 | tf_op jit(solution)/shard_map/ppermute | solution.py:462
  84.1 28.2 %collective-permute-start.14 = (bf16[128,2048]{1,0:T(8,128)(2,1)S(1)}, bf16[128,2048]{1,0:T(8,128)(2,1)S(1)}, u32[]{:S(2)}, u32[]{:S(2)}) collective-permute-start(bf16[128,2048]{1,0:T(8,128)(2,1)S(1)} %collective-permute-done.3.refs_3_), channel_id=1, source_target_pairs={{0,8},{8,16},{16,24},{24,28},{28,20},{20,12},{12,4},{4,0},{1,9},{9... | collective-permute-start | bytes 1572872 | tf_op jit(solution)/shard_map/ppermute | solution.py:461
  84.2 19.6 %collective-permute-start.23 = (bf16[4,256,128]{2,1,0:T(8,128)(2,1)S(1)}, bf16[4,256,128]{2,1,0:T(8,128)(2,1)S(1)}, u32[]{:S(2)}, u32[]{:S(2)}) collective-permute-start(bf16[4,256,128]{2,1,0:T(8,128)(2,1)S(1)} %get-tuple-element.33), channel_id=1, source_target_pairs={{0,4},{4,0},{8,12},{12,8},{16,20},{20,16},{24,28},{28,24},{1,5},{5... | collective-permute-start | bytes 786440 | tf_op jit(solution)/shard_map/ppermute | solution.py:323
  103.7 25.7 %collective-permute-start.10 = (bf16[128,2048]{1,0:T(8,128)(2,1)S(1)}, bf16[128,2048]{1,0:T(8,128)(2,1)S(1)}, u32[]{:S(2)}, u32[]{:S(2)}) collective-permute-start(bf16[128,2048]{1,0:T(8,128)(2,1)S(1)} %mixed_part.2.refs_6_.refs_3_), channel_id=1, source_target_pairs={{0,1},{1,0},{2,3},{3,2},{4,5},{5,4},{6,7},{7,6},{8,9},{9,8},{10,11... | collective-permute-start | bytes 1572872 | tf_op jit(solution)/shard_map/ppermute | solution.py:323
  103.8 25.6 %collective-permute-start.12 = (bf16[128,2048]{1,0:T(8,128)(2,1)S(1)}, bf16[128,2048]{1,0:T(8,128)(2,1)S(1)}, u32[]{:S(2)}, u32[]{:S(2)}) collective-permute-start(bf16[128,2048]{1,0:T(8,128)(2,1)S(1)} %add_convert_fusion.1), channel_id=1, source_target_pairs={{0,2},{1,3},{2,0},{3,1},{4,6},{5,7},{6,4},{7,5},{8,10},{9,11},{10,... | collective-permute-start | bytes 1572872 | tf_op jit(solution)/shard_map/ppermute | solution.py:323
  105.3 24.1 %collective-permute-start.25 = (bf16[8,256,128]{2,1,0:T(8,128)(2,1)S(1)}, bf16[8,256,128]{2,1,0:T(8,128)(2,1)S(1)}, u32[]{:S(2)}, u32[]{:S(2)}) collective-permute-start(bf16[8,256,128]{2,1,0:T(8,128)(2,1)S(1)} %maximum_bitcast_fusion.refs_9_), channel_id=1, source_target_pairs={{0,2},{1,3},{2,0},{3,1},{4,6},{5,7},{6,4},{7,5},{8,10},{9,11},{10,... | collective-permute-start | bytes 1572872 | tf_op jit(solution)/shard_map/ppermute | solution.py:323
  112.2 7.3 %collective-permute-start.18 = (bf16[512,128]{1,0:T(8,128)(2,1)S(1)}, bf16[512,128]{1,0:T(8,128)(2,1)S(1)}, u32[]{:S(2)}, u32[]{:S(2)}) collective-permute-start(bf16[512,128]{1,0:T(8,128)(2,1)S(1)} %added.4.refs_1_), channel_id=1, source_target_pairs={{0,16},{4,20},{8,24},{12,28},{16,0},{20,4},{24,8},{28,12},{1,17},{... | collective-permute-start | bytes 393224 | tf_op jit(solution)/shard_map/ppermute | solution.py:323
  112.4 11.2 %collective-permute-start.20 = (bf16[128,1024]{1,0:T(8,128)(2,1)S(1)}, bf16[128,1024]{1,0:T(8,128)(2,1)S(1)}, u32[]{:S(2)}, u32[]{:S(2)}) collective-permute-start(bf16[128,1024]{1,0:T(8,128)(2,1)S(1)} %slice.47), channel_id=1, source_target_pairs={{8,0},{16,8},{24,16},{28,24},{20,28},{12,20},{4,12},{0,4},{9,1},{1... | collective-permute-start | bytes 786440 | tf_op jit(solution)/shard_map/ppermute | solution.py:465
  119.6 6.4 %collective-permute-start.19 = (bf16[128,1024]{1,0:T(8,128)(2,1)S(1)}, bf16[128,1024]{1,0:T(8,128)(2,1)S(1)}, u32[]{:S(2)}, u32[]{:S(2)}) collective-permute-start(bf16[128,1024]{1,0:T(8,128)(2,1)S(1)} %slice.46), channel_id=1, source_target_pairs={{0,8},{8,16},{16,24},{24,28},{28,20},{20,12},{12,4},{4,0},{1,9},{9... | collective-permute-start | bytes 786440 | tf_op jit(solution)/shard_map/ppermute | solution.py:464
  123.5 10.9 %collective-permute-start.24 = (bf16[8,256,128]{2,1,0:T(8,128)(2,1)S(1)}, bf16[8,256,128]{2,1,0:T(8,128)(2,1)S(1)}, u32[]{:S(2)}, u32[]{:S(2)}) collective-permute-start(bf16[8,256,128]{2,1,0:T(8,128)(2,1)S(1)} %maximum_bitcast_fusion.refs_9_), channel_id=1, source_target_pairs={{0,1},{1,0},{2,3},{3,2},{4,5},{5,4},{6,7},{7,6},{8,9},{9,8},{10,11... | collective-permute-start | bytes 1572872 | tf_op jit(solution)/shard_map/ppermute | solution.py:323
  127.6 5.0 %collective-permute-start.21 = (bf16[512,128]{1,0:T(8,128)(2,1)S(1)}, bf16[512,128]{1,0:T(8,128)(2,1)S(1)}, u32[]{:S(2)}, u32[]{:S(2)}) collective-permute-start(bf16[512,128]{1,0:T(8,128)(2,1)S(1)} %added.5.refs_1_), channel_id=1, source_target_pairs={{0,8},{4,12},{8,0},{12,4},{16,24},{20,28},{24,16},{28,20},{1,9},{5... | collective-permute-start | bytes 393224 | tf_op jit(solution)/shard_map/ppermute | solution.py:323
  129.4 5.0 %collective-permute-start.26 = (bf16[8,256,128]{2,1,0:T(8,128)(2,1)S(1)}, bf16[8,256,128]{2,1,0:T(8,128)(2,1)S(1)}, u32[]{:S(2)}, u32[]{:S(2)}) collective-permute-start(bf16[8,256,128]{2,1,0:T(8,128)(2,1)S(1)} %collective-permute-done.25.refs_11_), channel_id=1, source_target_pairs={{0,1},{1,0},{2,3},{3,2},{4,5},{5,4},{6,7},{7,6},{8,9},{9,8},{10,11... | collective-permute-start | bytes 1572872 | tf_op jit(solution)/shard_map/ppermute | solution.py:323
  133.2 9.8 %collective-permute-start.22 = (bf16[1024,128]{1,0:T(8,128)(2,1)S(1)}, bf16[1024,128]{1,0:T(8,128)(2,1)S(1)}, u32[]{:S(2)}, u32[]{:S(2)}) collective-permute-start(bf16[1024,128]{1,0:T(8,128)(2,1)S(1)} %joined.2.refs_1_), channel_id=1, source_target_pairs={{0,4},{4,0},{8,12},{12,8},{16,20},{20,16},{24,28},{28,24},{1,5},{5... | collective-permute-start | bytes 786440 | tf_op jit(solution)/shard_map/ppermute | solution.py:323
  (7 other events, 59.6 us)

commit v8 on v7

--- a/solution.py
+++ b/solution.py
@@ -61,9 +61,9 @@
     gated_ref[...] = (q_ref[...].astype(F32) * filtered).astype(BF16)
 
 
-def tap_grad_kernel(taps, k_ref, v_ref, earlier_ref, gf_ref, f_ref, g_ref, out_ref):
+def tap_grad_kernel(taps, k_ref, v_ref, low_ref, high_ref, gf_ref, f_ref, g_ref, out_ref):
     product = (k_ref[...].astype(F32) * v_ref[...].astype(F32)).astype(BF16)
-    x = spectrum(f_ref, jnp.concatenate([earlier_ref[...], product], axis=0))
+    x = spectrum(f_ref, jnp.concatenate([of_half(low_ref, high_ref), product], axis=0))
     rows = gf_ref[...]
     g = mm(f_ref[0, :, :taps], rows) + mm(f_ref[1, :, :taps], rows)
     xr, xi, gr, gi = x[:taps], x[taps:], g[:taps], g[taps:]
@@ -91,40 +91,61 @@
     return kernel
 
 
-def by_channel(kernel, arrays, kinds, outs, name, after=()):
+def half_specs(shape, count):
+    middle = count // 2
+    return [
+        pl.BlockSpec(shape, lambda i, *ids: (0, jnp.minimum(i, middle - 1))),
+        pl.BlockSpec(shape, lambda i, *ids: (0, jnp.maximum(i - middle, 0))),
+    ]
+
+
+def of_half(low_ref, high_ref):
+    return jnp.where(pl.program_id(0) < pl.num_programs(0) // 2, low_ref[...], high_ref[...])
+
+
+def by_channel(kernel, arrays, kinds, outs, name, after=(), half=None):
     length, channels = arrays[0].shape
-    width = min(512, channels)
+    width = min(512, channels // 2)
+    steps = channels // width
+    first = 0
+    if half is not None:
+        channels, steps = channels // 2, steps // 2
+        first = half * steps
     specs = {
-        "t": pl.BlockSpec((length, width), lambda i: (0, i)),
-        "c": pl.BlockSpec((width, length), lambda i: (i, 0)),
+        "t": pl.BlockSpec((length, width), lambda i: (0, first + i)),
+        "c": pl.BlockSpec((width, length), lambda i: (first + i, 0)),
+        "n": pl.BlockSpec((length, width), lambda i: (0, i)),
     }
-
-    def spec_of(kind, shape):
-        if kind == "w":
-            return pl.BlockSpec(shape, lambda i: (0,) * len(shape))
-        return specs[kind]
-
+    operands, in_specs = [], []
+    for kind, array in zip(kinds, arrays):
+        if kind == "h":
+            operands += array
+            in_specs += half_specs((length, width), steps)
+            continue
+        operands.append(array)
+        in_specs.append(
+            pl.BlockSpec(array.shape, lambda i, rank=array.ndim: (0,) * rank) if kind == "w" else specs[kind]
+        )
     return pl.pallas_call(
-        ignoring(functools.partial(kernel, length), len(after), len(arrays)),
-        grid=(channels // width,),
-        in_specs=[spec_of(kind, a.shape) for kind, a in zip(kinds, arrays)]
-        + [pl.BlockSpec(memory_space=pl.ANY)] * len(after),
+        ignoring(functools.partial(kernel, length), len(after), len(operands)),
+        grid=(steps,),
+        in_specs=in_specs + [pl.BlockSpec(memory_space=pl.ANY)] * len(after),
         out_specs=[specs[kind] for kind, unused in outs],
         out_shape=[
-            jax.ShapeDtypeStruct((length, channels) if kind == "t" else (channels, length), dtype)
+            jax.ShapeDtypeStruct((channels, length) if kind == "c" else (length, channels), dtype)
             for kind, dtype in outs
         ],
         compiler_params=pltpu.CompilerParams(vmem_limit_bytes=VMEM_BYTES),
-        cost_estimate=estimate(3),
+        cost_estimate=estimate(0.7),
         name=name,
-    )(*arrays, *after)
+    )(*operands, *after)
 
 
 def pass_kernel(with_mixed, with_grad, has_sum, last, me_ref, w_ref, *refs):
     refs = list(refs)
     step = pl.program_id(0)
     if with_mixed:
-        gated_ref = refs.pop(0)
+        gated = of_half(refs.pop(0), refs.pop(0))
     if with_grad:
         cot_ref = refs.pop(0)
         sum_ref = refs.pop(0) if has_sum else None
@@ -138,15 +159,15 @@
         if has_sum:
             total = total + sum_ref[...]
         if last:
-            q_ref, filtered_ref, gq_ref, gf_ref = refs[:4]
+            q_ref, low_ref, high_ref, gq_ref, gf_ref = refs[:5]
             total = total.T
-            gq_ref[...] = (total * filtered_ref[...]).astype(BF16)
+            gq_ref[...] = (total * of_half(low_ref, high_ref)).astype(BF16)
             gf_ref[...] = (total * q_ref[...].astype(F32)).astype(BF16)
         else:
             refs[0][...] = total
     if with_mixed:
         held_ref, mixed_ref = refs.pop(), refs.pop()
-        part = mm(gated_ref[...], w_ref[...])
+        part = mm(gated, w_ref[...])
 
         @pl.when(step == 0)
         def first():
@@ -162,7 +183,7 @@
 
 
 def weight_pass(me, weight, off, gated=None, cot=None, sums=(), ends=(), after=()):
-    length = (cot if gated is None else gated).shape[0]
+    length = (cot if gated is None else gated[0]).shape[0]
     channels = weight.shape[0]
     tile = 512
     whole = pl.BlockSpec((length, channels), lambda r, me: (0, 0))
@@ -170,12 +191,13 @@
     by_row = pl.BlockSpec((tile, length), lambda r, me: (r, 0))
     arrays, in_specs = [weight], [pl.BlockSpec((tile, channels), lambda r, me: (r, me[1] ^ off))]
     out_specs, out_shape, scratch = [], [], []
+    by_half = half_specs((length, tile), channels // tile)
     if gated is not None:
-        arrays.append(gated)
-        in_specs.append(by_token)
+        arrays += gated
+        in_specs += by_half
     if cot is not None:
         arrays += [cot, *sums, *ends]
-        in_specs += [whole] + [by_row] * len(sums) + [by_token] * len(ends)
+        in_specs += [whole] + [by_row] * len(sums) + ([by_token] + by_half if ends else [])
         out_specs += [by_token] * 2 if ends else [by_row]
         out_shape += [jax.ShapeDtypeStruct((length, channels), BF16)] * 2 if ends else [
             jax.ShapeDtypeStruct((channels, length), F32)
@@ -198,7 +220,7 @@
         ),
         out_shape=out_shape,
         compiler_params=pltpu.CompilerParams(vmem_limit_bytes=VMEM_BYTES),
-        cost_estimate=estimate(3 * ((cot is not None) + (gated is not None))),
+        cost_estimate=estimate(0.7 * ((cot is not None) + (gated is not None))),
         name="grad_gated_part" if gated is None else "mixed_part" if cot is None else "grads_and_mixed",
     )(me, *arrays, *after)
 
@@ -253,14 +275,11 @@
     return parts[(order // per_chan ^ me[1]) * per_chan + order % per_chan]
 
 
-def weight_kernel(slots, parts, half, me_ref, owner_ref, *refs):
-    gated_refs = refs[: slots - 1]
-    far_low, far_high = refs[slots - 1 : slots + 1]
-    cot_refs = refs[slots + 1 : slots + 1 + parts]
+def weight_kernel(slots, parts, me_ref, owner_ref, *refs):
+    cot_refs = refs[slots : slots + parts]
     out_ref = refs[-1]
-    length = far_low.shape[0]
-    far = jnp.where(pl.program_id(0) < half, far_low[...], far_high[...])
-    columns = jnp.concatenate([ref[...] for ref in gated_refs] + [far], axis=0)
+    length = refs[0].shape[0]
+    columns = jnp.concatenate([ref[...] for ref in refs[:slots]], axis=0)
     for part in range(parts):
         rows = []
         for slot in range(slots):
@@ -274,30 +293,29 @@
         out_ref[:, pl.ds(place, piece)] = total.astype(BF16)
 
 
-def grad_weight_of(me, owners, blocks, far_low, far_high, cots):
+def grad_weight_of(me, owners, blocks, cots, earlier):
     length, channels = blocks[0].shape
     rows = cots[0].shape[1]
     piece = rows * 128 // length
     tile = 256
-    half = channels // tile // 2
-    slots, parts = len(blocks) + 1, len(cots)
+    first = len(earlier) * (channels // tile)
+    slots, parts = len(blocks), len(cots)
     in_specs = [pl.BlockSpec((length, tile), lambda i, *ids: (0, i)) for unused in blocks]
-    in_specs.append(pl.BlockSpec((length, tile), lambda i, *ids: (0, jnp.minimum(i, half - 1))))
-    in_specs.append(pl.BlockSpec((length, tile), lambda i, *ids: (0, jnp.maximum(i - half, 0))))
     in_specs += [pl.BlockSpec(cot.shape, lambda i, *ids: (0, 0, 0)) for cot in cots]
     return pl.pallas_call(
-        functools.partial(weight_kernel, slots, parts, half),
+        ignoring(functools.partial(weight_kernel, slots, parts), len(earlier), 2 + slots + parts),
         grid_spec=pltpu.PrefetchScalarGridSpec(
             num_scalar_prefetch=2,
             grid=(channels // tile,),
-            in_specs=in_specs,
-            out_specs=pl.BlockSpec((tile, piece * parts), lambda i, *ids: (i, 0)),
+            in_specs=in_specs + [pl.BlockSpec(memory_space=pl.ANY)] * len(earlier),
+            out_specs=pl.BlockSpec((tile, piece * parts), lambda i, *ids: (first + i, 0)),
         ),
-        out_shape=jax.ShapeDtypeStruct((channels, piece * parts), BF16),
+        out_shape=jax.ShapeDtypeStruct((2 * channels, piece * parts), BF16),
+        input_output_aliases={2 + slots + parts: 0} if earlier else {},
         compiler_params=pltpu.CompilerParams(vmem_limit_bytes=VMEM_BYTES),
-        cost_estimate=estimate(6),
+        cost_estimate=estimate(2),
         name="grad_weight",
-    )(me, owners, *blocks, far_low, far_high, *cots)
+    )(me, owners, *blocks, *cots, *earlier)
 
 
 def in_one_piece(me, columns, length):
@@ -316,6 +334,44 @@
         line = [row * across + column for row in range(count // across)]
         order += line if column % 2 == 0 else line[::-1]
     return order
+
+
+def held_until(arrays, kernels):
+    return lax.optimization_barrier((*arrays, *kernels))[: len(arrays)]
+
+
+class Gather:
+    def __init__(self, count):
+        self.order = cycle_of(count)
+        self.ahead = [(self.order[i], self.order[(i + 1) % count]) for i in range(count)]
+        self.behind = [(b, a) for a, b in self.ahead]
+        self.last = count // 2 - 1
+        self.ends = [None, None]
+        self.blocks = [[], []]
+        self.turns = []
+
+    def start(self, part, block):
+        self.ends[part] = (block, block)
+        self.blocks[part].append(block)
+        self.turns.insert(0, (part, 0))
+        self.step(())
+
+    def step(self, kernels):
+        if not self.turns:
+            return []
+        part, step = self.turns.pop(0)
+        came = list(self.ends[part]) if step else []
+        from_behind, from_ahead = held_until(self.ends[part], kernels) if kernels else self.ends[part]
+        if step == self.last:
+            far = lax.ppermute(from_ahead, "ctx", self.behind) if part else lax.ppermute(from_behind, "ctx", self.ahead)
+            self.blocks[part].append(far)
+            return came
+        self.ends[part] = (
+            lax.ppermute(from_behind, "ctx", self.ahead), lax.ppermute(from_ahead, "ctx", self.behind)
+        )
+        self.blocks[part] += self.ends[part]
+        self.turns.append((part, step + 1))
+        return came
 
 
 def swap(block, axis, bit):
@@ -378,7 +434,7 @@
         came = swap(send if step < 2 else sums, "ctx", bit)
         sums, *send = added(me, sums, came, bits[1] if step == 0 else 0, gates[step] if step < len(gates) else ())
         send = send[0] if send else None
-    sums = joined(me, sums, swap(sums, "ctx", bits[1]), bits[1], BF16, ())
+    sums = joined(me, sums, swap(sums, "ctx", bits[1]), bits[1], BF16, gates[-1])
     return sums, swap(sums, "ctx", bits[0]), bits[0]
 
 
@@ -407,15 +463,23 @@
     )(me, own, other, *after)
 
 
-def exchanged(pieces):
-    held, sources, stages = pieces[None], [0], []
-    for bit in reversed(bits_of(pieces.shape[0])):
-        give = held[:, bit:].reshape((-1,) + pieces.shape[1:])
-        stages.append(swap(give, "ctx", bit))
-        came = stages[-1].reshape((len(sources), bit) + pieces.shape[1:])
-        held = jnp.concatenate([held[:, :bit], came], axis=0)
-        sources += [source ^ bit for source in sources]
-    return held[:, 0], sources, stages
+class Exchange:
+    def __init__(self, pieces):
+        self.shape = pieces.shape[1:]
+        self.held, self.sources = pieces[None], [0]
+        self.bits = bits_of(pieces.shape[0])
+
+    def step(self, kernels):
+        if not self.bits:
+            return []
+        bit = self.bits.pop()
+        give = self.held[:, bit:].reshape((-1,) + self.shape)
+        came = swap(held_until([give], kernels)[0], "ctx", bit)
+        self.held = jnp.concatenate(
+            [self.held[:, :bit], came.reshape((len(self.sources), bit) + self.shape)], axis=0
+        )
+        self.sources += [source ^ bit for source in self.sources]
+        return [came]
 
 
 def per_device(query_proj, key_proj, value_proj, filters, out_weight, cotangent):
@@ -425,68 +489,79 @@
     me = jnp.stack([lax.axis_index("ctx"), lax.axis_index("chan")]).astype(jnp.int32)
     forward, late, early, lags = [jnp.asarray(m) for m in transforms(taps)]
 
-    product = (key_proj.astype(F32) * value_proj.astype(F32)).astype(BF16)
-    product, cotangent = lax.optimization_barrier((product, cotangent))
-    earlier = lax.ppermute(product, "ctx", [(i, i + 1) for i in range(n_ctx - 1)])
+    half = channels // 2
+    halves_at = [slice(0, half), slice(half, channels)]
+    products = [
+        (key_proj[:, at].astype(F32) * value_proj[:, at].astype(F32)).astype(BF16) for at in halves_at
+    ]
+    *products, cotangent = lax.optimization_barrier((*products, cotangent))
+    onward = [(i, i + 1) for i in range(n_ctx - 1)]
+    earlier = [lax.ppermute(product, "ctx", onward) for product in products]
 
     cots = {0: cotangent, 1: swap(cotangent, "chan", 1)}
     for bit in reversed(bits_of(n_chan)[1:]):
         cots.update({off ^ bit: swap(cots[off], "chan", bit) for off in list(cots) if off % 2 == 0})
     offs = sorted(off for off in cots if off % 2 == 0 and off)
+    sums = weight_pass(me, out_weight, 0, cot=cots[0])
     for off in offs:
-        cots[off + 1] = swap(cots[off], "chan", 1)
+        cots[off + 1] = swap(held_until([cots[off]], sums)[0], "chan", 1)
     offs = sorted(offs + [off + 1 for off in offs])
-    sums = weight_pass(me, out_weight, 0, cot=cots[0])
-    sums = weight_pass(me, out_weight, 1, cot=cots[1], sums=sums)
-
-    gated, filtered = by_channel(
-        forward_kernel,
-        [query_proj, key_proj, value_proj, earlier, filters, forward, late],
-        "ttttcww",
-        [("t", BF16), ("t", F32)],
-        "forward_filter",
-        after=sums,
-    )
+
+    gather = Gather(n_ctx)
+    gated, filtered = [], []
+    for part in (0, 1):
+        gated_half, filtered_half = by_channel(
+            forward_kernel,
+            [query_proj, key_proj, value_proj, earlier[part], filters, forward, late],
+            "tttncww",
+            [("n", BF16), ("n", F32)],
+            "forward_filter",
+            [*sums, *gated],
+            part,
+        )
+        gated.append(gated_half)
+        filtered.append(filtered_half)
+        gather.start(part, gated_half)
+    sums = weight_pass(me, out_weight, 1, cot=cots[1], sums=sums, after=gated)
+    came = gather.step(sums)
 
     pieces = pieces_of(me, [cots[off] for off in range(n_chan)], n_ctx, sums)
-    held, sources, stages = exchanged(pieces)
-
-    order = cycle_of(n_ctx)
-    ahead = [(order[i], order[(i + 1) % n_ctx]) for i in range(n_ctx)]
-    behind = [(b, a) for a, b in ahead]
-    half = channels // 2
-    from_behind, from_ahead = gated, gated
-    blocks = [gated]
-    for step in range(n_ctx // 2 - 1):
-        from_behind = lax.ppermute(from_behind, "ctx", ahead)
-        from_ahead = lax.ppermute(from_ahead, "ctx", behind)
-        blocks += [from_behind, from_ahead]
-    far_low = lax.ppermute(from_behind[:, :half], "ctx", ahead)
-    far_high = lax.ppermute(from_ahead[:, half:], "ctx", behind)
+    exchange = Exchange(pieces)
+    brought = exchange.step([pieces])
 
     terms = {}
     for off in offs[:-1]:
-        *sums, terms[off] = weight_pass(me, out_weight, off, gated, cots[off], sums, after=[pieces])
+        *sums, terms[off] = weight_pass(me, out_weight, off, gated, cots[off], sums, after=[pieces] + came)
+        came = gather.step(sums)
     grad_query, grad_filtered, terms[offs[-1]] = weight_pass(
-        me, out_weight, offs[-1], gated, cots[offs[-1]], sums, [query_proj, filtered]
+        me, out_weight, offs[-1], gated, cots[offs[-1]], sums, [query_proj, *filtered], came
     )
-    following = lax.ppermute(grad_filtered, "ctx", [(i + 1, i) for i in range(n_ctx - 1)])
+    came = gather.step([grad_filtered])
 
     tap_grad = by_channel(
         tap_grad_kernel,
         [key_proj, value_proj, earlier, grad_filtered, forward, lags],
-        "ttttww",
+        "tthtww",
         [("c", BF16)],
         "tap_grad",
+        came + brought,
     )[0]
-
-    terms[1] = weight_pass(me, out_weight, 1, gated, after=blocks[1:3] + stages[:1] + [tap_grad])[0]
-    terms[0] = weight_pass(me, out_weight, 0, gated, after=blocks[3:5] + stages[1:2] + [terms[1]])[0]
+    brought = exchange.step([tap_grad])
+    given = held_until([grad_filtered], [tap_grad])[0]
+    following = lax.ppermute(given, "ctx", [(b, a) for a, b in onward])
+    came = gather.step([tap_grad])
+
+    terms[1] = weight_pass(me, out_weight, 1, gated, after=came + [tap_grad])[0]
+    came = gather.step([terms[1]])
+    terms[0] = weight_pass(me, out_weight, 0, gated, after=came + brought + [terms[1]])[0]
+    came = gather.step([terms[0]])
+    while exchange.bits:
+        exchange.step([terms[0]])
     gates = [[terms[1]], [terms[0]]]
     for bit in bits_of(n_chan):
         for off in [off for off in sorted(terms, reverse=True) if off & bit]:
-            came = swap(terms.pop(off).astype(BF16), "chan", bit).astype(F32)
-            terms[off ^ bit] = terms[off ^ bit] + came
+            other = swap(terms.pop(off).astype(BF16), "chan", bit).astype(F32)
+            terms[off ^ bit] = terms[off ^ bit] + other
     mixed = terms[0].astype(BF16)
 
     grad_key, grad_value = by_channel(
@@ -495,20 +570,26 @@
         "ttttcww",
         [("t", BF16), ("t", BF16)],
         "backward_filter",
-        after=gates[-1] + blocks[5:7],
+        gates[-1] + came,
     )
-    halves_summed = summed(me, tap_grad, gates + [[grad_key, far_low, far_high]])
-
-    columns = gather_by_swaps(held)
+    while gather.turns:
+        gather.step(())
+    order, blocks = gather.order, gather.blocks
+    gates += [[grad_key, blocks[0][-1]], blocks[1][-1:]]
+    halves_summed = summed(me, tap_grad, gates)
+
+    columns = gather_by_swaps(exchange.held[:, 0])
     columns = [columns[off] for off in range(n_chan)]
     if (channels // n_ctx) % 128:
         columns = in_one_piece(me, columns, length)
     owners = []
     for c in range(n_ctx):
         spot = order.index(c)
-        steps = [0] + [sign * step for step in range(1, n_ctx // 2) for sign in (-1, 1)] + [n_ctx // 2]
-        owners.append([sources.index(order[(spot + step) % n_ctx] ^ c) for step in steps])
-    grad_weight = grad_weight_of(me, jnp.asarray(owners, jnp.int32), blocks, far_low, far_high, columns)
+        turns = [0] + [sign * step for step in range(1, n_ctx // 2) for sign in (-1, 1)] + [n_ctx // 2]
+        owners.append([exchange.sources.index(order[(spot + turn) % n_ctx] ^ c) for turn in turns])
+    owners = jnp.asarray(owners, jnp.int32)
+    grad_weight = grad_weight_of(me, owners, blocks[0], columns, [])
+    grad_weight = grad_weight_of(me, owners, blocks[1], columns, [grad_weight])
     grad_filters = joined(me, *halves_summed, F32, [grad_weight])
     return (mixed, grad_query, grad_key, grad_value, grad_filters, grad_weight)
 

time: 147 us -> 148 us (level)
  waiting for transfers between devices: 46.9 us -> 27.4 us
  starting transfers between devices: 27.9 us -> 37.9 us
  Pallas kernels: 63.9 us -> 69.7 us
  local copies, waits for them, and re-layouts: 4.45 us -> 7.82 us
    ppermute x17, waiting for transfers between devices: 44.4 us -> 17.9 us  [swap(): return lax.ppermute(block, axis, [(i, i ^ bit) for i in range(size)])]
    ppermute x10 -> x17, starting transfers between devices: 13.4 us -> 23.8 us  [the longest x7 9.72 us: step(): lax.ppermute(from_behind, 'ctx', self.ahead)]
    ppermute x10 -> x17, waiting for transfers between devices: 2.42 us -> 9.47 us  [the longest x7 5.56 us: step(): lax.ppermute(from_ahead, 'ctx', self.behind)]
    unnamed x24 -> x40, local copies, waits for them, and re-layouts: 4.32 us -> 7.73 us
    pallas_call x1 -> x2, Pallas kernels: 8.6 us -> 10.8 us  [grad_weight_of(): pl.pallas_call(ignoring(functools.partial(weight_kernel, slots, parts), l...]
    pallas_call x3 -> x4, Pallas kernels: 10.9 us -> 12.7 us  [by_channel(): pl.pallas_call(ignoring(functools.partial(kernel, length), len(after), le...]
  transfers between devices with their start and end apart: 27 -> 34, of which waited for: 7 -> 11; matrix products, arithmetic and copies ran while one was open for 1% -> 1% of each run, Pallas kernels for 42% -> 46%
where the time goes in v8:
time: 148 us; the launch traced here: 147 us
  Pallas kernels  69.7 us (47%)
  starting transfers between devices  37.9 us (26%)
  waiting for transfers between devices  27.4 us (19%)
  local copies, waits for them, and re-layouts  7.82 us (5%)
  other arithmetic  3.49 us (2%)
    pallas_call x6, Pallas kernels, weight_pass(): pl.pallas_call(ignoring(body, len(after), 1 + len(arrays)), grid_spec=plt...  40.3 us
    ppermute x17, waiting for transfers between devices, swap(): return lax.ppermute(block, axis, [(i, i ^ bit) for i in range(size)])  17.9 us
    ppermute x17, starting transfers between devices, swap(): return lax.ppermute(block, axis, [(i, i ^ bit) for i in range(size)])  14 us
    pallas_call x4, Pallas kernels, by_channel(): pl.pallas_call(ignoring(functools.partial(kernel, length), len(after), le...  12.7 us
    pallas_call x2, Pallas kernels, grad_weight_of(): pl.pallas_call(ignoring(functools.partial(weight_kernel, slots, parts), l...  10.8 us
    ppermute x7, starting transfers between devices, step(): lax.ppermute(from_behind, 'ctx', self.ahead)  9.72 us
    ppermute x2, starting transfers between devices, per_device(): earlier = [lax.ppermute(product, 'ctx', onward) for product in products]  7.8 us
    unnamed x40, local copies, waits for them, and re-layouts  7.73 us
  transfers between devices with their start and end apart: 34, of which 11 were waited for; matrix products, arithmetic and copies ran while one was open for 1% of the time, Pallas kernels for 46%

profile of v8, /device:TPU:0, one launch (start us, length us, event | category | flops | bytes accessed | tf_op | source)
XLA Modules:
  0.0 147.4 jit_solution(1513692846104026786)
XLA Ops:
  0.6 2.2 %multiply_convert_fusion = (bf16[128,1024]{1,0:T(8,128)(2,1)}, bf16[128,1024]{1,0:T(8,128)(2,1)}) fusion(bf16[128,2048]{1,0:T(8,128)(2,1)} %refs_1_.22, bf16[128,2048]{1,0:T(8,128)(2,1)} %refs_0_.7), kind=kLoop, calls=%fused_computation.7 | loop fusion | flops 1048576 | bytes 1572864 | tf_op jit(solution)/shard_map/convert_element_type | solution.py:495
  2.8 2.9 %collective-permute-start.7 = (bf16[128,2048]{1,0:T(8,128)(2,1)}, bf16[128,2048]{1,0:T(8,128)(2,1)}, u32[]{:S(2)}, u32[]{:S(2)}) collective-permute-start(bf16[128,2048]{1,0:T(8,128)(2,1)} %refs_1_.16), channel_id=1, source_target_pairs={{0,2},{1,3},{2,0},{3,1},{4,6},{5,7},{6,4},{7,5},{8,10},{9,11},{10,... | collective-permute-start | bytes 1572872 | tf_op jit(solution)/shard_map/ppermute | solution.py:379
  5.8 3.4 %collective-permute-start = (bf16[128,1024]{1,0:T(8,128)(2,1)}, bf16[128,1024]{1,0:T(8,128)(2,1)S(1)}, u32[]{:S(2)}, u32[]{:S(2)}) collective-permute-start(bf16[128,1024]{1,0:T(8,128)(2,1)} %get-tuple-element.37), channel_id=1, source_target_pairs={{0,4},{4,8},{8,12},{12,16},{16,20},{20,24},{24,28},{1,5},{5,9},{9,... | collective-permute-start | bytes 786440 | tf_op jit(solution)/shard_map/ppermute | solution.py:499
  10.3 6.4 %grad_gated_part.2.refs_7_.refs_3_ = f32[2048,128]{1,0:T(8,128)S(1)} custom-call(s32[2]{0:T(128)S(1)} %pad_add_fusion.refs_0_, bf16[2048,8192]{1,0:T(8,128)(2,1)} %refs_1_.21, bf16[128,2048]{1,0:T(8,128)(2,1)S(1)} %copy-done.8), custom_call_target="tpu_custom_call" | custom-call | flops 700000000 | tf_op jit(solution)/shard_map/grad_gated_part/pallas_call | solution.py:212
  18.0 4.4 %collective-permute-start.1 = (bf16[128,1024]{1,0:T(8,128)(2,1)}, bf16[128,1024]{1,0:T(8,128)(2,1)}, u32[]{:S(2)}, u32[]{:S(2)}) collective-permute-start(bf16[128,1024]{1,0:T(8,128)(2,1)} %get-tuple-element.40), channel_id=1, source_target_pairs={{0,4},{4,8},{8,12},{12,16},{16,20},{20,24},{24,28},{1,5},{5,9},{9,... | collective-permute-start | bytes 786440 | tf_op jit(solution)/shard_map/ppermute | solution.py:499
  29.5 2.5 %forward_filter.3 = (bf16[128,1024]{1,0:T(8,128)(2,1)S(1)}, f32[128,1024]{1,0:T(8,128)S(1)}) custom-call(bf16[128,2048]{1,0:T(8,128)(2,1)S(1)} %copy-done.3, bf16[128,2048]{1,0:T(8,128)(2,1)S(1)} %copy-done.1, bf16[128,2048]{1,0:T(8,128)(2,1)S(1)} %copy-done.2, bf16[128,1024]{1,0:T(8,128)(2,1)} %collective-permute-done.1.refs_3_, ...), custom_call_target="tpu_custom_call" | custom-call | flops 700000000 | tf_op jit(solution)/shard_map/forward_filter/pallas_call | solution.py:129
  32.1 2.5 %collective-permute-start.10 = (bf16[128,1024]{1,0:T(8,128)(2,1)S(1)}, bf16[128,1024]{1,0:T(8,128)(2,1)S(1)}, u32[]{:S(2)}, u32[]{:S(2)}) collective-permute-start(bf16[128,1024]{1,0:T(8,128)(2,1)S(1)} %get-tuple-element.41.refs_5_.refs_3_.refs_2_), channel_id=1, source_target_pairs={{8,0},{16,8},{24,16},{28,24},{20,28},{12,20},{4,12},{0,4},{9,1},{1... | collective-permute-start | bytes 786440 | tf_op jit(solution)/shard_map/ppermute | solution.py:370
  35.5 6.3 %grad_gated_part.3.refs_5_ = f32[2048,128]{1,0:T(8,128)S(1)} custom-call(s32[2]{0:T(128)S(1)} %pad_add_fusion.refs_0_, bf16[2048,8192]{1,0:T(8,128)(2,1)} %refs_1_.21, bf16[128,2048]{1,0:T(8,128)(2,1)} %collective-permute-done.4.refs_2_, f32[2048,128]{1,0:T(8,128)S(1)} %grad_gated_part.2.refs_7_.refs_3_, ...), custom_call_target="tpu_custom_call" | custom-call | flops 700000000 | tf_op jit(solution)/shard_map/grad_gated_part/pallas_call | solution.py:212
  41.9 2.0 %collective-permute-start.5 = (bf16[128,1024]{1,0:T(8,128)(2,1)}, bf16[128,1024]{1,0:T(8,128)(2,1)S(1)}, u32[]{:S(2)}, u32[]{:S(2)}) collective-permute-start(bf16[128,1024]{1,0:T(8,128)(2,1)} %collective-permute-done.2.refs_7_.refs_3_), channel_id=1, source_target_pairs={{0,8},{8,16},{16,24},{24,28},{28,20},{20,12},{12,4},{4,0},{1,9},{9... | collective-permute-start | bytes 786440 | tf_op jit(solution)/shard_map/ppermute | solution.py:370
  44.0 2.0 %pieces.1.refs_6_ = bf16[8,256,128]{2,1,0:T(8,128)(2,1)S(1)} custom-call(s32[2]{0:T(128)S(1)} %pad_add_fusion.refs_0_, bf16[128,2048]{1,0:T(8,128)(2,1)S(1)} %copy-done.9, bf16[128,2048]{1,0:T(8,128)(2,1)} %collective-permute-done.4.refs_2_, bf16[128,2048]{1,0:T(8,128)(2,1)} %collective-permute-done.7.refs_3_.refs_4_, ...), custom_call_target="tpu_custom_call" | custom-call | flops 500000000 | tf_op jit(solution)/shard_map/pieces/pallas_call | solution.py:250
  46.0 3.0 %collective-permute-start.13 = (bf16[4,256,128]{2,1,0:T(8,128)(2,1)S(1)}, bf16[4,256,128]{2,1,0:T(8,128)(2,1)S(1)}, u32[]{:S(2)}, u32[]{:S(2)}) collective-permute-start(bf16[4,256,128]{2,1,0:T(8,128)(2,1)S(1)} %get-tuple-element.51), channel_id=1, source_target_pairs={{0,16},{4,20},{8,24},{12,28},{16,0},{20,4},{24,8},{28,12},{1,17},{... | collective-permute-start | bytes 786440 | tf_op jit(solution)/shard_map/ppermute | solution.py:379
  49.0 7.6 %grads_and_mixed.2 = (f32[2048,128]{1,0:T(8,128)S(1)}, f32[128,2048]{1,0:T(8,128)S(1)}) custom-call(s32[2]{0:T(128)S(1)} %pad_add_fusion.refs_0_, bf16[2048,8192]{1,0:T(8,128)(2,1)} %refs_1_.21, bf16[128,1024]{1,0:T(8,128)(2,1)S(1)} %get-tuple-element.39.refs_8_.refs_4_.refs_2_, bf16[128,1024]{1,0:T(8,128)(2,1)S(1)} %get-tuple-element.41.refs_5_.refs_3_.refs_2_, ...), custom_call_target="tpu_custom_call" | custom-call | flops 1400000000 | tf_op jit(solution)/shard_map/grads_and_mixed/pallas_call | solution.py:212
  56.7 8.5 %grads_and_mixed.3 = (bf16[128,2048]{1,0:T(8,128)(2,1)}, bf16[128,2048]{1,0:T(8,128)(2,1)S(1)}, bf16[128,2048]{1,0:T(8,128)(2,1)S(1)}) custom-call(s32[2]{0:T(128)S(1)} %pad_add_fusion.refs_0_, bf16[2048,8192]{1,0:T(8,128)(2,1)} %refs_1_.21, bf16[128,1024]{1,0:T(8,128)(2,1)S(1)} %get-tuple-element.39.refs_8_.refs_4_.refs_2_, ...), custom_call_target="tpu_custom_call" | custom-call | flops 1400000000 | tf_op jit(solution)/shard_map/grads_and_mixed/pallas_call | solution.py:212
  65.2 1.8 %collective-permute-start.15 = (bf16[128,1024]{1,0:T(8,128)(2,1)S(1)}, bf16[128,1024]{1,0:T(8,128)(2,1)S(1)}, u32[]{:S(2)}, u32[]{:S(2)}) collective-permute-start(bf16[128,1024]{1,0:T(8,128)(2,1)S(1)} %collective-permute-done.9.refs_9_.refs_3_), channel_id=1, source_target_pairs={{0,8},{8,16},{16,24},{24,28},{28,20},{20,12},{12,4},{4,0},{1,9},{9... | collective-permute-start | bytes 786440 | tf_op jit(solution)/shard_map/ppermute | solution.py:370
  67.2 1.7 %collective-permute-start.11 = (bf16[128,1024]{1,0:T(8,128)(2,1)S(1)}, bf16[128,1024]{1,0:T(8,128)(2,1)S(1)}, u32[]{:S(2)}, u32[]{:S(2)}) collective-permute-start(bf16[128,1024]{1,0:T(8,128)(2,1)S(1)} %collective-permute-done.5.refs_7_.refs_5_), channel_id=1, source_target_pairs={{0,8},{8,16},{16,24},{24,28},{28,20},{20,12},{12,4},{4,0},{1,9},{9... | collective-permute-start | bytes 786440 | tf_op jit(solution)/shard_map/ppermute | solution.py:370
  69.3 4.5 %tap_grad.1.refs_6_ = bf16[2048,128]{1,0:T(8,128)(2,1)S(1)} custom-call(bf16[128,2048]{1,0:T(8,128)(2,1)S(1)} %copy-done.1, bf16[128,2048]{1,0:T(8,128)(2,1)S(1)} %copy-done.2, bf16[128,1024]{1,0:T(8,128)(2,1)S(1)} %copy-done.12, bf16[128,1024]{1,0:T(8,128)(2,1)} %collective-permute-done.1.refs_3_, bf16[128,2048]{1,0:T(8,128)(2,1)S(1)} %get-tuple-element.58.refs_4_.refs_2_, ...), custom_call_target="tpu_custom_call" | custom-call | flops 700000000 | tf_op jit(solution)/shard_map/tap_grad/pallas_call | solution.py:129
  73.9 1.8 %collective-permute-start.14 = (bf16[4,256,128]{2,1,0:T(8,128)(2,1)S(1)}, bf16[4,256,128]{2,1,0:T(8,128)(2,1)S(1)}, u32[]{:S(2)}, u32[]{:S(2)}) collective-permute-start(bf16[4,256,128]{2,1,0:T(8,128)(2,1)S(1)} %bitcast.19), channel_id=1, source_target_pairs={{0,8},{4,12},{8,0},{12,4},{16,24},{20,28},{24,16},{28,20},{1,9},{5... | collective-permute-start | bytes 786440 | tf_op jit(solution)/shard_map/ppermute | solution.py:379
  76.2 5.7 %mixed_part.2.refs_7_.refs_3_ = bf16[128,2048]{1,0:T(8,128)(2,1)S(1)} custom-call(s32[2]{0:T(128)S(1)} %pad_add_fusion.refs_0_, bf16[2048,8192]{1,0:T(8,128)(2,1)} %refs_1_.21, bf16[128,1024]{1,0:T(8,128)(2,1)S(1)} %get-tuple-element.39.refs_8_.refs_4_.refs_2_, bf16[128,1024]{1,0:T(8,128)(2,1)S(1)} %get-tuple-element.41.refs_5_.refs_3_.refs_2_, ...), custom_call_target="tpu_custom_call" | custom-call | flops 700000000 | tf_op jit(solution)/shard_map/mixed_part/pallas_call | solution.py:212
  81.9 2.1 %collective-permute-done.14.refs_6_ = bf16[4,256,128]{2,1,0:T(8,128)(2,1)S(1)} collective-permute-done((bf16[4,256,128]{2,1,0:T(8,128)(2,1)S(1)}, bf16[4,256,128]{2,1,0:T(8,128)(2,1)S(1)}, u32[]{:S(2)}, u32[]{:S(2)}) %collective-permute-start.14) | collective-permute-done | bytes 262176 | tf_op jit(solution)/shard_map/ppermute | solution.py:379
  84.1 5.8 %mixed_part.3.refs_7_.refs_3_ = f32[128,2048]{1,0:T(8,128)S(1)} custom-call(s32[2]{0:T(128)S(1)} %pad_add_fusion.refs_0_, bf16[2048,8192]{1,0:T(8,128)(2,1)} %refs_1_.21, bf16[128,1024]{1,0:T(8,128)(2,1)S(1)} %get-tuple-element.39.refs_8_.refs_4_.refs_2_, bf16[128,1024]{1,0:T(8,128)(2,1)S(1)} %get-tuple-element.41.refs_5_.refs_3_.refs_2_, ...), custom_call_target="tpu_custom_call" | custom-call | flops 700000000 | tf_op jit(solution)/shard_map/mixed_part/pallas_call | solution.py:212
  93.7 5.5 %collective-permute-done.30 = bf16[4,256,128]{2,1,0:T(8,128)(2,1)S(1)} collective-permute-done((bf16[4,256,128]{2,1,0:T(8,128)(2,1)S(1)}, bf16[4,256,128]{2,1,0:T(8,128)(2,1)S(1)}, u32[]{:S(2)}, u32[]{:S(2)}) %collective-permute-start.30) | collective-permute-done | bytes 262176 | tf_op jit(solution)/shard_map/ppermute | solution.py:379
  100.6 2.1 %collective-permute-start.24 = (bf16[512,128]{1,0:T(8,128)(2,1)S(1)}, bf16[512,128]{1,0:T(8,128)(2,1)S(1)}, u32[]{:S(2)}, u32[]{:S(2)}) collective-permute-start(bf16[512,128]{1,0:T(8,128)(2,1)S(1)} %get-tuple-element.64), channel_id=1, source_target_pairs={{0,8},{4,12},{8,0},{12,4},{16,24},{20,28},{24,16},{28,20},{1,9},{5... | collective-permute-start | bytes 393224 | tf_op jit(solution)/shard_map/ppermute | solution.py:379
  102.7 2.1 %collective-permute-done.21.refs_8_.refs_7_ = bf16[128,1024]{1,0:T(8,128)(2,1)S(1)} collective-permute-done((bf16[128,1024]{1,0:T(8,128)(2,1)S(1)}, bf16[128,1024]{1,0:T(8,128)(2,1)S(1)}, u32[]{:S(2)}, u32[]{:S(2)}) %collective-permute-start.21) | collective-permute-done | bytes 262176 | tf_op jit(solution)/shard_map/ppermute | solution.py:370
  106.5 3.6 %collective-permute-done.22.refs_9_.refs_8_ = bf16[128,1024]{1,0:T(8,128)(2,1)S(1)} collective-permute-done((bf16[128,1024]{1,0:T(8,128)(2,1)S(1)}, bf16[128,1024]{1,0:T(8,128)(2,1)S(1)}, u32[]{:S(2)}, u32[]{:S(2)}) %collective-permute-start.22) | collective-permute-done | bytes 262176 | tf_op jit(solution)/shard_map/ppermute | solution.py:370
  110.1 4.7 %collective-permute-done.24.refs_2_ = bf16[512,128]{1,0:T(8,128)(2,1)S(1)} collective-permute-done((bf16[512,128]{1,0:T(8,128)(2,1)S(1)}, bf16[512,128]{1,0:T(8,128)(2,1)S(1)}, u32[]{:S(2)}, u32[]{:S(2)}) %collective-permute-start.24) | collective-permute-done | bytes 131104 | tf_op jit(solution)/shard_map/ppermute | solution.py:379
  117.0 1.7 %collective-permute-done.20.refs_3_ = bf16[128,2048]{1,0:T(8,128)(2,1)S(1)} collective-permute-done((bf16[128,2048]{1,0:T(8,128)(2,1)S(1)}, bf16[128,2048]{1,0:T(8,128)(2,1)S(1)}, u32[]{:S(2)}, u32[]{:S(2)}) %collective-permute-start.20) | collective-permute-done | bytes 524320 | tf_op jit(solution)/shard_map/ppermute | solution.py:551
  118.7 4.0 %backward_filter.1 = (bf16[128,2048]{1,0:T(8,128)(2,1)}, bf16[128,2048]{1,0:T(8,128)(2,1)}) custom-call(bf16[128,2048]{1,0:T(8,128)(2,1)S(1)} %copy-done.1, bf16[128,2048]{1,0:T(8,128)(2,1)S(1)} %copy-done.2, bf16[128,2048]{1,0:T(8,128)(2,1)S(1)} %get-tuple-element.58.refs_4_.refs_2_, bf16[128,2048]{1,0:T(8,128)(2,1)S(1)} %collective-permute-done.20.refs_3_, ...), custom_call_target="tpu_custom_call" | custom-call | flops 700000000 | tf_op jit(solution)/shard_map/backward_filter/pallas_call | solution.py:129
  122.7 1.7 %collective-permute-done.25.refs_2_ = bf16[512,128]{1,0:T(8,128)(2,1)S(1)} collective-permute-done((bf16[512,128]{1,0:T(8,128)(2,1)S(1)}, bf16[512,128]{1,0:T(8,128)(2,1)S(1)}, u32[]{:S(2)}, u32[]{:S(2)}) %collective-permute-start.25) | collective-permute-done | bytes 131104 | tf_op jit(solution)/shard_map/ppermute | solution.py:379
  128.4 2.7 %collective-permute-done.27.refs_2_ = bf16[512,128]{1,0:T(8,128)(2,1)S(1)} collective-permute-done((bf16[512,128]{1,0:T(8,128)(2,1)S(1)}, bf16[512,128]{1,0:T(8,128)(2,1)S(1)}, u32[]{:S(2)}, u32[]{:S(2)}) %collective-permute-start.27) | collective-permute-done | bytes 131104 | tf_op jit(solution)/shard_map/ppermute | solution.py:379
  132.8 5.8 %grad_weight.2.refs_14_ = bf16[2048,1024]{1,0:T(8,128)(2,1)} custom-call(s32[2]{0:T(128)S(1)} %pad_add_fusion.refs_0_, s32[8,8]{1,0:T(8,128)S(1)} %copy-done.18, bf16[128,1024]{1,0:T(8,128)(2,1)S(1)} %get-tuple-element.39.refs_8_.refs_4_.refs_2_, bf16[128,1024]{1,0:T(8,128)(2,1)} %collective-permute-done.2.refs_7_.refs_3_, ...), custom_call_target="tpu_custom_call" | custom-call | flops 2000000000 | tf_op jit(solution)/shard_map/grad_weight/pallas_call | solution.py:305
  138.6 5.0 %grad_weight.3.refs_3_ = bf16[2048,1024]{1,0:T(8,128)(2,1)} custom-call(s32[2]{0:T(128)S(1)} %pad_add_fusion.refs_0_, s32[8,8]{1,0:T(8,128)S(1)} %copy-done.18, bf16[128,1024]{1,0:T(8,128)(2,1)S(1)} %get-tuple-element.41.refs_5_.refs_3_.refs_2_, bf16[128,1024]{1,0:T(8,128)(2,1)S(1)} %collective-permute-done.9.refs_9_.refs_3_, ...), custom_call_target="tpu_custom_call", output_to_operand_aliasing={{}: (14, {})} | custom-call | flops 2000000000 | tf_op jit(solution)/shard_map/grad_weight/pallas_call | solution.py:305
  143.6 2.2 %copy-done = bf16[2048,1024]{1,0:T(8,128)(2,1)S(1)} copy-done((bf16[2048,1024]{1,0:T(8,128)(2,1)S(1)}, bf16[2048,1024]{1,0:T(8,128)(2,1)}, u32[]{:S(2)}) %copy-start) | copy-done | bytes 4194328
  (105 shorter events, 28.1 us)
Async XLA Ops:
  2.8 15.2 %collective-permute-start.7 = (bf16[128,2048]{1,0:T(8,128)(2,1)}, bf16[128,2048]{1,0:T(8,128)(2,1)}, u32[]{:S(2)}, u32[]{:S(2)}) collective-permute-start(bf16[128,2048]{1,0:T(8,128)(2,1)} %refs_1_.16), channel_id=1, source_target_pairs={{0,2},{1,3},{2,0},{3,1},{4,6},{5,7},{6,4},{7,5},{8,10},{9,11},{10,... | collective-permute-start | bytes 1572872 | tf_op jit(solution)/shard_map/ppermute | solution.py:379
  5.7 28.8 %collective-permute-start.4 = (bf16[128,2048]{1,0:T(8,128)(2,1)}, bf16[128,2048]{1,0:T(8,128)(2,1)}, u32[]{:S(2)}, u32[]{:S(2)}) collective-permute-start(bf16[128,2048]{1,0:T(8,128)(2,1)} %refs_1_.16), channel_id=1, source_target_pairs={{0,1},{1,0},{2,3},{3,2},{4,5},{5,4},{6,7},{7,6},{8,9},{9,8},{10,11... | collective-permute-start | bytes 1572872 | tf_op jit(solution)/shard_map/ppermute | solution.py:379
  5.8 16.6 %collective-permute-start = (bf16[128,1024]{1,0:T(8,128)(2,1)}, bf16[128,1024]{1,0:T(8,128)(2,1)S(1)}, u32[]{:S(2)}, u32[]{:S(2)}) collective-permute-start(bf16[128,1024]{1,0:T(8,128)(2,1)} %get-tuple-element.37), channel_id=1, source_target_pairs={{0,4},{4,8},{8,12},{12,16},{16,20},{20,24},{24,28},{1,5},{5,9},{9,... | collective-permute-start | bytes 786440 | tf_op jit(solution)/shard_map/ppermute | solution.py:499
  18.0 26.0 %collective-permute-start.8 = (bf16[128,2048]{1,0:T(8,128)(2,1)}, bf16[128,2048]{1,0:T(8,128)(2,1)}, u32[]{:S(2)}, u32[]{:S(2)}) collective-permute-start(bf16[128,2048]{1,0:T(8,128)(2,1)} %collective-permute-done.7.refs_3_.refs_4_), channel_id=1, source_target_pairs={{0,1},{1,0},{2,3},{3,2},{4,5},{5,4},{6,7},{7,6},{8,9},{9,8},{10,11... | collective-permute-start | bytes 1572872 | tf_op jit(solution)/shard_map/ppermute | solution.py:379
  18.0 10.6 %collective-permute-start.1 = (bf16[128,1024]{1,0:T(8,128)(2,1)}, bf16[128,1024]{1,0:T(8,128)(2,1)}, u32[]{:S(2)}, u32[]{:S(2)}) collective-permute-start(bf16[128,1024]{1,0:T(8,128)(2,1)} %get-tuple-element.40), channel_id=1, source_target_pairs={{0,4},{4,8},{8,12},{12,16},{16,20},{20,24},{24,28},{1,5},{5,9},{9,... | collective-permute-start | bytes 786440 | tf_op jit(solution)/shard_map/ppermute | solution.py:499
  26.5 15.3 %collective-permute-start.3 = (bf16[128,1024]{1,0:T(8,128)(2,1)S(1)}, bf16[128,1024]{1,0:T(8,128)(2,1)}, u32[]{:S(2)}, u32[]{:S(2)}) collective-permute-start(bf16[128,1024]{1,0:T(8,128)(2,1)S(1)} %get-tuple-element.39.refs_8_.refs_4_.refs_2_), channel_id=1, source_target_pairs={{8,0},{16,8},{24,16},{28,24},{20,28},{12,20},{4,12},{0,4},{9,1},{1... | collective-permute-start | bytes 786440 | tf_op jit(solution)/shard_map/ppermute | solution.py:370
  27.4 14.5 %collective-permute-start.2 = (bf16[128,1024]{1,0:T(8,128)(2,1)S(1)}, bf16[128,1024]{1,0:T(8,128)(2,1)}, u32[]{:S(2)}, u32[]{:S(2)}) collective-permute-start(bf16[128,1024]{1,0:T(8,128)(2,1)S(1)} %get-tuple-element.39.refs_8_.refs_4_.refs_2_), channel_id=1, source_target_pairs={{0,8},{8,16},{16,24},{24,28},{28,20},{20,12},{12,4},{4,0},{1,9},{9... | collective-permute-start | bytes 786440 | tf_op jit(solution)/shard_map/ppermute | solution.py:370
  32.1 24.5 %collective-permute-start.10 = (bf16[128,1024]{1,0:T(8,128)(2,1)S(1)}, bf16[128,1024]{1,0:T(8,128)(2,1)S(1)}, u32[]{:S(2)}, u32[]{:S(2)}) collective-permute-start(bf16[128,1024]{1,0:T(8,128)(2,1)S(1)} %get-tuple-element.41.refs_5_.refs_3_.refs_2_), channel_id=1, source_target_pairs={{8,0},{16,8},{24,16},{28,24},{20,28},{12,20},{4,12},{0,4},{9,1},{1... | collective-permute-start | bytes 786440 | tf_op jit(solution)/shard_map/ppermute | solution.py:370
  34.5 22.1 %collective-permute-start.9 = (bf16[128,1024]{1,0:T(8,128)(2,1)S(1)}, bf16[128,1024]{1,0:T(8,128)(2,1)S(1)}, u32[]{:S(2)}, u32[]{:S(2)}) collective-permute-start(bf16[128,1024]{1,0:T(8,128)(2,1)S(1)} %get-tuple-element.41.refs_5_.refs_3_.refs_2_), channel_id=1, source_target_pairs={{0,8},{8,16},{16,24},{24,28},{28,20},{20,12},{12,4},{4,0},{1,9},{9... | collective-permute-start | bytes 786440 | tf_op jit(solution)/shard_map/ppermute | solution.py:370
  41.9 23.3 %collective-permute-start.5 = (bf16[128,1024]{1,0:T(8,128)(2,1)}, bf16[128,1024]{1,0:T(8,128)(2,1)S(1)}, u32[]{:S(2)}, u32[]{:S(2)}) collective-permute-start(bf16[128,1024]{1,0:T(8,128)(2,1)} %collective-permute-done.2.refs_7_.refs_3_), channel_id=1, source_target_pairs={{0,8},{8,16},{16,24},{24,28},{28,20},{20,12},{12,4},{4,0},{1,9},{9... | collective-permute-start | bytes 786440 | tf_op jit(solution)/shard_map/ppermute | solution.py:370
  43.9 21.3 %collective-permute-start.6 = (bf16[128,1024]{1,0:T(8,128)(2,1)}, bf16[128,1024]{1,0:T(8,128)(2,1)S(1)}, u32[]{:S(2)}, u32[]{:S(2)}) collective-permute-start(bf16[128,1024]{1,0:T(8,128)(2,1)} %collective-permute-done.3.refs_8_.refs_4_), channel_id=1, source_target_pairs={{8,0},{16,8},{24,16},{28,24},{20,28},{12,20},{4,12},{0,4},{9,1},{1... | collective-permute-start | bytes 786440 | tf_op jit(solution)/shard_map/ppermute | solution.py:370
  46.0 23.3 %collective-permute-start.13 = (bf16[4,256,128]{2,1,0:T(8,128)(2,1)S(1)}, bf16[4,256,128]{2,1,0:T(8,128)(2,1)S(1)}, u32[]{:S(2)}, u32[]{:S(2)}) collective-permute-start(bf16[4,256,128]{2,1,0:T(8,128)(2,1)S(1)} %get-tuple-element.51), channel_id=1, source_target_pairs={{0,16},{4,20},{8,24},{12,28},{16,0},{20,4},{24,8},{28,12},{1,17},{... | collective-permute-start | bytes 786440 | tf_op jit(solution)/shard_map/ppermute | solution.py:379
  65.2 10.5 %collective-permute-start.15 = (bf16[128,1024]{1,0:T(8,128)(2,1)S(1)}, bf16[128,1024]{1,0:T(8,128)(2,1)S(1)}, u32[]{:S(2)}, u32[]{:S(2)}) collective-permute-start(bf16[128,1024]{1,0:T(8,128)(2,1)S(1)} %collective-permute-done.9.refs_9_.refs_3_), channel_id=1, source_target_pairs={{0,8},{8,16},{16,24},{24,28},{28,20},{20,12},{12,4},{4,0},{1,9},{9... | collective-permute-start | bytes 786440 | tf_op jit(solution)/shard_map/ppermute | solution.py:370
  66.9 9.2 %collective-permute-start.16 = (bf16[128,1024]{1,0:T(8,128)(2,1)S(1)}, bf16[128,1024]{1,0:T(8,128)(2,1)S(1)}, u32[]{:S(2)}, u32[]{:S(2)}) collective-permute-start(bf16[128,1024]{1,0:T(8,128)(2,1)S(1)} %collective-permute-done.10.refs_10_.refs_4_), channel_id=1, source_target_pairs={{8,0},{16,8},{24,16},{28,24},{20,28},{12,20},{4,12},{0,4},{9,1},{1... | collective-permute-start | bytes 786440 | tf_op jit(solution)/shard_map/ppermute | solution.py:370
  67.2 16.9 %collective-permute-start.11 = (bf16[128,1024]{1,0:T(8,128)(2,1)S(1)}, bf16[128,1024]{1,0:T(8,128)(2,1)S(1)}, u32[]{:S(2)}, u32[]{:S(2)}) collective-permute-start(bf16[128,1024]{1,0:T(8,128)(2,1)S(1)} %collective-permute-done.5.refs_7_.refs_5_), channel_id=1, source_target_pairs={{0,8},{8,16},{16,24},{24,28},{28,20},{20,12},{12,4},{4,0},{1,9},{9... | collective-permute-start | bytes 786440 | tf_op jit(solution)/shard_map/ppermute | solution.py:370
  69.0 15.2 %collective-permute-start.12 = (bf16[128,1024]{1,0:T(8,128)(2,1)S(1)}, bf16[128,1024]{1,0:T(8,128)(2,1)S(1)}, u32[]{:S(2)}, u32[]{:S(2)}) collective-permute-start(bf16[128,1024]{1,0:T(8,128)(2,1)S(1)} %collective-permute-done.6.refs_8_.refs_6_), channel_id=1, source_target_pairs={{8,0},{16,8},{24,16},{28,24},{20,28},{12,20},{4,12},{0,4},{9,1},{1... | collective-permute-start | bytes 786440 | tf_op jit(solution)/shard_map/ppermute | solution.py:370
  73.9 10.2 %collective-permute-start.14 = (bf16[4,256,128]{2,1,0:T(8,128)(2,1)S(1)}, bf16[4,256,128]{2,1,0:T(8,128)(2,1)S(1)}, u32[]{:S(2)}, u32[]{:S(2)}) collective-permute-start(bf16[4,256,128]{2,1,0:T(8,128)(2,1)S(1)} %bitcast.19), channel_id=1, source_target_pairs={{0,8},{4,12},{8,0},{12,4},{16,24},{20,28},{24,16},{28,20},{1,9},{5... | collective-permute-start | bytes 786440 | tf_op jit(solution)/shard_map/ppermute | solution.py:379
  75.7 24.9 %collective-permute-start.18 = (bf16[128,2048]{1,0:T(8,128)(2,1)S(1)}, bf16[128,2048]{1,0:T(8,128)(2,1)S(1)}, u32[]{:S(2)}, u32[]{:S(2)}) collective-permute-start(bf16[128,2048]{1,0:T(8,128)(2,1)S(1)} %get-tuple-element.56), channel_id=1, source_target_pairs={{0,1},{1,0},{2,3},{3,2},{4,5},{5,4},{6,7},{7,6},{8,9},{9,8},{10,11... | collective-permute-start | bytes 1572872 | tf_op jit(solution)/shard_map/ppermute | solution.py:379
  76.2 15.9 %collective-permute-start.23 = (bf16[1024,128]{1,0:T(8,128)(2,1)S(1)}, bf16[1024,128]{1,0:T(8,128)(2,1)S(1)}, u32[]{:S(2)}, u32[]{:S(2)}) collective-permute-start(bf16[1024,128]{1,0:T(8,128)(2,1)S(1)} %get-tuple-element.72), channel_id=1, source_target_pairs={{0,4},{4,0},{8,12},{12,8},{16,20},{20,16},{24,28},{28,24},{1,5},{5... | collective-permute-start | bytes 786440 | tf_op jit(solution)/shard_map/ppermute | solution.py:379
  89.9 9.3 %collective-permute-start.30 = (bf16[4,256,128]{2,1,0:T(8,128)(2,1)S(1)}, bf16[4,256,128]{2,1,0:T(8,128)(2,1)S(1)}, u32[]{:S(2)}, u32[]{:S(2)}) collective-permute-start(bf16[4,256,128]{2,1,0:T(8,128)(2,1)S(1)} %get-tuple-element.67), channel_id=1, source_target_pairs={{0,4},{4,0},{8,12},{12,8},{16,20},{20,16},{24,28},{28,24},{1,5},{5... | collective-permute-start | bytes 786440 | tf_op jit(solution)/shard_map/ppermute | solution.py:379
  90.0 14.8 %collective-permute-start.21 = (bf16[128,1024]{1,0:T(8,128)(2,1)S(1)}, bf16[128,1024]{1,0:T(8,128)(2,1)S(1)}, u32[]{:S(2)}, u32[]{:S(2)}) collective-permute-start(bf16[128,1024]{1,0:T(8,128)(2,1)S(1)} %collective-permute-done.15.refs_4_.refs_5_), channel_id=1, source_target_pairs={{0,8},{8,16},{16,24},{24,28},{28,20},{20,12},{12,4},{4,0},{1,9},{9... | collective-permute-start | bytes 786440 | tf_op jit(solution)/shard_map/ppermute | solution.py:370
  91.1 19.1 %collective-permute-start.22 = (bf16[128,1024]{1,0:T(8,128)(2,1)S(1)}, bf16[128,1024]{1,0:T(8,128)(2,1)S(1)}, u32[]{:S(2)}, u32[]{:S(2)}) collective-permute-start(bf16[128,1024]{1,0:T(8,128)(2,1)S(1)} %collective-permute-done.16.refs_5_.refs_6_), channel_id=1, source_target_pairs={{8,0},{16,8},{24,16},{28,24},{20,28},{12,20},{4,12},{0,4},{9,1},{1... | collective-permute-start | bytes 786440 | tf_op jit(solution)/shard_map/ppermute | solution.py:370
  92.1 24.8 %collective-permute-start.26 = (bf16[128,1024]{1,0:T(8,128)(2,1)S(1)}, bf16[128,1024]{1,0:T(8,128)(2,1)S(1)}, u32[]{:S(2)}, u32[]{:S(2)}) collective-permute-start(bf16[128,1024]{1,0:T(8,128)(2,1)S(1)} %collective-permute-done.11.refs_4_.refs_7_), channel_id=1, source_target_pairs={{0,8},{8,16},{16,24},{24,28},{28,20},{20,12},{12,4},{4,0},{1,9},{9... | collective-permute-start | bytes 786440 | tf_op jit(solution)/shard_map/ppermute | solution.py:366
  99.2 19.5 %collective-permute-start.20 = (bf16[128,2048]{1,0:T(8,128)(2,1)S(1)}, bf16[128,2048]{1,0:T(8,128)(2,1)S(1)}, u32[]{:S(2)}, u32[]{:S(2)}) collective-permute-start(bf16[128,2048]{1,0:T(8,128)(2,1)S(1)} %get-tuple-element.58.refs_4_.refs_2_), channel_id=1, source_target_pairs={{4,0},{8,4},{12,8},{16,12},{20,16},{24,20},{28,24},{5,1},{9,5},{13... | collective-permute-start | bytes 1572872 | tf_op jit(solution)/shard_map/ppermute | solution.py:551
  100.6 14.2 %collective-permute-start.24 = (bf16[512,128]{1,0:T(8,128)(2,1)S(1)}, bf16[512,128]{1,0:T(8,128)(2,1)S(1)}, u32[]{:S(2)}, u32[]{:S(2)}) collective-permute-start(bf16[512,128]{1,0:T(8,128)(2,1)S(1)} %get-tuple-element.64), channel_id=1, source_target_pairs={{0,8},{4,12},{8,0},{12,4},{16,24},{20,28},{24,16},{28,20},{1,9},{5... | collective-permute-start | bytes 393224 | tf_op jit(solution)/shard_map/ppermute | solution.py:379
  104.9 23.1 %collective-permute-start.32 = (bf16[8,256,128]{2,1,0:T(8,128)(2,1)S(1)}, bf16[8,256,128]{2,1,0:T(8,128)(2,1)S(1)}, u32[]{:S(2)}, u32[]{:S(2)}) collective-permute-start(bf16[8,256,128]{2,1,0:T(8,128)(2,1)S(1)} %maximum_bitcast_fusion.refs_10_), channel_id=1, source_target_pairs={{0,2},{1,3},{2,0},{3,1},{4,6},{5,7},{6,4},{7,5},{8,10},{9,11},{10,... | collective-permute-start | bytes 1572872 | tf_op jit(solution)/shard_map/ppermute | solution.py:379
  110.1 21.7 %collective-permute-start.17 = (bf16[128,2048]{1,0:T(8,128)(2,1)S(1)}, bf16[128,2048]{1,0:T(8,128)(2,1)S(1)}, u32[]{:S(2)}, u32[]{:S(2)}) collective-permute-start(bf16[128,2048]{1,0:T(8,128)(2,1)S(1)} %mixed_part.2.refs_7_.refs_3_), channel_id=1, source_target_pairs={{0,1},{1,0},{2,3},{3,2},{4,5},{5,4},{6,7},{7,6},{8,9},{9,8},{10,11... | collective-permute-start | bytes 1572872 | tf_op jit(solution)/shard_map/ppermute | solution.py:379
  114.8 17.0 %collective-permute-start.19 = (bf16[128,2048]{1,0:T(8,128)(2,1)S(1)}, bf16[128,2048]{1,0:T(8,128)(2,1)S(1)}, u32[]{:S(2)}, u32[]{:S(2)}) collective-permute-start(bf16[128,2048]{1,0:T(8,128)(2,1)S(1)} %add_convert_fusion.1), channel_id=1, source_target_pairs={{0,2},{1,3},{2,0},{3,1},{4,6},{5,7},{6,4},{7,5},{8,10},{9,11},{10,... | collective-permute-start | bytes 1572872 | tf_op jit(solution)/shard_map/ppermute | solution.py:379
  116.9 7.5 %collective-permute-start.25 = (bf16[512,128]{1,0:T(8,128)(2,1)S(1)}, bf16[512,128]{1,0:T(8,128)(2,1)S(1)}, u32[]{:S(2)}, u32[]{:S(2)}) collective-permute-start(bf16[512,128]{1,0:T(8,128)(2,1)S(1)} %added.4.refs_1_), channel_id=1, source_target_pairs={{0,16},{4,20},{8,24},{12,28},{16,0},{20,4},{24,8},{28,12},{1,17},{... | collective-permute-start | bytes 393224 | tf_op jit(solution)/shard_map/ppermute | solution.py:379
  118.7 9.2 %collective-permute-start.28 = (bf16[128,1024]{1,0:T(8,128)(2,1)S(1)}, bf16[128,1024]{1,0:T(8,128)(2,1)S(1)}, u32[]{:S(2)}, u32[]{:S(2)}) collective-permute-start(bf16[128,1024]{1,0:T(8,128)(2,1)S(1)} %collective-permute-done.22.refs_9_.refs_8_), channel_id=1, source_target_pairs={{8,0},{16,8},{24,16},{28,24},{20,28},{12,20},{4,12},{0,4},{9,1},{1... | collective-permute-start | bytes 786440 | tf_op jit(solution)/shard_map/ppermute | solution.py:366
  126.1 5.0 %collective-permute-start.27 = (bf16[512,128]{1,0:T(8,128)(2,1)S(1)}, bf16[512,128]{1,0:T(8,128)(2,1)S(1)}, u32[]{:S(2)}, u32[]{:S(2)}) collective-permute-start(bf16[512,128]{1,0:T(8,128)(2,1)S(1)} %added.5.refs_1_), channel_id=1, source_target_pairs={{0,8},{4,12},{8,0},{12,4},{16,24},{20,28},{24,16},{28,20},{1,9},{5... | collective-permute-start | bytes 393224 | tf_op jit(solution)/shard_map/ppermute | solution.py:379
  131.7 11.9 %collective-permute-start.29 = (bf16[1024,128]{1,0:T(8,128)(2,1)S(1)}, bf16[1024,128]{1,0:T(8,128)(2,1)S(1)}, u32[]{:S(2)}, u32[]{:S(2)}) collective-permute-start(bf16[1024,128]{1,0:T(8,128)(2,1)S(1)} %joined.2.refs_1_), channel_id=1, source_target_pairs={{0,4},{4,0},{8,12},{12,8},{16,20},{20,16},{24,28},{28,24},{1,5},{5... | collective-permute-start | bytes 786440 | tf_op jit(solution)/shard_map/ppermute | solution.py:379
  (22 other events, 193.5 us)

commit v9 on v7

--- a/solution.py
+++ b/solution.py
@@ -318,6 +318,10 @@
     return order
 
 
+def held_until(arrays, kernels):
+    return lax.optimization_barrier((*arrays, *kernels))[: len(arrays)]
+
+
 def swap(block, axis, bit):
     size = lax.axis_size(axis)
     return lax.ppermute(block, axis, [(i, i ^ bit) for i in range(size)])
@@ -433,10 +437,10 @@
     for bit in reversed(bits_of(n_chan)[1:]):
         cots.update({off ^ bit: swap(cots[off], "chan", bit) for off in list(cots) if off % 2 == 0})
     offs = sorted(off for off in cots if off % 2 == 0 and off)
+    sums = weight_pass(me, out_weight, 0, cot=cots[0])
     for off in offs:
-        cots[off + 1] = swap(cots[off], "chan", 1)
+        cots[off + 1] = swap(held_until([cots[off]], sums)[0], "chan", 1)
     offs = sorted(offs + [off + 1 for off in offs])
-    sums = weight_pass(me, out_weight, 0, cot=cots[0])
     sums = weight_pass(me, out_weight, 1, cot=cots[1], sums=sums)
 
     gated, filtered = by_channel(
@@ -468,7 +472,8 @@
     for off in offs[:-1]:
         *sums, terms[off] = weight_pass(me, out_weight, off, gated, cots[off], sums, after=[pieces])
     grad_query, grad_filtered, terms[offs[-1]] = weight_pass(
-        me, out_weight, offs[-1], gated, cots[offs[-1]], sums, [query_proj, filtered]
+        me, out_weight, offs[-1], gated, cots[offs[-1]], sums, [query_proj, filtered],
+        blocks[1:3] + stages[:1],
     )
     following = lax.ppermute(grad_filtered, "ctx", [(i + 1, i) for i in range(n_ctx - 1)])
 
@@ -480,7 +485,7 @@
         "tap_grad",
     )[0]
 
-    terms[1] = weight_pass(me, out_weight, 1, gated, after=blocks[1:3] + stages[:1] + [tap_grad])[0]
+    terms[1] = weight_pass(me, out_weight, 1, gated, after=[tap_grad])[0]
     terms[0] = weight_pass(me, out_weight, 0, gated, after=blocks[3:5] + stages[1:2] + [terms[1]])[0]
     gates = [[terms[1]], [terms[0]]]
     for bit in bits_of(n_chan):
@@ -495,9 +500,9 @@
         "ttttcww",
         [("t", BF16), ("t", BF16)],
         "backward_filter",
-        after=gates[-1] + blocks[5:7],
+        after=gates[-1],
     )
-    halves_summed = summed(me, tap_grad, gates + [[grad_key, far_low, far_high]])
+    halves_summed = summed(me, held_until([tap_grad], blocks[3:5])[0], [gates[-1], blocks[5:7], [far_low, far_high]])
 
     columns = gather_by_swaps(held)
     columns = [columns[off] for off in range(n_chan)]
@@ -509,7 +514,8 @@
         steps = [0] + [sign * step for step in range(1, n_ctx // 2) for sign in (-1, 1)] + [n_ctx // 2]
         owners.append([sources.index(order[(spot + step) % n_ctx] ^ c) for step in steps])
     grad_weight = grad_weight_of(me, jnp.asarray(owners, jnp.int32), blocks, far_low, far_high, columns)
-    grad_filters = joined(me, *halves_summed, F32, [grad_weight])
+    own, other, bit = halves_summed
+    grad_filters = joined(me, own, held_until([other], [grad_weight])[0], bit, F32, ())
     return (mixed, grad_query, grad_key, grad_value, grad_filters, grad_weight)
 
 

time: 147 us -> 146 us (level)
  starting transfers between devices: 27.9 us -> 37 us
  waiting for transfers between devices: 46.9 us -> 39.2 us
  local copies, waits for them, and re-layouts: 4.45 us -> 1.22 us
    ppermute x17, waiting for transfers between devices: 44.4 us -> 33.7 us  [swap(): return lax.ppermute(block, axis, [(i, i ^ bit) for i in range(size)])]
    ppermute x3, starting transfers between devices: 1.31 us -> 7.74 us  [per_device(): from_behind = lax.ppermute(from_behind, 'ctx', ahead)]
    ppermute x17, starting transfers between devices: 14.5 us -> 20.8 us  [swap(): return lax.ppermute(block, axis, [(i, i ^ bit) for i in range(size)])]
    ppermute x3, starting transfers between devices: 7.04 us -> 3.58 us  [per_device(): from_ahead = lax.ppermute(from_ahead, 'ctx', behind)]
    unnamed x24 -> x20, local copies, waits for them, and re-layouts: 4.32 us -> 1.09 us
    ppermute x1, waiting for transfers between devices: 2.4 us -> 4.05 us  [per_device(): far_low = lax.ppermute(from_behind[:, :half], 'ctx', ahead)]
  transfers between devices with their start and end apart: 27 -> 27, of which waited for: 7 -> 8; matrix products, arithmetic and copies ran while one was open for 1% -> 1% of each run, Pallas kernels for 42% -> 43%
where the time goes in v9:
time: 146 us; the launch traced here: 145 us
  Pallas kernels  64 us (44%)
  waiting for transfers between devices  39.2 us (27%)
  starting transfers between devices  37 us (25%)
  other arithmetic  2.69 us (2%)
    pallas_call x6, Pallas kernels, weight_pass(): pl.pallas_call(ignoring(body, len(after), 1 + len(arrays)), grid_spec=plt...  39.8 us
    ppermute x17, waiting for transfers between devices, swap(): return lax.ppermute(block, axis, [(i, i ^ bit) for i in range(size)])  33.7 us
    ppermute x17, starting transfers between devices, swap(): return lax.ppermute(block, axis, [(i, i ^ bit) for i in range(size)])  20.8 us
    pallas_call x3, Pallas kernels, by_channel(): pl.pallas_call(ignoring(functools.partial(kernel, length), len(after), le...  10.8 us
    pallas_call x1, Pallas kernels, grad_weight_of(): pl.pallas_call(functools.partial(weight_kernel, slots, parts, half), grid...  8.75 us
    ppermute x3, starting transfers between devices, per_device(): from_behind = lax.ppermute(from_behind, 'ctx', ahead)  7.74 us
    ppermute x1, waiting for transfers between devices, per_device(): far_low = lax.ppermute(from_behind[:, :half], 'ctx', ahead)  4.05 us
    ppermute x3, starting transfers between devices, per_device(): from_ahead = lax.ppermute(from_ahead, 'ctx', behind)  3.58 us
  transfers between devices with their start and end apart: 27, of which 8 were waited for; matrix products, arithmetic and copies ran while one was open for 1% of the time, Pallas kernels for 43%

profile of v9, /device:TPU:0, one launch (start us, length us, event | category | flops | bytes accessed | tf_op | source)
XLA Modules:
  0.0 145.1 jit_solution(2592172878516804617)
XLA Ops:
  0.6 1.3 multiply_convert_fusion
  2.0 3.0 %collective-permute-start.6 = (bf16[128,2048]{1,0:T(8,128)(2,1)}, bf16[128,2048]{1,0:T(8,128)(2,1)S(1)}, u32[]{:S(2)}, u32[]{:S(2)}) collective-permute-start(bf16[128,2048]{1,0:T(8,128)(2,1)} %refs_1_.12), channel_id=1, source_target_pairs={{0,2},{1,3},{2,0},{3,1},{4,6},{5,7},{6,4},{7,5},{8,10},{9,11},{10,... | collective-permute-start | bytes 1572872 | tf_op jit(solution)/shard_map/ppermute | solution.py:327
  5.0 3.4 %collective-permute-start = (bf16[128,2048]{1,0:T(8,128)(2,1)S(1)}, bf16[128,2048]{1,0:T(8,128)(2,1)S(1)}, u32[]{:S(2)}, u32[]{:S(2)}) collective-permute-start(bf16[128,2048]{1,0:T(8,128)(2,1)S(1)} %multiply_convert_fusion), channel_id=1, source_target_pairs={{0,4},{4,8},{8,12},{12,16},{16,20},{20,24},{24,28},{1,5},{5,9},{9,... | collective-permute-start | bytes 1572872 | tf_op jit(solution)/shard_map/ppermute | solution.py:434
  9.6 6.4 %grad_gated_part.2.refs_3_ = f32[2048,128]{1,0:T(8,128)S(1)} custom-call(s32[2]{0:T(128)S(1)} %pad_add_fusion.refs_0_.me_ref, bf16[2048,8192]{1,0:T(8,128)(2,1)} %refs_1_.17, bf16[128,2048]{1,0:T(8,128)(2,1)S(1)} %copy-done), custom_call_target="tpu_custom_call" | custom-call | flops 3000000000 | tf_op jit(solution)/shard_map/grad_gated_part/pallas_call | solution.py:190
  17.1 6.2 %grad_gated_part.3.refs_7_.refs_5_.refs_4_ = f32[2048,128]{1,0:T(8,128)S(1)} custom-call(s32[2]{0:T(128)S(1)} %pad_add_fusion.refs_0_.me_ref, bf16[2048,8192]{1,0:T(8,128)(2,1)} %refs_1_.17, bf16[128,2048]{1,0:T(8,128)(2,1)S(1)} %collective-permute-done.1.refs_2_, f32[2048,128]{1,0:T(8,128)S(1)} %grad_gated_part.2.refs_3_), custom_call_target="tpu_custom_call" | custom-call | flops 3000000000 | tf_op jit(solution)/shard_map/grad_gated_part/pallas_call | solution.py:190
  23.4 3.4 %forward_filter.1 = (bf16[128,2048]{1,0:T(8,128)(2,1)S(1)}, f32[128,2048]{1,0:T(8,128)S(1)}) custom-call(bf16[128,2048]{1,0:T(8,128)(2,1)S(1)} %copy-done.1, bf16[128,2048]{1,0:T(8,128)(2,1)S(1)} %copy-done.2, bf16[128,2048]{1,0:T(8,128)(2,1)S(1)} %copy-done.3, bf16[128,2048]{1,0:T(8,128)(2,1)S(1)} %collective-permute-done.refs_3_.refs_2_, ...), custom_call_target="tpu_custom_call" | custom-call | flops 3000000000 | tf_op jit(solution)/shard_map/forward_filter/pallas_call | solution.py:107
  26.8 1.8 %collective-permute-start.4 = (bf16[128,2048]{1,0:T(8,128)(2,1)S(1)}, bf16[128,2048]{1,0:T(8,128)(2,1)S(1)}, u32[]{:S(2)}, u32[]{:S(2)}) collective-permute-start(bf16[128,2048]{1,0:T(8,128)(2,1)S(1)} %get-tuple-element.24.refs_2_.refs_0_), channel_id=1, source_target_pairs={{8,0},{16,8},{24,16},{28,24},{20,28},{12,20},{4,12},{0,4},{9,1},{1... | collective-permute-start | bytes 1572872 | tf_op jit(solution)/shard_map/ppermute | solution.py:466
  29.6 2.9 %collective-permute-start.8 = (bf16[4,256,128]{2,1,0:T(8,128)(2,1)S(1)}, bf16[4,256,128]{2,1,0:T(8,128)(2,1)S(1)}, u32[]{:S(2)}, u32[]{:S(2)}) collective-permute-start(bf16[4,256,128]{2,1,0:T(8,128)(2,1)S(1)} %get-tuple-element.43), channel_id=1, source_target_pairs={{0,16},{4,20},{8,24},{12,28},{16,0},{20,4},{24,8},{28,12},{1,17},{... | collective-permute-start | bytes 786440 | tf_op jit(solution)/shard_map/ppermute | solution.py:327
  32.5 7.4 %grads_and_mixed.2 = (f32[2048,128]{1,0:T(8,128)S(1)}, f32[128,2048]{1,0:T(8,128)S(1)}) custom-call(s32[2]{0:T(128)S(1)} %pad_add_fusion.refs_0_.me_ref, bf16[2048,8192]{1,0:T(8,128)(2,1)} %refs_1_.17, bf16[128,2048]{1,0:T(8,128)(2,1)S(1)} %get-tuple-element.24.refs_2_.refs_0_, bf16[128,2048]{1,0:T(8,128)(2,1)S(1)} %collective-permute-done.6.refs_3_, ...), custom_call_target="tpu_custom_call" | custom-call | flops 6000000000 | tf_op jit(solution)/shard_map/grads_and_mixed/pallas_call | solution.py:190
  39.9 1.4 collective-permute-done.4.refs_8_.refs_2_
  41.3 1.7 %collective-permute-start.5 = (bf16[128,2048]{1,0:T(8,128)(2,1)S(1)}, bf16[128,2048]{1,0:T(8,128)(2,1)S(1)}, u32[]{:S(2)}, u32[]{:S(2)}) collective-permute-start(bf16[128,2048]{1,0:T(8,128)(2,1)S(1)} %collective-permute-done.4.refs_8_.refs_2_), channel_id=1, source_target_pairs={{8,0},{16,8},{24,16},{28,24},{20,28},{12,20},{4,12},{0,4},{9,1},{1... | collective-permute-start | bytes 1572872 | tf_op jit(solution)/shard_map/ppermute | solution.py:466
  43.0 5.4 %collective-permute-start.3 = (bf16[128,2048]{1,0:T(8,128)(2,1)S(1)}, bf16[128,2048]{1,0:T(8,128)(2,1)S(1)}, u32[]{:S(2)}, u32[]{:S(2)}) collective-permute-start(bf16[128,2048]{1,0:T(8,128)(2,1)S(1)} %collective-permute-done.2.refs_7_.refs_1_), channel_id=1, source_target_pairs={{0,8},{8,16},{16,24},{24,28},{28,20},{20,12},{12,4},{4,0},{1,9},{9... | collective-permute-start | bytes 1572872 | tf_op jit(solution)/shard_map/ppermute | solution.py:465
  48.4 5.7 %collective-permute-done.8.refs_9_ = bf16[4,256,128]{2,1,0:T(8,128)(2,1)S(1)} collective-permute-done((bf16[4,256,128]{2,1,0:T(8,128)(2,1)S(1)}, bf16[4,256,128]{2,1,0:T(8,128)(2,1)S(1)}, u32[]{:S(2)}, u32[]{:S(2)}) %collective-permute-start.8) | collective-permute-done | bytes 262176 | tf_op jit(solution)/shard_map/ppermute | solution.py:327
  54.4 8.3 %grads_and_mixed.3 = (bf16[128,2048]{1,0:T(8,128)(2,1)}, bf16[128,2048]{1,0:T(8,128)(2,1)S(1)}, bf16[128,2048]{1,0:T(8,128)(2,1)S(1)}) custom-call(s32[2]{0:T(128)S(1)} %pad_add_fusion.refs_0_.me_ref, bf16[2048,8192]{1,0:T(8,128)(2,1)} %refs_1_.17, bf16[128,2048]{1,0:T(8,128)(2,1)S(1)} %get-tuple-element.24.refs_2_.refs_0_, ...), custom_call_target="tpu_custom_call" | custom-call | flops 6000000000 | tf_op jit(solution)/shard_map/grads_and_mixed/pallas_call | solution.py:190
  64.0 3.5 %tap_grad.1.refs_3_ = bf16[2048,128]{1,0:T(8,128)(2,1)S(1)} custom-call(bf16[128,2048]{1,0:T(8,128)(2,1)S(1)} %copy-done.2, bf16[128,2048]{1,0:T(8,128)(2,1)S(1)} %copy-done.3, bf16[128,2048]{1,0:T(8,128)(2,1)S(1)} %collective-permute-done.refs_3_.refs_2_, bf16[128,2048]{1,0:T(8,128)(2,1)S(1)} %get-tuple-element.28.refs_3_.refs_2_, ...), custom_call_target="tpu_custom_call" | custom-call | flops 3000000000 | tf_op jit(solution)/shard_map/tap_grad/pallas_call | solution.py:107
  67.5 5.7 %mixed_part.2.refs_6_ = bf16[128,2048]{1,0:T(8,128)(2,1)S(1)} custom-call(s32[2]{0:T(128)S(1)} %pad_add_fusion.refs_0_.me_ref, bf16[2048,8192]{1,0:T(8,128)(2,1)} %refs_1_.17, bf16[128,2048]{1,0:T(8,128)(2,1)S(1)} %get-tuple-element.24.refs_2_.refs_0_, bf16[2048,128]{1,0:T(8,128)(2,1)S(1)} %tap_grad.1.refs_3_), custom_call_target="tpu_custom_call" | custom-call | flops 3000000000 | tf_op jit(solution)/shard_map/mixed_part/pallas_call | solution.py:190
  73.4 3.7 %collective-permute-start.14 = (bf16[1024,128]{1,0:T(8,128)(2,1)S(1)}, bf16[1024,128]{1,0:T(8,128)(2,1)S(1)}, u32[]{:S(2)}, u32[]{:S(2)}) collective-permute-start(bf16[1024,128]{1,0:T(8,128)(2,1)S(1)} %get-tuple-element.40), channel_id=1, source_target_pairs={{0,4},{4,0},{8,12},{12,8},{16,20},{20,16},{24,28},{28,24},{1,5},{5... | collective-permute-start | bytes 786440 | tf_op jit(solution)/shard_map/ppermute | solution.py:327
  77.3 3.5 %collective-permute-start.23 = (bf16[4,256,128]{2,1,0:T(8,128)(2,1)S(1)}, bf16[4,256,128]{2,1,0:T(8,128)(2,1)S(1)}, u32[]{:S(2)}, u32[]{:S(2)}) collective-permute-start(bf16[4,256,128]{2,1,0:T(8,128)(2,1)S(1)} %get-tuple-element.39), channel_id=1, source_target_pairs={{0,4},{4,0},{8,12},{12,8},{16,20},{20,16},{24,28},{28,24},{1,5},{5... | collective-permute-start | bytes 786440 | tf_op jit(solution)/shard_map/ppermute | solution.py:327
  80.8 5.7 %mixed_part.3.refs_7_.refs_3_ = f32[128,2048]{1,0:T(8,128)S(1)} custom-call(s32[2]{0:T(128)S(1)} %pad_add_fusion.refs_0_.me_ref, bf16[2048,8192]{1,0:T(8,128)(2,1)} %refs_1_.17, bf16[128,2048]{1,0:T(8,128)(2,1)S(1)} %get-tuple-element.24.refs_2_.refs_0_, bf16[128,2048]{1,0:T(8,128)(2,1)S(1)} %collective-permute-done.3.refs_3_, ...), custom_call_target="tpu_custom_call" | custom-call | flops 3000000000 | tf_op jit(solution)/shard_map/mixed_part/pallas_call | solution.py:190
  86.5 2.0 %collective-permute-start.16 = (bf16[128,2048]{1,0:T(8,128)(2,1)S(1)}, bf16[128,2048]{1,0:T(8,128)(2,1)S(1)}, u32[]{:S(2)}, u32[]{:S(2)}) collective-permute-start(bf16[128,2048]{1,0:T(8,128)(2,1)S(1)} %collective-permute-done.3.refs_3_), channel_id=1, source_target_pairs={{0,8},{8,16},{16,24},{24,28},{28,20},{20,12},{12,4},{4,0},{1,9},{9... | collective-permute-start | bytes 1572872 | tf_op jit(solution)/shard_map/ppermute | solution.py:465
  89.2 11.9 %collective-permute-done.23 = bf16[4,256,128]{2,1,0:T(8,128)(2,1)S(1)} collective-permute-done((bf16[4,256,128]{2,1,0:T(8,128)(2,1)S(1)}, bf16[4,256,128]{2,1,0:T(8,128)(2,1)S(1)}, u32[]{:S(2)}, u32[]{:S(2)}) %collective-permute-start.23) | collective-permute-done | bytes 262176 | tf_op jit(solution)/shard_map/ppermute | solution.py:327
  101.1 1.5 %collective-permute-start.25 = (bf16[8,256,128]{2,1,0:T(8,128)(2,1)S(1)}, bf16[8,256,128]{2,1,0:T(8,128)(2,1)S(1)}, u32[]{:S(2)}, u32[]{:S(2)}) collective-permute-start(bf16[8,256,128]{2,1,0:T(8,128)(2,1)S(1)} %maximum_bitcast_fusion.refs_9_), channel_id=1, source_target_pairs={{0,2},{1,3},{2,0},{3,1},{4,6},{5,7},{6,4},{7,5},{8,10},{9,11},{10,... | collective-permute-start | bytes 1572872 | tf_op jit(solution)/shard_map/ppermute | solution.py:327
  102.8 3.7 %collective-permute-done.15.refs_2_ = bf16[512,128]{1,0:T(8,128)(2,1)S(1)} collective-permute-done((bf16[512,128]{1,0:T(8,128)(2,1)S(1)}, bf16[512,128]{1,0:T(8,128)(2,1)S(1)}, u32[]{:S(2)}, u32[]{:S(2)}) %collective-permute-start.15) | collective-permute-done | bytes 131104 | tf_op jit(solution)/shard_map/ppermute | solution.py:327
  106.5 1.5 %collective-permute-start.12 = (bf16[128,2048]{1,0:T(8,128)(2,1)S(1)}, bf16[128,2048]{1,0:T(8,128)(2,1)S(1)}, u32[]{:S(2)}, u32[]{:S(2)}) collective-permute-start(bf16[128,2048]{1,0:T(8,128)(2,1)S(1)} %add_convert_fusion.1), channel_id=1, source_target_pairs={{0,2},{1,3},{2,0},{3,1},{4,6},{5,7},{6,4},{7,5},{8,10},{9,11},{10,... | collective-permute-start | bytes 1572872 | tf_op jit(solution)/shard_map/ppermute | solution.py:327
  108.6 2.5 %collective-permute-start.18 = (bf16[512,128]{1,0:T(8,128)(2,1)S(1)}, bf16[512,128]{1,0:T(8,128)(2,1)S(1)}, u32[]{:S(2)}, u32[]{:S(2)}) collective-permute-start(bf16[512,128]{1,0:T(8,128)(2,1)S(1)} %added.4.refs_1_), channel_id=1, source_target_pairs={{0,16},{4,20},{8,24},{12,28},{16,0},{20,4},{24,8},{28,12},{1,17},{... | collective-permute-start | bytes 393224 | tf_op jit(solution)/shard_map/ppermute | solution.py:327
  111.2 7.4 %collective-permute-done.18.refs_2_ = bf16[512,128]{1,0:T(8,128)(2,1)S(1)} collective-permute-done((bf16[512,128]{1,0:T(8,128)(2,1)S(1)}, bf16[512,128]{1,0:T(8,128)(2,1)S(1)}, u32[]{:S(2)}, u32[]{:S(2)}) %collective-permute-start.18) | collective-permute-done | bytes 131104 | tf_op jit(solution)/shard_map/ppermute | solution.py:327
  118.7 3.9 %backward_filter.1 = (bf16[128,2048]{1,0:T(8,128)(2,1)}, bf16[128,2048]{1,0:T(8,128)(2,1)}) custom-call(bf16[128,2048]{1,0:T(8,128)(2,1)S(1)} %copy-done.2, bf16[128,2048]{1,0:T(8,128)(2,1)S(1)} %copy-done.3, bf16[128,2048]{1,0:T(8,128)(2,1)S(1)} %get-tuple-element.28.refs_3_.refs_2_, bf16[128,2048]{1,0:T(8,128)(2,1)S(1)} %collective-permute-done.13.refs_3_, ...), custom_call_target="tpu_custom_call" | custom-call | flops 3000000000 | tf_op jit(solution)/shard_map/backward_filter/pallas_call | solution.py:107
  122.6 4.0 %collective-permute-done.19.refs_3_.refs_7_ = bf16[128,1024]{1,0:T(8,128)(2,1)S(1)} collective-permute-done((bf16[128,1024]{1,0:T(8,128)(2,1)S(1)}, bf16[128,1024]{1,0:T(8,128)(2,1)S(1)}, u32[]{:S(2)}, u32[]{:S(2)}) %collective-permute-start.19) | collective-permute-done | bytes 262176 | tf_op jit(solution)/shard_map/ppermute | solution.py:468
  128.5 3.8 %collective-permute-done.21.refs_2_ = bf16[512,128]{1,0:T(8,128)(2,1)S(1)} collective-permute-done((bf16[512,128]{1,0:T(8,128)(2,1)S(1)}, bf16[512,128]{1,0:T(8,128)(2,1)S(1)}, u32[]{:S(2)}, u32[]{:S(2)}) %collective-permute-start.21) | collective-permute-done | bytes 131104 | tf_op jit(solution)/shard_map/ppermute | solution.py:327
  132.9 1.8 %collective-permute-start.22 = (bf16[1024,128]{1,0:T(8,128)(2,1)S(1)}, bf16[1024,128]{1,0:T(8,128)(2,1)S(1)}, u32[]{:S(2)}, u32[]{:S(2)}) collective-permute-start(bf16[1024,128]{1,0:T(8,128)(2,1)S(1)} %joined.2.refs_1_), channel_id=1, source_target_pairs={{0,4},{4,0},{8,12},{12,8},{16,20},{20,16},{24,28},{28,24},{1,5},{5... | collective-permute-start | bytes 786440 | tf_op jit(solution)/shard_map/ppermute | solution.py:327
  134.7 8.7 %grad_weight.1 = bf16[2048,1024]{1,0:T(8,128)(2,1)} custom-call(s32[2]{0:T(128)S(1)} %pad_add_fusion.refs_0_.me_ref, s32[8,8]{1,0:T(8,128)S(1)} %copy-done.9, bf16[128,2048]{1,0:T(8,128)(2,1)S(1)} %get-tuple-element.24.refs_2_.refs_0_, bf16[128,2048]{1,0:T(8,128)(2,1)S(1)} %collective-permute-done.2.refs_7_.refs_1_, ...), custom_call_target="tpu_custom_call" | custom-call | flops 6000000000 | tf_op jit(solution)/shard_map/grad_weight/pallas_call | solution.py:288
  143.5 1.6 %joined.3 = f32[2048,128]{1,0:T(8,128)} custom-call(s32[2]{0:T(128)S(1)} %pad_add_fusion.refs_0_.me_ref, bf16[1024,128]{1,0:T(8,128)(2,1)S(1)} %joined.2.refs_1_, bf16[1024,128]{1,0:T(8,128)(2,1)S(1)} %collective-permute-done.22.refs_2_), custom_call_target="tpu_custom_call" | custom-call | flops 500000000 | tf_op jit(solution)/shard_map/joined/pallas_call | solution.py:399
  (71 shorter events, 8.9 us)
Async XLA Ops:
  2.0 15.1 %collective-permute-start.6 = (bf16[128,2048]{1,0:T(8,128)(2,1)}, bf16[128,2048]{1,0:T(8,128)(2,1)S(1)}, u32[]{:S(2)}, u32[]{:S(2)}) collective-permute-start(bf16[128,2048]{1,0:T(8,128)(2,1)} %refs_1_.12), channel_id=1, source_target_pairs={{0,2},{1,3},{2,0},{3,1},{4,6},{5,7},{6,4},{7,5},{8,10},{9,11},{10,... | collective-permute-start | bytes 1572872 | tf_op jit(solution)/shard_map/ppermute | solution.py:327
  5.0 12.1 %collective-permute-start.1 = (bf16[128,2048]{1,0:T(8,128)(2,1)}, bf16[128,2048]{1,0:T(8,128)(2,1)S(1)}, u32[]{:S(2)}, u32[]{:S(2)}) collective-permute-start(bf16[128,2048]{1,0:T(8,128)(2,1)} %refs_1_.12), channel_id=1, source_target_pairs={{0,1},{1,0},{2,3},{3,2},{4,5},{5,4},{6,7},{7,6},{8,9},{9,8},{10,11... | collective-permute-start | bytes 1572872 | tf_op jit(solution)/shard_map/ppermute | solution.py:327
  5.0 18.4 %collective-permute-start = (bf16[128,2048]{1,0:T(8,128)(2,1)S(1)}, bf16[128,2048]{1,0:T(8,128)(2,1)S(1)}, u32[]{:S(2)}, u32[]{:S(2)}) collective-permute-start(bf16[128,2048]{1,0:T(8,128)(2,1)S(1)} %multiply_convert_fusion), channel_id=1, source_target_pairs={{0,4},{4,8},{8,12},{12,16},{16,20},{20,24},{24,28},{1,5},{5,9},{9,... | collective-permute-start | bytes 1572872 | tf_op jit(solution)/shard_map/ppermute | solution.py:434
  9.6 13.9 %copy-start.5 = (bf16[2,256,256]{2,1,0:T(8,128)(2,1)S(1)}, bf16[2,256,256]{2,1,0:T(8,128)(2,1)}, u32[]{:S(2)}) copy-start(bf16[2,256,256]{2,1,0:T(8,128)(2,1)} %constant.23.clone.refs_5_.refs_4_) | copy-start | bytes 786436
  9.6 13.9 %copy-start.8 = (bf16[2,128,256]{2,1,0:T(8,128)(2,1)S(1)}, bf16[2,128,256]{2,1,0:T(8,128)(2,1)}, u32[]{:S(2)}) copy-start(bf16[2,128,256]{2,1,0:T(8,128)(2,1)} %constant.24.clone.refs_6_) | copy-start | bytes 393220
  17.1 11.8 %collective-permute-start.7 = (bf16[128,2048]{1,0:T(8,128)(2,1)S(1)}, bf16[128,2048]{1,0:T(8,128)(2,1)S(1)}, u32[]{:S(2)}, u32[]{:S(2)}) collective-permute-start(bf16[128,2048]{1,0:T(8,128)(2,1)S(1)} %collective-permute-done.6.refs_3_), channel_id=1, source_target_pairs={{0,1},{1,0},{2,3},{3,2},{4,5},{5,4},{6,7},{7,6},{8,9},{9,8},{10,11... | collective-permute-start | bytes 1572872 | tf_op jit(solution)/shard_map/ppermute | solution.py:327
  26.8 14.5 %collective-permute-start.4 = (bf16[128,2048]{1,0:T(8,128)(2,1)S(1)}, bf16[128,2048]{1,0:T(8,128)(2,1)S(1)}, u32[]{:S(2)}, u32[]{:S(2)}) collective-permute-start(bf16[128,2048]{1,0:T(8,128)(2,1)S(1)} %get-tuple-element.24.refs_2_.refs_0_), channel_id=1, source_target_pairs={{8,0},{16,8},{24,16},{28,24},{20,28},{12,20},{4,12},{0,4},{9,1},{1... | collective-permute-start | bytes 1572872 | tf_op jit(solution)/shard_map/ppermute | solution.py:466
  28.6 14.3 %collective-permute-start.2 = (bf16[128,2048]{1,0:T(8,128)(2,1)S(1)}, bf16[128,2048]{1,0:T(8,128)(2,1)S(1)}, u32[]{:S(2)}, u32[]{:S(2)}) collective-permute-start(bf16[128,2048]{1,0:T(8,128)(2,1)S(1)} %get-tuple-element.24.refs_2_.refs_0_), channel_id=1, source_target_pairs={{0,8},{8,16},{16,24},{24,28},{28,20},{20,12},{12,4},{4,0},{1,9},{9... | collective-permute-start | bytes 1572872 | tf_op jit(solution)/shard_map/ppermute | solution.py:465
  29.6 34.4 %copy-start.7 = (bf16[2,128,256]{2,1,0:T(8,128)(2,1)S(1)}, bf16[2,128,256]{2,1,0:T(8,128)(2,1)}, u32[]{:S(2)}) copy-start(bf16[2,128,256]{2,1,0:T(8,128)(2,1)} %constant.26.clone.refs_5_) | copy-start | bytes 393220
  29.6 24.5 %collective-permute-start.8 = (bf16[4,256,128]{2,1,0:T(8,128)(2,1)S(1)}, bf16[4,256,128]{2,1,0:T(8,128)(2,1)S(1)}, u32[]{:S(2)}, u32[]{:S(2)}) collective-permute-start(bf16[4,256,128]{2,1,0:T(8,128)(2,1)S(1)} %get-tuple-element.43), channel_id=1, source_target_pairs={{0,16},{4,20},{8,24},{12,28},{16,0},{20,4},{24,8},{28,12},{1,17},{... | collective-permute-start | bytes 786440 | tf_op jit(solution)/shard_map/ppermute | solution.py:327
  41.3 32.1 %collective-permute-start.5 = (bf16[128,2048]{1,0:T(8,128)(2,1)S(1)}, bf16[128,2048]{1,0:T(8,128)(2,1)S(1)}, u32[]{:S(2)}, u32[]{:S(2)}) collective-permute-start(bf16[128,2048]{1,0:T(8,128)(2,1)S(1)} %collective-permute-done.4.refs_8_.refs_2_), channel_id=1, source_target_pairs={{8,0},{16,8},{24,16},{28,24},{20,28},{12,20},{4,12},{0,4},{9,1},{1... | collective-permute-start | bytes 1572872 | tf_op jit(solution)/shard_map/ppermute | solution.py:466
  43.0 30.4 %collective-permute-start.3 = (bf16[128,2048]{1,0:T(8,128)(2,1)S(1)}, bf16[128,2048]{1,0:T(8,128)(2,1)S(1)}, u32[]{:S(2)}, u32[]{:S(2)}) collective-permute-start(bf16[128,2048]{1,0:T(8,128)(2,1)S(1)} %collective-permute-done.2.refs_7_.refs_1_), channel_id=1, source_target_pairs={{0,8},{8,16},{16,24},{24,28},{28,20},{20,12},{12,4},{4,0},{1,9},{9... | collective-permute-start | bytes 1572872 | tf_op jit(solution)/shard_map/ppermute | solution.py:465
  54.2 23.0 %collective-permute-start.9 = (bf16[4,256,128]{2,1,0:T(8,128)(2,1)S(1)}, bf16[4,256,128]{2,1,0:T(8,128)(2,1)S(1)}, u32[]{:S(2)}, u32[]{:S(2)}) collective-permute-start(bf16[4,256,128]{2,1,0:T(8,128)(2,1)S(1)} %bitcast.19), channel_id=1, source_target_pairs={{0,8},{4,12},{8,0},{12,4},{16,24},{20,28},{24,16},{28,20},{1,9},{5... | collective-permute-start | bytes 786440 | tf_op jit(solution)/shard_map/ppermute | solution.py:327
  62.7 48.4 %collective-permute-start.13 = (bf16[128,2048]{1,0:T(8,128)(2,1)S(1)}, bf16[128,2048]{1,0:T(8,128)(2,1)S(1)}, u32[]{:S(2)}, u32[]{:S(2)}) collective-permute-start(bf16[128,2048]{1,0:T(8,128)(2,1)S(1)} %get-tuple-element.28.refs_3_.refs_2_), channel_id=1, source_target_pairs={{4,0},{8,4},{12,8},{16,12},{20,16},{24,20},{28,24},{5,1},{9,5},{13... | collective-permute-start | bytes 1572872 | tf_op jit(solution)/shard_map/ppermute | solution.py:478
  67.5 51.2 %copy-start.6 = (bf16[2,128,256]{2,1,0:T(8,128)(2,1)S(1)}, bf16[2,128,256]{2,1,0:T(8,128)(2,1)}, u32[]{:S(2)}) copy-start(bf16[2,128,256]{2,1,0:T(8,128)(2,1)} %constant.25.clone.refs_6_) | copy-start | bytes 393220
  73.3 61.4 %copy-start.9 = (s32[8,8]{1,0:T(8,128)S(1)}, s32[8,8]{1,0:T(8,128)}, u32[]{:S(2)}) copy-start(s32[8,8]{1,0:T(8,128)} %constant.27.clone.owner_ref) | copy-start | bytes 772
  73.3 27.8 %collective-permute-start.11 = (bf16[128,2048]{1,0:T(8,128)(2,1)S(1)}, bf16[128,2048]{1,0:T(8,128)(2,1)S(1)}, u32[]{:S(2)}, u32[]{:S(2)}) collective-permute-start(bf16[128,2048]{1,0:T(8,128)(2,1)S(1)} %get-tuple-element.30), channel_id=1, source_target_pairs={{0,1},{1,0},{2,3},{3,2},{4,5},{5,4},{6,7},{7,6},{8,9},{9,8},{10,11... | collective-permute-start | bytes 1572872 | tf_op jit(solution)/shard_map/ppermute | solution.py:327
  73.4 13.1 %collective-permute-start.14 = (bf16[1024,128]{1,0:T(8,128)(2,1)S(1)}, bf16[1024,128]{1,0:T(8,128)(2,1)S(1)}, u32[]{:S(2)}, u32[]{:S(2)}) collective-permute-start(bf16[1024,128]{1,0:T(8,128)(2,1)S(1)} %get-tuple-element.40), channel_id=1, source_target_pairs={{0,4},{4,0},{8,12},{12,8},{16,20},{20,16},{24,28},{28,24},{1,5},{5... | collective-permute-start | bytes 786440 | tf_op jit(solution)/shard_map/ppermute | solution.py:327
  77.1 29.4 %collective-permute-start.17 = (bf16[128,2048]{1,0:T(8,128)(2,1)S(1)}, bf16[128,2048]{1,0:T(8,128)(2,1)S(1)}, u32[]{:S(2)}, u32[]{:S(2)}) collective-permute-start(bf16[128,2048]{1,0:T(8,128)(2,1)S(1)} %collective-permute-done.5.refs_4_), channel_id=1, source_target_pairs={{8,0},{16,8},{24,16},{28,24},{20,28},{12,20},{4,12},{0,4},{9,1},{1... | collective-permute-start | bytes 1572872 | tf_op jit(solution)/shard_map/ppermute | solution.py:466
  77.3 23.8 %collective-permute-start.23 = (bf16[4,256,128]{2,1,0:T(8,128)(2,1)S(1)}, bf16[4,256,128]{2,1,0:T(8,128)(2,1)S(1)}, u32[]{:S(2)}, u32[]{:S(2)}) collective-permute-start(bf16[4,256,128]{2,1,0:T(8,128)(2,1)S(1)} %get-tuple-element.39), channel_id=1, source_target_pairs={{0,4},{4,0},{8,12},{12,8},{16,20},{20,16},{24,28},{28,24},{1,5},{5... | collective-permute-start | bytes 786440 | tf_op jit(solution)/shard_map/ppermute | solution.py:327
  86.5 21.5 %collective-permute-start.16 = (bf16[128,2048]{1,0:T(8,128)(2,1)S(1)}, bf16[128,2048]{1,0:T(8,128)(2,1)S(1)}, u32[]{:S(2)}, u32[]{:S(2)}) collective-permute-start(bf16[128,2048]{1,0:T(8,128)(2,1)S(1)} %collective-permute-done.3.refs_3_), channel_id=1, source_target_pairs={{0,8},{8,16},{16,24},{24,28},{28,20},{20,12},{12,4},{4,0},{1,9},{9... | collective-permute-start | bytes 1572872 | tf_op jit(solution)/shard_map/ppermute | solution.py:465
  101.1 5.5 %collective-permute-start.15 = (bf16[512,128]{1,0:T(8,128)(2,1)S(1)}, bf16[512,128]{1,0:T(8,128)(2,1)S(1)}, u32[]{:S(2)}, u32[]{:S(2)}) collective-permute-start(bf16[512,128]{1,0:T(8,128)(2,1)S(1)} %get-tuple-element.36), channel_id=1, source_target_pairs={{0,8},{4,12},{8,0},{12,4},{16,24},{20,28},{24,16},{28,20},{1,9},{5... | collective-permute-start | bytes 393224 | tf_op jit(solution)/shard_map/ppermute | solution.py:327
  101.1 26.3 %collective-permute-start.25 = (bf16[8,256,128]{2,1,0:T(8,128)(2,1)S(1)}, bf16[8,256,128]{2,1,0:T(8,128)(2,1)S(1)}, u32[]{:S(2)}, u32[]{:S(2)}) collective-permute-start(bf16[8,256,128]{2,1,0:T(8,128)(2,1)S(1)} %maximum_bitcast_fusion.refs_9_), channel_id=1, source_target_pairs={{0,2},{1,3},{2,0},{3,1},{4,6},{5,7},{6,4},{7,5},{8,10},{9,11},{10,... | collective-permute-start | bytes 1572872 | tf_op jit(solution)/shard_map/ppermute | solution.py:327
  106.5 20.9 %collective-permute-start.10 = (bf16[128,2048]{1,0:T(8,128)(2,1)S(1)}, bf16[128,2048]{1,0:T(8,128)(2,1)S(1)}, u32[]{:S(2)}, u32[]{:S(2)}) collective-permute-start(bf16[128,2048]{1,0:T(8,128)(2,1)S(1)} %mixed_part.2.refs_6_), channel_id=1, source_target_pairs={{0,1},{1,0},{2,3},{3,2},{4,5},{5,4},{6,7},{7,6},{8,9},{9,8},{10,11... | collective-permute-start | bytes 1572872 | tf_op jit(solution)/shard_map/ppermute | solution.py:327
  106.5 20.9 %collective-permute-start.12 = (bf16[128,2048]{1,0:T(8,128)(2,1)S(1)}, bf16[128,2048]{1,0:T(8,128)(2,1)S(1)}, u32[]{:S(2)}, u32[]{:S(2)}) collective-permute-start(bf16[128,2048]{1,0:T(8,128)(2,1)S(1)} %add_convert_fusion.1), channel_id=1, source_target_pairs={{0,2},{1,3},{2,0},{3,1},{4,6},{5,7},{6,4},{7,5},{8,10},{9,11},{10,... | collective-permute-start | bytes 1572872 | tf_op jit(solution)/shard_map/ppermute | solution.py:327
  108.6 10.1 %collective-permute-start.18 = (bf16[512,128]{1,0:T(8,128)(2,1)S(1)}, bf16[512,128]{1,0:T(8,128)(2,1)S(1)}, u32[]{:S(2)}, u32[]{:S(2)}) collective-permute-start(bf16[512,128]{1,0:T(8,128)(2,1)S(1)} %added.4.refs_1_), channel_id=1, source_target_pairs={{0,16},{4,20},{8,24},{12,28},{16,0},{20,4},{24,8},{28,12},{1,17},{... | collective-permute-start | bytes 393224 | tf_op jit(solution)/shard_map/ppermute | solution.py:327
  111.1 11.5 %collective-permute-start.20 = (bf16[128,1024]{1,0:T(8,128)(2,1)S(1)}, bf16[128,1024]{1,0:T(8,128)(2,1)S(1)}, u32[]{:S(2)}, u32[]{:S(2)}) collective-permute-start(bf16[128,1024]{1,0:T(8,128)(2,1)S(1)} %slice.45), channel_id=1, source_target_pairs={{8,0},{16,8},{24,16},{28,24},{20,28},{12,20},{4,12},{0,4},{9,1},{1... | collective-permute-start | bytes 786440 | tf_op jit(solution)/shard_map/ppermute | solution.py:469
  118.7 8.0 %collective-permute-start.19 = (bf16[128,1024]{1,0:T(8,128)(2,1)S(1)}, bf16[128,1024]{1,0:T(8,128)(2,1)S(1)}, u32[]{:S(2)}, u32[]{:S(2)}) collective-permute-start(bf16[128,1024]{1,0:T(8,128)(2,1)S(1)} %slice.44), channel_id=1, source_target_pairs={{0,8},{8,16},{16,24},{24,28},{28,20},{20,12},{12,4},{4,0},{1,9},{9... | collective-permute-start | bytes 786440 | tf_op jit(solution)/shard_map/ppermute | solution.py:468
  122.6 12.1 %collective-permute-start.24 = (bf16[8,256,128]{2,1,0:T(8,128)(2,1)S(1)}, bf16[8,256,128]{2,1,0:T(8,128)(2,1)S(1)}, u32[]{:S(2)}, u32[]{:S(2)}) collective-permute-start(bf16[8,256,128]{2,1,0:T(8,128)(2,1)S(1)} %maximum_bitcast_fusion.refs_9_), channel_id=1, source_target_pairs={{0,1},{1,0},{2,3},{3,2},{4,5},{5,4},{6,7},{7,6},{8,9},{9,8},{10,11... | collective-permute-start | bytes 1572872 | tf_op jit(solution)/shard_map/ppermute | solution.py:327
  127.3 5.0 %collective-permute-start.21 = (bf16[512,128]{1,0:T(8,128)(2,1)S(1)}, bf16[512,128]{1,0:T(8,128)(2,1)S(1)}, u32[]{:S(2)}, u32[]{:S(2)}) collective-permute-start(bf16[512,128]{1,0:T(8,128)(2,1)S(1)} %added.5.refs_1_), channel_id=1, source_target_pairs={{0,8},{4,12},{8,0},{12,4},{16,24},{20,28},{24,16},{28,20},{1,9},{5... | collective-permute-start | bytes 393224 | tf_op jit(solution)/shard_map/ppermute | solution.py:327
  127.4 7.3 %collective-permute-start.26 = (bf16[8,256,128]{2,1,0:T(8,128)(2,1)S(1)}, bf16[8,256,128]{2,1,0:T(8,128)(2,1)S(1)}, u32[]{:S(2)}, u32[]{:S(2)}) collective-permute-start(bf16[8,256,128]{2,1,0:T(8,128)(2,1)S(1)} %collective-permute-done.25.refs_11_), channel_id=1, source_target_pairs={{0,1},{1,0},{2,3},{3,2},{4,5},{5,4},{6,7},{7,6},{8,9},{9,8},{10,11... | collective-permute-start | bytes 1572872 | tf_op jit(solution)/shard_map/ppermute | solution.py:327
  132.9 10.6 %collective-permute-start.22 = (bf16[1024,128]{1,0:T(8,128)(2,1)S(1)}, bf16[1024,128]{1,0:T(8,128)(2,1)S(1)}, u32[]{:S(2)}, u32[]{:S(2)}) collective-permute-start(bf16[1024,128]{1,0:T(8,128)(2,1)S(1)} %joined.2.refs_1_), channel_id=1, source_target_pairs={{0,4},{4,0},{8,12},{12,8},{16,20},{20,16},{24,28},{28,24},{1,5},{5... | collective-permute-start | bytes 786440 | tf_op jit(solution)/shard_map/ppermute | solution.py:327
  (5 other events, 56.4 us)

commit v10 on v9

--- a/solution.py
+++ b/solution.py
@@ -120,11 +120,12 @@
     )(*arrays, *after)
 
 
-def pass_kernel(with_mixed, with_grad, has_sum, last, me_ref, w_ref, *refs):
+def pass_kernel(with_mixed, with_grad, has_sum, last, adds, me_ref, w_ref, *refs):
     refs = list(refs)
     step = pl.program_id(0)
     if with_mixed:
         gated_ref = refs.pop(0)
+    add_refs = [refs.pop(0) for unused in range(adds)]
     if with_grad:
         cot_ref = refs.pop(0)
         sum_ref = refs.pop(0) if has_sum else None
@@ -158,10 +159,13 @@
 
         @pl.when(step == pl.num_programs(0) - 1)
         def give():
-            mixed_ref[...] = held_ref[...].astype(mixed_ref.dtype)
-
-
-def weight_pass(me, weight, off, gated=None, cot=None, sums=(), ends=(), after=()):
+            mixed = held_ref[...]
+            for add_ref in add_refs:
+                mixed = mixed + add_ref[...].astype(F32)
+            mixed_ref[...] = mixed.astype(mixed_ref.dtype)
+
+
+def weight_pass(me, weight, off, gated=None, cot=None, sums=(), ends=(), adds=(), after=()):
     length = (cot if gated is None else gated).shape[0]
     channels = weight.shape[0]
     tile = 512
@@ -173,6 +177,8 @@
     if gated is not None:
         arrays.append(gated)
         in_specs.append(by_token)
+        arrays += adds
+        in_specs += [whole] * len(adds)
     if cot is not None:
         arrays += [cot, *sums, *ends]
         in_specs += [whole] + [by_row] * len(sums) + [by_token] * len(ends)
@@ -182,11 +188,11 @@
         ]
     if gated is not None:
         out_specs.append(whole)
-        out_shape.append(jax.ShapeDtypeStruct((length, channels), BF16 if off % 2 else F32))
+        out_shape.append(jax.ShapeDtypeStruct((length, channels), BF16 if off % 2 or adds else F32))
         scratch.append(pltpu.VMEM((length, channels), F32))
     if cot is not None:
         scratch.append(pltpu.VMEM((channels, length), BF16))
-    body = functools.partial(pass_kernel, gated is not None, cot is not None, bool(sums), bool(ends))
+    body = functools.partial(pass_kernel, gated is not None, cot is not None, bool(sums), bool(ends), len(adds))
     return pl.pallas_call(
         ignoring(body, len(after), 1 + len(arrays)),
         grid_spec=pltpu.PrefetchScalarGridSpec(
@@ -375,14 +381,14 @@
     return jnp.where(mine, high, low), jnp.where(mine, low, high)
 
 
-def summed(me, partial, gates):
+def summed(me, partial, gates, join_gate):
     bits = bits_of(lax.axis_size("ctx"))
     sums, send = split(me, partial, bits[0])
     for step, bit in enumerate(bits):
         came = swap(send if step < 2 else sums, "ctx", bit)
         sums, *send = added(me, sums, came, bits[1] if step == 0 else 0, gates[step] if step < len(gates) else ())
         send = send[0] if send else None
-    sums = joined(me, sums, swap(sums, "ctx", bits[1]), bits[1], BF16, ())
+    sums = joined(me, sums, swap(sums, "ctx", bits[1]), bits[1], BF16, join_gate)
     return sums, swap(sums, "ctx", bits[0]), bits[0]
 
 
@@ -411,15 +417,23 @@
     )(me, own, other, *after)
 
 
-def exchanged(pieces):
-    held, sources, stages = pieces[None], [0], []
-    for bit in reversed(bits_of(pieces.shape[0])):
-        give = held[:, bit:].reshape((-1,) + pieces.shape[1:])
-        stages.append(swap(give, "ctx", bit))
-        came = stages[-1].reshape((len(sources), bit) + pieces.shape[1:])
-        held = jnp.concatenate([held[:, :bit], came], axis=0)
-        sources += [source ^ bit for source in sources]
-    return held[:, 0], sources, stages
+class Exchange:
+    def __init__(self, pieces):
+        self.shape = pieces.shape[1:]
+        self.held, self.sources = pieces[None], [0]
+        self.bits = bits_of(pieces.shape[0])
+
+    def step(self, kernels):
+        if not self.bits:
+            return []
+        bit = self.bits.pop()
+        give = self.held[:, bit:].reshape((-1,) + self.shape)
+        came = swap(held_until([give], kernels)[0], "ctx", bit)
+        self.held = jnp.concatenate(
+            [self.held[:, :bit], came.reshape((len(self.sources), bit) + self.shape)], axis=0
+        )
+        self.sources += [source ^ bit for source in self.sources]
+        return [came]
 
 
 def per_device(query_proj, key_proj, value_proj, filters, out_weight, cotangent):
@@ -441,7 +455,6 @@
     for off in offs:
         cots[off + 1] = swap(held_until([cots[off]], sums)[0], "chan", 1)
     offs = sorted(offs + [off + 1 for off in offs])
-    sums = weight_pass(me, out_weight, 1, cot=cots[1], sums=sums)
 
     gated, filtered = by_channel(
         forward_kernel,
@@ -452,8 +465,9 @@
         after=sums,
     )
 
-    pieces = pieces_of(me, [cots[off] for off in range(n_chan)], n_ctx, sums)
-    held, sources, stages = exchanged(pieces)
+    pieces = pieces_of(me, [cots[off] for off in range(n_chan)], n_ctx, [gated])
+    exchange = Exchange(pieces)
+    stages = exchange.step([pieces])
 
     order = cycle_of(n_ctx)
     ahead = [(order[i], order[(i + 1) % n_ctx]) for i in range(n_ctx)]
@@ -468,13 +482,16 @@
     far_low = lax.ppermute(from_behind[:, :half], "ctx", ahead)
     far_high = lax.ppermute(from_ahead[:, half:], "ctx", behind)
 
+    sums = weight_pass(me, out_weight, 1, cot=cots[1], sums=sums, after=[pieces])
     terms = {}
     for off in offs[:-1]:
-        *sums, terms[off] = weight_pass(me, out_weight, off, gated, cots[off], sums, after=[pieces])
+        *sums, terms[off] = weight_pass(me, out_weight, off, gated, cots[off], sums)
     grad_query, grad_filtered, terms[offs[-1]] = weight_pass(
         me, out_weight, offs[-1], gated, cots[offs[-1]], sums, [query_proj, filtered],
-        blocks[1:3] + stages[:1],
+        (),
+        blocks[1:3] + stages,
     )
+    stages = exchange.step(stages)
     following = lax.ppermute(grad_filtered, "ctx", [(i + 1, i) for i in range(n_ctx - 1)])
 
     tap_grad = by_channel(
@@ -485,14 +502,20 @@
         "tap_grad",
     )[0]
 
-    terms[1] = weight_pass(me, out_weight, 1, gated, after=[tap_grad])[0]
-    terms[0] = weight_pass(me, out_weight, 0, gated, after=blocks[3:5] + stages[1:2] + [terms[1]])[0]
-    gates = [[terms[1]], [terms[0]]]
-    for bit in bits_of(n_chan):
+    for off in [off for off in sorted(terms) if off % 2]:
+        came = swap(terms.pop(off), "chan", 1)
+        terms[off ^ 1] = terms[off ^ 1] + came.astype(F32)
+    terms[1] = weight_pass(me, out_weight, 1, gated, after=[tap_grad, came])[0]
+    while exchange.bits:
+        exchange.step([terms[1]])
+    final = [swap(terms.pop(1), "chan", 1)]
+    for bit in bits_of(n_chan)[1:]:
         for off in [off for off in sorted(terms, reverse=True) if off & bit]:
-            came = swap(terms.pop(off).astype(BF16), "chan", bit).astype(F32)
-            terms[off ^ bit] = terms[off ^ bit] + came
-    mixed = terms[0].astype(BF16)
+            came = swap(terms.pop(off).astype(BF16), "chan", bit)
+            if off == bit:
+                final.append(came)
+            else:
+                terms[off ^ bit] = terms[off ^ bit] + came.astype(F32)
 
     grad_key, grad_value = by_channel(
         backward_kernel,
@@ -500,11 +523,12 @@
         "ttttcww",
         [("t", BF16), ("t", BF16)],
         "backward_filter",
-        after=gates[-1],
+        after=blocks[3:5] + stages,
     )
-    halves_summed = summed(me, held_until([tap_grad], blocks[3:5])[0], [gates[-1], blocks[5:7], [far_low, far_high]])
-
-    columns = gather_by_swaps(held)
+    mixed = weight_pass(me, out_weight, 0, gated, adds=final, after=[grad_key] + blocks[5:7])[0]
+    halves_summed = summed(me, held_until([tap_grad], [grad_key])[0], [(), [mixed]], [far_low, far_high])
+
+    columns = gather_by_swaps(exchange.held[:, 0])
     columns = [columns[off] for off in range(n_chan)]
     if (channels // n_ctx) % 128:
         columns = in_one_piece(me, columns, length)
@@ -512,7 +536,7 @@
     for c in range(n_ctx):
         spot = order.index(c)
         steps = [0] + [sign * step for step in range(1, n_ctx // 2) for sign in (-1, 1)] + [n_ctx // 2]
-        owners.append([sources.index(order[(spot + step) % n_ctx] ^ c) for step in steps])
+        owners.append([exchange.sources.index(order[(spot + step) % n_ctx] ^ c) for step in steps])
     grad_weight = grad_weight_of(me, jnp.asarray(owners, jnp.int32), blocks, far_low, far_high, columns)
     own, other, bit = halves_summed
     grad_filters = joined(me, own, held_until([other], [grad_weight])[0], bit, F32, ())

time: 146 us -> 164 us (1.12)
  waiting for transfers between devices: 39.2 us -> 52.8 us
  local copies, waits for them, and re-layouts: 1.22 us -> 7.48 us
  starting transfers between devices: 37 us -> 32.7 us
  Pallas kernels: 64 us -> 66.6 us
    ppermute x17, waiting for transfers between devices: 33.7 us -> 46.3 us  [swap(): return lax.ppermute(block, axis, [(i, i ^ bit) for i in range(size)])]
    ppermute x17, starting transfers between devices: 20.8 us -> 14 us  [swap(): return lax.ppermute(block, axis, [(i, i ^ bit) for i in range(size)])]
    unnamed x20 -> x34, local copies, waits for them, and re-layouts: 1.09 us -> 7.35 us
    ppermute x1, waiting for transfers between devices: 4.05 us -> 0.01 us  [per_device(): far_low = lax.ppermute(from_behind[:, :half], 'ctx', ahead)]
    ppermute x1, waiting for transfers between devices: 0.01 us -> 3.44 us  [per_device(): lax.ppermute(product, 'ctx', [(i, i + 1) for i in range(n_ctx - 1)])]
    ppermute x3, starting transfers between devices: 7.74 us -> 4.36 us  [per_device(): from_behind = lax.ppermute(from_behind, 'ctx', ahead)]
    ppermute x1, waiting for transfers between devices: 0.01 us -> 2.82 us  [per_device(): far_high = lax.ppermute(from_ahead[:, half:], 'ctx', behind)]
    ppermute x3, starting transfers between devices: 3.58 us -> 6.03 us  [per_device(): from_ahead = lax.ppermute(from_ahead, 'ctx', behind)]
  transfers between devices with their start and end apart: 27 -> 27, of which waited for: 8 -> 11; matrix products, arithmetic and copies ran while one was open for 1% -> 0% of each run, Pallas kernels for 43% -> 40%
where the time goes in v10:
time: 164 us; the launch traced here: 163 us
  Pallas kernels  66.6 us (41%)
  waiting for transfers between devices  52.8 us (32%)
  starting transfers between devices  32.7 us (20%)
  local copies, waits for them, and re-layouts  7.48 us (5%)
  other arithmetic  2.57 us (2%)
    ppermute x17, waiting for transfers between devices, swap(): return lax.ppermute(block, axis, [(i, i ^ bit) for i in range(size)])  46.3 us
    pallas_call x6, Pallas kernels, weight_pass(): pl.pallas_call(ignoring(body, len(after), 1 + len(arrays)), grid_spec=plt...  40.6 us
    ppermute x17, starting transfers between devices, swap(): return lax.ppermute(block, axis, [(i, i ^ bit) for i in range(size)])  14 us
    pallas_call x3, Pallas kernels, by_channel(): pl.pallas_call(ignoring(functools.partial(kernel, length), len(after), le...  12.7 us
    pallas_call x1, Pallas kernels, grad_weight_of(): pl.pallas_call(functools.partial(weight_kernel, slots, parts, half), grid...  8.75 us
    unnamed x34, local copies, waits for them, and re-layouts  7.35 us
    ppermute x3, starting transfers between devices, per_device(): from_ahead = lax.ppermute(from_ahead, 'ctx', behind)  6.03 us
    ppermute x3, starting transfers between devices, per_device(): from_behind = lax.ppermute(from_behind, 'ctx', ahead)  4.36 us
  transfers between devices with their start and end apart: 27, of which 11 were waited for; matrix products, arithmetic and copies ran while one was open for 0% of the time, Pallas kernels for 40%

profile of v10, /device:TPU:0, one launch (start us, length us, event | category | flops | bytes accessed | tf_op | source)
XLA Modules:
  0.0 163.2 jit_solution(13479116077972306129)
XLA Ops:
  0.7 2.2 %multiply_convert_fusion = bf16[128,2048]{1,0:T(8,128)(2,1)} fusion(bf16[128,2048]{1,0:T(8,128)(2,1)} %refs_1_.17, bf16[128,2048]{1,0:T(8,128)(2,1)} %refs_0_.5), kind=kLoop, calls=%fused_computation.1 | loop fusion | flops 1048576 | bytes 1572864 | tf_op jit(solution)/shard_map/convert_element_type | solution.py:446
  2.9 2.9 %collective-permute-start.1 = (bf16[128,2048]{1,0:T(8,128)(2,1)}, bf16[128,2048]{1,0:T(8,128)(2,1)S(1)}, u32[]{:S(2)}, u32[]{:S(2)}) collective-permute-start(bf16[128,2048]{1,0:T(8,128)(2,1)} %refs_1_.11), channel_id=1, source_target_pairs={{0,2},{1,3},{2,0},{3,1},{4,6},{5,7},{6,4},{7,5},{8,10},{9,11},{10,... | collective-permute-start | bytes 1572872 | tf_op jit(solution)/shard_map/ppermute | solution.py:333
  5.8 4.2 %collective-permute-start = (bf16[128,2048]{1,0:T(8,128)(2,1)}, bf16[128,2048]{1,0:T(8,128)(2,1)}, u32[]{:S(2)}, u32[]{:S(2)}) collective-permute-start(bf16[128,2048]{1,0:T(8,128)(2,1)} %multiply_convert_fusion), channel_id=1, source_target_pairs={{0,4},{4,8},{8,12},{12,16},{16,20},{20,24},{24,28},{1,5},{5,9},{9,... | collective-permute-start | bytes 1572872 | tf_op jit(solution)/shard_map/ppermute | solution.py:448
  11.1 6.2 %grad_gated_part.2.refs_7_.refs_3_ = f32[2048,128]{1,0:T(8,128)S(1)} custom-call(s32[2]{0:T(128)S(1)} %pad_add_fusion.refs_0_.me_ref, bf16[2048,8192]{1,0:T(8,128)(2,1)} %refs_1_.18, bf16[128,2048]{1,0:T(8,128)(2,1)S(1)} %copy-done), custom_call_target="tpu_custom_call" | custom-call | flops 3000000000 | tf_op jit(solution)/shard_map/grad_gated_part/pallas_call | solution.py:196
  17.9 3.4 %collective-permute-done.refs_3_.refs_2_ = bf16[128,2048]{1,0:T(8,128)(2,1)} collective-permute-done((bf16[128,2048]{1,0:T(8,128)(2,1)}, bf16[128,2048]{1,0:T(8,128)(2,1)}, u32[]{:S(2)}, u32[]{:S(2)}) %collective-permute-start) | collective-permute-done | bytes 524320 | tf_op jit(solution)/shard_map/ppermute | solution.py:448
  25.6 4.3 %forward_filter.1 = (bf16[128,2048]{1,0:T(8,128)(2,1)S(1)}, f32[128,2048]{1,0:T(8,128)S(1)}) custom-call(bf16[128,2048]{1,0:T(8,128)(2,1)S(1)} %copy-done.2, bf16[128,2048]{1,0:T(8,128)(2,1)S(1)} %copy-done.6, bf16[128,2048]{1,0:T(8,128)(2,1)S(1)} %copy-done.8, bf16[128,2048]{1,0:T(8,128)(2,1)} %collective-permute-done.refs_3_.refs_2_, ...), custom_call_target="tpu_custom_call" | custom-call | flops 3000000000 | tf_op jit(solution)/shard_map/forward_filter/pallas_call | solution.py:107
  29.9 2.5 %collective-permute-start.5 = (bf16[128,2048]{1,0:T(8,128)(2,1)S(1)}, bf16[128,2048]{1,0:T(8,128)(2,1)S(1)}, u32[]{:S(2)}, u32[]{:S(2)}) collective-permute-start(bf16[128,2048]{1,0:T(8,128)(2,1)S(1)} %get-tuple-element.27.refs_5_.refs_2_.refs_0_), channel_id=1, source_target_pairs={{8,0},{16,8},{24,16},{28,24},{20,28},{12,20},{4,12},{0,4},{9,1},{1... | collective-permute-start | bytes 1572872 | tf_op jit(solution)/shard_map/ppermute | solution.py:480
  34.1 3.0 %collective-permute-start.6 = (bf16[4,256,128]{2,1,0:T(8,128)(2,1)S(1)}, bf16[4,256,128]{2,1,0:T(8,128)(2,1)S(1)}, u32[]{:S(2)}, u32[]{:S(2)}) collective-permute-start(bf16[4,256,128]{2,1,0:T(8,128)(2,1)S(1)} %get-tuple-element.31), channel_id=1, source_target_pairs={{0,16},{4,20},{8,24},{12,28},{16,0},{20,4},{24,8},{28,12},{1,17},{... | collective-permute-start | bytes 786440 | tf_op jit(solution)/shard_map/ppermute | solution.py:333
  37.2 6.2 %grad_gated_part.3.refs_4_ = f32[2048,128]{1,0:T(8,128)S(1)} custom-call(s32[2]{0:T(128)S(1)} %pad_add_fusion.refs_0_.me_ref, bf16[2048,8192]{1,0:T(8,128)(2,1)} %refs_1_.18, bf16[128,2048]{1,0:T(8,128)(2,1)S(1)} %collective-permute-done.3.refs_2_, f32[2048,128]{1,0:T(8,128)S(1)} %grad_gated_part.2.refs_7_.refs_3_, bf16[8,256,128]{2,1,0:T(8,128)(2,1)S(1)} %pieces.1.refs_4_), custom_call_target="tpu_custom_call" | custom-call | flops 3000000000 | tf_op jit(solution)/shard_map/grad_gated_part/pallas_call | solution.py:196
  43.5 7.4 %grads_and_mixed.2 = (f32[2048,128]{1,0:T(8,128)S(1)}, f32[128,2048]{1,0:T(8,128)S(1)}) custom-call(s32[2]{0:T(128)S(1)} %pad_add_fusion.refs_0_.me_ref, bf16[2048,8192]{1,0:T(8,128)(2,1)} %refs_1_.18, bf16[128,2048]{1,0:T(8,128)(2,1)S(1)} %get-tuple-element.27.refs_5_.refs_2_.refs_0_, bf16[128,2048]{1,0:T(8,128)(2,1)S(1)} %collective-permute-done.1.refs_3_, ...), custom_call_target="tpu_custom_call" | custom-call | flops 6000000000 | tf_op jit(solution)/shard_map/grads_and_mixed/pallas_call | solution.py:196
  51.6 1.8 %collective-permute-start.11 = (bf16[128,2048]{1,0:T(8,128)(2,1)S(1)}, bf16[128,2048]{1,0:T(8,128)(2,1)S(1)}, u32[]{:S(2)}, u32[]{:S(2)}) collective-permute-start(bf16[128,2048]{1,0:T(8,128)(2,1)S(1)} %collective-permute-done.4.refs_7_.refs_1_), channel_id=1, source_target_pairs={{0,8},{8,16},{16,24},{24,28},{28,20},{20,12},{12,4},{4,0},{1,9},{9... | collective-permute-start | bytes 1572872 | tf_op jit(solution)/shard_map/ppermute | solution.py:479
  53.4 5.5 %collective-permute-done.6.refs_9_ = bf16[4,256,128]{2,1,0:T(8,128)(2,1)S(1)} collective-permute-done((bf16[4,256,128]{2,1,0:T(8,128)(2,1)S(1)}, bf16[4,256,128]{2,1,0:T(8,128)(2,1)S(1)}, u32[]{:S(2)}, u32[]{:S(2)}) %collective-permute-start.6) | collective-permute-done | bytes 262176 | tf_op jit(solution)/shard_map/ppermute | solution.py:333
  59.2 8.3 %grads_and_mixed.3 = (bf16[128,2048]{1,0:T(8,128)(2,1)}, bf16[128,2048]{1,0:T(8,128)(2,1)S(1)}, bf16[128,2048]{1,0:T(8,128)(2,1)S(1)}) custom-call(s32[2]{0:T(128)S(1)} %pad_add_fusion.refs_0_.me_ref, bf16[2048,8192]{1,0:T(8,128)(2,1)} %refs_1_.18, bf16[128,2048]{1,0:T(8,128)(2,1)S(1)} %get-tuple-element.27.refs_5_.refs_2_.refs_0_, ...), custom_call_target="tpu_custom_call" | custom-call | flops 6000000000 | tf_op jit(solution)/shard_map/grads_and_mixed/pallas_call | solution.py:196
  67.5 1.4 collective-permute-start.10
  69.0 4.4 %tap_grad.1.refs_3_ = bf16[2048,128]{1,0:T(8,128)(2,1)S(1)} custom-call(bf16[128,2048]{1,0:T(8,128)(2,1)S(1)} %copy-done.7, bf16[128,2048]{1,0:T(8,128)(2,1)S(1)} %copy-done.9, bf16[128,2048]{1,0:T(8,128)(2,1)} %collective-permute-done.refs_3_.refs_2_, bf16[128,2048]{1,0:T(8,128)(2,1)S(1)} %get-tuple-element.32.refs_3_.refs_2_, ...), custom_call_target="tpu_custom_call" | custom-call | flops 3000000000 | tf_op jit(solution)/shard_map/tap_grad/pallas_call | solution.py:107
  73.4 2.8 %collective-permute-start.15 = (bf16[128,2048]{1,0:T(8,128)(2,1)S(1)}, bf16[128,2048]{1,0:T(8,128)(2,1)S(1)}, u32[]{:S(2)}, u32[]{:S(2)}) collective-permute-start(bf16[128,2048]{1,0:T(8,128)(2,1)S(1)} %collective-permute-done.12.refs_8_.refs_4_), channel_id=1, source_target_pairs={{8,0},{16,8},{24,16},{28,24},{20,28},{12,20},{4,12},{0,4},{9,1},{1... | collective-permute-start | bytes 1572872 | tf_op jit(solution)/shard_map/ppermute | solution.py:480
  76.2 1.5 collective-permute-start.14
  77.8 5.7 %mixed_part.2 = bf16[128,2048]{1,0:T(8,128)(2,1)S(1)} custom-call(s32[2]{0:T(128)S(1)} %pad_add_fusion.refs_0_.me_ref, bf16[2048,8192]{1,0:T(8,128)(2,1)} %refs_1_.18, bf16[128,2048]{1,0:T(8,128)(2,1)S(1)} %get-tuple-element.27.refs_5_.refs_2_.refs_0_, bf16[2048,128]{1,0:T(8,128)(2,1)S(1)} %tap_grad.1.refs_3_, ...), custom_call_target="tpu_custom_call" | custom-call | flops 3000000000 | tf_op jit(solution)/shard_map/mixed_part/pallas_call | solution.py:196
  84.4 4.0 %backward_filter.1 = (bf16[128,2048]{1,0:T(8,128)(2,1)}, bf16[128,2048]{1,0:T(8,128)(2,1)}) custom-call(bf16[128,2048]{1,0:T(8,128)(2,1)S(1)} %copy-done.7, bf16[128,2048]{1,0:T(8,128)(2,1)S(1)} %copy-done.9, bf16[128,2048]{1,0:T(8,128)(2,1)S(1)} %get-tuple-element.32.refs_3_.refs_2_, bf16[128,2048]{1,0:T(8,128)(2,1)S(1)} %collective-permute-done.10.refs_3_, ...), custom_call_target="tpu_custom_call" | custom-call | flops 3000000000 | tf_op jit(solution)/shard_map/backward_filter/pallas_call | solution.py:107
  88.4 3.0 %collective-permute-start.16 = (bf16[1024,128]{1,0:T(8,128)(2,1)S(1)}, bf16[1024,128]{1,0:T(8,128)(2,1)S(1)}, u32[]{:S(2)}, u32[]{:S(2)}) collective-permute-start(bf16[1024,128]{1,0:T(8,128)(2,1)S(1)} %get-tuple-element.46), channel_id=1, source_target_pairs={{0,4},{4,0},{8,12},{12,8},{16,20},{20,16},{24,28},{28,24},{1,5},{5... | collective-permute-start | bytes 786440 | tf_op jit(solution)/shard_map/ppermute | solution.py:333
  91.4 9.9 %collective-permute-done.23 = bf16[4,256,128]{2,1,0:T(8,128)(2,1)S(1)} collective-permute-done((bf16[4,256,128]{2,1,0:T(8,128)(2,1)S(1)}, bf16[4,256,128]{2,1,0:T(8,128)(2,1)S(1)}, u32[]{:S(2)}, u32[]{:S(2)}) %collective-permute-start.23) | collective-permute-done | bytes 262176 | tf_op jit(solution)/shard_map/ppermute | solution.py:333
  102.1 4.7 %collective-permute-done.16.refs_2_ = bf16[1024,128]{1,0:T(8,128)(2,1)S(1)} collective-permute-done((bf16[1024,128]{1,0:T(8,128)(2,1)S(1)}, bf16[1024,128]{1,0:T(8,128)(2,1)S(1)}, u32[]{:S(2)}, u32[]{:S(2)}) %collective-permute-start.16) | collective-permute-done | bytes 262176 | tf_op jit(solution)/shard_map/ppermute | solution.py:333
  108.1 8.1 %collective-permute-done.25.refs_11_ = bf16[8,256,128]{2,1,0:T(8,128)(2,1)S(1)} collective-permute-done((bf16[8,256,128]{2,1,0:T(8,128)(2,1)S(1)}, bf16[8,256,128]{2,1,0:T(8,128)(2,1)S(1)}, u32[]{:S(2)}, u32[]{:S(2)}) %collective-permute-start.25) | collective-permute-done | bytes 524320 | tf_op jit(solution)/shard_map/ppermute | solution.py:333
  116.2 10.1 %collective-permute-done.9.refs_4_ = bf16[128,2048]{1,0:T(8,128)(2,1)S(1)} collective-permute-done((bf16[128,2048]{1,0:T(8,128)(2,1)S(1)}, bf16[128,2048]{1,0:T(8,128)(2,1)S(1)}, u32[]{:S(2)}, u32[]{:S(2)}) %collective-permute-start.9) | collective-permute-done | bytes 524320 | tf_op jit(solution)/shard_map/ppermute | solution.py:333
  127.4 6.6 %mixed_part.3.refs_3_ = bf16[128,2048]{1,0:T(8,128)(2,1)} custom-call(s32[2]{0:T(128)S(1)} %pad_add_fusion.refs_0_.me_ref, bf16[2048,8192]{1,0:T(8,128)(2,1)} %refs_1_.18, bf16[128,2048]{1,0:T(8,128)(2,1)S(1)} %get-tuple-element.27.refs_5_.refs_2_.refs_0_, bf16[128,2048]{1,0:T(8,128)(2,1)S(1)} %collective-permute-done.8.refs_3_, ...), custom_call_target="tpu_custom_call" | custom-call | flops 3000000000 | tf_op jit(solution)/shard_map/mixed_part/pallas_call | solution.py:196
  135.8 2.5 %collective-permute-start.21 = (bf16[128,1024]{1,0:T(8,128)(2,1)S(1)}, bf16[128,1024]{1,0:T(8,128)(2,1)S(1)}, u32[]{:S(2)}, u32[]{:S(2)}) collective-permute-start(bf16[128,1024]{1,0:T(8,128)(2,1)S(1)} %slice.45), channel_id=1, source_target_pairs={{8,0},{16,8},{24,16},{28,24},{20,28},{12,20},{4,12},{0,4},{9,1},{1... | collective-permute-start | bytes 786440 | tf_op jit(solution)/shard_map/ppermute | solution.py:483
  138.4 5.3 %collective-permute-done.18.refs_2_ = bf16[512,128]{1,0:T(8,128)(2,1)S(1)} collective-permute-done((bf16[512,128]{1,0:T(8,128)(2,1)S(1)}, bf16[512,128]{1,0:T(8,128)(2,1)S(1)}, u32[]{:S(2)}, u32[]{:S(2)}) %collective-permute-start.18) | collective-permute-done | bytes 131104 | tf_op jit(solution)/shard_map/ppermute | solution.py:333
  144.4 2.8 %collective-permute-done.21.refs_4_.refs_8_ = bf16[128,1024]{1,0:T(8,128)(2,1)S(1)} collective-permute-done((bf16[128,1024]{1,0:T(8,128)(2,1)S(1)}, bf16[128,1024]{1,0:T(8,128)(2,1)S(1)}, u32[]{:S(2)}, u32[]{:S(2)}) %collective-permute-start.21) | collective-permute-done | bytes 262176 | tf_op jit(solution)/shard_map/ppermute | solution.py:483
  147.2 2.1 %collective-permute-done.19.refs_2_ = bf16[512,128]{1,0:T(8,128)(2,1)S(1)} collective-permute-done((bf16[512,128]{1,0:T(8,128)(2,1)S(1)}, bf16[512,128]{1,0:T(8,128)(2,1)S(1)}, u32[]{:S(2)}, u32[]{:S(2)}) %collective-permute-start.19) | collective-permute-done | bytes 131104 | tf_op jit(solution)/shard_map/ppermute | solution.py:333
  149.9 2.8 %collective-permute-start.22 = (bf16[1024,128]{1,0:T(8,128)(2,1)S(1)}, bf16[1024,128]{1,0:T(8,128)(2,1)S(1)}, u32[]{:S(2)}, u32[]{:S(2)}) collective-permute-start(bf16[1024,128]{1,0:T(8,128)(2,1)S(1)} %joined.2.refs_1_), channel_id=1, source_target_pairs={{0,4},{4,0},{8,12},{12,8},{16,20},{20,16},{24,28},{28,24},{1,5},{5... | collective-permute-start | bytes 786440 | tf_op jit(solution)/shard_map/ppermute | solution.py:333
  152.8 8.8 %grad_weight.1 = bf16[2048,1024]{1,0:T(8,128)(2,1)} custom-call(s32[2]{0:T(128)S(1)} %pad_add_fusion.refs_0_.me_ref, s32[8,8]{1,0:T(8,128)S(1)} %copy-done.16, bf16[128,2048]{1,0:T(8,128)(2,1)S(1)} %get-tuple-element.27.refs_5_.refs_2_.refs_0_, bf16[128,2048]{1,0:T(8,128)(2,1)S(1)} %collective-permute-done.4.refs_7_.refs_1_, ...), custom_call_target="tpu_custom_call" | custom-call | flops 6000000000 | tf_op jit(solution)/shard_map/grad_weight/pallas_call | solution.py:294
  161.5 1.6 joined.3
  (84 shorter events, 15.6 us)
Async XLA Ops:
  0.7 32.8 %copy-start.1 = (bf16[128,2048]{1,0:T(8,128)(2,1)S(1)}, bf16[128,2048]{1,0:T(8,128)(2,1)}, u32[]{:S(2)}) copy-start(bf16[128,2048]{1,0:T(8,128)(2,1)} %refs_1_.11) | copy-start | bytes 1572868
  2.9 15.1 %collective-permute-start.1 = (bf16[128,2048]{1,0:T(8,128)(2,1)}, bf16[128,2048]{1,0:T(8,128)(2,1)S(1)}, u32[]{:S(2)}, u32[]{:S(2)}) collective-permute-start(bf16[128,2048]{1,0:T(8,128)(2,1)} %refs_1_.11), channel_id=1, source_target_pairs={{0,2},{1,3},{2,0},{3,1},{4,6},{5,7},{6,4},{7,5},{8,10},{9,11},{10,... | collective-permute-start | bytes 1572872 | tf_op jit(solution)/shard_map/ppermute | solution.py:333
  5.8 27.6 %collective-permute-start.3 = (bf16[128,2048]{1,0:T(8,128)(2,1)}, bf16[128,2048]{1,0:T(8,128)(2,1)S(1)}, u32[]{:S(2)}, u32[]{:S(2)}) collective-permute-start(bf16[128,2048]{1,0:T(8,128)(2,1)} %refs_1_.11), channel_id=1, source_target_pairs={{0,1},{1,0},{2,3},{3,2},{4,5},{5,4},{6,7},{7,6},{8,9},{9,8},{10,11... | collective-permute-start | bytes 1572872 | tf_op jit(solution)/shard_map/ppermute | solution.py:333
  5.8 15.6 %collective-permute-start = (bf16[128,2048]{1,0:T(8,128)(2,1)}, bf16[128,2048]{1,0:T(8,128)(2,1)}, u32[]{:S(2)}, u32[]{:S(2)}) collective-permute-start(bf16[128,2048]{1,0:T(8,128)(2,1)} %multiply_convert_fusion), channel_id=1, source_target_pairs={{0,4},{4,8},{8,12},{12,16},{16,20},{20,24},{24,28},{1,5},{5,9},{9,... | collective-permute-start | bytes 1572872 | tf_op jit(solution)/shard_map/ppermute | solution.py:448
  17.9 15.5 %collective-permute-start.2 = (bf16[128,2048]{1,0:T(8,128)(2,1)S(1)}, bf16[128,2048]{1,0:T(8,128)(2,1)S(1)}, u32[]{:S(2)}, u32[]{:S(2)}) collective-permute-start(bf16[128,2048]{1,0:T(8,128)(2,1)S(1)} %collective-permute-done.1.refs_3_), channel_id=1, source_target_pairs={{0,1},{1,0},{2,3},{3,2},{4,5},{5,4},{6,7},{7,6},{8,9},{9,8},{10,11... | collective-permute-start | bytes 1572872 | tf_op jit(solution)/shard_map/ppermute | solution.py:333
  29.9 21.0 %collective-permute-start.5 = (bf16[128,2048]{1,0:T(8,128)(2,1)S(1)}, bf16[128,2048]{1,0:T(8,128)(2,1)S(1)}, u32[]{:S(2)}, u32[]{:S(2)}) collective-permute-start(bf16[128,2048]{1,0:T(8,128)(2,1)S(1)} %get-tuple-element.27.refs_5_.refs_2_.refs_0_), channel_id=1, source_target_pairs={{8,0},{16,8},{24,16},{28,24},{20,28},{12,20},{4,12},{0,4},{9,1},{1... | collective-permute-start | bytes 1572872 | tf_op jit(solution)/shard_map/ppermute | solution.py:480
  32.4 19.2 %collective-permute-start.4 = (bf16[128,2048]{1,0:T(8,128)(2,1)S(1)}, bf16[128,2048]{1,0:T(8,128)(2,1)S(1)}, u32[]{:S(2)}, u32[]{:S(2)}) collective-permute-start(bf16[128,2048]{1,0:T(8,128)(2,1)S(1)} %get-tuple-element.27.refs_5_.refs_2_.refs_0_), channel_id=1, source_target_pairs={{0,8},{8,16},{16,24},{24,28},{28,20},{20,12},{12,4},{4,0},{1,9},{9... | collective-permute-start | bytes 1572872 | tf_op jit(solution)/shard_map/ppermute | solution.py:479
  34.1 24.8 %collective-permute-start.6 = (bf16[4,256,128]{2,1,0:T(8,128)(2,1)S(1)}, bf16[4,256,128]{2,1,0:T(8,128)(2,1)S(1)}, u32[]{:S(2)}, u32[]{:S(2)}) collective-permute-start(bf16[4,256,128]{2,1,0:T(8,128)(2,1)S(1)} %get-tuple-element.31), channel_id=1, source_target_pairs={{0,16},{4,20},{8,24},{12,28},{16,0},{20,4},{24,8},{28,12},{1,17},{... | collective-permute-start | bytes 786440 | tf_op jit(solution)/shard_map/ppermute | solution.py:333
  43.4 25.5 %copy-start.7 = (bf16[128,2048]{1,0:T(8,128)(2,1)S(1)}, bf16[128,2048]{1,0:T(8,128)(2,1)}, u32[]{:S(2)}) copy-start(bf16[128,2048]{1,0:T(8,128)(2,1)} %refs_0_.5) | copy-start | bytes 1572868
  43.4 25.5 %copy-start.9 = (bf16[128,2048]{1,0:T(8,128)(2,1)S(1)}, bf16[128,2048]{1,0:T(8,128)(2,1)}, u32[]{:S(2)}) copy-start(bf16[128,2048]{1,0:T(8,128)(2,1)} %refs_1_.17) | copy-start | bytes 1572868
  43.4 25.5 %copy-start.14 = (bf16[2,128,256]{2,1,0:T(8,128)(2,1)S(1)}, bf16[2,128,256]{2,1,0:T(8,128)(2,1)}, u32[]{:S(2)}) copy-start(bf16[2,128,256]{2,1,0:T(8,128)(2,1)} %constant.26.clone.refs_5_) | copy-start | bytes 393220
  50.9 22.5 %collective-permute-start.12 = (bf16[128,2048]{1,0:T(8,128)(2,1)S(1)}, bf16[128,2048]{1,0:T(8,128)(2,1)S(1)}, u32[]{:S(2)}, u32[]{:S(2)}) collective-permute-start(bf16[128,2048]{1,0:T(8,128)(2,1)S(1)} %collective-permute-done.5.refs_8_.refs_2_), channel_id=1, source_target_pairs={{8,0},{16,8},{24,16},{28,24},{20,28},{12,20},{4,12},{0,4},{9,1},{1... | collective-permute-start | bytes 1572872 | tf_op jit(solution)/shard_map/ppermute | solution.py:480
  51.6 24.6 %collective-permute-start.11 = (bf16[128,2048]{1,0:T(8,128)(2,1)S(1)}, bf16[128,2048]{1,0:T(8,128)(2,1)S(1)}, u32[]{:S(2)}, u32[]{:S(2)}) collective-permute-start(bf16[128,2048]{1,0:T(8,128)(2,1)S(1)} %collective-permute-done.4.refs_7_.refs_1_), channel_id=1, source_target_pairs={{0,8},{8,16},{16,24},{24,28},{28,20},{20,12},{12,4},{4,0},{1,9},{9... | collective-permute-start | bytes 1572872 | tf_op jit(solution)/shard_map/ppermute | solution.py:479
  59.0 18.8 %collective-permute-start.13 = (bf16[4,256,128]{2,1,0:T(8,128)(2,1)S(1)}, bf16[4,256,128]{2,1,0:T(8,128)(2,1)S(1)}, u32[]{:S(2)}, u32[]{:S(2)}) collective-permute-start(bf16[4,256,128]{2,1,0:T(8,128)(2,1)S(1)} %bitcast.19), channel_id=1, source_target_pairs={{0,8},{4,12},{8,0},{12,4},{16,24},{20,28},{24,16},{28,20},{1,9},{5... | collective-permute-start | bytes 786440 | tf_op jit(solution)/shard_map/ppermute | solution.py:333
  67.5 10.3 %collective-permute-start.7 = (bf16[128,2048]{1,0:T(8,128)(2,1)S(1)}, bf16[128,2048]{1,0:T(8,128)(2,1)S(1)}, u32[]{:S(2)}, u32[]{:S(2)}) collective-permute-start(bf16[128,2048]{1,0:T(8,128)(2,1)S(1)} %get-tuple-element.33), channel_id=1, source_target_pairs={{0,1},{1,0},{2,3},{3,2},{4,5},{5,4},{6,7},{7,6},{8,9},{9,8},{10,11... | collective-permute-start | bytes 1572872 | tf_op jit(solution)/shard_map/ppermute | solution.py:333
  67.5 16.9 %collective-permute-start.10 = (bf16[128,2048]{1,0:T(8,128)(2,1)S(1)}, bf16[128,2048]{1,0:T(8,128)(2,1)S(1)}, u32[]{:S(2)}, u32[]{:S(2)}) collective-permute-start(bf16[128,2048]{1,0:T(8,128)(2,1)S(1)} %get-tuple-element.32.refs_3_.refs_2_), channel_id=1, source_target_pairs={{4,0},{8,4},{12,8},{16,12},{20,16},{24,20},{28,24},{5,1},{9,5},{13... | collective-permute-start | bytes 1572872 | tf_op jit(solution)/shard_map/ppermute | solution.py:495
  73.4 34.5 %collective-permute-start.15 = (bf16[128,2048]{1,0:T(8,128)(2,1)S(1)}, bf16[128,2048]{1,0:T(8,128)(2,1)S(1)}, u32[]{:S(2)}, u32[]{:S(2)}) collective-permute-start(bf16[128,2048]{1,0:T(8,128)(2,1)S(1)} %collective-permute-done.12.refs_8_.refs_4_), channel_id=1, source_target_pairs={{8,0},{16,8},{24,16},{28,24},{20,28},{12,20},{4,12},{0,4},{9,1},{1... | collective-permute-start | bytes 1572872 | tf_op jit(solution)/shard_map/ppermute | solution.py:480
  76.2 31.8 %collective-permute-start.14 = (bf16[128,2048]{1,0:T(8,128)(2,1)S(1)}, bf16[128,2048]{1,0:T(8,128)(2,1)S(1)}, u32[]{:S(2)}, u32[]{:S(2)}) collective-permute-start(bf16[128,2048]{1,0:T(8,128)(2,1)S(1)} %collective-permute-done.11.refs_7_.refs_3_), channel_id=1, source_target_pairs={{0,8},{8,16},{16,24},{24,28},{28,20},{20,12},{12,4},{4,0},{1,9},{9... | collective-permute-start | bytes 1572872 | tf_op jit(solution)/shard_map/ppermute | solution.py:479
  83.6 69.2 %copy-start.16 = (s32[8,8]{1,0:T(8,128)S(1)}, s32[8,8]{1,0:T(8,128)}, u32[]{:S(2)}) copy-start(s32[8,8]{1,0:T(8,128)} %constant.27.clone.owner_ref) | copy-start | bytes 772
  83.6 32.6 %collective-permute-start.8 = (bf16[128,2048]{1,0:T(8,128)(2,1)S(1)}, bf16[128,2048]{1,0:T(8,128)(2,1)S(1)}, u32[]{:S(2)}, u32[]{:S(2)}) collective-permute-start(bf16[128,2048]{1,0:T(8,128)(2,1)S(1)} %mixed_part.2), channel_id=1, source_target_pairs={{0,1},{1,0},{2,3},{3,2},{4,5},{5,4},{6,7},{7,6},{8,9},{9,8},{10,11... | collective-permute-start | bytes 1572872 | tf_op jit(solution)/shard_map/ppermute | solution.py:333
  83.7 17.6 %collective-permute-start.23 = (bf16[4,256,128]{2,1,0:T(8,128)(2,1)S(1)}, bf16[4,256,128]{2,1,0:T(8,128)(2,1)S(1)}, u32[]{:S(2)}, u32[]{:S(2)}) collective-permute-start(bf16[4,256,128]{2,1,0:T(8,128)(2,1)S(1)} %get-tuple-element.42), channel_id=1, source_target_pairs={{0,4},{4,0},{8,12},{12,8},{16,20},{20,16},{24,28},{28,24},{1,5},{5... | collective-permute-start | bytes 786440 | tf_op jit(solution)/shard_map/ppermute | solution.py:333
  88.4 18.3 %collective-permute-start.16 = (bf16[1024,128]{1,0:T(8,128)(2,1)S(1)}, bf16[1024,128]{1,0:T(8,128)(2,1)S(1)}, u32[]{:S(2)}, u32[]{:S(2)}) collective-permute-start(bf16[1024,128]{1,0:T(8,128)(2,1)S(1)} %get-tuple-element.46), channel_id=1, source_target_pairs={{0,4},{4,0},{8,12},{12,8},{16,20},{20,16},{24,28},{28,24},{1,5},{5... | collective-permute-start | bytes 786440 | tf_op jit(solution)/shard_map/ppermute | solution.py:333
  101.3 14.9 %collective-permute-start.25 = (bf16[8,256,128]{2,1,0:T(8,128)(2,1)S(1)}, bf16[8,256,128]{2,1,0:T(8,128)(2,1)S(1)}, u32[]{:S(2)}, u32[]{:S(2)}) collective-permute-start(bf16[8,256,128]{2,1,0:T(8,128)(2,1)S(1)} %maximum_bitcast_fusion.refs_9_), channel_id=1, source_target_pairs={{0,2},{1,3},{2,0},{3,1},{4,6},{5,7},{6,4},{7,5},{8,10},{9,11},{10,... | collective-permute-start | bytes 1572872 | tf_op jit(solution)/shard_map/ppermute | solution.py:333
  106.8 19.6 %collective-permute-start.9 = (bf16[128,2048]{1,0:T(8,128)(2,1)S(1)}, bf16[128,2048]{1,0:T(8,128)(2,1)S(1)}, u32[]{:S(2)}, u32[]{:S(2)}) collective-permute-start(bf16[128,2048]{1,0:T(8,128)(2,1)S(1)} %add_convert_fusion), channel_id=1, source_target_pairs={{0,2},{1,3},{2,0},{3,1},{4,6},{5,7},{6,4},{7,5},{8,10},{9,11},{10,... | collective-permute-start | bytes 1572872 | tf_op jit(solution)/shard_map/ppermute | solution.py:333
  107.9 44.8 %collective-permute-start.24 = (bf16[8,256,128]{2,1,0:T(8,128)(2,1)S(1)}, bf16[8,256,128]{2,1,0:T(8,128)(2,1)S(1)}, u32[]{:S(2)}, u32[]{:S(2)}) collective-permute-start(bf16[8,256,128]{2,1,0:T(8,128)(2,1)S(1)} %maximum_bitcast_fusion.refs_9_), channel_id=1, source_target_pairs={{0,1},{1,0},{2,3},{3,2},{4,5},{5,4},{6,7},{7,6},{8,9},{9,8},{10,11... | collective-permute-start | bytes 1572872 | tf_op jit(solution)/shard_map/ppermute | solution.py:333
  108.0 26.0 %collective-permute-start.17 = (bf16[512,128]{1,0:T(8,128)(2,1)S(1)}, bf16[512,128]{1,0:T(8,128)(2,1)S(1)}, u32[]{:S(2)}, u32[]{:S(2)}) collective-permute-start(bf16[512,128]{1,0:T(8,128)(2,1)S(1)} %get-tuple-element.41), channel_id=1, source_target_pairs={{0,8},{4,12},{8,0},{12,4},{16,24},{20,28},{24,16},{28,20},{1,9},{5... | collective-permute-start | bytes 393224 | tf_op jit(solution)/shard_map/ppermute | solution.py:333
  116.2 36.6 %collective-permute-start.26 = (bf16[8,256,128]{2,1,0:T(8,128)(2,1)S(1)}, bf16[8,256,128]{2,1,0:T(8,128)(2,1)S(1)}, u32[]{:S(2)}, u32[]{:S(2)}) collective-permute-start(bf16[8,256,128]{2,1,0:T(8,128)(2,1)S(1)} %collective-permute-done.25.refs_11_), channel_id=1, source_target_pairs={{0,1},{1,0},{2,3},{3,2},{4,5},{5,4},{6,7},{7,6},{8,9},{9,8},{10,11... | collective-permute-start | bytes 1572872 | tf_op jit(solution)/shard_map/ppermute | solution.py:333
  135.7 8.1 %collective-permute-start.18 = (bf16[512,128]{1,0:T(8,128)(2,1)S(1)}, bf16[512,128]{1,0:T(8,128)(2,1)S(1)}, u32[]{:S(2)}, u32[]{:S(2)}) collective-permute-start(bf16[512,128]{1,0:T(8,128)(2,1)S(1)} %added.4.refs_1_), channel_id=1, source_target_pairs={{0,16},{4,20},{8,24},{12,28},{16,0},{20,4},{24,8},{28,12},{1,17},{... | collective-permute-start | bytes 393224 | tf_op jit(solution)/shard_map/ppermute | solution.py:333
  135.8 11.4 %collective-permute-start.21 = (bf16[128,1024]{1,0:T(8,128)(2,1)S(1)}, bf16[128,1024]{1,0:T(8,128)(2,1)S(1)}, u32[]{:S(2)}, u32[]{:S(2)}) collective-permute-start(bf16[128,1024]{1,0:T(8,128)(2,1)S(1)} %slice.45), channel_id=1, source_target_pairs={{8,0},{16,8},{24,16},{28,24},{20,28},{12,20},{4,12},{0,4},{9,1},{1... | collective-permute-start | bytes 786440 | tf_op jit(solution)/shard_map/ppermute | solution.py:483
  138.3 8.9 %collective-permute-start.20 = (bf16[128,1024]{1,0:T(8,128)(2,1)S(1)}, bf16[128,1024]{1,0:T(8,128)(2,1)S(1)}, u32[]{:S(2)}, u32[]{:S(2)}) collective-permute-start(bf16[128,1024]{1,0:T(8,128)(2,1)S(1)} %slice.44), channel_id=1, source_target_pairs={{0,8},{8,16},{16,24},{24,28},{28,20},{20,12},{12,4},{4,0},{1,9},{9... | collective-permute-start | bytes 786440 | tf_op jit(solution)/shard_map/ppermute | solution.py:482
  144.3 5.0 %collective-permute-start.19 = (bf16[512,128]{1,0:T(8,128)(2,1)S(1)}, bf16[512,128]{1,0:T(8,128)(2,1)S(1)}, u32[]{:S(2)}, u32[]{:S(2)}) collective-permute-start(bf16[512,128]{1,0:T(8,128)(2,1)S(1)} %added.5.refs_1_), channel_id=1, source_target_pairs={{0,8},{4,12},{8,0},{12,4},{16,24},{20,28},{24,16},{28,20},{1,9},{5... | collective-permute-start | bytes 393224 | tf_op jit(solution)/shard_map/ppermute | solution.py:333
  149.9 11.6 %collective-permute-start.22 = (bf16[1024,128]{1,0:T(8,128)(2,1)S(1)}, bf16[1024,128]{1,0:T(8,128)(2,1)S(1)}, u32[]{:S(2)}, u32[]{:S(2)}) collective-permute-start(bf16[1024,128]{1,0:T(8,128)(2,1)S(1)} %joined.2.refs_1_), channel_id=1, source_target_pairs={{0,4},{4,0},{8,12},{12,8},{16,20},{20,16},{24,28},{28,24},{1,5},{5... | collective-permute-start | bytes 786440 | tf_op jit(solution)/shard_map/ppermute | solution.py:333
  (12 other events, 107.7 us)

commit v11 on v9

--- a/solution.py
+++ b/solution.py
@@ -198,115 +198,126 @@
         ),
         out_shape=out_shape,
         compiler_params=pltpu.CompilerParams(vmem_limit_bytes=VMEM_BYTES),
-        cost_estimate=estimate(3 * ((cot is not None) + (gated is not None))),
+        cost_estimate=estimate(3 if gated is None else 0.5),
         name="grad_gated_part" if gated is None else "mixed_part" if cot is None else "grads_and_mixed",
     )(me, *arrays, *after)
 
 
-def pieces_kernel(per_chan, me_ref, *refs):
+def pieces_kernel(per_chan, me_ref, slot_ref, *refs):
     out_ref = refs[-1]
     length, width = refs[0].shape
     span = width // per_chan
     count = len(refs) - 1
     piece = span // count
+    rows = length * piece // width
     for off in range(count):
         for part in range(per_chan):
             target = (me_ref[1] ^ off) * per_chan + part
             start = pl.multiple_of(part * span + me_ref[1] * piece, 128)
             block = refs[off][:, pl.ds(start, piece)]
-            out_ref[target ^ me_ref[0]] = jnp.concatenate(
-                [block[:, at : at + 128] for at in range(0, piece, 128)], axis=0
+            place = pl.multiple_of(slot_ref[me_ref[0], target] * rows, rows)
+            out_ref[pl.ds(place, rows), :] = jnp.concatenate(
+                [block[at : at + rows] for at in range(0, length, rows)], axis=1
             )
 
 
-def pieces_of(me, cots, n_ctx, after):
+def pieces_of(me, slots, cots, after):
     length, width = cots[0].shape
+    n_ctx = slots.shape[0]
     piece = width // n_ctx
-    rows = length * piece // 128
     if piece % 128:
-        return pieces_by_slices(me, cots, n_ctx)
+        return pieces_by_slices(me, slots, cots)
     return pl.pallas_call(
-        ignoring(functools.partial(pieces_kernel, n_ctx // len(cots)), len(after), 1 + len(cots)),
+        ignoring(functools.partial(pieces_kernel, n_ctx // len(cots)), len(after), 2 + len(cots)),
         grid_spec=pltpu.PrefetchScalarGridSpec(
-            num_scalar_prefetch=1,
+            num_scalar_prefetch=2,
             grid=(1,),
-            in_specs=[pl.BlockSpec((length, width), lambda i, me: (0, 0))] * len(cots)
+            in_specs=[pl.BlockSpec((length, width), lambda i, *ids: (0, 0))] * len(cots)
             + [pl.BlockSpec(memory_space=pl.ANY)] * len(after),
-            out_specs=pl.BlockSpec((n_ctx, rows, 128), lambda i, me: (0, 0, 0)),
+            out_specs=pl.BlockSpec((length, width), lambda i, *ids: (0, 0)),
         ),
-        out_shape=jax.ShapeDtypeStruct((n_ctx, rows, 128), BF16),
+        out_shape=jax.ShapeDtypeStruct((length, width), BF16),
         compiler_params=pltpu.CompilerParams(vmem_limit_bytes=VMEM_BYTES),
         cost_estimate=estimate(0.5),
         name="pieces",
-    )(me, *cots, *after)
-
-
-def pieces_by_slices(me, cots, n_ctx):
+    )(me, slots, *cots, *after)
+
+
+def pieces_by_slices(me, slots, cots):
     length, width = cots[0].shape
-    count = len(cots)
-    piece = width // n_ctx
-    table = jnp.stack(cots).reshape(count, length, n_ctx // count, count, piece)
+    n_ctx, count = slots.shape[0], len(cots)
+    piece, per_chan = width // n_ctx, n_ctx // count
+    rows = length * piece // width
+    table = jnp.stack(cots).reshape(count, length, per_chan, count, piece)
     mine = lax.dynamic_index_in_dim(table, me[1], 3, False)
-    parts = mine.transpose(0, 2, 1, 3).reshape(n_ctx, length * piece // 128, 128)
-    order = jnp.arange(n_ctx, dtype=jnp.int32) ^ me[0]
-    per_chan = n_ctx // count
-    return parts[(order // per_chan ^ me[1]) * per_chan + order % per_chan]
-
-
-def weight_kernel(slots, parts, half, me_ref, owner_ref, *refs):
-    gated_refs = refs[: slots - 1]
-    far_low, far_high = refs[slots - 1 : slots + 1]
-    cot_refs = refs[slots + 1 : slots + 1 + parts]
+    parts = mine.transpose(0, 2, 1, 3).reshape(n_ctx, length // rows, rows, piece)
+    parts = parts.transpose(0, 2, 1, 3).reshape(n_ctx, rows, width)
+    order = jnp.argsort(slots[me[0]])
+    return parts[(order // per_chan ^ me[1]) * per_chan + order % per_chan].reshape(length, width)
+
+
+def weight_kernel(places, parts, me_ref, *refs):
     out_ref = refs[-1]
-    length = far_low.shape[0]
-    far = jnp.where(pl.program_id(0) < half, far_low[...], far_high[...])
-    columns = jnp.concatenate([ref[...] for ref in gated_refs] + [far], axis=0)
+    length = sum(rows for unused, rows in places[0])
+    blocks = []
+    at = 0
+    for place in places:
+        for start, rows in place:
+            blocks.append(refs[at][start : start + rows, :])
+            at += 1
+    columns = jnp.concatenate(blocks, axis=0)
     for part in range(parts):
-        rows = []
-        for slot in range(slots):
-            block = cot_refs[part][owner_ref[me_ref[0], slot]]
-            rows.append(
-                jnp.concatenate([block[at : at + length] for at in range(0, block.shape[0], length)], axis=1)
-            )
-        total = mm(columns, jnp.concatenate(rows, axis=0), TN)
-        piece = total.shape[1]
-        place = pl.multiple_of((me_ref[1] ^ part) * piece, piece) if parts > 1 else 0
+        packed = jnp.concatenate([ref[...] for ref in refs[at + 2 * part : at + 2 * part + 2]], axis=0)
+        rows = packed.shape[0] // len(places)
+        piece = packed.shape[1] * rows // length
+        wide = [
+            packed[slot * rows : (slot + 1) * rows, lane : lane + piece]
+            for slot in range(len(places))
+            for lane in range(0, packed.shape[1], piece)
+        ]
+        total = mm(columns, jnp.concatenate(wide, axis=0), TN)
+        place = pl.multiple_of((me_ref[1] ^ part) * piece, piece)
         out_ref[:, pl.ds(place, piece)] = total.astype(BF16)
 
 
-def grad_weight_of(me, owners, blocks, far_low, far_high, cots):
-    length, channels = blocks[0].shape
-    rows = cots[0].shape[1]
-    piece = rows * 128 // length
+def grad_weight_of(me, arrays, places, cots):
+    channels = arrays[0].shape[1]
+    slots, parts = len(places), len(cots)
+    pieces = [array for pair in cots for array, unused in pair]
+    half = cots[0][0][0].shape[0]
     tile = 256
-    half = channels // tile // 2
-    slots, parts = len(blocks) + 1, len(cots)
-    in_specs = [pl.BlockSpec((length, tile), lambda i, *ids: (0, i)) for unused in blocks]
-    in_specs.append(pl.BlockSpec((length, tile), lambda i, *ids: (0, jnp.minimum(i, half - 1))))
-    in_specs.append(pl.BlockSpec((length, tile), lambda i, *ids: (0, jnp.maximum(i - half, 0))))
-    in_specs += [pl.BlockSpec(cot.shape, lambda i, *ids: (0, 0, 0)) for cot in cots]
+    width = 2 * half * channels // (slots * sum(count for unused, count in places[0])) * parts
     return pl.pallas_call(
-        functools.partial(weight_kernel, slots, parts, half),
+        functools.partial(weight_kernel, places, parts),
         grid_spec=pltpu.PrefetchScalarGridSpec(
-            num_scalar_prefetch=2,
+            num_scalar_prefetch=1,
             grid=(channels // tile,),
-            in_specs=in_specs,
-            out_specs=pl.BlockSpec((tile, piece * parts), lambda i, *ids: (i, 0)),
+            in_specs=[pl.BlockSpec((array.shape[0], tile), lambda i, me: (0, i)) for array in arrays]
+            + [pl.BlockSpec((half, channels), lambda i, me, at=at: (at, 0)) for pair in cots for unused, at in pair],
+            out_specs=pl.BlockSpec((tile, width), lambda i, me: (i, 0)),
         ),
-        out_shape=jax.ShapeDtypeStruct((channels, piece * parts), BF16),
+        out_shape=jax.ShapeDtypeStruct((channels, width), BF16),
         compiler_params=pltpu.CompilerParams(vmem_limit_bytes=VMEM_BYTES),
-        cost_estimate=estimate(6),
+        cost_estimate=estimate(2),
         name="grad_weight",
-    )(me, owners, *blocks, far_low, far_high, *cots)
-
-
-def in_one_piece(me, columns, length):
-    count, rows, unused = columns[0].shape
-    table = jnp.stack(columns)[jnp.arange(len(columns), dtype=jnp.int32) ^ me[1]]
-    piece = rows * 128 // length
-    flat = table.reshape(len(columns), count, length, piece).transpose(1, 2, 0, 3)
-    flat = flat.reshape(count, length, piece * len(columns) // 128, 128).transpose(0, 2, 1, 3)
-    return [flat.reshape(count, -1, 128)]
+    )(me, *arrays, *pieces)
+
+
+def narrow_grad_weight(me, arrays, places, cots):
+    blocks, at = [], 0
+    for place in places:
+        for start, rows in place:
+            blocks.append(arrays[at][start : start + rows])
+            at += 1
+    columns = jnp.concatenate(blocks, axis=0)
+    length = columns.shape[0] // len(places)
+    packed = jnp.stack([jnp.concatenate(pair, axis=0) for pair in cots])
+    packed = packed[jnp.arange(len(cots), dtype=jnp.int32) ^ me[1]]
+    parts, height, width = packed.shape
+    rows = height // len(places)
+    piece = rows * width // length
+    wide = packed.reshape(parts, len(places), rows, length // rows, piece).transpose(1, 3, 2, 0, 4)
+    return mm(columns, wide.reshape(columns.shape[0], parts * piece), TN).astype(BF16)
 
 
 def cycle_of(count):
@@ -331,9 +342,9 @@
     return [1 << place for place in range(size.bit_length() - 1)]
 
 
-def gather_by_swaps(block):
+def gather_of_chips(block):
     held = {0: block}
-    for bit in reversed(bits_of(lax.axis_size("chan"))):
+    for bit in reversed(bits_of(lax.axis_size("chan"))[1:]):
         held.update({off ^ bit: swap(held[off], "chan", bit) for off in list(held)})
     return held
 
@@ -375,14 +386,14 @@
     return jnp.where(mine, high, low), jnp.where(mine, low, high)
 
 
-def summed(me, partial, gates):
+def summed(me, partial, gates, join_gate):
     bits = bits_of(lax.axis_size("ctx"))
     sums, send = split(me, partial, bits[0])
     for step, bit in enumerate(bits):
         came = swap(send if step < 2 else sums, "ctx", bit)
         sums, *send = added(me, sums, came, bits[1] if step == 0 else 0, gates[step] if step < len(gates) else ())
         send = send[0] if send else None
-    sums = joined(me, sums, swap(sums, "ctx", bits[1]), bits[1], BF16, ())
+    sums = joined(me, sums, swap(sums, "ctx", bits[1]), bits[1], BF16, join_gate)
     return sums, swap(sums, "ctx", bits[0]), bits[0]
 
 
@@ -411,23 +422,12 @@
     )(me, own, other, *after)
 
 
-def exchanged(pieces):
-    held, sources, stages = pieces[None], [0], []
-    for bit in reversed(bits_of(pieces.shape[0])):
-        give = held[:, bit:].reshape((-1,) + pieces.shape[1:])
-        stages.append(swap(give, "ctx", bit))
-        came = stages[-1].reshape((len(sources), bit) + pieces.shape[1:])
-        held = jnp.concatenate([held[:, :bit], came], axis=0)
-        sources += [source ^ bit for source in sources]
-    return held[:, 0], sources, stages
-
-
 def per_device(query_proj, key_proj, value_proj, filters, out_weight, cotangent):
     length, channels = query_proj.shape
     taps = filters.shape[1]
     n_ctx, n_chan = lax.axis_size("ctx"), lax.axis_size("chan")
     me = jnp.stack([lax.axis_index("ctx"), lax.axis_index("chan")]).astype(jnp.int32)
-    forward, late, early, lags = [jnp.asarray(m) for m in transforms(taps)]
+    forward, late, early_rows, lags = [jnp.asarray(m) for m in transforms(taps)]
 
     product = (key_proj.astype(F32) * value_proj.astype(F32)).astype(BF16)
     product, cotangent = lax.optimization_barrier((product, cotangent))
@@ -441,7 +441,17 @@
     for off in offs:
         cots[off + 1] = swap(held_until([cots[off]], sums)[0], "chan", 1)
     offs = sorted(offs + [off + 1 for off in offs])
+
     sums = weight_pass(me, out_weight, 1, cot=cots[1], sums=sums)
+
+    order = cycle_of(n_ctx)
+    slots = []
+    for c in range(n_ctx):
+        spot = order.index(c)
+        turn = [0, n_ctx // 2] + list(range(1, n_ctx // 2)) + list(range(1 - n_ctx // 2, 0))
+        targets = [order[(spot + step) % n_ctx] for step in turn]
+        slots.append([targets.index(target) for target in range(n_ctx)])
+    pieces = pieces_of(me, jnp.asarray(slots, jnp.int32), [cots[off] for off in range(n_chan)], sums)
 
     gated, filtered = by_channel(
         forward_kernel,
@@ -452,28 +462,40 @@
         after=sums,
     )
 
-    pieces = pieces_of(me, [cots[off] for off in range(n_chan)], n_ctx, sums)
-    held, sources, stages = exchanged(pieces)
-
-    order = cycle_of(n_ctx)
     ahead = [(order[i], order[(i + 1) % n_ctx]) for i in range(n_ctx)]
     behind = [(b, a) for a, b in ahead]
-    half = channels // 2
-    from_behind, from_ahead = gated, gated
-    blocks = [gated]
-    for step in range(n_ctx // 2 - 1):
-        from_behind = lax.ppermute(from_behind, "ctx", ahead)
-        from_ahead = lax.ppermute(from_ahead, "ctx", behind)
-        blocks += [from_behind, from_ahead]
-    far_low = lax.ppermute(from_behind[:, :half], "ctx", ahead)
-    far_high = lax.ppermute(from_ahead[:, half:], "ctx", behind)
+    turns = n_ctx // 2
+    rows, piece = length // n_ctx, channels // n_ctx
+    span = (turns - 1) * rows
+    across = lax.ppermute(
+        pieces[rows : 2 * rows], "ctx", [(order[i], order[(i + turns) % n_ctx]) for i in range(n_ctx)]
+    )
+    onto = jnp.concatenate([pieces[2 * rows : 2 * rows + span], gated], axis=0)
+    back = jnp.concatenate([gated, pieces[2 * rows + span :]], axis=0)
+    arrays, places = [gated], [[(0, length)]]
+    brought, arrived = [pieces[:rows], across], []
+    for step in range(1, turns):
+        onto, back = lax.ppermute(onto, "ctx", ahead), lax.ppermute(back, "ctx", behind)
+        arrived.append([onto, back])
+        arrays += [onto, back]
+        places += [[(onto.shape[0] - length, length)], [(0, length)]]
+        brought += [onto[:rows], back[-rows:]]
+        onto, back = onto[rows:], back[:-rows]
+    half = length // 2
+    far = [lax.ppermute(onto[:half], "ctx", ahead), lax.ppermute(back[half:], "ctx", behind)]
+    arrays = arrays[:1] + far + arrays[1:]
+    places.insert(1, [(0, half), (0, half)])
+
+    early = 2 + 2 * min(1, turns - 1)
+    cols = [gather_of_chips(jnp.concatenate(part, axis=0)) for part in (brought[:early], brought[early:])]
 
     terms = {}
     for off in offs[:-1]:
-        *sums, terms[off] = weight_pass(me, out_weight, off, gated, cots[off], sums, after=[pieces])
+        *sums, terms[off] = weight_pass(me, out_weight, off, gated, cots[off], sums)
+    terms[1] = weight_pass(me, out_weight, 1, gated, after=sums)[0]
     grad_query, grad_filtered, terms[offs[-1]] = weight_pass(
         me, out_weight, offs[-1], gated, cots[offs[-1]], sums, [query_proj, filtered],
-        blocks[1:3] + stages[:1],
+        arrived[0] + [terms[1]],
     )
     following = lax.ppermute(grad_filtered, "ctx", [(i + 1, i) for i in range(n_ctx - 1)])
 
@@ -485,36 +507,39 @@
         "tap_grad",
     )[0]
 
-    terms[1] = weight_pass(me, out_weight, 1, gated, after=[tap_grad])[0]
-    terms[0] = weight_pass(me, out_weight, 0, gated, after=blocks[3:5] + stages[1:2] + [terms[1]])[0]
-    gates = [[terms[1]], [terms[0]]]
-    for bit in bits_of(n_chan):
+    for off in [off for off in sorted(terms) if off > 1 and off % 2]:
+        terms[off ^ 1] = terms[off ^ 1] + swap(terms.pop(off), "chan", 1).astype(F32)
+    terms[0] = weight_pass(me, out_weight, 0, gated, after=arrived[1] + [tap_grad])[0]
+    last_part = terms[0]
+    terms[0] = terms[0] + swap(terms.pop(1), "chan", 1).astype(F32)
+    for bit in bits_of(n_chan)[1:]:
         for off in [off for off in sorted(terms, reverse=True) if off & bit]:
-            came = swap(terms.pop(off).astype(BF16), "chan", bit).astype(F32)
-            terms[off ^ bit] = terms[off ^ bit] + came
+            terms[off ^ bit] = terms[off ^ bit] + swap(terms.pop(off).astype(BF16), "chan", bit).astype(F32)
     mixed = terms[0].astype(BF16)
 
     grad_key, grad_value = by_channel(
         backward_kernel,
-        [key_proj, value_proj, grad_filtered, following, filters, forward, early],
+        [key_proj, value_proj, grad_filtered, following, filters, forward, early_rows],
         "ttttcww",
         [("t", BF16), ("t", BF16)],
         "backward_filter",
-        after=gates[-1],
+        after=[last_part],
     )
-    halves_summed = summed(me, held_until([tap_grad], blocks[3:5])[0], [gates[-1], blocks[5:7], [far_low, far_high]])
-
-    columns = gather_by_swaps(held)
-    columns = [columns[off] for off in range(n_chan)]
-    if (channels // n_ctx) % 128:
-        columns = in_one_piece(me, columns, length)
-    owners = []
-    for c in range(n_ctx):
-        spot = order.index(c)
-        steps = [0] + [sign * step for step in range(1, n_ctx // 2) for sign in (-1, 1)] + [n_ctx // 2]
-        owners.append([sources.index(order[(spot + step) % n_ctx] ^ c) for step in steps])
-    grad_weight = grad_weight_of(me, jnp.asarray(owners, jnp.int32), blocks, far_low, far_high, columns)
-    own, other, bit = halves_summed
+    own, other, bit = summed(me, tap_grad, [[], arrived[2]], far)
+
+    evens = [off for off in range(n_chan) if off % 2 == 0]
+    wide = piece % 128 == 0 and 2 * early == n_ctx
+    columns = {off: [(part[off], 0) for part in cols] for off in evens}
+    crossed = swap(jnp.concatenate([part[off] for off in evens for part in cols], axis=0), "chan", 1)
+    if wide:
+        for at, off in enumerate(evens):
+            columns[off + 1] = [(crossed, 2 * at), (crossed, 2 * at + 1)]
+        grad_weight = grad_weight_of(me, arrays, places, [columns[off] for off in range(n_chan)])
+    else:
+        for at, off in enumerate(evens):
+            columns[off + 1] = [(crossed[at * length : (at + 1) * length], 0)]
+        pairs = [[array for array, unused in columns[off]] for off in range(n_chan)]
+        grad_weight = narrow_grad_weight(me, arrays, places, pairs)
     grad_filters = joined(me, own, held_until([other], [grad_weight])[0], bit, F32, ())
     return (mixed, grad_query, grad_key, grad_value, grad_filters, grad_weight)
 

time: 146 us -> 160 us (1.096)
  waiting for transfers between devices: 39.2 us -> 62.4 us
  starting transfers between devices: 37 us -> 29.2 us
    ppermute x8 -> x9, waiting for transfers between devices: 5.46 us -> 25.2 us  [the longest x3 20.8 us: per_device(): lax.ppermute(onto, 'ctx', ahead)]
    ppermute x17 -> x14, starting transfers between devices: 20.8 us -> 12.9 us  [swap(): return lax.ppermute(block, axis, [(i, i ^ bit) for i in range(size)])]
    ppermute x17 -> x14, waiting for transfers between devices: 33.7 us -> 37.1 us  [swap(): return lax.ppermute(block, axis, [(i, i ^ bit) for i in range(size)])]
    ppermute x8 -> x9, starting transfers between devices: 11.4 us -> 11.5 us  [the longest x1 4.85 us: per_device(): lax.ppermute(pieces[rows:2 * rows], 'ctx', [(order[i], order[(i + turns)...]
  transfers between devices with their start and end apart: 27 -> 25, of which waited for: 8 -> 9; matrix products, arithmetic and copies ran while one was open for 1% -> 1% of each run, Pallas kernels for 43% -> 38%
where the time goes in v11:
time: 160 us
  Pallas kernels  63.9 us (40%)
  waiting for transfers between devices  62.4 us (39%)
  starting transfers between devices  29.2 us (18%)
  other arithmetic  2.78 us (2%)
    pallas_call x6, Pallas kernels, weight_pass(): pl.pallas_call(ignoring(body, len(after), 1 + len(arrays)), grid_spec=plt...  39.7 us
    ppermute x14, waiting for transfers between devices, swap(): return lax.ppermute(block, axis, [(i, i ^ bit) for i in range(size)])  37.1 us
    ppermute x3, waiting for transfers between devices, per_device(): lax.ppermute(onto, 'ctx', ahead)  20.8 us
    ppermute x14, starting transfers between devices, swap(): return lax.ppermute(block, axis, [(i, i ^ bit) for i in range(size)])  12.9 us
    pallas_call x3, Pallas kernels, by_channel(): pl.pallas_call(ignoring(functools.partial(kernel, length), len(after), le...  10.8 us
    pallas_call x1, Pallas kernels, grad_weight_of(): pl.pallas_call(functools.partial(weight_kernel, places, parts), grid_spec...  8.65 us
    ppermute x1, starting transfers between devices, per_device(): lax.ppermute(pieces[rows:2 * rows], 'ctx', [(order[i], order[(i + turns)...  4.85 us
    ppermute x1, waiting for transfers between devices, per_device(): lax.ppermute(pieces[rows:2 * rows], 'ctx', [(order[i], order[(i + turns)...  4.45 us
  transfers between devices with their start and end apart: 25, of which 9 were waited for; matrix products, arithmetic and copies ran while one was open for 1% of the time, Pallas kernels for 38%

profile of v11, /device:TPU:0, one launch (start us, length us, event | category | flops | bytes accessed | tf_op | source)
XLA Modules:
  0.0 159.9 jit_solution(17828608504971812205)
XLA Ops:
  0.6 1.4 multiply_convert_fusion
  2.0 3.0 %collective-permute-start.2 = (bf16[128,2048]{1,0:T(8,128)(2,1)S(1)}, bf16[128,2048]{1,0:T(8,128)(2,1)S(1)}, u32[]{:S(2)}, u32[]{:S(2)}) collective-permute-start(bf16[128,2048]{1,0:T(8,128)(2,1)S(1)} %copy-done), channel_id=1, source_target_pairs={{0,2},{1,3},{2,0},{3,1},{4,6},{5,7},{6,4},{7,5},{8,10},{9,11},{10,... | collective-permute-start | bytes 1572872 | tf_op jit(solution)/shard_map/ppermute | solution.py:338
  5.0 3.4 %collective-permute-start = (bf16[128,2048]{1,0:T(8,128)(2,1)S(1)}, bf16[128,2048]{1,0:T(8,128)(2,1)S(1)}, u32[]{:S(2)}, u32[]{:S(2)}) collective-permute-start(bf16[128,2048]{1,0:T(8,128)(2,1)S(1)} %multiply_convert_fusion), channel_id=1, source_target_pairs={{0,4},{4,8},{8,12},{12,16},{16,20},{20,24},{24,28},{1,5},{5,9},{9,... | collective-permute-start | bytes 1572872 | tf_op jit(solution)/shard_map/ppermute | solution.py:434
  8.6 6.2 %grad_gated_part.2.refs_3_ = f32[2048,128]{1,0:T(8,128)S(1)} custom-call(s32[2]{0:T(128)S(1)} %pad_add_fusion.refs_0_.me_ref, bf16[2048,8192]{1,0:T(8,128)(2,1)} %refs_1_.17, bf16[128,2048]{1,0:T(8,128)(2,1)S(1)} %copy-done), custom_call_target="tpu_custom_call" | custom-call | flops 3000000000 | tf_op jit(solution)/shard_map/grad_gated_part/pallas_call | solution.py:190
  14.9 2.1 %collective-permute-done.2.refs_4_.refs_3_ = bf16[128,2048]{1,0:T(8,128)(2,1)S(1)} collective-permute-done((bf16[128,2048]{1,0:T(8,128)(2,1)S(1)}, bf16[128,2048]{1,0:T(8,128)(2,1)S(1)}, u32[]{:S(2)}, u32[]{:S(2)}) %collective-permute-start.2) | collective-permute-done | bytes 524320 | tf_op jit(solution)/shard_map/ppermute | solution.py:338
  17.0 6.2 %grad_gated_part.3.refs_7_.refs_6_.refs_4_ = f32[2048,128]{1,0:T(8,128)S(1)} custom-call(s32[2]{0:T(128)S(1)} %pad_add_fusion.refs_0_.me_ref, bf16[2048,8192]{1,0:T(8,128)(2,1)} %refs_1_.17, bf16[128,2048]{1,0:T(8,128)(2,1)S(1)} %collective-permute-done.1.refs_2_.refs_3_, f32[2048,128]{1,0:T(8,128)S(1)} %grad_gated_part.2.refs_3_), custom_call_target="tpu_custom_call" | custom-call | flops 3000000000 | tf_op jit(solution)/shard_map/grad_gated_part/pallas_call | solution.py:190
  23.3 3.4 %forward_filter.1 = (bf16[128,2048]{1,0:T(8,128)(2,1)S(1)}, f32[128,2048]{1,0:T(8,128)S(1)}) custom-call(bf16[128,2048]{1,0:T(8,128)(2,1)S(1)} %copy-done.3, bf16[128,2048]{1,0:T(8,128)(2,1)S(1)} %copy-done.1, bf16[128,2048]{1,0:T(8,128)(2,1)S(1)} %copy-done.2, bf16[128,2048]{1,0:T(8,128)(2,1)S(1)} %collective-permute-done.refs_3_.refs_2_, ...), custom_call_target="tpu_custom_call" | custom-call | flops 3000000000 | tf_op jit(solution)/shard_map/forward_filter/pallas_call | solution.py:107
  27.6 1.8 %collective-permute-start.6 = (bf16[176,2048]{1,0:T(8,128)(2,1)S(1)}, bf16[176,2048]{1,0:T(8,128)(2,1)S(1)}, u32[]{:S(2)}, u32[]{:S(2)}) collective-permute-start(bf16[176,2048]{1,0:T(8,128)(2,1)S(1)} %get-tuple-element.53), channel_id=1, source_target_pairs={{8,0},{16,8},{24,16},{28,24},{20,28},{12,20},{4,12},{0,4},{9,1},{1... | collective-permute-start | bytes 2162696 | tf_op jit(solution)/shard_map/ppermute | solution.py:478
  29.7 4.8 %collective-permute-start.21 = (bf16[16,2048]{1,0:T(8,128)(2,1)S(1)}, bf16[16,2048]{1,0:T(8,128)(2,1)S(1)}, u32[]{:S(2)}, u32[]{:S(2)}) collective-permute-start(bf16[16,2048]{1,0:T(8,128)(2,1)S(1)} %get-tuple-element.49), channel_id=1, source_target_pairs={{0,28},{8,20},{16,12},{24,4},{28,0},{20,8},{12,16},{4,24},{1,29},{... | collective-permute-start | bytes 196616 | tf_op jit(solution)/shard_map/ppermute | solution.py:470
  34.5 7.4 %grads_and_mixed.2 = (f32[2048,128]{1,0:T(8,128)S(1)}, f32[128,2048]{1,0:T(8,128)S(1)}) custom-call(s32[2]{0:T(128)S(1)} %pad_add_fusion.refs_0_.me_ref, bf16[2048,8192]{1,0:T(8,128)(2,1)} %refs_1_.17, bf16[128,2048]{1,0:T(8,128)(2,1)S(1)} %get-tuple-element.23.refs_2_.refs_0_, bf16[128,2048]{1,0:T(8,128)(2,1)S(1)} %collective-permute-done.2.refs_4_.refs_3_, ...), custom_call_target="tpu_custom_call" | custom-call | flops 500000000 | tf_op jit(solution)/shard_map/grads_and_mixed/pallas_call | solution.py:190
  41.9 5.7 %mixed_part.2.refs_9_ = bf16[128,2048]{1,0:T(8,128)(2,1)S(1)} custom-call(s32[2]{0:T(128)S(1)} %pad_add_fusion.refs_0_.me_ref, bf16[2048,8192]{1,0:T(8,128)(2,1)} %refs_1_.17, bf16[128,2048]{1,0:T(8,128)(2,1)S(1)} %get-tuple-element.23.refs_2_.refs_0_, f32[2048,128]{1,0:T(8,128)S(1)} %get-tuple-element.25.refs_3_.refs_4_), custom_call_target="tpu_custom_call" | custom-call | flops 500000000 | tf_op jit(solution)/shard_map/mixed_part/pallas_call | solution.py:190
  47.8 4.4 %collective-permute-done.21 = bf16[16,2048]{1,0:T(8,128)(2,1)S(1)} collective-permute-done((bf16[16,2048]{1,0:T(8,128)(2,1)S(1)}, bf16[16,2048]{1,0:T(8,128)(2,1)S(1)}, u32[]{:S(2)}, u32[]{:S(2)}) %collective-permute-start.21) | collective-permute-done | bytes 65568 | tf_op jit(solution)/shard_map/ppermute | solution.py:470
  52.4 8.3 %grads_and_mixed.3 = (bf16[128,2048]{1,0:T(8,128)(2,1)}, bf16[128,2048]{1,0:T(8,128)(2,1)S(1)}, bf16[128,2048]{1,0:T(8,128)(2,1)S(1)}) custom-call(s32[2]{0:T(128)S(1)} %pad_add_fusion.refs_0_.me_ref, bf16[2048,8192]{1,0:T(8,128)(2,1)} %refs_1_.17, bf16[128,2048]{1,0:T(8,128)(2,1)S(1)} %get-tuple-element.23.refs_2_.refs_0_, ...), custom_call_target="tpu_custom_call" | custom-call | flops 500000000 | tf_op jit(solution)/shard_map/grads_and_mixed/pallas_call | solution.py:190
  62.0 3.5 %tap_grad.1.refs_5_ = bf16[2048,128]{1,0:T(8,128)(2,1)S(1)} custom-call(bf16[128,2048]{1,0:T(8,128)(2,1)S(1)} %copy-done.1, bf16[128,2048]{1,0:T(8,128)(2,1)S(1)} %copy-done.2, bf16[128,2048]{1,0:T(8,128)(2,1)S(1)} %collective-permute-done.refs_3_.refs_2_, bf16[128,2048]{1,0:T(8,128)(2,1)S(1)} %get-tuple-element.27.refs_3_.refs_2_, ...), custom_call_target="tpu_custom_call" | custom-call | flops 3000000000 | tf_op jit(solution)/shard_map/tap_grad/pallas_call | solution.py:107
  65.6 2.7 %collective-permute-start.12 = (bf16[1024,128]{1,0:T(8,128)(2,1)S(1)}, bf16[1024,128]{1,0:T(8,128)(2,1)S(1)}, u32[]{:S(2)}, u32[]{:S(2)}) collective-permute-start(bf16[1024,128]{1,0:T(8,128)(2,1)S(1)} %get-tuple-element.51), channel_id=1, source_target_pairs={{0,4},{4,0},{8,12},{12,8},{16,20},{20,16},{24,28},{28,24},{1,5},{5... | collective-permute-start | bytes 786440 | tf_op jit(solution)/shard_map/ppermute | solution.py:338
  68.3 2.0 %collective-permute-start.5 = (bf16[160,2048]{1,0:T(8,128)(2,1)S(1)}, bf16[160,2048]{1,0:T(8,128)(2,1)S(1)}, u32[]{:S(2)}, u32[]{:S(2)}) collective-permute-start(bf16[160,2048]{1,0:T(8,128)(2,1)S(1)} %slice.77), channel_id=1, source_target_pairs={{0,8},{8,16},{16,24},{24,28},{28,20},{20,12},{12,4},{4,0},{1,9},{9... | collective-permute-start | bytes 1966088 | tf_op jit(solution)/shard_map/ppermute | solution.py:478
  70.4 12.6 %collective-permute-done.12.refs_2_ = bf16[1024,128]{1,0:T(8,128)(2,1)S(1)} collective-permute-done((bf16[1024,128]{1,0:T(8,128)(2,1)S(1)}, bf16[1024,128]{1,0:T(8,128)(2,1)S(1)}, u32[]{:S(2)}, u32[]{:S(2)}) %collective-permute-start.12) | collective-permute-done | bytes 262176 | tf_op jit(solution)/shard_map/ppermute | solution.py:338
  83.1 1.5 collective-permute-start.22
  85.2 2.3 %collective-permute-start.15 = (bf16[144,2048]{1,0:T(8,128)(2,1)S(1)}, bf16[144,2048]{1,0:T(8,128)(2,1)S(1)}, u32[]{:S(2)}, u32[]{:S(2)}) collective-permute-start(bf16[144,2048]{1,0:T(8,128)(2,1)S(1)} %slice.83), channel_id=1, source_target_pairs={{8,0},{16,8},{24,16},{28,24},{20,28},{12,20},{4,12},{0,4},{9,1},{1... | collective-permute-start | bytes 1769480 | tf_op jit(solution)/shard_map/ppermute | solution.py:478
  87.6 7.5 %collective-permute-done.5.refs_3_.refs_5_ = bf16[160,2048]{1,0:T(8,128)(2,1)S(1)} collective-permute-done((bf16[160,2048]{1,0:T(8,128)(2,1)S(1)}, bf16[160,2048]{1,0:T(8,128)(2,1)S(1)}, u32[]{:S(2)}, u32[]{:S(2)}) %collective-permute-start.5) | collective-permute-done | bytes 655392 | tf_op jit(solution)/shard_map/ppermute | solution.py:478
  95.3 13.3 %collective-permute-done.14.refs_3_.refs_7_ = bf16[144,2048]{1,0:T(8,128)(2,1)S(1)} collective-permute-done((bf16[144,2048]{1,0:T(8,128)(2,1)S(1)}, bf16[144,2048]{1,0:T(8,128)(2,1)S(1)}, u32[]{:S(2)}, u32[]{:S(2)}) %collective-permute-start.14) | collective-permute-done | bytes 589856 | tf_op jit(solution)/shard_map/ppermute | solution.py:478
  109.0 5.6 %collective-permute-done.13.refs_2_ = bf16[512,128]{1,0:T(8,128)(2,1)S(1)} collective-permute-done((bf16[512,128]{1,0:T(8,128)(2,1)S(1)}, bf16[512,128]{1,0:T(8,128)(2,1)S(1)}, u32[]{:S(2)}, u32[]{:S(2)}) %collective-permute-start.13) | collective-permute-done | bytes 131104 | tf_op jit(solution)/shard_map/ppermute | solution.py:338
  114.5 1.4 collective-permute-start.23
  116.7 5.8 %collective-permute-done.23.refs_14_ = bf16[64,2048]{1,0:T(8,128)(2,1)S(1)} collective-permute-done((bf16[64,2048]{1,0:T(8,128)(2,1)S(1)}, bf16[64,2048]{1,0:T(8,128)(2,1)S(1)}, u32[]{:S(2)}, u32[]{:S(2)}) %collective-permute-start.23) | collective-permute-done | bytes 262176 | tf_op jit(solution)/shard_map/ppermute | solution.py:338
  122.7 7.4 %collective-permute-done.16.refs_2_ = bf16[512,128]{1,0:T(8,128)(2,1)S(1)} collective-permute-done((bf16[512,128]{1,0:T(8,128)(2,1)S(1)}, bf16[512,128]{1,0:T(8,128)(2,1)S(1)}, u32[]{:S(2)}, u32[]{:S(2)}) %collective-permute-start.16) | collective-permute-done | bytes 131104 | tf_op jit(solution)/shard_map/ppermute | solution.py:338
  130.1 1.4 collective-permute-start.10
  131.6 5.7 %mixed_part.3.refs_7_ = f32[128,2048]{1,0:T(8,128)S(1)} custom-call(s32[2]{0:T(128)S(1)} %pad_add_fusion.refs_0_.me_ref, bf16[2048,8192]{1,0:T(8,128)(2,1)} %refs_1_.17, bf16[128,2048]{1,0:T(8,128)(2,1)S(1)} %get-tuple-element.23.refs_2_.refs_0_, bf16[160,2048]{1,0:T(8,128)(2,1)S(1)} %collective-permute-done.5.refs_3_.refs_5_, ...), custom_call_target="tpu_custom_call" | custom-call | flops 500000000 | tf_op jit(solution)/shard_map/mixed_part/pallas_call | solution.py:190
  138.2 3.9 %backward_filter.1 = (bf16[128,2048]{1,0:T(8,128)(2,1)}, bf16[128,2048]{1,0:T(8,128)(2,1)}) custom-call(bf16[128,2048]{1,0:T(8,128)(2,1)S(1)} %copy-done.1, bf16[128,2048]{1,0:T(8,128)(2,1)S(1)} %copy-done.2, bf16[128,2048]{1,0:T(8,128)(2,1)S(1)} %get-tuple-element.27.refs_3_.refs_2_, bf16[128,2048]{1,0:T(8,128)(2,1)S(1)} %collective-permute-done.11.refs_3_, ...), custom_call_target="tpu_custom_call" | custom-call | flops 3000000000 | tf_op jit(solution)/shard_map/backward_filter/pallas_call | solution.py:107
  142.2 3.6 %collective-permute-done.17.refs_2_ = bf16[512,128]{1,0:T(8,128)(2,1)S(1)} collective-permute-done((bf16[512,128]{1,0:T(8,128)(2,1)S(1)}, bf16[512,128]{1,0:T(8,128)(2,1)S(1)}, u32[]{:S(2)}, u32[]{:S(2)}) %collective-permute-start.17) | collective-permute-done | bytes 131104 | tf_op jit(solution)/shard_map/ppermute | solution.py:338
  146.4 2.3 %collective-permute-start.20 = (bf16[1024,128]{1,0:T(8,128)(2,1)S(1)}, bf16[1024,128]{1,0:T(8,128)(2,1)S(1)}, u32[]{:S(2)}, u32[]{:S(2)}) collective-permute-start(bf16[1024,128]{1,0:T(8,128)(2,1)S(1)} %joined.2.refs_1_), channel_id=1, source_target_pairs={{0,4},{4,0},{8,12},{12,8},{16,20},{20,16},{24,28},{28,24},{1,5},{5... | collective-permute-start | bytes 786440 | tf_op jit(solution)/shard_map/ppermute | solution.py:338
  149.6 8.7 %grad_weight.1 = bf16[2048,1024]{1,0:T(8,128)(2,1)} custom-call(s32[2]{0:T(128)S(1)} %pad_add_fusion.refs_0_.me_ref, bf16[128,2048]{1,0:T(8,128)(2,1)S(1)} %get-tuple-element.23.refs_2_.refs_0_, bf16[64,2048]{1,0:T(8,128)(2,1)S(1)} %collective-permute-done.18.refs_3_.refs_1_, bf16[64,2048]{1,0:T(8,128)(2,1)S(1)} %collective-permute-done.19.refs_4_.refs_2_, ...), custom_call_target="tpu_custom_call" | custom-call | flops 2000000000 | tf_op jit(solution)/shard_map/grad_weight/pallas_call | solution.py:290
  158.3 1.6 %joined.3 = f32[2048,128]{1,0:T(8,128)} custom-call(s32[2]{0:T(128)S(1)} %pad_add_fusion.refs_0_.me_ref, bf16[1024,128]{1,0:T(8,128)(2,1)S(1)} %joined.2.refs_1_, bf16[1024,128]{1,0:T(8,128)(2,1)S(1)} %collective-permute-done.20.refs_2_), custom_call_target="tpu_custom_call" | custom-call | flops 500000000 | tf_op jit(solution)/shard_map/joined/pallas_call | solution.py:410
  (79 shorter events, 7.4 us)
Async XLA Ops:
  2.0 14.9 %collective-permute-start.2 = (bf16[128,2048]{1,0:T(8,128)(2,1)S(1)}, bf16[128,2048]{1,0:T(8,128)(2,1)S(1)}, u32[]{:S(2)}, u32[]{:S(2)}) collective-permute-start(bf16[128,2048]{1,0:T(8,128)(2,1)S(1)} %copy-done), channel_id=1, source_target_pairs={{0,2},{1,3},{2,0},{3,1},{4,6},{5,7},{6,4},{7,5},{8,10},{9,11},{10,... | collective-permute-start | bytes 1572872 | tf_op jit(solution)/shard_map/ppermute | solution.py:338
  5.0 11.9 %collective-permute-start.1 = (bf16[128,2048]{1,0:T(8,128)(2,1)S(1)}, bf16[128,2048]{1,0:T(8,128)(2,1)S(1)}, u32[]{:S(2)}, u32[]{:S(2)}) collective-permute-start(bf16[128,2048]{1,0:T(8,128)(2,1)S(1)} %copy-done), channel_id=1, source_target_pairs={{0,1},{1,0},{2,3},{3,2},{4,5},{5,4},{6,7},{7,6},{8,9},{9,8},{10,11... | collective-permute-start | bytes 1572872 | tf_op jit(solution)/shard_map/ppermute | solution.py:338
  5.0 18.2 %collective-permute-start = (bf16[128,2048]{1,0:T(8,128)(2,1)S(1)}, bf16[128,2048]{1,0:T(8,128)(2,1)S(1)}, u32[]{:S(2)}, u32[]{:S(2)}) collective-permute-start(bf16[128,2048]{1,0:T(8,128)(2,1)S(1)} %multiply_convert_fusion), channel_id=1, source_target_pairs={{0,4},{4,8},{8,12},{12,16},{16,20},{20,24},{24,28},{1,5},{5,9},{9,... | collective-permute-start | bytes 1572872 | tf_op jit(solution)/shard_map/ppermute | solution.py:434
  14.8 8.4 %copy-start.1 = (bf16[128,2048]{1,0:T(8,128)(2,1)S(1)}, bf16[128,2048]{1,0:T(8,128)(2,1)}, u32[]{:S(2)}) copy-start(bf16[128,2048]{1,0:T(8,128)(2,1)} %refs_0_.5) | copy-start | bytes 1572868
  14.8 8.4 %copy-start.2 = (bf16[128,2048]{1,0:T(8,128)(2,1)S(1)}, bf16[128,2048]{1,0:T(8,128)(2,1)}, u32[]{:S(2)}) copy-start(bf16[128,2048]{1,0:T(8,128)(2,1)} %refs_1_.18) | copy-start | bytes 1572868
  14.9 8.4 %copy-start.3 = (bf16[128,2048]{1,0:T(8,128)(2,1)S(1)}, bf16[128,2048]{1,0:T(8,128)(2,1)}, u32[]{:S(2)}) copy-start(bf16[128,2048]{1,0:T(8,128)(2,1)} %refs_5_.4) | copy-start | bytes 1572868
  14.9 8.4 %copy-start.5 = (bf16[2048,128]{1,0:T(8,128)(2,1)S(1)}, bf16[2048,128]{1,0:T(8,128)(2,1)}, u32[]{:S(2)}) copy-start(bf16[2048,128]{1,0:T(8,128)(2,1)} %refs_4_.4) | copy-start | bytes 1572868
  14.9 8.4 %copy-start.6 = (bf16[2,256,256]{2,1,0:T(8,128)(2,1)S(1)}, bf16[2,256,256]{2,1,0:T(8,128)(2,1)}, u32[]{:S(2)}) copy-start(bf16[2,256,256]{2,1,0:T(8,128)(2,1)} %constant.23.clone.refs_5_.refs_4_) | copy-start | bytes 786436
  14.9 8.4 %copy-start.9 = (bf16[2,128,256]{2,1,0:T(8,128)(2,1)S(1)}, bf16[2,128,256]{2,1,0:T(8,128)(2,1)}, u32[]{:S(2)}) copy-start(bf16[2,128,256]{2,1,0:T(8,128)(2,1)} %constant.24.clone.refs_6_) | copy-start | bytes 393220
  17.0 9.7 %collective-permute-start.3 = (bf16[128,2048]{1,0:T(8,128)(2,1)S(1)}, bf16[128,2048]{1,0:T(8,128)(2,1)S(1)}, u32[]{:S(2)}, u32[]{:S(2)}) collective-permute-start(bf16[128,2048]{1,0:T(8,128)(2,1)S(1)} %collective-permute-done.2.refs_4_.refs_3_), channel_id=1, source_target_pairs={{0,1},{1,0},{2,3},{3,2},{4,5},{5,4},{6,7},{7,6},{8,9},{9,8},{10,11... | collective-permute-start | bytes 1572872 | tf_op jit(solution)/shard_map/ppermute | solution.py:338
  27.6 24.6 %collective-permute-start.6 = (bf16[176,2048]{1,0:T(8,128)(2,1)S(1)}, bf16[176,2048]{1,0:T(8,128)(2,1)S(1)}, u32[]{:S(2)}, u32[]{:S(2)}) collective-permute-start(bf16[176,2048]{1,0:T(8,128)(2,1)S(1)} %get-tuple-element.53), channel_id=1, source_target_pairs={{8,0},{16,8},{24,16},{28,24},{20,28},{12,20},{4,12},{0,4},{9,1},{1... | collective-permute-start | bytes 2162696 | tf_op jit(solution)/shard_map/ppermute | solution.py:478
  29.4 23.0 %collective-permute-start.4 = (bf16[176,2048]{1,0:T(8,128)(2,1)S(1)}, bf16[176,2048]{1,0:T(8,128)(2,1)S(1)}, u32[]{:S(2)}, u32[]{:S(2)}) collective-permute-start(bf16[176,2048]{1,0:T(8,128)(2,1)S(1)} %get-tuple-element.54), channel_id=1, source_target_pairs={{0,8},{8,16},{16,24},{24,28},{28,20},{20,12},{12,4},{4,0},{1,9},{9... | collective-permute-start | bytes 2162696 | tf_op jit(solution)/shard_map/ppermute | solution.py:478
  29.7 22.5 %collective-permute-start.21 = (bf16[16,2048]{1,0:T(8,128)(2,1)S(1)}, bf16[16,2048]{1,0:T(8,128)(2,1)S(1)}, u32[]{:S(2)}, u32[]{:S(2)}) collective-permute-start(bf16[16,2048]{1,0:T(8,128)(2,1)S(1)} %get-tuple-element.49), channel_id=1, source_target_pairs={{0,28},{8,20},{16,12},{24,4},{28,0},{20,8},{12,16},{4,24},{1,29},{... | collective-permute-start | bytes 196616 | tf_op jit(solution)/shard_map/ppermute | solution.py:470
  47.7 101.0 %collective-permute-start.8 = (bf16[128,2048]{1,0:T(8,128)(2,1)S(1)}, bf16[128,2048]{1,0:T(8,128)(2,1)S(1)}, u32[]{:S(2)}, u32[]{:S(2)}) collective-permute-start(bf16[128,2048]{1,0:T(8,128)(2,1)S(1)} %mixed_part.2.refs_9_), channel_id=1, source_target_pairs={{0,1},{1,0},{2,3},{3,2},{4,5},{5,4},{6,7},{7,6},{8,9},{9,8},{10,11... | collective-permute-start | bytes 1572872 | tf_op jit(solution)/shard_map/ppermute | solution.py:338
  52.3 32.9 %collective-permute-start.7 = (bf16[160,2048]{1,0:T(8,128)(2,1)S(1)}, bf16[160,2048]{1,0:T(8,128)(2,1)S(1)}, u32[]{:S(2)}, u32[]{:S(2)}) collective-permute-start(bf16[160,2048]{1,0:T(8,128)(2,1)S(1)} %slice.79), channel_id=1, source_target_pairs={{8,0},{16,8},{24,16},{28,24},{20,28},{12,20},{4,12},{0,4},{9,1},{1... | collective-permute-start | bytes 1966088 | tf_op jit(solution)/shard_map/ppermute | solution.py:478
  52.4 9.6 %copy-start.8 = (bf16[2,128,256]{2,1,0:T(8,128)(2,1)S(1)}, bf16[2,128,256]{2,1,0:T(8,128)(2,1)}, u32[]{:S(2)}) copy-start(bf16[2,128,256]{2,1,0:T(8,128)(2,1)} %constant.26.clone.refs_5_) | copy-start | bytes 393220
  60.7 77.2 %collective-permute-start.11 = (bf16[128,2048]{1,0:T(8,128)(2,1)S(1)}, bf16[128,2048]{1,0:T(8,128)(2,1)S(1)}, u32[]{:S(2)}, u32[]{:S(2)}) collective-permute-start(bf16[128,2048]{1,0:T(8,128)(2,1)S(1)} %get-tuple-element.27.refs_3_.refs_2_), channel_id=1, source_target_pairs={{4,0},{8,4},{12,8},{16,12},{20,16},{24,20},{28,24},{5,1},{9,5},{13... | collective-permute-start | bytes 1572872 | tf_op jit(solution)/shard_map/ppermute | solution.py:500
  65.6 17.5 %collective-permute-start.12 = (bf16[1024,128]{1,0:T(8,128)(2,1)S(1)}, bf16[1024,128]{1,0:T(8,128)(2,1)S(1)}, u32[]{:S(2)}, u32[]{:S(2)}) collective-permute-start(bf16[1024,128]{1,0:T(8,128)(2,1)S(1)} %get-tuple-element.51), channel_id=1, source_target_pairs={{0,4},{4,0},{8,12},{12,8},{16,20},{20,16},{24,28},{28,24},{1,5},{5... | collective-permute-start | bytes 786440 | tf_op jit(solution)/shard_map/ppermute | solution.py:338
  68.3 26.8 %collective-permute-start.5 = (bf16[160,2048]{1,0:T(8,128)(2,1)S(1)}, bf16[160,2048]{1,0:T(8,128)(2,1)S(1)}, u32[]{:S(2)}, u32[]{:S(2)}) collective-permute-start(bf16[160,2048]{1,0:T(8,128)(2,1)S(1)} %slice.77), channel_id=1, source_target_pairs={{0,8},{8,16},{16,24},{24,28},{28,20},{20,12},{12,4},{4,0},{1,9},{9... | collective-permute-start | bytes 1966088 | tf_op jit(solution)/shard_map/ppermute | solution.py:478
  83.1 33.5 %collective-permute-start.22 = (bf16[64,2048]{1,0:T(8,128)(2,1)S(1)}, bf16[64,2048]{1,0:T(8,128)(2,1)S(1)}, u32[]{:S(2)}, u32[]{:S(2)}) collective-permute-start(bf16[64,2048]{1,0:T(8,128)(2,1)S(1)} %pad_maximum_fusion.2.refs_9_), channel_id=1, source_target_pairs={{0,2},{1,3},{2,0},{3,1},{4,6},{5,7},{6,4},{7,5},{8,10},{9,11},{10,... | collective-permute-start | bytes 786440 | tf_op jit(solution)/shard_map/ppermute | solution.py:338
  85.2 23.3 %collective-permute-start.15 = (bf16[144,2048]{1,0:T(8,128)(2,1)S(1)}, bf16[144,2048]{1,0:T(8,128)(2,1)S(1)}, u32[]{:S(2)}, u32[]{:S(2)}) collective-permute-start(bf16[144,2048]{1,0:T(8,128)(2,1)S(1)} %slice.83), channel_id=1, source_target_pairs={{8,0},{16,8},{24,16},{28,24},{20,28},{12,20},{4,12},{0,4},{9,1},{1... | collective-permute-start | bytes 1769480 | tf_op jit(solution)/shard_map/ppermute | solution.py:478
  95.2 13.4 %collective-permute-start.14 = (bf16[144,2048]{1,0:T(8,128)(2,1)S(1)}, bf16[144,2048]{1,0:T(8,128)(2,1)S(1)}, u32[]{:S(2)}, u32[]{:S(2)}) collective-permute-start(bf16[144,2048]{1,0:T(8,128)(2,1)S(1)} %slice.82), channel_id=1, source_target_pairs={{0,8},{8,16},{16,24},{24,28},{28,20},{20,12},{12,4},{4,0},{1,9},{9... | collective-permute-start | bytes 1769480 | tf_op jit(solution)/shard_map/ppermute | solution.py:478
  108.5 14.0 %collective-permute-start.9 = (bf16[128,2048]{1,0:T(8,128)(2,1)S(1)}, bf16[128,2048]{1,0:T(8,128)(2,1)S(1)}, u32[]{:S(2)}, u32[]{:S(2)}) collective-permute-start(bf16[128,2048]{1,0:T(8,128)(2,1)S(1)} %get-tuple-element.29), channel_id=1, source_target_pairs={{0,1},{1,0},{2,3},{3,2},{4,5},{5,4},{6,7},{7,6},{8,9},{9,8},{10,11... | collective-permute-start | bytes 1572872 | tf_op jit(solution)/shard_map/ppermute | solution.py:338
  108.6 6.0 %collective-permute-start.13 = (bf16[512,128]{1,0:T(8,128)(2,1)S(1)}, bf16[512,128]{1,0:T(8,128)(2,1)S(1)}, u32[]{:S(2)}, u32[]{:S(2)}) collective-permute-start(bf16[512,128]{1,0:T(8,128)(2,1)S(1)} %get-tuple-element.34), channel_id=1, source_target_pairs={{0,8},{4,12},{8,0},{12,4},{16,24},{20,28},{24,16},{28,20},{1,9},{5... | collective-permute-start | bytes 393224 | tf_op jit(solution)/shard_map/ppermute | solution.py:338
  114.5 7.9 %collective-permute-start.23 = (bf16[64,2048]{1,0:T(8,128)(2,1)S(1)}, bf16[64,2048]{1,0:T(8,128)(2,1)S(1)}, u32[]{:S(2)}, u32[]{:S(2)}) collective-permute-start(bf16[64,2048]{1,0:T(8,128)(2,1)S(1)} %pad_maximum_fusion.3.refs_10_), channel_id=1, source_target_pairs={{0,2},{1,3},{2,0},{3,1},{4,6},{5,7},{6,4},{7,5},{8,10},{9,11},{10,... | collective-permute-start | bytes 786440 | tf_op jit(solution)/shard_map/ppermute | solution.py:338
  116.6 21.5 %collective-permute-start.19 = (bf16[64,2048]{1,0:T(8,128)(2,1)S(1)}, bf16[64,2048]{1,0:T(8,128)(2,1)S(1)}, u32[]{:S(2)}, u32[]{:S(2)}) collective-permute-start(bf16[64,2048]{1,0:T(8,128)(2,1)S(1)} %slice.85), channel_id=1, source_target_pairs={{8,0},{16,8},{24,16},{28,24},{20,28},{12,20},{4,12},{0,4},{9,1},{1... | collective-permute-start | bytes 786440 | tf_op jit(solution)/shard_map/ppermute | solution.py:485
  122.5 7.7 %collective-permute-start.16 = (bf16[512,128]{1,0:T(8,128)(2,1)S(1)}, bf16[512,128]{1,0:T(8,128)(2,1)S(1)}, u32[]{:S(2)}, u32[]{:S(2)}) collective-permute-start(bf16[512,128]{1,0:T(8,128)(2,1)S(1)} %added.4.refs_1_), channel_id=1, source_target_pairs={{0,16},{4,20},{8,24},{12,28},{16,0},{20,4},{24,8},{28,12},{1,17},{... | collective-permute-start | bytes 393224 | tf_op jit(solution)/shard_map/ppermute | solution.py:338
  122.5 27.1 %collective-permute-start.24 = (bf16[256,2048]{1,0:T(8,128)(2,1)S(1)}, bf16[256,2048]{1,0:T(8,128)(2,1)S(1)}, u32[]{:S(2)}, u32[]{:S(2)}) collective-permute-start(bf16[256,2048]{1,0:T(8,128)(2,1)S(1)} %constant_dynamic-update-slice_fusion), channel_id=1, source_target_pairs={{0,1},{1,0},{2,3},{3,2},{4,5},{5,4},{6,7},{7,6},{8,9},{9,8},{10,11... | collective-permute-start | bytes 3145736 | tf_op jit(solution)/shard_map/ppermute | solution.py:338
  130.1 18.5 %collective-permute-start.10 = (bf16[128,2048]{1,0:T(8,128)(2,1)S(1)}, bf16[128,2048]{1,0:T(8,128)(2,1)S(1)}, u32[]{:S(2)}, u32[]{:S(2)}) collective-permute-start(bf16[128,2048]{1,0:T(8,128)(2,1)S(1)} %add_convert_fusion.1), channel_id=1, source_target_pairs={{0,2},{1,3},{2,0},{3,1},{4,6},{5,7},{6,4},{7,5},{8,10},{9,11},{10,... | collective-permute-start | bytes 1572872 | tf_op jit(solution)/shard_map/ppermute | solution.py:338
  138.0 7.8 %collective-permute-start.18 = (bf16[64,2048]{1,0:T(8,128)(2,1)S(1)}, bf16[64,2048]{1,0:T(8,128)(2,1)S(1)}, u32[]{:S(2)}, u32[]{:S(2)}) collective-permute-start(bf16[64,2048]{1,0:T(8,128)(2,1)S(1)} %slice.84), channel_id=1, source_target_pairs={{0,8},{8,16},{16,24},{24,28},{28,20},{20,12},{12,4},{4,0},{1,9},{9... | collective-permute-start | bytes 786440 | tf_op jit(solution)/shard_map/ppermute | solution.py:485
  138.0 7.7 %collective-permute-start.17 = (bf16[512,128]{1,0:T(8,128)(2,1)S(1)}, bf16[512,128]{1,0:T(8,128)(2,1)S(1)}, u32[]{:S(2)}, u32[]{:S(2)}) collective-permute-start(bf16[512,128]{1,0:T(8,128)(2,1)S(1)} %added.5.refs_1_), channel_id=1, source_target_pairs={{0,8},{4,12},{8,0},{12,4},{16,24},{20,28},{24,16},{28,20},{1,9},{5... | collective-permute-start | bytes 393224 | tf_op jit(solution)/shard_map/ppermute | solution.py:338
  146.4 11.9 %collective-permute-start.20 = (bf16[1024,128]{1,0:T(8,128)(2,1)S(1)}, bf16[1024,128]{1,0:T(8,128)(2,1)S(1)}, u32[]{:S(2)}, u32[]{:S(2)}) collective-permute-start(bf16[1024,128]{1,0:T(8,128)(2,1)S(1)} %joined.2.refs_1_), channel_id=1, source_target_pairs={{0,4},{4,0},{8,12},{12,8},{16,20},{20,16},{24,28},{28,24},{1,5},{5... | collective-permute-start | bytes 786440 | tf_op jit(solution)/shard_map/ppermute | solution.py:338
  (3 other events, 5.8 us)

commit v12 on v11

--- a/solution.py
+++ b/solution.py
@@ -280,27 +280,32 @@
         out_ref[:, pl.ds(place, piece)] = total.astype(BF16)
 
 
-def grad_weight_of(me, arrays, places, cots):
+def grad_weight_of(me, arrays, places, cots, earlier):
     channels = arrays[0].shape[1]
     slots, parts = len(places), len(cots)
     pieces = [array for pair in cots for array, unused in pair]
     half = cots[0][0][0].shape[0]
     tile = 256
     width = 2 * half * channels // (slots * sum(count for unused, count in places[0])) * parts
+    steps = channels // tile // 2
+    first = steps * len(earlier)
+    count = 1 + len(arrays) + len(pieces)
     return pl.pallas_call(
-        functools.partial(weight_kernel, places, parts),
+        ignoring(functools.partial(weight_kernel, places, parts), len(earlier), count),
         grid_spec=pltpu.PrefetchScalarGridSpec(
             num_scalar_prefetch=1,
-            grid=(channels // tile,),
-            in_specs=[pl.BlockSpec((array.shape[0], tile), lambda i, me: (0, i)) for array in arrays]
-            + [pl.BlockSpec((half, channels), lambda i, me, at=at: (at, 0)) for pair in cots for unused, at in pair],
-            out_specs=pl.BlockSpec((tile, width), lambda i, me: (i, 0)),
+            grid=(steps,),
+            in_specs=[pl.BlockSpec((array.shape[0], tile), lambda i, me: (0, first + i)) for array in arrays]
+            + [pl.BlockSpec((half, channels), lambda i, me, at=at: (at, 0)) for pair in cots for unused, at in pair]
+            + [pl.BlockSpec(memory_space=pl.ANY)] * len(earlier),
+            out_specs=pl.BlockSpec((tile, width), lambda i, me: (first + i, 0)),
         ),
         out_shape=jax.ShapeDtypeStruct((channels, width), BF16),
+        input_output_aliases={count: 0} if earlier else {},
         compiler_params=pltpu.CompilerParams(vmem_limit_bytes=VMEM_BYTES),
         cost_estimate=estimate(2),
         name="grad_weight",
-    )(me, *arrays, *pieces)
+    )(me, *arrays, *pieces, *earlier)
 
 
 def narrow_grad_weight(me, arrays, places, cots):
@@ -386,15 +391,14 @@
     return jnp.where(mine, high, low), jnp.where(mine, low, high)
 
 
-def summed(me, partial, gates, join_gate):
+def summed(me, partial, gates):
     bits = bits_of(lax.axis_size("ctx"))
     sums, send = split(me, partial, bits[0])
     for step, bit in enumerate(bits):
         came = swap(send if step < 2 else sums, "ctx", bit)
         sums, *send = added(me, sums, came, bits[1] if step == 0 else 0, gates[step] if step < len(gates) else ())
         send = send[0] if send else None
-    sums = joined(me, sums, swap(sums, "ctx", bits[1]), bits[1], BF16, join_gate)
-    return sums, swap(sums, "ctx", bits[0]), bits[0]
+    return sums, swap(sums, "ctx", bits[1]), bits[:2]
 
 
 def joined_kernel(bit, me_ref, own_ref, other_ref, out_ref):
@@ -487,15 +491,16 @@
     places.insert(1, [(0, half), (0, half)])
 
     early = 2 + 2 * min(1, turns - 1)
-    cols = [gather_of_chips(jnp.concatenate(part, axis=0)) for part in (brought[:early], brought[early:])]
+    first = held_until([jnp.concatenate(brought[:early], axis=0)], arrived[1])[0]
+    cols = [gather_of_chips(part) for part in (first, jnp.concatenate(brought[early:], axis=0))]
 
     terms = {}
     for off in offs[:-1]:
         *sums, terms[off] = weight_pass(me, out_weight, off, gated, cots[off], sums)
-    terms[1] = weight_pass(me, out_weight, 1, gated, after=sums)[0]
+    from_core = [swap(weight_pass(me, out_weight, 1, gated, after=sums)[0], "chan", 1)]
     grad_query, grad_filtered, terms[offs[-1]] = weight_pass(
         me, out_weight, offs[-1], gated, cots[offs[-1]], sums, [query_proj, filtered],
-        arrived[0] + [terms[1]],
+        arrived[0] + from_core,
     )
     following = lax.ppermute(grad_filtered, "ctx", [(i + 1, i) for i in range(n_ctx - 1)])
 
@@ -507,15 +512,10 @@
         "tap_grad",
     )[0]
 
-    for off in [off for off in sorted(terms) if off > 1 and off % 2]:
-        terms[off ^ 1] = terms[off ^ 1] + swap(terms.pop(off), "chan", 1).astype(F32)
-    terms[0] = weight_pass(me, out_weight, 0, gated, after=arrived[1] + [tap_grad])[0]
-    last_part = terms[0]
-    terms[0] = terms[0] + swap(terms.pop(1), "chan", 1).astype(F32)
-    for bit in bits_of(n_chan)[1:]:
-        for off in [off for off in sorted(terms, reverse=True) if off & bit]:
-            terms[off ^ bit] = terms[off ^ bit] + swap(terms.pop(off).astype(BF16), "chan", bit).astype(F32)
-    mixed = terms[0].astype(BF16)
+    for off in [off for off in sorted(terms) if off % 2]:
+        from_core.append(swap(terms.pop(off), "chan", 1))
+        terms[off ^ 1] = terms[off ^ 1] + from_core[-1].astype(F32)
+    terms = dict(zip(terms, held_until(terms.values(), arrived[1])))
 
     grad_key, grad_value = by_channel(
         backward_kernel,
@@ -523,24 +523,35 @@
         "ttttcww",
         [("t", BF16), ("t", BF16)],
         "backward_filter",
-        after=[last_part],
+        after=far,
     )
-    own, other, bit = summed(me, tap_grad, [[], arrived[2]], far)
+    terms[0] = weight_pass(me, out_weight, 0, gated, after=from_core[1:] + [cols[0][off] for off in cols[0] if off])[0] + from_core[0].astype(F32)
+    for bit in bits_of(n_chan)[1:]:
+        for off in [off for off in sorted(terms, reverse=True) if off & bit]:
+            terms[off ^ bit] = terms[off ^ bit] + swap(terms.pop(off).astype(BF16), "chan", bit).astype(F32)
+    mixed = terms[0].astype(BF16)
+
+    own, other, bits = summed(me, held_until([tap_grad], arrived[1])[0], [[], far])
 
     evens = [off for off in range(n_chan) if off % 2 == 0]
     wide = piece % 128 == 0 and 2 * early == n_ctx
     columns = {off: [(part[off], 0) for part in cols] for off in evens}
-    crossed = swap(jnp.concatenate([part[off] for off in evens for part in cols], axis=0), "chan", 1)
+    crossed = jnp.concatenate([part[off] for off in evens for part in cols], axis=0)
+    crossed = swap(held_until([crossed], far)[0], "chan", 1)
     if wide:
         for at, off in enumerate(evens):
             columns[off + 1] = [(crossed, 2 * at), (crossed, 2 * at + 1)]
-        grad_weight = grad_weight_of(me, arrays, places, [columns[off] for off in range(n_chan)])
+        columns = [columns[off] for off in range(n_chan)]
+        low_half = grad_weight_of(me, arrays, places, columns, [])
+        grad_weight = grad_weight_of(me, arrays, places, columns, [low_half])
     else:
         for at, off in enumerate(evens):
             columns[off + 1] = [(crossed[at * length : (at + 1) * length], 0)]
         pairs = [[array for array, unused in columns[off]] for off in range(n_chan)]
-        grad_weight = narrow_grad_weight(me, arrays, places, pairs)
-    grad_filters = joined(me, own, held_until([other], [grad_weight])[0], bit, F32, ())
+        low_half = grad_weight = narrow_grad_weight(me, arrays, places, pairs)
+    own = joined(me, own, held_until([other], [low_half])[0], bits[1], BF16, ())
+    other = swap(own, "ctx", bits[0])
+    grad_filters = joined(me, own, held_until([other], [grad_weight])[0], bits[0], F32, ())
     return (mixed, grad_query, grad_key, grad_value, grad_filters, grad_weight)
 
 

time: 160 us -> 156 us (0.975)
  waiting for transfers between devices: 62.4 us -> 48.7 us
  local copies, waits for them, and re-layouts: 0.56 us -> 6.2 us
  Pallas kernels: 63.9 us -> 66.1 us
    ppermute x14, waiting for transfers between devices: 37.1 us -> 18.3 us  [swap(): return lax.ppermute(block, axis, [(i, i ^ bit) for i in range(size)])]
    ppermute x3, waiting for transfers between devices: 0.01 us -> 12.5 us  [per_device(): lax.ppermute(back, 'ctx', behind)]
    ppermute x3, waiting for transfers between devices: 20.8 us -> 14.5 us  [per_device(): lax.ppermute(onto, 'ctx', ahead)]
    unnamed x29 -> x54, local copies, waits for them, and re-layouts: 0.28 us -> 4.93 us
    ppermute x1, waiting for transfers between devices: 4.45 us -> 0.01 us  [per_device(): lax.ppermute(pieces[rows:2 * rows], 'ctx', [(order[i], order[(i + turns)...]
    ppermute x1, waiting for transfers between devices: 0.01 us -> 1.71 us  [per_device(): lax.ppermute(onto[:half], 'ctx', ahead)]
    pallas_call x1 -> x2, Pallas kernels: 8.65 us -> 10.2 us  [grad_weight_of(): pl.pallas_call(ignoring(functools.partial(weight_kernel, places, parts),...]
  transfers between devices with their start and end apart: 25 -> 25, of which waited for: 9 -> 10; matrix products, arithmetic and copies ran while one was open for 1% -> 2% of each run, Pallas kernels for 38% -> 36%
where the time goes in v12:
time: 156 us; the launch traced here: 155 us
  Pallas kernels  66.1 us (42%)
  waiting for transfers between devices  48.7 us (31%)
  starting transfers between devices  29.1 us (19%)
  local copies, waits for them, and re-layouts  6.2 us (4%)
  other arithmetic  3.94 us (3%)
    pallas_call x6, Pallas kernels, weight_pass(): pl.pallas_call(ignoring(body, len(after), 1 + len(arrays)), grid_spec=plt...  40.4 us
    ppermute x14, waiting for transfers between devices, swap(): return lax.ppermute(block, axis, [(i, i ^ bit) for i in range(size)])  18.3 us
    ppermute x3, waiting for transfers between devices, per_device(): lax.ppermute(onto, 'ctx', ahead)  14.5 us
    ppermute x3, waiting for transfers between devices, per_device(): lax.ppermute(back, 'ctx', behind)  12.5 us
    ppermute x14, starting transfers between devices, swap(): return lax.ppermute(block, axis, [(i, i ^ bit) for i in range(size)])  12.1 us
    pallas_call x3, Pallas kernels, by_channel(): pl.pallas_call(ignoring(functools.partial(kernel, length), len(after), le...  10.8 us
    pallas_call x2, Pallas kernels, grad_weight_of(): pl.pallas_call(ignoring(functools.partial(weight_kernel, places, parts),...  10.2 us
    unnamed x54, local copies, waits for them, and re-layouts  4.93 us
  transfers between devices with their start and end apart: 25, of which 10 were waited for; matrix products, arithmetic and copies ran while one was open for 2% of the time, Pallas kernels for 36%

profile of v12, /device:TPU:0, one launch (start us, length us, event | category | flops | bytes accessed | tf_op | source)
XLA Modules:
  0.0 155.1 jit_solution(14759890114935961458)
XLA Ops:
  0.6 1.4 multiply_convert_fusion
  2.0 3.0 %collective-permute-start.2 = (bf16[128,2048]{1,0:T(8,128)(2,1)S(1)}, bf16[128,2048]{1,0:T(8,128)(2,1)S(1)}, u32[]{:S(2)}, u32[]{:S(2)}) collective-permute-start(bf16[128,2048]{1,0:T(8,128)(2,1)S(1)} %copy-done), channel_id=1, source_target_pairs={{0,2},{1,3},{2,0},{3,1},{4,6},{5,7},{6,4},{7,5},{8,10},{9,11},{10,... | collective-permute-start | bytes 1572872 | tf_op jit(solution)/shard_map/ppermute | solution.py:343
  5.0 3.4 %collective-permute-start = (bf16[128,2048]{1,0:T(8,128)(2,1)S(1)}, bf16[128,2048]{1,0:T(8,128)(2,1)S(1)}, u32[]{:S(2)}, u32[]{:S(2)}) collective-permute-start(bf16[128,2048]{1,0:T(8,128)(2,1)S(1)} %multiply_convert_fusion), channel_id=1, source_target_pairs={{0,4},{4,8},{8,12},{12,16},{16,20},{20,24},{24,28},{1,5},{5,9},{9,... | collective-permute-start | bytes 1572872 | tf_op jit(solution)/shard_map/ppermute | solution.py:438
  8.6 6.2 %grad_gated_part.2.refs_3_ = f32[2048,128]{1,0:T(8,128)S(1)} custom-call(s32[2]{0:T(128)S(1)} %pad_add_fusion.refs_0_, bf16[2048,8192]{1,0:T(8,128)(2,1)} %refs_1_.16, bf16[128,2048]{1,0:T(8,128)(2,1)S(1)} %copy-done), custom_call_target="tpu_custom_call" | custom-call | flops 3000000000 | tf_op jit(solution)/shard_map/grad_gated_part/pallas_call | solution.py:190
  14.9 2.1 %collective-permute-done.2.refs_3_.refs_4_ = bf16[128,2048]{1,0:T(8,128)(2,1)S(1)} collective-permute-done((bf16[128,2048]{1,0:T(8,128)(2,1)S(1)}, bf16[128,2048]{1,0:T(8,128)(2,1)S(1)}, u32[]{:S(2)}, u32[]{:S(2)}) %collective-permute-start.2) | collective-permute-done | bytes 524320 | tf_op jit(solution)/shard_map/ppermute | solution.py:343
  17.0 6.2 %grad_gated_part.3.refs_7_.refs_4_.refs_6_ = f32[2048,128]{1,0:T(8,128)S(1)} custom-call(s32[2]{0:T(128)S(1)} %pad_add_fusion.refs_0_, bf16[2048,8192]{1,0:T(8,128)(2,1)} %refs_1_.16, bf16[128,2048]{1,0:T(8,128)(2,1)S(1)} %collective-permute-done.1.refs_2_.refs_3_, f32[2048,128]{1,0:T(8,128)S(1)} %grad_gated_part.2.refs_3_), custom_call_target="tpu_custom_call" | custom-call | flops 3000000000 | tf_op jit(solution)/shard_map/grad_gated_part/pallas_call | solution.py:190
  23.3 3.3 %forward_filter.1 = (bf16[128,2048]{1,0:T(8,128)(2,1)S(1)}, f32[128,2048]{1,0:T(8,128)S(1)}) custom-call(bf16[128,2048]{1,0:T(8,128)(2,1)S(1)} %copy-done.12, bf16[128,2048]{1,0:T(8,128)(2,1)S(1)} %copy-done.8, bf16[128,2048]{1,0:T(8,128)(2,1)S(1)} %copy-done.10, bf16[128,2048]{1,0:T(8,128)(2,1)S(1)} %collective-permute-done.refs_3_.refs_2_, ...), custom_call_target="tpu_custom_call" | custom-call | flops 3000000000 | tf_op jit(solution)/shard_map/forward_filter/pallas_call | solution.py:107
  28.5 1.3 pad_maximum_fusion.1
  29.8 1.8 %collective-permute-start.5 = (bf16[176,2048]{1,0:T(8,128)(2,1)}, bf16[176,2048]{1,0:T(8,128)(2,1)S(1)}, u32[]{:S(2)}, u32[]{:S(2)}) collective-permute-start(bf16[176,2048]{1,0:T(8,128)(2,1)} %get-tuple-element.58), channel_id=1, source_target_pairs={{8,0},{16,8},{24,16},{28,24},{20,28},{12,20},{4,12},{0,4},{9,1},{1... | collective-permute-start | bytes 2162696 | tf_op jit(solution)/shard_map/ppermute | solution.py:482
  31.8 7.4 %grads_and_mixed.2 = (f32[2048,128]{1,0:T(8,128)S(1)}, f32[128,2048]{1,0:T(8,128)S(1)}) custom-call(s32[2]{0:T(128)S(1)} %pad_add_fusion.refs_0_, bf16[2048,8192]{1,0:T(8,128)(2,1)} %refs_1_.16, bf16[128,2048]{1,0:T(8,128)(2,1)S(1)} %get-tuple-element.28.refs_2_.refs_1_, bf16[128,2048]{1,0:T(8,128)(2,1)S(1)} %collective-permute-done.2.refs_3_.refs_4_, ...), custom_call_target="tpu_custom_call" | custom-call | flops 500000000 | tf_op jit(solution)/shard_map/grads_and_mixed/pallas_call | solution.py:190
  39.2 6.5 %mixed_part.2 = bf16[128,2048]{1,0:T(8,128)(2,1)} custom-call(s32[2]{0:T(128)S(1)} %pad_add_fusion.refs_0_, bf16[2048,8192]{1,0:T(8,128)(2,1)} %refs_1_.16, bf16[128,2048]{1,0:T(8,128)(2,1)S(1)} %get-tuple-element.28.refs_2_.refs_1_, f32[2048,128]{1,0:T(8,128)S(1)} %get-tuple-element.30.refs_3_.refs_4_), custom_call_target="tpu_custom_call" | custom-call | flops 500000000 | tf_op jit(solution)/shard_map/mixed_part/pallas_call | solution.py:190
  45.8 2.1 %collective-permute-done.6.refs_9_ = bf16[128,2048]{1,0:T(8,128)(2,1)S(1)} collective-permute-done((bf16[128,2048]{1,0:T(8,128)(2,1)}, bf16[128,2048]{1,0:T(8,128)(2,1)S(1)}, u32[]{:S(2)}, u32[]{:S(2)}) %collective-permute-start.6) | collective-permute-done | bytes 524320 | tf_op jit(solution)/shard_map/ppermute | solution.py:343
  48.6 1.4 collective-permute-done.4.refs_7_.refs_4_
  53.4 8.3 %grads_and_mixed.3 = (bf16[128,2048]{1,0:T(8,128)(2,1)}, bf16[128,2048]{1,0:T(8,128)(2,1)S(1)}, bf16[128,2048]{1,0:T(8,128)(2,1)S(1)}) custom-call(s32[2]{0:T(128)S(1)} %pad_add_fusion.refs_0_, bf16[2048,8192]{1,0:T(8,128)(2,1)} %refs_1_.16, bf16[128,2048]{1,0:T(8,128)(2,1)S(1)} %get-tuple-element.28.refs_2_.refs_1_, bf16[128,2048]{1,0:T(8,128)(2,1)S(1)} %copy-done.3, ...), custom_call_target="tpu_custom_call" | custom-call | flops 500000000 | tf_op jit(solution)/shard_map/grads_and_mixed/pallas_call | solution.py:190
  62.8 3.6 %collective-permute-start.8 = (bf16[16,2048]{1,0:T(8,128)(2,1)S(1)}, bf16[16,2048]{1,0:T(8,128)(2,1)S(1)}, u32[]{:S(2)}, u32[]{:S(2)}) collective-permute-start(bf16[16,2048]{1,0:T(8,128)(2,1)S(1)} %get-tuple-element.57), channel_id=1, source_target_pairs={{0,28},{8,20},{16,12},{24,4},{28,0},{20,8},{12,16},{4,24},{1,29},{... | collective-permute-start | bytes 196616 | tf_op jit(solution)/shard_map/ppermute | solution.py:474
  67.0 1.6 %collective-permute-start.9 = (bf16[160,2048]{1,0:T(8,128)(2,1)S(1)}, bf16[160,2048]{1,0:T(8,128)(2,1)S(1)}, u32[]{:S(2)}, u32[]{:S(2)}) collective-permute-start(bf16[160,2048]{1,0:T(8,128)(2,1)S(1)} %slice.82), channel_id=1, source_target_pairs={{0,8},{8,16},{16,24},{24,28},{28,20},{20,12},{12,4},{4,0},{1,9},{9... | collective-permute-start | bytes 1966088 | tf_op jit(solution)/shard_map/ppermute | solution.py:482
  68.7 3.5 %tap_grad.1 = bf16[2048,128]{1,0:T(8,128)(2,1)S(1)} custom-call(bf16[128,2048]{1,0:T(8,128)(2,1)S(1)} %copy-done.9, bf16[128,2048]{1,0:T(8,128)(2,1)S(1)} %copy-done.11, bf16[128,2048]{1,0:T(8,128)(2,1)S(1)} %copy-done.18, bf16[128,2048]{1,0:T(8,128)(2,1)S(1)} %get-tuple-element.37.refs_2_.refs_3_, bf16[2,256,256]{2,1,0:T(8,128)(2,1)S(1)} %copy-done.20, ...), custom_call_target="tpu_custom_call" | custom-call | flops 3000000000 | tf_op jit(solution)/shard_map/tap_grad/pallas_call | solution.py:107
  72.4 11.8 %collective-permute-done.10.refs_7_ = bf16[160,2048]{1,0:T(8,128)(2,1)S(1)} collective-permute-done((bf16[160,2048]{1,0:T(8,128)(2,1)S(1)}, bf16[160,2048]{1,0:T(8,128)(2,1)S(1)}, u32[]{:S(2)}, u32[]{:S(2)}) %collective-permute-start.10) | collective-permute-done | bytes 655392 | tf_op jit(solution)/shard_map/ppermute | solution.py:482
  84.2 1.5 collective-permute-start.11
  87.9 13.1 %collective-permute-done.14.refs_8_ = bf16[144,2048]{1,0:T(8,128)(2,1)S(1)} collective-permute-done((bf16[144,2048]{1,0:T(8,128)(2,1)S(1)}, bf16[144,2048]{1,0:T(8,128)(2,1)S(1)}, u32[]{:S(2)}, u32[]{:S(2)}) %collective-permute-start.14) | collective-permute-done | bytes 589856 | tf_op jit(solution)/shard_map/ppermute | solution.py:482
  102.6 1.5 collective-permute-start.12
  106.3 4.1 %collective-permute-done.22.refs_15_ = bf16[64,2048]{1,0:T(8,128)(2,1)S(1)} collective-permute-done((bf16[64,2048]{1,0:T(8,128)(2,1)S(1)}, bf16[64,2048]{1,0:T(8,128)(2,1)S(1)}, u32[]{:S(2)}, u32[]{:S(2)}) %collective-permute-start.22) | collective-permute-done | bytes 262176 | tf_op jit(solution)/shard_map/ppermute | solution.py:343
  110.4 1.5 collective-permute-done.17.refs_8_.refs_4_.refs_3_
  112.0 1.7 %collective-permute-done.15.refs_7_.refs_3_.refs_2_ = bf16[64,2048]{1,0:T(8,128)(2,1)S(1)} collective-permute-done((bf16[64,2048]{1,0:T(8,128)(2,1)S(1)}, bf16[64,2048]{1,0:T(8,128)(2,1)S(1)}, u32[]{:S(2)}, u32[]{:S(2)}) %collective-permute-start.15) | collective-permute-done | bytes 262176 | tf_op jit(solution)/shard_map/ppermute | solution.py:489
  114.4 1.5 collective-permute-start.13
  115.9 5.7 %mixed_part.3 = f32[128,2048]{1,0:T(8,128)S(1)} custom-call(s32[2]{0:T(128)S(1)} %pad_add_fusion.refs_0_, bf16[2048,8192]{1,0:T(8,128)(2,1)} %refs_1_.16, bf16[128,2048]{1,0:T(8,128)(2,1)S(1)} %get-tuple-element.28.refs_2_.refs_1_, bf16[128,2048]{1,0:T(8,128)(2,1)S(1)} %collective-permute-done.7.refs_3_, ...), custom_call_target="tpu_custom_call" | custom-call | flops 500000000 | tf_op jit(solution)/shard_map/mixed_part/pallas_call | solution.py:190
  122.3 4.4 %collective-permute-start.20 = (bf16[512,128]{1,0:T(8,128)(2,1)S(1)}, bf16[512,128]{1,0:T(8,128)(2,1)S(1)}, u32[]{:S(2)}, u32[]{:S(2)}) collective-permute-start(bf16[512,128]{1,0:T(8,128)(2,1)S(1)} %added.4.refs_1_), channel_id=1, source_target_pairs={{0,16},{4,20},{8,24},{12,28},{16,0},{20,4},{24,8},{28,12},{1,17},{... | collective-permute-start | bytes 393224 | tf_op jit(solution)/shard_map/ppermute | solution.py:343
  127.6 10.0 %collective-permute-done.20.refs_2_ = bf16[512,128]{1,0:T(8,128)(2,1)S(1)} collective-permute-done((bf16[512,128]{1,0:T(8,128)(2,1)S(1)}, bf16[512,128]{1,0:T(8,128)(2,1)S(1)}, u32[]{:S(2)}, u32[]{:S(2)}) %collective-permute-start.20) | collective-permute-done | bytes 131104 | tf_op jit(solution)/shard_map/ppermute | solution.py:343
  138.3 5.1 %grad_weight.2.refs_18_ = bf16[2048,1024]{1,0:T(8,128)(2,1)} custom-call(s32[2]{0:T(128)S(1)} %pad_add_fusion.refs_0_, bf16[128,2048]{1,0:T(8,128)(2,1)S(1)} %get-tuple-element.28.refs_2_.refs_1_, bf16[64,2048]{1,0:T(8,128)(2,1)S(1)} %collective-permute-done.15.refs_7_.refs_3_.refs_2_, bf16[64,2048]{1,0:T(8,128)(2,1)S(1)} %collective-permute-done.17.refs_8_.refs_4_.refs_3_, ...), custom_call_target="tpu_custom_call" | custom-call | flops 2000000000 | tf_op jit(solution)/shard_map/grad_weight/pallas_call | solution.py:293
  144.5 3.9 %backward_filter.1 = (bf16[128,2048]{1,0:T(8,128)(2,1)}, bf16[128,2048]{1,0:T(8,128)(2,1)}) custom-call(bf16[128,2048]{1,0:T(8,128)(2,1)S(1)} %copy-done.9, bf16[128,2048]{1,0:T(8,128)(2,1)S(1)} %copy-done.11, bf16[128,2048]{1,0:T(8,128)(2,1)S(1)} %get-tuple-element.37.refs_2_.refs_3_, bf16[128,2048]{1,0:T(8,128)(2,1)S(1)} %collective-permute-done.13.refs_3_, ...), custom_call_target="tpu_custom_call" | custom-call | flops 3000000000 | tf_op jit(solution)/shard_map/backward_filter/pallas_call | solution.py:107
  148.4 5.1 %grad_weight.3 = bf16[2048,1024]{1,0:T(8,128)(2,1)} custom-call(s32[2]{0:T(128)S(1)} %pad_add_fusion.refs_0_, bf16[128,2048]{1,0:T(8,128)(2,1)S(1)} %get-tuple-element.28.refs_2_.refs_1_, bf16[64,2048]{1,0:T(8,128)(2,1)S(1)} %collective-permute-done.15.refs_7_.refs_3_.refs_2_, ...), custom_call_target="tpu_custom_call", output_to_operand_aliasing={{}: (18, {})} | custom-call | flops 2000000000 | tf_op jit(solution)/shard_map/grad_weight/pallas_call | solution.py:293
  153.5 1.6 %joined.3 = f32[2048,128]{1,0:T(8,128)} custom-call(s32[2]{0:T(128)S(1)} %pad_add_fusion.refs_0_, bf16[1024,128]{1,0:T(8,128)(2,1)S(1)} %joined.2.refs_1_, bf16[1024,128]{1,0:T(8,128)(2,1)S(1)} %collective-permute-done.24.refs_2_), custom_call_target="tpu_custom_call" | custom-call | flops 500000000 | tf_op jit(solution)/shard_map/joined/pallas_call | solution.py:414
  (108 shorter events, 18.0 us)
Async XLA Ops:
  2.0 14.9 %collective-permute-start.2 = (bf16[128,2048]{1,0:T(8,128)(2,1)S(1)}, bf16[128,2048]{1,0:T(8,128)(2,1)S(1)}, u32[]{:S(2)}, u32[]{:S(2)}) collective-permute-start(bf16[128,2048]{1,0:T(8,128)(2,1)S(1)} %copy-done), channel_id=1, source_target_pairs={{0,2},{1,3},{2,0},{3,1},{4,6},{5,7},{6,4},{7,5},{8,10},{9,11},{10,... | collective-permute-start | bytes 1572872 | tf_op jit(solution)/shard_map/ppermute | solution.py:343
  5.0 11.9 %collective-permute-start.1 = (bf16[128,2048]{1,0:T(8,128)(2,1)S(1)}, bf16[128,2048]{1,0:T(8,128)(2,1)S(1)}, u32[]{:S(2)}, u32[]{:S(2)}) collective-permute-start(bf16[128,2048]{1,0:T(8,128)(2,1)S(1)} %copy-done), channel_id=1, source_target_pairs={{0,1},{1,0},{2,3},{3,2},{4,5},{5,4},{6,7},{7,6},{8,9},{9,8},{10,11... | collective-permute-start | bytes 1572872 | tf_op jit(solution)/shard_map/ppermute | solution.py:343
  5.0 18.2 %collective-permute-start = (bf16[128,2048]{1,0:T(8,128)(2,1)S(1)}, bf16[128,2048]{1,0:T(8,128)(2,1)S(1)}, u32[]{:S(2)}, u32[]{:S(2)}) collective-permute-start(bf16[128,2048]{1,0:T(8,128)(2,1)S(1)} %multiply_convert_fusion), channel_id=1, source_target_pairs={{0,4},{4,8},{8,12},{12,16},{16,20},{20,24},{24,28},{1,5},{5,9},{9,... | collective-permute-start | bytes 1572872 | tf_op jit(solution)/shard_map/ppermute | solution.py:438
  14.8 8.4 %copy-start.8 = (bf16[128,2048]{1,0:T(8,128)(2,1)S(1)}, bf16[128,2048]{1,0:T(8,128)(2,1)}, u32[]{:S(2)}) copy-start(bf16[128,2048]{1,0:T(8,128)(2,1)} %refs_0_.5) | copy-start | bytes 1572868
  14.8 8.4 %copy-start.10 = (bf16[128,2048]{1,0:T(8,128)(2,1)S(1)}, bf16[128,2048]{1,0:T(8,128)(2,1)}, u32[]{:S(2)}) copy-start(bf16[128,2048]{1,0:T(8,128)(2,1)} %refs_1_.18) | copy-start | bytes 1572868
  14.8 8.4 %copy-start.12 = (bf16[128,2048]{1,0:T(8,128)(2,1)S(1)}, bf16[128,2048]{1,0:T(8,128)(2,1)}, u32[]{:S(2)}) copy-start(bf16[128,2048]{1,0:T(8,128)(2,1)} %refs_5_.4) | copy-start | bytes 1572868
  14.9 8.4 %copy-start.15 = (bf16[2048,128]{1,0:T(8,128)(2,1)S(1)}, bf16[2048,128]{1,0:T(8,128)(2,1)}, u32[]{:S(2)}) copy-start(bf16[2048,128]{1,0:T(8,128)(2,1)} %refs_4_.4) | copy-start | bytes 1572868
  14.9 8.4 %copy-start.19 = (bf16[2,256,256]{2,1,0:T(8,128)(2,1)S(1)}, bf16[2,256,256]{2,1,0:T(8,128)(2,1)}, u32[]{:S(2)}) copy-start(bf16[2,256,256]{2,1,0:T(8,128)(2,1)} %constant.23.clone.refs_5_.refs_4_) | copy-start | bytes 786436
  14.9 8.4 %copy-start.23 = (bf16[2,128,256]{2,1,0:T(8,128)(2,1)S(1)}, bf16[2,128,256]{2,1,0:T(8,128)(2,1)}, u32[]{:S(2)}) copy-start(bf16[2,128,256]{2,1,0:T(8,128)(2,1)} %constant.24.clone.refs_6_) | copy-start | bytes 393220
  17.0 10.7 %collective-permute-start.3 = (bf16[128,2048]{1,0:T(8,128)(2,1)S(1)}, bf16[128,2048]{1,0:T(8,128)(2,1)S(1)}, u32[]{:S(2)}, u32[]{:S(2)}) collective-permute-start(bf16[128,2048]{1,0:T(8,128)(2,1)S(1)} %collective-permute-done.2.refs_3_.refs_4_), channel_id=1, source_target_pairs={{0,1},{1,0},{2,3},{3,2},{4,5},{5,4},{6,7},{7,6},{8,9},{9,8},{10,11... | collective-permute-start | bytes 1572872 | tf_op jit(solution)/shard_map/ppermute | solution.py:343
  29.8 18.8 %collective-permute-start.5 = (bf16[176,2048]{1,0:T(8,128)(2,1)}, bf16[176,2048]{1,0:T(8,128)(2,1)S(1)}, u32[]{:S(2)}, u32[]{:S(2)}) collective-permute-start(bf16[176,2048]{1,0:T(8,128)(2,1)} %get-tuple-element.58), channel_id=1, source_target_pairs={{8,0},{16,8},{24,16},{28,24},{20,28},{12,20},{4,12},{0,4},{9,1},{1... | collective-permute-start | bytes 2162696 | tf_op jit(solution)/shard_map/ppermute | solution.py:482
  31.6 18.5 %collective-permute-start.4 = (bf16[176,2048]{1,0:T(8,128)(2,1)}, bf16[176,2048]{1,0:T(8,128)(2,1)S(1)}, u32[]{:S(2)}, u32[]{:S(2)}) collective-permute-start(bf16[176,2048]{1,0:T(8,128)(2,1)} %get-tuple-element.59), channel_id=1, source_target_pairs={{0,8},{8,16},{16,24},{24,28},{28,20},{20,12},{12,4},{4,0},{1,9},{9... | collective-permute-start | bytes 2162696 | tf_op jit(solution)/shard_map/ppermute | solution.py:482
  45.8 2.1 %collective-permute-start.6 = (bf16[128,2048]{1,0:T(8,128)(2,1)}, bf16[128,2048]{1,0:T(8,128)(2,1)S(1)}, u32[]{:S(2)}, u32[]{:S(2)}) collective-permute-start(bf16[128,2048]{1,0:T(8,128)(2,1)} %mixed_part.2), channel_id=1, source_target_pairs={{0,1},{1,0},{2,3},{3,2},{4,5},{5,4},{6,7},{7,6},{8,9},{9,8},{10,11... | collective-permute-start | bytes 1572872 | tf_op jit(solution)/shard_map/ppermute | solution.py:343
  61.7 7.0 %copy-start.20 = (bf16[2,256,256]{2,1,0:T(8,128)(2,1)S(1)}, bf16[2,256,256]{2,1,0:T(8,128)(2,1)}, u32[]{:S(2)}) copy-start(bf16[2,256,256]{2,1,0:T(8,128)(2,1)} %constant.23.clone.refs_5_.refs_4_) | copy-start | bytes 786436
  61.7 10.6 %collective-permute-start.7 = (bf16[128,2048]{1,0:T(8,128)(2,1)S(1)}, bf16[128,2048]{1,0:T(8,128)(2,1)S(1)}, u32[]{:S(2)}, u32[]{:S(2)}) collective-permute-start(bf16[128,2048]{1,0:T(8,128)(2,1)S(1)} %get-tuple-element.32), channel_id=1, source_target_pairs={{0,1},{1,0},{2,3},{3,2},{4,5},{5,4},{6,7},{7,6},{8,9},{9,8},{10,11... | collective-permute-start | bytes 1572872 | tf_op jit(solution)/shard_map/ppermute | solution.py:343
  62.8 9.4 %collective-permute-start.8 = (bf16[16,2048]{1,0:T(8,128)(2,1)S(1)}, bf16[16,2048]{1,0:T(8,128)(2,1)S(1)}, u32[]{:S(2)}, u32[]{:S(2)}) collective-permute-start(bf16[16,2048]{1,0:T(8,128)(2,1)S(1)} %get-tuple-element.57), channel_id=1, source_target_pairs={{0,28},{8,20},{16,12},{24,4},{28,0},{20,8},{12,16},{4,24},{1,29},{... | collective-permute-start | bytes 196616 | tf_op jit(solution)/shard_map/ppermute | solution.py:474
  66.5 17.7 %collective-permute-start.10 = (bf16[160,2048]{1,0:T(8,128)(2,1)S(1)}, bf16[160,2048]{1,0:T(8,128)(2,1)S(1)}, u32[]{:S(2)}, u32[]{:S(2)}) collective-permute-start(bf16[160,2048]{1,0:T(8,128)(2,1)S(1)} %slice.83), channel_id=1, source_target_pairs={{8,0},{16,8},{24,16},{28,24},{20,28},{12,20},{4,12},{0,4},{9,1},{1... | collective-permute-start | bytes 1966088 | tf_op jit(solution)/shard_map/ppermute | solution.py:482
  67.0 17.2 %collective-permute-start.9 = (bf16[160,2048]{1,0:T(8,128)(2,1)S(1)}, bf16[160,2048]{1,0:T(8,128)(2,1)S(1)}, u32[]{:S(2)}, u32[]{:S(2)}) collective-permute-start(bf16[160,2048]{1,0:T(8,128)(2,1)S(1)} %slice.82), channel_id=1, source_target_pairs={{0,8},{8,16},{16,24},{24,28},{28,20},{20,12},{12,4},{4,0},{1,9},{9... | collective-permute-start | bytes 1966088 | tf_op jit(solution)/shard_map/ppermute | solution.py:482
  84.2 21.2 %collective-permute-start.11 = (bf16[64,2048]{1,0:T(8,128)(2,1)S(1)}, bf16[64,2048]{1,0:T(8,128)(2,1)S(1)}, u32[]{:S(2)}, u32[]{:S(2)}) collective-permute-start(bf16[64,2048]{1,0:T(8,128)(2,1)S(1)} %pad_maximum_fusion.2.refs_10_), channel_id=1, source_target_pairs={{0,2},{1,3},{2,0},{3,1},{4,6},{5,7},{6,4},{7,5},{8,10},{9,11},{10,... | collective-permute-start | bytes 786440 | tf_op jit(solution)/shard_map/ppermute | solution.py:343
  85.7 15.3 %collective-permute-start.16 = (bf16[144,2048]{1,0:T(8,128)(2,1)S(1)}, bf16[144,2048]{1,0:T(8,128)(2,1)S(1)}, u32[]{:S(2)}, u32[]{:S(2)}) collective-permute-start(bf16[144,2048]{1,0:T(8,128)(2,1)S(1)} %slice.86), channel_id=1, source_target_pairs={{8,0},{16,8},{24,16},{28,24},{20,28},{12,20},{4,12},{0,4},{9,1},{1... | collective-permute-start | bytes 1769480 | tf_op jit(solution)/shard_map/ppermute | solution.py:482
  86.8 14.3 %collective-permute-start.14 = (bf16[144,2048]{1,0:T(8,128)(2,1)S(1)}, bf16[144,2048]{1,0:T(8,128)(2,1)S(1)}, u32[]{:S(2)}, u32[]{:S(2)}) collective-permute-start(bf16[144,2048]{1,0:T(8,128)(2,1)S(1)} %slice.84), channel_id=1, source_target_pairs={{0,8},{8,16},{16,24},{24,28},{28,20},{20,12},{12,4},{4,0},{1,9},{9... | collective-permute-start | bytes 1769480 | tf_op jit(solution)/shard_map/ppermute | solution.py:482
  101.1 9.3 %collective-permute-start.22 = (bf16[64,2048]{1,0:T(8,128)(2,1)S(1)}, bf16[64,2048]{1,0:T(8,128)(2,1)S(1)}, u32[]{:S(2)}, u32[]{:S(2)}) collective-permute-start(bf16[64,2048]{1,0:T(8,128)(2,1)S(1)} %pad_maximum_fusion.3.refs_11_), channel_id=1, source_target_pairs={{0,2},{1,3},{2,0},{3,1},{4,6},{5,7},{6,4},{7,5},{8,10},{9,11},{10,... | collective-permute-start | bytes 786440 | tf_op jit(solution)/shard_map/ppermute | solution.py:343
  101.8 11.9 %collective-permute-start.18 = (bf16[1024,128]{1,0:T(8,128)(2,1)S(1)}, bf16[1024,128]{1,0:T(8,128)(2,1)S(1)}, u32[]{:S(2)}, u32[]{:S(2)}) collective-permute-start(bf16[1024,128]{1,0:T(8,128)(2,1)S(1)} %get-tuple-element.54), channel_id=1, source_target_pairs={{0,4},{4,0},{8,12},{12,8},{16,20},{20,16},{24,28},{28,24},{1,5},{5... | collective-permute-start | bytes 786440 | tf_op jit(solution)/shard_map/ppermute | solution.py:343
  102.6 24.0 %collective-permute-start.12 = (bf16[128,2048]{1,0:T(8,128)(2,1)S(1)}, bf16[128,2048]{1,0:T(8,128)(2,1)S(1)}, u32[]{:S(2)}, u32[]{:S(2)}) collective-permute-start(bf16[128,2048]{1,0:T(8,128)(2,1)S(1)} %convert_add_fusion), channel_id=1, source_target_pairs={{0,2},{1,3},{2,0},{3,1},{4,6},{5,7},{6,4},{7,5},{8,10},{9,11},{10,... | collective-permute-start | bytes 1572872 | tf_op jit(solution)/shard_map/ppermute | solution.py:343
  104.2 7.8 %collective-permute-start.17 = (bf16[64,2048]{1,0:T(8,128)(2,1)S(1)}, bf16[64,2048]{1,0:T(8,128)(2,1)S(1)}, u32[]{:S(2)}, u32[]{:S(2)}) collective-permute-start(bf16[64,2048]{1,0:T(8,128)(2,1)S(1)} %slice.87), channel_id=1, source_target_pairs={{8,0},{16,8},{24,16},{28,24},{20,28},{12,20},{4,12},{0,4},{9,1},{1... | collective-permute-start | bytes 786440 | tf_op jit(solution)/shard_map/ppermute | solution.py:489
  105.4 8.3 %collective-permute-start.15 = (bf16[64,2048]{1,0:T(8,128)(2,1)S(1)}, bf16[64,2048]{1,0:T(8,128)(2,1)S(1)}, u32[]{:S(2)}, u32[]{:S(2)}) collective-permute-start(bf16[64,2048]{1,0:T(8,128)(2,1)S(1)} %slice.85), channel_id=1, source_target_pairs={{0,8},{8,16},{16,24},{24,28},{28,20},{20,12},{12,4},{4,0},{1,9},{9... | collective-permute-start | bytes 786440 | tf_op jit(solution)/shard_map/ppermute | solution.py:489
  113.7 24.6 %collective-permute-start.23 = (bf16[256,2048]{1,0:T(8,128)(2,1)S(1)}, bf16[256,2048]{1,0:T(8,128)(2,1)S(1)}, u32[]{:S(2)}, u32[]{:S(2)}) collective-permute-start(bf16[256,2048]{1,0:T(8,128)(2,1)S(1)} %constant_dynamic-update-slice_fusion), channel_id=1, source_target_pairs={{0,1},{1,0},{2,3},{3,2},{4,5},{5,4},{6,7},{7,6},{8,9},{9,8},{10,11... | collective-permute-start | bytes 3145736 | tf_op jit(solution)/shard_map/ppermute | solution.py:343
  114.4 7.3 %collective-permute-start.19 = (bf16[512,128]{1,0:T(8,128)(2,1)S(1)}, bf16[512,128]{1,0:T(8,128)(2,1)S(1)}, u32[]{:S(2)}, u32[]{:S(2)}) collective-permute-start(bf16[512,128]{1,0:T(8,128)(2,1)S(1)} %get-tuple-element.42), channel_id=1, source_target_pairs={{0,8},{4,12},{8,0},{12,4},{16,24},{20,28},{24,16},{28,20},{1,9},{5... | collective-permute-start | bytes 393224 | tf_op jit(solution)/shard_map/ppermute | solution.py:343
  114.4 29.7 %collective-permute-start.13 = (bf16[128,2048]{1,0:T(8,128)(2,1)S(1)}, bf16[128,2048]{1,0:T(8,128)(2,1)S(1)}, u32[]{:S(2)}, u32[]{:S(2)}) collective-permute-start(bf16[128,2048]{1,0:T(8,128)(2,1)S(1)} %get-tuple-element.37.refs_2_.refs_3_), channel_id=1, source_target_pairs={{4,0},{8,4},{12,8},{16,12},{20,16},{24,20},{28,24},{5,1},{9,5},{13... | collective-permute-start | bytes 1572872 | tf_op jit(solution)/shard_map/ppermute | solution.py:505
  122.3 15.4 %collective-permute-start.20 = (bf16[512,128]{1,0:T(8,128)(2,1)S(1)}, bf16[512,128]{1,0:T(8,128)(2,1)S(1)}, u32[]{:S(2)}, u32[]{:S(2)}) collective-permute-start(bf16[512,128]{1,0:T(8,128)(2,1)S(1)} %added.4.refs_1_), channel_id=1, source_target_pairs={{0,16},{4,20},{8,24},{12,28},{16,0},{20,4},{24,8},{28,12},{1,17},{... | collective-permute-start | bytes 393224 | tf_op jit(solution)/shard_map/ppermute | solution.py:343
  138.2 5.2 %collective-permute-start.21 = (bf16[512,128]{1,0:T(8,128)(2,1)S(1)}, bf16[512,128]{1,0:T(8,128)(2,1)S(1)}, u32[]{:S(2)}, u32[]{:S(2)}) collective-permute-start(bf16[512,128]{1,0:T(8,128)(2,1)S(1)} %added.5.refs_1_), channel_id=1, source_target_pairs={{0,8},{4,12},{8,0},{12,4},{16,24},{20,28},{24,16},{28,20},{1,9},{5... | collective-permute-start | bytes 393224 | tf_op jit(solution)/shard_map/ppermute | solution.py:343
  144.0 9.5 %collective-permute-start.24 = (bf16[1024,128]{1,0:T(8,128)(2,1)S(1)}, bf16[1024,128]{1,0:T(8,128)(2,1)S(1)}, u32[]{:S(2)}, u32[]{:S(2)}) collective-permute-start(bf16[1024,128]{1,0:T(8,128)(2,1)S(1)} %joined.2.refs_1_), channel_id=1, source_target_pairs={{0,4},{4,0},{8,12},{12,8},{16,20},{20,16},{24,28},{28,24},{1,5},{5... | collective-permute-start | bytes 786440 | tf_op jit(solution)/shard_map/ppermute | solution.py:343
  (17 other events, 55.7 us)

commit v13 on v12

--- a/solution.py
+++ b/solution.py
@@ -391,14 +391,21 @@
     return jnp.where(mine, high, low), jnp.where(mine, low, high)
 
 
-def summed(me, partial, gates):
-    bits = bits_of(lax.axis_size("ctx"))
-    sums, send = split(me, partial, bits[0])
-    for step, bit in enumerate(bits):
-        came = swap(send if step < 2 else sums, "ctx", bit)
-        sums, *send = added(me, sums, came, bits[1] if step == 0 else 0, gates[step] if step < len(gates) else ())
-        send = send[0] if send else None
-    return sums, swap(sums, "ctx", bits[1]), bits[:2]
+class Sum:
+    def __init__(self, me, partial):
+        self.me = me
+        self.bits = bits_of(lax.axis_size("ctx"))
+        self.step = 0
+        self.sums, self.send = split(me, partial, self.bits[0])
+
+    def add(self, after):
+        if self.step == len(self.bits):
+            return []
+        came = swap(self.send if self.step < 2 else self.sums, "ctx", self.bits[self.step])
+        self.sums, *send = added(self.me, self.sums, came, 0 if self.step else self.bits[1], after)
+        self.send = send[0] if send else None
+        self.step += 1
+        return [self.sums]
 
 
 def joined_kernel(bit, me_ref, own_ref, other_ref, out_ref):
@@ -471,51 +478,54 @@
     turns = n_ctx // 2
     rows, piece = length // n_ctx, channels // n_ctx
     span = (turns - 1) * rows
+    ends = [
+        jnp.concatenate([pieces[2 * rows : 2 * rows + span], gated], axis=0),
+        jnp.concatenate([gated, pieces[2 * rows + span :]], axis=0),
+    ]
+    arrays, places, brought = [gated], [[(0, length)]], [pieces[:rows]]
+
+    def passed_on(kernels):
+        onto, back = held_until(ends, kernels)
+        came = [lax.ppermute(onto, "ctx", ahead), lax.ppermute(back, "ctx", behind)]
+        arrays.extend(came)
+        places.extend([[(came[0].shape[0] - length, length)], [(0, length)]])
+        brought.extend([came[0][:rows], came[1][-rows:]])
+        ends[:] = [came[0][rows:], came[1][:-rows]]
+        return came
+
+    landed = passed_on([])
     across = lax.ppermute(
-        pieces[rows : 2 * rows], "ctx", [(order[i], order[(i + turns) % n_ctx]) for i in range(n_ctx)]
+        held_until([pieces[rows : 2 * rows]], [gated])[0],
+        "ctx",
+        [(order[i], order[(i + turns) % n_ctx]) for i in range(n_ctx)],
     )
-    onto = jnp.concatenate([pieces[2 * rows : 2 * rows + span], gated], axis=0)
-    back = jnp.concatenate([gated, pieces[2 * rows + span :]], axis=0)
-    arrays, places = [gated], [[(0, length)]]
-    brought, arrived = [pieces[:rows], across], []
-    for step in range(1, turns):
-        onto, back = lax.ppermute(onto, "ctx", ahead), lax.ppermute(back, "ctx", behind)
-        arrived.append([onto, back])
-        arrays += [onto, back]
-        places += [[(onto.shape[0] - length, length)], [(0, length)]]
-        brought += [onto[:rows], back[-rows:]]
-        onto, back = onto[rows:], back[:-rows]
-    half = length // 2
-    far = [lax.ppermute(onto[:half], "ctx", ahead), lax.ppermute(back[half:], "ctx", behind)]
-    arrays = arrays[:1] + far + arrays[1:]
-    places.insert(1, [(0, half), (0, half)])
-
-    early = 2 + 2 * min(1, turns - 1)
-    first = held_until([jnp.concatenate(brought[:early], axis=0)], arrived[1])[0]
-    cols = [gather_of_chips(part) for part in (first, jnp.concatenate(brought[early:], axis=0))]
+    brought.insert(1, across)
 
     terms = {}
     for off in offs[:-1]:
         *sums, terms[off] = weight_pass(me, out_weight, off, gated, cots[off], sums)
-    from_core = [swap(weight_pass(me, out_weight, 1, gated, after=sums)[0], "chan", 1)]
     grad_query, grad_filtered, terms[offs[-1]] = weight_pass(
-        me, out_weight, offs[-1], gated, cots[offs[-1]], sums, [query_proj, filtered],
-        arrived[0] + from_core,
+        me, out_weight, offs[-1], gated, cots[offs[-1]], sums, [query_proj, filtered]
     )
+    previous, landed = landed, passed_on([grad_filtered])
+
     following = lax.ppermute(grad_filtered, "ctx", [(i + 1, i) for i in range(n_ctx - 1)])
-
     tap_grad = by_channel(
         tap_grad_kernel,
         [key_proj, value_proj, earlier, grad_filtered, forward, lags],
         "ttttww",
         [("c", BF16)],
         "tap_grad",
+        after=previous,
     )[0]
-
+    from_core = []
     for off in [off for off in sorted(terms) if off % 2]:
         from_core.append(swap(terms.pop(off), "chan", 1))
         terms[off ^ 1] = terms[off ^ 1] + from_core[-1].astype(F32)
-    terms = dict(zip(terms, held_until(terms.values(), arrived[1])))
+    mixed_one = weight_pass(me, out_weight, 1, gated, after=[tap_grad])[0]
+    last_part = weight_pass(me, out_weight, 0, gated, after=[mixed_one])[0]
+    tap_sum = Sum(me, held_until([tap_grad], [mixed_one])[0])
+    previous, landed = landed, passed_on([last_part] + tap_sum.add(()))
 
     grad_key, grad_value = by_channel(
         backward_kernel,
@@ -523,15 +533,31 @@
         "ttttcww",
         [("t", BF16), ("t", BF16)],
         "backward_filter",
-        after=far,
+        after=previous + from_core,
     )
-    terms[0] = weight_pass(me, out_weight, 0, gated, after=from_core[1:] + [cols[0][off] for off in cols[0] if off])[0] + from_core[0].astype(F32)
+    terms = dict(zip(terms, held_until(terms.values(), previous)))
+    terms[0] = last_part + swap(mixed_one, "chan", 1).astype(F32)
     for bit in bits_of(n_chan)[1:]:
         for off in [off for off in sorted(terms, reverse=True) if off & bit]:
             terms[off ^ bit] = terms[off ^ bit] + swap(terms.pop(off).astype(BF16), "chan", bit).astype(F32)
     mixed = terms[0].astype(BF16)
-
-    own, other, bits = summed(me, held_until([tap_grad], arrived[1])[0], [[], far])
+    early = 2 + 2 * min(1, turns - 1)
+    first = jnp.concatenate(held_until(brought[:early], previous), axis=0)
+
+    for unused in range(turns - 4):
+        landed = passed_on([grad_key])
+    half = length // 2
+    onto, back = held_until(ends, [following] + tap_sum.add(()))
+    far = [lax.ppermute(onto[:half], "ctx", ahead), lax.ppermute(back[half:], "ctx", behind)]
+    arrays = arrays[:1] + far + arrays[1:]
+    places.insert(1, [(0, half), (0, half)])
+
+    cols = [gather_of_chips(part) for part in (first, jnp.concatenate(brought[early:], axis=0))]
+
+    while tap_sum.add(far):
+        pass
+    own, bits = tap_sum.sums, tap_sum.bits
+    other = swap(own, "ctx", bits[1])
 
     evens = [off for off in range(n_chan) if off % 2 == 0]
     wide = piece % 128 == 0 and 2 * early == n_ctx

time: 156 us -> 154 us (0.987)
  starting transfers between devices: 29.1 us -> 32 us
  local copies, waits for them, and re-layouts: 6.2 us -> 3.7 us
  waiting for transfers between devices: 48.7 us -> 46.8 us
    ppermute x14, waiting for transfers between devices: 18.3 us -> 29.7 us  [swap(): return lax.ppermute(block, axis, [(i, i ^ bit) for i in range(size)])]
    ppermute x7, waiting for transfers between devices: 27.1 us -> 16.5 us  [the longest x6 16.5 us: passed_on(): came = [lax.ppermute(onto, 'ctx', ahead), lax.ppermute(back, 'ctx', behind)]]
    ppermute x7, starting transfers between devices: 9.92 us -> 12.6 us  [the longest x6 6.7 us: passed_on(): came = [lax.ppermute(onto, 'ctx', ahead), lax.ppermute(back, 'ctx', behind)]]
    unnamed x54 -> x63, local copies, waits for them, and re-layouts: 4.93 us -> 2.47 us
    ppermute x1, starting transfers between devices: 1.27 us -> 3.08 us  [per_device(): lax.ppermute(back[half:], 'ctx', behind)]
  transfers between devices with their start and end apart: 25 -> 25, of which waited for: 10 -> 11; matrix products, arithmetic and copies ran while one was open for 2% -> 2% of each run, Pallas kernels for 36% -> 35%
where the time goes in v13:
time: 154 us
  Pallas kernels  65.3 us (42%)
  waiting for transfers between devices  46.8 us (30%)
  starting transfers between devices  32 us (21%)
  other arithmetic  4.75 us (3%)
  local copies, waits for them, and re-layouts  3.7 us (2%)
    pallas_call x6, Pallas kernels, weight_pass(): pl.pallas_call(ignoring(body, len(after), 1 + len(arrays)), grid_spec=plt...  39.7 us
    ppermute x14, waiting for transfers between devices, swap(): return lax.ppermute(block, axis, [(i, i ^ bit) for i in range(size)])  29.7 us
    ppermute x6, waiting for transfers between devices, passed_on(): came = [lax.ppermute(onto, 'ctx', ahead), lax.ppermute(back, 'ctx', behind)]  16.5 us
    ppermute x14, starting transfers between devices, swap(): return lax.ppermute(block, axis, [(i, i ^ bit) for i in range(size)])  11.6 us
    pallas_call x3, Pallas kernels, by_channel(): pl.pallas_call(ignoring(functools.partial(kernel, length), len(after), le...  10.8 us
    pallas_call x2, Pallas kernels, grad_weight_of(): pl.pallas_call(ignoring(functools.partial(weight_kernel, places, parts),...  10 us
    ppermute x6, starting transfers between devices, passed_on(): came = [lax.ppermute(onto, 'ctx', ahead), lax.ppermute(back, 'ctx', behind)]  6.7 us
    ppermute x1, starting transfers between devices, per_device(): lax.ppermute(held_until([pieces[rows:2 * rows]], [gated])[0], 'ctx', [(or...  5.89 us
  transfers between devices with their start and end apart: 25, of which 11 were waited for; matrix products, arithmetic and copies ran while one was open for 2% of the time, Pallas kernels for 35%

profile of v13, /device:TPU:0, one launch (start us, length us, event | category | flops | bytes accessed | tf_op | source)
XLA Modules:
  0.0 153.8 jit_solution(8172035595127241880)
XLA Ops:
  0.6 2.2 %multiply_convert_fusion = bf16[128,2048]{1,0:T(8,128)(2,1)} fusion(bf16[128,2048]{1,0:T(8,128)(2,1)} %refs_1_.18, bf16[128,2048]{1,0:T(8,128)(2,1)} %refs_0_.5), kind=kLoop, calls=%fused_computation.2 | loop fusion | flops 1048576 | bytes 1572864 | tf_op jit(solution)/shard_map/convert_element_type | solution.py:443
  2.8 2.9 %collective-permute-start.2 = (bf16[128,2048]{1,0:T(8,128)(2,1)S(1)}, bf16[128,2048]{1,0:T(8,128)(2,1)S(1)}, u32[]{:S(2)}, u32[]{:S(2)}) collective-permute-start(bf16[128,2048]{1,0:T(8,128)(2,1)S(1)} %copy-done.4), channel_id=1, source_target_pairs={{0,2},{1,3},{2,0},{3,1},{4,6},{5,7},{6,4},{7,5},{8,10},{9,11},{10,... | collective-permute-start | bytes 1572872 | tf_op jit(solution)/shard_map/ppermute | solution.py:343
  5.8 3.4 %collective-permute-start = (bf16[128,2048]{1,0:T(8,128)(2,1)}, bf16[128,2048]{1,0:T(8,128)(2,1)S(1)}, u32[]{:S(2)}, u32[]{:S(2)}) collective-permute-start(bf16[128,2048]{1,0:T(8,128)(2,1)} %multiply_convert_fusion), channel_id=1, source_target_pairs={{0,4},{4,8},{8,12},{12,16},{16,20},{20,24},{24,28},{1,5},{5,9},{9,... | collective-permute-start | bytes 1572872 | tf_op jit(solution)/shard_map/ppermute | solution.py:445
  9.3 6.2 %grad_gated_part.2.refs_3_ = f32[2048,128]{1,0:T(8,128)S(1)} custom-call(s32[2]{0:T(128)S(1)} %pad_add_fusion.refs_0_, bf16[2048,8192]{1,0:T(8,128)(2,1)} %refs_1_.17, bf16[128,2048]{1,0:T(8,128)(2,1)S(1)} %copy-done.4), custom_call_target="tpu_custom_call" | custom-call | flops 3000000000 | tf_op jit(solution)/shard_map/grad_gated_part/pallas_call | solution.py:190
  15.6 2.1 %collective-permute-done.2.refs_3_.refs_4_ = bf16[128,2048]{1,0:T(8,128)(2,1)S(1)} collective-permute-done((bf16[128,2048]{1,0:T(8,128)(2,1)S(1)}, bf16[128,2048]{1,0:T(8,128)(2,1)S(1)}, u32[]{:S(2)}, u32[]{:S(2)}) %collective-permute-start.2) | collective-permute-done | bytes 524320 | tf_op jit(solution)/shard_map/ppermute | solution.py:343
  17.7 6.2 %grad_gated_part.3.refs_7_.refs_4_.refs_6_ = f32[2048,128]{1,0:T(8,128)S(1)} custom-call(s32[2]{0:T(128)S(1)} %pad_add_fusion.refs_0_, bf16[2048,8192]{1,0:T(8,128)(2,1)} %refs_1_.17, bf16[128,2048]{1,0:T(8,128)(2,1)S(1)} %collective-permute-done.1.refs_2_.refs_3_, f32[2048,128]{1,0:T(8,128)S(1)} %grad_gated_part.2.refs_3_), custom_call_target="tpu_custom_call" | custom-call | flops 3000000000 | tf_op jit(solution)/shard_map/grad_gated_part/pallas_call | solution.py:190
  25.8 3.3 %forward_filter.1 = (bf16[128,2048]{1,0:T(8,128)(2,1)S(1)}, f32[128,2048]{1,0:T(8,128)S(1)}) custom-call(bf16[128,2048]{1,0:T(8,128)(2,1)S(1)} %copy-done.10, bf16[128,2048]{1,0:T(8,128)(2,1)S(1)} %copy-done.12, bf16[128,2048]{1,0:T(8,128)(2,1)S(1)} %copy-done.14, bf16[128,2048]{1,0:T(8,128)(2,1)S(1)} %copy-done.20, bf16[2048,128]{1,0:T(8,128)(2,1)S(1)} %copy-done.17, ...), custom_call_target="tpu_custom_call" | custom-call | flops 3000000000 | tf_op jit(solution)/shard_map/forward_filter/pallas_call | solution.py:107
  30.4 1.3 pad_maximum_fusion.1
  31.7 1.8 %collective-permute-start.4 = (bf16[176,2048]{1,0:T(8,128)(2,1)}, bf16[176,2048]{1,0:T(8,128)(2,1)S(1)}, u32[]{:S(2)}, u32[]{:S(2)}) collective-permute-start(bf16[176,2048]{1,0:T(8,128)(2,1)} %get-tuple-element.45), channel_id=1, source_target_pairs={{0,8},{8,16},{16,24},{24,28},{28,20},{20,12},{12,4},{4,0},{1,9},{9... | collective-permute-start | bytes 2162696 | tf_op jit(solution)/shard_map/ppermute | solution.py:489
  33.7 7.5 %grads_and_mixed.2 = (f32[2048,128]{1,0:T(8,128)S(1)}, f32[128,2048]{1,0:T(8,128)S(1)}) custom-call(s32[2]{0:T(128)S(1)} %pad_add_fusion.refs_0_, bf16[2048,8192]{1,0:T(8,128)(2,1)} %refs_1_.17, bf16[128,2048]{1,0:T(8,128)(2,1)S(1)} %get-tuple-element.40.refs_2_.refs_1_, bf16[128,2048]{1,0:T(8,128)(2,1)S(1)} %collective-permute-done.2.refs_3_.refs_4_, ...), custom_call_target="tpu_custom_call" | custom-call | flops 500000000 | tf_op jit(solution)/shard_map/grads_and_mixed/pallas_call | solution.py:190
  41.3 8.3 %grads_and_mixed.3 = (bf16[128,2048]{1,0:T(8,128)(2,1)}, bf16[128,2048]{1,0:T(8,128)(2,1)S(1)}, bf16[128,2048]{1,0:T(8,128)(2,1)S(1)}) custom-call(s32[2]{0:T(128)S(1)} %pad_add_fusion.refs_0_, bf16[2048,8192]{1,0:T(8,128)(2,1)} %refs_1_.17, bf16[128,2048]{1,0:T(8,128)(2,1)S(1)} %get-tuple-element.40.refs_2_.refs_1_, bf16[128,2048]{1,0:T(8,128)(2,1)S(1)} %copy-done.6, ...), custom_call_target="tpu_custom_call" | custom-call | flops 500000000 | tf_op jit(solution)/shard_map/grads_and_mixed/pallas_call | solution.py:190
  50.5 1.5 collective-permute-done.5.refs_7_.refs_5_
  52.0 3.5 %tap_grad.1.refs_3_ = bf16[2048,128]{1,0:T(8,128)(2,1)S(1)} custom-call(bf16[128,2048]{1,0:T(8,128)(2,1)S(1)} %copy-done.13, bf16[128,2048]{1,0:T(8,128)(2,1)S(1)} %copy-done.15, bf16[128,2048]{1,0:T(8,128)(2,1)S(1)} %copy-done.21, bf16[128,2048]{1,0:T(8,128)(2,1)S(1)} %get-tuple-element.44.refs_3_.refs_2_, bf16[2,256,256]{2,1,0:T(8,128)(2,1)S(1)} %copy-done.23, ...), custom_call_target="tpu_custom_call" | custom-call | flops 3000000000 | tf_op jit(solution)/shard_map/tap_grad/pallas_call | solution.py:107
  55.6 5.7 %mixed_part.2.refs_3_ = bf16[128,2048]{1,0:T(8,128)(2,1)S(1)} custom-call(s32[2]{0:T(128)S(1)} %pad_add_fusion.refs_0_, bf16[2048,8192]{1,0:T(8,128)(2,1)} %refs_1_.17, bf16[128,2048]{1,0:T(8,128)(2,1)S(1)} %get-tuple-element.40.refs_2_.refs_1_, bf16[2048,128]{1,0:T(8,128)(2,1)S(1)} %tap_grad.1.refs_3_), custom_call_target="tpu_custom_call" | custom-call | flops 500000000 | tf_op jit(solution)/shard_map/mixed_part/pallas_call | solution.py:190
  61.4 1.6 %collective-permute-start.8 = (bf16[160,2048]{1,0:T(8,128)(2,1)S(1)}, bf16[160,2048]{1,0:T(8,128)(2,1)S(1)}, u32[]{:S(2)}, u32[]{:S(2)}) collective-permute-start(bf16[160,2048]{1,0:T(8,128)(2,1)S(1)} %slice.82), channel_id=1, source_target_pairs={{0,8},{8,16},{16,24},{24,28},{28,20},{20,12},{12,4},{4,0},{1,9},{9... | collective-permute-start | bytes 1966088 | tf_op jit(solution)/shard_map/ppermute | solution.py:489
  66.1 5.9 %collective-permute-start.20 = (bf16[16,2048]{1,0:T(8,128)(2,1)S(1)}, bf16[16,2048]{1,0:T(8,128)(2,1)S(1)}, u32[]{:S(2)}, u32[]{:S(2)}) collective-permute-start(bf16[16,2048]{1,0:T(8,128)(2,1)S(1)} %get-tuple-element.62), channel_id=1, source_target_pairs={{0,28},{8,20},{16,12},{24,4},{28,0},{20,8},{12,16},{4,24},{1,29},{... | collective-permute-start | bytes 196616 | tf_op jit(solution)/shard_map/ppermute | solution.py:497
  72.0 5.7 %mixed_part.3 = f32[128,2048]{1,0:T(8,128)S(1)} custom-call(s32[2]{0:T(128)S(1)} %pad_add_fusion.refs_0_, bf16[2048,8192]{1,0:T(8,128)(2,1)} %refs_1_.17, bf16[128,2048]{1,0:T(8,128)(2,1)S(1)} %get-tuple-element.40.refs_2_.refs_1_, bf16[128,2048]{1,0:T(8,128)(2,1)S(1)} %mixed_part.2.refs_3_), custom_call_target="tpu_custom_call" | custom-call | flops 500000000 | tf_op jit(solution)/shard_map/mixed_part/pallas_call | solution.py:190
  77.7 17.3 %collective-permute-done.12.refs_2_ = bf16[1024,128]{1,0:T(8,128)(2,1)S(1)} collective-permute-done((bf16[1024,128]{1,0:T(8,128)(2,1)S(1)}, bf16[1024,128]{1,0:T(8,128)(2,1)S(1)}, u32[]{:S(2)}, u32[]{:S(2)}) %collective-permute-start.12) | collective-permute-done | bytes 262176 | tf_op jit(solution)/shard_map/ppermute | solution.py:343
  95.9 2.0 %collective-permute-start.15 = (bf16[144,2048]{1,0:T(8,128)(2,1)S(1)}, bf16[144,2048]{1,0:T(8,128)(2,1)S(1)}, u32[]{:S(2)}, u32[]{:S(2)}) collective-permute-start(bf16[144,2048]{1,0:T(8,128)(2,1)S(1)} %slice.84), channel_id=1, source_target_pairs={{0,8},{8,16},{16,24},{24,28},{28,20},{20,12},{12,4},{4,0},{1,9},{9... | collective-permute-start | bytes 1769480 | tf_op jit(solution)/shard_map/ppermute | solution.py:489
  98.7 13.8 %collective-permute-done.15.refs_8_ = bf16[144,2048]{1,0:T(8,128)(2,1)S(1)} collective-permute-done((bf16[144,2048]{1,0:T(8,128)(2,1)S(1)}, bf16[144,2048]{1,0:T(8,128)(2,1)S(1)}, u32[]{:S(2)}, u32[]{:S(2)}) %collective-permute-start.15) | collective-permute-done | bytes 589856 | tf_op jit(solution)/shard_map/ppermute | solution.py:489
  112.5 1.5 collective-permute-start.21
  114.4 1.6 %collective-permute-start.22 = (bf16[64,2048]{1,0:T(8,128)(2,1)S(1)}, bf16[64,2048]{1,0:T(8,128)(2,1)S(1)}, u32[]{:S(2)}, u32[]{:S(2)}) collective-permute-start(bf16[64,2048]{1,0:T(8,128)(2,1)S(1)} %pad_maximum_fusion.2.refs_11_), channel_id=1, source_target_pairs={{0,2},{1,3},{2,0},{3,1},{4,6},{5,7},{6,4},{7,5},{8,10},{9,11},{10,... | collective-permute-start | bytes 786440 | tf_op jit(solution)/shard_map/ppermute | solution.py:343
  116.7 3.1 %collective-permute-start.18 = (bf16[64,2048]{1,0:T(8,128)(2,1)S(1)}, bf16[64,2048]{1,0:T(8,128)(2,1)S(1)}, u32[]{:S(2)}, u32[]{:S(2)}) collective-permute-start(bf16[64,2048]{1,0:T(8,128)(2,1)S(1)} %slice.71), channel_id=1, source_target_pairs={{8,0},{16,8},{24,16},{28,24},{20,28},{12,20},{4,12},{0,4},{9,1},{1... | collective-permute-start | bytes 786440 | tf_op jit(solution)/shard_map/ppermute | solution.py:551
  119.8 1.9 %collective-permute-done.21.refs_14_ = bf16[64,2048]{1,0:T(8,128)(2,1)S(1)} collective-permute-done((bf16[64,2048]{1,0:T(8,128)(2,1)S(1)}, bf16[64,2048]{1,0:T(8,128)(2,1)S(1)}, u32[]{:S(2)}, u32[]{:S(2)}) %collective-permute-start.21) | collective-permute-done | bytes 262176 | tf_op jit(solution)/shard_map/ppermute | solution.py:343
  121.7 4.5 %collective-permute-done.22.refs_15_ = bf16[64,2048]{1,0:T(8,128)(2,1)S(1)} collective-permute-done((bf16[64,2048]{1,0:T(8,128)(2,1)S(1)}, bf16[64,2048]{1,0:T(8,128)(2,1)S(1)}, u32[]{:S(2)}, u32[]{:S(2)}) %collective-permute-start.22) | collective-permute-done | bytes 262176 | tf_op jit(solution)/shard_map/ppermute | solution.py:343
  127.6 1.5 collective-permute-start.10
  129.1 3.9 %backward_filter.1 = (bf16[128,2048]{1,0:T(8,128)(2,1)}, bf16[128,2048]{1,0:T(8,128)(2,1)}) custom-call(bf16[128,2048]{1,0:T(8,128)(2,1)S(1)} %copy-done.13, bf16[128,2048]{1,0:T(8,128)(2,1)S(1)} %copy-done.15, bf16[128,2048]{1,0:T(8,128)(2,1)S(1)} %get-tuple-element.44.refs_3_.refs_2_, bf16[128,2048]{1,0:T(8,128)(2,1)S(1)} %collective-permute-done.11.refs_3_, ...), custom_call_target="tpu_custom_call" | custom-call | flops 3000000000 | tf_op jit(solution)/shard_map/backward_filter/pallas_call | solution.py:107
  133.0 3.7 %collective-permute-done.14.refs_2_ = bf16[512,128]{1,0:T(8,128)(2,1)S(1)} collective-permute-done((bf16[512,128]{1,0:T(8,128)(2,1)S(1)}, bf16[512,128]{1,0:T(8,128)(2,1)S(1)}, u32[]{:S(2)}, u32[]{:S(2)}) %collective-permute-start.14) | collective-permute-done | bytes 131104 | tf_op jit(solution)/shard_map/ppermute | solution.py:343
  137.4 5.0 %grad_weight.2.refs_18_ = bf16[2048,1024]{1,0:T(8,128)(2,1)} custom-call(s32[2]{0:T(128)S(1)} %pad_add_fusion.refs_0_, bf16[128,2048]{1,0:T(8,128)(2,1)S(1)} %get-tuple-element.40.refs_2_.refs_1_, bf16[64,2048]{1,0:T(8,128)(2,1)S(1)} %collective-permute-done.17.refs_3_.refs_2_, bf16[64,2048]{1,0:T(8,128)(2,1)S(1)} %collective-permute-done.18.refs_4_.refs_3_, ...), custom_call_target="tpu_custom_call" | custom-call | flops 2000000000 | tf_op jit(solution)/shard_map/grad_weight/pallas_call | solution.py:293
  143.0 3.0 %collective-permute-start.24 = (bf16[1024,128]{1,0:T(8,128)(2,1)S(1)}, bf16[1024,128]{1,0:T(8,128)(2,1)S(1)}, u32[]{:S(2)}, u32[]{:S(2)}) collective-permute-start(bf16[1024,128]{1,0:T(8,128)(2,1)S(1)} %joined.2.refs_1_), channel_id=1, source_target_pairs={{0,4},{4,0},{8,12},{12,8},{16,20},{20,16},{24,28},{28,24},{1,5},{5... | collective-permute-start | bytes 786440 | tf_op jit(solution)/shard_map/ppermute | solution.py:343
  147.1 5.0 %grad_weight.3 = bf16[2048,1024]{1,0:T(8,128)(2,1)} custom-call(s32[2]{0:T(128)S(1)} %pad_add_fusion.refs_0_, bf16[128,2048]{1,0:T(8,128)(2,1)S(1)} %get-tuple-element.40.refs_2_.refs_1_, bf16[64,2048]{1,0:T(8,128)(2,1)S(1)} %collective-permute-done.17.refs_3_.refs_2_, ...), custom_call_target="tpu_custom_call", output_to_operand_aliasing={{}: (18, {})} | custom-call | flops 2000000000 | tf_op jit(solution)/shard_map/grad_weight/pallas_call | solution.py:293
  152.2 1.6 %joined.3 = f32[2048,128]{1,0:T(8,128)} custom-call(s32[2]{0:T(128)S(1)} %pad_add_fusion.refs_0_, bf16[1024,128]{1,0:T(8,128)(2,1)S(1)} %joined.2.refs_1_, bf16[1024,128]{1,0:T(8,128)(2,1)S(1)} %collective-permute-done.24.refs_2_), custom_call_target="tpu_custom_call" | custom-call | flops 500000000 | tf_op jit(solution)/shard_map/joined/pallas_call | solution.py:421
  (120 shorter events, 13.5 us)
Async XLA Ops:
  2.8 14.9 %collective-permute-start.2 = (bf16[128,2048]{1,0:T(8,128)(2,1)S(1)}, bf16[128,2048]{1,0:T(8,128)(2,1)S(1)}, u32[]{:S(2)}, u32[]{:S(2)}) collective-permute-start(bf16[128,2048]{1,0:T(8,128)(2,1)S(1)} %copy-done.4), channel_id=1, source_target_pairs={{0,2},{1,3},{2,0},{3,1},{4,6},{5,7},{6,4},{7,5},{8,10},{9,11},{10,... | collective-permute-start | bytes 1572872 | tf_op jit(solution)/shard_map/ppermute | solution.py:343
  5.8 11.9 %collective-permute-start.1 = (bf16[128,2048]{1,0:T(8,128)(2,1)S(1)}, bf16[128,2048]{1,0:T(8,128)(2,1)S(1)}, u32[]{:S(2)}, u32[]{:S(2)}) collective-permute-start(bf16[128,2048]{1,0:T(8,128)(2,1)S(1)} %copy-done.4), channel_id=1, source_target_pairs={{0,1},{1,0},{2,3},{3,2},{4,5},{5,4},{6,7},{7,6},{8,9},{9,8},{10,11... | collective-permute-start | bytes 1572872 | tf_op jit(solution)/shard_map/ppermute | solution.py:343
  5.8 18.2 %collective-permute-start = (bf16[128,2048]{1,0:T(8,128)(2,1)}, bf16[128,2048]{1,0:T(8,128)(2,1)S(1)}, u32[]{:S(2)}, u32[]{:S(2)}) collective-permute-start(bf16[128,2048]{1,0:T(8,128)(2,1)} %multiply_convert_fusion), channel_id=1, source_target_pairs={{0,4},{4,8},{8,12},{12,16},{16,20},{20,24},{24,28},{1,5},{5,9},{9,... | collective-permute-start | bytes 1572872 | tf_op jit(solution)/shard_map/ppermute | solution.py:445
  17.7 11.5 %collective-permute-start.3 = (bf16[128,2048]{1,0:T(8,128)(2,1)S(1)}, bf16[128,2048]{1,0:T(8,128)(2,1)S(1)}, u32[]{:S(2)}, u32[]{:S(2)}) collective-permute-start(bf16[128,2048]{1,0:T(8,128)(2,1)S(1)} %collective-permute-done.2.refs_3_.refs_4_), channel_id=1, source_target_pairs={{0,1},{1,0},{2,3},{3,2},{4,5},{5,4},{6,7},{7,6},{8,9},{9,8},{10,11... | collective-permute-start | bytes 1572872 | tf_op jit(solution)/shard_map/ppermute | solution.py:343
  31.7 18.8 %collective-permute-start.4 = (bf16[176,2048]{1,0:T(8,128)(2,1)}, bf16[176,2048]{1,0:T(8,128)(2,1)S(1)}, u32[]{:S(2)}, u32[]{:S(2)}) collective-permute-start(bf16[176,2048]{1,0:T(8,128)(2,1)} %get-tuple-element.45), channel_id=1, source_target_pairs={{0,8},{8,16},{16,24},{24,28},{28,20},{20,12},{12,4},{4,0},{1,9},{9... | collective-permute-start | bytes 2162696 | tf_op jit(solution)/shard_map/ppermute | solution.py:489
  33.5 18.5 %collective-permute-start.5 = (bf16[176,2048]{1,0:T(8,128)(2,1)}, bf16[176,2048]{1,0:T(8,128)(2,1)S(1)}, u32[]{:S(2)}, u32[]{:S(2)}) collective-permute-start(bf16[176,2048]{1,0:T(8,128)(2,1)} %get-tuple-element.46), channel_id=1, source_target_pairs={{8,0},{16,8},{24,16},{28,24},{20,28},{12,20},{4,12},{0,4},{9,1},{1... | collective-permute-start | bytes 2162696 | tf_op jit(solution)/shard_map/ppermute | solution.py:489
  41.2 10.8 %copy-start.13 = (bf16[128,2048]{1,0:T(8,128)(2,1)S(1)}, bf16[128,2048]{1,0:T(8,128)(2,1)}, u32[]{:S(2)}) copy-start(bf16[128,2048]{1,0:T(8,128)(2,1)} %refs_0_.5) | copy-start | bytes 1572868
  41.3 10.7 %copy-start.15 = (bf16[128,2048]{1,0:T(8,128)(2,1)S(1)}, bf16[128,2048]{1,0:T(8,128)(2,1)}, u32[]{:S(2)}) copy-start(bf16[128,2048]{1,0:T(8,128)(2,1)} %refs_1_.18) | copy-start | bytes 1572868
  41.3 10.7 %copy-start.21 = (bf16[128,2048]{1,0:T(8,128)(2,1)S(1)}, bf16[128,2048]{1,0:T(8,128)(2,1)}, u32[]{:S(2)}) copy-start(bf16[128,2048]{1,0:T(8,128)(2,1)} %copy-done.19) | copy-start | bytes 1572868
  41.3 10.7 %copy-start.23 = (bf16[2,256,256]{2,1,0:T(8,128)(2,1)S(1)}, bf16[2,256,256]{2,1,0:T(8,128)(2,1)}, u32[]{:S(2)}) copy-start(bf16[2,256,256]{2,1,0:T(8,128)(2,1)} %constant.23.clone.refs_5_.refs_4_) | copy-start | bytes 786436
  41.3 10.7 %copy-start.25 = (bf16[2,128,256]{2,1,0:T(8,128)(2,1)S(1)}, bf16[2,128,256]{2,1,0:T(8,128)(2,1)}, u32[]{:S(2)}) copy-start(bf16[2,128,256]{2,1,0:T(8,128)(2,1)} %constant.26.clone.refs_5_) | copy-start | bytes 393220
  50.5 27.2 %copy-start = (bf16[176,2048]{1,0:T(8,128)(2,1)}, bf16[176,2048]{1,0:T(8,128)(2,1)S(1)}, u32[]{:S(2)}) copy-start(bf16[176,2048]{1,0:T(8,128)(2,1)S(1)} %collective-permute-done.4.refs_6_.refs_4_) | copy-start | bytes 2162692
  52.0 25.7 %copy-start.2 = (bf16[176,2048]{1,0:T(8,128)(2,1)}, bf16[176,2048]{1,0:T(8,128)(2,1)S(1)}, u32[]{:S(2)}) copy-start(bf16[176,2048]{1,0:T(8,128)(2,1)S(1)} %collective-permute-done.5.refs_7_.refs_5_) | copy-start | bytes 2162692
  61.4 34.4 %collective-permute-start.8 = (bf16[160,2048]{1,0:T(8,128)(2,1)S(1)}, bf16[160,2048]{1,0:T(8,128)(2,1)S(1)}, u32[]{:S(2)}, u32[]{:S(2)}) collective-permute-start(bf16[160,2048]{1,0:T(8,128)(2,1)S(1)} %slice.82), channel_id=1, source_target_pairs={{0,8},{8,16},{16,24},{24,28},{28,20},{20,12},{12,4},{4,0},{1,9},{9... | collective-permute-start | bytes 1966088 | tf_op jit(solution)/shard_map/ppermute | solution.py:489
  63.0 32.8 %collective-permute-start.9 = (bf16[160,2048]{1,0:T(8,128)(2,1)S(1)}, bf16[160,2048]{1,0:T(8,128)(2,1)S(1)}, u32[]{:S(2)}, u32[]{:S(2)}) collective-permute-start(bf16[160,2048]{1,0:T(8,128)(2,1)S(1)} %slice.83), channel_id=1, source_target_pairs={{8,0},{16,8},{24,16},{28,24},{20,28},{12,20},{4,12},{0,4},{9,1},{1... | collective-permute-start | bytes 1966088 | tf_op jit(solution)/shard_map/ppermute | solution.py:489
  63.5 31.5 %collective-permute-start.12 = (bf16[1024,128]{1,0:T(8,128)(2,1)S(1)}, bf16[1024,128]{1,0:T(8,128)(2,1)S(1)}, u32[]{:S(2)}, u32[]{:S(2)}) collective-permute-start(bf16[1024,128]{1,0:T(8,128)(2,1)S(1)} %get-tuple-element.80), channel_id=1, source_target_pairs={{0,4},{4,0},{8,12},{12,8},{16,20},{20,16},{24,28},{28,24},{1,5},{5... | collective-permute-start | bytes 786440 | tf_op jit(solution)/shard_map/ppermute | solution.py:343
  64.8 51.9 %collective-permute-start.11 = (bf16[128,2048]{1,0:T(8,128)(2,1)S(1)}, bf16[128,2048]{1,0:T(8,128)(2,1)S(1)}, u32[]{:S(2)}, u32[]{:S(2)}) collective-permute-start(bf16[128,2048]{1,0:T(8,128)(2,1)S(1)} %get-tuple-element.44.refs_3_.refs_2_), channel_id=1, source_target_pairs={{4,0},{8,4},{12,8},{16,12},{20,16},{24,20},{28,24},{5,1},{9,5},{13... | collective-permute-start | bytes 1572872 | tf_op jit(solution)/shard_map/ppermute | solution.py:512
  66.1 29.6 %collective-permute-start.20 = (bf16[16,2048]{1,0:T(8,128)(2,1)S(1)}, bf16[16,2048]{1,0:T(8,128)(2,1)S(1)}, u32[]{:S(2)}, u32[]{:S(2)}) collective-permute-start(bf16[16,2048]{1,0:T(8,128)(2,1)S(1)} %get-tuple-element.62), channel_id=1, source_target_pairs={{0,28},{8,20},{16,12},{24,4},{28,0},{20,8},{12,16},{4,24},{1,29},{... | collective-permute-start | bytes 196616 | tf_op jit(solution)/shard_map/ppermute | solution.py:497
  95.0 31.8 %collective-permute-start.7 = (bf16[128,2048]{1,0:T(8,128)(2,1)S(1)}, bf16[128,2048]{1,0:T(8,128)(2,1)S(1)}, u32[]{:S(2)}, u32[]{:S(2)}) collective-permute-start(bf16[128,2048]{1,0:T(8,128)(2,1)S(1)} %get-tuple-element.48), channel_id=1, source_target_pairs={{0,1},{1,0},{2,3},{3,2},{4,5},{5,4},{6,7},{7,6},{8,9},{9,8},{10,11... | collective-permute-start | bytes 1572872 | tf_op jit(solution)/shard_map/ppermute | solution.py:343
  95.7 20.2 %collective-permute-start.13 = (bf16[512,128]{1,0:T(8,128)(2,1)S(1)}, bf16[512,128]{1,0:T(8,128)(2,1)S(1)}, u32[]{:S(2)}, u32[]{:S(2)}) collective-permute-start(bf16[512,128]{1,0:T(8,128)(2,1)S(1)} %get-tuple-element.57), channel_id=1, source_target_pairs={{0,8},{4,12},{8,0},{12,4},{16,24},{20,28},{24,16},{28,20},{1,9},{5... | collective-permute-start | bytes 393224 | tf_op jit(solution)/shard_map/ppermute | solution.py:343
  95.9 16.5 %collective-permute-start.15 = (bf16[144,2048]{1,0:T(8,128)(2,1)S(1)}, bf16[144,2048]{1,0:T(8,128)(2,1)S(1)}, u32[]{:S(2)}, u32[]{:S(2)}) collective-permute-start(bf16[144,2048]{1,0:T(8,128)(2,1)S(1)} %slice.84), channel_id=1, source_target_pairs={{0,8},{8,16},{16,24},{24,28},{28,20},{20,12},{12,4},{4,0},{1,9},{9... | collective-permute-start | bytes 1769480 | tf_op jit(solution)/shard_map/ppermute | solution.py:489
  98.0 16.4 %collective-permute-start.16 = (bf16[144,2048]{1,0:T(8,128)(2,1)S(1)}, bf16[144,2048]{1,0:T(8,128)(2,1)S(1)}, u32[]{:S(2)}, u32[]{:S(2)}) collective-permute-start(bf16[144,2048]{1,0:T(8,128)(2,1)S(1)} %slice.85), channel_id=1, source_target_pairs={{8,0},{16,8},{24,16},{28,24},{20,28},{12,20},{4,12},{0,4},{9,1},{1... | collective-permute-start | bytes 1769480 | tf_op jit(solution)/shard_map/ppermute | solution.py:489
  112.5 9.2 %collective-permute-start.21 = (bf16[64,2048]{1,0:T(8,128)(2,1)S(1)}, bf16[64,2048]{1,0:T(8,128)(2,1)S(1)}, u32[]{:S(2)}, u32[]{:S(2)}) collective-permute-start(bf16[64,2048]{1,0:T(8,128)(2,1)S(1)} %get-tuple-element.87.refs_10_), channel_id=1, source_target_pairs={{0,2},{1,3},{2,0},{3,1},{4,6},{5,7},{6,4},{7,5},{8,10},{9,11},{10,... | collective-permute-start | bytes 786440 | tf_op jit(solution)/shard_map/ppermute | solution.py:343
  114.4 11.9 %collective-permute-start.22 = (bf16[64,2048]{1,0:T(8,128)(2,1)S(1)}, bf16[64,2048]{1,0:T(8,128)(2,1)S(1)}, u32[]{:S(2)}, u32[]{:S(2)}) collective-permute-start(bf16[64,2048]{1,0:T(8,128)(2,1)S(1)} %pad_maximum_fusion.2.refs_11_), channel_id=1, source_target_pairs={{0,2},{1,3},{2,0},{3,1},{4,6},{5,7},{6,4},{7,5},{8,10},{9,11},{10,... | collective-permute-start | bytes 786440 | tf_op jit(solution)/shard_map/ppermute | solution.py:343
  116.7 9.6 %collective-permute-start.18 = (bf16[64,2048]{1,0:T(8,128)(2,1)S(1)}, bf16[64,2048]{1,0:T(8,128)(2,1)S(1)}, u32[]{:S(2)}, u32[]{:S(2)}) collective-permute-start(bf16[64,2048]{1,0:T(8,128)(2,1)S(1)} %slice.71), channel_id=1, source_target_pairs={{8,0},{16,8},{24,16},{28,24},{20,28},{12,20},{4,12},{0,4},{9,1},{1... | collective-permute-start | bytes 786440 | tf_op jit(solution)/shard_map/ppermute | solution.py:551
  119.8 7.1 %collective-permute-start.17 = (bf16[64,2048]{1,0:T(8,128)(2,1)S(1)}, bf16[64,2048]{1,0:T(8,128)(2,1)S(1)}, u32[]{:S(2)}, u32[]{:S(2)}) collective-permute-start(bf16[64,2048]{1,0:T(8,128)(2,1)S(1)} %slice.70), channel_id=1, source_target_pairs={{0,8},{8,16},{16,24},{24,28},{28,20},{20,12},{12,4},{4,0},{1,9},{9... | collective-permute-start | bytes 786440 | tf_op jit(solution)/shard_map/ppermute | solution.py:551
  126.9 10.5 %collective-permute-start.23 = (bf16[256,2048]{1,0:T(8,128)(2,1)S(1)}, bf16[256,2048]{1,0:T(8,128)(2,1)S(1)}, u32[]{:S(2)}, u32[]{:S(2)}) collective-permute-start(bf16[256,2048]{1,0:T(8,128)(2,1)S(1)} %constant_dynamic-update-slice_fusion.4), channel_id=1, source_target_pairs={{0,1},{1,0},{2,3},{3,2},{4,5},{5,4},{6,7},{7,6},{8,9},{9,8},{10,11... | collective-permute-start | bytes 3145736 | tf_op jit(solution)/shard_map/ppermute | solution.py:343
  127.0 19.1 %collective-permute-start.6 = (bf16[128,2048]{1,0:T(8,128)(2,1)S(1)}, bf16[128,2048]{1,0:T(8,128)(2,1)S(1)}, u32[]{:S(2)}, u32[]{:S(2)}) collective-permute-start(bf16[128,2048]{1,0:T(8,128)(2,1)S(1)} %mixed_part.2.refs_3_), channel_id=1, source_target_pairs={{0,1},{1,0},{2,3},{3,2},{4,5},{5,4},{6,7},{7,6},{8,9},{9,8},{10,11... | collective-permute-start | bytes 1572872 | tf_op jit(solution)/shard_map/ppermute | solution.py:343
  127.5 9.2 %collective-permute-start.14 = (bf16[512,128]{1,0:T(8,128)(2,1)S(1)}, bf16[512,128]{1,0:T(8,128)(2,1)S(1)}, u32[]{:S(2)}, u32[]{:S(2)}) collective-permute-start(bf16[512,128]{1,0:T(8,128)(2,1)S(1)} %added.4.refs_1_), channel_id=1, source_target_pairs={{0,16},{4,20},{8,24},{12,28},{16,0},{20,4},{24,8},{28,12},{1,17},{... | collective-permute-start | bytes 393224 | tf_op jit(solution)/shard_map/ppermute | solution.py:343
  127.6 18.5 %collective-permute-start.10 = (bf16[128,2048]{1,0:T(8,128)(2,1)S(1)}, bf16[128,2048]{1,0:T(8,128)(2,1)S(1)}, u32[]{:S(2)}, u32[]{:S(2)}) collective-permute-start(bf16[128,2048]{1,0:T(8,128)(2,1)S(1)} %convert_add_fusion), channel_id=1, source_target_pairs={{0,2},{1,3},{2,0},{3,1},{4,6},{5,7},{6,4},{7,5},{8,10},{9,11},{10,... | collective-permute-start | bytes 1572872 | tf_op jit(solution)/shard_map/ppermute | solution.py:343
  137.3 5.1 %collective-permute-start.19 = (bf16[512,128]{1,0:T(8,128)(2,1)S(1)}, bf16[512,128]{1,0:T(8,128)(2,1)S(1)}, u32[]{:S(2)}, u32[]{:S(2)}) collective-permute-start(bf16[512,128]{1,0:T(8,128)(2,1)S(1)} %added.5.refs_1_), channel_id=1, source_target_pairs={{0,8},{4,12},{8,0},{12,4},{16,24},{20,28},{24,16},{28,20},{1,9},{5... | collective-permute-start | bytes 393224 | tf_op jit(solution)/shard_map/ppermute | solution.py:343
  143.0 9.2 %collective-permute-start.24 = (bf16[1024,128]{1,0:T(8,128)(2,1)S(1)}, bf16[1024,128]{1,0:T(8,128)(2,1)S(1)}, u32[]{:S(2)}, u32[]{:S(2)}) collective-permute-start(bf16[1024,128]{1,0:T(8,128)(2,1)S(1)} %joined.2.refs_1_), channel_id=1, source_target_pairs={{0,4},{4,0},{8,12},{12,8},{16,20},{20,16},{24,28},{28,24},{1,5},{5... | collective-permute-start | bytes 786440 | tf_op jit(solution)/shard_map/ppermute | solution.py:343
  (22 other events, 119.7 us)

commit v14 on v13

--- a/solution.py
+++ b/solution.py
@@ -509,7 +509,6 @@
     )
     previous, landed = landed, passed_on([grad_filtered])
 
-    following = lax.ppermute(grad_filtered, "ctx", [(i + 1, i) for i in range(n_ctx - 1)])
     tap_grad = by_channel(
         tap_grad_kernel,
         [key_proj, value_proj, earlier, grad_filtered, forward, lags],
@@ -524,17 +523,8 @@
         terms[off ^ 1] = terms[off ^ 1] + from_core[-1].astype(F32)
     mixed_one = weight_pass(me, out_weight, 1, gated, after=[tap_grad])[0]
     last_part = weight_pass(me, out_weight, 0, gated, after=[mixed_one])[0]
-    tap_sum = Sum(me, held_until([tap_grad], [mixed_one])[0])
-    previous, landed = landed, passed_on([last_part] + tap_sum.add(()))
-
-    grad_key, grad_value = by_channel(
-        backward_kernel,
-        [key_proj, value_proj, grad_filtered, following, filters, forward, early_rows],
-        "ttttcww",
-        [("t", BF16), ("t", BF16)],
-        "backward_filter",
-        after=previous + from_core,
-    )
+    previous, landed = landed, passed_on([last_part])
+
     terms = dict(zip(terms, held_until(terms.values(), previous)))
     terms[0] = last_part + swap(mixed_one, "chan", 1).astype(F32)
     for bit in bits_of(n_chan)[1:]:
@@ -545,14 +535,25 @@
     first = jnp.concatenate(held_until(brought[:early], previous), axis=0)
 
     for unused in range(turns - 4):
-        landed = passed_on([grad_key])
+        landed = passed_on([last_part])
     half = length // 2
-    onto, back = held_until(ends, [following] + tap_sum.add(()))
+    tap_sum = Sum(me, held_until([tap_grad], previous)[0])
+    onto, back = held_until(ends, tap_sum.add(()))
     far = [lax.ppermute(onto[:half], "ctx", ahead), lax.ppermute(back[half:], "ctx", behind)]
     arrays = arrays[:1] + far + arrays[1:]
     places.insert(1, [(0, half), (0, half)])
 
     cols = [gather_of_chips(part) for part in (first, jnp.concatenate(brought[early:], axis=0))]
+
+    given = held_until([grad_filtered], far)[0]
+    following = lax.ppermute(given, "ctx", [(i + 1, i) for i in range(n_ctx - 1)])
+    grad_key, grad_value = by_channel(
+        backward_kernel,
+        [key_proj, value_proj, grad_filtered, following, filters, forward, early_rows],
+        "ttttcww",
+        [("t", BF16), ("t", BF16)],
+        "backward_filter",
+    )
 
     while tap_sum.add(far):
         pass

time: 154 us -> 149 us (0.968)
  starting transfers between devices: 32 us -> 23.4 us
  waiting for transfers between devices: 46.8 us -> 49.4 us
    ppermute x14, starting transfers between devices: 11.6 us -> 7.4 us  [swap(): return lax.ppermute(block, axis, [(i, i ^ bit) for i in range(size)])]
    ppermute x1, starting transfers between devices: 3.08 us -> 0.06 us  [per_device(): lax.ppermute(back[half:], 'ctx', behind)]
  transfers between devices with their start and end apart: 25 -> 25, of which waited for: 11 -> 8; matrix products, arithmetic and copies ran while one was open for 2% -> 2% of each run, Pallas kernels for 35% -> 42%
where the time goes in v14:
time: 149 us; the launch traced here: 148 us
  Pallas kernels  65.4 us (44%)
  waiting for transfers between devices  49.4 us (33%)
  starting transfers between devices  23.4 us (16%)
  other arithmetic  5.75 us (4%)
  local copies, waits for them, and re-layouts  3.19 us (2%)
    pallas_call x6, Pallas kernels, weight_pass(): pl.pallas_call(ignoring(body, len(after), 1 + len(arrays)), grid_spec=plt...  39.9 us
    ppermute x14, waiting for transfers between devices, swap(): return lax.ppermute(block, axis, [(i, i ^ bit) for i in range(size)])  30.3 us
    ppermute x6, waiting for transfers between devices, passed_on(): came = [lax.ppermute(onto, 'ctx', ahead), lax.ppermute(back, 'ctx', behind)]  17 us
    pallas_call x3, Pallas kernels, by_channel(): pl.pallas_call(ignoring(functools.partial(kernel, length), len(after), le...  10.8 us
    pallas_call x2, Pallas kernels, grad_weight_of(): pl.pallas_call(ignoring(functools.partial(weight_kernel, places, parts),...  10 us
    ppermute x14, starting transfers between devices, swap(): return lax.ppermute(block, axis, [(i, i ^ bit) for i in range(size)])  7.4 us
    ppermute x6, starting transfers between devices, passed_on(): came = [lax.ppermute(onto, 'ctx', ahead), lax.ppermute(back, 'ctx', behind)]  6.17 us
    ppermute x1, starting transfers between devices, per_device(): lax.ppermute(held_until([pieces[rows:2 * rows]], [gated])[0], 'ctx', [(or...  4.84 us
  transfers between devices with their start and end apart: 25, of which 8 were waited for; matrix products, arithmetic and copies ran while one was open for 2% of the time, Pallas kernels for 42%

profile of v14, /device:TPU:0, one launch (start us, length us, event | category | flops | bytes accessed | tf_op | source)
XLA Modules:
  0.0 148.5 jit_solution(10544623287697186122)
XLA Ops:
  0.6 2.2 %multiply_convert_fusion = bf16[128,2048]{1,0:T(8,128)(2,1)} fusion(bf16[128,2048]{1,0:T(8,128)(2,1)} %refs_1_.18, bf16[128,2048]{1,0:T(8,128)(2,1)} %refs_0_.5), kind=kLoop, calls=%fused_computation.2 | loop fusion | flops 1048576 | bytes 1572864 | tf_op jit(solution)/shard_map/convert_element_type | solution.py:443
  2.8 2.9 %collective-permute-start.2 = (bf16[128,2048]{1,0:T(8,128)(2,1)S(1)}, bf16[128,2048]{1,0:T(8,128)(2,1)S(1)}, u32[]{:S(2)}, u32[]{:S(2)}) collective-permute-start(bf16[128,2048]{1,0:T(8,128)(2,1)S(1)} %copy-done.4), channel_id=1, source_target_pairs={{0,2},{1,3},{2,0},{3,1},{4,6},{5,7},{6,4},{7,5},{8,10},{9,11},{10,... | collective-permute-start | bytes 1572872 | tf_op jit(solution)/shard_map/ppermute | solution.py:343
  5.8 3.4 %collective-permute-start = (bf16[128,2048]{1,0:T(8,128)(2,1)}, bf16[128,2048]{1,0:T(8,128)(2,1)S(1)}, u32[]{:S(2)}, u32[]{:S(2)}) collective-permute-start(bf16[128,2048]{1,0:T(8,128)(2,1)} %multiply_convert_fusion), channel_id=1, source_target_pairs={{0,4},{4,8},{8,12},{12,16},{16,20},{20,24},{24,28},{1,5},{5,9},{9,... | collective-permute-start | bytes 1572872 | tf_op jit(solution)/shard_map/ppermute | solution.py:445
  9.3 6.2 %grad_gated_part.2.refs_3_ = f32[2048,128]{1,0:T(8,128)S(1)} custom-call(s32[2]{0:T(128)S(1)} %pad_add_fusion.refs_0_, bf16[2048,8192]{1,0:T(8,128)(2,1)} %refs_1_.17, bf16[128,2048]{1,0:T(8,128)(2,1)S(1)} %copy-done.4), custom_call_target="tpu_custom_call" | custom-call | flops 3000000000 | tf_op jit(solution)/shard_map/grad_gated_part/pallas_call | solution.py:190
  15.6 2.1 %collective-permute-done.2.refs_3_.refs_4_ = bf16[128,2048]{1,0:T(8,128)(2,1)S(1)} collective-permute-done((bf16[128,2048]{1,0:T(8,128)(2,1)S(1)}, bf16[128,2048]{1,0:T(8,128)(2,1)S(1)}, u32[]{:S(2)}, u32[]{:S(2)}) %collective-permute-start.2) | collective-permute-done | bytes 524320 | tf_op jit(solution)/shard_map/ppermute | solution.py:343
  17.7 6.2 %grad_gated_part.3.refs_7_.refs_4_.refs_6_ = f32[2048,128]{1,0:T(8,128)S(1)} custom-call(s32[2]{0:T(128)S(1)} %pad_add_fusion.refs_0_, bf16[2048,8192]{1,0:T(8,128)(2,1)} %refs_1_.17, bf16[128,2048]{1,0:T(8,128)(2,1)S(1)} %collective-permute-done.1.refs_2_.refs_3_, f32[2048,128]{1,0:T(8,128)S(1)} %grad_gated_part.2.refs_3_), custom_call_target="tpu_custom_call" | custom-call | flops 3000000000 | tf_op jit(solution)/shard_map/grad_gated_part/pallas_call | solution.py:190
  25.8 3.3 %forward_filter.1 = (bf16[128,2048]{1,0:T(8,128)(2,1)S(1)}, f32[128,2048]{1,0:T(8,128)S(1)}) custom-call(bf16[128,2048]{1,0:T(8,128)(2,1)S(1)} %copy-done.7, bf16[128,2048]{1,0:T(8,128)(2,1)S(1)} %copy-done.8, bf16[128,2048]{1,0:T(8,128)(2,1)S(1)} %copy-done.9, bf16[128,2048]{1,0:T(8,128)(2,1)S(1)} %copy-done.17, bf16[2048,128]{1,0:T(8,128)(2,1)S(1)} %copy-done.12, ...), custom_call_target="tpu_custom_call" | custom-call | flops 3000000000 | tf_op jit(solution)/shard_map/forward_filter/pallas_call | solution.py:107
  29.9 1.3 pad_maximum_fusion.1
  31.2 1.8 %collective-permute-start.4 = (bf16[176,2048]{1,0:T(8,128)(2,1)}, bf16[176,2048]{1,0:T(8,128)(2,1)S(1)}, u32[]{:S(2)}, u32[]{:S(2)}) collective-permute-start(bf16[176,2048]{1,0:T(8,128)(2,1)} %get-tuple-element.46), channel_id=1, source_target_pairs={{0,8},{8,16},{16,24},{24,28},{28,20},{20,12},{12,4},{4,0},{1,9},{9... | collective-permute-start | bytes 2162696 | tf_op jit(solution)/shard_map/ppermute | solution.py:489
  33.2 7.4 %grads_and_mixed.2 = (f32[2048,128]{1,0:T(8,128)S(1)}, f32[128,2048]{1,0:T(8,128)S(1)}) custom-call(s32[2]{0:T(128)S(1)} %pad_add_fusion.refs_0_, bf16[2048,8192]{1,0:T(8,128)(2,1)} %refs_1_.17, bf16[128,2048]{1,0:T(8,128)(2,1)S(1)} %get-tuple-element.41.refs_2_.refs_1_, bf16[128,2048]{1,0:T(8,128)(2,1)S(1)} %collective-permute-done.2.refs_3_.refs_4_, ...), custom_call_target="tpu_custom_call" | custom-call | flops 500000000 | tf_op jit(solution)/shard_map/grads_and_mixed/pallas_call | solution.py:190
  40.6 8.5 %grads_and_mixed.3 = (bf16[128,2048]{1,0:T(8,128)(2,1)}, bf16[128,2048]{1,0:T(8,128)(2,1)S(1)}, bf16[128,2048]{1,0:T(8,128)(2,1)}) custom-call(s32[2]{0:T(128)S(1)} %pad_add_fusion.refs_0_, bf16[2048,8192]{1,0:T(8,128)(2,1)} %refs_1_.17, bf16[128,2048]{1,0:T(8,128)(2,1)S(1)} %get-tuple-element.41.refs_2_.refs_1_, ...), custom_call_target="tpu_custom_call" | custom-call | flops 500000000 | tf_op jit(solution)/shard_map/grads_and_mixed/pallas_call | solution.py:190
  50.0 4.8 %collective-permute-start.20 = (bf16[16,2048]{1,0:T(8,128)(2,1)S(1)}, bf16[16,2048]{1,0:T(8,128)(2,1)S(1)}, u32[]{:S(2)}, u32[]{:S(2)}) collective-permute-start(bf16[16,2048]{1,0:T(8,128)(2,1)S(1)} %get-tuple-element.64), channel_id=1, source_target_pairs={{0,28},{8,20},{16,12},{24,4},{28,0},{20,8},{12,16},{4,24},{1,29},{... | collective-permute-start | bytes 196616 | tf_op jit(solution)/shard_map/ppermute | solution.py:497
  55.1 2.0 %collective-permute-start.9 = (bf16[160,2048]{1,0:T(8,128)(2,1)S(1)}, bf16[160,2048]{1,0:T(8,128)(2,1)S(1)}, u32[]{:S(2)}, u32[]{:S(2)}) collective-permute-start(bf16[160,2048]{1,0:T(8,128)(2,1)S(1)} %slice.83), channel_id=1, source_target_pairs={{8,0},{16,8},{24,16},{28,24},{20,28},{12,20},{4,12},{0,4},{9,1},{1... | collective-permute-start | bytes 1966088 | tf_op jit(solution)/shard_map/ppermute | solution.py:489
  57.1 1.2 convert_add_fusion
  58.3 3.5 %tap_grad.1.refs_3_ = bf16[2048,128]{1,0:T(8,128)(2,1)S(1)} custom-call(bf16[128,2048]{1,0:T(8,128)(2,1)S(1)} %copy-done.8, bf16[128,2048]{1,0:T(8,128)(2,1)S(1)} %copy-done.10, bf16[128,2048]{1,0:T(8,128)(2,1)S(1)} %copy-done.18, bf16[128,2048]{1,0:T(8,128)(2,1)S(1)} %copy-done.15, bf16[2,256,256]{2,1,0:T(8,128)(2,1)S(1)} %copy-done.20, ...), custom_call_target="tpu_custom_call" | custom-call | flops 3000000000 | tf_op jit(solution)/shard_map/tap_grad/pallas_call | solution.py:107
  61.9 5.7 %mixed_part.2.refs_3_ = bf16[128,2048]{1,0:T(8,128)(2,1)S(1)} custom-call(s32[2]{0:T(128)S(1)} %pad_add_fusion.refs_0_, bf16[2048,8192]{1,0:T(8,128)(2,1)} %refs_1_.17, bf16[128,2048]{1,0:T(8,128)(2,1)S(1)} %get-tuple-element.41.refs_2_.refs_1_, bf16[2048,128]{1,0:T(8,128)(2,1)S(1)} %tap_grad.1.refs_3_), custom_call_target="tpu_custom_call" | custom-call | flops 500000000 | tf_op jit(solution)/shard_map/mixed_part/pallas_call | solution.py:190
  67.7 5.7 %mixed_part.3 = f32[128,2048]{1,0:T(8,128)S(1)} custom-call(s32[2]{0:T(128)S(1)} %pad_add_fusion.refs_0_, bf16[2048,8192]{1,0:T(8,128)(2,1)} %refs_1_.17, bf16[128,2048]{1,0:T(8,128)(2,1)S(1)} %get-tuple-element.41.refs_2_.refs_1_, bf16[128,2048]{1,0:T(8,128)(2,1)S(1)} %mixed_part.2.refs_3_), custom_call_target="tpu_custom_call" | custom-call | flops 500000000 | tf_op jit(solution)/shard_map/mixed_part/pallas_call | solution.py:190
  74.1 1.5 collective-permute-start.10
  76.0 1.8 %collective-permute-start.12 = (bf16[144,2048]{1,0:T(8,128)(2,1)S(1)}, bf16[144,2048]{1,0:T(8,128)(2,1)S(1)}, u32[]{:S(2)}, u32[]{:S(2)}) collective-permute-start(bf16[144,2048]{1,0:T(8,128)(2,1)S(1)} %slice.85), channel_id=1, source_target_pairs={{8,0},{16,8},{24,16},{28,24},{20,28},{12,20},{4,12},{0,4},{9,1},{1... | collective-permute-start | bytes 1769480 | tf_op jit(solution)/shard_map/ppermute | solution.py:489
  77.9 17.0 %collective-permute-done.11.refs_8_ = bf16[144,2048]{1,0:T(8,128)(2,1)S(1)} collective-permute-done((bf16[144,2048]{1,0:T(8,128)(2,1)S(1)}, bf16[144,2048]{1,0:T(8,128)(2,1)S(1)}, u32[]{:S(2)}, u32[]{:S(2)}) %collective-permute-start.11) | collective-permute-done | bytes 589856 | tf_op jit(solution)/shard_map/ppermute | solution.py:489
  94.9 1.5 %collective-permute-start.21 = (bf16[64,2048]{1,0:T(8,128)(2,1)S(1)}, bf16[64,2048]{1,0:T(8,128)(2,1)S(1)}, u32[]{:S(2)}, u32[]{:S(2)}) collective-permute-start(bf16[64,2048]{1,0:T(8,128)(2,1)S(1)} %get-tuple-element.89.refs_10_), channel_id=1, source_target_pairs={{0,2},{1,3},{2,0},{3,1},{4,6},{5,7},{6,4},{7,5},{8,10},{9,11},{10,... | collective-permute-start | bytes 786440 | tf_op jit(solution)/shard_map/ppermute | solution.py:343
  98.0 6.2 %collective-permute-done.21.refs_14_ = bf16[64,2048]{1,0:T(8,128)(2,1)S(1)} collective-permute-done((bf16[64,2048]{1,0:T(8,128)(2,1)S(1)}, bf16[64,2048]{1,0:T(8,128)(2,1)S(1)}, u32[]{:S(2)}, u32[]{:S(2)}) %collective-permute-start.21) | collective-permute-done | bytes 262176 | tf_op jit(solution)/shard_map/ppermute | solution.py:343
  104.2 4.3 %collective-permute-done.22.refs_15_ = bf16[64,2048]{1,0:T(8,128)(2,1)S(1)} collective-permute-done((bf16[64,2048]{1,0:T(8,128)(2,1)S(1)}, bf16[64,2048]{1,0:T(8,128)(2,1)S(1)}, u32[]{:S(2)}, u32[]{:S(2)}) %collective-permute-start.22) | collective-permute-done | bytes 262176 | tf_op jit(solution)/shard_map/ppermute | solution.py:343
  108.5 2.0 %collective-permute-done.14.refs_3_.refs_2_ = bf16[64,2048]{1,0:T(8,128)(2,1)S(1)} collective-permute-done((bf16[64,2048]{1,0:T(8,128)(2,1)S(1)}, bf16[64,2048]{1,0:T(8,128)(2,1)S(1)}, u32[]{:S(2)}, u32[]{:S(2)}) %collective-permute-start.14) | collective-permute-done | bytes 262176 | tf_op jit(solution)/shard_map/ppermute | solution.py:542
  110.5 5.9 %collective-permute-done.17.refs_2_ = bf16[512,128]{1,0:T(8,128)(2,1)S(1)} collective-permute-done((bf16[512,128]{1,0:T(8,128)(2,1)S(1)}, bf16[512,128]{1,0:T(8,128)(2,1)S(1)}, u32[]{:S(2)}, u32[]{:S(2)}) %collective-permute-start.17) | collective-permute-done | bytes 131104 | tf_op jit(solution)/shard_map/ppermute | solution.py:343
  117.1 1.5 collective-permute-start.16
  119.6 6.4 %collective-permute-done.18.refs_2_ = bf16[512,128]{1,0:T(8,128)(2,1)S(1)} collective-permute-done((bf16[512,128]{1,0:T(8,128)(2,1)S(1)}, bf16[512,128]{1,0:T(8,128)(2,1)S(1)}, u32[]{:S(2)}, u32[]{:S(2)}) %collective-permute-start.18) | collective-permute-done | bytes 131104 | tf_op jit(solution)/shard_map/ppermute | solution.py:343
  126.7 5.0 %grad_weight.2.refs_18_ = bf16[2048,1024]{1,0:T(8,128)(2,1)} custom-call(s32[2]{0:T(128)S(1)} %pad_add_fusion.refs_0_, bf16[128,2048]{1,0:T(8,128)(2,1)S(1)} %get-tuple-element.41.refs_2_.refs_1_, bf16[64,2048]{1,0:T(8,128)(2,1)S(1)} %collective-permute-done.14.refs_3_.refs_2_, bf16[64,2048]{1,0:T(8,128)(2,1)S(1)} %collective-permute-done.15.refs_4_.refs_3_, ...), custom_call_target="tpu_custom_call" | custom-call | flops 2000000000 | tf_op jit(solution)/shard_map/grad_weight/pallas_call | solution.py:293
  131.7 5.5 %collective-permute-done.19.refs_2_ = bf16[512,128]{1,0:T(8,128)(2,1)S(1)} collective-permute-done((bf16[512,128]{1,0:T(8,128)(2,1)S(1)}, bf16[512,128]{1,0:T(8,128)(2,1)S(1)}, u32[]{:S(2)}, u32[]{:S(2)}) %collective-permute-start.19) | collective-permute-done | bytes 131104 | tf_op jit(solution)/shard_map/ppermute | solution.py:343
  137.8 4.0 %backward_filter.1 = (bf16[128,2048]{1,0:T(8,128)(2,1)}, bf16[128,2048]{1,0:T(8,128)(2,1)}) custom-call(bf16[128,2048]{1,0:T(8,128)(2,1)S(1)} %copy-done.8, bf16[128,2048]{1,0:T(8,128)(2,1)S(1)} %copy-done.10, bf16[128,2048]{1,0:T(8,128)(2,1)S(1)} %copy-done.15, bf16[128,2048]{1,0:T(8,128)(2,1)S(1)} %collective-permute-done.16.refs_3_, ...), custom_call_target="tpu_custom_call" | custom-call | flops 3000000000 | tf_op jit(solution)/shard_map/backward_filter/pallas_call | solution.py:107
  141.8 5.0 %grad_weight.3 = bf16[2048,1024]{1,0:T(8,128)(2,1)} custom-call(s32[2]{0:T(128)S(1)} %pad_add_fusion.refs_0_, bf16[128,2048]{1,0:T(8,128)(2,1)S(1)} %get-tuple-element.41.refs_2_.refs_1_, bf16[64,2048]{1,0:T(8,128)(2,1)S(1)} %collective-permute-done.14.refs_3_.refs_2_, ...), custom_call_target="tpu_custom_call", output_to_operand_aliasing={{}: (18, {})} | custom-call | flops 2000000000 | tf_op jit(solution)/shard_map/grad_weight/pallas_call | solution.py:293
  146.8 1.6 %joined.3 = f32[2048,128]{1,0:T(8,128)} custom-call(s32[2]{0:T(128)S(1)} %pad_add_fusion.refs_0_, bf16[1024,128]{1,0:T(8,128)(2,1)S(1)} %joined.2.refs_1_, bf16[1024,128]{1,0:T(8,128)(2,1)S(1)} %collective-permute-done.24.refs_2_), custom_call_target="tpu_custom_call" | custom-call | flops 500000000 | tf_op jit(solution)/shard_map/joined/pallas_call | solution.py:421
  (114 shorter events, 9.5 us)
Async XLA Ops:
  2.8 14.9 %collective-permute-start.2 = (bf16[128,2048]{1,0:T(8,128)(2,1)S(1)}, bf16[128,2048]{1,0:T(8,128)(2,1)S(1)}, u32[]{:S(2)}, u32[]{:S(2)}) collective-permute-start(bf16[128,2048]{1,0:T(8,128)(2,1)S(1)} %copy-done.4), channel_id=1, source_target_pairs={{0,2},{1,3},{2,0},{3,1},{4,6},{5,7},{6,4},{7,5},{8,10},{9,11},{10,... | collective-permute-start | bytes 1572872 | tf_op jit(solution)/shard_map/ppermute | solution.py:343
  5.8 11.9 %collective-permute-start.1 = (bf16[128,2048]{1,0:T(8,128)(2,1)S(1)}, bf16[128,2048]{1,0:T(8,128)(2,1)S(1)}, u32[]{:S(2)}, u32[]{:S(2)}) collective-permute-start(bf16[128,2048]{1,0:T(8,128)(2,1)S(1)} %copy-done.4), channel_id=1, source_target_pairs={{0,1},{1,0},{2,3},{3,2},{4,5},{5,4},{6,7},{7,6},{8,9},{9,8},{10,11... | collective-permute-start | bytes 1572872 | tf_op jit(solution)/shard_map/ppermute | solution.py:343
  5.8 18.2 %collective-permute-start = (bf16[128,2048]{1,0:T(8,128)(2,1)}, bf16[128,2048]{1,0:T(8,128)(2,1)S(1)}, u32[]{:S(2)}, u32[]{:S(2)}) collective-permute-start(bf16[128,2048]{1,0:T(8,128)(2,1)} %multiply_convert_fusion), channel_id=1, source_target_pairs={{0,4},{4,8},{8,12},{12,16},{16,20},{20,24},{24,28},{1,5},{5,9},{9,... | collective-permute-start | bytes 1572872 | tf_op jit(solution)/shard_map/ppermute | solution.py:445
  15.5 9.2 %copy-start.7 = (bf16[128,2048]{1,0:T(8,128)(2,1)S(1)}, bf16[128,2048]{1,0:T(8,128)(2,1)}, u32[]{:S(2)}) copy-start(bf16[128,2048]{1,0:T(8,128)(2,1)} %refs_5_.4) | copy-start | bytes 1572868
  15.6 9.2 %copy-start.8 = (bf16[128,2048]{1,0:T(8,128)(2,1)S(1)}, bf16[128,2048]{1,0:T(8,128)(2,1)}, u32[]{:S(2)}) copy-start(bf16[128,2048]{1,0:T(8,128)(2,1)} %refs_0_.5) | copy-start | bytes 1572868
  15.6 9.2 %copy-start.9 = (bf16[128,2048]{1,0:T(8,128)(2,1)S(1)}, bf16[128,2048]{1,0:T(8,128)(2,1)}, u32[]{:S(2)}) copy-start(bf16[128,2048]{1,0:T(8,128)(2,1)} %refs_1_.18) | copy-start | bytes 1572868
  15.6 9.2 %copy-start.12 = (bf16[2048,128]{1,0:T(8,128)(2,1)S(1)}, bf16[2048,128]{1,0:T(8,128)(2,1)}, u32[]{:S(2)}) copy-start(bf16[2048,128]{1,0:T(8,128)(2,1)} %refs_4_.4) | copy-start | bytes 1572868
  15.6 9.2 %copy-start.19 = (bf16[2,256,256]{2,1,0:T(8,128)(2,1)S(1)}, bf16[2,256,256]{2,1,0:T(8,128)(2,1)}, u32[]{:S(2)}) copy-start(bf16[2,256,256]{2,1,0:T(8,128)(2,1)} %constant.23.clone.refs_5_.refs_4_) | copy-start | bytes 786436
  17.7 11.5 %collective-permute-start.3 = (bf16[128,2048]{1,0:T(8,128)(2,1)S(1)}, bf16[128,2048]{1,0:T(8,128)(2,1)S(1)}, u32[]{:S(2)}, u32[]{:S(2)}) collective-permute-start(bf16[128,2048]{1,0:T(8,128)(2,1)S(1)} %collective-permute-done.2.refs_3_.refs_4_), channel_id=1, source_target_pairs={{0,1},{1,0},{2,3},{3,2},{4,5},{5,4},{6,7},{7,6},{8,9},{9,8},{10,11... | collective-permute-start | bytes 1572872 | tf_op jit(solution)/shard_map/ppermute | solution.py:343
  31.2 23.6 %collective-permute-start.4 = (bf16[176,2048]{1,0:T(8,128)(2,1)}, bf16[176,2048]{1,0:T(8,128)(2,1)S(1)}, u32[]{:S(2)}, u32[]{:S(2)}) collective-permute-start(bf16[176,2048]{1,0:T(8,128)(2,1)} %get-tuple-element.46), channel_id=1, source_target_pairs={{0,8},{8,16},{16,24},{24,28},{28,20},{20,12},{12,4},{4,0},{1,9},{9... | collective-permute-start | bytes 2162696 | tf_op jit(solution)/shard_map/ppermute | solution.py:489
  33.0 21.9 %collective-permute-start.5 = (bf16[176,2048]{1,0:T(8,128)(2,1)}, bf16[176,2048]{1,0:T(8,128)(2,1)S(1)}, u32[]{:S(2)}, u32[]{:S(2)}) collective-permute-start(bf16[176,2048]{1,0:T(8,128)(2,1)} %get-tuple-element.47), channel_id=1, source_target_pairs={{8,0},{16,8},{24,16},{28,24},{20,28},{12,20},{4,12},{0,4},{9,1},{1... | collective-permute-start | bytes 2162696 | tf_op jit(solution)/shard_map/ppermute | solution.py:489
  49.9 7.2 %collective-permute-start.7 = (bf16[128,2048]{1,0:T(8,128)(2,1)}, bf16[128,2048]{1,0:T(8,128)(2,1)}, u32[]{:S(2)}, u32[]{:S(2)}) collective-permute-start(bf16[128,2048]{1,0:T(8,128)(2,1)} %get-tuple-element.49), channel_id=1, source_target_pairs={{0,1},{1,0},{2,3},{3,2},{4,5},{5,4},{6,7},{7,6},{8,9},{9,8},{10,11... | collective-permute-start | bytes 1572872 | tf_op jit(solution)/shard_map/ppermute | solution.py:343
  50.0 23.5 %collective-permute-start.20 = (bf16[16,2048]{1,0:T(8,128)(2,1)S(1)}, bf16[16,2048]{1,0:T(8,128)(2,1)S(1)}, u32[]{:S(2)}, u32[]{:S(2)}) collective-permute-start(bf16[16,2048]{1,0:T(8,128)(2,1)S(1)} %get-tuple-element.64), channel_id=1, source_target_pairs={{0,28},{8,20},{16,12},{24,4},{28,0},{20,8},{12,16},{4,24},{1,29},{... | collective-permute-start | bytes 196616 | tf_op jit(solution)/shard_map/ppermute | solution.py:497
  54.8 12.8 %copy-start = (bf16[176,2048]{1,0:T(8,128)(2,1)}, bf16[176,2048]{1,0:T(8,128)(2,1)S(1)}, u32[]{:S(2)}) copy-start(bf16[176,2048]{1,0:T(8,128)(2,1)S(1)} %collective-permute-done.4.refs_6_.refs_4_) | copy-start | bytes 2162692
  55.0 12.7 %copy-start.2 = (bf16[176,2048]{1,0:T(8,128)(2,1)}, bf16[176,2048]{1,0:T(8,128)(2,1)S(1)}, u32[]{:S(2)}) copy-start(bf16[176,2048]{1,0:T(8,128)(2,1)S(1)} %collective-permute-done.5.refs_7_.refs_5_) | copy-start | bytes 2162692
  55.0 18.4 %collective-permute-start.8 = (bf16[160,2048]{1,0:T(8,128)(2,1)S(1)}, bf16[160,2048]{1,0:T(8,128)(2,1)S(1)}, u32[]{:S(2)}, u32[]{:S(2)}) collective-permute-start(bf16[160,2048]{1,0:T(8,128)(2,1)S(1)} %slice.82), channel_id=1, source_target_pairs={{0,8},{8,16},{16,24},{24,28},{28,20},{20,12},{12,4},{4,0},{1,9},{9... | collective-permute-start | bytes 1966088 | tf_op jit(solution)/shard_map/ppermute | solution.py:489
  55.1 18.4 %collective-permute-start.9 = (bf16[160,2048]{1,0:T(8,128)(2,1)S(1)}, bf16[160,2048]{1,0:T(8,128)(2,1)S(1)}, u32[]{:S(2)}, u32[]{:S(2)}) collective-permute-start(bf16[160,2048]{1,0:T(8,128)(2,1)S(1)} %slice.83), channel_id=1, source_target_pairs={{8,0},{16,8},{24,16},{28,24},{20,28},{12,20},{4,12},{0,4},{9,1},{1... | collective-permute-start | bytes 1966088 | tf_op jit(solution)/shard_map/ppermute | solution.py:489
  67.6 51.0 %collective-permute-start.6 = (bf16[128,2048]{1,0:T(8,128)(2,1)S(1)}, bf16[128,2048]{1,0:T(8,128)(2,1)S(1)}, u32[]{:S(2)}, u32[]{:S(2)}) collective-permute-start(bf16[128,2048]{1,0:T(8,128)(2,1)S(1)} %mixed_part.2.refs_3_), channel_id=1, source_target_pairs={{0,1},{1,0},{2,3},{3,2},{4,5},{5,4},{6,7},{7,6},{8,9},{9,8},{10,11... | collective-permute-start | bytes 1572872 | tf_op jit(solution)/shard_map/ppermute | solution.py:343
  73.5 23.6 %collective-permute-start.13 = (bf16[1024,128]{1,0:T(8,128)(2,1)S(1)}, bf16[1024,128]{1,0:T(8,128)(2,1)S(1)}, u32[]{:S(2)}, u32[]{:S(2)}) collective-permute-start(bf16[1024,128]{1,0:T(8,128)(2,1)S(1)} %get-tuple-element.82), channel_id=1, source_target_pairs={{0,4},{4,0},{8,12},{12,8},{16,20},{20,16},{24,28},{28,24},{1,5},{5... | collective-permute-start | bytes 786440 | tf_op jit(solution)/shard_map/ppermute | solution.py:343
  74.1 44.5 %collective-permute-start.10 = (bf16[128,2048]{1,0:T(8,128)(2,1)S(1)}, bf16[128,2048]{1,0:T(8,128)(2,1)S(1)}, u32[]{:S(2)}, u32[]{:S(2)}) collective-permute-start(bf16[128,2048]{1,0:T(8,128)(2,1)S(1)} %convert_add_fusion), channel_id=1, source_target_pairs={{0,2},{1,3},{2,0},{3,1},{4,6},{5,7},{6,4},{7,5},{8,10},{9,11},{10,... | collective-permute-start | bytes 1572872 | tf_op jit(solution)/shard_map/ppermute | solution.py:343
  75.7 19.2 %collective-permute-start.11 = (bf16[144,2048]{1,0:T(8,128)(2,1)S(1)}, bf16[144,2048]{1,0:T(8,128)(2,1)S(1)}, u32[]{:S(2)}, u32[]{:S(2)}) collective-permute-start(bf16[144,2048]{1,0:T(8,128)(2,1)S(1)} %slice.84), channel_id=1, source_target_pairs={{0,8},{8,16},{16,24},{24,28},{28,20},{20,12},{12,4},{4,0},{1,9},{9... | collective-permute-start | bytes 1769480 | tf_op jit(solution)/shard_map/ppermute | solution.py:489
  76.0 20.5 %collective-permute-start.12 = (bf16[144,2048]{1,0:T(8,128)(2,1)S(1)}, bf16[144,2048]{1,0:T(8,128)(2,1)S(1)}, u32[]{:S(2)}, u32[]{:S(2)}) collective-permute-start(bf16[144,2048]{1,0:T(8,128)(2,1)S(1)} %slice.85), channel_id=1, source_target_pairs={{8,0},{16,8},{24,16},{28,24},{20,28},{12,20},{4,12},{0,4},{9,1},{1... | collective-permute-start | bytes 1769480 | tf_op jit(solution)/shard_map/ppermute | solution.py:489
  94.9 9.2 %collective-permute-start.21 = (bf16[64,2048]{1,0:T(8,128)(2,1)S(1)}, bf16[64,2048]{1,0:T(8,128)(2,1)S(1)}, u32[]{:S(2)}, u32[]{:S(2)}) collective-permute-start(bf16[64,2048]{1,0:T(8,128)(2,1)S(1)} %get-tuple-element.89.refs_10_), channel_id=1, source_target_pairs={{0,2},{1,3},{2,0},{3,1},{4,6},{5,7},{6,4},{7,5},{8,10},{9,11},{10,... | collective-permute-start | bytes 786440 | tf_op jit(solution)/shard_map/ppermute | solution.py:343
  96.5 11.9 %collective-permute-start.22 = (bf16[64,2048]{1,0:T(8,128)(2,1)S(1)}, bf16[64,2048]{1,0:T(8,128)(2,1)S(1)}, u32[]{:S(2)}, u32[]{:S(2)}) collective-permute-start(bf16[64,2048]{1,0:T(8,128)(2,1)S(1)} %pad_maximum_fusion.2.refs_11_), channel_id=1, source_target_pairs={{0,2},{1,3},{2,0},{3,1},{4,6},{5,7},{6,4},{7,5},{8,10},{9,11},{10,... | collective-permute-start | bytes 786440 | tf_op jit(solution)/shard_map/ppermute | solution.py:343
  97.9 10.6 %collective-permute-start.15 = (bf16[64,2048]{1,0:T(8,128)(2,1)S(1)}, bf16[64,2048]{1,0:T(8,128)(2,1)S(1)}, u32[]{:S(2)}, u32[]{:S(2)}) collective-permute-start(bf16[64,2048]{1,0:T(8,128)(2,1)S(1)} %slice.71), channel_id=1, source_target_pairs={{8,0},{16,8},{24,16},{28,24},{20,28},{12,20},{4,12},{0,4},{9,1},{1... | collective-permute-start | bytes 786440 | tf_op jit(solution)/shard_map/ppermute | solution.py:542
  104.2 6.4 %collective-permute-start.14 = (bf16[64,2048]{1,0:T(8,128)(2,1)S(1)}, bf16[64,2048]{1,0:T(8,128)(2,1)S(1)}, u32[]{:S(2)}, u32[]{:S(2)}) collective-permute-start(bf16[64,2048]{1,0:T(8,128)(2,1)S(1)} %slice.70), channel_id=1, source_target_pairs={{0,8},{8,16},{16,24},{24,28},{28,20},{20,12},{12,4},{4,0},{1,9},{9... | collective-permute-start | bytes 786440 | tf_op jit(solution)/shard_map/ppermute | solution.py:542
  110.5 16.1 %collective-permute-start.23 = (bf16[256,2048]{1,0:T(8,128)(2,1)S(1)}, bf16[256,2048]{1,0:T(8,128)(2,1)S(1)}, u32[]{:S(2)}, u32[]{:S(2)}) collective-permute-start(bf16[256,2048]{1,0:T(8,128)(2,1)S(1)} %constant_dynamic-update-slice_fusion.4), channel_id=1, source_target_pairs={{0,1},{1,0},{2,3},{3,2},{4,5},{5,4},{6,7},{7,6},{8,9},{9,8},{10,11... | collective-permute-start | bytes 3145736 | tf_op jit(solution)/shard_map/ppermute | solution.py:343
  110.5 5.9 %collective-permute-start.17 = (bf16[512,128]{1,0:T(8,128)(2,1)S(1)}, bf16[512,128]{1,0:T(8,128)(2,1)S(1)}, u32[]{:S(2)}, u32[]{:S(2)}) collective-permute-start(bf16[512,128]{1,0:T(8,128)(2,1)S(1)} %get-tuple-element.63), channel_id=1, source_target_pairs={{0,8},{4,12},{8,0},{12,4},{16,24},{20,28},{24,16},{28,20},{1,9},{5... | collective-permute-start | bytes 393224 | tf_op jit(solution)/shard_map/ppermute | solution.py:343
  117.0 9.0 %collective-permute-start.18 = (bf16[512,128]{1,0:T(8,128)(2,1)S(1)}, bf16[512,128]{1,0:T(8,128)(2,1)S(1)}, u32[]{:S(2)}, u32[]{:S(2)}) collective-permute-start(bf16[512,128]{1,0:T(8,128)(2,1)S(1)} %added.4.refs_1_), channel_id=1, source_target_pairs={{0,16},{4,20},{8,24},{12,28},{16,0},{20,4},{24,8},{28,12},{1,17},{... | collective-permute-start | bytes 393224 | tf_op jit(solution)/shard_map/ppermute | solution.py:343
  117.1 20.7 %collective-permute-start.16 = (bf16[128,2048]{1,0:T(8,128)(2,1)S(1)}, bf16[128,2048]{1,0:T(8,128)(2,1)S(1)}, u32[]{:S(2)}, u32[]{:S(2)}) collective-permute-start(bf16[128,2048]{1,0:T(8,128)(2,1)S(1)} %copy-done.15), channel_id=1, source_target_pairs={{4,0},{8,4},{12,8},{16,12},{20,16},{24,20},{28,24},{5,1},{9,5},{13... | collective-permute-start | bytes 1572872 | tf_op jit(solution)/shard_map/ppermute | solution.py:549
  126.6 10.6 %collective-permute-start.19 = (bf16[512,128]{1,0:T(8,128)(2,1)S(1)}, bf16[512,128]{1,0:T(8,128)(2,1)S(1)}, u32[]{:S(2)}, u32[]{:S(2)}) collective-permute-start(bf16[512,128]{1,0:T(8,128)(2,1)S(1)} %added.5.refs_1_), channel_id=1, source_target_pairs={{0,8},{4,12},{8,0},{12,4},{16,24},{20,28},{24,16},{28,20},{1,9},{5... | collective-permute-start | bytes 393224 | tf_op jit(solution)/shard_map/ppermute | solution.py:343
  137.7 9.1 %collective-permute-start.24 = (bf16[1024,128]{1,0:T(8,128)(2,1)S(1)}, bf16[1024,128]{1,0:T(8,128)(2,1)S(1)}, u32[]{:S(2)}, u32[]{:S(2)}) collective-permute-start(bf16[1024,128]{1,0:T(8,128)(2,1)S(1)} %joined.2.refs_1_), channel_id=1, source_target_pairs={{0,4},{4,0},{8,12},{12,8},{16,20},{20,16},{24,28},{28,24},{1,5},{5... | collective-permute-start | bytes 786440 | tf_op jit(solution)/shard_map/ppermute | solution.py:343
  (19 other events, 87.0 us)

commit v15 on v14

--- a/solution.py
+++ b/solution.py
@@ -494,13 +494,6 @@
         return came
 
     landed = passed_on([])
-    across = lax.ppermute(
-        held_until([pieces[rows : 2 * rows]], [gated])[0],
-        "ctx",
-        [(order[i], order[(i + turns) % n_ctx]) for i in range(n_ctx)],
-    )
-    brought.insert(1, across)
-
     terms = {}
     for off in offs[:-1]:
         *sums, terms[off] = weight_pass(me, out_weight, off, gated, cots[off], sums)
@@ -522,7 +515,14 @@
         from_core.append(swap(terms.pop(off), "chan", 1))
         terms[off ^ 1] = terms[off ^ 1] + from_core[-1].astype(F32)
     mixed_one = weight_pass(me, out_weight, 1, gated, after=[tap_grad])[0]
+    across = lax.ppermute(
+        held_until([pieces[rows : 2 * rows]], [mixed_one])[0],
+        "ctx",
+        [(order[i], order[(i + turns) % n_ctx]) for i in range(n_ctx)],
+    )
+    brought.insert(1, across)
     last_part = weight_pass(me, out_weight, 0, gated, after=[mixed_one])[0]
+    tap_sum = Sum(me, held_until([tap_grad], [mixed_one])[0])
     previous, landed = landed, passed_on([last_part])
 
     terms = dict(zip(terms, held_until(terms.values(), previous)))
@@ -537,13 +537,14 @@
     for unused in range(turns - 4):
         landed = passed_on([last_part])
     half = length // 2
-    tap_sum = Sum(me, held_until([tap_grad], previous)[0])
-    onto, back = held_until(ends, tap_sum.add(()))
+    cols = [gather_of_chips(first)]
+    onto, back = held_until(ends, tap_sum.add([last_part]) + [cols[0][off] for off in cols[0] if off])
+    tap_sum.add(landed)
     far = [lax.ppermute(onto[:half], "ctx", ahead), lax.ppermute(back[half:], "ctx", behind)]
     arrays = arrays[:1] + far + arrays[1:]
     places.insert(1, [(0, half), (0, half)])
 
-    cols = [gather_of_chips(part) for part in (first, jnp.concatenate(brought[early:], axis=0))]
+    cols.append(gather_of_chips(jnp.concatenate(brought[early:], axis=0)))
 
     given = held_until([grad_filtered], far)[0]
     following = lax.ppermute(given, "ctx", [(i + 1, i) for i in range(n_ctx - 1)])

time: 149 us -> 142 us (0.953)
  waiting for transfers between devices: 49.4 us -> 39.5 us
  starting transfers between devices: 23.4 us -> 26 us
    ppermute x14, waiting for transfers between devices: 30.3 us -> 24.9 us  [swap(): return lax.ppermute(block, axis, [(i, i ^ bit) for i in range(size)])]
    ppermute x6, waiting for transfers between devices: 17 us -> 12.9 us  [passed_on(): came = [lax.ppermute(onto, 'ctx', ahead), lax.ppermute(back, 'ctx', behind)]]
    ppermute x14, starting transfers between devices: 7.4 us -> 9.33 us  [swap(): return lax.ppermute(block, axis, [(i, i ^ bit) for i in range(size)])]
    ppermute x1, starting transfers between devices: 0.06 us -> 1.73 us  [per_device(): lax.ppermute(back[half:], 'ctx', behind)]
  transfers between devices with their start and end apart: 25 -> 25, of which waited for: 8 -> 10; matrix products, arithmetic and copies ran while one was open for 2% -> 2% of each run, Pallas kernels for 42% -> 45%
where the time goes in v15:
time: 142 us; the launch traced here: 141 us
  Pallas kernels  65.4 us (46%)
  waiting for transfers between devices  39.5 us (28%)
  starting transfers between devices  26 us (18%)
  other arithmetic  5.74 us (4%)
  local copies, waits for them, and re-layouts  3.19 us (2%)
    pallas_call x6, Pallas kernels, weight_pass(): pl.pallas_call(ignoring(body, len(after), 1 + len(arrays)), grid_spec=plt...  39.9 us
    ppermute x14, waiting for transfers between devices, swap(): return lax.ppermute(block, axis, [(i, i ^ bit) for i in range(size)])  24.9 us
    ppermute x6, waiting for transfers between devices, passed_on(): came = [lax.ppermute(onto, 'ctx', ahead), lax.ppermute(back, 'ctx', behind)]  12.9 us
    pallas_call x3, Pallas kernels, by_channel(): pl.pallas_call(ignoring(functools.partial(kernel, length), len(after), le...  10.8 us
    pallas_call x2, Pallas kernels, grad_weight_of(): pl.pallas_call(ignoring(functools.partial(weight_kernel, places, parts),...  10 us
    ppermute x14, starting transfers between devices, swap(): return lax.ppermute(block, axis, [(i, i ^ bit) for i in range(size)])  9.33 us
    ppermute x6, starting transfers between devices, passed_on(): came = [lax.ppermute(onto, 'ctx', ahead), lax.ppermute(back, 'ctx', behind)]  6.17 us
    ppermute x1, starting transfers between devices, per_device(): lax.ppermute(held_until([pieces[rows:2 * rows]], [mixed_one])[0], 'ctx',...  3.52 us
  transfers between devices with their start and end apart: 25, of which 10 were waited for; matrix products, arithmetic and copies ran while one was open for 2% of the time, Pallas kernels for 45%

profile of v15, /device:TPU:0, one launch (start us, length us, event | category | flops | bytes accessed | tf_op | source)
XLA Modules:
  0.0 141.1 jit_solution(1562919734250820127)
XLA Ops:
  0.6 2.2 %multiply_convert_fusion = bf16[128,2048]{1,0:T(8,128)(2,1)} fusion(bf16[128,2048]{1,0:T(8,128)(2,1)} %refs_1_.18, bf16[128,2048]{1,0:T(8,128)(2,1)} %refs_0_.5), kind=kLoop, calls=%fused_computation.2 | loop fusion | flops 1048576 | bytes 1572864 | tf_op jit(solution)/shard_map/convert_element_type | solution.py:443
  2.8 2.9 %collective-permute-start.2 = (bf16[128,2048]{1,0:T(8,128)(2,1)S(1)}, bf16[128,2048]{1,0:T(8,128)(2,1)S(1)}, u32[]{:S(2)}, u32[]{:S(2)}) collective-permute-start(bf16[128,2048]{1,0:T(8,128)(2,1)S(1)} %copy-done.4), channel_id=1, source_target_pairs={{0,2},{1,3},{2,0},{3,1},{4,6},{5,7},{6,4},{7,5},{8,10},{9,11},{10,... | collective-permute-start | bytes 1572872 | tf_op jit(solution)/shard_map/ppermute | solution.py:343
  5.8 3.4 %collective-permute-start = (bf16[128,2048]{1,0:T(8,128)(2,1)}, bf16[128,2048]{1,0:T(8,128)(2,1)S(1)}, u32[]{:S(2)}, u32[]{:S(2)}) collective-permute-start(bf16[128,2048]{1,0:T(8,128)(2,1)} %multiply_convert_fusion), channel_id=1, source_target_pairs={{0,4},{4,8},{8,12},{12,16},{16,20},{20,24},{24,28},{1,5},{5,9},{9,... | collective-permute-start | bytes 1572872 | tf_op jit(solution)/shard_map/ppermute | solution.py:445
  9.3 6.2 %grad_gated_part.2.refs_3_ = f32[2048,128]{1,0:T(8,128)S(1)} custom-call(s32[2]{0:T(128)S(1)} %pad_add_fusion.refs_0_, bf16[2048,8192]{1,0:T(8,128)(2,1)} %refs_1_.17, bf16[128,2048]{1,0:T(8,128)(2,1)S(1)} %copy-done.4), custom_call_target="tpu_custom_call" | custom-call | flops 3000000000 | tf_op jit(solution)/shard_map/grad_gated_part/pallas_call | solution.py:190
  15.6 2.1 %collective-permute-done.2.refs_3_.refs_4_ = bf16[128,2048]{1,0:T(8,128)(2,1)S(1)} collective-permute-done((bf16[128,2048]{1,0:T(8,128)(2,1)S(1)}, bf16[128,2048]{1,0:T(8,128)(2,1)S(1)}, u32[]{:S(2)}, u32[]{:S(2)}) %collective-permute-start.2) | collective-permute-done | bytes 524320 | tf_op jit(solution)/shard_map/ppermute | solution.py:343
  17.7 6.2 %grad_gated_part.3.refs_7_.refs_4_.refs_6_ = f32[2048,128]{1,0:T(8,128)S(1)} custom-call(s32[2]{0:T(128)S(1)} %pad_add_fusion.refs_0_, bf16[2048,8192]{1,0:T(8,128)(2,1)} %refs_1_.17, bf16[128,2048]{1,0:T(8,128)(2,1)S(1)} %collective-permute-done.1.refs_2_.refs_3_, f32[2048,128]{1,0:T(8,128)S(1)} %grad_gated_part.2.refs_3_), custom_call_target="tpu_custom_call" | custom-call | flops 3000000000 | tf_op jit(solution)/shard_map/grad_gated_part/pallas_call | solution.py:190
  25.8 3.3 %forward_filter.1 = (bf16[128,2048]{1,0:T(8,128)(2,1)S(1)}, f32[128,2048]{1,0:T(8,128)S(1)}) custom-call(bf16[128,2048]{1,0:T(8,128)(2,1)S(1)} %copy-done.7, bf16[128,2048]{1,0:T(8,128)(2,1)S(1)} %copy-done.8, bf16[128,2048]{1,0:T(8,128)(2,1)S(1)} %copy-done.9, bf16[128,2048]{1,0:T(8,128)(2,1)S(1)} %copy-done.17, bf16[2048,128]{1,0:T(8,128)(2,1)S(1)} %copy-done.12, ...), custom_call_target="tpu_custom_call" | custom-call | flops 3000000000 | tf_op jit(solution)/shard_map/forward_filter/pallas_call | solution.py:107
  31.2 1.8 %collective-permute-start.4 = (bf16[176,2048]{1,0:T(8,128)(2,1)}, bf16[176,2048]{1,0:T(8,128)(2,1)S(1)}, u32[]{:S(2)}, u32[]{:S(2)}) collective-permute-start(bf16[176,2048]{1,0:T(8,128)(2,1)} %get-tuple-element.46), channel_id=1, source_target_pairs={{0,8},{8,16},{16,24},{24,28},{28,20},{20,12},{12,4},{4,0},{1,9},{9... | collective-permute-start | bytes 2162696 | tf_op jit(solution)/shard_map/ppermute | solution.py:489
  33.2 7.4 %grads_and_mixed.2 = (f32[2048,128]{1,0:T(8,128)S(1)}, f32[128,2048]{1,0:T(8,128)S(1)}) custom-call(s32[2]{0:T(128)S(1)} %pad_add_fusion.refs_0_, bf16[2048,8192]{1,0:T(8,128)(2,1)} %refs_1_.17, bf16[128,2048]{1,0:T(8,128)(2,1)S(1)} %get-tuple-element.41.refs_2_.refs_1_, bf16[128,2048]{1,0:T(8,128)(2,1)S(1)} %collective-permute-done.2.refs_3_.refs_4_, ...), custom_call_target="tpu_custom_call" | custom-call | flops 500000000 | tf_op jit(solution)/shard_map/grads_and_mixed/pallas_call | solution.py:190
  40.6 8.5 %grads_and_mixed.3 = (bf16[128,2048]{1,0:T(8,128)(2,1)}, bf16[128,2048]{1,0:T(8,128)(2,1)S(1)}, bf16[128,2048]{1,0:T(8,128)(2,1)}) custom-call(s32[2]{0:T(128)S(1)} %pad_add_fusion.refs_0_, bf16[2048,8192]{1,0:T(8,128)(2,1)} %refs_1_.17, bf16[128,2048]{1,0:T(8,128)(2,1)S(1)} %get-tuple-element.41.refs_2_.refs_1_, ...), custom_call_target="tpu_custom_call" | custom-call | flops 500000000 | tf_op jit(solution)/shard_map/grads_and_mixed/pallas_call | solution.py:190
  50.1 1.4 collective-permute-done.5.refs_7_.refs_5_
  51.5 1.6 %collective-permute-start.8 = (bf16[160,2048]{1,0:T(8,128)(2,1)S(1)}, bf16[160,2048]{1,0:T(8,128)(2,1)S(1)}, u32[]{:S(2)}, u32[]{:S(2)}) collective-permute-start(bf16[160,2048]{1,0:T(8,128)(2,1)S(1)} %slice.82), channel_id=1, source_target_pairs={{0,8},{8,16},{16,24},{24,28},{28,20},{20,12},{12,4},{4,0},{1,9},{9... | collective-permute-start | bytes 1966088 | tf_op jit(solution)/shard_map/ppermute | solution.py:489
  54.9 3.5 %tap_grad.1.refs_3_ = bf16[2048,128]{1,0:T(8,128)(2,1)S(1)} custom-call(bf16[128,2048]{1,0:T(8,128)(2,1)S(1)} %copy-done.8, bf16[128,2048]{1,0:T(8,128)(2,1)S(1)} %copy-done.10, bf16[128,2048]{1,0:T(8,128)(2,1)S(1)} %copy-done.18, bf16[128,2048]{1,0:T(8,128)(2,1)S(1)} %copy-done.15, bf16[2,256,256]{2,1,0:T(8,128)(2,1)S(1)} %copy-done.20, ...), custom_call_target="tpu_custom_call" | custom-call | flops 3000000000 | tf_op jit(solution)/shard_map/tap_grad/pallas_call | solution.py:107
  58.4 5.7 %mixed_part.2.refs_3_ = bf16[128,2048]{1,0:T(8,128)(2,1)S(1)} custom-call(s32[2]{0:T(128)S(1)} %pad_add_fusion.refs_0_, bf16[2048,8192]{1,0:T(8,128)(2,1)} %refs_1_.17, bf16[128,2048]{1,0:T(8,128)(2,1)S(1)} %get-tuple-element.41.refs_2_.refs_1_, bf16[2048,128]{1,0:T(8,128)(2,1)S(1)} %tap_grad.1.refs_3_), custom_call_target="tpu_custom_call" | custom-call | flops 500000000 | tf_op jit(solution)/shard_map/mixed_part/pallas_call | solution.py:190
  64.2 3.5 %collective-permute-start.14 = (bf16[16,2048]{1,0:T(8,128)(2,1)S(1)}, bf16[16,2048]{1,0:T(8,128)(2,1)S(1)}, u32[]{:S(2)}, u32[]{:S(2)}) collective-permute-start(bf16[16,2048]{1,0:T(8,128)(2,1)S(1)} %get-tuple-element.58), channel_id=1, source_target_pairs={{0,28},{8,20},{16,12},{24,4},{28,0},{20,8},{12,16},{4,24},{1,29},{... | collective-permute-start | bytes 196616 | tf_op jit(solution)/shard_map/ppermute | solution.py:518
  67.7 1.7 %collective-permute-start.13 = (bf16[1024,128]{1,0:T(8,128)(2,1)S(1)}, bf16[1024,128]{1,0:T(8,128)(2,1)S(1)}, u32[]{:S(2)}, u32[]{:S(2)}) collective-permute-start(bf16[1024,128]{1,0:T(8,128)(2,1)S(1)} %get-tuple-element.82), channel_id=1, source_target_pairs={{0,4},{4,0},{8,12},{12,8},{16,20},{20,16},{24,28},{28,24},{1,5},{5... | collective-permute-start | bytes 786440 | tf_op jit(solution)/shard_map/ppermute | solution.py:343
  69.4 5.7 %mixed_part.3.refs_3_ = f32[128,2048]{1,0:T(8,128)S(1)} custom-call(s32[2]{0:T(128)S(1)} %pad_add_fusion.refs_0_, bf16[2048,8192]{1,0:T(8,128)(2,1)} %refs_1_.17, bf16[128,2048]{1,0:T(8,128)(2,1)S(1)} %get-tuple-element.41.refs_2_.refs_1_, bf16[128,2048]{1,0:T(8,128)(2,1)S(1)} %mixed_part.2.refs_3_), custom_call_target="tpu_custom_call" | custom-call | flops 500000000 | tf_op jit(solution)/shard_map/mixed_part/pallas_call | solution.py:190
  75.4 2.0 %collective-permute-start.12 = (bf16[144,2048]{1,0:T(8,128)(2,1)S(1)}, bf16[144,2048]{1,0:T(8,128)(2,1)S(1)}, u32[]{:S(2)}, u32[]{:S(2)}) collective-permute-start(bf16[144,2048]{1,0:T(8,128)(2,1)S(1)} %slice.85), channel_id=1, source_target_pairs={{8,0},{16,8},{24,16},{28,24},{20,28},{12,20},{4,12},{0,4},{9,1},{1... | collective-permute-start | bytes 1769480 | tf_op jit(solution)/shard_map/ppermute | solution.py:489
  77.5 1.5 %collective-permute-start.15 = (bf16[64,2048]{1,0:T(8,128)(2,1)S(1)}, bf16[64,2048]{1,0:T(8,128)(2,1)S(1)}, u32[]{:S(2)}, u32[]{:S(2)}) collective-permute-start(bf16[64,2048]{1,0:T(8,128)(2,1)S(1)} %get-tuple-element.89.refs_10_), channel_id=1, source_target_pairs={{0,2},{1,3},{2,0},{3,1},{4,6},{5,7},{6,4},{7,5},{8,10},{9,11},{10,... | collective-permute-start | bytes 786440 | tf_op jit(solution)/shard_map/ppermute | solution.py:343
  79.1 11.4 %collective-permute-done.11.refs_3_.refs_8_ = bf16[144,2048]{1,0:T(8,128)(2,1)S(1)} collective-permute-done((bf16[144,2048]{1,0:T(8,128)(2,1)S(1)}, bf16[144,2048]{1,0:T(8,128)(2,1)S(1)}, u32[]{:S(2)}, u32[]{:S(2)}) %collective-permute-start.11) | collective-permute-done | bytes 589856 | tf_op jit(solution)/shard_map/ppermute | solution.py:489
  90.6 1.5 %collective-permute-start.22 = (bf16[64,2048]{1,0:T(8,128)(2,1)S(1)}, bf16[64,2048]{1,0:T(8,128)(2,1)S(1)}, u32[]{:S(2)}, u32[]{:S(2)}) collective-permute-start(bf16[64,2048]{1,0:T(8,128)(2,1)S(1)} %pad_maximum_fusion.2.refs_11_), channel_id=1, source_target_pairs={{0,2},{1,3},{2,0},{3,1},{4,6},{5,7},{6,4},{7,5},{8,10},{9,11},{10,... | collective-permute-start | bytes 786440 | tf_op jit(solution)/shard_map/ppermute | solution.py:343
  93.5 1.7 %collective-permute-start.17 = (bf16[64,2048]{1,0:T(8,128)(2,1)S(1)}, bf16[64,2048]{1,0:T(8,128)(2,1)S(1)}, u32[]{:S(2)}, u32[]{:S(2)}) collective-permute-start(bf16[64,2048]{1,0:T(8,128)(2,1)S(1)} %slice.75), channel_id=1, source_target_pairs={{8,0},{16,8},{24,16},{28,24},{20,28},{12,20},{4,12},{0,4},{9,1},{1... | collective-permute-start | bytes 786440 | tf_op jit(solution)/shard_map/ppermute | solution.py:543
  95.6 4.3 %collective-permute-done.22.refs_15_ = bf16[64,2048]{1,0:T(8,128)(2,1)S(1)} collective-permute-done((bf16[64,2048]{1,0:T(8,128)(2,1)S(1)}, bf16[64,2048]{1,0:T(8,128)(2,1)S(1)}, u32[]{:S(2)}, u32[]{:S(2)}) %collective-permute-start.22) | collective-permute-done | bytes 262176 | tf_op jit(solution)/shard_map/ppermute | solution.py:343
  100.3 1.4 collective-permute-done.16.refs_3_.refs_2_
  102.0 5.5 %collective-permute-done.19.refs_2_ = bf16[512,128]{1,0:T(8,128)(2,1)S(1)} collective-permute-done((bf16[512,128]{1,0:T(8,128)(2,1)S(1)}, bf16[512,128]{1,0:T(8,128)(2,1)S(1)}, u32[]{:S(2)}, u32[]{:S(2)}) %collective-permute-start.19) | collective-permute-done | bytes 131104 | tf_op jit(solution)/shard_map/ppermute | solution.py:343
  108.6 1.5 %collective-permute-start.18 = (bf16[128,2048]{1,0:T(8,128)(2,1)S(1)}, bf16[128,2048]{1,0:T(8,128)(2,1)S(1)}, u32[]{:S(2)}, u32[]{:S(2)}) collective-permute-start(bf16[128,2048]{1,0:T(8,128)(2,1)S(1)} %copy-done.15), channel_id=1, source_target_pairs={{4,0},{8,4},{12,8},{16,12},{20,16},{24,20},{28,24},{5,1},{9,5},{13... | collective-permute-start | bytes 1572872 | tf_op jit(solution)/shard_map/ppermute | solution.py:550
  111.1 5.9 %collective-permute-done.20.refs_2_ = bf16[512,128]{1,0:T(8,128)(2,1)S(1)} collective-permute-done((bf16[512,128]{1,0:T(8,128)(2,1)S(1)}, bf16[512,128]{1,0:T(8,128)(2,1)S(1)}, u32[]{:S(2)}, u32[]{:S(2)}) %collective-permute-start.20) | collective-permute-done | bytes 131104 | tf_op jit(solution)/shard_map/ppermute | solution.py:343
  117.7 5.0 %grad_weight.2.refs_18_ = bf16[2048,1024]{1,0:T(8,128)(2,1)} custom-call(s32[2]{0:T(128)S(1)} %pad_add_fusion.refs_0_, bf16[128,2048]{1,0:T(8,128)(2,1)S(1)} %get-tuple-element.41.refs_2_.refs_1_, bf16[64,2048]{1,0:T(8,128)(2,1)S(1)} %collective-permute-done.16.refs_3_.refs_2_, bf16[64,2048]{1,0:T(8,128)(2,1)S(1)} %collective-permute-done.17.refs_4_.refs_3_, ...), custom_call_target="tpu_custom_call" | custom-call | flops 2000000000 | tf_op jit(solution)/shard_map/grad_weight/pallas_call | solution.py:293
  122.7 7.1 %collective-permute-done.21.refs_2_ = bf16[512,128]{1,0:T(8,128)(2,1)S(1)} collective-permute-done((bf16[512,128]{1,0:T(8,128)(2,1)S(1)}, bf16[512,128]{1,0:T(8,128)(2,1)S(1)}, u32[]{:S(2)}, u32[]{:S(2)}) %collective-permute-start.21) | collective-permute-done | bytes 131104 | tf_op jit(solution)/shard_map/ppermute | solution.py:343
  130.5 4.0 %backward_filter.1 = (bf16[128,2048]{1,0:T(8,128)(2,1)}, bf16[128,2048]{1,0:T(8,128)(2,1)}) custom-call(bf16[128,2048]{1,0:T(8,128)(2,1)S(1)} %copy-done.8, bf16[128,2048]{1,0:T(8,128)(2,1)S(1)} %copy-done.10, bf16[128,2048]{1,0:T(8,128)(2,1)S(1)} %copy-done.15, bf16[128,2048]{1,0:T(8,128)(2,1)S(1)} %collective-permute-done.18.refs_3_, ...), custom_call_target="tpu_custom_call" | custom-call | flops 3000000000 | tf_op jit(solution)/shard_map/backward_filter/pallas_call | solution.py:107
  134.4 5.0 %grad_weight.3 = bf16[2048,1024]{1,0:T(8,128)(2,1)} custom-call(s32[2]{0:T(128)S(1)} %pad_add_fusion.refs_0_, bf16[128,2048]{1,0:T(8,128)(2,1)S(1)} %get-tuple-element.41.refs_2_.refs_1_, bf16[64,2048]{1,0:T(8,128)(2,1)S(1)} %collective-permute-done.16.refs_3_.refs_2_, ...), custom_call_target="tpu_custom_call", output_to_operand_aliasing={{}: (18, {})} | custom-call | flops 2000000000 | tf_op jit(solution)/shard_map/grad_weight/pallas_call | solution.py:293
  139.4 1.6 %joined.3 = f32[2048,128]{1,0:T(8,128)} custom-call(s32[2]{0:T(128)S(1)} %pad_add_fusion.refs_0_, bf16[1024,128]{1,0:T(8,128)(2,1)S(1)} %joined.2.refs_1_, bf16[1024,128]{1,0:T(8,128)(2,1)S(1)} %collective-permute-done.24.refs_2_), custom_call_target="tpu_custom_call" | custom-call | flops 500000000 | tf_op jit(solution)/shard_map/joined/pallas_call | solution.py:421
  (114 shorter events, 12.9 us)
Async XLA Ops:
  2.8 14.9 %collective-permute-start.2 = (bf16[128,2048]{1,0:T(8,128)(2,1)S(1)}, bf16[128,2048]{1,0:T(8,128)(2,1)S(1)}, u32[]{:S(2)}, u32[]{:S(2)}) collective-permute-start(bf16[128,2048]{1,0:T(8,128)(2,1)S(1)} %copy-done.4), channel_id=1, source_target_pairs={{0,2},{1,3},{2,0},{3,1},{4,6},{5,7},{6,4},{7,5},{8,10},{9,11},{10,... | collective-permute-start | bytes 1572872 | tf_op jit(solution)/shard_map/ppermute | solution.py:343
  5.8 11.9 %collective-permute-start.1 = (bf16[128,2048]{1,0:T(8,128)(2,1)S(1)}, bf16[128,2048]{1,0:T(8,128)(2,1)S(1)}, u32[]{:S(2)}, u32[]{:S(2)}) collective-permute-start(bf16[128,2048]{1,0:T(8,128)(2,1)S(1)} %copy-done.4), channel_id=1, source_target_pairs={{0,1},{1,0},{2,3},{3,2},{4,5},{5,4},{6,7},{7,6},{8,9},{9,8},{10,11... | collective-permute-start | bytes 1572872 | tf_op jit(solution)/shard_map/ppermute | solution.py:343
  5.8 18.2 %collective-permute-start = (bf16[128,2048]{1,0:T(8,128)(2,1)}, bf16[128,2048]{1,0:T(8,128)(2,1)S(1)}, u32[]{:S(2)}, u32[]{:S(2)}) collective-permute-start(bf16[128,2048]{1,0:T(8,128)(2,1)} %multiply_convert_fusion), channel_id=1, source_target_pairs={{0,4},{4,8},{8,12},{12,16},{16,20},{20,24},{24,28},{1,5},{5,9},{9,... | collective-permute-start | bytes 1572872 | tf_op jit(solution)/shard_map/ppermute | solution.py:445
  15.5 9.2 %copy-start.7 = (bf16[128,2048]{1,0:T(8,128)(2,1)S(1)}, bf16[128,2048]{1,0:T(8,128)(2,1)}, u32[]{:S(2)}) copy-start(bf16[128,2048]{1,0:T(8,128)(2,1)} %refs_5_.4) | copy-start | bytes 1572868
  15.6 9.2 %copy-start.8 = (bf16[128,2048]{1,0:T(8,128)(2,1)S(1)}, bf16[128,2048]{1,0:T(8,128)(2,1)}, u32[]{:S(2)}) copy-start(bf16[128,2048]{1,0:T(8,128)(2,1)} %refs_0_.5) | copy-start | bytes 1572868
  15.6 9.2 %copy-start.9 = (bf16[128,2048]{1,0:T(8,128)(2,1)S(1)}, bf16[128,2048]{1,0:T(8,128)(2,1)}, u32[]{:S(2)}) copy-start(bf16[128,2048]{1,0:T(8,128)(2,1)} %refs_1_.18) | copy-start | bytes 1572868
  15.6 9.2 %copy-start.12 = (bf16[2048,128]{1,0:T(8,128)(2,1)S(1)}, bf16[2048,128]{1,0:T(8,128)(2,1)}, u32[]{:S(2)}) copy-start(bf16[2048,128]{1,0:T(8,128)(2,1)} %refs_4_.4) | copy-start | bytes 1572868
  15.6 9.2 %copy-start.19 = (bf16[2,256,256]{2,1,0:T(8,128)(2,1)S(1)}, bf16[2,256,256]{2,1,0:T(8,128)(2,1)}, u32[]{:S(2)}) copy-start(bf16[2,256,256]{2,1,0:T(8,128)(2,1)} %constant.23.clone.refs_5_.refs_4_) | copy-start | bytes 786436
  17.7 11.5 %collective-permute-start.3 = (bf16[128,2048]{1,0:T(8,128)(2,1)S(1)}, bf16[128,2048]{1,0:T(8,128)(2,1)S(1)}, u32[]{:S(2)}, u32[]{:S(2)}) collective-permute-start(bf16[128,2048]{1,0:T(8,128)(2,1)S(1)} %collective-permute-done.2.refs_3_.refs_4_), channel_id=1, source_target_pairs={{0,1},{1,0},{2,3},{3,2},{4,5},{5,4},{6,7},{7,6},{8,9},{9,8},{10,11... | collective-permute-start | bytes 1572872 | tf_op jit(solution)/shard_map/ppermute | solution.py:343
  31.2 18.8 %collective-permute-start.4 = (bf16[176,2048]{1,0:T(8,128)(2,1)}, bf16[176,2048]{1,0:T(8,128)(2,1)S(1)}, u32[]{:S(2)}, u32[]{:S(2)}) collective-permute-start(bf16[176,2048]{1,0:T(8,128)(2,1)} %get-tuple-element.46), channel_id=1, source_target_pairs={{0,8},{8,16},{16,24},{24,28},{28,20},{20,12},{12,4},{4,0},{1,9},{9... | collective-permute-start | bytes 2162696 | tf_op jit(solution)/shard_map/ppermute | solution.py:489
  33.0 18.5 %collective-permute-start.5 = (bf16[176,2048]{1,0:T(8,128)(2,1)}, bf16[176,2048]{1,0:T(8,128)(2,1)S(1)}, u32[]{:S(2)}, u32[]{:S(2)}) collective-permute-start(bf16[176,2048]{1,0:T(8,128)(2,1)} %get-tuple-element.47), channel_id=1, source_target_pairs={{8,0},{16,8},{24,16},{28,24},{20,28},{12,20},{4,12},{0,4},{9,1},{1... | collective-permute-start | bytes 2162696 | tf_op jit(solution)/shard_map/ppermute | solution.py:489
  49.9 3.7 %collective-permute-start.7 = (bf16[128,2048]{1,0:T(8,128)(2,1)}, bf16[128,2048]{1,0:T(8,128)(2,1)}, u32[]{:S(2)}, u32[]{:S(2)}) collective-permute-start(bf16[128,2048]{1,0:T(8,128)(2,1)} %get-tuple-element.49), channel_id=1, source_target_pairs={{0,1},{1,0},{2,3},{3,2},{4,5},{5,4},{6,7},{7,6},{8,9},{9,8},{10,11... | collective-permute-start | bytes 1572872 | tf_op jit(solution)/shard_map/ppermute | solution.py:343
  50.0 19.4 %copy-start = (bf16[176,2048]{1,0:T(8,128)(2,1)}, bf16[176,2048]{1,0:T(8,128)(2,1)S(1)}, u32[]{:S(2)}) copy-start(bf16[176,2048]{1,0:T(8,128)(2,1)S(1)} %collective-permute-done.4.refs_6_.refs_4_) | copy-start | bytes 2162692
  51.5 17.9 %copy-start.2 = (bf16[176,2048]{1,0:T(8,128)(2,1)}, bf16[176,2048]{1,0:T(8,128)(2,1)S(1)}, u32[]{:S(2)}) copy-start(bf16[176,2048]{1,0:T(8,128)(2,1)S(1)} %collective-permute-done.5.refs_7_.refs_5_) | copy-start | bytes 2162692
  51.5 23.6 %collective-permute-start.8 = (bf16[160,2048]{1,0:T(8,128)(2,1)S(1)}, bf16[160,2048]{1,0:T(8,128)(2,1)S(1)}, u32[]{:S(2)}, u32[]{:S(2)}) collective-permute-start(bf16[160,2048]{1,0:T(8,128)(2,1)S(1)} %slice.82), channel_id=1, source_target_pairs={{0,8},{8,16},{16,24},{24,28},{28,20},{20,12},{12,4},{4,0},{1,9},{9... | collective-permute-start | bytes 1966088 | tf_op jit(solution)/shard_map/ppermute | solution.py:489
  53.2 22.0 %collective-permute-start.9 = (bf16[160,2048]{1,0:T(8,128)(2,1)S(1)}, bf16[160,2048]{1,0:T(8,128)(2,1)S(1)}, u32[]{:S(2)}, u32[]{:S(2)}) collective-permute-start(bf16[160,2048]{1,0:T(8,128)(2,1)S(1)} %slice.83), channel_id=1, source_target_pairs={{8,0},{16,8},{24,16},{28,24},{20,28},{12,20},{4,12},{0,4},{9,1},{1... | collective-permute-start | bytes 1966088 | tf_op jit(solution)/shard_map/ppermute | solution.py:489
  64.1 45.9 %collective-permute-start.6 = (bf16[128,2048]{1,0:T(8,128)(2,1)S(1)}, bf16[128,2048]{1,0:T(8,128)(2,1)S(1)}, u32[]{:S(2)}, u32[]{:S(2)}) collective-permute-start(bf16[128,2048]{1,0:T(8,128)(2,1)S(1)} %mixed_part.2.refs_3_), channel_id=1, source_target_pairs={{0,1},{1,0},{2,3},{3,2},{4,5},{5,4},{6,7},{7,6},{8,9},{9,8},{10,11... | collective-permute-start | bytes 1572872 | tf_op jit(solution)/shard_map/ppermute | solution.py:343
  64.2 11.0 %collective-permute-start.14 = (bf16[16,2048]{1,0:T(8,128)(2,1)S(1)}, bf16[16,2048]{1,0:T(8,128)(2,1)S(1)}, u32[]{:S(2)}, u32[]{:S(2)}) collective-permute-start(bf16[16,2048]{1,0:T(8,128)(2,1)S(1)} %get-tuple-element.58), channel_id=1, source_target_pairs={{0,28},{8,20},{16,12},{24,4},{28,0},{20,8},{12,16},{4,24},{1,29},{... | collective-permute-start | bytes 196616 | tf_op jit(solution)/shard_map/ppermute | solution.py:518
  67.7 24.4 %collective-permute-start.13 = (bf16[1024,128]{1,0:T(8,128)(2,1)S(1)}, bf16[1024,128]{1,0:T(8,128)(2,1)S(1)}, u32[]{:S(2)}, u32[]{:S(2)}) collective-permute-start(bf16[1024,128]{1,0:T(8,128)(2,1)S(1)} %get-tuple-element.82), channel_id=1, source_target_pairs={{0,4},{4,0},{8,12},{12,8},{16,20},{20,16},{24,28},{28,24},{1,5},{5... | collective-permute-start | bytes 786440 | tf_op jit(solution)/shard_map/ppermute | solution.py:343
  75.3 15.2 %collective-permute-start.11 = (bf16[144,2048]{1,0:T(8,128)(2,1)S(1)}, bf16[144,2048]{1,0:T(8,128)(2,1)S(1)}, u32[]{:S(2)}, u32[]{:S(2)}) collective-permute-start(bf16[144,2048]{1,0:T(8,128)(2,1)S(1)} %slice.84), channel_id=1, source_target_pairs={{0,8},{8,16},{16,24},{24,28},{28,20},{20,12},{12,4},{4,0},{1,9},{9... | collective-permute-start | bytes 1769480 | tf_op jit(solution)/shard_map/ppermute | solution.py:489
  75.4 15.2 %collective-permute-start.12 = (bf16[144,2048]{1,0:T(8,128)(2,1)S(1)}, bf16[144,2048]{1,0:T(8,128)(2,1)S(1)}, u32[]{:S(2)}, u32[]{:S(2)}) collective-permute-start(bf16[144,2048]{1,0:T(8,128)(2,1)S(1)} %slice.85), channel_id=1, source_target_pairs={{8,0},{16,8},{24,16},{28,24},{20,28},{12,20},{4,12},{0,4},{9,1},{1... | collective-permute-start | bytes 1769480 | tf_op jit(solution)/shard_map/ppermute | solution.py:489
  77.5 16.0 %collective-permute-start.15 = (bf16[64,2048]{1,0:T(8,128)(2,1)S(1)}, bf16[64,2048]{1,0:T(8,128)(2,1)S(1)}, u32[]{:S(2)}, u32[]{:S(2)}) collective-permute-start(bf16[64,2048]{1,0:T(8,128)(2,1)S(1)} %get-tuple-element.89.refs_10_), channel_id=1, source_target_pairs={{0,2},{1,3},{2,0},{3,1},{4,6},{5,7},{6,4},{7,5},{8,10},{9,11},{10,... | collective-permute-start | bytes 786440 | tf_op jit(solution)/shard_map/ppermute | solution.py:343
  90.6 9.3 %collective-permute-start.22 = (bf16[64,2048]{1,0:T(8,128)(2,1)S(1)}, bf16[64,2048]{1,0:T(8,128)(2,1)S(1)}, u32[]{:S(2)}, u32[]{:S(2)}) collective-permute-start(bf16[64,2048]{1,0:T(8,128)(2,1)S(1)} %pad_maximum_fusion.2.refs_11_), channel_id=1, source_target_pairs={{0,2},{1,3},{2,0},{3,1},{4,6},{5,7},{6,4},{7,5},{8,10},{9,11},{10,... | collective-permute-start | bytes 786440 | tf_op jit(solution)/shard_map/ppermute | solution.py:343
  92.8 17.3 %collective-permute-start.10 = (bf16[128,2048]{1,0:T(8,128)(2,1)S(1)}, bf16[128,2048]{1,0:T(8,128)(2,1)S(1)}, u32[]{:S(2)}, u32[]{:S(2)}) collective-permute-start(bf16[128,2048]{1,0:T(8,128)(2,1)S(1)} %convert_add_fusion), channel_id=1, source_target_pairs={{0,2},{1,3},{2,0},{3,1},{4,6},{5,7},{6,4},{7,5},{8,10},{9,11},{10,... | collective-permute-start | bytes 1572872 | tf_op jit(solution)/shard_map/ppermute | solution.py:343
  93.5 6.7 %collective-permute-start.17 = (bf16[64,2048]{1,0:T(8,128)(2,1)S(1)}, bf16[64,2048]{1,0:T(8,128)(2,1)S(1)}, u32[]{:S(2)}, u32[]{:S(2)}) collective-permute-start(bf16[64,2048]{1,0:T(8,128)(2,1)S(1)} %slice.75), channel_id=1, source_target_pairs={{8,0},{16,8},{24,16},{28,24},{20,28},{12,20},{4,12},{0,4},{9,1},{1... | collective-permute-start | bytes 786440 | tf_op jit(solution)/shard_map/ppermute | solution.py:543
  95.3 6.4 %collective-permute-start.16 = (bf16[64,2048]{1,0:T(8,128)(2,1)S(1)}, bf16[64,2048]{1,0:T(8,128)(2,1)S(1)}, u32[]{:S(2)}, u32[]{:S(2)}) collective-permute-start(bf16[64,2048]{1,0:T(8,128)(2,1)S(1)} %slice.74), channel_id=1, source_target_pairs={{0,8},{8,16},{16,24},{24,28},{28,20},{20,12},{12,4},{4,0},{1,9},{9... | collective-permute-start | bytes 786440 | tf_op jit(solution)/shard_map/ppermute | solution.py:543
  101.7 16.0 %collective-permute-start.23 = (bf16[256,2048]{1,0:T(8,128)(2,1)S(1)}, bf16[256,2048]{1,0:T(8,128)(2,1)S(1)}, u32[]{:S(2)}, u32[]{:S(2)}) collective-permute-start(bf16[256,2048]{1,0:T(8,128)(2,1)S(1)} %constant_dynamic-update-slice_fusion.4), channel_id=1, source_target_pairs={{0,1},{1,0},{2,3},{3,2},{4,5},{5,4},{6,7},{7,6},{8,9},{9,8},{10,11... | collective-permute-start | bytes 3145736 | tf_op jit(solution)/shard_map/ppermute | solution.py:343
  101.7 5.9 %collective-permute-start.19 = (bf16[512,128]{1,0:T(8,128)(2,1)S(1)}, bf16[512,128]{1,0:T(8,128)(2,1)S(1)}, u32[]{:S(2)}, u32[]{:S(2)}) collective-permute-start(bf16[512,128]{1,0:T(8,128)(2,1)S(1)} %get-tuple-element.68), channel_id=1, source_target_pairs={{0,8},{4,12},{8,0},{12,4},{16,24},{20,28},{24,16},{28,20},{1,9},{5... | collective-permute-start | bytes 393224 | tf_op jit(solution)/shard_map/ppermute | solution.py:343
  108.1 8.8 %collective-permute-start.20 = (bf16[512,128]{1,0:T(8,128)(2,1)S(1)}, bf16[512,128]{1,0:T(8,128)(2,1)S(1)}, u32[]{:S(2)}, u32[]{:S(2)}) collective-permute-start(bf16[512,128]{1,0:T(8,128)(2,1)S(1)} %added.4.refs_1_), channel_id=1, source_target_pairs={{0,16},{4,20},{8,24},{12,28},{16,0},{20,4},{24,8},{28,12},{1,17},{... | collective-permute-start | bytes 393224 | tf_op jit(solution)/shard_map/ppermute | solution.py:343
  108.6 21.8 %collective-permute-start.18 = (bf16[128,2048]{1,0:T(8,128)(2,1)S(1)}, bf16[128,2048]{1,0:T(8,128)(2,1)S(1)}, u32[]{:S(2)}, u32[]{:S(2)}) collective-permute-start(bf16[128,2048]{1,0:T(8,128)(2,1)S(1)} %copy-done.15), channel_id=1, source_target_pairs={{4,0},{8,4},{12,8},{16,12},{20,16},{24,20},{28,24},{5,1},{9,5},{13... | collective-permute-start | bytes 1572872 | tf_op jit(solution)/shard_map/ppermute | solution.py:550
  117.6 12.2 %collective-permute-start.21 = (bf16[512,128]{1,0:T(8,128)(2,1)S(1)}, bf16[512,128]{1,0:T(8,128)(2,1)S(1)}, u32[]{:S(2)}, u32[]{:S(2)}) collective-permute-start(bf16[512,128]{1,0:T(8,128)(2,1)S(1)} %added.5.refs_1_), channel_id=1, source_target_pairs={{0,8},{4,12},{8,0},{12,4},{16,24},{20,28},{24,16},{28,20},{1,9},{5... | collective-permute-start | bytes 393224 | tf_op jit(solution)/shard_map/ppermute | solution.py:343
  130.3 9.1 %collective-permute-start.24 = (bf16[1024,128]{1,0:T(8,128)(2,1)S(1)}, bf16[1024,128]{1,0:T(8,128)(2,1)S(1)}, u32[]{:S(2)}, u32[]{:S(2)}) collective-permute-start(bf16[1024,128]{1,0:T(8,128)(2,1)S(1)} %joined.2.refs_1_), channel_id=1, source_target_pairs={{0,4},{4,0},{8,12},{12,8},{16,20},{20,16},{24,28},{28,24},{1,5},{5... | collective-permute-start | bytes 786440 | tf_op jit(solution)/shard_map/ppermute | solution.py:343
  (19 other events, 88.4 us)

commit v16 on v15

--- a/solution.py
+++ b/solution.py
@@ -398,10 +398,11 @@
         self.step = 0
         self.sums, self.send = split(me, partial, self.bits[0])
 
-    def add(self, after):
+    def add(self, after, kernels=()):
         if self.step == len(self.bits):
             return []
         came = swap(self.send if self.step < 2 else self.sums, "ctx", self.bits[self.step])
+        came = held_until([came], kernels)[0]
         self.sums, *send = added(self.me, self.sums, came, 0 if self.step else self.bits[1], after)
         self.send = send[0] if send else None
         self.step += 1
@@ -521,15 +522,17 @@
         [(order[i], order[(i + turns) % n_ctx]) for i in range(n_ctx)],
     )
     brought.insert(1, across)
-    last_part = weight_pass(me, out_weight, 0, gated, after=[mixed_one])[0]
     tap_sum = Sum(me, held_until([tap_grad], [mixed_one])[0])
-    previous, landed = landed, passed_on([last_part])
+    previous, landed = landed, passed_on([mixed_one])
+    last_part = weight_pass(me, out_weight, 0, gated, after=landed + [mixed_one])[0]
 
     terms = dict(zip(terms, held_until(terms.values(), previous)))
     terms[0] = last_part + swap(mixed_one, "chan", 1).astype(F32)
+    to_chips = []
     for bit in bits_of(n_chan)[1:]:
         for off in [off for off in sorted(terms, reverse=True) if off & bit]:
-            terms[off ^ bit] = terms[off ^ bit] + swap(terms.pop(off).astype(BF16), "chan", bit).astype(F32)
+            to_chips.append(terms.pop(off).astype(BF16))
+            terms[off ^ bit] = terms[off ^ bit] + swap(to_chips[-1], "chan", bit).astype(F32)
     mixed = terms[0].astype(BF16)
     early = 2 + 2 * min(1, turns - 1)
     first = jnp.concatenate(held_until(brought[:early], previous), axis=0)
@@ -538,8 +541,7 @@
         landed = passed_on([last_part])
     half = length // 2
     cols = [gather_of_chips(first)]
-    onto, back = held_until(ends, tap_sum.add([last_part]) + [cols[0][off] for off in cols[0] if off])
-    tap_sum.add(landed)
+    onto, back = held_until(ends, tap_sum.add((), landed) + [cols[0][off] for off in cols[0] if off] + to_chips[:1])
     far = [lax.ppermute(onto[:half], "ctx", ahead), lax.ppermute(back[half:], "ctx", behind)]
     arrays = arrays[:1] + far + arrays[1:]
     places.insert(1, [(0, half), (0, half)])
@@ -548,24 +550,12 @@
 
     given = held_until([grad_filtered], far)[0]
     following = lax.ppermute(given, "ctx", [(i + 1, i) for i in range(n_ctx - 1)])
-    grad_key, grad_value = by_channel(
-        backward_kernel,
-        [key_proj, value_proj, grad_filtered, following, filters, forward, early_rows],
-        "ttttcww",
-        [("t", BF16), ("t", BF16)],
-        "backward_filter",
-    )
-
-    while tap_sum.add(far):
-        pass
-    own, bits = tap_sum.sums, tap_sum.bits
-    other = swap(own, "ctx", bits[1])
 
     evens = [off for off in range(n_chan) if off % 2 == 0]
     wide = piece % 128 == 0 and 2 * early == n_ctx
     columns = {off: [(part[off], 0) for part in cols] for off in evens}
     crossed = jnp.concatenate([part[off] for off in evens for part in cols], axis=0)
-    crossed = swap(held_until([crossed], far)[0], "chan", 1)
+    crossed = swap(held_until([crossed], far + [last_part])[0], "chan", 1)
     if wide:
         for at, off in enumerate(evens):
             columns[off + 1] = [(crossed, 2 * at), (crossed, 2 * at + 1)]
@@ -577,9 +567,24 @@
             columns[off + 1] = [(crossed[at * length : (at + 1) * length], 0)]
         pairs = [[array for array, unused in columns[off]] for off in range(n_chan)]
         low_half = grad_weight = narrow_grad_weight(me, arrays, places, pairs)
-    own = joined(me, own, held_until([other], [low_half])[0], bits[1], BF16, ())
-    other = swap(own, "ctx", bits[0])
-    grad_filters = joined(me, own, held_until([other], [grad_weight])[0], bits[0], F32, ())
+
+    tap_sum.add((), [low_half])
+    while tap_sum.add((), [grad_weight]):
+        pass
+    own, bits = tap_sum.sums, tap_sum.bits
+    grad_key, grad_value = by_channel(
+        backward_kernel,
+        [
+            key_proj, value_proj, grad_filtered, held_until([following], [grad_weight])[0],
+            filters, forward, early_rows,
+        ],
+        "ttttcww",
+        [("t", BF16), ("t", BF16)],
+        "backward_filter",
+    )
+    other = held_until([swap(own, "ctx", bits[1])], [grad_key])[0]
+    own = joined(me, own, other, bits[1], BF16, ())
+    grad_filters = joined(me, own, swap(own, "ctx", bits[0]), bits[0], F32, ())
     return (mixed, grad_query, grad_key, grad_value, grad_filters, grad_weight)
 
 

time: 142 us -> 144 us (1.014)
  starting transfers between devices: 26 us -> 30.4 us
  waiting for transfers between devices: 39.5 us -> 37.2 us
    ppermute x14, starting transfers between devices: 9.33 us -> 13.8 us  [swap(): return lax.ppermute(block, axis, [(i, i ^ bit) for i in range(size)])]
    ppermute x14, waiting for transfers between devices: 24.9 us -> 21 us  [swap(): return lax.ppermute(block, axis, [(i, i ^ bit) for i in range(size)])]
    ppermute x1, waiting for transfers between devices: 0.01 us -> 2.83 us  [per_device(): lax.ppermute(held_until([pieces[rows:2 * rows]], [mixed_one])[0], 'ctx',...]
  transfers between devices with their start and end apart: 25 -> 25, of which waited for: 10 -> 9; matrix products, arithmetic and copies ran while one was open for 2% -> 2% of each run, Pallas kernels for 45% -> 44%
where the time goes in v16:
time: 144 us
  Pallas kernels  65.4 us (45%)
  waiting for transfers between devices  37.2 us (26%)
  starting transfers between devices  30.4 us (21%)
  other arithmetic  5.75 us (4%)
  local copies, waits for them, and re-layouts  3.63 us (3%)
    pallas_call x6, Pallas kernels, weight_pass(): pl.pallas_call(ignoring(body, len(after), 1 + len(arrays)), grid_spec=plt...  39.9 us
    ppermute x14, waiting for transfers between devices, swap(): return lax.ppermute(block, axis, [(i, i ^ bit) for i in range(size)])  21 us
    ppermute x14, starting transfers between devices, swap(): return lax.ppermute(block, axis, [(i, i ^ bit) for i in range(size)])  13.8 us
    ppermute x6, waiting for transfers between devices, passed_on(): came = [lax.ppermute(onto, 'ctx', ahead), lax.ppermute(back, 'ctx', behind)]  13.4 us
    pallas_call x3, Pallas kernels, by_channel(): pl.pallas_call(ignoring(functools.partial(kernel, length), len(after), le...  10.8 us
    pallas_call x2, Pallas kernels, grad_weight_of(): pl.pallas_call(ignoring(functools.partial(weight_kernel, places, parts),...  10 us
    ppermute x6, starting transfers between devices, passed_on(): came = [lax.ppermute(onto, 'ctx', ahead), lax.ppermute(back, 'ctx', behind)]  6.18 us
    ppermute x1, starting transfers between devices, per_device(): lax.ppermute(held_until([pieces[rows:2 * rows]], [mixed_one])[0], 'ctx',...  3.5 us
  transfers between devices with their start and end apart: 25, of which 9 were waited for; matrix products, arithmetic and copies ran while one was open for 2% of the time, Pallas kernels for 44%

profile of v16, /device:TPU:0, one launch (start us, length us, event | category | flops | bytes accessed | tf_op | source)
XLA Modules:
  0.0 143.7 jit_solution(1655932870788804442)
XLA Ops:
  0.6 2.2 %multiply_convert_fusion = bf16[128,2048]{1,0:T(8,128)(2,1)} fusion(bf16[128,2048]{1,0:T(8,128)(2,1)} %refs_1_.18, bf16[128,2048]{1,0:T(8,128)(2,1)} %refs_0_.5), kind=kLoop, calls=%fused_computation.2 | loop fusion | flops 1048576 | bytes 1572864 | tf_op jit(solution)/shard_map/convert_element_type | solution.py:444
  2.8 2.9 %collective-permute-start.2 = (bf16[128,2048]{1,0:T(8,128)(2,1)S(1)}, bf16[128,2048]{1,0:T(8,128)(2,1)S(1)}, u32[]{:S(2)}, u32[]{:S(2)}) collective-permute-start(bf16[128,2048]{1,0:T(8,128)(2,1)S(1)} %copy-done.8), channel_id=1, source_target_pairs={{0,2},{1,3},{2,0},{3,1},{4,6},{5,7},{6,4},{7,5},{8,10},{9,11},{10,... | collective-permute-start | bytes 1572872 | tf_op jit(solution)/shard_map/ppermute | solution.py:343
  5.8 3.4 %collective-permute-start = (bf16[128,2048]{1,0:T(8,128)(2,1)}, bf16[128,2048]{1,0:T(8,128)(2,1)S(1)}, u32[]{:S(2)}, u32[]{:S(2)}) collective-permute-start(bf16[128,2048]{1,0:T(8,128)(2,1)} %multiply_convert_fusion), channel_id=1, source_target_pairs={{0,4},{4,8},{8,12},{12,16},{16,20},{20,24},{24,28},{1,5},{5,9},{9,... | collective-permute-start | bytes 1572872 | tf_op jit(solution)/shard_map/ppermute | solution.py:446
  9.3 6.2 %grad_gated_part.2.refs_3_ = f32[2048,128]{1,0:T(8,128)S(1)} custom-call(s32[2]{0:T(128)S(1)} %pad_add_fusion.refs_0_, bf16[2048,8192]{1,0:T(8,128)(2,1)} %refs_1_.17, bf16[128,2048]{1,0:T(8,128)(2,1)S(1)} %copy-done.8), custom_call_target="tpu_custom_call" | custom-call | flops 3000000000 | tf_op jit(solution)/shard_map/grad_gated_part/pallas_call | solution.py:190
  15.6 2.1 %collective-permute-done.2.refs_4_.refs_3_ = bf16[128,2048]{1,0:T(8,128)(2,1)S(1)} collective-permute-done((bf16[128,2048]{1,0:T(8,128)(2,1)S(1)}, bf16[128,2048]{1,0:T(8,128)(2,1)S(1)}, u32[]{:S(2)}, u32[]{:S(2)}) %collective-permute-start.2) | collective-permute-done | bytes 524320 | tf_op jit(solution)/shard_map/ppermute | solution.py:343
  17.7 6.3 %grad_gated_part.3.refs_7_.refs_6_.refs_4_ = f32[2048,128]{1,0:T(8,128)S(1)} custom-call(s32[2]{0:T(128)S(1)} %pad_add_fusion.refs_0_, bf16[2048,8192]{1,0:T(8,128)(2,1)} %refs_1_.17, bf16[128,2048]{1,0:T(8,128)(2,1)S(1)} %collective-permute-done.1.refs_2_.refs_3_, f32[2048,128]{1,0:T(8,128)S(1)} %grad_gated_part.2.refs_3_), custom_call_target="tpu_custom_call" | custom-call | flops 3000000000 | tf_op jit(solution)/shard_map/grad_gated_part/pallas_call | solution.py:190
  25.9 3.3 %forward_filter.1 = (bf16[128,2048]{1,0:T(8,128)(2,1)S(1)}, f32[128,2048]{1,0:T(8,128)S(1)}) custom-call(bf16[128,2048]{1,0:T(8,128)(2,1)S(1)} %copy-done.11, bf16[128,2048]{1,0:T(8,128)(2,1)S(1)} %copy-done.12, bf16[128,2048]{1,0:T(8,128)(2,1)S(1)} %copy-done.13, bf16[128,2048]{1,0:T(8,128)(2,1)S(1)} %copy-done.21, bf16[2048,128]{1,0:T(8,128)(2,1)S(1)} %copy-done.16, ...), custom_call_target="tpu_custom_call" | custom-call | flops 3000000000 | tf_op jit(solution)/shard_map/forward_filter/pallas_call | solution.py:107
  31.2 1.8 %collective-permute-start.4 = (bf16[176,2048]{1,0:T(8,128)(2,1)}, bf16[176,2048]{1,0:T(8,128)(2,1)S(1)}, u32[]{:S(2)}, u32[]{:S(2)}) collective-permute-start(bf16[176,2048]{1,0:T(8,128)(2,1)} %get-tuple-element.46), channel_id=1, source_target_pairs={{0,8},{8,16},{16,24},{24,28},{28,20},{20,12},{12,4},{4,0},{1,9},{9... | collective-permute-start | bytes 2162696 | tf_op jit(solution)/shard_map/ppermute | solution.py:490
  33.2 7.4 %grads_and_mixed.2 = (f32[2048,128]{1,0:T(8,128)S(1)}, f32[128,2048]{1,0:T(8,128)S(1)}) custom-call(s32[2]{0:T(128)S(1)} %pad_add_fusion.refs_0_, bf16[2048,8192]{1,0:T(8,128)(2,1)} %refs_1_.17, bf16[128,2048]{1,0:T(8,128)(2,1)S(1)} %get-tuple-element.44.refs_2_.refs_1_, bf16[128,2048]{1,0:T(8,128)(2,1)S(1)} %collective-permute-done.2.refs_4_.refs_3_, ...), custom_call_target="tpu_custom_call" | custom-call | flops 500000000 | tf_op jit(solution)/shard_map/grads_and_mixed/pallas_call | solution.py:190
  40.7 8.5 %grads_and_mixed.3 = (bf16[128,2048]{1,0:T(8,128)(2,1)}, bf16[128,2048]{1,0:T(8,128)(2,1)S(1)}, bf16[128,2048]{1,0:T(8,128)(2,1)}) custom-call(s32[2]{0:T(128)S(1)} %pad_add_fusion.refs_0_, bf16[2048,8192]{1,0:T(8,128)(2,1)} %refs_1_.17, bf16[128,2048]{1,0:T(8,128)(2,1)S(1)} %get-tuple-element.44.refs_2_.refs_1_, ...), custom_call_target="tpu_custom_call" | custom-call | flops 500000000 | tf_op jit(solution)/shard_map/grads_and_mixed/pallas_call | solution.py:190
  51.6 1.6 %collective-permute-start.6 = (bf16[160,2048]{1,0:T(8,128)(2,1)S(1)}, bf16[160,2048]{1,0:T(8,128)(2,1)S(1)}, u32[]{:S(2)}, u32[]{:S(2)}) collective-permute-start(bf16[160,2048]{1,0:T(8,128)(2,1)S(1)} %slice.82), channel_id=1, source_target_pairs={{0,8},{8,16},{16,24},{24,28},{28,20},{20,12},{12,4},{4,0},{1,9},{9... | collective-permute-start | bytes 1966088 | tf_op jit(solution)/shard_map/ppermute | solution.py:490
  54.9 3.5 %tap_grad.1.refs_3_ = bf16[2048,128]{1,0:T(8,128)(2,1)S(1)} custom-call(bf16[128,2048]{1,0:T(8,128)(2,1)S(1)} %copy-done.12, bf16[128,2048]{1,0:T(8,128)(2,1)S(1)} %copy-done.14, bf16[128,2048]{1,0:T(8,128)(2,1)S(1)} %copy-done.22, bf16[128,2048]{1,0:T(8,128)(2,1)S(1)} %copy-done.19, bf16[2,256,256]{2,1,0:T(8,128)(2,1)S(1)} %copy-done.24, ...), custom_call_target="tpu_custom_call" | custom-call | flops 3000000000 | tf_op jit(solution)/shard_map/tap_grad/pallas_call | solution.py:107
  58.4 5.7 %mixed_part.2.refs_5_ = bf16[128,2048]{1,0:T(8,128)(2,1)S(1)} custom-call(s32[2]{0:T(128)S(1)} %pad_add_fusion.refs_0_, bf16[2048,8192]{1,0:T(8,128)(2,1)} %refs_1_.17, bf16[128,2048]{1,0:T(8,128)(2,1)S(1)} %get-tuple-element.44.refs_2_.refs_1_, bf16[2048,128]{1,0:T(8,128)(2,1)S(1)} %tap_grad.1.refs_3_), custom_call_target="tpu_custom_call" | custom-call | flops 500000000 | tf_op jit(solution)/shard_map/mixed_part/pallas_call | solution.py:190
  64.1 3.5 %collective-permute-start.14 = (bf16[16,2048]{1,0:T(8,128)(2,1)S(1)}, bf16[16,2048]{1,0:T(8,128)(2,1)S(1)}, u32[]{:S(2)}, u32[]{:S(2)}) collective-permute-start(bf16[16,2048]{1,0:T(8,128)(2,1)S(1)} %get-tuple-element.62), channel_id=1, source_target_pairs={{0,28},{8,20},{16,12},{24,4},{28,0},{20,8},{12,16},{4,24},{1,29},{... | collective-permute-start | bytes 196616 | tf_op jit(solution)/shard_map/ppermute | solution.py:519
  67.7 1.6 %collective-permute-start.13 = (bf16[1024,128]{1,0:T(8,128)(2,1)S(1)}, bf16[1024,128]{1,0:T(8,128)(2,1)S(1)}, u32[]{:S(2)}, u32[]{:S(2)}) collective-permute-start(bf16[1024,128]{1,0:T(8,128)(2,1)S(1)} %get-tuple-element.88), channel_id=1, source_target_pairs={{0,4},{4,0},{8,12},{12,8},{16,20},{20,16},{24,28},{28,24},{1,5},{5... | collective-permute-start | bytes 786440 | tf_op jit(solution)/shard_map/ppermute | solution.py:343
  69.3 2.8 %collective-permute-done.14 = bf16[16,2048]{1,0:T(8,128)(2,1)S(1)} collective-permute-done((bf16[16,2048]{1,0:T(8,128)(2,1)S(1)}, bf16[16,2048]{1,0:T(8,128)(2,1)S(1)}, u32[]{:S(2)}, u32[]{:S(2)}) %collective-permute-start.14) | collective-permute-done | bytes 65568 | tf_op jit(solution)/shard_map/ppermute | solution.py:519
  74.4 1.6 %collective-permute-start.15 = (bf16[64,2048]{1,0:T(8,128)(2,1)S(1)}, bf16[64,2048]{1,0:T(8,128)(2,1)S(1)}, u32[]{:S(2)}, u32[]{:S(2)}) collective-permute-start(bf16[64,2048]{1,0:T(8,128)(2,1)S(1)} %get-tuple-element.95.refs_10_), channel_id=1, source_target_pairs={{0,2},{1,3},{2,0},{3,1},{4,6},{5,7},{6,4},{7,5},{8,10},{9,11},{10,... | collective-permute-start | bytes 786440 | tf_op jit(solution)/shard_map/ppermute | solution.py:343
  76.1 1.7 %collective-permute-done.13.refs_2_ = bf16[1024,128]{1,0:T(8,128)(2,1)S(1)} collective-permute-done((bf16[1024,128]{1,0:T(8,128)(2,1)S(1)}, bf16[1024,128]{1,0:T(8,128)(2,1)S(1)}, u32[]{:S(2)}, u32[]{:S(2)}) %collective-permute-start.13) | collective-permute-done | bytes 262176 | tf_op jit(solution)/shard_map/ppermute | solution.py:343
  77.7 12.0 %collective-permute-done.8.refs_3_.refs_8_ = bf16[144,2048]{1,0:T(8,128)(2,1)S(1)} collective-permute-done((bf16[144,2048]{1,0:T(8,128)(2,1)S(1)}, bf16[144,2048]{1,0:T(8,128)(2,1)S(1)}, u32[]{:S(2)}, u32[]{:S(2)}) %collective-permute-start.8) | collective-permute-done | bytes 589856 | tf_op jit(solution)/shard_map/ppermute | solution.py:490
  89.8 1.6 %collective-permute-start.19 = (bf16[64,2048]{1,0:T(8,128)(2,1)S(1)}, bf16[64,2048]{1,0:T(8,128)(2,1)S(1)}, u32[]{:S(2)}, u32[]{:S(2)}) collective-permute-start(bf16[64,2048]{1,0:T(8,128)(2,1)S(1)} %pad_maximum_fusion.2.refs_11_), channel_id=1, source_target_pairs={{0,2},{1,3},{2,0},{3,1},{4,6},{5,7},{6,4},{7,5},{8,10},{9,11},{10,... | collective-permute-start | bytes 786440 | tf_op jit(solution)/shard_map/ppermute | solution.py:343
  93.1 1.6 %collective-permute-start.16 = (bf16[64,2048]{1,0:T(8,128)(2,1)S(1)}, bf16[64,2048]{1,0:T(8,128)(2,1)S(1)}, u32[]{:S(2)}, u32[]{:S(2)}) collective-permute-start(bf16[64,2048]{1,0:T(8,128)(2,1)S(1)} %slice.74), channel_id=1, source_target_pairs={{0,8},{8,16},{16,24},{24,28},{28,20},{20,12},{12,4},{4,0},{1,9},{9... | collective-permute-start | bytes 786440 | tf_op jit(solution)/shard_map/ppermute | solution.py:545
  94.8 5.7 %mixed_part.3 = f32[128,2048]{1,0:T(8,128)S(1)} custom-call(s32[2]{0:T(128)S(1)} %pad_add_fusion.refs_0_, bf16[2048,8192]{1,0:T(8,128)(2,1)} %refs_1_.17, bf16[128,2048]{1,0:T(8,128)(2,1)S(1)} %get-tuple-element.44.refs_2_.refs_1_, bf16[144,2048]{1,0:T(8,128)(2,1)S(1)} %copy-done.1, bf16[144,2048]{1,0:T(8,128)(2,1)S(1)} %copy-done.3, ...), custom_call_target="tpu_custom_call" | custom-call | flops 500000000 | tf_op jit(solution)/shard_map/mixed_part/pallas_call | solution.py:190
  100.7 1.5 %collective-permute-start.18 = (bf16[128,2048]{1,0:T(8,128)(2,1)S(1)}, bf16[128,2048]{1,0:T(8,128)(2,1)S(1)}, u32[]{:S(2)}, u32[]{:S(2)}) collective-permute-start(bf16[128,2048]{1,0:T(8,128)(2,1)S(1)} %copy-done.19), channel_id=1, source_target_pairs={{4,0},{8,4},{12,8},{16,12},{20,16},{24,20},{28,24},{5,1},{9,5},{13... | collective-permute-start | bytes 1572872 | tf_op jit(solution)/shard_map/ppermute | solution.py:552
  103.6 2.1 %collective-permute-start.21 = (bf16[512,128]{1,0:T(8,128)(2,1)S(1)}, bf16[512,128]{1,0:T(8,128)(2,1)S(1)}, u32[]{:S(2)}, u32[]{:S(2)}) collective-permute-start(bf16[512,128]{1,0:T(8,128)(2,1)S(1)} %get-tuple-element.74), channel_id=1, source_target_pairs={{0,8},{4,12},{8,0},{12,4},{16,24},{20,28},{24,16},{28,20},{1,9},{5... | collective-permute-start | bytes 393224 | tf_op jit(solution)/shard_map/ppermute | solution.py:343
  105.7 5.0 %grad_weight.2.refs_18_ = bf16[2048,1024]{1,0:T(8,128)(2,1)} custom-call(s32[2]{0:T(128)S(1)} %pad_add_fusion.refs_0_, bf16[128,2048]{1,0:T(8,128)(2,1)S(1)} %get-tuple-element.44.refs_2_.refs_1_, bf16[64,2048]{1,0:T(8,128)(2,1)S(1)} %collective-permute-done.16.refs_2_, bf16[64,2048]{1,0:T(8,128)(2,1)S(1)} %collective-permute-done.17.refs_3_, ...), custom_call_target="tpu_custom_call" | custom-call | flops 2000000000 | tf_op jit(solution)/shard_map/grad_weight/pallas_call | solution.py:293
  110.7 8.8 %collective-permute-done.21.refs_2_ = bf16[512,128]{1,0:T(8,128)(2,1)S(1)} collective-permute-done((bf16[512,128]{1,0:T(8,128)(2,1)S(1)}, bf16[512,128]{1,0:T(8,128)(2,1)S(1)}, u32[]{:S(2)}, u32[]{:S(2)}) %collective-permute-start.21) | collective-permute-done | bytes 131104 | tf_op jit(solution)/shard_map/ppermute | solution.py:343
  120.1 2.2 %collective-permute-start.22 = (bf16[512,128]{1,0:T(8,128)(2,1)S(1)}, bf16[512,128]{1,0:T(8,128)(2,1)S(1)}, u32[]{:S(2)}, u32[]{:S(2)}) collective-permute-start(bf16[512,128]{1,0:T(8,128)(2,1)S(1)} %added.4.refs_1_), channel_id=1, source_target_pairs={{0,16},{4,20},{8,24},{12,28},{16,0},{20,4},{24,8},{28,12},{1,17},{... | collective-permute-start | bytes 393224 | tf_op jit(solution)/shard_map/ppermute | solution.py:343
  122.4 5.0 %grad_weight.3 = bf16[2048,1024]{1,0:T(8,128)(2,1)} custom-call(s32[2]{0:T(128)S(1)} %pad_add_fusion.refs_0_, bf16[128,2048]{1,0:T(8,128)(2,1)S(1)} %get-tuple-element.44.refs_2_.refs_1_, bf16[64,2048]{1,0:T(8,128)(2,1)S(1)} %collective-permute-done.16.refs_2_, ...), custom_call_target="tpu_custom_call", output_to_operand_aliasing={{}: (18, {})} | custom-call | flops 2000000000 | tf_op jit(solution)/shard_map/grad_weight/pallas_call | solution.py:293
  128.7 4.0 %backward_filter.1 = (bf16[128,2048]{1,0:T(8,128)(2,1)}, bf16[128,2048]{1,0:T(8,128)(2,1)}) custom-call(bf16[128,2048]{1,0:T(8,128)(2,1)S(1)} %copy-done.12, bf16[128,2048]{1,0:T(8,128)(2,1)S(1)} %copy-done.14, bf16[128,2048]{1,0:T(8,128)(2,1)S(1)} %copy-done.19, bf16[128,2048]{1,0:T(8,128)(2,1)S(1)} %collective-permute-done.18.refs_3_, ...), custom_call_target="tpu_custom_call" | custom-call | flops 3000000000 | tf_op jit(solution)/shard_map/backward_filter/pallas_call | solution.py:107
  132.6 1.4 collective-permute-done.23.refs_2_
  135.7 6.3 %collective-permute-done.24.refs_2_ = bf16[1024,128]{1,0:T(8,128)(2,1)S(1)} collective-permute-done((bf16[1024,128]{1,0:T(8,128)(2,1)S(1)}, bf16[1024,128]{1,0:T(8,128)(2,1)S(1)}, u32[]{:S(2)}, u32[]{:S(2)}) %collective-permute-start.24) | collective-permute-done | bytes 262176 | tf_op jit(solution)/shard_map/ppermute | solution.py:343
  142.1 1.6 %joined.3 = f32[2048,128]{1,0:T(8,128)} custom-call(s32[2]{0:T(128)S(1)} %pad_add_fusion.refs_0_, bf16[1024,128]{1,0:T(8,128)(2,1)S(1)} %joined.2.refs_1_, bf16[1024,128]{1,0:T(8,128)(2,1)S(1)} %collective-permute-done.24.refs_2_), custom_call_target="tpu_custom_call" | custom-call | flops 500000000 | tf_op jit(solution)/shard_map/joined/pallas_call | solution.py:422
  (124 shorter events, 17.2 us)
Async XLA Ops:
  2.8 14.9 %collective-permute-start.2 = (bf16[128,2048]{1,0:T(8,128)(2,1)S(1)}, bf16[128,2048]{1,0:T(8,128)(2,1)S(1)}, u32[]{:S(2)}, u32[]{:S(2)}) collective-permute-start(bf16[128,2048]{1,0:T(8,128)(2,1)S(1)} %copy-done.8), channel_id=1, source_target_pairs={{0,2},{1,3},{2,0},{3,1},{4,6},{5,7},{6,4},{7,5},{8,10},{9,11},{10,... | collective-permute-start | bytes 1572872 | tf_op jit(solution)/shard_map/ppermute | solution.py:343
  5.8 11.9 %collective-permute-start.1 = (bf16[128,2048]{1,0:T(8,128)(2,1)S(1)}, bf16[128,2048]{1,0:T(8,128)(2,1)S(1)}, u32[]{:S(2)}, u32[]{:S(2)}) collective-permute-start(bf16[128,2048]{1,0:T(8,128)(2,1)S(1)} %copy-done.8), channel_id=1, source_target_pairs={{0,1},{1,0},{2,3},{3,2},{4,5},{5,4},{6,7},{7,6},{8,9},{9,8},{10,11... | collective-permute-start | bytes 1572872 | tf_op jit(solution)/shard_map/ppermute | solution.py:343
  5.8 18.2 %collective-permute-start = (bf16[128,2048]{1,0:T(8,128)(2,1)}, bf16[128,2048]{1,0:T(8,128)(2,1)S(1)}, u32[]{:S(2)}, u32[]{:S(2)}) collective-permute-start(bf16[128,2048]{1,0:T(8,128)(2,1)} %multiply_convert_fusion), channel_id=1, source_target_pairs={{0,4},{4,8},{8,12},{12,16},{16,20},{20,24},{24,28},{1,5},{5,9},{9,... | collective-permute-start | bytes 1572872 | tf_op jit(solution)/shard_map/ppermute | solution.py:446
  15.5 9.2 %copy-start.11 = (bf16[128,2048]{1,0:T(8,128)(2,1)S(1)}, bf16[128,2048]{1,0:T(8,128)(2,1)}, u32[]{:S(2)}) copy-start(bf16[128,2048]{1,0:T(8,128)(2,1)} %refs_5_.4) | copy-start | bytes 1572868
  15.6 9.2 %copy-start.12 = (bf16[128,2048]{1,0:T(8,128)(2,1)S(1)}, bf16[128,2048]{1,0:T(8,128)(2,1)}, u32[]{:S(2)}) copy-start(bf16[128,2048]{1,0:T(8,128)(2,1)} %refs_0_.5) | copy-start | bytes 1572868
  15.6 9.2 %copy-start.13 = (bf16[128,2048]{1,0:T(8,128)(2,1)S(1)}, bf16[128,2048]{1,0:T(8,128)(2,1)}, u32[]{:S(2)}) copy-start(bf16[128,2048]{1,0:T(8,128)(2,1)} %refs_1_.18) | copy-start | bytes 1572868
  17.7 11.5 %collective-permute-start.3 = (bf16[128,2048]{1,0:T(8,128)(2,1)S(1)}, bf16[128,2048]{1,0:T(8,128)(2,1)S(1)}, u32[]{:S(2)}, u32[]{:S(2)}) collective-permute-start(bf16[128,2048]{1,0:T(8,128)(2,1)S(1)} %collective-permute-done.2.refs_4_.refs_3_), channel_id=1, source_target_pairs={{0,1},{1,0},{2,3},{3,2},{4,5},{5,4},{6,7},{7,6},{8,9},{9,8},{10,11... | collective-permute-start | bytes 1572872 | tf_op jit(solution)/shard_map/ppermute | solution.py:343
  31.2 18.8 %collective-permute-start.4 = (bf16[176,2048]{1,0:T(8,128)(2,1)}, bf16[176,2048]{1,0:T(8,128)(2,1)S(1)}, u32[]{:S(2)}, u32[]{:S(2)}) collective-permute-start(bf16[176,2048]{1,0:T(8,128)(2,1)} %get-tuple-element.46), channel_id=1, source_target_pairs={{0,8},{8,16},{16,24},{24,28},{28,20},{20,12},{12,4},{4,0},{1,9},{9... | collective-permute-start | bytes 2162696 | tf_op jit(solution)/shard_map/ppermute | solution.py:490
  33.0 18.5 %collective-permute-start.5 = (bf16[176,2048]{1,0:T(8,128)(2,1)}, bf16[176,2048]{1,0:T(8,128)(2,1)S(1)}, u32[]{:S(2)}, u32[]{:S(2)}) collective-permute-start(bf16[176,2048]{1,0:T(8,128)(2,1)} %get-tuple-element.47), channel_id=1, source_target_pairs={{8,0},{16,8},{24,16},{28,24},{20,28},{12,20},{4,12},{0,4},{9,1},{1... | collective-permute-start | bytes 2162696 | tf_op jit(solution)/shard_map/ppermute | solution.py:490
  50.0 3.7 %collective-permute-start.11 = (bf16[128,2048]{1,0:T(8,128)(2,1)}, bf16[128,2048]{1,0:T(8,128)(2,1)}, u32[]{:S(2)}, u32[]{:S(2)}) collective-permute-start(bf16[128,2048]{1,0:T(8,128)(2,1)} %get-tuple-element.56), channel_id=1, source_target_pairs={{0,1},{1,0},{2,3},{3,2},{4,5},{5,4},{6,7},{7,6},{8,9},{9,8},{10,11... | collective-permute-start | bytes 1572872 | tf_op jit(solution)/shard_map/ppermute | solution.py:343
  50.0 19.3 %copy-start.4 = (bf16[176,2048]{1,0:T(8,128)(2,1)}, bf16[176,2048]{1,0:T(8,128)(2,1)S(1)}, u32[]{:S(2)}) copy-start(bf16[176,2048]{1,0:T(8,128)(2,1)S(1)} %collective-permute-done.4.refs_6_.refs_4_) | copy-start | bytes 2162692
  51.5 17.8 %copy-start.6 = (bf16[176,2048]{1,0:T(8,128)(2,1)}, bf16[176,2048]{1,0:T(8,128)(2,1)S(1)}, u32[]{:S(2)}) copy-start(bf16[176,2048]{1,0:T(8,128)(2,1)S(1)} %collective-permute-done.5.refs_7_.refs_5_) | copy-start | bytes 2162692
  51.6 20.6 %collective-permute-start.6 = (bf16[160,2048]{1,0:T(8,128)(2,1)S(1)}, bf16[160,2048]{1,0:T(8,128)(2,1)S(1)}, u32[]{:S(2)}, u32[]{:S(2)}) collective-permute-start(bf16[160,2048]{1,0:T(8,128)(2,1)S(1)} %slice.82), channel_id=1, source_target_pairs={{0,8},{8,16},{16,24},{24,28},{28,20},{20,12},{12,4},{4,0},{1,9},{9... | collective-permute-start | bytes 1966088 | tf_op jit(solution)/shard_map/ppermute | solution.py:490
  53.2 19.0 %collective-permute-start.7 = (bf16[160,2048]{1,0:T(8,128)(2,1)S(1)}, bf16[160,2048]{1,0:T(8,128)(2,1)S(1)}, u32[]{:S(2)}, u32[]{:S(2)}) collective-permute-start(bf16[160,2048]{1,0:T(8,128)(2,1)S(1)} %slice.83), channel_id=1, source_target_pairs={{8,0},{16,8},{24,16},{28,24},{20,28},{12,20},{4,12},{0,4},{9,1},{1... | collective-permute-start | bytes 1966088 | tf_op jit(solution)/shard_map/ppermute | solution.py:490
  64.1 8.0 %collective-permute-start.14 = (bf16[16,2048]{1,0:T(8,128)(2,1)S(1)}, bf16[16,2048]{1,0:T(8,128)(2,1)S(1)}, u32[]{:S(2)}, u32[]{:S(2)}) collective-permute-start(bf16[16,2048]{1,0:T(8,128)(2,1)S(1)} %get-tuple-element.62), channel_id=1, source_target_pairs={{0,28},{8,20},{16,12},{24,4},{28,0},{20,8},{12,16},{4,24},{1,29},{... | collective-permute-start | bytes 196616 | tf_op jit(solution)/shard_map/ppermute | solution.py:519
  67.7 10.1 %collective-permute-start.13 = (bf16[1024,128]{1,0:T(8,128)(2,1)S(1)}, bf16[1024,128]{1,0:T(8,128)(2,1)S(1)}, u32[]{:S(2)}, u32[]{:S(2)}) collective-permute-start(bf16[1024,128]{1,0:T(8,128)(2,1)S(1)} %get-tuple-element.88), channel_id=1, source_target_pairs={{0,4},{4,0},{8,12},{12,8},{16,20},{20,16},{24,28},{28,24},{1,5},{5... | collective-permute-start | bytes 786440 | tf_op jit(solution)/shard_map/ppermute | solution.py:343
  72.3 17.5 %collective-permute-start.8 = (bf16[144,2048]{1,0:T(8,128)(2,1)S(1)}, bf16[144,2048]{1,0:T(8,128)(2,1)S(1)}, u32[]{:S(2)}, u32[]{:S(2)}) collective-permute-start(bf16[144,2048]{1,0:T(8,128)(2,1)S(1)} %slice.84), channel_id=1, source_target_pairs={{0,8},{8,16},{16,24},{24,28},{28,20},{20,12},{12,4},{4,0},{1,9},{9... | collective-permute-start | bytes 1769480 | tf_op jit(solution)/shard_map/ppermute | solution.py:490
  73.2 16.5 %collective-permute-start.9 = (bf16[144,2048]{1,0:T(8,128)(2,1)S(1)}, bf16[144,2048]{1,0:T(8,128)(2,1)S(1)}, u32[]{:S(2)}, u32[]{:S(2)}) collective-permute-start(bf16[144,2048]{1,0:T(8,128)(2,1)S(1)} %slice.85), channel_id=1, source_target_pairs={{8,0},{16,8},{24,16},{28,24},{20,28},{12,20},{4,12},{0,4},{9,1},{1... | collective-permute-start | bytes 1769480 | tf_op jit(solution)/shard_map/ppermute | solution.py:490
  74.4 17.7 %collective-permute-start.15 = (bf16[64,2048]{1,0:T(8,128)(2,1)S(1)}, bf16[64,2048]{1,0:T(8,128)(2,1)S(1)}, u32[]{:S(2)}, u32[]{:S(2)}) collective-permute-start(bf16[64,2048]{1,0:T(8,128)(2,1)S(1)} %get-tuple-element.95.refs_10_), channel_id=1, source_target_pairs={{0,2},{1,3},{2,0},{3,1},{4,6},{5,7},{6,4},{7,5},{8,10},{9,11},{10,... | collective-permute-start | bytes 786440 | tf_op jit(solution)/shard_map/ppermute | solution.py:343
  89.8 10.7 %collective-permute-start.19 = (bf16[64,2048]{1,0:T(8,128)(2,1)S(1)}, bf16[64,2048]{1,0:T(8,128)(2,1)S(1)}, u32[]{:S(2)}, u32[]{:S(2)}) collective-permute-start(bf16[64,2048]{1,0:T(8,128)(2,1)S(1)} %pad_maximum_fusion.2.refs_11_), channel_id=1, source_target_pairs={{0,2},{1,3},{2,0},{3,1},{4,6},{5,7},{6,4},{7,5},{8,10},{9,11},{10,... | collective-permute-start | bytes 786440 | tf_op jit(solution)/shard_map/ppermute | solution.py:343
  92.6 7.9 %collective-permute-start.17 = (bf16[64,2048]{1,0:T(8,128)(2,1)S(1)}, bf16[64,2048]{1,0:T(8,128)(2,1)S(1)}, u32[]{:S(2)}, u32[]{:S(2)}) collective-permute-start(bf16[64,2048]{1,0:T(8,128)(2,1)S(1)} %slice.75), channel_id=1, source_target_pairs={{8,0},{16,8},{24,16},{28,24},{20,28},{12,20},{4,12},{0,4},{9,1},{1... | collective-permute-start | bytes 786440 | tf_op jit(solution)/shard_map/ppermute | solution.py:545
  93.1 7.5 %collective-permute-start.16 = (bf16[64,2048]{1,0:T(8,128)(2,1)S(1)}, bf16[64,2048]{1,0:T(8,128)(2,1)S(1)}, u32[]{:S(2)}, u32[]{:S(2)}) collective-permute-start(bf16[64,2048]{1,0:T(8,128)(2,1)S(1)} %slice.74), channel_id=1, source_target_pairs={{0,8},{8,16},{16,24},{24,28},{28,20},{20,12},{12,4},{4,0},{1,9},{9... | collective-permute-start | bytes 786440 | tf_op jit(solution)/shard_map/ppermute | solution.py:545
  94.8 10.9 %copy-start.5 = (bf16[176,2048]{1,0:T(8,128)(2,1)S(1)}, bf16[176,2048]{1,0:T(8,128)(2,1)}, u32[]{:S(2)}) copy-start(bf16[176,2048]{1,0:T(8,128)(2,1)} %copy-done.4) | copy-start | bytes 2162692
  94.8 10.9 %copy-start.7 = (bf16[176,2048]{1,0:T(8,128)(2,1)S(1)}, bf16[176,2048]{1,0:T(8,128)(2,1)}, u32[]{:S(2)}) copy-start(bf16[176,2048]{1,0:T(8,128)(2,1)} %copy-done.6) | copy-start | bytes 2162692
  100.6 5.1 %collective-permute-start.20 = (bf16[256,2048]{1,0:T(8,128)(2,1)S(1)}, bf16[256,2048]{1,0:T(8,128)(2,1)S(1)}, u32[]{:S(2)}, u32[]{:S(2)}) collective-permute-start(bf16[256,2048]{1,0:T(8,128)(2,1)S(1)} %constant_dynamic-update-slice_fusion.4), channel_id=1, source_target_pairs={{0,1},{1,0},{2,3},{3,2},{4,5},{5,4},{6,7},{7,6},{8,9},{9,8},{10,11... | collective-permute-start | bytes 3145736 | tf_op jit(solution)/shard_map/ppermute | solution.py:343
  100.7 26.7 %collective-permute-start.18 = (bf16[128,2048]{1,0:T(8,128)(2,1)S(1)}, bf16[128,2048]{1,0:T(8,128)(2,1)S(1)}, u32[]{:S(2)}, u32[]{:S(2)}) collective-permute-start(bf16[128,2048]{1,0:T(8,128)(2,1)S(1)} %copy-done.19), channel_id=1, source_target_pairs={{4,0},{8,4},{12,8},{16,12},{20,16},{24,20},{28,24},{5,1},{9,5},{13... | collective-permute-start | bytes 1572872 | tf_op jit(solution)/shard_map/ppermute | solution.py:552
  102.2 32.6 %collective-permute-start.10 = (bf16[128,2048]{1,0:T(8,128)(2,1)S(1)}, bf16[128,2048]{1,0:T(8,128)(2,1)S(1)}, u32[]{:S(2)}, u32[]{:S(2)}) collective-permute-start(bf16[128,2048]{1,0:T(8,128)(2,1)S(1)} %mixed_part.2.refs_5_), channel_id=1, source_target_pairs={{0,1},{1,0},{2,3},{3,2},{4,5},{5,4},{6,7},{7,6},{8,9},{9,8},{10,11... | collective-permute-start | bytes 1572872 | tf_op jit(solution)/shard_map/ppermute | solution.py:343
  102.7 32.0 %collective-permute-start.12 = (bf16[128,2048]{1,0:T(8,128)(2,1)S(1)}, bf16[128,2048]{1,0:T(8,128)(2,1)S(1)}, u32[]{:S(2)}, u32[]{:S(2)}) collective-permute-start(bf16[128,2048]{1,0:T(8,128)(2,1)S(1)} %convert_add_fusion), channel_id=1, source_target_pairs={{0,2},{1,3},{2,0},{3,1},{4,6},{5,7},{6,4},{7,5},{8,10},{9,11},{10,... | collective-permute-start | bytes 1572872 | tf_op jit(solution)/shard_map/ppermute | solution.py:343
  103.6 16.0 %collective-permute-start.21 = (bf16[512,128]{1,0:T(8,128)(2,1)S(1)}, bf16[512,128]{1,0:T(8,128)(2,1)S(1)}, u32[]{:S(2)}, u32[]{:S(2)}) collective-permute-start(bf16[512,128]{1,0:T(8,128)(2,1)S(1)} %get-tuple-element.74), channel_id=1, source_target_pairs={{0,8},{4,12},{8,0},{12,4},{16,24},{20,28},{24,16},{28,20},{1,9},{5... | collective-permute-start | bytes 393224 | tf_op jit(solution)/shard_map/ppermute | solution.py:343
  120.1 7.9 %collective-permute-start.22 = (bf16[512,128]{1,0:T(8,128)(2,1)S(1)}, bf16[512,128]{1,0:T(8,128)(2,1)S(1)}, u32[]{:S(2)}, u32[]{:S(2)}) collective-permute-start(bf16[512,128]{1,0:T(8,128)(2,1)S(1)} %added.4.refs_1_), channel_id=1, source_target_pairs={{0,16},{4,20},{8,24},{12,28},{16,0},{20,4},{24,8},{28,12},{1,17},{... | collective-permute-start | bytes 393224 | tf_op jit(solution)/shard_map/ppermute | solution.py:343
  128.6 5.5 %collective-permute-start.23 = (bf16[512,128]{1,0:T(8,128)(2,1)S(1)}, bf16[512,128]{1,0:T(8,128)(2,1)S(1)}, u32[]{:S(2)}, u32[]{:S(2)}) collective-permute-start(bf16[512,128]{1,0:T(8,128)(2,1)S(1)} %added.5.refs_1_), channel_id=1, source_target_pairs={{0,8},{4,12},{8,0},{12,4},{16,24},{20,28},{24,16},{28,20},{1,9},{5... | collective-permute-start | bytes 393224 | tf_op jit(solution)/shard_map/ppermute | solution.py:343
  134.6 7.4 %collective-permute-start.24 = (bf16[1024,128]{1,0:T(8,128)(2,1)S(1)}, bf16[1024,128]{1,0:T(8,128)(2,1)S(1)}, u32[]{:S(2)}, u32[]{:S(2)}) collective-permute-start(bf16[1024,128]{1,0:T(8,128)(2,1)S(1)} %joined.2.refs_1_), channel_id=1, source_target_pairs={{0,4},{4,0},{8,12},{12,8},{16,20},{20,16},{24,28},{28,24},{1,5},{5... | collective-permute-start | bytes 786440 | tf_op jit(solution)/shard_map/ppermute | solution.py:343
  (25 other events, 95.7 us)

commit v17 on v16

--- a/solution.py
+++ b/solution.py
@@ -524,7 +524,9 @@
     brought.insert(1, across)
     tap_sum = Sum(me, held_until([tap_grad], [mixed_one])[0])
     previous, landed = landed, passed_on([mixed_one])
-    last_part = weight_pass(me, out_weight, 0, gated, after=landed + [mixed_one])[0]
+    given = held_until([grad_filtered], previous)[0]
+    following = lax.ppermute(given, "ctx", [(i + 1, i) for i in range(n_ctx - 1)])
+    last_part = weight_pass(me, out_weight, 0, gated, after=landed + [mixed_one, following])[0]
 
     terms = dict(zip(terms, held_until(terms.values(), previous)))
     terms[0] = last_part + swap(mixed_one, "chan", 1).astype(F32)
@@ -547,9 +549,6 @@
     places.insert(1, [(0, half), (0, half)])
 
     cols.append(gather_of_chips(jnp.concatenate(brought[early:], axis=0)))
-
-    given = held_until([grad_filtered], far)[0]
-    following = lax.ppermute(given, "ctx", [(i + 1, i) for i in range(n_ctx - 1)])
 
     evens = [off for off in range(n_chan) if off % 2 == 0]
     wide = piece % 128 == 0 and 2 * early == n_ctx

time: 144 us -> 145 us (level)
    ppermute x14, waiting for transfers between devices: 21 us -> 11.1 us  [swap(): return lax.ppermute(block, axis, [(i, i ^ bit) for i in range(size)])]
    ppermute x6, waiting for transfers between devices: 13.4 us -> 23.1 us  [passed_on(): came = [lax.ppermute(onto, 'ctx', ahead), lax.ppermute(back, 'ctx', behind)]]
    ppermute x6, starting transfers between devices: 6.18 us -> 8.07 us  [passed_on(): came = [lax.ppermute(onto, 'ctx', ahead), lax.ppermute(back, 'ctx', behind)]]
where the time goes in v17:
time: 145 us; the launch traced here: 144 us
  Pallas kernels  65.4 us (45%)
  waiting for transfers between devices  37.1 us (26%)
  starting transfers between devices  31.1 us (21%)
  other arithmetic  5.75 us (4%)
  local copies, waits for them, and re-layouts  3.54 us (2%)
    pallas_call x6, Pallas kernels, weight_pass(): pl.pallas_call(ignoring(body, len(after), 1 + len(arrays)), grid_spec=plt...  39.9 us
    ppermute x6, waiting for transfers between devices, passed_on(): came = [lax.ppermute(onto, 'ctx', ahead), lax.ppermute(back, 'ctx', behind)]  23.1 us
    ppermute x14, starting transfers between devices, swap(): return lax.ppermute(block, axis, [(i, i ^ bit) for i in range(size)])  12.6 us
    ppermute x14, waiting for transfers between devices, swap(): return lax.ppermute(block, axis, [(i, i ^ bit) for i in range(size)])  11.1 us
    pallas_call x3, Pallas kernels, by_channel(): pl.pallas_call(ignoring(functools.partial(kernel, length), len(after), le...  10.8 us
    pallas_call x2, Pallas kernels, grad_weight_of(): pl.pallas_call(ignoring(functools.partial(weight_kernel, places, parts),...  10 us
    ppermute x6, starting transfers between devices, passed_on(): came = [lax.ppermute(onto, 'ctx', ahead), lax.ppermute(back, 'ctx', behind)]  8.07 us
    ppermute x1, starting transfers between devices, per_device(): lax.ppermute(held_until([pieces[rows:2 * rows]], [mixed_one])[0], 'ctx',...  3.5 us
  transfers between devices with their start and end apart: 25, of which 9 were waited for; matrix products, arithmetic and copies ran while one was open for 2% of the time, Pallas kernels for 44%

profile of v17, /device:TPU:0, one launch (start us, length us, event | category | flops | bytes accessed | tf_op | source)
XLA Modules:
  0.0 144.1 jit_solution(3438901305884633302)
XLA Ops:
  0.6 2.2 %multiply_convert_fusion = bf16[128,2048]{1,0:T(8,128)(2,1)} fusion(bf16[128,2048]{1,0:T(8,128)(2,1)} %refs_1_.18, bf16[128,2048]{1,0:T(8,128)(2,1)} %refs_0_.5), kind=kLoop, calls=%fused_computation.2 | loop fusion | flops 1048576 | bytes 1572864 | tf_op jit(solution)/shard_map/convert_element_type | solution.py:444
  2.8 2.9 %collective-permute-start.2 = (bf16[128,2048]{1,0:T(8,128)(2,1)S(1)}, bf16[128,2048]{1,0:T(8,128)(2,1)S(1)}, u32[]{:S(2)}, u32[]{:S(2)}) collective-permute-start(bf16[128,2048]{1,0:T(8,128)(2,1)S(1)} %copy-done.6), channel_id=1, source_target_pairs={{0,2},{1,3},{2,0},{3,1},{4,6},{5,7},{6,4},{7,5},{8,10},{9,11},{10,... | collective-permute-start | bytes 1572872 | tf_op jit(solution)/shard_map/ppermute | solution.py:343
  5.8 3.4 %collective-permute-start = (bf16[128,2048]{1,0:T(8,128)(2,1)}, bf16[128,2048]{1,0:T(8,128)(2,1)S(1)}, u32[]{:S(2)}, u32[]{:S(2)}) collective-permute-start(bf16[128,2048]{1,0:T(8,128)(2,1)} %multiply_convert_fusion), channel_id=1, source_target_pairs={{0,4},{4,8},{8,12},{12,16},{16,20},{20,24},{24,28},{1,5},{5,9},{9,... | collective-permute-start | bytes 1572872 | tf_op jit(solution)/shard_map/ppermute | solution.py:446
  9.3 6.2 %grad_gated_part.2.refs_3_ = f32[2048,128]{1,0:T(8,128)S(1)} custom-call(s32[2]{0:T(128)S(1)} %pad_add_fusion.refs_0_, bf16[2048,8192]{1,0:T(8,128)(2,1)} %refs_1_.17, bf16[128,2048]{1,0:T(8,128)(2,1)S(1)} %copy-done.6), custom_call_target="tpu_custom_call" | custom-call | flops 3000000000 | tf_op jit(solution)/shard_map/grad_gated_part/pallas_call | solution.py:190
  15.6 2.1 %collective-permute-done.2.refs_4_.refs_3_ = bf16[128,2048]{1,0:T(8,128)(2,1)S(1)} collective-permute-done((bf16[128,2048]{1,0:T(8,128)(2,1)S(1)}, bf16[128,2048]{1,0:T(8,128)(2,1)S(1)}, u32[]{:S(2)}, u32[]{:S(2)}) %collective-permute-start.2) | collective-permute-done | bytes 524320 | tf_op jit(solution)/shard_map/ppermute | solution.py:343
  17.7 6.3 %grad_gated_part.3.refs_7_.refs_6_.refs_4_ = f32[2048,128]{1,0:T(8,128)S(1)} custom-call(s32[2]{0:T(128)S(1)} %pad_add_fusion.refs_0_, bf16[2048,8192]{1,0:T(8,128)(2,1)} %refs_1_.17, bf16[128,2048]{1,0:T(8,128)(2,1)S(1)} %collective-permute-done.1.refs_2_.refs_3_, f32[2048,128]{1,0:T(8,128)S(1)} %grad_gated_part.2.refs_3_), custom_call_target="tpu_custom_call" | custom-call | flops 3000000000 | tf_op jit(solution)/shard_map/grad_gated_part/pallas_call | solution.py:190
  25.9 3.3 %forward_filter.1 = (bf16[128,2048]{1,0:T(8,128)(2,1)S(1)}, f32[128,2048]{1,0:T(8,128)S(1)}) custom-call(bf16[128,2048]{1,0:T(8,128)(2,1)S(1)} %copy-done.9, bf16[128,2048]{1,0:T(8,128)(2,1)S(1)} %copy-done.10, bf16[128,2048]{1,0:T(8,128)(2,1)S(1)} %copy-done.11, bf16[128,2048]{1,0:T(8,128)(2,1)S(1)} %copy-done.19, bf16[2048,128]{1,0:T(8,128)(2,1)S(1)} %copy-done.14, ...), custom_call_target="tpu_custom_call" | custom-call | flops 3000000000 | tf_op jit(solution)/shard_map/forward_filter/pallas_call | solution.py:107
  31.2 1.8 %collective-permute-start.4 = (bf16[176,2048]{1,0:T(8,128)(2,1)}, bf16[176,2048]{1,0:T(8,128)(2,1)S(1)}, u32[]{:S(2)}, u32[]{:S(2)}) collective-permute-start(bf16[176,2048]{1,0:T(8,128)(2,1)} %get-tuple-element.46), channel_id=1, source_target_pairs={{0,8},{8,16},{16,24},{24,28},{28,20},{20,12},{12,4},{4,0},{1,9},{9... | collective-permute-start | bytes 2162696 | tf_op jit(solution)/shard_map/ppermute | solution.py:490
  33.2 7.4 %grads_and_mixed.2 = (f32[2048,128]{1,0:T(8,128)S(1)}, f32[128,2048]{1,0:T(8,128)S(1)}) custom-call(s32[2]{0:T(128)S(1)} %pad_add_fusion.refs_0_, bf16[2048,8192]{1,0:T(8,128)(2,1)} %refs_1_.17, bf16[128,2048]{1,0:T(8,128)(2,1)S(1)} %get-tuple-element.44.refs_2_.refs_1_, bf16[128,2048]{1,0:T(8,128)(2,1)S(1)} %collective-permute-done.2.refs_4_.refs_3_, ...), custom_call_target="tpu_custom_call" | custom-call | flops 500000000 | tf_op jit(solution)/shard_map/grads_and_mixed/pallas_call | solution.py:190
  40.7 8.5 %grads_and_mixed.3 = (bf16[128,2048]{1,0:T(8,128)(2,1)}, bf16[128,2048]{1,0:T(8,128)(2,1)S(1)}, bf16[128,2048]{1,0:T(8,128)(2,1)}) custom-call(s32[2]{0:T(128)S(1)} %pad_add_fusion.refs_0_, bf16[2048,8192]{1,0:T(8,128)(2,1)} %refs_1_.17, bf16[128,2048]{1,0:T(8,128)(2,1)S(1)} %get-tuple-element.44.refs_2_.refs_1_, ...), custom_call_target="tpu_custom_call" | custom-call | flops 500000000 | tf_op jit(solution)/shard_map/grads_and_mixed/pallas_call | solution.py:190
  50.1 1.4 collective-permute-done.5.refs_7_.refs_5_
  51.6 1.6 %collective-permute-start.6 = (bf16[160,2048]{1,0:T(8,128)(2,1)S(1)}, bf16[160,2048]{1,0:T(8,128)(2,1)S(1)}, u32[]{:S(2)}, u32[]{:S(2)}) collective-permute-start(bf16[160,2048]{1,0:T(8,128)(2,1)S(1)} %slice.82), channel_id=1, source_target_pairs={{0,8},{8,16},{16,24},{24,28},{28,20},{20,12},{12,4},{4,0},{1,9},{9... | collective-permute-start | bytes 1966088 | tf_op jit(solution)/shard_map/ppermute | solution.py:490
  54.9 3.5 %tap_grad.1.refs_3_ = bf16[2048,128]{1,0:T(8,128)(2,1)S(1)} custom-call(bf16[128,2048]{1,0:T(8,128)(2,1)S(1)} %copy-done.10, bf16[128,2048]{1,0:T(8,128)(2,1)S(1)} %copy-done.12, bf16[128,2048]{1,0:T(8,128)(2,1)S(1)} %copy-done.20, bf16[128,2048]{1,0:T(8,128)(2,1)S(1)} %copy-done.17, bf16[2,256,256]{2,1,0:T(8,128)(2,1)S(1)} %copy-done.22, ...), custom_call_target="tpu_custom_call" | custom-call | flops 3000000000 | tf_op jit(solution)/shard_map/tap_grad/pallas_call | solution.py:107
  58.4 5.7 %mixed_part.2.refs_5_ = bf16[128,2048]{1,0:T(8,128)(2,1)S(1)} custom-call(s32[2]{0:T(128)S(1)} %pad_add_fusion.refs_0_, bf16[2048,8192]{1,0:T(8,128)(2,1)} %refs_1_.17, bf16[128,2048]{1,0:T(8,128)(2,1)S(1)} %get-tuple-element.44.refs_2_.refs_1_, bf16[2048,128]{1,0:T(8,128)(2,1)S(1)} %tap_grad.1.refs_3_), custom_call_target="tpu_custom_call" | custom-call | flops 500000000 | tf_op jit(solution)/shard_map/mixed_part/pallas_call | solution.py:190
  64.1 3.5 %collective-permute-start.15 = (bf16[16,2048]{1,0:T(8,128)(2,1)S(1)}, bf16[16,2048]{1,0:T(8,128)(2,1)S(1)}, u32[]{:S(2)}, u32[]{:S(2)}) collective-permute-start(bf16[16,2048]{1,0:T(8,128)(2,1)S(1)} %get-tuple-element.63), channel_id=1, source_target_pairs={{0,28},{8,20},{16,12},{24,4},{28,0},{20,8},{12,16},{4,24},{1,29},{... | collective-permute-start | bytes 196616 | tf_op jit(solution)/shard_map/ppermute | solution.py:519
  67.7 1.6 %collective-permute-start.14 = (bf16[1024,128]{1,0:T(8,128)(2,1)S(1)}, bf16[1024,128]{1,0:T(8,128)(2,1)S(1)}, u32[]{:S(2)}, u32[]{:S(2)}) collective-permute-start(bf16[1024,128]{1,0:T(8,128)(2,1)S(1)} %get-tuple-element.88), channel_id=1, source_target_pairs={{0,4},{4,0},{8,12},{12,8},{16,20},{20,16},{24,28},{28,24},{1,5},{5... | collective-permute-start | bytes 786440 | tf_op jit(solution)/shard_map/ppermute | solution.py:343
  69.3 2.8 %collective-permute-done.15 = bf16[16,2048]{1,0:T(8,128)(2,1)S(1)} collective-permute-done((bf16[16,2048]{1,0:T(8,128)(2,1)S(1)}, bf16[16,2048]{1,0:T(8,128)(2,1)S(1)}, u32[]{:S(2)}, u32[]{:S(2)}) %collective-permute-start.15) | collective-permute-done | bytes 65568 | tf_op jit(solution)/shard_map/ppermute | solution.py:519
  72.2 1.4 collective-permute-start.10
  73.7 4.0 %collective-permute-start.8 = (bf16[144,2048]{1,0:T(8,128)(2,1)S(1)}, bf16[144,2048]{1,0:T(8,128)(2,1)S(1)}, u32[]{:S(2)}, u32[]{:S(2)}) collective-permute-start(bf16[144,2048]{1,0:T(8,128)(2,1)S(1)} %slice.84), channel_id=1, source_target_pairs={{0,8},{8,16},{16,24},{24,28},{28,20},{20,12},{12,4},{4,0},{1,9},{9... | collective-permute-start | bytes 1769480 | tf_op jit(solution)/shard_map/ppermute | solution.py:490
  77.8 1.5 %collective-permute-start.16 = (bf16[64,2048]{1,0:T(8,128)(2,1)S(1)}, bf16[64,2048]{1,0:T(8,128)(2,1)S(1)}, u32[]{:S(2)}, u32[]{:S(2)}) collective-permute-start(bf16[64,2048]{1,0:T(8,128)(2,1)S(1)} %get-tuple-element.95.refs_10_), channel_id=1, source_target_pairs={{0,2},{1,3},{2,0},{3,1},{4,6},{5,7},{6,4},{7,5},{8,10},{9,11},{10,... | collective-permute-start | bytes 786440 | tf_op jit(solution)/shard_map/ppermute | solution.py:343
  79.3 21.7 %collective-permute-done.8.refs_3_.refs_8_ = bf16[144,2048]{1,0:T(8,128)(2,1)S(1)} collective-permute-done((bf16[144,2048]{1,0:T(8,128)(2,1)S(1)}, bf16[144,2048]{1,0:T(8,128)(2,1)S(1)}, u32[]{:S(2)}, u32[]{:S(2)}) %collective-permute-start.8) | collective-permute-done | bytes 589856 | tf_op jit(solution)/shard_map/ppermute | solution.py:490
  101.1 1.6 %collective-permute-start.19 = (bf16[64,2048]{1,0:T(8,128)(2,1)S(1)}, bf16[64,2048]{1,0:T(8,128)(2,1)S(1)}, u32[]{:S(2)}, u32[]{:S(2)}) collective-permute-start(bf16[64,2048]{1,0:T(8,128)(2,1)S(1)} %pad_maximum_fusion.2.refs_11_), channel_id=1, source_target_pairs={{0,2},{1,3},{2,0},{3,1},{4,6},{5,7},{6,4},{7,5},{8,10},{9,11},{10,... | collective-permute-start | bytes 786440 | tf_op jit(solution)/shard_map/ppermute | solution.py:343
  104.3 1.6 %collective-permute-start.17 = (bf16[64,2048]{1,0:T(8,128)(2,1)S(1)}, bf16[64,2048]{1,0:T(8,128)(2,1)S(1)}, u32[]{:S(2)}, u32[]{:S(2)}) collective-permute-start(bf16[64,2048]{1,0:T(8,128)(2,1)S(1)} %slice.74), channel_id=1, source_target_pairs={{0,8},{8,16},{16,24},{24,28},{28,20},{20,12},{12,4},{4,0},{1,9},{9... | collective-permute-start | bytes 786440 | tf_op jit(solution)/shard_map/ppermute | solution.py:547
  106.0 5.7 %mixed_part.3 = f32[128,2048]{1,0:T(8,128)S(1)} custom-call(s32[2]{0:T(128)S(1)} %pad_add_fusion.refs_0_, bf16[2048,8192]{1,0:T(8,128)(2,1)} %refs_1_.17, bf16[128,2048]{1,0:T(8,128)(2,1)S(1)} %get-tuple-element.44.refs_2_.refs_1_, bf16[144,2048]{1,0:T(8,128)(2,1)S(1)} %copy-done.1, bf16[144,2048]{1,0:T(8,128)(2,1)S(1)} %collective-permute-done.9.refs_4_.refs_9_, ...), custom_call_target="tpu_custom_call" | custom-call | flops 500000000 | tf_op jit(solution)/shard_map/mixed_part/pallas_call | solution.py:190
  113.0 1.4 collective-permute-start.21
  114.5 5.0 %grad_weight.2.refs_18_ = bf16[2048,1024]{1,0:T(8,128)(2,1)} custom-call(s32[2]{0:T(128)S(1)} %pad_add_fusion.refs_0_, bf16[128,2048]{1,0:T(8,128)(2,1)S(1)} %get-tuple-element.44.refs_2_.refs_1_, bf16[64,2048]{1,0:T(8,128)(2,1)S(1)} %collective-permute-done.17.refs_2_, bf16[64,2048]{1,0:T(8,128)(2,1)S(1)} %collective-permute-done.18.refs_3_, ...), custom_call_target="tpu_custom_call" | custom-call | flops 2000000000 | tf_op jit(solution)/shard_map/grad_weight/pallas_call | solution.py:293
  120.1 1.3 collective-permute-start.22
  121.4 5.0 %grad_weight.3 = bf16[2048,1024]{1,0:T(8,128)(2,1)} custom-call(s32[2]{0:T(128)S(1)} %pad_add_fusion.refs_0_, bf16[128,2048]{1,0:T(8,128)(2,1)S(1)} %get-tuple-element.44.refs_2_.refs_1_, bf16[64,2048]{1,0:T(8,128)(2,1)S(1)} %collective-permute-done.17.refs_2_, ...), custom_call_target="tpu_custom_call", output_to_operand_aliasing={{}: (18, {})} | custom-call | flops 2000000000 | tf_op jit(solution)/shard_map/grad_weight/pallas_call | solution.py:293
  126.4 3.0 %collective-permute-done.22.refs_2_ = bf16[512,128]{1,0:T(8,128)(2,1)S(1)} collective-permute-done((bf16[512,128]{1,0:T(8,128)(2,1)S(1)}, bf16[512,128]{1,0:T(8,128)(2,1)S(1)}, u32[]{:S(2)}, u32[]{:S(2)}) %collective-permute-start.22) | collective-permute-done | bytes 131104 | tf_op jit(solution)/shard_map/ppermute | solution.py:343
  130.1 4.0 %backward_filter.1 = (bf16[128,2048]{1,0:T(8,128)(2,1)}, bf16[128,2048]{1,0:T(8,128)(2,1)}) custom-call(bf16[128,2048]{1,0:T(8,128)(2,1)S(1)} %copy-done.10, bf16[128,2048]{1,0:T(8,128)(2,1)S(1)} %copy-done.12, bf16[128,2048]{1,0:T(8,128)(2,1)S(1)} %copy-done.17, bf16[128,2048]{1,0:T(8,128)(2,1)S(1)} %collective-permute-done.10.refs_6_.refs_3_, ...), custom_call_target="tpu_custom_call" | custom-call | flops 3000000000 | tf_op jit(solution)/shard_map/backward_filter/pallas_call | solution.py:107
  137.6 4.8 %collective-permute-done.24.refs_2_ = bf16[1024,128]{1,0:T(8,128)(2,1)S(1)} collective-permute-done((bf16[1024,128]{1,0:T(8,128)(2,1)S(1)}, bf16[1024,128]{1,0:T(8,128)(2,1)S(1)}, u32[]{:S(2)}, u32[]{:S(2)}) %collective-permute-start.24) | collective-permute-done | bytes 262176 | tf_op jit(solution)/shard_map/ppermute | solution.py:343
  142.5 1.6 %joined.3 = f32[2048,128]{1,0:T(8,128)} custom-call(s32[2]{0:T(128)S(1)} %pad_add_fusion.refs_0_, bf16[1024,128]{1,0:T(8,128)(2,1)S(1)} %joined.2.refs_1_, bf16[1024,128]{1,0:T(8,128)(2,1)S(1)} %collective-permute-done.24.refs_2_), custom_call_target="tpu_custom_call" | custom-call | flops 500000000 | tf_op jit(solution)/shard_map/joined/pallas_call | solution.py:422
  (119 shorter events, 14.7 us)
Async XLA Ops:
  2.8 14.9 %collective-permute-start.2 = (bf16[128,2048]{1,0:T(8,128)(2,1)S(1)}, bf16[128,2048]{1,0:T(8,128)(2,1)S(1)}, u32[]{:S(2)}, u32[]{:S(2)}) collective-permute-start(bf16[128,2048]{1,0:T(8,128)(2,1)S(1)} %copy-done.6), channel_id=1, source_target_pairs={{0,2},{1,3},{2,0},{3,1},{4,6},{5,7},{6,4},{7,5},{8,10},{9,11},{10,... | collective-permute-start | bytes 1572872 | tf_op jit(solution)/shard_map/ppermute | solution.py:343
  5.8 11.9 %collective-permute-start.1 = (bf16[128,2048]{1,0:T(8,128)(2,1)S(1)}, bf16[128,2048]{1,0:T(8,128)(2,1)S(1)}, u32[]{:S(2)}, u32[]{:S(2)}) collective-permute-start(bf16[128,2048]{1,0:T(8,128)(2,1)S(1)} %copy-done.6), channel_id=1, source_target_pairs={{0,1},{1,0},{2,3},{3,2},{4,5},{5,4},{6,7},{7,6},{8,9},{9,8},{10,11... | collective-permute-start | bytes 1572872 | tf_op jit(solution)/shard_map/ppermute | solution.py:343
  5.8 18.2 %collective-permute-start = (bf16[128,2048]{1,0:T(8,128)(2,1)}, bf16[128,2048]{1,0:T(8,128)(2,1)S(1)}, u32[]{:S(2)}, u32[]{:S(2)}) collective-permute-start(bf16[128,2048]{1,0:T(8,128)(2,1)} %multiply_convert_fusion), channel_id=1, source_target_pairs={{0,4},{4,8},{8,12},{12,16},{16,20},{20,24},{24,28},{1,5},{5,9},{9,... | collective-permute-start | bytes 1572872 | tf_op jit(solution)/shard_map/ppermute | solution.py:446
  15.5 9.2 %copy-start.9 = (bf16[128,2048]{1,0:T(8,128)(2,1)S(1)}, bf16[128,2048]{1,0:T(8,128)(2,1)}, u32[]{:S(2)}) copy-start(bf16[128,2048]{1,0:T(8,128)(2,1)} %refs_5_.4) | copy-start | bytes 1572868
  15.6 9.2 %copy-start.10 = (bf16[128,2048]{1,0:T(8,128)(2,1)S(1)}, bf16[128,2048]{1,0:T(8,128)(2,1)}, u32[]{:S(2)}) copy-start(bf16[128,2048]{1,0:T(8,128)(2,1)} %refs_0_.5) | copy-start | bytes 1572868
  15.6 9.2 %copy-start.11 = (bf16[128,2048]{1,0:T(8,128)(2,1)S(1)}, bf16[128,2048]{1,0:T(8,128)(2,1)}, u32[]{:S(2)}) copy-start(bf16[128,2048]{1,0:T(8,128)(2,1)} %refs_1_.18) | copy-start | bytes 1572868
  15.6 9.2 %copy-start.14 = (bf16[2048,128]{1,0:T(8,128)(2,1)S(1)}, bf16[2048,128]{1,0:T(8,128)(2,1)}, u32[]{:S(2)}) copy-start(bf16[2048,128]{1,0:T(8,128)(2,1)} %refs_4_.4) | copy-start | bytes 1572868
  15.6 9.2 %copy-start.21 = (bf16[2,256,256]{2,1,0:T(8,128)(2,1)S(1)}, bf16[2,256,256]{2,1,0:T(8,128)(2,1)}, u32[]{:S(2)}) copy-start(bf16[2,256,256]{2,1,0:T(8,128)(2,1)} %constant.23.clone.refs_5_.refs_4_) | copy-start | bytes 786436
  17.7 11.5 %collective-permute-start.3 = (bf16[128,2048]{1,0:T(8,128)(2,1)S(1)}, bf16[128,2048]{1,0:T(8,128)(2,1)S(1)}, u32[]{:S(2)}, u32[]{:S(2)}) collective-permute-start(bf16[128,2048]{1,0:T(8,128)(2,1)S(1)} %collective-permute-done.2.refs_4_.refs_3_), channel_id=1, source_target_pairs={{0,1},{1,0},{2,3},{3,2},{4,5},{5,4},{6,7},{7,6},{8,9},{9,8},{10,11... | collective-permute-start | bytes 1572872 | tf_op jit(solution)/shard_map/ppermute | solution.py:343
  31.2 18.8 %collective-permute-start.4 = (bf16[176,2048]{1,0:T(8,128)(2,1)}, bf16[176,2048]{1,0:T(8,128)(2,1)S(1)}, u32[]{:S(2)}, u32[]{:S(2)}) collective-permute-start(bf16[176,2048]{1,0:T(8,128)(2,1)} %get-tuple-element.46), channel_id=1, source_target_pairs={{0,8},{8,16},{16,24},{24,28},{28,20},{20,12},{12,4},{4,0},{1,9},{9... | collective-permute-start | bytes 2162696 | tf_op jit(solution)/shard_map/ppermute | solution.py:490
  33.0 18.5 %collective-permute-start.5 = (bf16[176,2048]{1,0:T(8,128)(2,1)}, bf16[176,2048]{1,0:T(8,128)(2,1)S(1)}, u32[]{:S(2)}, u32[]{:S(2)}) collective-permute-start(bf16[176,2048]{1,0:T(8,128)(2,1)} %get-tuple-element.47), channel_id=1, source_target_pairs={{8,0},{16,8},{24,16},{28,24},{20,28},{12,20},{4,12},{0,4},{9,1},{1... | collective-permute-start | bytes 2162696 | tf_op jit(solution)/shard_map/ppermute | solution.py:490
  50.0 3.7 %collective-permute-start.12 = (bf16[128,2048]{1,0:T(8,128)(2,1)}, bf16[128,2048]{1,0:T(8,128)(2,1)}, u32[]{:S(2)}, u32[]{:S(2)}) collective-permute-start(bf16[128,2048]{1,0:T(8,128)(2,1)} %get-tuple-element.57), channel_id=1, source_target_pairs={{0,1},{1,0},{2,3},{3,2},{4,5},{5,4},{6,7},{7,6},{8,9},{9,8},{10,11... | collective-permute-start | bytes 1572872 | tf_op jit(solution)/shard_map/ppermute | solution.py:343
  50.0 19.3 %copy-start.2 = (bf16[176,2048]{1,0:T(8,128)(2,1)}, bf16[176,2048]{1,0:T(8,128)(2,1)S(1)}, u32[]{:S(2)}) copy-start(bf16[176,2048]{1,0:T(8,128)(2,1)S(1)} %collective-permute-done.4.refs_6_.refs_4_) | copy-start | bytes 2162692
  51.5 17.8 %copy-start.4 = (bf16[176,2048]{1,0:T(8,128)(2,1)}, bf16[176,2048]{1,0:T(8,128)(2,1)S(1)}, u32[]{:S(2)}) copy-start(bf16[176,2048]{1,0:T(8,128)(2,1)S(1)} %collective-permute-done.5.refs_7_.refs_5_) | copy-start | bytes 2162692
  51.6 20.6 %collective-permute-start.6 = (bf16[160,2048]{1,0:T(8,128)(2,1)S(1)}, bf16[160,2048]{1,0:T(8,128)(2,1)S(1)}, u32[]{:S(2)}, u32[]{:S(2)}) collective-permute-start(bf16[160,2048]{1,0:T(8,128)(2,1)S(1)} %slice.82), channel_id=1, source_target_pairs={{0,8},{8,16},{16,24},{24,28},{28,20},{20,12},{12,4},{4,0},{1,9},{9... | collective-permute-start | bytes 1966088 | tf_op jit(solution)/shard_map/ppermute | solution.py:490
  53.2 19.0 %collective-permute-start.7 = (bf16[160,2048]{1,0:T(8,128)(2,1)S(1)}, bf16[160,2048]{1,0:T(8,128)(2,1)S(1)}, u32[]{:S(2)}, u32[]{:S(2)}) collective-permute-start(bf16[160,2048]{1,0:T(8,128)(2,1)S(1)} %slice.83), channel_id=1, source_target_pairs={{8,0},{16,8},{24,16},{28,24},{20,28},{12,20},{4,12},{0,4},{9,1},{1... | collective-permute-start | bytes 1966088 | tf_op jit(solution)/shard_map/ppermute | solution.py:490
  64.1 8.0 %collective-permute-start.15 = (bf16[16,2048]{1,0:T(8,128)(2,1)S(1)}, bf16[16,2048]{1,0:T(8,128)(2,1)S(1)}, u32[]{:S(2)}, u32[]{:S(2)}) collective-permute-start(bf16[16,2048]{1,0:T(8,128)(2,1)S(1)} %get-tuple-element.63), channel_id=1, source_target_pairs={{0,28},{8,20},{16,12},{24,4},{28,0},{20,8},{12,16},{4,24},{1,29},{... | collective-permute-start | bytes 196616 | tf_op jit(solution)/shard_map/ppermute | solution.py:519
  67.7 33.4 %collective-permute-start.14 = (bf16[1024,128]{1,0:T(8,128)(2,1)S(1)}, bf16[1024,128]{1,0:T(8,128)(2,1)S(1)}, u32[]{:S(2)}, u32[]{:S(2)}) collective-permute-start(bf16[1024,128]{1,0:T(8,128)(2,1)S(1)} %get-tuple-element.88), channel_id=1, source_target_pairs={{0,4},{4,0},{8,12},{12,8},{16,20},{20,16},{24,28},{28,24},{1,5},{5... | collective-permute-start | bytes 786440 | tf_op jit(solution)/shard_map/ppermute | solution.py:343
  72.2 33.8 %collective-permute-start.10 = (bf16[128,2048]{1,0:T(8,128)(2,1)S(1)}, bf16[128,2048]{1,0:T(8,128)(2,1)S(1)}, u32[]{:S(2)}, u32[]{:S(2)}) collective-permute-start(bf16[128,2048]{1,0:T(8,128)(2,1)S(1)} %copy-done.17), channel_id=1, source_target_pairs={{4,0},{8,4},{12,8},{16,12},{20,16},{24,20},{28,24},{5,1},{9,5},{13... | collective-permute-start | bytes 1572872 | tf_op jit(solution)/shard_map/ppermute | solution.py:528
  73.7 27.3 %collective-permute-start.8 = (bf16[144,2048]{1,0:T(8,128)(2,1)S(1)}, bf16[144,2048]{1,0:T(8,128)(2,1)S(1)}, u32[]{:S(2)}, u32[]{:S(2)}) collective-permute-start(bf16[144,2048]{1,0:T(8,128)(2,1)S(1)} %slice.84), channel_id=1, source_target_pairs={{0,8},{8,16},{16,24},{24,28},{28,20},{20,12},{12,4},{4,0},{1,9},{9... | collective-permute-start | bytes 1769480 | tf_op jit(solution)/shard_map/ppermute | solution.py:490
  77.7 23.4 %collective-permute-start.9 = (bf16[144,2048]{1,0:T(8,128)(2,1)S(1)}, bf16[144,2048]{1,0:T(8,128)(2,1)S(1)}, u32[]{:S(2)}, u32[]{:S(2)}) collective-permute-start(bf16[144,2048]{1,0:T(8,128)(2,1)S(1)} %slice.85), channel_id=1, source_target_pairs={{8,0},{16,8},{24,16},{28,24},{20,28},{12,20},{4,12},{0,4},{9,1},{1... | collective-permute-start | bytes 1769480 | tf_op jit(solution)/shard_map/ppermute | solution.py:490
  77.8 25.6 %collective-permute-start.16 = (bf16[64,2048]{1,0:T(8,128)(2,1)S(1)}, bf16[64,2048]{1,0:T(8,128)(2,1)S(1)}, u32[]{:S(2)}, u32[]{:S(2)}) collective-permute-start(bf16[64,2048]{1,0:T(8,128)(2,1)S(1)} %get-tuple-element.95.refs_10_), channel_id=1, source_target_pairs={{0,2},{1,3},{2,0},{3,1},{4,6},{5,7},{6,4},{7,5},{8,10},{9,11},{10,... | collective-permute-start | bytes 786440 | tf_op jit(solution)/shard_map/ppermute | solution.py:343
  101.1 10.6 %collective-permute-start.19 = (bf16[64,2048]{1,0:T(8,128)(2,1)S(1)}, bf16[64,2048]{1,0:T(8,128)(2,1)S(1)}, u32[]{:S(2)}, u32[]{:S(2)}) collective-permute-start(bf16[64,2048]{1,0:T(8,128)(2,1)S(1)} %pad_maximum_fusion.2.refs_11_), channel_id=1, source_target_pairs={{0,2},{1,3},{2,0},{3,1},{4,6},{5,7},{6,4},{7,5},{8,10},{9,11},{10,... | collective-permute-start | bytes 786440 | tf_op jit(solution)/shard_map/ppermute | solution.py:343
  103.8 7.9 %collective-permute-start.18 = (bf16[64,2048]{1,0:T(8,128)(2,1)S(1)}, bf16[64,2048]{1,0:T(8,128)(2,1)S(1)}, u32[]{:S(2)}, u32[]{:S(2)}) collective-permute-start(bf16[64,2048]{1,0:T(8,128)(2,1)S(1)} %slice.75), channel_id=1, source_target_pairs={{8,0},{16,8},{24,16},{28,24},{20,28},{12,20},{4,12},{0,4},{9,1},{1... | collective-permute-start | bytes 786440 | tf_op jit(solution)/shard_map/ppermute | solution.py:547
  104.3 7.6 %collective-permute-start.17 = (bf16[64,2048]{1,0:T(8,128)(2,1)S(1)}, bf16[64,2048]{1,0:T(8,128)(2,1)S(1)}, u32[]{:S(2)}, u32[]{:S(2)}) collective-permute-start(bf16[64,2048]{1,0:T(8,128)(2,1)S(1)} %slice.74), channel_id=1, source_target_pairs={{0,8},{8,16},{16,24},{24,28},{28,20},{20,12},{12,4},{4,0},{1,9},{9... | collective-permute-start | bytes 786440 | tf_op jit(solution)/shard_map/ppermute | solution.py:547
  111.9 2.7 %collective-permute-start.20 = (bf16[256,2048]{1,0:T(8,128)(2,1)S(1)}, bf16[256,2048]{1,0:T(8,128)(2,1)S(1)}, u32[]{:S(2)}, u32[]{:S(2)}) collective-permute-start(bf16[256,2048]{1,0:T(8,128)(2,1)S(1)} %constant_dynamic-update-slice_fusion.4), channel_id=1, source_target_pairs={{0,1},{1,0},{2,3},{3,2},{4,5},{5,4},{6,7},{7,6},{8,9},{9,8},{10,11... | collective-permute-start | bytes 3145736 | tf_op jit(solution)/shard_map/ppermute | solution.py:343
  111.9 24.7 %collective-permute-start.11 = (bf16[128,2048]{1,0:T(8,128)(2,1)S(1)}, bf16[128,2048]{1,0:T(8,128)(2,1)S(1)}, u32[]{:S(2)}, u32[]{:S(2)}) collective-permute-start(bf16[128,2048]{1,0:T(8,128)(2,1)S(1)} %mixed_part.2.refs_5_), channel_id=1, source_target_pairs={{0,1},{1,0},{2,3},{3,2},{4,5},{5,4},{6,7},{7,6},{8,9},{9,8},{10,11... | collective-permute-start | bytes 1572872 | tf_op jit(solution)/shard_map/ppermute | solution.py:343
  112.4 24.2 %collective-permute-start.13 = (bf16[128,2048]{1,0:T(8,128)(2,1)S(1)}, bf16[128,2048]{1,0:T(8,128)(2,1)S(1)}, u32[]{:S(2)}, u32[]{:S(2)}) collective-permute-start(bf16[128,2048]{1,0:T(8,128)(2,1)S(1)} %convert_add_fusion), channel_id=1, source_target_pairs={{0,2},{1,3},{2,0},{3,1},{4,6},{5,7},{6,4},{7,5},{8,10},{9,11},{10,... | collective-permute-start | bytes 1572872 | tf_op jit(solution)/shard_map/ppermute | solution.py:343
  113.0 6.6 %collective-permute-start.21 = (bf16[512,128]{1,0:T(8,128)(2,1)S(1)}, bf16[512,128]{1,0:T(8,128)(2,1)S(1)}, u32[]{:S(2)}, u32[]{:S(2)}) collective-permute-start(bf16[512,128]{1,0:T(8,128)(2,1)S(1)} %get-tuple-element.74), channel_id=1, source_target_pairs={{0,8},{4,12},{8,0},{12,4},{16,24},{20,28},{24,16},{28,20},{1,9},{5... | collective-permute-start | bytes 393224 | tf_op jit(solution)/shard_map/ppermute | solution.py:343
  120.1 9.3 %collective-permute-start.22 = (bf16[512,128]{1,0:T(8,128)(2,1)S(1)}, bf16[512,128]{1,0:T(8,128)(2,1)S(1)}, u32[]{:S(2)}, u32[]{:S(2)}) collective-permute-start(bf16[512,128]{1,0:T(8,128)(2,1)S(1)} %added.4.refs_1_), channel_id=1, source_target_pairs={{0,16},{4,20},{8,24},{12,28},{16,0},{20,4},{24,8},{28,12},{1,17},{... | collective-permute-start | bytes 393224 | tf_op jit(solution)/shard_map/ppermute | solution.py:343
  130.0 5.0 %collective-permute-start.23 = (bf16[512,128]{1,0:T(8,128)(2,1)S(1)}, bf16[512,128]{1,0:T(8,128)(2,1)S(1)}, u32[]{:S(2)}, u32[]{:S(2)}) collective-permute-start(bf16[512,128]{1,0:T(8,128)(2,1)S(1)} %added.5.refs_1_), channel_id=1, source_target_pairs={{0,8},{4,12},{8,0},{12,4},{16,24},{20,28},{24,16},{28,20},{1,9},{5... | collective-permute-start | bytes 393224 | tf_op jit(solution)/shard_map/ppermute | solution.py:343
  135.6 6.8 %collective-permute-start.24 = (bf16[1024,128]{1,0:T(8,128)(2,1)S(1)}, bf16[1024,128]{1,0:T(8,128)(2,1)S(1)}, u32[]{:S(2)}, u32[]{:S(2)}) collective-permute-start(bf16[1024,128]{1,0:T(8,128)(2,1)S(1)} %joined.2.refs_1_), channel_id=1, source_target_pairs={{0,4},{4,0},{8,12},{12,8},{16,20},{20,16},{24,28},{28,24},{1,5},{5... | collective-permute-start | bytes 786440 | tf_op jit(solution)/shard_map/ppermute | solution.py:343
  (22 other events, 99.7 us)

commit v18 on v17

--- a/solution.py
+++ b/solution.py
@@ -10,7 +10,7 @@
 
 F32 = jnp.float32
 BF16 = jnp.bfloat16
-VMEM_BYTES = 40 * 2**20
+VMEM_BYTES = 20 * 2**20
 NT = (((1,), (1,)), ((), ()))
 TN = (((0,), (0,)), ((), ()))
 
@@ -524,9 +524,9 @@
     brought.insert(1, across)
     tap_sum = Sum(me, held_until([tap_grad], [mixed_one])[0])
     previous, landed = landed, passed_on([mixed_one])
-    given = held_until([grad_filtered], previous)[0]
+    given = held_until([grad_filtered], landed)[0]
     following = lax.ppermute(given, "ctx", [(i + 1, i) for i in range(n_ctx - 1)])
-    last_part = weight_pass(me, out_weight, 0, gated, after=landed + [mixed_one, following])[0]
+    last_part = weight_pass(me, out_weight, 0, gated, after=landed + [mixed_one])[0]
 
     terms = dict(zip(terms, held_until(terms.values(), previous)))
     terms[0] = last_part + swap(mixed_one, "chan", 1).astype(F32)
@@ -554,7 +554,7 @@
     wide = piece % 128 == 0 and 2 * early == n_ctx
     columns = {off: [(part[off], 0) for part in cols] for off in evens}
     crossed = jnp.concatenate([part[off] for off in evens for part in cols], axis=0)
-    crossed = swap(held_until([crossed], far + [last_part])[0], "chan", 1)
+    crossed = swap(held_until([crossed], far + [last_part, following])[0], "chan", 1)
     if wide:
         for at, off in enumerate(evens):
             columns[off + 1] = [(crossed, 2 * at), (crossed, 2 * at + 1)]

time: 145 us -> 157 us (1.083)
  local copies, waits for them, and re-layouts: 3.54 us -> 23.5 us
  starting transfers between devices: 31.1 us -> 25.6 us
  Pallas kernels: 65.4 us -> 61.1 us
  waiting for transfers between devices: 37.1 us -> 38.8 us
    unnamed x61 -> x57, local copies, waits for them, and re-layouts: 2.85 us -> 23.1 us
    ppermute x6, waiting for transfers between devices: 23.1 us -> 12.4 us  [passed_on(): came = [lax.ppermute(onto, 'ctx', ahead), lax.ppermute(back, 'ctx', behind)]]
    ppermute x1, waiting for transfers between devices: 0.01 us -> 8.95 us  [per_device(): lax.ppermute(back[half:], 'ctx', behind)]
    ppermute x14, starting transfers between devices: 12.6 us -> 7.51 us  [swap(): return lax.ppermute(block, axis, [(i, i ^ bit) for i in range(size)])]
    pallas_call x6, Pallas kernels: 39.9 us -> 35.5 us  [weight_pass(): pl.pallas_call(ignoring(body, len(after), 1 + len(arrays)), grid_spec=plt...]
    ppermute x14, waiting for transfers between devices: 11.1 us -> 14.3 us  [swap(): return lax.ppermute(block, axis, [(i, i ^ bit) for i in range(size)])]
    ppermute x1, starting transfers between devices: 0.44 us -> 2.69 us  [per_device(): lax.ppermute(back[half:], 'ctx', behind)]
    ppermute x6, starting transfers between devices: 8.07 us -> 6.17 us  [passed_on(): came = [lax.ppermute(onto, 'ctx', ahead), lax.ppermute(back, 'ctx', behind)]]
  transfers between devices with their start and end apart: 25 -> 25, of which waited for: 9 -> 10; matrix products, arithmetic and copies ran while one was open for 2% -> 2% of each run, Pallas kernels for 44% -> 38%
where the time goes in v18:
time: 157 us; the launch traced here: 156 us
  Pallas kernels  61.1 us (39%)
  waiting for transfers between devices  38.8 us (25%)
  starting transfers between devices  25.6 us (16%)
  local copies, waits for them, and re-layouts  23.5 us (15%)
  other arithmetic  5.74 us (4%)
    pallas_call x6, Pallas kernels, weight_pass(): pl.pallas_call(ignoring(body, len(after), 1 + len(arrays)), grid_spec=plt...  35.5 us
    unnamed x57, local copies, waits for them, and re-layouts  23.1 us
    ppermute x14, waiting for transfers between devices, swap(): return lax.ppermute(block, axis, [(i, i ^ bit) for i in range(size)])  14.3 us
    ppermute x6, waiting for transfers between devices, passed_on(): came = [lax.ppermute(onto, 'ctx', ahead), lax.ppermute(back, 'ctx', behind)]  12.4 us
    pallas_call x3, Pallas kernels, by_channel(): pl.pallas_call(ignoring(functools.partial(kernel, length), len(after), le...  10.8 us
    pallas_call x2, Pallas kernels, grad_weight_of(): pl.pallas_call(ignoring(functools.partial(weight_kernel, places, parts),...  10 us
    ppermute x1, waiting for transfers between devices, per_device(): lax.ppermute(back[half:], 'ctx', behind)  8.95 us
    ppermute x14, starting transfers between devices, swap(): return lax.ppermute(block, axis, [(i, i ^ bit) for i in range(size)])  7.51 us
  transfers between devices with their start and end apart: 25, of which 10 were waited for; matrix products, arithmetic and copies ran while one was open for 2% of the time, Pallas kernels for 38%

profile of v18, /device:TPU:0, one launch (start us, length us, event | category | flops | bytes accessed | tf_op | source)
XLA Modules:
  0.0 156.0 jit_solution(14736759838153763189)
XLA Ops:
  0.6 2.2 %multiply_convert_fusion = bf16[128,2048]{1,0:T(8,128)(2,1)} fusion(bf16[128,2048]{1,0:T(8,128)(2,1)} %refs_1_.18, bf16[128,2048]{1,0:T(8,128)(2,1)} %refs_0_.5), kind=kLoop, calls=%fused_computation.2 | loop fusion | flops 1048576 | bytes 1572864 | tf_op jit(solution)/shard_map/convert_element_type | solution.py:444
  2.8 2.9 %collective-permute-start.2 = (bf16[128,2048]{1,0:T(8,128)(2,1)S(1)}, bf16[128,2048]{1,0:T(8,128)(2,1)S(1)}, u32[]{:S(2)}, u32[]{:S(2)}) collective-permute-start(bf16[128,2048]{1,0:T(8,128)(2,1)S(1)} %copy-done.6), channel_id=1, source_target_pairs={{0,2},{1,3},{2,0},{3,1},{4,6},{5,7},{6,4},{7,5},{8,10},{9,11},{10,... | collective-permute-start | bytes 1572872 | tf_op jit(solution)/shard_map/ppermute | solution.py:343
  5.8 3.4 %collective-permute-start = (bf16[128,2048]{1,0:T(8,128)(2,1)}, bf16[128,2048]{1,0:T(8,128)(2,1)S(1)}, u32[]{:S(2)}, u32[]{:S(2)}) collective-permute-start(bf16[128,2048]{1,0:T(8,128)(2,1)} %multiply_convert_fusion), channel_id=1, source_target_pairs={{0,4},{4,8},{8,12},{12,16},{16,20},{20,24},{24,28},{1,5},{5,9},{9,... | collective-permute-start | bytes 1572872 | tf_op jit(solution)/shard_map/ppermute | solution.py:446
  9.3 10.5 %copy-done = bf16[2048,8192]{1,0:T(8,128)(2,1)S(1)} copy-done((bf16[2048,8192]{1,0:T(8,128)(2,1)S(1)}, bf16[2048,8192]{1,0:T(8,128)(2,1)}, u32[]{:S(2)}) %copy-start) | copy-done | bytes 33554456
  19.8 4.2 %grad_gated_part.2.refs_3_ = f32[2048,128]{1,0:T(8,128)S(1)} custom-call(s32[2]{0:T(128)S(1)} %pad_add_fusion.refs_0_, bf16[2048,8192]{1,0:T(8,128)(2,1)S(1)} %copy-done, bf16[128,2048]{1,0:T(8,128)(2,1)S(1)} %copy-done.6), custom_call_target="tpu_custom_call" | custom-call | flops 3000000000 | tf_op jit(solution)/shard_map/grad_gated_part/pallas_call | solution.py:190
  24.4 6.3 %grad_gated_part.3.refs_7_.refs_6_.refs_4_ = f32[2048,128]{1,0:T(8,128)S(1)} custom-call(s32[2]{0:T(128)S(1)} %pad_add_fusion.refs_0_, bf16[2048,8192]{1,0:T(8,128)(2,1)} %refs_1_.17, bf16[128,2048]{1,0:T(8,128)(2,1)S(1)} %collective-permute-done.1.refs_2_.refs_3_, f32[2048,128]{1,0:T(8,128)S(1)} %grad_gated_part.2.refs_3_), custom_call_target="tpu_custom_call" | custom-call | flops 3000000000 | tf_op jit(solution)/shard_map/grad_gated_part/pallas_call | solution.py:190
  32.6 3.3 %forward_filter.1 = (bf16[128,2048]{1,0:T(8,128)(2,1)S(1)}, f32[128,2048]{1,0:T(8,128)S(1)}) custom-call(bf16[128,2048]{1,0:T(8,128)(2,1)S(1)} %copy-done.9, bf16[128,2048]{1,0:T(8,128)(2,1)S(1)} %copy-done.10, bf16[128,2048]{1,0:T(8,128)(2,1)S(1)} %copy-done.11, bf16[128,2048]{1,0:T(8,128)(2,1)S(1)} %copy-done.17, bf16[2048,128]{1,0:T(8,128)(2,1)S(1)} %copy-done.14, ...), custom_call_target="tpu_custom_call" | custom-call | flops 3000000000 | tf_op jit(solution)/shard_map/forward_filter/pallas_call | solution.py:107
  38.0 1.5 collective-permute-start.4
  40.0 7.4 %grads_and_mixed.2 = (f32[2048,128]{1,0:T(8,128)S(1)}, f32[128,2048]{1,0:T(8,128)S(1)}) custom-call(s32[2]{0:T(128)S(1)} %pad_add_fusion.refs_0_, bf16[2048,8192]{1,0:T(8,128)(2,1)} %refs_1_.17, bf16[128,2048]{1,0:T(8,128)(2,1)S(1)} %get-tuple-element.44.refs_2_.refs_1_, bf16[128,2048]{1,0:T(8,128)(2,1)S(1)} %collective-permute-done.2.refs_4_.refs_3_, ...), custom_call_target="tpu_custom_call" | custom-call | flops 500000000 | tf_op jit(solution)/shard_map/grads_and_mixed/pallas_call | solution.py:190
  47.4 8.5 %grads_and_mixed.3 = (bf16[128,2048]{1,0:T(8,128)(2,1)}, bf16[128,2048]{1,0:T(8,128)(2,1)S(1)}, bf16[128,2048]{1,0:T(8,128)(2,1)}) custom-call(s32[2]{0:T(128)S(1)} %pad_add_fusion.refs_0_, bf16[2048,8192]{1,0:T(8,128)(2,1)} %refs_1_.17, bf16[128,2048]{1,0:T(8,128)(2,1)S(1)} %get-tuple-element.44.refs_2_.refs_1_, ...), custom_call_target="tpu_custom_call" | custom-call | flops 500000000 | tf_op jit(solution)/shard_map/grads_and_mixed/pallas_call | solution.py:190
  57.8 1.6 %collective-permute-start.6 = (bf16[160,2048]{1,0:T(8,128)(2,1)S(1)}, bf16[160,2048]{1,0:T(8,128)(2,1)S(1)}, u32[]{:S(2)}, u32[]{:S(2)}) collective-permute-start(bf16[160,2048]{1,0:T(8,128)(2,1)S(1)} %slice.82), channel_id=1, source_target_pairs={{0,8},{8,16},{16,24},{24,28},{28,20},{20,12},{12,4},{4,0},{1,9},{9... | collective-permute-start | bytes 1966088 | tf_op jit(solution)/shard_map/ppermute | solution.py:490
  61.1 3.5 %tap_grad.1.refs_3_ = bf16[2048,128]{1,0:T(8,128)(2,1)S(1)} custom-call(bf16[128,2048]{1,0:T(8,128)(2,1)S(1)} %copy-done.10, bf16[128,2048]{1,0:T(8,128)(2,1)S(1)} %copy-done.12, bf16[128,2048]{1,0:T(8,128)(2,1)S(1)} %copy-done.18, bf16[128,2048]{1,0:T(8,128)(2,1)S(1)} %get-tuple-element.59.refs_3_.refs_2_, bf16[2,256,256]{2,1,0:T(8,128)(2,1)S(1)} %copy-done.20, ...), custom_call_target="tpu_custom_call" | custom-call | flops 3000000000 | tf_op jit(solution)/shard_map/tap_grad/pallas_call | solution.py:107
  64.6 10.5 %copy-done.1 = bf16[2048,8192]{1,0:T(8,128)(2,1)S(1)} copy-done((bf16[2048,8192]{1,0:T(8,128)(2,1)S(1)}, bf16[2048,8192]{1,0:T(8,128)(2,1)}, u32[]{:S(2)}) %copy-start.1) | copy-done | bytes 33554456
  75.2 3.4 %mixed_part.2.refs_5_ = bf16[128,2048]{1,0:T(8,128)(2,1)S(1)} custom-call(s32[2]{0:T(128)S(1)} %pad_add_fusion.refs_0_, bf16[2048,8192]{1,0:T(8,128)(2,1)S(1)} %copy-done.1, bf16[128,2048]{1,0:T(8,128)(2,1)S(1)} %get-tuple-element.44.refs_2_.refs_1_, bf16[2048,128]{1,0:T(8,128)(2,1)S(1)} %tap_grad.1.refs_3_), custom_call_target="tpu_custom_call" | custom-call | flops 500000000 | tf_op jit(solution)/shard_map/mixed_part/pallas_call | solution.py:190
  78.6 3.5 %collective-permute-start.15 = (bf16[16,2048]{1,0:T(8,128)(2,1)S(1)}, bf16[16,2048]{1,0:T(8,128)(2,1)S(1)}, u32[]{:S(2)}, u32[]{:S(2)}) collective-permute-start(bf16[16,2048]{1,0:T(8,128)(2,1)S(1)} %get-tuple-element.63), channel_id=1, source_target_pairs={{0,28},{8,20},{16,12},{24,4},{28,0},{20,8},{12,16},{4,24},{1,29},{... | collective-permute-start | bytes 196616 | tf_op jit(solution)/shard_map/ppermute | solution.py:519
  82.7 3.1 %collective-permute-done.15 = bf16[16,2048]{1,0:T(8,128)(2,1)S(1)} collective-permute-done((bf16[16,2048]{1,0:T(8,128)(2,1)S(1)}, bf16[16,2048]{1,0:T(8,128)(2,1)S(1)}, u32[]{:S(2)}, u32[]{:S(2)}) %collective-permute-start.15) | collective-permute-done | bytes 65568 | tf_op jit(solution)/shard_map/ppermute | solution.py:519
  85.9 2.0 %collective-permute-start.9 = (bf16[144,2048]{1,0:T(8,128)(2,1)S(1)}, bf16[144,2048]{1,0:T(8,128)(2,1)S(1)}, u32[]{:S(2)}, u32[]{:S(2)}) collective-permute-start(bf16[144,2048]{1,0:T(8,128)(2,1)S(1)} %slice.85), channel_id=1, source_target_pairs={{8,0},{16,8},{24,16},{28,24},{20,28},{12,20},{4,12},{0,4},{9,1},{1... | collective-permute-start | bytes 1769480 | tf_op jit(solution)/shard_map/ppermute | solution.py:490
  88.6 2.8 %collective-permute-done.14.refs_2_ = bf16[1024,128]{1,0:T(8,128)(2,1)S(1)} collective-permute-done((bf16[1024,128]{1,0:T(8,128)(2,1)S(1)}, bf16[1024,128]{1,0:T(8,128)(2,1)S(1)}, u32[]{:S(2)}, u32[]{:S(2)}) %collective-permute-start.14) | collective-permute-done | bytes 262176 | tf_op jit(solution)/shard_map/ppermute | solution.py:343
  91.5 10.8 %collective-permute-done.8.refs_3_.refs_8_ = bf16[144,2048]{1,0:T(8,128)(2,1)S(1)} collective-permute-done((bf16[144,2048]{1,0:T(8,128)(2,1)S(1)}, bf16[144,2048]{1,0:T(8,128)(2,1)S(1)}, u32[]{:S(2)}, u32[]{:S(2)}) %collective-permute-start.8) | collective-permute-done | bytes 589856 | tf_op jit(solution)/shard_map/ppermute | solution.py:490
  102.2 1.3 collective-permute-start.13
  104.9 2.7 %collective-permute-start.18 = (bf16[64,2048]{1,0:T(8,128)(2,1)S(1)}, bf16[64,2048]{1,0:T(8,128)(2,1)S(1)}, u32[]{:S(2)}, u32[]{:S(2)}) collective-permute-start(bf16[64,2048]{1,0:T(8,128)(2,1)S(1)} %slice.75), channel_id=1, source_target_pairs={{8,0},{16,8},{24,16},{28,24},{20,28},{12,20},{4,12},{0,4},{9,1},{1... | collective-permute-start | bytes 786440 | tf_op jit(solution)/shard_map/ppermute | solution.py:547
  108.7 5.7 %mixed_part.3 = f32[128,2048]{1,0:T(8,128)S(1)} custom-call(s32[2]{0:T(128)S(1)} %pad_add_fusion.refs_0_, bf16[2048,8192]{1,0:T(8,128)(2,1)} %refs_1_.17, bf16[128,2048]{1,0:T(8,128)(2,1)S(1)} %get-tuple-element.44.refs_2_.refs_1_, bf16[144,2048]{1,0:T(8,128)(2,1)S(1)} %collective-permute-done.8.refs_3_.refs_8_, ...), custom_call_target="tpu_custom_call" | custom-call | flops 500000000 | tf_op jit(solution)/shard_map/mixed_part/pallas_call | solution.py:190
  114.5 8.9 %collective-permute-done.18.refs_3_ = bf16[64,2048]{1,0:T(8,128)(2,1)S(1)} collective-permute-done((bf16[64,2048]{1,0:T(8,128)(2,1)S(1)}, bf16[64,2048]{1,0:T(8,128)(2,1)S(1)}, u32[]{:S(2)}, u32[]{:S(2)}) %collective-permute-start.18) | collective-permute-done | bytes 262176 | tf_op jit(solution)/shard_map/ppermute | solution.py:547
  124.4 1.7 %collective-permute-done.20.refs_12_.refs_13_.refs_16_.refs_17_ = bf16[256,2048]{1,0:T(8,128)(2,1)S(1)} collective-permute-done((bf16[256,2048]{1,0:T(8,128)(2,1)S(1)}, bf16[256,2048]{1,0:T(8,128)(2,1)S(1)}, u32[]{:S(2)}, u32[]{:S(2)}) %collective-permute-start.20) | collective-permute-done | bytes 1048608 | tf_op jit(solution)/shard_map/ppermute | solution.py:343
  126.1 5.0 %grad_weight.2.refs_18_ = bf16[2048,1024]{1,0:T(8,128)(2,1)} custom-call(s32[2]{0:T(128)S(1)} %pad_add_fusion.refs_0_, bf16[128,2048]{1,0:T(8,128)(2,1)S(1)} %get-tuple-element.44.refs_2_.refs_1_, bf16[64,2048]{1,0:T(8,128)(2,1)S(1)} %collective-permute-done.17.refs_2_, bf16[64,2048]{1,0:T(8,128)(2,1)S(1)} %collective-permute-done.18.refs_3_, ...), custom_call_target="tpu_custom_call" | custom-call | flops 2000000000 | tf_op jit(solution)/shard_map/grad_weight/pallas_call | solution.py:293
  131.8 5.0 %grad_weight.3 = bf16[2048,1024]{1,0:T(8,128)(2,1)} custom-call(s32[2]{0:T(128)S(1)} %pad_add_fusion.refs_0_, bf16[128,2048]{1,0:T(8,128)(2,1)S(1)} %get-tuple-element.44.refs_2_.refs_1_, bf16[64,2048]{1,0:T(8,128)(2,1)S(1)} %collective-permute-done.17.refs_2_, ...), custom_call_target="tpu_custom_call", output_to_operand_aliasing={{}: (18, {})} | custom-call | flops 2000000000 | tf_op jit(solution)/shard_map/grad_weight/pallas_call | solution.py:293
  136.8 3.4 %collective-permute-done.22.refs_2_ = bf16[512,128]{1,0:T(8,128)(2,1)S(1)} collective-permute-done((bf16[512,128]{1,0:T(8,128)(2,1)S(1)}, bf16[512,128]{1,0:T(8,128)(2,1)S(1)}, u32[]{:S(2)}, u32[]{:S(2)}) %collective-permute-start.22) | collective-permute-done | bytes 131104 | tf_op jit(solution)/shard_map/ppermute | solution.py:343
  140.9 4.0 %backward_filter.1 = (bf16[128,2048]{1,0:T(8,128)(2,1)}, bf16[128,2048]{1,0:T(8,128)(2,1)}) custom-call(bf16[128,2048]{1,0:T(8,128)(2,1)S(1)} %copy-done.10, bf16[128,2048]{1,0:T(8,128)(2,1)S(1)} %copy-done.12, bf16[128,2048]{1,0:T(8,128)(2,1)S(1)} %get-tuple-element.59.refs_3_.refs_2_, bf16[128,2048]{1,0:T(8,128)(2,1)S(1)} %collective-permute-done.13.refs_3_, ...), custom_call_target="tpu_custom_call" | custom-call | flops 3000000000 | tf_op jit(solution)/shard_map/backward_filter/pallas_call | solution.py:107
  144.8 1.4 collective-permute-done.23.refs_2_
  146.9 1.5 collective-permute-start.24
  149.3 5.0 %collective-permute-done.24.refs_2_ = bf16[1024,128]{1,0:T(8,128)(2,1)S(1)} collective-permute-done((bf16[1024,128]{1,0:T(8,128)(2,1)S(1)}, bf16[1024,128]{1,0:T(8,128)(2,1)S(1)}, u32[]{:S(2)}, u32[]{:S(2)}) %collective-permute-start.24) | collective-permute-done | bytes 262176 | tf_op jit(solution)/shard_map/ppermute | solution.py:343
  154.3 1.6 %joined.3 = f32[2048,128]{1,0:T(8,128)} custom-call(s32[2]{0:T(128)S(1)} %pad_add_fusion.refs_0_, bf16[1024,128]{1,0:T(8,128)(2,1)S(1)} %joined.2.refs_1_, bf16[1024,128]{1,0:T(8,128)(2,1)S(1)} %collective-permute-done.24.refs_2_), custom_call_target="tpu_custom_call" | custom-call | flops 500000000 | tf_op jit(solution)/shard_map/joined/pallas_call | solution.py:422
  (114 shorter events, 15.8 us)
Async XLA Ops:
  2.8 21.3 %collective-permute-start.2 = (bf16[128,2048]{1,0:T(8,128)(2,1)S(1)}, bf16[128,2048]{1,0:T(8,128)(2,1)S(1)}, u32[]{:S(2)}, u32[]{:S(2)}) collective-permute-start(bf16[128,2048]{1,0:T(8,128)(2,1)S(1)} %copy-done.6), channel_id=1, source_target_pairs={{0,2},{1,3},{2,0},{3,1},{4,6},{5,7},{6,4},{7,5},{8,10},{9,11},{10,... | collective-permute-start | bytes 1572872 | tf_op jit(solution)/shard_map/ppermute | solution.py:343
  5.8 18.7 %collective-permute-start.1 = (bf16[128,2048]{1,0:T(8,128)(2,1)S(1)}, bf16[128,2048]{1,0:T(8,128)(2,1)S(1)}, u32[]{:S(2)}, u32[]{:S(2)}) collective-permute-start(bf16[128,2048]{1,0:T(8,128)(2,1)S(1)} %copy-done.6), channel_id=1, source_target_pairs={{0,1},{1,0},{2,3},{3,2},{4,5},{5,4},{6,7},{7,6},{8,9},{9,8},{10,11... | collective-permute-start | bytes 1572872 | tf_op jit(solution)/shard_map/ppermute | solution.py:343
  5.8 25.0 %collective-permute-start = (bf16[128,2048]{1,0:T(8,128)(2,1)}, bf16[128,2048]{1,0:T(8,128)(2,1)S(1)}, u32[]{:S(2)}, u32[]{:S(2)}) collective-permute-start(bf16[128,2048]{1,0:T(8,128)(2,1)} %multiply_convert_fusion), channel_id=1, source_target_pairs={{0,4},{4,8},{8,12},{12,16},{16,20},{20,24},{24,28},{1,5},{5,9},{9,... | collective-permute-start | bytes 1572872 | tf_op jit(solution)/shard_map/ppermute | solution.py:446
  9.3 10.5 %copy-start = (bf16[2048,8192]{1,0:T(8,128)(2,1)S(1)}, bf16[2048,8192]{1,0:T(8,128)(2,1)}, u32[]{:S(2)}) copy-start(bf16[2048,8192]{1,0:T(8,128)(2,1)} %refs_1_.17) | copy-start | bytes 100663296
  24.1 11.8 %collective-permute-start.3 = (bf16[128,2048]{1,0:T(8,128)(2,1)S(1)}, bf16[128,2048]{1,0:T(8,128)(2,1)S(1)}, u32[]{:S(2)}, u32[]{:S(2)}) collective-permute-start(bf16[128,2048]{1,0:T(8,128)(2,1)S(1)} %collective-permute-done.2.refs_4_.refs_3_), channel_id=1, source_target_pairs={{0,1},{1,0},{2,3},{3,2},{4,5},{5,4},{6,7},{7,6},{8,9},{9,8},{10,11... | collective-permute-start | bytes 1572872 | tf_op jit(solution)/shard_map/ppermute | solution.py:343
  38.0 18.5 %collective-permute-start.4 = (bf16[176,2048]{1,0:T(8,128)(2,1)}, bf16[176,2048]{1,0:T(8,128)(2,1)S(1)}, u32[]{:S(2)}, u32[]{:S(2)}) collective-permute-start(bf16[176,2048]{1,0:T(8,128)(2,1)} %get-tuple-element.46), channel_id=1, source_target_pairs={{0,8},{8,16},{16,24},{24,28},{28,20},{20,12},{12,4},{4,0},{1,9},{9... | collective-permute-start | bytes 2162696 | tf_op jit(solution)/shard_map/ppermute | solution.py:490
  39.5 18.2 %collective-permute-start.5 = (bf16[176,2048]{1,0:T(8,128)(2,1)}, bf16[176,2048]{1,0:T(8,128)(2,1)S(1)}, u32[]{:S(2)}, u32[]{:S(2)}) collective-permute-start(bf16[176,2048]{1,0:T(8,128)(2,1)} %get-tuple-element.47), channel_id=1, source_target_pairs={{8,0},{16,8},{24,16},{28,24},{20,28},{12,20},{4,12},{0,4},{9,1},{1... | collective-permute-start | bytes 2162696 | tf_op jit(solution)/shard_map/ppermute | solution.py:490
  47.4 8.5 %copy-start.7 = (f32[128,2048]{1,0:T(8,128)}, f32[128,2048]{1,0:T(8,128)S(1)}, u32[]{:S(2)}) copy-start(f32[128,2048]{1,0:T(8,128)S(1)} %get-tuple-element.55) | copy-start | bytes 3145732
  55.9 4.0 %collective-permute-start.11 = (bf16[128,2048]{1,0:T(8,128)(2,1)}, bf16[128,2048]{1,0:T(8,128)(2,1)}, u32[]{:S(2)}, u32[]{:S(2)}) collective-permute-start(bf16[128,2048]{1,0:T(8,128)(2,1)} %get-tuple-element.56), channel_id=1, source_target_pairs={{0,1},{1,0},{2,3},{3,2},{4,5},{5,4},{6,7},{7,6},{8,9},{9,8},{10,11... | collective-permute-start | bytes 1572872 | tf_op jit(solution)/shard_map/ppermute | solution.py:343
  56.5 26.2 %copy-start.2 = (bf16[176,2048]{1,0:T(8,128)(2,1)}, bf16[176,2048]{1,0:T(8,128)(2,1)S(1)}, u32[]{:S(2)}) copy-start(bf16[176,2048]{1,0:T(8,128)(2,1)S(1)} %collective-permute-done.4.refs_6_.refs_4_) | copy-start | bytes 2162692
  57.7 24.9 %copy-start.4 = (bf16[176,2048]{1,0:T(8,128)(2,1)}, bf16[176,2048]{1,0:T(8,128)(2,1)S(1)}, u32[]{:S(2)}) copy-start(bf16[176,2048]{1,0:T(8,128)(2,1)S(1)} %collective-permute-done.5.refs_7_.refs_5_) | copy-start | bytes 2162692
  57.8 28.0 %collective-permute-start.6 = (bf16[160,2048]{1,0:T(8,128)(2,1)S(1)}, bf16[160,2048]{1,0:T(8,128)(2,1)S(1)}, u32[]{:S(2)}, u32[]{:S(2)}) collective-permute-start(bf16[160,2048]{1,0:T(8,128)(2,1)S(1)} %slice.82), channel_id=1, source_target_pairs={{0,8},{8,16},{16,24},{24,28},{28,20},{20,12},{12,4},{4,0},{1,9},{9... | collective-permute-start | bytes 1966088 | tf_op jit(solution)/shard_map/ppermute | solution.py:490
  59.4 26.3 %collective-permute-start.7 = (bf16[160,2048]{1,0:T(8,128)(2,1)S(1)}, bf16[160,2048]{1,0:T(8,128)(2,1)S(1)}, u32[]{:S(2)}, u32[]{:S(2)}) collective-permute-start(bf16[160,2048]{1,0:T(8,128)(2,1)S(1)} %slice.83), channel_id=1, source_target_pairs={{8,0},{16,8},{24,16},{28,24},{20,28},{12,20},{4,12},{0,4},{9,1},{1... | collective-permute-start | bytes 1966088 | tf_op jit(solution)/shard_map/ppermute | solution.py:490
  64.6 10.5 %copy-start.1 = (bf16[2048,8192]{1,0:T(8,128)(2,1)S(1)}, bf16[2048,8192]{1,0:T(8,128)(2,1)}, u32[]{:S(2)}) copy-start(bf16[2048,8192]{1,0:T(8,128)(2,1)} %refs_1_.17) | copy-start | bytes 100663296
  78.6 7.1 %collective-permute-start.15 = (bf16[16,2048]{1,0:T(8,128)(2,1)S(1)}, bf16[16,2048]{1,0:T(8,128)(2,1)S(1)}, u32[]{:S(2)}, u32[]{:S(2)}) collective-permute-start(bf16[16,2048]{1,0:T(8,128)(2,1)S(1)} %get-tuple-element.63), channel_id=1, source_target_pairs={{0,28},{8,20},{16,12},{24,4},{28,0},{20,8},{12,16},{4,24},{1,29},{... | collective-permute-start | bytes 196616 | tf_op jit(solution)/shard_map/ppermute | solution.py:519
  82.1 9.3 %collective-permute-start.14 = (bf16[1024,128]{1,0:T(8,128)(2,1)S(1)}, bf16[1024,128]{1,0:T(8,128)(2,1)S(1)}, u32[]{:S(2)}, u32[]{:S(2)}) collective-permute-start(bf16[1024,128]{1,0:T(8,128)(2,1)S(1)} %get-tuple-element.88), channel_id=1, source_target_pairs={{0,4},{4,0},{8,12},{12,8},{16,20},{20,16},{24,28},{28,24},{1,5},{5... | collective-permute-start | bytes 786440 | tf_op jit(solution)/shard_map/ppermute | solution.py:343
  85.9 16.4 %collective-permute-start.8 = (bf16[144,2048]{1,0:T(8,128)(2,1)S(1)}, bf16[144,2048]{1,0:T(8,128)(2,1)S(1)}, u32[]{:S(2)}, u32[]{:S(2)}) collective-permute-start(bf16[144,2048]{1,0:T(8,128)(2,1)S(1)} %slice.84), channel_id=1, source_target_pairs={{0,8},{8,16},{16,24},{24,28},{28,20},{20,12},{12,4},{4,0},{1,9},{9... | collective-permute-start | bytes 1769480 | tf_op jit(solution)/shard_map/ppermute | solution.py:490
  85.9 16.3 %collective-permute-start.9 = (bf16[144,2048]{1,0:T(8,128)(2,1)S(1)}, bf16[144,2048]{1,0:T(8,128)(2,1)S(1)}, u32[]{:S(2)}, u32[]{:S(2)}) collective-permute-start(bf16[144,2048]{1,0:T(8,128)(2,1)S(1)} %slice.85), channel_id=1, source_target_pairs={{8,0},{16,8},{24,16},{28,24},{20,28},{12,20},{4,12},{0,4},{9,1},{1... | collective-permute-start | bytes 1769480 | tf_op jit(solution)/shard_map/ppermute | solution.py:490
  88.0 16.8 %collective-permute-start.16 = (bf16[64,2048]{1,0:T(8,128)(2,1)S(1)}, bf16[64,2048]{1,0:T(8,128)(2,1)S(1)}, u32[]{:S(2)}, u32[]{:S(2)}) collective-permute-start(bf16[64,2048]{1,0:T(8,128)(2,1)S(1)} %get-tuple-element.95.refs_10_), channel_id=1, source_target_pairs={{0,2},{1,3},{2,0},{3,1},{4,6},{5,7},{6,4},{7,5},{8,10},{9,11},{10,... | collective-permute-start | bytes 786440 | tf_op jit(solution)/shard_map/ppermute | solution.py:343
  102.2 21.2 %collective-permute-start.13 = (bf16[128,2048]{1,0:T(8,128)(2,1)S(1)}, bf16[128,2048]{1,0:T(8,128)(2,1)S(1)}, u32[]{:S(2)}, u32[]{:S(2)}) collective-permute-start(bf16[128,2048]{1,0:T(8,128)(2,1)S(1)} %get-tuple-element.59.refs_3_.refs_2_), channel_id=1, source_target_pairs={{4,0},{8,4},{12,8},{16,12},{20,16},{24,20},{28,24},{5,1},{9,5},{13... | collective-permute-start | bytes 1572872 | tf_op jit(solution)/shard_map/ppermute | solution.py:528
  103.6 10.9 %collective-permute-start.19 = (bf16[64,2048]{1,0:T(8,128)(2,1)S(1)}, bf16[64,2048]{1,0:T(8,128)(2,1)S(1)}, u32[]{:S(2)}, u32[]{:S(2)}) collective-permute-start(bf16[64,2048]{1,0:T(8,128)(2,1)S(1)} %pad_maximum_fusion.2.refs_11_), channel_id=1, source_target_pairs={{0,2},{1,3},{2,0},{3,1},{4,6},{5,7},{6,4},{7,5},{8,10},{9,11},{10,... | collective-permute-start | bytes 786440 | tf_op jit(solution)/shard_map/ppermute | solution.py:343
  104.9 18.5 %collective-permute-start.18 = (bf16[64,2048]{1,0:T(8,128)(2,1)S(1)}, bf16[64,2048]{1,0:T(8,128)(2,1)S(1)}, u32[]{:S(2)}, u32[]{:S(2)}) collective-permute-start(bf16[64,2048]{1,0:T(8,128)(2,1)S(1)} %slice.75), channel_id=1, source_target_pairs={{8,0},{16,8},{24,16},{28,24},{20,28},{12,20},{4,12},{0,4},{9,1},{1... | collective-permute-start | bytes 786440 | tf_op jit(solution)/shard_map/ppermute | solution.py:547
  107.6 15.8 %collective-permute-start.17 = (bf16[64,2048]{1,0:T(8,128)(2,1)S(1)}, bf16[64,2048]{1,0:T(8,128)(2,1)S(1)}, u32[]{:S(2)}, u32[]{:S(2)}) collective-permute-start(bf16[64,2048]{1,0:T(8,128)(2,1)S(1)} %slice.74), channel_id=1, source_target_pairs={{0,8},{8,16},{16,24},{24,28},{28,20},{20,12},{12,4},{4,0},{1,9},{9... | collective-permute-start | bytes 786440 | tf_op jit(solution)/shard_map/ppermute | solution.py:547
  108.7 17.4 %copy-start.3 = (bf16[176,2048]{1,0:T(8,128)(2,1)S(1)}, bf16[176,2048]{1,0:T(8,128)(2,1)}, u32[]{:S(2)}) copy-start(bf16[176,2048]{1,0:T(8,128)(2,1)} %copy-done.2) | copy-start | bytes 2162692
  108.7 17.4 %copy-start.5 = (bf16[176,2048]{1,0:T(8,128)(2,1)S(1)}, bf16[176,2048]{1,0:T(8,128)(2,1)}, u32[]{:S(2)}) copy-start(bf16[176,2048]{1,0:T(8,128)(2,1)} %copy-done.4) | copy-start | bytes 2162692
  123.4 2.7 %collective-permute-start.20 = (bf16[256,2048]{1,0:T(8,128)(2,1)S(1)}, bf16[256,2048]{1,0:T(8,128)(2,1)S(1)}, u32[]{:S(2)}, u32[]{:S(2)}) collective-permute-start(bf16[256,2048]{1,0:T(8,128)(2,1)S(1)} %constant_dynamic-update-slice_fusion.4), channel_id=1, source_target_pairs={{0,1},{1,0},{2,3},{3,2},{4,5},{5,4},{6,7},{7,6},{8,9},{9,8},{10,11... | collective-permute-start | bytes 3145736 | tf_op jit(solution)/shard_map/ppermute | solution.py:343
  123.4 24.9 %collective-permute-start.10 = (bf16[128,2048]{1,0:T(8,128)(2,1)S(1)}, bf16[128,2048]{1,0:T(8,128)(2,1)S(1)}, u32[]{:S(2)}, u32[]{:S(2)}) collective-permute-start(bf16[128,2048]{1,0:T(8,128)(2,1)S(1)} %mixed_part.2.refs_5_), channel_id=1, source_target_pairs={{0,1},{1,0},{2,3},{3,2},{4,5},{5,4},{6,7},{7,6},{8,9},{9,8},{10,11... | collective-permute-start | bytes 1572872 | tf_op jit(solution)/shard_map/ppermute | solution.py:343
  123.9 24.4 %collective-permute-start.12 = (bf16[128,2048]{1,0:T(8,128)(2,1)S(1)}, bf16[128,2048]{1,0:T(8,128)(2,1)S(1)}, u32[]{:S(2)}, u32[]{:S(2)}) collective-permute-start(bf16[128,2048]{1,0:T(8,128)(2,1)S(1)} %convert_add_fusion), channel_id=1, source_target_pairs={{0,2},{1,3},{2,0},{3,1},{4,6},{5,7},{6,4},{7,5},{8,10},{9,11},{10,... | collective-permute-start | bytes 1572872 | tf_op jit(solution)/shard_map/ppermute | solution.py:343
  124.4 6.7 %collective-permute-start.21 = (bf16[512,128]{1,0:T(8,128)(2,1)S(1)}, bf16[512,128]{1,0:T(8,128)(2,1)S(1)}, u32[]{:S(2)}, u32[]{:S(2)}) collective-permute-start(bf16[512,128]{1,0:T(8,128)(2,1)S(1)} %get-tuple-element.74), channel_id=1, source_target_pairs={{0,8},{4,12},{8,0},{12,4},{16,24},{20,28},{24,16},{28,20},{1,9},{5... | collective-permute-start | bytes 393224 | tf_op jit(solution)/shard_map/ppermute | solution.py:343
  131.7 8.5 %collective-permute-start.22 = (bf16[512,128]{1,0:T(8,128)(2,1)S(1)}, bf16[512,128]{1,0:T(8,128)(2,1)S(1)}, u32[]{:S(2)}, u32[]{:S(2)}) collective-permute-start(bf16[512,128]{1,0:T(8,128)(2,1)S(1)} %added.4.refs_1_), channel_id=1, source_target_pairs={{0,16},{4,20},{8,24},{12,28},{16,0},{20,4},{24,8},{28,12},{1,17},{... | collective-permute-start | bytes 393224 | tf_op jit(solution)/shard_map/ppermute | solution.py:343
  140.8 5.5 %collective-permute-start.23 = (bf16[512,128]{1,0:T(8,128)(2,1)S(1)}, bf16[512,128]{1,0:T(8,128)(2,1)S(1)}, u32[]{:S(2)}, u32[]{:S(2)}) collective-permute-start(bf16[512,128]{1,0:T(8,128)(2,1)S(1)} %added.5.refs_1_), channel_id=1, source_target_pairs={{0,8},{4,12},{8,0},{12,4},{16,24},{20,28},{24,16},{28,20},{1,9},{5... | collective-permute-start | bytes 393224 | tf_op jit(solution)/shard_map/ppermute | solution.py:343
  146.9 7.5 %collective-permute-start.24 = (bf16[1024,128]{1,0:T(8,128)(2,1)S(1)}, bf16[1024,128]{1,0:T(8,128)(2,1)S(1)}, u32[]{:S(2)}, u32[]{:S(2)}) collective-permute-start(bf16[1024,128]{1,0:T(8,128)(2,1)S(1)} %joined.2.refs_1_), channel_id=1, source_target_pairs={{0,4},{4,0},{8,12},{12,8},{16,20},{20,16},{24,28},{28,24},{1,5},{5... | collective-permute-start | bytes 786440 | tf_op jit(solution)/shard_map/ppermute | solution.py:343
  (19 other events, 91.8 us)

commit v19 on v18

--- a/solution.py
+++ b/solution.py
@@ -10,7 +10,7 @@
 
 F32 = jnp.float32
 BF16 = jnp.bfloat16
-VMEM_BYTES = 20 * 2**20
+VMEM_BYTES = 40 * 2**20
 NT = (((1,), (1,)), ((), ()))
 TN = (((0,), (0,)), ((), ()))
 

time: 157 us -> 144 us (0.917)
  local copies, waits for them, and re-layouts: 23.5 us -> 3.2 us
  Pallas kernels: 61.1 us -> 65.4 us
  starting transfers between devices: 25.6 us -> 29.9 us
    unnamed x57, local copies, waits for them, and re-layouts: 23.1 us -> 2.84 us
    ppermute x14, starting transfers between devices: 7.51 us -> 12.7 us  [swap(): return lax.ppermute(block, axis, [(i, i ^ bit) for i in range(size)])]
    pallas_call x6, Pallas kernels: 35.5 us -> 39.9 us  [weight_pass(): pl.pallas_call(ignoring(body, len(after), 1 + len(arrays)), grid_spec=plt...]
  transfers between devices with their start and end apart: 25 -> 25, of which waited for: 10 -> 11; matrix products, arithmetic and copies ran while one was open for 2% -> 2% of each run, Pallas kernels for 38% -> 44%
where the time goes in v19:
time: 144 us
  Pallas kernels  65.4 us (45%)
  waiting for transfers between devices  38.2 us (27%)
  starting transfers between devices  29.9 us (21%)
  other arithmetic  5.75 us (4%)
  local copies, waits for them, and re-layouts  3.2 us (2%)
    pallas_call x6, Pallas kernels, weight_pass(): pl.pallas_call(ignoring(body, len(after), 1 + len(arrays)), grid_spec=plt...  39.9 us
    ppermute x14, waiting for transfers between devices, swap(): return lax.ppermute(block, axis, [(i, i ^ bit) for i in range(size)])  13.4 us
    ppermute x6, waiting for transfers between devices, passed_on(): came = [lax.ppermute(onto, 'ctx', ahead), lax.ppermute(back, 'ctx', behind)]  13.4 us
    ppermute x14, starting transfers between devices, swap(): return lax.ppermute(block, axis, [(i, i ^ bit) for i in range(size)])  12.7 us
    pallas_call x3, Pallas kernels, by_channel(): pl.pallas_call(ignoring(functools.partial(kernel, length), len(after), le...  10.8 us
    pallas_call x2, Pallas kernels, grad_weight_of(): pl.pallas_call(ignoring(functools.partial(weight_kernel, places, parts),...  10 us
    ppermute x1, waiting for transfers between devices, per_device(): lax.ppermute(back[half:], 'ctx', behind)  7.68 us
    ppermute x6, starting transfers between devices, passed_on(): came = [lax.ppermute(onto, 'ctx', ahead), lax.ppermute(back, 'ctx', behind)]  6.18 us
  transfers between devices with their start and end apart: 25, of which 11 were waited for; matrix products, arithmetic and copies ran while one was open for 2% of the time, Pallas kernels for 44%

profile of v19, /device:TPU:0, one launch (start us, length us, event | category | flops | bytes accessed | tf_op | source)
XLA Modules:
  0.0 143.6 jit_solution(13306906205558421780)
XLA Ops:
  0.6 2.2 %multiply_convert_fusion = bf16[128,2048]{1,0:T(8,128)(2,1)} fusion(bf16[128,2048]{1,0:T(8,128)(2,1)} %refs_1_.18, bf16[128,2048]{1,0:T(8,128)(2,1)} %refs_0_.5), kind=kLoop, calls=%fused_computation.2 | loop fusion | flops 1048576 | bytes 1572864 | tf_op jit(solution)/shard_map/convert_element_type | solution.py:444
  2.8 2.9 %collective-permute-start.2 = (bf16[128,2048]{1,0:T(8,128)(2,1)S(1)}, bf16[128,2048]{1,0:T(8,128)(2,1)S(1)}, u32[]{:S(2)}, u32[]{:S(2)}) collective-permute-start(bf16[128,2048]{1,0:T(8,128)(2,1)S(1)} %copy-done.4), channel_id=1, source_target_pairs={{0,2},{1,3},{2,0},{3,1},{4,6},{5,7},{6,4},{7,5},{8,10},{9,11},{10,... | collective-permute-start | bytes 1572872 | tf_op jit(solution)/shard_map/ppermute | solution.py:343
  5.8 3.4 %collective-permute-start = (bf16[128,2048]{1,0:T(8,128)(2,1)}, bf16[128,2048]{1,0:T(8,128)(2,1)S(1)}, u32[]{:S(2)}, u32[]{:S(2)}) collective-permute-start(bf16[128,2048]{1,0:T(8,128)(2,1)} %multiply_convert_fusion), channel_id=1, source_target_pairs={{0,4},{4,8},{8,12},{12,16},{16,20},{20,24},{24,28},{1,5},{5,9},{9,... | collective-permute-start | bytes 1572872 | tf_op jit(solution)/shard_map/ppermute | solution.py:446
  9.3 6.2 %grad_gated_part.2.refs_3_ = f32[2048,128]{1,0:T(8,128)S(1)} custom-call(s32[2]{0:T(128)S(1)} %pad_add_fusion.refs_0_, bf16[2048,8192]{1,0:T(8,128)(2,1)} %refs_1_.17, bf16[128,2048]{1,0:T(8,128)(2,1)S(1)} %copy-done.4), custom_call_target="tpu_custom_call" | custom-call | flops 3000000000 | tf_op jit(solution)/shard_map/grad_gated_part/pallas_call | solution.py:190
  15.6 2.1 %collective-permute-done.2.refs_4_.refs_3_ = bf16[128,2048]{1,0:T(8,128)(2,1)S(1)} collective-permute-done((bf16[128,2048]{1,0:T(8,128)(2,1)S(1)}, bf16[128,2048]{1,0:T(8,128)(2,1)S(1)}, u32[]{:S(2)}, u32[]{:S(2)}) %collective-permute-start.2) | collective-permute-done | bytes 524320 | tf_op jit(solution)/shard_map/ppermute | solution.py:343
  17.7 6.2 %grad_gated_part.3.refs_7_.refs_6_.refs_4_ = f32[2048,128]{1,0:T(8,128)S(1)} custom-call(s32[2]{0:T(128)S(1)} %pad_add_fusion.refs_0_, bf16[2048,8192]{1,0:T(8,128)(2,1)} %refs_1_.17, bf16[128,2048]{1,0:T(8,128)(2,1)S(1)} %collective-permute-done.1.refs_2_.refs_3_, f32[2048,128]{1,0:T(8,128)S(1)} %grad_gated_part.2.refs_3_), custom_call_target="tpu_custom_call" | custom-call | flops 3000000000 | tf_op jit(solution)/shard_map/grad_gated_part/pallas_call | solution.py:190
  25.8 3.3 %forward_filter.1 = (bf16[128,2048]{1,0:T(8,128)(2,1)S(1)}, f32[128,2048]{1,0:T(8,128)S(1)}) custom-call(bf16[128,2048]{1,0:T(8,128)(2,1)S(1)} %copy-done.7, bf16[128,2048]{1,0:T(8,128)(2,1)S(1)} %copy-done.8, bf16[128,2048]{1,0:T(8,128)(2,1)S(1)} %copy-done.9, bf16[128,2048]{1,0:T(8,128)(2,1)S(1)} %copy-done.17, bf16[2048,128]{1,0:T(8,128)(2,1)S(1)} %copy-done.12, ...), custom_call_target="tpu_custom_call" | custom-call | flops 3000000000 | tf_op jit(solution)/shard_map/forward_filter/pallas_call | solution.py:107
  31.2 1.8 %collective-permute-start.4 = (bf16[176,2048]{1,0:T(8,128)(2,1)}, bf16[176,2048]{1,0:T(8,128)(2,1)S(1)}, u32[]{:S(2)}, u32[]{:S(2)}) collective-permute-start(bf16[176,2048]{1,0:T(8,128)(2,1)} %get-tuple-element.46), channel_id=1, source_target_pairs={{0,8},{8,16},{16,24},{24,28},{28,20},{20,12},{12,4},{4,0},{1,9},{9... | collective-permute-start | bytes 2162696 | tf_op jit(solution)/shard_map/ppermute | solution.py:490
  33.2 7.4 %grads_and_mixed.2 = (f32[2048,128]{1,0:T(8,128)S(1)}, f32[128,2048]{1,0:T(8,128)S(1)}) custom-call(s32[2]{0:T(128)S(1)} %pad_add_fusion.refs_0_, bf16[2048,8192]{1,0:T(8,128)(2,1)} %refs_1_.17, bf16[128,2048]{1,0:T(8,128)(2,1)S(1)} %get-tuple-element.44.refs_2_.refs_1_, bf16[128,2048]{1,0:T(8,128)(2,1)S(1)} %collective-permute-done.2.refs_4_.refs_3_, ...), custom_call_target="tpu_custom_call" | custom-call | flops 500000000 | tf_op jit(solution)/shard_map/grads_and_mixed/pallas_call | solution.py:190
  40.6 8.5 %grads_and_mixed.3 = (bf16[128,2048]{1,0:T(8,128)(2,1)}, bf16[128,2048]{1,0:T(8,128)(2,1)S(1)}, bf16[128,2048]{1,0:T(8,128)(2,1)}) custom-call(s32[2]{0:T(128)S(1)} %pad_add_fusion.refs_0_, bf16[2048,8192]{1,0:T(8,128)(2,1)} %refs_1_.17, bf16[128,2048]{1,0:T(8,128)(2,1)S(1)} %get-tuple-element.44.refs_2_.refs_1_, ...), custom_call_target="tpu_custom_call" | custom-call | flops 500000000 | tf_op jit(solution)/shard_map/grads_and_mixed/pallas_call | solution.py:190
  50.1 1.4 collective-permute-done.5.refs_7_.refs_5_
  51.5 1.6 %collective-permute-start.6 = (bf16[160,2048]{1,0:T(8,128)(2,1)S(1)}, bf16[160,2048]{1,0:T(8,128)(2,1)S(1)}, u32[]{:S(2)}, u32[]{:S(2)}) collective-permute-start(bf16[160,2048]{1,0:T(8,128)(2,1)S(1)} %slice.82), channel_id=1, source_target_pairs={{0,8},{8,16},{16,24},{24,28},{28,20},{20,12},{12,4},{4,0},{1,9},{9... | collective-permute-start | bytes 1966088 | tf_op jit(solution)/shard_map/ppermute | solution.py:490
  54.9 3.5 %tap_grad.1.refs_3_ = bf16[2048,128]{1,0:T(8,128)(2,1)S(1)} custom-call(bf16[128,2048]{1,0:T(8,128)(2,1)S(1)} %copy-done.8, bf16[128,2048]{1,0:T(8,128)(2,1)S(1)} %copy-done.10, bf16[128,2048]{1,0:T(8,128)(2,1)S(1)} %copy-done.18, bf16[128,2048]{1,0:T(8,128)(2,1)S(1)} %copy-done.15, bf16[2,256,256]{2,1,0:T(8,128)(2,1)S(1)} %copy-done.20, ...), custom_call_target="tpu_custom_call" | custom-call | flops 3000000000 | tf_op jit(solution)/shard_map/tap_grad/pallas_call | solution.py:107
  58.4 5.7 %mixed_part.2.refs_5_ = bf16[128,2048]{1,0:T(8,128)(2,1)S(1)} custom-call(s32[2]{0:T(128)S(1)} %pad_add_fusion.refs_0_, bf16[2048,8192]{1,0:T(8,128)(2,1)} %refs_1_.17, bf16[128,2048]{1,0:T(8,128)(2,1)S(1)} %get-tuple-element.44.refs_2_.refs_1_, bf16[2048,128]{1,0:T(8,128)(2,1)S(1)} %tap_grad.1.refs_3_), custom_call_target="tpu_custom_call" | custom-call | flops 500000000 | tf_op jit(solution)/shard_map/mixed_part/pallas_call | solution.py:190
  64.1 3.5 %collective-permute-start.15 = (bf16[16,2048]{1,0:T(8,128)(2,1)S(1)}, bf16[16,2048]{1,0:T(8,128)(2,1)S(1)}, u32[]{:S(2)}, u32[]{:S(2)}) collective-permute-start(bf16[16,2048]{1,0:T(8,128)(2,1)S(1)} %get-tuple-element.63), channel_id=1, source_target_pairs={{0,28},{8,20},{16,12},{24,4},{28,0},{20,8},{12,16},{4,24},{1,29},{... | collective-permute-start | bytes 196616 | tf_op jit(solution)/shard_map/ppermute | solution.py:519
  67.6 1.7 %collective-permute-start.14 = (bf16[1024,128]{1,0:T(8,128)(2,1)S(1)}, bf16[1024,128]{1,0:T(8,128)(2,1)S(1)}, u32[]{:S(2)}, u32[]{:S(2)}) collective-permute-start(bf16[1024,128]{1,0:T(8,128)(2,1)S(1)} %get-tuple-element.88), channel_id=1, source_target_pairs={{0,4},{4,0},{8,12},{12,8},{16,20},{20,16},{24,28},{28,24},{1,5},{5... | collective-permute-start | bytes 786440 | tf_op jit(solution)/shard_map/ppermute | solution.py:343
  69.3 2.8 %collective-permute-done.15 = bf16[16,2048]{1,0:T(8,128)(2,1)S(1)} collective-permute-done((bf16[16,2048]{1,0:T(8,128)(2,1)S(1)}, bf16[16,2048]{1,0:T(8,128)(2,1)S(1)}, u32[]{:S(2)}, u32[]{:S(2)}) %collective-permute-start.15) | collective-permute-done | bytes 65568 | tf_op jit(solution)/shard_map/ppermute | solution.py:519
  74.4 1.6 %collective-permute-start.16 = (bf16[64,2048]{1,0:T(8,128)(2,1)S(1)}, bf16[64,2048]{1,0:T(8,128)(2,1)S(1)}, u32[]{:S(2)}, u32[]{:S(2)}) collective-permute-start(bf16[64,2048]{1,0:T(8,128)(2,1)S(1)} %get-tuple-element.95.refs_10_), channel_id=1, source_target_pairs={{0,2},{1,3},{2,0},{3,1},{4,6},{5,7},{6,4},{7,5},{8,10},{9,11},{10,... | collective-permute-start | bytes 786440 | tf_op jit(solution)/shard_map/ppermute | solution.py:343
  76.0 1.7 %collective-permute-done.14.refs_2_ = bf16[1024,128]{1,0:T(8,128)(2,1)S(1)} collective-permute-done((bf16[1024,128]{1,0:T(8,128)(2,1)S(1)}, bf16[1024,128]{1,0:T(8,128)(2,1)S(1)}, u32[]{:S(2)}, u32[]{:S(2)}) %collective-permute-start.14) | collective-permute-done | bytes 262176 | tf_op jit(solution)/shard_map/ppermute | solution.py:343
  77.7 12.0 %collective-permute-done.8.refs_3_.refs_8_ = bf16[144,2048]{1,0:T(8,128)(2,1)S(1)} collective-permute-done((bf16[144,2048]{1,0:T(8,128)(2,1)S(1)}, bf16[144,2048]{1,0:T(8,128)(2,1)S(1)}, u32[]{:S(2)}, u32[]{:S(2)}) %collective-permute-start.8) | collective-permute-done | bytes 589856 | tf_op jit(solution)/shard_map/ppermute | solution.py:490
  91.1 1.6 %collective-permute-start.19 = (bf16[64,2048]{1,0:T(8,128)(2,1)S(1)}, bf16[64,2048]{1,0:T(8,128)(2,1)S(1)}, u32[]{:S(2)}, u32[]{:S(2)}) collective-permute-start(bf16[64,2048]{1,0:T(8,128)(2,1)S(1)} %pad_maximum_fusion.2.refs_11_), channel_id=1, source_target_pairs={{0,2},{1,3},{2,0},{3,1},{4,6},{5,7},{6,4},{7,5},{8,10},{9,11},{10,... | collective-permute-start | bytes 786440 | tf_op jit(solution)/shard_map/ppermute | solution.py:343
  93.5 2.7 %collective-permute-start.18 = (bf16[64,2048]{1,0:T(8,128)(2,1)S(1)}, bf16[64,2048]{1,0:T(8,128)(2,1)S(1)}, u32[]{:S(2)}, u32[]{:S(2)}) collective-permute-start(bf16[64,2048]{1,0:T(8,128)(2,1)S(1)} %slice.75), channel_id=1, source_target_pairs={{8,0},{16,8},{24,16},{28,24},{20,28},{12,20},{4,12},{0,4},{9,1},{1... | collective-permute-start | bytes 786440 | tf_op jit(solution)/shard_map/ppermute | solution.py:547
  96.3 5.8 %mixed_part.3 = f32[128,2048]{1,0:T(8,128)S(1)} custom-call(s32[2]{0:T(128)S(1)} %pad_add_fusion.refs_0_, bf16[2048,8192]{1,0:T(8,128)(2,1)} %refs_1_.17, bf16[128,2048]{1,0:T(8,128)(2,1)S(1)} %get-tuple-element.44.refs_2_.refs_1_, bf16[144,2048]{1,0:T(8,128)(2,1)S(1)} %collective-permute-done.8.refs_3_.refs_8_, ...), custom_call_target="tpu_custom_call" | custom-call | flops 500000000 | tf_op jit(solution)/shard_map/mixed_part/pallas_call | solution.py:190
  102.1 7.7 %collective-permute-done.18.refs_3_ = bf16[64,2048]{1,0:T(8,128)(2,1)S(1)} collective-permute-done((bf16[64,2048]{1,0:T(8,128)(2,1)S(1)}, bf16[64,2048]{1,0:T(8,128)(2,1)S(1)}, u32[]{:S(2)}, u32[]{:S(2)}) %collective-permute-start.18) | collective-permute-done | bytes 262176 | tf_op jit(solution)/shard_map/ppermute | solution.py:547
  111.1 1.5 %collective-permute-start.12 = (bf16[128,2048]{1,0:T(8,128)(2,1)S(1)}, bf16[128,2048]{1,0:T(8,128)(2,1)S(1)}, u32[]{:S(2)}, u32[]{:S(2)}) collective-permute-start(bf16[128,2048]{1,0:T(8,128)(2,1)S(1)} %convert_add_fusion), channel_id=1, source_target_pairs={{0,2},{1,3},{2,0},{3,1},{4,6},{5,7},{6,4},{7,5},{8,10},{9,11},{10,... | collective-permute-start | bytes 1572872 | tf_op jit(solution)/shard_map/ppermute | solution.py:343
  113.3 5.0 %grad_weight.2.refs_18_ = bf16[2048,1024]{1,0:T(8,128)(2,1)} custom-call(s32[2]{0:T(128)S(1)} %pad_add_fusion.refs_0_, bf16[128,2048]{1,0:T(8,128)(2,1)S(1)} %get-tuple-element.44.refs_2_.refs_1_, bf16[64,2048]{1,0:T(8,128)(2,1)S(1)} %collective-permute-done.17.refs_2_, bf16[64,2048]{1,0:T(8,128)(2,1)S(1)} %collective-permute-done.18.refs_3_, ...), custom_call_target="tpu_custom_call" | custom-call | flops 2000000000 | tf_op jit(solution)/shard_map/grad_weight/pallas_call | solution.py:293
  118.9 2.2 %collective-permute-start.22 = (bf16[512,128]{1,0:T(8,128)(2,1)S(1)}, bf16[512,128]{1,0:T(8,128)(2,1)S(1)}, u32[]{:S(2)}, u32[]{:S(2)}) collective-permute-start(bf16[512,128]{1,0:T(8,128)(2,1)S(1)} %added.4.refs_1_), channel_id=1, source_target_pairs={{0,16},{4,20},{8,24},{12,28},{16,0},{20,4},{24,8},{28,12},{1,17},{... | collective-permute-start | bytes 393224 | tf_op jit(solution)/shard_map/ppermute | solution.py:343
  121.1 5.0 %grad_weight.3 = bf16[2048,1024]{1,0:T(8,128)(2,1)} custom-call(s32[2]{0:T(128)S(1)} %pad_add_fusion.refs_0_, bf16[128,2048]{1,0:T(8,128)(2,1)S(1)} %get-tuple-element.44.refs_2_.refs_1_, bf16[64,2048]{1,0:T(8,128)(2,1)S(1)} %collective-permute-done.17.refs_2_, ...), custom_call_target="tpu_custom_call", output_to_operand_aliasing={{}: (18, {})} | custom-call | flops 2000000000 | tf_op jit(solution)/shard_map/grad_weight/pallas_call | solution.py:293
  126.1 2.1 %collective-permute-done.22.refs_2_ = bf16[512,128]{1,0:T(8,128)(2,1)S(1)} collective-permute-done((bf16[512,128]{1,0:T(8,128)(2,1)S(1)}, bf16[512,128]{1,0:T(8,128)(2,1)S(1)}, u32[]{:S(2)}, u32[]{:S(2)}) %collective-permute-start.22) | collective-permute-done | bytes 131104 | tf_op jit(solution)/shard_map/ppermute | solution.py:343
  128.9 4.0 %backward_filter.1 = (bf16[128,2048]{1,0:T(8,128)(2,1)}, bf16[128,2048]{1,0:T(8,128)(2,1)}) custom-call(bf16[128,2048]{1,0:T(8,128)(2,1)S(1)} %copy-done.8, bf16[128,2048]{1,0:T(8,128)(2,1)S(1)} %copy-done.10, bf16[128,2048]{1,0:T(8,128)(2,1)S(1)} %copy-done.15, bf16[128,2048]{1,0:T(8,128)(2,1)S(1)} %collective-permute-done.13.refs_3_, ...), custom_call_target="tpu_custom_call" | custom-call | flops 3000000000 | tf_op jit(solution)/shard_map/backward_filter/pallas_call | solution.py:107
  136.3 5.7 %collective-permute-done.24.refs_2_ = bf16[1024,128]{1,0:T(8,128)(2,1)S(1)} collective-permute-done((bf16[1024,128]{1,0:T(8,128)(2,1)S(1)}, bf16[1024,128]{1,0:T(8,128)(2,1)S(1)}, u32[]{:S(2)}, u32[]{:S(2)}) %collective-permute-start.24) | collective-permute-done | bytes 262176 | tf_op jit(solution)/shard_map/ppermute | solution.py:343
  142.0 1.6 %joined.3 = f32[2048,128]{1,0:T(8,128)} custom-call(s32[2]{0:T(128)S(1)} %pad_add_fusion.refs_0_, bf16[1024,128]{1,0:T(8,128)(2,1)S(1)} %joined.2.refs_1_, bf16[1024,128]{1,0:T(8,128)(2,1)S(1)} %collective-permute-done.24.refs_2_), custom_call_target="tpu_custom_call" | custom-call | flops 500000000 | tf_op jit(solution)/shard_map/joined/pallas_call | solution.py:422
  (114 shorter events, 17.9 us)
Async XLA Ops:
  2.8 14.9 %collective-permute-start.2 = (bf16[128,2048]{1,0:T(8,128)(2,1)S(1)}, bf16[128,2048]{1,0:T(8,128)(2,1)S(1)}, u32[]{:S(2)}, u32[]{:S(2)}) collective-permute-start(bf16[128,2048]{1,0:T(8,128)(2,1)S(1)} %copy-done.4), channel_id=1, source_target_pairs={{0,2},{1,3},{2,0},{3,1},{4,6},{5,7},{6,4},{7,5},{8,10},{9,11},{10,... | collective-permute-start | bytes 1572872 | tf_op jit(solution)/shard_map/ppermute | solution.py:343
  5.8 11.9 %collective-permute-start.1 = (bf16[128,2048]{1,0:T(8,128)(2,1)S(1)}, bf16[128,2048]{1,0:T(8,128)(2,1)S(1)}, u32[]{:S(2)}, u32[]{:S(2)}) collective-permute-start(bf16[128,2048]{1,0:T(8,128)(2,1)S(1)} %copy-done.4), channel_id=1, source_target_pairs={{0,1},{1,0},{2,3},{3,2},{4,5},{5,4},{6,7},{7,6},{8,9},{9,8},{10,11... | collective-permute-start | bytes 1572872 | tf_op jit(solution)/shard_map/ppermute | solution.py:343
  5.8 18.2 %collective-permute-start = (bf16[128,2048]{1,0:T(8,128)(2,1)}, bf16[128,2048]{1,0:T(8,128)(2,1)S(1)}, u32[]{:S(2)}, u32[]{:S(2)}) collective-permute-start(bf16[128,2048]{1,0:T(8,128)(2,1)} %multiply_convert_fusion), channel_id=1, source_target_pairs={{0,4},{4,8},{8,12},{12,16},{16,20},{20,24},{24,28},{1,5},{5,9},{9,... | collective-permute-start | bytes 1572872 | tf_op jit(solution)/shard_map/ppermute | solution.py:446
  15.5 9.2 %copy-start.7 = (bf16[128,2048]{1,0:T(8,128)(2,1)S(1)}, bf16[128,2048]{1,0:T(8,128)(2,1)}, u32[]{:S(2)}) copy-start(bf16[128,2048]{1,0:T(8,128)(2,1)} %refs_5_.4) | copy-start | bytes 1572868
  15.6 9.2 %copy-start.8 = (bf16[128,2048]{1,0:T(8,128)(2,1)S(1)}, bf16[128,2048]{1,0:T(8,128)(2,1)}, u32[]{:S(2)}) copy-start(bf16[128,2048]{1,0:T(8,128)(2,1)} %refs_0_.5) | copy-start | bytes 1572868
  15.6 9.2 %copy-start.9 = (bf16[128,2048]{1,0:T(8,128)(2,1)S(1)}, bf16[128,2048]{1,0:T(8,128)(2,1)}, u32[]{:S(2)}) copy-start(bf16[128,2048]{1,0:T(8,128)(2,1)} %refs_1_.18) | copy-start | bytes 1572868
  17.7 11.5 %collective-permute-start.3 = (bf16[128,2048]{1,0:T(8,128)(2,1)S(1)}, bf16[128,2048]{1,0:T(8,128)(2,1)S(1)}, u32[]{:S(2)}, u32[]{:S(2)}) collective-permute-start(bf16[128,2048]{1,0:T(8,128)(2,1)S(1)} %collective-permute-done.2.refs_4_.refs_3_), channel_id=1, source_target_pairs={{0,1},{1,0},{2,3},{3,2},{4,5},{5,4},{6,7},{7,6},{8,9},{9,8},{10,11... | collective-permute-start | bytes 1572872 | tf_op jit(solution)/shard_map/ppermute | solution.py:343
  31.2 18.8 %collective-permute-start.4 = (bf16[176,2048]{1,0:T(8,128)(2,1)}, bf16[176,2048]{1,0:T(8,128)(2,1)S(1)}, u32[]{:S(2)}, u32[]{:S(2)}) collective-permute-start(bf16[176,2048]{1,0:T(8,128)(2,1)} %get-tuple-element.46), channel_id=1, source_target_pairs={{0,8},{8,16},{16,24},{24,28},{28,20},{20,12},{12,4},{4,0},{1,9},{9... | collective-permute-start | bytes 2162696 | tf_op jit(solution)/shard_map/ppermute | solution.py:490
  33.0 18.5 %collective-permute-start.5 = (bf16[176,2048]{1,0:T(8,128)(2,1)}, bf16[176,2048]{1,0:T(8,128)(2,1)S(1)}, u32[]{:S(2)}, u32[]{:S(2)}) collective-permute-start(bf16[176,2048]{1,0:T(8,128)(2,1)} %get-tuple-element.47), channel_id=1, source_target_pairs={{8,0},{16,8},{24,16},{28,24},{20,28},{12,20},{4,12},{0,4},{9,1},{1... | collective-permute-start | bytes 2162696 | tf_op jit(solution)/shard_map/ppermute | solution.py:490
  49.9 3.7 %collective-permute-start.11 = (bf16[128,2048]{1,0:T(8,128)(2,1)}, bf16[128,2048]{1,0:T(8,128)(2,1)}, u32[]{:S(2)}, u32[]{:S(2)}) collective-permute-start(bf16[128,2048]{1,0:T(8,128)(2,1)} %get-tuple-element.56), channel_id=1, source_target_pairs={{0,1},{1,0},{2,3},{3,2},{4,5},{5,4},{6,7},{7,6},{8,9},{9,8},{10,11... | collective-permute-start | bytes 1572872 | tf_op jit(solution)/shard_map/ppermute | solution.py:343
  50.0 19.3 %copy-start = (bf16[176,2048]{1,0:T(8,128)(2,1)}, bf16[176,2048]{1,0:T(8,128)(2,1)S(1)}, u32[]{:S(2)}) copy-start(bf16[176,2048]{1,0:T(8,128)(2,1)S(1)} %collective-permute-done.4.refs_6_.refs_4_) | copy-start | bytes 2162692
  51.5 17.8 %copy-start.2 = (bf16[176,2048]{1,0:T(8,128)(2,1)}, bf16[176,2048]{1,0:T(8,128)(2,1)S(1)}, u32[]{:S(2)}) copy-start(bf16[176,2048]{1,0:T(8,128)(2,1)S(1)} %collective-permute-done.5.refs_7_.refs_5_) | copy-start | bytes 2162692
  51.5 20.6 %collective-permute-start.6 = (bf16[160,2048]{1,0:T(8,128)(2,1)S(1)}, bf16[160,2048]{1,0:T(8,128)(2,1)S(1)}, u32[]{:S(2)}, u32[]{:S(2)}) collective-permute-start(bf16[160,2048]{1,0:T(8,128)(2,1)S(1)} %slice.82), channel_id=1, source_target_pairs={{0,8},{8,16},{16,24},{24,28},{28,20},{20,12},{12,4},{4,0},{1,9},{9... | collective-permute-start | bytes 1966088 | tf_op jit(solution)/shard_map/ppermute | solution.py:490
  53.2 19.0 %collective-permute-start.7 = (bf16[160,2048]{1,0:T(8,128)(2,1)S(1)}, bf16[160,2048]{1,0:T(8,128)(2,1)S(1)}, u32[]{:S(2)}, u32[]{:S(2)}) collective-permute-start(bf16[160,2048]{1,0:T(8,128)(2,1)S(1)} %slice.83), channel_id=1, source_target_pairs={{8,0},{16,8},{24,16},{28,24},{20,28},{12,20},{4,12},{0,4},{9,1},{1... | collective-permute-start | bytes 1966088 | tf_op jit(solution)/shard_map/ppermute | solution.py:490
  64.1 8.0 %collective-permute-start.15 = (bf16[16,2048]{1,0:T(8,128)(2,1)S(1)}, bf16[16,2048]{1,0:T(8,128)(2,1)S(1)}, u32[]{:S(2)}, u32[]{:S(2)}) collective-permute-start(bf16[16,2048]{1,0:T(8,128)(2,1)S(1)} %get-tuple-element.63), channel_id=1, source_target_pairs={{0,28},{8,20},{16,12},{24,4},{28,0},{20,8},{12,16},{4,24},{1,29},{... | collective-permute-start | bytes 196616 | tf_op jit(solution)/shard_map/ppermute | solution.py:519
  67.6 10.1 %collective-permute-start.14 = (bf16[1024,128]{1,0:T(8,128)(2,1)S(1)}, bf16[1024,128]{1,0:T(8,128)(2,1)S(1)}, u32[]{:S(2)}, u32[]{:S(2)}) collective-permute-start(bf16[1024,128]{1,0:T(8,128)(2,1)S(1)} %get-tuple-element.88), channel_id=1, source_target_pairs={{0,4},{4,0},{8,12},{12,8},{16,20},{20,16},{24,28},{28,24},{1,5},{5... | collective-permute-start | bytes 786440 | tf_op jit(solution)/shard_map/ppermute | solution.py:343
  72.3 17.5 %collective-permute-start.8 = (bf16[144,2048]{1,0:T(8,128)(2,1)S(1)}, bf16[144,2048]{1,0:T(8,128)(2,1)S(1)}, u32[]{:S(2)}, u32[]{:S(2)}) collective-permute-start(bf16[144,2048]{1,0:T(8,128)(2,1)S(1)} %slice.84), channel_id=1, source_target_pairs={{0,8},{8,16},{16,24},{24,28},{28,20},{20,12},{12,4},{4,0},{1,9},{9... | collective-permute-start | bytes 1769480 | tf_op jit(solution)/shard_map/ppermute | solution.py:490
  73.2 16.5 %collective-permute-start.9 = (bf16[144,2048]{1,0:T(8,128)(2,1)S(1)}, bf16[144,2048]{1,0:T(8,128)(2,1)S(1)}, u32[]{:S(2)}, u32[]{:S(2)}) collective-permute-start(bf16[144,2048]{1,0:T(8,128)(2,1)S(1)} %slice.85), channel_id=1, source_target_pairs={{8,0},{16,8},{24,16},{28,24},{20,28},{12,20},{4,12},{0,4},{9,1},{1... | collective-permute-start | bytes 1769480 | tf_op jit(solution)/shard_map/ppermute | solution.py:490
  74.4 19.0 %collective-permute-start.16 = (bf16[64,2048]{1,0:T(8,128)(2,1)S(1)}, bf16[64,2048]{1,0:T(8,128)(2,1)S(1)}, u32[]{:S(2)}, u32[]{:S(2)}) collective-permute-start(bf16[64,2048]{1,0:T(8,128)(2,1)S(1)} %get-tuple-element.95.refs_10_), channel_id=1, source_target_pairs={{0,2},{1,3},{2,0},{3,1},{4,6},{5,7},{6,4},{7,5},{8,10},{9,11},{10,... | collective-permute-start | bytes 786440 | tf_op jit(solution)/shard_map/ppermute | solution.py:343
  89.8 20.8 %collective-permute-start.13 = (bf16[128,2048]{1,0:T(8,128)(2,1)S(1)}, bf16[128,2048]{1,0:T(8,128)(2,1)S(1)}, u32[]{:S(2)}, u32[]{:S(2)}) collective-permute-start(bf16[128,2048]{1,0:T(8,128)(2,1)S(1)} %copy-done.15), channel_id=1, source_target_pairs={{4,0},{8,4},{12,8},{16,12},{20,16},{24,20},{28,24},{5,1},{9,5},{13... | collective-permute-start | bytes 1572872 | tf_op jit(solution)/shard_map/ppermute | solution.py:528
  91.1 11.0 %collective-permute-start.19 = (bf16[64,2048]{1,0:T(8,128)(2,1)S(1)}, bf16[64,2048]{1,0:T(8,128)(2,1)S(1)}, u32[]{:S(2)}, u32[]{:S(2)}) collective-permute-start(bf16[64,2048]{1,0:T(8,128)(2,1)S(1)} %pad_maximum_fusion.2.refs_11_), channel_id=1, source_target_pairs={{0,2},{1,3},{2,0},{3,1},{4,6},{5,7},{6,4},{7,5},{8,10},{9,11},{10,... | collective-permute-start | bytes 786440 | tf_op jit(solution)/shard_map/ppermute | solution.py:343
  93.5 16.3 %collective-permute-start.18 = (bf16[64,2048]{1,0:T(8,128)(2,1)S(1)}, bf16[64,2048]{1,0:T(8,128)(2,1)S(1)}, u32[]{:S(2)}, u32[]{:S(2)}) collective-permute-start(bf16[64,2048]{1,0:T(8,128)(2,1)S(1)} %slice.75), channel_id=1, source_target_pairs={{8,0},{16,8},{24,16},{28,24},{20,28},{12,20},{4,12},{0,4},{9,1},{1... | collective-permute-start | bytes 786440 | tf_op jit(solution)/shard_map/ppermute | solution.py:547
  96.2 14.4 %collective-permute-start.17 = (bf16[64,2048]{1,0:T(8,128)(2,1)S(1)}, bf16[64,2048]{1,0:T(8,128)(2,1)S(1)}, u32[]{:S(2)}, u32[]{:S(2)}) collective-permute-start(bf16[64,2048]{1,0:T(8,128)(2,1)S(1)} %slice.74), channel_id=1, source_target_pairs={{0,8},{8,16},{16,24},{24,28},{28,20},{20,12},{12,4},{4,0},{1,9},{9... | collective-permute-start | bytes 786440 | tf_op jit(solution)/shard_map/ppermute | solution.py:547
  96.3 17.0 %copy-start.1 = (bf16[176,2048]{1,0:T(8,128)(2,1)S(1)}, bf16[176,2048]{1,0:T(8,128)(2,1)}, u32[]{:S(2)}) copy-start(bf16[176,2048]{1,0:T(8,128)(2,1)} %copy-done) | copy-start | bytes 2162692
  96.3 17.0 %copy-start.3 = (bf16[176,2048]{1,0:T(8,128)(2,1)S(1)}, bf16[176,2048]{1,0:T(8,128)(2,1)}, u32[]{:S(2)}) copy-start(bf16[176,2048]{1,0:T(8,128)(2,1)} %copy-done.2) | copy-start | bytes 2162692
  110.6 2.7 %collective-permute-start.20 = (bf16[256,2048]{1,0:T(8,128)(2,1)S(1)}, bf16[256,2048]{1,0:T(8,128)(2,1)S(1)}, u32[]{:S(2)}, u32[]{:S(2)}) collective-permute-start(bf16[256,2048]{1,0:T(8,128)(2,1)S(1)} %constant_dynamic-update-slice_fusion.4), channel_id=1, source_target_pairs={{0,1},{1,0},{2,3},{3,2},{4,5},{5,4},{6,7},{7,6},{8,9},{9,8},{10,11... | collective-permute-start | bytes 3145736 | tf_op jit(solution)/shard_map/ppermute | solution.py:343
  110.6 24.7 %collective-permute-start.10 = (bf16[128,2048]{1,0:T(8,128)(2,1)S(1)}, bf16[128,2048]{1,0:T(8,128)(2,1)S(1)}, u32[]{:S(2)}, u32[]{:S(2)}) collective-permute-start(bf16[128,2048]{1,0:T(8,128)(2,1)S(1)} %mixed_part.2.refs_5_), channel_id=1, source_target_pairs={{0,1},{1,0},{2,3},{3,2},{4,5},{5,4},{6,7},{7,6},{8,9},{9,8},{10,11... | collective-permute-start | bytes 1572872 | tf_op jit(solution)/shard_map/ppermute | solution.py:343
  111.1 24.2 %collective-permute-start.12 = (bf16[128,2048]{1,0:T(8,128)(2,1)S(1)}, bf16[128,2048]{1,0:T(8,128)(2,1)S(1)}, u32[]{:S(2)}, u32[]{:S(2)}) collective-permute-start(bf16[128,2048]{1,0:T(8,128)(2,1)S(1)} %convert_add_fusion), channel_id=1, source_target_pairs={{0,2},{1,3},{2,0},{3,1},{4,6},{5,7},{6,4},{7,5},{8,10},{9,11},{10,... | collective-permute-start | bytes 1572872 | tf_op jit(solution)/shard_map/ppermute | solution.py:343
  112.6 5.7 %collective-permute-start.21 = (bf16[512,128]{1,0:T(8,128)(2,1)S(1)}, bf16[512,128]{1,0:T(8,128)(2,1)S(1)}, u32[]{:S(2)}, u32[]{:S(2)}) collective-permute-start(bf16[512,128]{1,0:T(8,128)(2,1)S(1)} %get-tuple-element.74), channel_id=1, source_target_pairs={{0,8},{4,12},{8,0},{12,4},{16,24},{20,28},{24,16},{28,20},{1,9},{5... | collective-permute-start | bytes 393224 | tf_op jit(solution)/shard_map/ppermute | solution.py:343
  118.9 9.3 %collective-permute-start.22 = (bf16[512,128]{1,0:T(8,128)(2,1)S(1)}, bf16[512,128]{1,0:T(8,128)(2,1)S(1)}, u32[]{:S(2)}, u32[]{:S(2)}) collective-permute-start(bf16[512,128]{1,0:T(8,128)(2,1)S(1)} %added.4.refs_1_), channel_id=1, source_target_pairs={{0,16},{4,20},{8,24},{12,28},{16,0},{20,4},{24,8},{28,12},{1,17},{... | collective-permute-start | bytes 393224 | tf_op jit(solution)/shard_map/ppermute | solution.py:343
  128.8 5.3 %collective-permute-start.23 = (bf16[512,128]{1,0:T(8,128)(2,1)S(1)}, bf16[512,128]{1,0:T(8,128)(2,1)S(1)}, u32[]{:S(2)}, u32[]{:S(2)}) collective-permute-start(bf16[512,128]{1,0:T(8,128)(2,1)S(1)} %added.5.refs_1_), channel_id=1, source_target_pairs={{0,8},{4,12},{8,0},{12,4},{16,24},{20,28},{24,16},{28,20},{1,9},{5... | collective-permute-start | bytes 393224 | tf_op jit(solution)/shard_map/ppermute | solution.py:343
  134.7 7.3 %collective-permute-start.24 = (bf16[1024,128]{1,0:T(8,128)(2,1)S(1)}, bf16[1024,128]{1,0:T(8,128)(2,1)S(1)}, u32[]{:S(2)}, u32[]{:S(2)}) collective-permute-start(bf16[1024,128]{1,0:T(8,128)(2,1)S(1)} %joined.2.refs_1_), channel_id=1, source_target_pairs={{0,4},{4,0},{8,12},{12,8},{16,20},{20,16},{24,28},{28,24},{1,5},{5... | collective-permute-start | bytes 786440 | tf_op jit(solution)/shard_map/ppermute | solution.py:343
  (19 other events, 86.4 us)

commit v20 on v16

--- a/solution.py
+++ b/solution.py
@@ -548,9 +548,6 @@
 
     cols.append(gather_of_chips(jnp.concatenate(brought[early:], axis=0)))
 
-    given = held_until([grad_filtered], far)[0]
-    following = lax.ppermute(given, "ctx", [(i + 1, i) for i in range(n_ctx - 1)])
-
     evens = [off for off in range(n_chan) if off % 2 == 0]
     wide = piece % 128 == 0 and 2 * early == n_ctx
     columns = {off: [(part[off], 0) for part in cols] for off in evens}
@@ -568,7 +565,8 @@
         pairs = [[array for array, unused in columns[off]] for off in range(n_chan)]
         low_half = grad_weight = narrow_grad_weight(me, arrays, places, pairs)
 
-    tap_sum.add((), [low_half])
+    given = held_until([grad_filtered], tap_sum.add((), [low_half]))[0]
+    following = lax.ppermute(given, "ctx", [(i + 1, i) for i in range(n_ctx - 1)])
     while tap_sum.add((), [grad_weight]):
         pass
     own, bits = tap_sum.sums, tap_sum.bits

time: 144 us -> 146 us (1.014)
  waiting for transfers between devices: 37.2 us -> 39.3 us
    ppermute x14, waiting for transfers between devices: 21 us -> 23 us  [swap(): return lax.ppermute(block, axis, [(i, i ^ bit) for i in range(size)])]
  transfers between devices with their start and end apart: 25 -> 25, of which waited for: 9 -> 9; matrix products, arithmetic and copies ran while one was open for 2% -> 2% of each run, Pallas kernels for 44% -> 43%
where the time goes in v20:
time: 146 us; the launch traced here: 145 us
  Pallas kernels  65.3 us (45%)
  waiting for transfers between devices  39.3 us (27%)
  starting transfers between devices  29.8 us (20%)
  other arithmetic  5.75 us (4%)
  local copies, waits for them, and re-layouts  3.63 us (2%)
    pallas_call x6, Pallas kernels, weight_pass(): pl.pallas_call(ignoring(body, len(after), 1 + len(arrays)), grid_spec=plt...  39.9 us
    ppermute x14, waiting for transfers between devices, swap(): return lax.ppermute(block, axis, [(i, i ^ bit) for i in range(size)])  23 us
    ppermute x6, waiting for transfers between devices, passed_on(): came = [lax.ppermute(onto, 'ctx', ahead), lax.ppermute(back, 'ctx', behind)]  13.4 us
    ppermute x14, starting transfers between devices, swap(): return lax.ppermute(block, axis, [(i, i ^ bit) for i in range(size)])  13.3 us
    pallas_call x3, Pallas kernels, by_channel(): pl.pallas_call(ignoring(functools.partial(kernel, length), len(after), le...  10.8 us
    pallas_call x2, Pallas kernels, grad_weight_of(): pl.pallas_call(ignoring(functools.partial(weight_kernel, places, parts),...  10 us
    ppermute x6, starting transfers between devices, passed_on(): came = [lax.ppermute(onto, 'ctx', ahead), lax.ppermute(back, 'ctx', behind)]  6.18 us
    ppermute x1, starting transfers between devices, per_device(): lax.ppermute(held_until([pieces[rows:2 * rows]], [mixed_one])[0], 'ctx',...  3.5 us
  transfers between devices with their start and end apart: 25, of which 9 were waited for; matrix products, arithmetic and copies ran while one was open for 2% of the time, Pallas kernels for 43%

profile of v20, /device:TPU:0, one launch (start us, length us, event | category | flops | bytes accessed | tf_op | source)
XLA Modules:
  0.0 145.1 jit_solution(17581033562138396472)
XLA Ops:
  0.6 2.2 %multiply_convert_fusion = bf16[128,2048]{1,0:T(8,128)(2,1)} fusion(bf16[128,2048]{1,0:T(8,128)(2,1)} %refs_1_.18, bf16[128,2048]{1,0:T(8,128)(2,1)} %refs_0_.5), kind=kLoop, calls=%fused_computation.2 | loop fusion | flops 1048576 | bytes 1572864 | tf_op jit(solution)/shard_map/convert_element_type | solution.py:444
  2.8 2.9 %collective-permute-start.2 = (bf16[128,2048]{1,0:T(8,128)(2,1)S(1)}, bf16[128,2048]{1,0:T(8,128)(2,1)S(1)}, u32[]{:S(2)}, u32[]{:S(2)}) collective-permute-start(bf16[128,2048]{1,0:T(8,128)(2,1)S(1)} %copy-done.8), channel_id=1, source_target_pairs={{0,2},{1,3},{2,0},{3,1},{4,6},{5,7},{6,4},{7,5},{8,10},{9,11},{10,... | collective-permute-start | bytes 1572872 | tf_op jit(solution)/shard_map/ppermute | solution.py:343
  5.8 3.4 %collective-permute-start = (bf16[128,2048]{1,0:T(8,128)(2,1)}, bf16[128,2048]{1,0:T(8,128)(2,1)S(1)}, u32[]{:S(2)}, u32[]{:S(2)}) collective-permute-start(bf16[128,2048]{1,0:T(8,128)(2,1)} %multiply_convert_fusion), channel_id=1, source_target_pairs={{0,4},{4,8},{8,12},{12,16},{16,20},{20,24},{24,28},{1,5},{5,9},{9,... | collective-permute-start | bytes 1572872 | tf_op jit(solution)/shard_map/ppermute | solution.py:446
  9.3 6.2 %grad_gated_part.2.refs_3_ = f32[2048,128]{1,0:T(8,128)S(1)} custom-call(s32[2]{0:T(128)S(1)} %pad_add_fusion.refs_0_, bf16[2048,8192]{1,0:T(8,128)(2,1)} %refs_1_.17, bf16[128,2048]{1,0:T(8,128)(2,1)S(1)} %copy-done.8), custom_call_target="tpu_custom_call" | custom-call | flops 3000000000 | tf_op jit(solution)/shard_map/grad_gated_part/pallas_call | solution.py:190
  15.6 2.1 %collective-permute-done.2.refs_4_.refs_3_ = bf16[128,2048]{1,0:T(8,128)(2,1)S(1)} collective-permute-done((bf16[128,2048]{1,0:T(8,128)(2,1)S(1)}, bf16[128,2048]{1,0:T(8,128)(2,1)S(1)}, u32[]{:S(2)}, u32[]{:S(2)}) %collective-permute-start.2) | collective-permute-done | bytes 524320 | tf_op jit(solution)/shard_map/ppermute | solution.py:343
  17.7 6.2 %grad_gated_part.3.refs_7_.refs_6_.refs_4_ = f32[2048,128]{1,0:T(8,128)S(1)} custom-call(s32[2]{0:T(128)S(1)} %pad_add_fusion.refs_0_, bf16[2048,8192]{1,0:T(8,128)(2,1)} %refs_1_.17, bf16[128,2048]{1,0:T(8,128)(2,1)S(1)} %collective-permute-done.1.refs_2_.refs_3_, f32[2048,128]{1,0:T(8,128)S(1)} %grad_gated_part.2.refs_3_), custom_call_target="tpu_custom_call" | custom-call | flops 3000000000 | tf_op jit(solution)/shard_map/grad_gated_part/pallas_call | solution.py:190
  25.8 3.3 %forward_filter.1 = (bf16[128,2048]{1,0:T(8,128)(2,1)S(1)}, f32[128,2048]{1,0:T(8,128)S(1)}) custom-call(bf16[128,2048]{1,0:T(8,128)(2,1)S(1)} %copy-done.11, bf16[128,2048]{1,0:T(8,128)(2,1)S(1)} %copy-done.12, bf16[128,2048]{1,0:T(8,128)(2,1)S(1)} %copy-done.13, bf16[128,2048]{1,0:T(8,128)(2,1)S(1)} %copy-done.21, bf16[2048,128]{1,0:T(8,128)(2,1)S(1)} %copy-done.16, ...), custom_call_target="tpu_custom_call" | custom-call | flops 3000000000 | tf_op jit(solution)/shard_map/forward_filter/pallas_call | solution.py:107
  31.2 1.8 %collective-permute-start.4 = (bf16[176,2048]{1,0:T(8,128)(2,1)}, bf16[176,2048]{1,0:T(8,128)(2,1)S(1)}, u32[]{:S(2)}, u32[]{:S(2)}) collective-permute-start(bf16[176,2048]{1,0:T(8,128)(2,1)} %get-tuple-element.46), channel_id=1, source_target_pairs={{0,8},{8,16},{16,24},{24,28},{28,20},{20,12},{12,4},{4,0},{1,9},{9... | collective-permute-start | bytes 2162696 | tf_op jit(solution)/shard_map/ppermute | solution.py:490
  33.2 7.4 %grads_and_mixed.2 = (f32[2048,128]{1,0:T(8,128)S(1)}, f32[128,2048]{1,0:T(8,128)S(1)}) custom-call(s32[2]{0:T(128)S(1)} %pad_add_fusion.refs_0_, bf16[2048,8192]{1,0:T(8,128)(2,1)} %refs_1_.17, bf16[128,2048]{1,0:T(8,128)(2,1)S(1)} %get-tuple-element.44.refs_2_.refs_1_, bf16[128,2048]{1,0:T(8,128)(2,1)S(1)} %collective-permute-done.2.refs_4_.refs_3_, ...), custom_call_target="tpu_custom_call" | custom-call | flops 500000000 | tf_op jit(solution)/shard_map/grads_and_mixed/pallas_call | solution.py:190
  40.6 8.5 %grads_and_mixed.3 = (bf16[128,2048]{1,0:T(8,128)(2,1)}, bf16[128,2048]{1,0:T(8,128)(2,1)S(1)}, bf16[128,2048]{1,0:T(8,128)(2,1)}) custom-call(s32[2]{0:T(128)S(1)} %pad_add_fusion.refs_0_, bf16[2048,8192]{1,0:T(8,128)(2,1)} %refs_1_.17, bf16[128,2048]{1,0:T(8,128)(2,1)S(1)} %get-tuple-element.44.refs_2_.refs_1_, ...), custom_call_target="tpu_custom_call" | custom-call | flops 500000000 | tf_op jit(solution)/shard_map/grads_and_mixed/pallas_call | solution.py:190
  50.1 1.4 collective-permute-done.5.refs_7_.refs_5_
  51.6 1.6 %collective-permute-start.6 = (bf16[160,2048]{1,0:T(8,128)(2,1)S(1)}, bf16[160,2048]{1,0:T(8,128)(2,1)S(1)}, u32[]{:S(2)}, u32[]{:S(2)}) collective-permute-start(bf16[160,2048]{1,0:T(8,128)(2,1)S(1)} %slice.82), channel_id=1, source_target_pairs={{0,8},{8,16},{16,24},{24,28},{28,20},{20,12},{12,4},{4,0},{1,9},{9... | collective-permute-start | bytes 1966088 | tf_op jit(solution)/shard_map/ppermute | solution.py:490
  54.9 3.5 %tap_grad.1.refs_3_ = bf16[2048,128]{1,0:T(8,128)(2,1)S(1)} custom-call(bf16[128,2048]{1,0:T(8,128)(2,1)S(1)} %copy-done.12, bf16[128,2048]{1,0:T(8,128)(2,1)S(1)} %copy-done.14, bf16[128,2048]{1,0:T(8,128)(2,1)S(1)} %copy-done.22, bf16[128,2048]{1,0:T(8,128)(2,1)S(1)} %copy-done.19, bf16[2,256,256]{2,1,0:T(8,128)(2,1)S(1)} %copy-done.24, ...), custom_call_target="tpu_custom_call" | custom-call | flops 3000000000 | tf_op jit(solution)/shard_map/tap_grad/pallas_call | solution.py:107
  58.4 5.7 %mixed_part.2.refs_5_ = bf16[128,2048]{1,0:T(8,128)(2,1)S(1)} custom-call(s32[2]{0:T(128)S(1)} %pad_add_fusion.refs_0_, bf16[2048,8192]{1,0:T(8,128)(2,1)} %refs_1_.17, bf16[128,2048]{1,0:T(8,128)(2,1)S(1)} %get-tuple-element.44.refs_2_.refs_1_, bf16[2048,128]{1,0:T(8,128)(2,1)S(1)} %tap_grad.1.refs_3_), custom_call_target="tpu_custom_call" | custom-call | flops 500000000 | tf_op jit(solution)/shard_map/mixed_part/pallas_call | solution.py:190
  64.1 3.5 %collective-permute-start.15 = (bf16[16,2048]{1,0:T(8,128)(2,1)S(1)}, bf16[16,2048]{1,0:T(8,128)(2,1)S(1)}, u32[]{:S(2)}, u32[]{:S(2)}) collective-permute-start(bf16[16,2048]{1,0:T(8,128)(2,1)S(1)} %get-tuple-element.63), channel_id=1, source_target_pairs={{0,28},{8,20},{16,12},{24,4},{28,0},{20,8},{12,16},{4,24},{1,29},{... | collective-permute-start | bytes 196616 | tf_op jit(solution)/shard_map/ppermute | solution.py:519
  67.7 1.6 %collective-permute-start.13 = (bf16[1024,128]{1,0:T(8,128)(2,1)S(1)}, bf16[1024,128]{1,0:T(8,128)(2,1)S(1)}, u32[]{:S(2)}, u32[]{:S(2)}) collective-permute-start(bf16[1024,128]{1,0:T(8,128)(2,1)S(1)} %get-tuple-element.88), channel_id=1, source_target_pairs={{0,4},{4,0},{8,12},{12,8},{16,20},{20,16},{24,28},{28,24},{1,5},{5... | collective-permute-start | bytes 786440 | tf_op jit(solution)/shard_map/ppermute | solution.py:343
  69.3 2.9 %collective-permute-done.15 = bf16[16,2048]{1,0:T(8,128)(2,1)S(1)} collective-permute-done((bf16[16,2048]{1,0:T(8,128)(2,1)S(1)}, bf16[16,2048]{1,0:T(8,128)(2,1)S(1)}, u32[]{:S(2)}, u32[]{:S(2)}) %collective-permute-start.15) | collective-permute-done | bytes 65568 | tf_op jit(solution)/shard_map/ppermute | solution.py:519
  74.5 1.5 %collective-permute-start.16 = (bf16[64,2048]{1,0:T(8,128)(2,1)S(1)}, bf16[64,2048]{1,0:T(8,128)(2,1)S(1)}, u32[]{:S(2)}, u32[]{:S(2)}) collective-permute-start(bf16[64,2048]{1,0:T(8,128)(2,1)S(1)} %get-tuple-element.95.refs_10_), channel_id=1, source_target_pairs={{0,2},{1,3},{2,0},{3,1},{4,6},{5,7},{6,4},{7,5},{8,10},{9,11},{10,... | collective-permute-start | bytes 786440 | tf_op jit(solution)/shard_map/ppermute | solution.py:343
  76.0 1.7 %collective-permute-done.13.refs_2_ = bf16[1024,128]{1,0:T(8,128)(2,1)S(1)} collective-permute-done((bf16[1024,128]{1,0:T(8,128)(2,1)S(1)}, bf16[1024,128]{1,0:T(8,128)(2,1)S(1)}, u32[]{:S(2)}, u32[]{:S(2)}) %collective-permute-start.13) | collective-permute-done | bytes 262176 | tf_op jit(solution)/shard_map/ppermute | solution.py:343
  77.8 12.0 %collective-permute-done.8.refs_3_.refs_8_ = bf16[144,2048]{1,0:T(8,128)(2,1)S(1)} collective-permute-done((bf16[144,2048]{1,0:T(8,128)(2,1)S(1)}, bf16[144,2048]{1,0:T(8,128)(2,1)S(1)}, u32[]{:S(2)}, u32[]{:S(2)}) %collective-permute-start.8) | collective-permute-done | bytes 589856 | tf_op jit(solution)/shard_map/ppermute | solution.py:490
  89.9 1.5 %collective-permute-start.19 = (bf16[64,2048]{1,0:T(8,128)(2,1)S(1)}, bf16[64,2048]{1,0:T(8,128)(2,1)S(1)}, u32[]{:S(2)}, u32[]{:S(2)}) collective-permute-start(bf16[64,2048]{1,0:T(8,128)(2,1)S(1)} %pad_maximum_fusion.2.refs_11_), channel_id=1, source_target_pairs={{0,2},{1,3},{2,0},{3,1},{4,6},{5,7},{6,4},{7,5},{8,10},{9,11},{10,... | collective-permute-start | bytes 786440 | tf_op jit(solution)/shard_map/ppermute | solution.py:343
  93.1 1.6 %collective-permute-start.17 = (bf16[64,2048]{1,0:T(8,128)(2,1)S(1)}, bf16[64,2048]{1,0:T(8,128)(2,1)S(1)}, u32[]{:S(2)}, u32[]{:S(2)}) collective-permute-start(bf16[64,2048]{1,0:T(8,128)(2,1)S(1)} %slice.74), channel_id=1, source_target_pairs={{0,8},{8,16},{16,24},{24,28},{28,20},{20,12},{12,4},{4,0},{1,9},{9... | collective-permute-start | bytes 786440 | tf_op jit(solution)/shard_map/ppermute | solution.py:545
  94.8 5.7 %mixed_part.3 = f32[128,2048]{1,0:T(8,128)S(1)} custom-call(s32[2]{0:T(128)S(1)} %pad_add_fusion.refs_0_, bf16[2048,8192]{1,0:T(8,128)(2,1)} %refs_1_.17, bf16[128,2048]{1,0:T(8,128)(2,1)S(1)} %get-tuple-element.44.refs_2_.refs_1_, bf16[144,2048]{1,0:T(8,128)(2,1)S(1)} %copy-done.1, bf16[144,2048]{1,0:T(8,128)(2,1)S(1)} %copy-done.3, ...), custom_call_target="tpu_custom_call" | custom-call | flops 500000000 | tf_op jit(solution)/shard_map/mixed_part/pallas_call | solution.py:190
  101.9 1.4 collective-permute-done.20.refs_12_.refs_13_.refs_16_.refs_17_
  103.3 5.0 %grad_weight.2.refs_18_ = bf16[2048,1024]{1,0:T(8,128)(2,1)} custom-call(s32[2]{0:T(128)S(1)} %pad_add_fusion.refs_0_, bf16[128,2048]{1,0:T(8,128)(2,1)S(1)} %get-tuple-element.44.refs_2_.refs_1_, bf16[64,2048]{1,0:T(8,128)(2,1)S(1)} %collective-permute-done.17.refs_2_, bf16[64,2048]{1,0:T(8,128)(2,1)S(1)} %collective-permute-done.18.refs_3_, ...), custom_call_target="tpu_custom_call" | custom-call | flops 2000000000 | tf_op jit(solution)/shard_map/grad_weight/pallas_call | solution.py:293
  108.9 1.3 collective-permute-start.21
  111.3 3.1 %collective-permute-start.22 = (bf16[512,128]{1,0:T(8,128)(2,1)S(1)}, bf16[512,128]{1,0:T(8,128)(2,1)S(1)}, u32[]{:S(2)}, u32[]{:S(2)}) collective-permute-start(bf16[512,128]{1,0:T(8,128)(2,1)S(1)} %added.4.refs_1_), channel_id=1, source_target_pairs={{0,16},{4,20},{8,24},{12,28},{16,0},{20,4},{24,8},{28,12},{1,17},{... | collective-permute-start | bytes 393224 | tf_op jit(solution)/shard_map/ppermute | solution.py:343
  114.4 5.0 %grad_weight.3 = bf16[2048,1024]{1,0:T(8,128)(2,1)} custom-call(s32[2]{0:T(128)S(1)} %pad_add_fusion.refs_0_, bf16[128,2048]{1,0:T(8,128)(2,1)S(1)} %get-tuple-element.44.refs_2_.refs_1_, bf16[64,2048]{1,0:T(8,128)(2,1)S(1)} %collective-permute-done.17.refs_2_, ...), custom_call_target="tpu_custom_call", output_to_operand_aliasing={{}: (18, {})} | custom-call | flops 2000000000 | tf_op jit(solution)/shard_map/grad_weight/pallas_call | solution.py:293
  119.4 11.2 %collective-permute-done.22.refs_2_ = bf16[512,128]{1,0:T(8,128)(2,1)S(1)} collective-permute-done((bf16[512,128]{1,0:T(8,128)(2,1)S(1)}, bf16[512,128]{1,0:T(8,128)(2,1)S(1)}, u32[]{:S(2)}, u32[]{:S(2)}) %collective-permute-start.22) | collective-permute-done | bytes 131104 | tf_op jit(solution)/shard_map/ppermute | solution.py:343
  131.3 4.0 %backward_filter.1 = (bf16[128,2048]{1,0:T(8,128)(2,1)}, bf16[128,2048]{1,0:T(8,128)(2,1)}) custom-call(bf16[128,2048]{1,0:T(8,128)(2,1)S(1)} %copy-done.12, bf16[128,2048]{1,0:T(8,128)(2,1)S(1)} %copy-done.14, bf16[128,2048]{1,0:T(8,128)(2,1)S(1)} %copy-done.19, bf16[128,2048]{1,0:T(8,128)(2,1)S(1)} %collective-permute-done.21.refs_3_, ...), custom_call_target="tpu_custom_call" | custom-call | flops 3000000000 | tf_op jit(solution)/shard_map/backward_filter/pallas_call | solution.py:107
  137.9 5.5 %collective-permute-done.24.refs_2_ = bf16[1024,128]{1,0:T(8,128)(2,1)S(1)} collective-permute-done((bf16[1024,128]{1,0:T(8,128)(2,1)S(1)}, bf16[1024,128]{1,0:T(8,128)(2,1)S(1)}, u32[]{:S(2)}, u32[]{:S(2)}) %collective-permute-start.24) | collective-permute-done | bytes 262176 | tf_op jit(solution)/shard_map/ppermute | solution.py:343
  143.4 1.6 %joined.3 = f32[2048,128]{1,0:T(8,128)} custom-call(s32[2]{0:T(128)S(1)} %pad_add_fusion.refs_0_, bf16[1024,128]{1,0:T(8,128)(2,1)S(1)} %joined.2.refs_1_, bf16[1024,128]{1,0:T(8,128)(2,1)S(1)} %collective-permute-done.24.refs_2_), custom_call_target="tpu_custom_call" | custom-call | flops 500000000 | tf_op jit(solution)/shard_map/joined/pallas_call | solution.py:422
  (124 shorter events, 17.1 us)
Async XLA Ops:
  2.8 14.9 %collective-permute-start.2 = (bf16[128,2048]{1,0:T(8,128)(2,1)S(1)}, bf16[128,2048]{1,0:T(8,128)(2,1)S(1)}, u32[]{:S(2)}, u32[]{:S(2)}) collective-permute-start(bf16[128,2048]{1,0:T(8,128)(2,1)S(1)} %copy-done.8), channel_id=1, source_target_pairs={{0,2},{1,3},{2,0},{3,1},{4,6},{5,7},{6,4},{7,5},{8,10},{9,11},{10,... | collective-permute-start | bytes 1572872 | tf_op jit(solution)/shard_map/ppermute | solution.py:343
  5.8 11.9 %collective-permute-start.1 = (bf16[128,2048]{1,0:T(8,128)(2,1)S(1)}, bf16[128,2048]{1,0:T(8,128)(2,1)S(1)}, u32[]{:S(2)}, u32[]{:S(2)}) collective-permute-start(bf16[128,2048]{1,0:T(8,128)(2,1)S(1)} %copy-done.8), channel_id=1, source_target_pairs={{0,1},{1,0},{2,3},{3,2},{4,5},{5,4},{6,7},{7,6},{8,9},{9,8},{10,11... | collective-permute-start | bytes 1572872 | tf_op jit(solution)/shard_map/ppermute | solution.py:343
  5.8 18.2 %collective-permute-start = (bf16[128,2048]{1,0:T(8,128)(2,1)}, bf16[128,2048]{1,0:T(8,128)(2,1)S(1)}, u32[]{:S(2)}, u32[]{:S(2)}) collective-permute-start(bf16[128,2048]{1,0:T(8,128)(2,1)} %multiply_convert_fusion), channel_id=1, source_target_pairs={{0,4},{4,8},{8,12},{12,16},{16,20},{20,24},{24,28},{1,5},{5,9},{9,... | collective-permute-start | bytes 1572872 | tf_op jit(solution)/shard_map/ppermute | solution.py:446
  15.5 9.2 %copy-start.11 = (bf16[128,2048]{1,0:T(8,128)(2,1)S(1)}, bf16[128,2048]{1,0:T(8,128)(2,1)}, u32[]{:S(2)}) copy-start(bf16[128,2048]{1,0:T(8,128)(2,1)} %refs_5_.4) | copy-start | bytes 1572868
  15.6 9.2 %copy-start.12 = (bf16[128,2048]{1,0:T(8,128)(2,1)S(1)}, bf16[128,2048]{1,0:T(8,128)(2,1)}, u32[]{:S(2)}) copy-start(bf16[128,2048]{1,0:T(8,128)(2,1)} %refs_0_.5) | copy-start | bytes 1572868
  15.6 9.2 %copy-start.13 = (bf16[128,2048]{1,0:T(8,128)(2,1)S(1)}, bf16[128,2048]{1,0:T(8,128)(2,1)}, u32[]{:S(2)}) copy-start(bf16[128,2048]{1,0:T(8,128)(2,1)} %refs_1_.18) | copy-start | bytes 1572868
  17.7 11.5 %collective-permute-start.3 = (bf16[128,2048]{1,0:T(8,128)(2,1)S(1)}, bf16[128,2048]{1,0:T(8,128)(2,1)S(1)}, u32[]{:S(2)}, u32[]{:S(2)}) collective-permute-start(bf16[128,2048]{1,0:T(8,128)(2,1)S(1)} %collective-permute-done.2.refs_4_.refs_3_), channel_id=1, source_target_pairs={{0,1},{1,0},{2,3},{3,2},{4,5},{5,4},{6,7},{7,6},{8,9},{9,8},{10,11... | collective-permute-start | bytes 1572872 | tf_op jit(solution)/shard_map/ppermute | solution.py:343
  31.2 18.8 %collective-permute-start.4 = (bf16[176,2048]{1,0:T(8,128)(2,1)}, bf16[176,2048]{1,0:T(8,128)(2,1)S(1)}, u32[]{:S(2)}, u32[]{:S(2)}) collective-permute-start(bf16[176,2048]{1,0:T(8,128)(2,1)} %get-tuple-element.46), channel_id=1, source_target_pairs={{0,8},{8,16},{16,24},{24,28},{28,20},{20,12},{12,4},{4,0},{1,9},{9... | collective-permute-start | bytes 2162696 | tf_op jit(solution)/shard_map/ppermute | solution.py:490
  33.0 18.5 %collective-permute-start.5 = (bf16[176,2048]{1,0:T(8,128)(2,1)}, bf16[176,2048]{1,0:T(8,128)(2,1)S(1)}, u32[]{:S(2)}, u32[]{:S(2)}) collective-permute-start(bf16[176,2048]{1,0:T(8,128)(2,1)} %get-tuple-element.47), channel_id=1, source_target_pairs={{8,0},{16,8},{24,16},{28,24},{20,28},{12,20},{4,12},{0,4},{9,1},{1... | collective-permute-start | bytes 2162696 | tf_op jit(solution)/shard_map/ppermute | solution.py:490
  49.9 3.7 %collective-permute-start.11 = (bf16[128,2048]{1,0:T(8,128)(2,1)}, bf16[128,2048]{1,0:T(8,128)(2,1)}, u32[]{:S(2)}, u32[]{:S(2)}) collective-permute-start(bf16[128,2048]{1,0:T(8,128)(2,1)} %get-tuple-element.56), channel_id=1, source_target_pairs={{0,1},{1,0},{2,3},{3,2},{4,5},{5,4},{6,7},{7,6},{8,9},{9,8},{10,11... | collective-permute-start | bytes 1572872 | tf_op jit(solution)/shard_map/ppermute | solution.py:343
  50.0 19.3 %copy-start.4 = (bf16[176,2048]{1,0:T(8,128)(2,1)}, bf16[176,2048]{1,0:T(8,128)(2,1)S(1)}, u32[]{:S(2)}) copy-start(bf16[176,2048]{1,0:T(8,128)(2,1)S(1)} %collective-permute-done.4.refs_6_.refs_4_) | copy-start | bytes 2162692
  51.5 17.8 %copy-start.6 = (bf16[176,2048]{1,0:T(8,128)(2,1)}, bf16[176,2048]{1,0:T(8,128)(2,1)S(1)}, u32[]{:S(2)}) copy-start(bf16[176,2048]{1,0:T(8,128)(2,1)S(1)} %collective-permute-done.5.refs_7_.refs_5_) | copy-start | bytes 2162692
  51.6 20.6 %collective-permute-start.6 = (bf16[160,2048]{1,0:T(8,128)(2,1)S(1)}, bf16[160,2048]{1,0:T(8,128)(2,1)S(1)}, u32[]{:S(2)}, u32[]{:S(2)}) collective-permute-start(bf16[160,2048]{1,0:T(8,128)(2,1)S(1)} %slice.82), channel_id=1, source_target_pairs={{0,8},{8,16},{16,24},{24,28},{28,20},{20,12},{12,4},{4,0},{1,9},{9... | collective-permute-start | bytes 1966088 | tf_op jit(solution)/shard_map/ppermute | solution.py:490
  53.2 19.0 %collective-permute-start.7 = (bf16[160,2048]{1,0:T(8,128)(2,1)S(1)}, bf16[160,2048]{1,0:T(8,128)(2,1)S(1)}, u32[]{:S(2)}, u32[]{:S(2)}) collective-permute-start(bf16[160,2048]{1,0:T(8,128)(2,1)S(1)} %slice.83), channel_id=1, source_target_pairs={{8,0},{16,8},{24,16},{28,24},{20,28},{12,20},{4,12},{0,4},{9,1},{1... | collective-permute-start | bytes 1966088 | tf_op jit(solution)/shard_map/ppermute | solution.py:490
  64.1 8.1 %collective-permute-start.15 = (bf16[16,2048]{1,0:T(8,128)(2,1)S(1)}, bf16[16,2048]{1,0:T(8,128)(2,1)S(1)}, u32[]{:S(2)}, u32[]{:S(2)}) collective-permute-start(bf16[16,2048]{1,0:T(8,128)(2,1)S(1)} %get-tuple-element.63), channel_id=1, source_target_pairs={{0,28},{8,20},{16,12},{24,4},{28,0},{20,8},{12,16},{4,24},{1,29},{... | collective-permute-start | bytes 196616 | tf_op jit(solution)/shard_map/ppermute | solution.py:519
  67.7 10.1 %collective-permute-start.13 = (bf16[1024,128]{1,0:T(8,128)(2,1)S(1)}, bf16[1024,128]{1,0:T(8,128)(2,1)S(1)}, u32[]{:S(2)}, u32[]{:S(2)}) collective-permute-start(bf16[1024,128]{1,0:T(8,128)(2,1)S(1)} %get-tuple-element.88), channel_id=1, source_target_pairs={{0,4},{4,0},{8,12},{12,8},{16,20},{20,16},{24,28},{28,24},{1,5},{5... | collective-permute-start | bytes 786440 | tf_op jit(solution)/shard_map/ppermute | solution.py:343
  72.3 17.5 %collective-permute-start.8 = (bf16[144,2048]{1,0:T(8,128)(2,1)S(1)}, bf16[144,2048]{1,0:T(8,128)(2,1)S(1)}, u32[]{:S(2)}, u32[]{:S(2)}) collective-permute-start(bf16[144,2048]{1,0:T(8,128)(2,1)S(1)} %slice.84), channel_id=1, source_target_pairs={{0,8},{8,16},{16,24},{24,28},{28,20},{20,12},{12,4},{4,0},{1,9},{9... | collective-permute-start | bytes 1769480 | tf_op jit(solution)/shard_map/ppermute | solution.py:490
  73.2 16.6 %collective-permute-start.9 = (bf16[144,2048]{1,0:T(8,128)(2,1)S(1)}, bf16[144,2048]{1,0:T(8,128)(2,1)S(1)}, u32[]{:S(2)}, u32[]{:S(2)}) collective-permute-start(bf16[144,2048]{1,0:T(8,128)(2,1)S(1)} %slice.85), channel_id=1, source_target_pairs={{8,0},{16,8},{24,16},{28,24},{20,28},{12,20},{4,12},{0,4},{9,1},{1... | collective-permute-start | bytes 1769480 | tf_op jit(solution)/shard_map/ppermute | solution.py:490
  74.5 17.6 %collective-permute-start.16 = (bf16[64,2048]{1,0:T(8,128)(2,1)S(1)}, bf16[64,2048]{1,0:T(8,128)(2,1)S(1)}, u32[]{:S(2)}, u32[]{:S(2)}) collective-permute-start(bf16[64,2048]{1,0:T(8,128)(2,1)S(1)} %get-tuple-element.95.refs_10_), channel_id=1, source_target_pairs={{0,2},{1,3},{2,0},{3,1},{4,6},{5,7},{6,4},{7,5},{8,10},{9,11},{10,... | collective-permute-start | bytes 786440 | tf_op jit(solution)/shard_map/ppermute | solution.py:343
  89.9 10.7 %collective-permute-start.19 = (bf16[64,2048]{1,0:T(8,128)(2,1)S(1)}, bf16[64,2048]{1,0:T(8,128)(2,1)S(1)}, u32[]{:S(2)}, u32[]{:S(2)}) collective-permute-start(bf16[64,2048]{1,0:T(8,128)(2,1)S(1)} %pad_maximum_fusion.2.refs_11_), channel_id=1, source_target_pairs={{0,2},{1,3},{2,0},{3,1},{4,6},{5,7},{6,4},{7,5},{8,10},{9,11},{10,... | collective-permute-start | bytes 786440 | tf_op jit(solution)/shard_map/ppermute | solution.py:343
  92.6 7.9 %collective-permute-start.18 = (bf16[64,2048]{1,0:T(8,128)(2,1)S(1)}, bf16[64,2048]{1,0:T(8,128)(2,1)S(1)}, u32[]{:S(2)}, u32[]{:S(2)}) collective-permute-start(bf16[64,2048]{1,0:T(8,128)(2,1)S(1)} %slice.75), channel_id=1, source_target_pairs={{8,0},{16,8},{24,16},{28,24},{20,28},{12,20},{4,12},{0,4},{9,1},{1... | collective-permute-start | bytes 786440 | tf_op jit(solution)/shard_map/ppermute | solution.py:545
  93.1 7.4 %collective-permute-start.17 = (bf16[64,2048]{1,0:T(8,128)(2,1)S(1)}, bf16[64,2048]{1,0:T(8,128)(2,1)S(1)}, u32[]{:S(2)}, u32[]{:S(2)}) collective-permute-start(bf16[64,2048]{1,0:T(8,128)(2,1)S(1)} %slice.74), channel_id=1, source_target_pairs={{0,8},{8,16},{16,24},{24,28},{28,20},{20,12},{12,4},{4,0},{1,9},{9... | collective-permute-start | bytes 786440 | tf_op jit(solution)/shard_map/ppermute | solution.py:545
  100.6 2.7 %collective-permute-start.20 = (bf16[256,2048]{1,0:T(8,128)(2,1)S(1)}, bf16[256,2048]{1,0:T(8,128)(2,1)S(1)}, u32[]{:S(2)}, u32[]{:S(2)}) collective-permute-start(bf16[256,2048]{1,0:T(8,128)(2,1)S(1)} %constant_dynamic-update-slice_fusion.4), channel_id=1, source_target_pairs={{0,1},{1,0},{2,3},{3,2},{4,5},{5,4},{6,7},{7,6},{8,9},{9,8},{10,11... | collective-permute-start | bytes 3145736 | tf_op jit(solution)/shard_map/ppermute | solution.py:343
  100.7 7.7 %collective-permute-start.14 = (bf16[512,128]{1,0:T(8,128)(2,1)S(1)}, bf16[512,128]{1,0:T(8,128)(2,1)S(1)}, u32[]{:S(2)}, u32[]{:S(2)}) collective-permute-start(bf16[512,128]{1,0:T(8,128)(2,1)S(1)} %get-tuple-element.62), channel_id=1, source_target_pairs={{0,8},{4,12},{8,0},{12,4},{16,24},{20,28},{24,16},{28,20},{1,9},{5... | collective-permute-start | bytes 393224 | tf_op jit(solution)/shard_map/ppermute | solution.py:343
  108.9 22.3 %collective-permute-start.21 = (bf16[128,2048]{1,0:T(8,128)(2,1)S(1)}, bf16[128,2048]{1,0:T(8,128)(2,1)S(1)}, u32[]{:S(2)}, u32[]{:S(2)}) collective-permute-start(bf16[128,2048]{1,0:T(8,128)(2,1)S(1)} %copy-done.19), channel_id=1, source_target_pairs={{4,0},{8,4},{12,8},{16,12},{20,16},{24,20},{28,24},{5,1},{9,5},{13... | collective-permute-start | bytes 1572872 | tf_op jit(solution)/shard_map/ppermute | solution.py:569
  110.2 26.7 %collective-permute-start.10 = (bf16[128,2048]{1,0:T(8,128)(2,1)S(1)}, bf16[128,2048]{1,0:T(8,128)(2,1)S(1)}, u32[]{:S(2)}, u32[]{:S(2)}) collective-permute-start(bf16[128,2048]{1,0:T(8,128)(2,1)S(1)} %mixed_part.2.refs_5_), channel_id=1, source_target_pairs={{0,1},{1,0},{2,3},{3,2},{4,5},{5,4},{6,7},{7,6},{8,9},{9,8},{10,11... | collective-permute-start | bytes 1572872 | tf_op jit(solution)/shard_map/ppermute | solution.py:343
  110.4 26.5 %collective-permute-start.12 = (bf16[128,2048]{1,0:T(8,128)(2,1)S(1)}, bf16[128,2048]{1,0:T(8,128)(2,1)S(1)}, u32[]{:S(2)}, u32[]{:S(2)}) collective-permute-start(bf16[128,2048]{1,0:T(8,128)(2,1)S(1)} %convert_add_fusion), channel_id=1, source_target_pairs={{0,2},{1,3},{2,0},{3,1},{4,6},{5,7},{6,4},{7,5},{8,10},{9,11},{10,... | collective-permute-start | bytes 1572872 | tf_op jit(solution)/shard_map/ppermute | solution.py:343
  111.3 19.3 %collective-permute-start.22 = (bf16[512,128]{1,0:T(8,128)(2,1)S(1)}, bf16[512,128]{1,0:T(8,128)(2,1)S(1)}, u32[]{:S(2)}, u32[]{:S(2)}) collective-permute-start(bf16[512,128]{1,0:T(8,128)(2,1)S(1)} %added.4.refs_1_), channel_id=1, source_target_pairs={{0,16},{4,20},{8,24},{12,28},{16,0},{20,4},{24,8},{28,12},{1,17},{... | collective-permute-start | bytes 393224 | tf_op jit(solution)/shard_map/ppermute | solution.py:343
  119.4 11.9 %copy-start.17 = (bf16[2048,128]{1,0:T(8,128)(2,1)S(1)}, bf16[2048,128]{1,0:T(8,128)(2,1)}, u32[]{:S(2)}) copy-start(bf16[2048,128]{1,0:T(8,128)(2,1)} %refs_4_.4) | copy-start | bytes 1572868
  119.4 11.9 %copy-start.25 = (bf16[2,128,256]{2,1,0:T(8,128)(2,1)S(1)}, bf16[2,128,256]{2,1,0:T(8,128)(2,1)}, u32[]{:S(2)}) copy-start(bf16[2,128,256]{2,1,0:T(8,128)(2,1)} %constant.25.clone.refs_6_) | copy-start | bytes 393220
  131.2 5.0 %collective-permute-start.23 = (bf16[512,128]{1,0:T(8,128)(2,1)S(1)}, bf16[512,128]{1,0:T(8,128)(2,1)S(1)}, u32[]{:S(2)}, u32[]{:S(2)}) collective-permute-start(bf16[512,128]{1,0:T(8,128)(2,1)S(1)} %added.5.refs_1_), channel_id=1, source_target_pairs={{0,8},{4,12},{8,0},{12,4},{16,24},{20,28},{24,16},{28,20},{1,9},{5... | collective-permute-start | bytes 393224 | tf_op jit(solution)/shard_map/ppermute | solution.py:343
  136.8 6.6 %collective-permute-start.24 = (bf16[1024,128]{1,0:T(8,128)(2,1)S(1)}, bf16[1024,128]{1,0:T(8,128)(2,1)S(1)}, u32[]{:S(2)}, u32[]{:S(2)}) collective-permute-start(bf16[1024,128]{1,0:T(8,128)(2,1)S(1)} %joined.2.refs_1_), channel_id=1, source_target_pairs={{0,4},{4,0},{8,12},{12,8},{16,20},{20,16},{24,28},{28,24},{1,5},{5... | collective-permute-start | bytes 786440 | tf_op jit(solution)/shard_map/ppermute | solution.py:343
  (25 other events, 110.1 us)
